TPU v7x, 128 devices: a whole 4x4x4 slice. The times are simulated.
128 devices in a mesh: seq: 16 (over z, x), head: 8 (over y, core).
Axes of the slice: x: 4, y: 4, z: 4, core: 2. Of those that a mesh axis runs over, the one named last changes fastest.
Arguments:
- queries: float32 [16384, 4096], P('seq', 'head'), may hold values from -8 to 8
- key_rows: float32 [16384, 1024], P('seq', 'head'), may hold values from -8 to 8
- value_vectors: float32 [16384, 1024], P('seq', 'head'), may hold values from -6 to 6
- vertical_blocks: int32 [32, 8], replicated, may hold values from 0 to 255, all different within a row
- slash_offsets: int32 [32, 3], replicated, may hold values from 0 to 31, all different within a row
- prompt_length: int32 [1], replicated, may hold values from 4096 to 8191
- out_weight: float32 [4096, 4096], P('head'), may hold values from -0.09375 to 0.09375
Outputs:
- projected: float32 [16384, 4096], P('seq', 'head')
Inputs may be any that keep to these rules, and one draw needn't show every extreme that they name: `vertical_blocks`: each head's 8 blocks are all different, and every block of the slab is named by some head. `slash_offsets`: each head's 3 values are all different.
All inputs are finite; a program needn't handle non-finite values.
Results may differ from a plain program's by a relative error of at most 0.0003.
Values sent between devices are 32-bit elements; how exact they have to be, the bound alone decides.
No kernel may reach another device: no remote copies, remote signals or barrier semaphores. Data moves between devices by JAX's collectives and lax.ppermute only.
A program may use at most 128 MiB of HBM per device.

v0:
```python
import math

import jax
import jax.numpy as jnp
from jax import lax
from jax.sharding import PartitionSpec as P

HEAD_SIZE = 128


def arrange(first_rows, second_rows, count, kv_local):
    stacked = jnp.stack([first_rows, second_rows]).reshape(2, count, 64, kv_local, HEAD_SIZE)
    return stacked.transpose(3, 1, 0, 2, 4)


def body(
    queries, key_rows, value_vectors, vertical_blocks, slash_offsets, prompt_length, out_weight
):
    rows_local = queries.shape[0]
    blocks_local = rows_local // 64
    heads_local = queries.shape[1] // HEAD_SIZE
    kv_local = key_rows.shape[1] // HEAD_SIZE
    query_group_width = heads_local // kv_local
    score_scale = 1.0 / math.sqrt(HEAD_SIZE)
    seq_index = lax.axis_index("seq")
    head_index = lax.axis_index("head")
    vert_local = lax.dynamic_slice_in_dim(vertical_blocks, head_index * heads_local, heads_local, 0)
    slash_local = lax.dynamic_slice_in_dim(slash_offsets, head_index * heads_local, heads_local, 0)
    kv_of_head = jnp.arange(heads_local, dtype=jnp.int32) // query_group_width
    whole_keys, whole_values = (
        lax.all_gather(key_rows, "seq", axis=0, tiled=True),
        lax.all_gather(value_vectors, "seq", axis=0, tiled=True),
    )
    whole_rows = arrange(whole_keys, whole_values, whole_keys.shape[0] // 64, kv_local)
    picked = whole_rows[kv_of_head[:, None], vert_local]
    front_pad = jnp.zeros((2 * rows_local, whole_keys.shape[1]), jnp.float32)
    padded_keys = jnp.concatenate([front_pad, whole_keys], axis=0)
    padded_values = jnp.concatenate([front_pad, whole_values], axis=0)
    near_keys = lax.dynamic_slice_in_dim(padded_keys, seq_index * rows_local, 3 * rows_local, 0)
    near_values = lax.dynamic_slice_in_dim(padded_values, seq_index * rows_local, 3 * rows_local, 0)
    vert_count = vert_local.shape[1]
    vert_keys = picked[:, :, 0].reshape(heads_local, vert_count * 64, HEAD_SIZE)
    vert_values = picked[:, :, 1].reshape(heads_local, vert_count * 64, HEAD_SIZE)
    near_rows = arrange(near_keys, near_values, 3 * blocks_local, kv_local)
    offsets = jnp.concatenate([jnp.zeros((heads_local, 1), jnp.int32), slash_local + 1], axis=1)
    local_ids = jnp.arange(blocks_local, dtype=jnp.int32)
    block_ids = seq_index * blocks_local + local_ids
    slash_block = block_ids[None, :, None] - offsets[:, None, :]
    repeated = jnp.any(slash_block[:, :, :, None] == vert_local[:, None, None, :], axis=-1)
    usable = (slash_block >= 0) & jnp.logical_not(repeated)
    clipped = jnp.maximum(slash_block, 0)
    near_index = local_ids[None, :, None] + 2 * blocks_local - offsets[:, None, :]
    slash_pairs = near_rows[kv_of_head[:, None, None], near_index]
    slash_keys = slash_pairs[:, :, :, 0]
    slash_values = slash_pairs[:, :, :, 1]
    query_blocks = queries.reshape(blocks_local, 64, heads_local, HEAD_SIZE).transpose(2, 0, 1, 3)
    inside = jnp.arange(64, dtype=jnp.int32)
    query_pos = block_ids[:, None] * 64 + inside[None, :]
    prompt_end = prompt_length[0]
    vert_pos = (vert_local[:, :, None] * 64 + inside[None, None, :]).reshape(
        heads_local, vert_count * 64
    )
    vert_scores = (
        jnp.einsum("hbrd,hkd->hbrk", query_blocks, vert_keys, precision=lax.Precision.HIGHEST)
        * score_scale
    )
    vert_seen = (vert_pos[:, None, None, :] <= query_pos[None, :, :, None]) | (
        vert_pos[:, None, None, :] < prompt_end
    )
    slash_scores = (
        jnp.einsum("hbrd,hbnkd->hbrnk", query_blocks, slash_keys, precision=lax.Precision.HIGHEST)
        * score_scale
    )
    slash_pos = clipped[:, :, None, :, None] * 64 + inside[None, None, None, None, :]
    slash_seen = usable[:, :, None, :, None] & (
        (slash_pos <= query_pos[None, :, :, None, None]) | (slash_pos < prompt_end)
    )
    vert_scores = jnp.where(vert_seen, vert_scores, -jnp.inf)
    slash_scores = jnp.where(slash_seen, slash_scores, -jnp.inf)
    row_max = jnp.maximum(jnp.max(vert_scores, axis=-1), jnp.max(slash_scores, axis=(-2, -1)))
    vert_weights = jnp.exp(vert_scores - row_max[..., None])
    slash_weights = jnp.exp(slash_scores - row_max[..., None, None])
    row_total = jnp.sum(vert_weights, axis=-1) + jnp.sum(slash_weights, axis=(-2, -1))
    mixed_rows = jnp.einsum(
        "hbrk,hkd->hbrd", vert_weights, vert_values, precision=lax.Precision.HIGHEST
    )
    mixed_rows = mixed_rows + jnp.einsum(
        "hbrnk,hbnkd->hbrd", slash_weights, slash_values, precision=lax.Precision.HIGHEST
    )
    attended = (
        (mixed_rows / row_total[..., None])
        .transpose(1, 2, 0, 3)
        .reshape(rows_local, heads_local * HEAD_SIZE)
    )
    partial_value = jnp.dot(
        attended, out_weight, precision=lax.Precision.HIGHEST, preferred_element_type=jnp.float32
    )
    return lax.psum_scatter(partial_value, "head", scatter_dimension=1, tiled=True)


def solution(mesh):
    placed = (P("seq", "head"), P("seq", "head"), P("seq", "head"), P(), P(), P(), P("head", None))
    return jax.shard_map(
        body, mesh=mesh, in_specs=placed, out_specs=P("seq", "head"), check_vma=False
    )
```

profile of v0, /device:TPU:2, one launch (start us, length us, event | category | flops | bytes accessed | tf_op | source)
XLA Modules:
  0.0 384.6 jit_solution(16882773366807261475)
XLA Ops:
  6.5 0.7 all-gather.5.cloned.1.call-update
  7.3 0.0 all-gather.3.cloned.1.call-start
  7.3 0.7 all-gather.3.cloned.1.call-update
  8.0 0.0 reduce-scatter.2.cloned.1.call-start
  8.1 0.8 broadcast_multiply_fusion
  8.8 0.1 copy.31
  8.9 0.1 copy.27
  9.0 0.1 bitcast_or_fusion
  9.1 0.1 reshape.193
  9.8 0.1 copy.26
  9.9 0.1 add.171
  10.0 0.1 add.172
  10.1 0.1 add.174
  10.1 2.9 reshape.191
  13.0 0.8 dynamic-slice_add_fusion
  13.8 0.1 copy.43
  13.9 0.1 concatenate.18.clone
  13.9 0.1 broadcast_subtract_fusion
  14.0 0.1 copy.33
  14.1 0.1 compare_reduce_fusion
  14.2 0.1 not_and_fusion
  14.3 0.1 copy.32
  14.4 0.1 fusion.24
  14.5 0.1 reshape.199
  14.6 0.1 iota_add_fusion.1
  14.7 0.1 broadcast_compare_fusion
  14.9 0.1 iota_add_fusion
  15.0 67.7 %all-gather.5.cloned.1.call-done = f32[16384,128]{1,0:T(8,128)} async-done(((f32[1024,128]{1,0:T(8,128)}), f32[16384,128]{1,0:T(8,128)}) %all-gather.5.cloned.1.call-update) | async-done | bytes 8388624 | tf_op jit(solution)/shard_map/all_gather | solution.py:32
  82.8 72.6 %all-gather.3.cloned.1.call-done = f32[16384,128]{1,0:T(8,128)} async-done(((f32[1024,128]{1,0:T(8,128)}), f32[16384,128]{1,0:T(8,128)}) %all-gather.3.cloned.1.call-update) | async-done | bytes 8388624 | tf_op jit(solution)/shard_map/all_gather | solution.py:31
  155.4 11.8 %maximum_bitcast_fusion = f32[1,256,2,64,128]{4,3,1,0,2:T(8,128)} fusion(f32[1,256,64,1,128]{4,2,1,3,0:T(8,128)} %bitcast.91, f32[1,256,64,1,128]{4,2,1,3,0:T(8,128)} %bitcast.92), kind=kLoop, calls=%fused_computation.2 | loop fusion | flops 4194304 | bytes 33554432 | tf_op jit(solution)/shard_map/transpose | solution.py:13
  167.2 6.4 %gather_fusion = f32[32,2,64,128]{3,2,1,0:T(8,128)S(1)} fusion(f32[1,256,2,64,128]{4,3,1,0,2:T(8,128)} %maximum_bitcast_fusion, s32[32]{0:T(128)S(1)} %reshape.193), kind=kCustom, calls=%fused_computation | custom fusion | bytes 4194560 | tf_op jit(solution)/shard_map/gather | solution.py:35
  173.6 0.2 copy.28
  173.9 1.5 fusion.33
  175.4 1.8 pad_dynamic-slice_fusion
  177.2 1.2 slice-done.1
  178.4 0.3 pad_dynamic-slice_fusion.1
  178.7 0.4 maximum_bitcast_fusion.1
  179.2 7.4 %gather_fusion.1 = f32[256,2,64,128]{3,2,1,0:T(8,128)} fusion(f32[1,48,2,64,128]{4,3,2,1,0:T(8,128)S(1)} %maximum_bitcast_fusion.1, s32[256]{0:T(256)S(1)} %reshape.199), kind=kCustom, calls=%fused_computation.1 | custom fusion | bytes 33556480 | tf_op jit(solution)/shard_map/gather | solution.py:53
  186.5 7.8 %copy.35 = f32[256,2,64,128]{3,2,0,1:T(8,128)S(1)} copy(f32[256,2,64,128]{3,2,1,0:T(8,128)} %gather_fusion.1) | data formatting | bytes 33554432 | tf_op jit(solution)/shard_map/gather | solution.py:53
  194.3 8.3 %fusion.5 = (f32[4,16,64]{2,1,0:T(8,128)S(1)}, f32[4,512,16,64]{1,3,2,0:T(8,128)S(1)}) fusion(s32[16,64]{1,0:T(8,128)S(1)} %iota_add_fusion.1, s32[4,512]{1,0:T(4,128)S(1)} %get-tuple-element.6, pred[4,512]{1,0:T(4,128)(4,1)S(1)} %get-tuple-element.5, f32[4,512,128,1]{2,1,3,0:T(8,128)S(1)} %bitcast.104, f32[16,64,4,128]{3,2,1,0:T(4,128)S(1)} %copy-done), kind=kOutput, calls=%fused_computation.16 | convolution fusion | flops 3231707136 | bytes 11565056 | tf_op jit(solution)/shard_map/hbrd,hkd->hbrk/dot_general | solution.py:64
  202.6 10.8 %fusion.13 = (f32[4,16,64]{2,1,0:T(8,128)S(1)}, f32[4,16,4,64,64]{4,3,2,1,0:T(8,128)S(1)}) fusion(pred[4,16,4,64]{3,2,1,0:T(4,128)(4,1)S(1)} %broadcast_compare_fusion, s32[16,64]{1,0:T(8,128)S(1)} %iota_add_fusion.1, s32[4,16,4,64]{3,2,1,0:T(4,128)S(1)} %iota_add_fusion, pred[4,16,4]{2,1,0:T(8,128)(4,1)S(1)} %copy.32, f32[16,64,4,128]{3,2,1,0:T(4,128)S(1)} %copy-done, ...), kind=kOutput, calls=%fused_computation.24 | convolution fusion | flops 1616900096 | bytes 14876672 | tf_op jit(solution)/shard_map/hbrd,hbnkd->hbrnk/dot_general | solution.py:71
  213.4 3.7 fusion.2
  217.1 9.6 %fusion.3 = f32[4,16,64,128]{3,2,1,0:T(8,128)S(1)} fusion(f32[4,512,128,1]{2,1,3,0:T(8,128)S(1)} %bitcast.103, f32[4,512,16,64]{1,3,2,0:T(8,128)S(1)} %get-tuple-element.14, f32[4,16,64]{2,1,0:T(8,128)S(1)} %max.19, s32[16,64]{1,0:T(8,128)S(1)} %iota_add_fusion.1, s32[4,512]{1,0:T(4,128)S(1)} %get-tuple-element.6, pred[4,512]{1,0:T(4,128)(4,1)S(1)} %get-tuple-element.5), kind=kOutput, calls=%fused_computation.14 | convolution fusion | flops 3231711232 | bytes 11565056 | tf_op jit(solution)/shard_map/hbrk,hkd->hbrd/dot_general | solution.py:84
  226.7 6.2 %fusion.4 = f32[4,16,64]{2,1,0:T(8,128)S(1)} fusion(f32[4,16,64]{2,1,0:T(8,128)S(1)} %max.19, f32[4,16,4,64,64]{4,3,2,1,0:T(8,128)S(1)} %get-tuple-element.16, pred[4,16,4,64]{3,2,1,0:T(4,128)(4,1)S(1)} %broadcast_compare_fusion, s32[16,64]{1,0:T(8,128)S(1)} %iota_add_fusion.1, s32[4,16,4,64]{3,2,1,0:T(4,128)S(1)} %iota_add_fusion, ...), kind=kLoop, calls=%fused_computation.15 | loop fusion | flops 7335936 | bytes 4313344 | tf_op jit(solution)/shard_map/reduce_sum | solution.py:83
  232.9 22.6 %bitcast_divide_fusion = f32[16,64,4,128]{3,1,0,2:T(8,128)S(1)} fusion(f32[4,16,64,128]{3,2,1,0:T(8,128)S(1)} %fusion.3, f32[4,16,4,2,64,128]{5,4,2,1,0,3:T(8,128)S(1)} %bitcast.96, f32[4,16,64]{2,1,0:T(8,128)S(1)} %max.19, f32[4,16,4,64,64]{4,3,2,1,0:T(8,128)S(1)} %get-tuple-element.16, pred[4,16,4,64]{3,2,1,0:T(4,128)(4,1)S(1)} %broadcast_compare_fusion, ...), kind=kOutput, calls=%fused_computation.30 | convolution fusion | flops 1617952768 | bytes 21217280 | tf_op jit(solution)/shard_map/hbrnk,hbnkd->hbrd/dot_general | solution.py:87
  255.5 1.4 copy.37
  256.9 29.4 %fusion.14 = f32[1024,4096]{1,0:T(8,128)} fusion(f32[512,4096]{1,0:T(8,128)S(1)} %bitcast.98, f32[128,8,4,128]{3,2,1,0:T(4,128)S(1)} %bitcast.100), kind=kOutput, calls=%fused_computation.26 | convolution fusion | flops 25769803776 | bytes 27262976 | tf_op jit(solution)/shard_map/dot_general | solution.py:95
  286.4 91.7 %reduce-scatter.2.cloned.1.call-done = f32[1024,512]{1,0:T(8,128)} async-done(((f32[1024,4096]{1,0:T(8,128)}), f32[1024,512]{1,0:T(8,128)}) %reduce-scatter.2.cloned.1.call-update) | async-done | bytes 2097168 | tf_op jit(solution)/shard_map/reduce_scatter | solution.py:98
  (25 shorter events, 0.1 us)
Async XLA Ops:
  6.5 76.2 %all-gather.5.cloned.1.call-start = ((), (), s32[]{:S(2)}) async-start(), calls=%async_computation.2 | async-start | bytes 8912896 | tf_op jit(solution)/shard_map/all_gather | solution.py:32
  7.3 148.1 %all-gather.3.cloned.1.call-start = ((), (), s32[]{:S(2)}) async-start(), calls=%async_computation.1 | async-start | bytes 8912896 | tf_op jit(solution)/shard_map/all_gather | solution.py:31
  8.0 370.1 %reduce-scatter.2.cloned.1.call-start = ((), (), s32[]{:S(2)}) async-start(), calls=%async_computation.3 | async-start | bytes 18874368 | tf_op jit(solution)/shard_map/reduce_scatter | solution.py:98
  173.6 3.6 slice-start
  175.4 3.0 slice-start.1
  186.5 7.8 %copy-start = (f32[16,64,4,128]{3,2,1,0:T(4,128)S(1)}, f32[16,64,4,128]{3,2,1,0:T(4,128)}, u32[]{:S(2)}) copy-start(f32[16,64,4,128]{3,2,1,0:T(4,128)} %reshape.191) | copy-start | bytes 6291460
  186.5 7.8 %copy-start.2 = (f32[4,8,1,64,128]{4,3,1,0,2:T(8,128)S(1)}, f32[4,8,1,64,128]{4,3,1,0,2:T(8,128)}, u32[]{:S(2)}) copy-start(f32[4,8,1,64,128]{4,3,1,0,2:T(8,128)} %get-tuple-element.9) | copy-start | bytes 3145732
  213.4 3.8 copy-start.1
  226.7 30.2 %slice-start.2 = ((s8[8388608]{0:T(1024)(128)(4,1)}), s8[4194304]{0:T(1024)(128)(4,1)S(1)}, s32[]{:S(2)}) async-start(s8[8388608]{0:T(1024)(128)(4,1)} %bitcast.97), calls=%async_computation.6 | async-start | bytes 8388608
  232.9 24.0 %slice-start.3 = ((s8[8388608]{0:T(1024)(128)(4,1)}), s8[4194304]{0:T(1024)(128)(4,1)S(1)}, s32[]{:S(2)}) async-start(s8[8388608]{0:T(1024)(128)(4,1)} %bitcast.97), calls=%async_computation.7 | async-start | bytes 8388608
Sparse Core Ops, SparseCore 0:
  9.5 73.2 all-gather.4
  84.9 70.4 all-gather.2
  286.5 91.4 reduce-scatter.1
where the time goes:
time: 385 us
  waiting for transfers between devices  233 us (61%)
  matrix products  80.6 us (21%)
  local copies, waits for them, and re-layouts  32 us (8%)
  other arithmetic  24.4 us (6%)
  between operations  14 us (4%)
    reduce_scatter x1, waiting for transfers between devices, body(): lax.psum_scatter(partial_value, 'head', scatter_dimension=1, tiled=True)  91.7 us
    all_gather x1, waiting for transfers between devices, body(): lax.all_gather(key_rows, 'seq', axis=0, tiled=True)  72.6 us
    all_gather x1, waiting for transfers between devices, body(): lax.all_gather(value_vectors, 'seq', axis=0, tiled=True)  67.7 us
    dot_general x1, matrix products, body(): jnp.dot(attended, out_weight, precision=lax.Precision.HIGHEST, preferred_...  29.4 us
    dot_general x1, matrix products, body(): jnp.einsum('hbrnk,hbnkd->hbrd', slash_weights, slash_values, precision=la...  22.6 us
    gather x2, local copies, waits for them, and re-layouts, body(): slash_pairs = near_rows[kv_of_head[:, None, None], near_index]  15.1 us
    transpose x2, other arithmetic, arrange(): return stacked.transpose(3, 1, 0, 2, 4)  12.2 us
    dot_general x1, matrix products, body(): jnp.einsum('hbrd,hbnkd->hbrnk', query_blocks, slash_keys, precision=lax.P...  10.8 us
  transfers between devices with their start and end apart: 3, of which 3 were waited for; matrix products, arithmetic and copies ran while one was open for 2% of the time, Pallas kernels for 0%

commit v1 on v0

v1 whole, which is shorter than its diff:
```python
import functools
import math

import jax
import jax.numpy as jnp
from jax import lax
from jax.experimental import pallas as pl
from jax.experimental.pallas import tpu as pltpu
from jax.sharding import PartitionSpec as P

HEAD_SIZE = 128
BLOCK = 64
TILE = 256
FAR = 1 << 30
LOW = -1e30
SMALL = pl.CostEstimate(flops=1024, bytes_accessed=1024, transcendentals=0)


def pick_kernel(place, held, keys, values, both, picked):
    both[:, 0:HEAD_SIZE] = keys[...]
    both[:, HEAD_SIZE:] = values[...]
    for slot in range(picked.shape[0] // BLOCK):
        rows = pl.ds(slot * BLOCK, BLOCK)

        @pl.when(held[slot] == 1)
        def _():
            source = pl.ds(pl.multiple_of(place[slot] * BLOCK, BLOCK), BLOCK)
            picked[rows, 0:HEAD_SIZE] = keys[source, :]
            picked[rows, HEAD_SIZE:] = values[source, :]

        @pl.when(held[slot] == 0)
        def _():
            picked[rows, :] = jnp.zeros((BLOCK, 2 * HEAD_SIZE), jnp.float32)


def pick_blocks(place, held, keys, values):
    slots = place.shape[0]
    smem = pl.BlockSpec(memory_space=pltpu.SMEM)
    vmem = pl.BlockSpec(memory_space=pltpu.VMEM)
    return pl.pallas_call(
        pick_kernel,
        out_shape=[
            jax.ShapeDtypeStruct((keys.shape[0], 2 * HEAD_SIZE), jnp.float32),
            jax.ShapeDtypeStruct((slots * BLOCK, 2 * HEAD_SIZE), jnp.float32),
        ],
        in_specs=[smem, smem, vmem, vmem],
        out_specs=[vmem, vmem],
        compiler_params=pltpu.CompilerParams(vmem_limit_bytes=16 << 20),
    )(place, held, keys, values)


def split(x):
    high = x.astype(jnp.bfloat16)
    return high, (x - high.astype(jnp.float32)).astype(jnp.bfloat16)


def attend_kernel(
    first_row, scale, back, start, q, kv2, kv1, kv0, named, vert_pos, slash_pos, out,
    near_k, near_v, vert_k, vert_v,
):
    tile = pl.program_id(0)
    head = pl.program_id(1)

    def put_key(target, at, x):
        high, low = split(x)
        target[at, 0:128] = high
        target[at, 128:256] = high
        target[at, 256:384] = low

    def put_value(target, at, x):
        high, low = split(x)
        target[at, 0:128] = high
        target[at, 128:256] = low

    @pl.when((tile == 0) & (head == 0))
    def _():
        rows = kv0.shape[0]
        for part, kv in enumerate((kv2, kv1, kv0)):
            for step in range(rows // TILE):
                at = pl.ds(part * rows + step * TILE, TILE)
                put_key(near_k, at, kv[pl.ds(step * TILE, TILE), 0:HEAD_SIZE])
                put_value(near_v, at, kv[pl.ds(step * TILE, TILE), HEAD_SIZE:])
        for step in range(named.shape[0] // TILE):
            at = pl.ds(step * TILE, TILE)
            put_key(vert_k, at, named[at, 0:HEAD_SIZE])
            put_value(vert_v, at, named[at, HEAD_SIZE:])

    dot = functools.partial(lax.dot_general, preferred_element_type=jnp.float32)
    rows_by_rows = (((1,), (1,)), ((), ()))
    plain = (((1,), (0,)), ((), ()))
    q_high, q_low = split(q[...] * scale)
    q_parts = jnp.concatenate([q_high, q_low, q_high], axis=1)
    vert = vert_k.shape[0] // 4
    vert_rows = pl.ds(pl.multiple_of(head * vert, vert), vert)
    vert_scores = dot(q_parts, vert_k[vert_rows, :], rows_by_rows)
    place = first_row[0] + start + tile * TILE
    q_pos = place + lax.broadcasted_iota(jnp.int32, (TILE, 1), 0)
    vert_scores = jnp.where(vert_pos[head] <= q_pos, vert_scores, LOW)

    local = start // BLOCK + tile * (TILE // BLOCK)
    slash_scores = []
    near = []
    for j in range(TILE // BLOCK):
        spots = [
            pl.ds(pl.multiple_of((local + j + back[head, n]) * BLOCK, BLOCK), BLOCK)
            for n in range(4)
        ]
        near.append(spots)
        keys = jnp.concatenate([near_k[s, :] for s in spots], axis=0)
        score = dot(q_parts[j * BLOCK : (j + 1) * BLOCK], keys, rows_by_rows)
        seen = slash_pos[head, local + j] <= q_pos[j * BLOCK : (j + 1) * BLOCK]
        slash_scores.append(jnp.where(seen, score, LOW))
    slash_scores = jnp.concatenate(slash_scores, axis=0)

    top = jnp.maximum(
        jnp.max(vert_scores, axis=1, keepdims=True), jnp.max(slash_scores, axis=1, keepdims=True)
    )
    vert_w = jnp.exp(vert_scores - top)
    slash_w = jnp.exp(slash_scores - top)
    total = jnp.sum(vert_w, axis=1, keepdims=True) + jnp.sum(slash_w, axis=1, keepdims=True)
    vert_high, vert_low = split(vert_w)
    slash_high, slash_low = split(slash_w)
    wide = dot(vert_high, vert_v[vert_rows, :], plain)
    mixed = wide[:, :128] + wide[:, 128:] + dot(vert_low, vert_v[vert_rows, 0:128], plain)
    parts = []
    for j in range(TILE // BLOCK):
        values = jnp.concatenate([near_v[s, :] for s in near[j]], axis=0)
        mine = slice(j * BLOCK, (j + 1) * BLOCK)
        wide = dot(slash_high[mine], values, plain)
        parts.append(wide[:, :128] + wide[:, 128:] + dot(slash_low[mine], values[:, :128], plain))
    out[...] = (mixed + jnp.concatenate(parts, axis=0)) / total


def attend(q, start, rows, first_row, back, near, named, vert_pos, slash_pos):
    heads = q.shape[1] // HEAD_SIZE
    smem = pl.BlockSpec(memory_space=pltpu.SMEM)
    vmem = pl.BlockSpec(memory_space=pltpu.VMEM)
    window = sum(kv.shape[0] for kv in near)
    kernel = lambda first, back_ref, *refs: attend_kernel(
        first, 1.0 / math.sqrt(HEAD_SIZE), back_ref, start, *refs
    )
    base = start // TILE
    return pl.pallas_call(
        kernel,
        grid=(rows // TILE, heads),
        out_shape=jax.ShapeDtypeStruct((rows, heads * HEAD_SIZE), jnp.float32),
        in_specs=[smem, smem, pl.BlockSpec((TILE, HEAD_SIZE), lambda t, h: (base + t, h))]
        + [vmem] * 6,
        out_specs=pl.BlockSpec((TILE, HEAD_SIZE), lambda t, h: (t, h)),
        scratch_shapes=[
            pltpu.VMEM((window, 384), jnp.bfloat16),
            pltpu.VMEM((window, 256), jnp.bfloat16),
            pltpu.VMEM((named.shape[0], 384), jnp.bfloat16),
            pltpu.VMEM((named.shape[0], 256), jnp.bfloat16),
        ],
        compiler_params=pltpu.CompilerParams(vmem_limit_bytes=40 << 20),
        cost_estimate=SMALL,
    )(first_row, back, q, *near, named, vert_pos, slash_pos)


def take_kernel(core, w, out):
    out[...] = w[...]


def take_columns(weight, core, width):
    rows, columns = weight.shape
    count = columns // (2 * width)
    return pl.pallas_call(
        take_kernel,
        out_shape=jax.ShapeDtypeStruct((rows, count * width), jnp.float32),
        grid_spec=pltpu.PrefetchScalarGridSpec(
            num_scalar_prefetch=1,
            grid=(count,),
            in_specs=[pl.BlockSpec((rows, width), lambda i, c: (0, 2 * i + c[0]))],
            out_specs=pl.BlockSpec((rows, width), lambda i, c: (0, i)),
        ),
        compiler_params=pltpu.CompilerParams(vmem_limit_bytes=16 << 20),
        cost_estimate=SMALL,
    )(core, weight)


def halves_kernel(core, own, other, high, low):
    rows = own.shape[0]
    for first, ref in ((0, own), (rows, other)):
        high[0, first : first + rows], low[0, first : first + rows] = split(ref[...])


def weight_halves(own, other, core, width):
    rows = own.shape[0]
    count = other.shape[1] // width
    shape = jax.ShapeDtypeStruct((count, 2 * rows, width), jnp.bfloat16)
    spec = pl.BlockSpec((1, 2 * rows, width), lambda i, c: (i, 0, 0))
    return pl.pallas_call(
        halves_kernel,
        out_shape=[shape, shape],
        grid_spec=pltpu.PrefetchScalarGridSpec(
            num_scalar_prefetch=1,
            grid=(count,),
            in_specs=[
                pl.BlockSpec((rows, width), lambda i, c: (0, 2 * i + c[0])),
                pl.BlockSpec((rows, width), lambda i, c: (0, i)),
            ],
            out_specs=[spec, spec],
        ),
        compiler_params=pltpu.CompilerParams(vmem_limit_bytes=24 << 20),
        cost_estimate=SMALL,
    )(core, own, other)


def project_kernel(order, own, other, high, low, first, rest, x_high, x_low):
    depth = own.shape[1]

    @pl.when(pl.program_id(0) == 0)
    def _():
        x_high[:, :depth], x_low[:, :depth] = split(own[...])
        x_high[:, depth:], x_low[:, depth:] = split(other[...])

    dot = functools.partial(jnp.dot, preferred_element_type=jnp.float32)
    term = dot(x_high[...], high[0]) + (dot(x_high[...], low[0]) + dot(x_low[...], high[0]))

    @pl.when(pl.program_id(0) == 0)
    def _():
        first[...] = term

    @pl.when(pl.program_id(0) > 0)
    def _():
        rest[0] = term


def project(own, other, high, low, order):
    rows, depth = own.shape
    count, _, width = high.shape
    x_spec = pl.BlockSpec((rows, depth), lambda i, o: (0, 0))
    w_spec = pl.BlockSpec((1, 2 * depth, width), lambda i, o: (o[i], 0, 0))
    return pl.pallas_call(
        project_kernel,
        out_shape=[
            jax.ShapeDtypeStruct((rows, width), jnp.float32),
            jax.ShapeDtypeStruct((count - 1, rows, width), jnp.float32),
        ],
        grid_spec=pltpu.PrefetchScalarGridSpec(
            num_scalar_prefetch=1,
            grid=(count,),
            in_specs=[x_spec, x_spec, w_spec, w_spec],
            out_specs=[
                pl.BlockSpec((rows, width), lambda i, o: (0, 0)),
                pl.BlockSpec((1, rows, width), lambda i, o: (jnp.maximum(i - 1, 0), 0, 0)),
            ],
            scratch_shapes=[pltpu.VMEM((rows, 2 * depth), jnp.bfloat16)] * 2,
        ),
        compiler_params=pltpu.CompilerParams(vmem_limit_bytes=24 << 20),
        cost_estimate=SMALL,
    )(order, own, other, high, low)


def body(
    queries, key_rows, value_vectors, vertical_blocks, slash_offsets, prompt_length, out_weight
):
    rows = queries.shape[0]
    blocks = rows // BLOCK
    heads = queries.shape[1] // HEAD_SIZE
    seq_size = lax.axis_size("seq")
    seq_index = lax.axis_index("seq")
    head_index = lax.axis_index("head")
    vert = lax.dynamic_slice_in_dim(vertical_blocks, head_index * heads, heads, 0)
    slash = lax.dynamic_slice_in_dim(slash_offsets, head_index * heads, heads, 0)
    prompt = prompt_length[0]

    def shift(x, far):
        return lax.ppermute(x, "seq", [(i, i + far) for i in range(seq_size - far)])

    named = vert.reshape(-1)
    held = (named // blocks == seq_index).astype(jnp.int32)
    both, part = pick_blocks(named % blocks, held, key_rows, value_vectors)
    near = (shift(both, 2), shift(both, 1), both)
    part = part.reshape(seq_size, part.shape[0] // seq_size, part.shape[1])
    share = jnp.sum(lax.all_to_all(part, "seq", 0, 0), axis=0)
    copies = jnp.broadcast_to(share[None], part.shape)
    named_rows = lax.all_to_all(copies, "seq", 0, 0).reshape(-1, part.shape[2])

    head_size = lax.axis_size("head")
    swap = [(i, i ^ 1) for i in range(head_size)]
    core = (head_index % 2).reshape(1)
    width = out_weight.shape[1] // head_size
    other_weight = lax.ppermute(take_columns(out_weight, 1 - core, width), "head", swap)
    high, low = weight_halves(out_weight, other_weight, core, width)

    inside = jnp.arange(BLOCK, dtype=jnp.int32)
    vert_pos = vert[:, :, None] * BLOCK + inside
    vert_pos = jnp.where(vert_pos < prompt, -1, vert_pos).reshape(heads, 1, -1)
    offsets = jnp.concatenate([jnp.zeros((heads, 1), jnp.int32), slash + 1], axis=1)
    ids = seq_index * blocks + jnp.arange(blocks, dtype=jnp.int32)
    slash_block = ids[None, :, None] - offsets[:, None, :]
    repeated = jnp.any(slash_block[:, :, :, None] == vert[:, None, None, :], axis=-1)
    usable = (slash_block >= 0) & jnp.logical_not(repeated)
    slash_pos = slash_block[..., None] * BLOCK + inside
    slash_pos = jnp.where(slash_pos < prompt, -1, slash_pos)
    slash_pos = jnp.where(usable[..., None], slash_pos, FAR).reshape(heads, blocks, 1, -1)
    first_row = (seq_index * rows).reshape(1)
    back = 2 * blocks - offsets

    chips = head_size // 2
    chip = head_index // 2
    steps = jnp.arange(chips, dtype=jnp.int32)
    orders = ((chip + 2 * chips - 1 - steps) % chips, (chip + 1 + steps) % chips)
    rings = (
        [(i, (i + 2) % head_size) for i in range(head_size)],
        [(i, (i + head_size - 2) % head_size) for i in range(head_size)],
    )
    piece = rows // 4
    sums, terms = [], []
    q, high, low = lax.optimization_barrier((queries, high, low))
    for part in range(4):
        own = attend(
            q, part * piece, piece, first_row, back, near, named_rows, vert_pos, slash_pos
        )
        other = lax.ppermute(own, "head", swap)
        first, rest = project(own, other, high, low, orders[part % 2])
        sums.append(first)
        terms.append(rest)
        if part == 1:
            q, *sums = lax.optimization_barrier((q, *sums))
    for step in range(chips - 1):
        for part in range(4):
            moved = lax.ppermute(sums[part], "head", rings[part % 2])
            sums[part] = moved + terms[part][step]
    return jnp.concatenate(sums, axis=0)


def solution(mesh):
    placed = (P("seq", "head"), P("seq", "head"), P("seq", "head"), P(), P(), P(), P("head", None))
    return jax.shard_map(
        body, mesh=mesh, in_specs=placed, out_specs=P("seq", "head"), check_vma=False
    )
```

time: 385 us -> 244 us (0.63)
  waiting for transfers between devices: 233 us -> 85.3 us
  matrix products: 80.6 us -> 0 us
  Pallas kernels: 0 us -> 57.9 us
  blocking collectives: 0 us -> 35.9 us
  starting transfers between devices: 0.08 us -> 35.1 us
  other arithmetic: 24.4 us -> 3.25 us
  between operations: 14 us -> 0.96 us
  local copies, waits for them, and re-layouts: 32 us -> 21.8 us
    all_gather x2 -> x0, waiting for transfers between devices: 140 us -> none  [the longest x1 72.6 us: body(): lax.all_gather(key_rows, 'seq', axis=0, tiled=True)]
    reduce_scatter x1 -> x0, waiting for transfers between devices: 91.7 us -> none  [body(): lax.psum_scatter(partial_value, 'head', scatter_dimension=1, tiled=True)]
    ppermute x0 -> x19, waiting for transfers between devices: none -> 85.3 us  [the longest x2 48.4 us: shift(): return lax.ppermute(x, 'seq', [(i, i + far) for i in range(seq_size - far)])]
    dot_general x5 -> x0, matrix products: 80.6 us -> none  [the longest x1 29.4 us: body(): jnp.dot(attended, out_weight, precision=lax.Precision.HIGHEST, preferred_...]
    pallas_call x0 -> x11, Pallas kernels: none -> 57.9 us  [the longest x4 28.2 us: attend(): pl.pallas_call(kernel, grid=(rows // TILE, heads), out_shape=jax.ShapeDty...]
    all_to_all x0 -> x1, blocking collectives: none -> 35.9 us  [body(): share = jnp.sum(lax.all_to_all(part, 'seq', 0, 0), axis=0)]
    ppermute x0 -> x19, starting transfers between devices: none -> 30.1 us  [the longest x12 21.1 us: body(): moved = lax.ppermute(sums[part], 'head', rings[part % 2])]
    gather x4 -> x0, local copies, waits for them, and re-layouts: 21.8 us -> none  [the longest x2 15.1 us: body(): slash_pairs = near_rows[kv_of_head[:, None, None], near_index]]
  transfers between devices with their start and end apart: 3 -> 20, of which waited for: 3 -> 10; matrix products, arithmetic and copies ran while one was open for 2% -> 2% of each run, Pallas kernels for 0% -> 17%
where the time goes in v1:
time: 244 us; the launch traced here: 240 us
  waiting for transfers between devices  85.3 us (35%)
  Pallas kernels  57.9 us (24%)
  blocking collectives  35.9 us (15%)
  starting transfers between devices  35.1 us (14%)
  local copies, waits for them, and re-layouts  21.8 us (9%)
  other arithmetic  3.25 us (1%)
    ppermute x2, waiting for transfers between devices, shift(): return lax.ppermute(x, 'seq', [(i, i + far) for i in range(seq_size - far)])  48.4 us
    ppermute x12, waiting for transfers between devices, body(): moved = lax.ppermute(sums[part], 'head', rings[part % 2])  36.9 us
    all_to_all x1, blocking collectives, body(): share = jnp.sum(lax.all_to_all(part, 'seq', 0, 0), axis=0)  35.9 us
    pallas_call x4, Pallas kernels, attend(): pl.pallas_call(kernel, grid=(rows // TILE, heads), out_shape=jax.ShapeDty...  28.2 us
    pallas_call x4, Pallas kernels, project(): pl.pallas_call(project_kernel, out_shape=[jax.ShapeDtypeStruct((rows, wid...  22 us
    ppermute x12, starting transfers between devices, body(): moved = lax.ppermute(sums[part], 'head', rings[part % 2])  21.1 us
    unnamed x31, local copies, waits for them, and re-layouts  18.9 us
    ppermute x2, starting transfers between devices, shift(): return lax.ppermute(x, 'seq', [(i, i + far) for i in range(seq_size - far)])  8.36 us
  transfers between devices with their start and end apart: 20, of which 10 were waited for; matrix products, arithmetic and copies ran while one was open for 2% of the time, Pallas kernels for 17%

profile of v1, /device:TPU:2, one launch (start us, length us, event | category | flops | bytes accessed | tf_op | source)
XLA Modules:
  0.0 240.3 jit_solution(8235686660858475569)
XLA Ops:
  0.0 3.4 %copy-done.8 = f32[512,4096]{1,0:T(8,128)S(1)} copy-done((f32[512,4096]{1,0:T(8,128)S(1)}, f32[512,4096]{1,0:T(8,128)}, u32[]{:S(2)}) %copy-start.8) | copy-done | bytes 8388632
  3.4 2.9 %shard_map.73 = f32[512,2048]{1,0:T(8,128)} custom-call(s32[1]{0:T(128)S(6)} %sub.48.core, f32[512,4096]{1,0:T(8,128)S(1)} %copy-done.8), custom_call_target="tpu_custom_call" | custom-call | flops 1024 | bytes 1024 | tf_op jit(solution)/shard_map/pallas_call | solution.py:168
  6.6 1.0 copy-done.12
  7.6 1.0 copy-done.13
  8.7 1.2 shard_map.75
  9.8 35.9 %all_to_all.10 = f32[16,128,256]{2,1,0:T(8,128)S(1)} all-to-all(f32[16,128,256]{2,1,0:T(8,128)S(1)} %bitcast.35), channel_id=1, replica_groups=mesh['seq'=16,'head'=8] {'seq'}, dimensions={0} | all-to-all | bytes 4194304 | tf_op jit(solution)/shard_map/all_to_all | solution.py:277
  45.9 1.5 broadcast_in_dim.20
  47.4 5.0 %all-to-all-start.1 = ((f32[16,128,256]{2,1,0:T(8,128)}), f32[16,128,256]{2,1,0:T(8,128)S(1)}, u32[]{:S(2)}, u32[]{:S(2)}) async-start(f32[16,128,256]{2,1,0:T(8,128)} %broadcast_in_dim.20), calls=%async_computation.1 | async-start | bytes 4194304 | tf_op jit(solution)/shard_map/all_to_all | solution.py:279
  52.4 3.4 %collective-permute-start.2 = (f32[1024,256]{1,0:T(8,128)S(1)}, f32[1024,256]{1,0:T(8,128)}, u32[]{:S(2)}, u32[]{:S(2)}) collective-permute-start(f32[1024,256]{1,0:T(8,128)S(1)} %get-tuple-element.26.refs_3_), channel_id=1, source_target_pairs={{0,8},{8,16},{16,24},{24,32},{32,40},{40,48},{48,56},{56,64},{64,7... | collective-permute-start | bytes 3145736 | tf_op jit(solution)/shard_map/ppermute | solution.py:270
  55.8 5.0 %collective-permute-start.1 = (f32[1024,256]{1,0:T(8,128)S(1)}, f32[1024,256]{1,0:T(8,128)}, u32[]{:S(2)}, u32[]{:S(2)}) collective-permute-start(f32[1024,256]{1,0:T(8,128)S(1)} %get-tuple-element.26.refs_3_), channel_id=1, source_target_pairs={{0,16},{8,24},{16,32},{24,40},{32,48},{40,56},{48,64},{56,72},{64,... | collective-permute-start | bytes 3145736 | tf_op jit(solution)/shard_map/ppermute | solution.py:270
  63.3 3.4 %copy-done.9 = f32[512,4096]{1,0:T(8,128)S(1)} copy-done((f32[512,4096]{1,0:T(8,128)S(1)}, f32[512,4096]{1,0:T(8,128)}, u32[]{:S(2)}) %copy-start.9) | copy-done | bytes 8388632
  66.6 3.6 %shard_map.74 = (bf16[4,1024,512]{2,1,0:T(8,128)(2,1)S(1)}, bf16[4,1024,512]{2,1,0:T(8,128)(2,1)S(1)}) custom-call(s32[1]{0:T(128)} %bitcast.core, f32[512,4096]{1,0:T(8,128)S(1)} %copy-done.9, f32[512,2048]{1,0:T(8,128)} %collective-permute-done.other), custom_call_target="tpu_custom_call" | custom-call | flops 1024 | bytes 1024 | tf_op jit(solution)/shard_map/pallas_call | solution.py:193
  70.3 2.0 copy-done.2
  72.3 2.0 copy-done.5
  74.3 48.4 %collective-permute-done.2.refs_2_ = f32[1024,256]{1,0:T(8,128)} collective-permute-done((f32[1024,256]{1,0:T(8,128)S(1)}, f32[1024,256]{1,0:T(8,128)}, u32[]{:S(2)}, u32[]{:S(2)}) %collective-permute-start.2) | collective-permute-done | bytes 1048608 | tf_op jit(solution)/shard_map/ppermute | solution.py:270
  122.7 1.6 copy-done.10
  124.3 7.3 %shard_map.78.own = f32[256,512]{1,0:T(8,128)} custom-call(s32[1]{0:T(128)} %bitcast.1.first, s32[4,4]{1,0:T(4,128)S(1)} %get-tuple-element.46.back_ref, f32[1024,512]{1,0:T(8,128)S(1)} %copy-done.10, f32[1024,256]{1,0:T(8,128)} %collective-permute-done.1.refs_1_, f32[1024,256]{1,0:T(8,128)} %collective-permute-done.2.refs_2_, ...), custom_call_target="tpu_custom_call" | custom-call | flops 1024 | bytes 1024 | tf_op jit(solution)/shard_map/pallas_call | solution.py:143
  131.6 7.3 %shard_map.76.own = f32[256,512]{1,0:T(8,128)} custom-call(s32[1]{0:T(128)} %bitcast.1.first, s32[4,4]{1,0:T(4,128)S(1)} %get-tuple-element.46.back_ref, f32[1024,512]{1,0:T(8,128)S(1)} %copy-done.10, f32[1024,256]{1,0:T(8,128)} %collective-permute-done.1.refs_1_, f32[1024,256]{1,0:T(8,128)} %collective-permute-done.2.refs_2_, ...), custom_call_target="tpu_custom_call" | custom-call | flops 1024 | bytes 1024 | tf_op jit(solution)/shard_map/pallas_call | solution.py:143
  138.9 0.5 collective-permute-start.3
  139.4 2.2 copy-done.3
  141.6 2.2 copy-done.6
  143.8 6.1 %shard_map.79 = (f32[256,512]{1,0:T(8,128)S(1)}, f32[3,256,512]{2,1,0:T(8,128)S(1)}) custom-call(s32[4]{0:T(128)S(1)} %and_select_fusion.order, f32[256,512]{1,0:T(8,128)} %shard_map.78.own, f32[256,512]{1,0:T(8,128)} %collective-permute-done.4.other, bf16[4,1024,512]{2,1,0:T(8,128)(2,1)S(1)} %copy-done.3, bf16[4,1024,512]{2,1,0:T(8,128)(2,1)S(1)} %copy-done.6), custom_call_target="tpu_custom_call" | custom-call | flops 1024 | bytes 1024 | tf_op jit(solution)/shard_map/pallas_call | solution.py:235
  149.9 6.2 %shard_map.77 = (f32[256,512]{1,0:T(8,128)S(1)}, f32[3,256,512]{2,1,0:T(8,128)S(1)}) custom-call(s32[4]{0:T(128)S(1)} %and_select_fusion.3.order, f32[256,512]{1,0:T(8,128)} %shard_map.76.own, f32[256,512]{1,0:T(8,128)} %collective-permute-done.3.other, bf16[4,1024,512]{2,1,0:T(8,128)(2,1)S(1)} %copy-done.3, bf16[4,1024,512]{2,1,0:T(8,128)(2,1)S(1)} %copy-done.6), custom_call_target="tpu_custom_call" | custom-call | flops 1024 | bytes 1024 | tf_op jit(solution)/shard_map/pallas_call | solution.py:235
  156.1 1.6 collective-permute-start.5
  157.8 6.7 %shard_map.82.own = f32[256,512]{1,0:T(8,128)S(1)} custom-call(s32[1]{0:T(128)} %bitcast.1.first, s32[4,4]{1,0:T(4,128)S(1)} %get-tuple-element.46.back_ref, f32[1024,512]{1,0:T(8,128)S(1)} %copy-done.11, f32[1024,256]{1,0:T(8,128)} %collective-permute-done.1.refs_1_, f32[1024,256]{1,0:T(8,128)} %collective-permute-done.2.refs_2_, ...), custom_call_target="tpu_custom_call" | custom-call | flops 1024 | bytes 1024 | tf_op jit(solution)/shard_map/pallas_call | solution.py:143
  164.6 1.9 collective-permute-start.8
  166.5 6.9 %shard_map.80.own = f32[256,512]{1,0:T(8,128)S(1)} custom-call(s32[1]{0:T(128)} %bitcast.1.first, s32[4,4]{1,0:T(4,128)S(1)} %get-tuple-element.46.back_ref, f32[1024,512]{1,0:T(8,128)S(1)} %copy-done.11, f32[1024,256]{1,0:T(8,128)} %collective-permute-done.1.refs_1_, f32[1024,256]{1,0:T(8,128)} %collective-permute-done.2.refs_2_, ...), custom_call_target="tpu_custom_call" | custom-call | flops 1024 | bytes 1024 | tf_op jit(solution)/shard_map/pallas_call | solution.py:143
  173.6 0.4 collective-permute-start.6
  174.0 4.9 %shard_map.83 = (f32[256,512]{1,0:T(8,128)S(1)}, f32[3,256,512]{2,1,0:T(8,128)S(1)}) custom-call(s32[4]{0:T(128)S(1)} %and_select_fusion.order, f32[256,512]{1,0:T(8,128)S(1)} %shard_map.82.own, f32[256,512]{1,0:T(8,128)S(1)} %collective-permute-done.15.other, bf16[4,1024,512]{2,1,0:T(8,128)(2,1)S(1)} %copy-done.4, bf16[4,1024,512]{2,1,0:T(8,128)(2,1)S(1)} %copy-done.7), custom_call_target="tpu_custom_call" | custom-call | flops 1024 | bytes 1024 | tf_op jit(solution)/shard_map/pallas_call | solution.py:235
  178.9 2.9 %collective-permute-start.16 = (f32[256,512]{1,0:T(8,128)S(1)}, f32[256,512]{1,0:T(8,128)S(1)}, u32[]{:S(2)}, u32[]{:S(2)}) collective-permute-start(f32[256,512]{1,0:T(8,128)S(1)} %get-tuple-element.39), channel_id=1, source_target_pairs={{0,6},{1,7},{2,0},{3,1},{4,2},{5,3},{6,4},{7,5},{8,14},{9,15},{10,... | collective-permute-start | bytes 1572872 | tf_op jit(solution)/shard_map/ppermute | solution.py:325
  181.9 0.7 collective-permute-start.9
  182.6 4.9 %shard_map.81 = (f32[256,512]{1,0:T(8,128)S(1)}, f32[3,256,512]{2,1,0:T(8,128)S(1)}) custom-call(s32[4]{0:T(128)S(1)} %and_select_fusion.3.order, f32[256,512]{1,0:T(8,128)S(1)} %shard_map.80.own, f32[256,512]{1,0:T(8,128)S(1)} %collective-permute-done.11.other, bf16[4,1024,512]{2,1,0:T(8,128)(2,1)S(1)} %copy-done.4, bf16[4,1024,512]{2,1,0:T(8,128)(2,1)S(1)} %copy-done.7), custom_call_target="tpu_custom_call" | custom-call | flops 1024 | bytes 1024 | tf_op jit(solution)/shard_map/pallas_call | solution.py:235
  187.5 1.5 collective-permute-start.12
  189.0 0.2 collective-permute-done.6
  189.3 4.8 %collective-permute-done.16 = f32[256,512]{1,0:T(8,128)S(1)} collective-permute-done((f32[256,512]{1,0:T(8,128)S(1)}, f32[256,512]{1,0:T(8,128)S(1)}, u32[]{:S(2)}, u32[]{:S(2)}) %collective-permute-start.16) | collective-permute-done | bytes 524320 | tf_op jit(solution)/shard_map/ppermute | solution.py:325
  194.2 3.8 %collective-permute-start.17 = (f32[256,512]{1,0:T(8,128)S(1)}, f32[256,512]{1,0:T(8,128)S(1)}, u32[]{:S(2)}, u32[]{:S(2)}) collective-permute-start(f32[256,512]{1,0:T(8,128)S(1)} %bitcast_add_fusion.2), channel_id=1, source_target_pairs={{0,6},{1,7},{2,0},{3,1},{4,2},{5,3},{6,4},{7,5},{8,14},{9,15},{10,... | collective-permute-start | bytes 1572872 | tf_op jit(solution)/shard_map/ppermute | solution.py:325
  198.0 5.6 %collective-permute-done.12 = f32[256,512]{1,0:T(8,128)S(1)} collective-permute-done((f32[256,512]{1,0:T(8,128)S(1)}, f32[256,512]{1,0:T(8,128)S(1)}, u32[]{:S(2)}, u32[]{:S(2)}) %collective-permute-start.12) | collective-permute-done | bytes 524320 | tf_op jit(solution)/shard_map/ppermute | solution.py:325
  203.7 0.3 collective-permute-start.13
  204.0 1.4 collective-permute-done.9
  205.4 3.8 %collective-permute-start.10 = (f32[256,512]{1,0:T(8,128)S(1)}, f32[256,512]{1,0:T(8,128)S(1)}, u32[]{:S(2)}, u32[]{:S(2)}) collective-permute-start(f32[256,512]{1,0:T(8,128)S(1)} %bitcast_add_fusion.7), channel_id=1, source_target_pairs={{0,6},{1,7},{2,0},{3,1},{4,2},{5,3},{6,4},{7,5},{8,14},{9,15},{10,... | collective-permute-start | bytes 1572872 | tf_op jit(solution)/shard_map/ppermute | solution.py:325
  209.2 7.4 %collective-permute-done.17 = f32[256,512]{1,0:T(8,128)S(1)} collective-permute-done((f32[256,512]{1,0:T(8,128)S(1)}, f32[256,512]{1,0:T(8,128)S(1)}, u32[]{:S(2)}, u32[]{:S(2)}) %collective-permute-start.17) | collective-permute-done | bytes 524320 | tf_op jit(solution)/shard_map/ppermute | solution.py:325
  216.7 3.8 %collective-permute-start.18 = (f32[256,512]{1,0:T(8,128)S(1)}, f32[256,512]{1,0:T(8,128)S(1)}, u32[]{:S(2)}, u32[]{:S(2)}) collective-permute-start(f32[256,512]{1,0:T(8,128)S(1)} %bitcast_add_fusion.1), channel_id=1, source_target_pairs={{0,6},{1,7},{2,0},{3,1},{4,2},{5,3},{6,4},{7,5},{8,14},{9,15},{10,... | collective-permute-start | bytes 1572872 | tf_op jit(solution)/shard_map/ppermute | solution.py:325
  220.4 4.3 %collective-permute-done.13 = f32[256,512]{1,0:T(8,128)S(1)} collective-permute-done((f32[256,512]{1,0:T(8,128)S(1)}, f32[256,512]{1,0:T(8,128)S(1)}, u32[]{:S(2)}, u32[]{:S(2)}) %collective-permute-start.13) | collective-permute-done | bytes 524320 | tf_op jit(solution)/shard_map/ppermute | solution.py:325
  224.8 0.3 collective-permute-start.14
  225.2 2.7 %collective-permute-done.10 = f32[256,512]{1,0:T(8,128)S(1)} collective-permute-done((f32[256,512]{1,0:T(8,128)S(1)}, f32[256,512]{1,0:T(8,128)S(1)}, u32[]{:S(2)}, u32[]{:S(2)}) %collective-permute-start.10) | collective-permute-done | bytes 524320 | tf_op jit(solution)/shard_map/ppermute | solution.py:325
  227.9 10.4 %collective-permute-done.18 = f32[256,512]{1,0:T(8,128)S(1)} collective-permute-done((f32[256,512]{1,0:T(8,128)S(1)}, f32[256,512]{1,0:T(8,128)S(1)}, u32[]{:S(2)}, u32[]{:S(2)}) %collective-permute-start.18) | collective-permute-done | bytes 524320 | tf_op jit(solution)/shard_map/ppermute | solution.py:325
  238.4 0.2 collective-permute-done.14
  238.7 1.5 pad_maximum_fusion
  (79 shorter events, 3.5 us)
Async XLA Ops:
  0.0 60.8 %copy-start = (s32[32,3]{0,1:T(4,128)S(1)}, s32[32,3]{0,1:T(4,128)}, u32[]{:S(2)}) copy-start(s32[32,3]{0,1:T(4,128)} %param.11) | copy-start | bytes 1156
  0.0 3.4 %copy-start.8 = (f32[512,4096]{1,0:T(8,128)S(1)}, f32[512,4096]{1,0:T(8,128)}, u32[]{:S(2)}) copy-start(f32[512,4096]{1,0:T(8,128)} %own.1) | copy-start | bytes 25165828
  3.4 2.9 %copy-start.14 = (s32[32,8]{0,1:T(8,128)S(1)}, s32[32,8]{0,1:T(8,128)}, u32[]{:S(2)}) copy-start(s32[32,8]{0,1:T(8,128)} %param.10) | copy-start | bytes 3076
  6.3 56.9 %collective-permute-start = (f32[512,2048]{1,0:T(8,128)}, f32[512,2048]{1,0:T(8,128)}, u32[]{:S(2)}, u32[]{:S(2)}) collective-permute-start(f32[512,2048]{1,0:T(8,128)} %shard_map.73), channel_id=1, source_target_pairs={{0,1},{1,0},{2,3},{3,2},{4,5},{5,4},{6,7},{7,6},{8,9},{9,8},{10,11... | collective-permute-start | bytes 12582920 | tf_op jit(solution)/shard_map/ppermute | solution.py:285
  6.6 1.0 copy-start.12
  7.6 1.0 copy-start.13
  47.4 75.3 %all-to-all-start.1 = ((f32[16,128,256]{2,1,0:T(8,128)}), f32[16,128,256]{2,1,0:T(8,128)S(1)}, u32[]{:S(2)}, u32[]{:S(2)}) async-start(f32[16,128,256]{2,1,0:T(8,128)} %broadcast_in_dim.20), calls=%async_computation.1 | async-start | bytes 4194304 | tf_op jit(solution)/shard_map/all_to_all | solution.py:279
  52.4 70.3 %collective-permute-start.2 = (f32[1024,256]{1,0:T(8,128)S(1)}, f32[1024,256]{1,0:T(8,128)}, u32[]{:S(2)}, u32[]{:S(2)}) collective-permute-start(f32[1024,256]{1,0:T(8,128)S(1)} %get-tuple-element.26.refs_3_), channel_id=1, source_target_pairs={{0,8},{8,16},{16,24},{24,32},{32,40},{40,48},{48,56},{56,64},{64,7... | collective-permute-start | bytes 3145736 | tf_op jit(solution)/shard_map/ppermute | solution.py:270
  55.8 66.9 %collective-permute-start.1 = (f32[1024,256]{1,0:T(8,128)S(1)}, f32[1024,256]{1,0:T(8,128)}, u32[]{:S(2)}, u32[]{:S(2)}) collective-permute-start(f32[1024,256]{1,0:T(8,128)S(1)} %get-tuple-element.26.refs_3_), channel_id=1, source_target_pairs={{0,16},{8,24},{16,32},{24,40},{32,48},{40,56},{48,64},{56,72},{64,... | collective-permute-start | bytes 3145736 | tf_op jit(solution)/shard_map/ppermute | solution.py:270
  63.3 3.4 %copy-start.9 = (f32[512,4096]{1,0:T(8,128)S(1)}, f32[512,4096]{1,0:T(8,128)}, u32[]{:S(2)}) copy-start(f32[512,4096]{1,0:T(8,128)} %own.1) | copy-start | bytes 25165828
  70.3 2.0 copy-start.2
  72.3 2.0 copy-start.5
  122.7 1.6 copy-start.10
  131.6 7.9 %collective-permute-start.4 = (f32[256,512]{1,0:T(8,128)}, f32[256,512]{1,0:T(8,128)}, u32[]{:S(2)}, u32[]{:S(2)}) collective-permute-start(f32[256,512]{1,0:T(8,128)} %shard_map.78.own), channel_id=1, source_target_pairs={{0,1},{1,0},{2,3},{3,2},{4,5},{5,4},{6,7},{7,6},{8,9},{9,8},{10,11... | collective-permute-start | bytes 1572872 | tf_op jit(solution)/shard_map/ppermute | solution.py:317
  138.9 11.0 %collective-permute-start.3 = (f32[256,512]{1,0:T(8,128)}, f32[256,512]{1,0:T(8,128)}, u32[]{:S(2)}, u32[]{:S(2)}) collective-permute-start(f32[256,512]{1,0:T(8,128)} %shard_map.76.own), channel_id=1, source_target_pairs={{0,1},{1,0},{2,3},{3,2},{4,5},{5,4},{6,7},{7,6},{8,9},{9,8},{10,11... | collective-permute-start | bytes 1572872 | tf_op jit(solution)/shard_map/ppermute | solution.py:317
  139.4 2.2 copy-start.3
  141.6 2.2 copy-start.6
  149.9 7.8 %copy-start.11 = (f32[1024,512]{1,0:T(8,128)S(1)}, f32[1024,512]{1,0:T(8,128)}, u32[]{:S(2)}) copy-start(f32[1024,512]{1,0:T(8,128)} %refs_0_.3) | copy-start | bytes 6291460
  156.1 17.4 %collective-permute-start.5 = (f32[256,512]{1,0:T(8,128)S(1)}, f32[256,512]{1,0:T(8,128)S(1)}, u32[]{:S(2)}, u32[]{:S(2)}) collective-permute-start(f32[256,512]{1,0:T(8,128)S(1)} %get-tuple-element.32), channel_id=1, source_target_pairs={{0,2},{1,3},{2,4},{3,5},{4,6},{5,7},{6,0},{7,1},{8,10},{9,11},{10,... | collective-permute-start | bytes 1572872 | tf_op jit(solution)/shard_map/ppermute | solution.py:325
  164.5 9.5 %collective-permute-start.15 = (f32[256,512]{1,0:T(8,128)S(1)}, f32[256,512]{1,0:T(8,128)S(1)}, u32[]{:S(2)}, u32[]{:S(2)}) collective-permute-start(f32[256,512]{1,0:T(8,128)S(1)} %shard_map.82.own), channel_id=1, source_target_pairs={{0,1},{1,0},{2,3},{3,2},{4,5},{5,4},{6,7},{7,6},{8,9},{9,8},{10,11... | collective-permute-start | bytes 1572872 | tf_op jit(solution)/shard_map/ppermute | solution.py:317
  164.6 17.3 %collective-permute-start.8 = (f32[256,512]{1,0:T(8,128)S(1)}, f32[256,512]{1,0:T(8,128)S(1)}, u32[]{:S(2)}, u32[]{:S(2)}) collective-permute-start(f32[256,512]{1,0:T(8,128)S(1)} %get-tuple-element.34), channel_id=1, source_target_pairs={{0,6},{1,7},{2,0},{3,1},{4,2},{5,3},{6,4},{7,5},{8,14},{9,15},{10,... | collective-permute-start | bytes 1572872 | tf_op jit(solution)/shard_map/ppermute | solution.py:325
  166.5 7.5 %copy-start.4 = (bf16[4,1024,512]{2,1,0:T(8,128)(2,1)S(1)}, bf16[4,1024,512]{2,1,0:T(8,128)(2,1)}, u32[]{:S(2)}) copy-start(bf16[4,1024,512]{2,1,0:T(8,128)(2,1)} %copy-done.2) | copy-start | bytes 12582916
  166.5 7.5 %copy-start.7 = (bf16[4,1024,512]{2,1,0:T(8,128)(2,1)S(1)}, bf16[4,1024,512]{2,1,0:T(8,128)(2,1)}, u32[]{:S(2)}) copy-start(bf16[4,1024,512]{2,1,0:T(8,128)(2,1)} %copy-done.5) | copy-start | bytes 12582916
  173.4 9.2 %collective-permute-start.11 = (f32[256,512]{1,0:T(8,128)S(1)}, f32[256,512]{1,0:T(8,128)S(1)}, u32[]{:S(2)}, u32[]{:S(2)}) collective-permute-start(f32[256,512]{1,0:T(8,128)S(1)} %shard_map.80.own), channel_id=1, source_target_pairs={{0,1},{1,0},{2,3},{3,2},{4,5},{5,4},{6,7},{7,6},{8,9},{9,8},{10,11... | collective-permute-start | bytes 1572872 | tf_op jit(solution)/shard_map/ppermute | solution.py:317
  173.6 15.6 %collective-permute-start.6 = (f32[256,512]{1,0:T(8,128)S(1)}, f32[256,512]{1,0:T(8,128)S(1)}, u32[]{:S(2)}, u32[]{:S(2)}) collective-permute-start(f32[256,512]{1,0:T(8,128)S(1)} %bitcast_add_fusion.11), channel_id=1, source_target_pairs={{0,2},{1,3},{2,4},{3,5},{4,6},{5,7},{6,0},{7,1},{8,10},{9,11},{10,... | collective-permute-start | bytes 1572872 | tf_op jit(solution)/shard_map/ppermute | solution.py:325
  178.9 15.2 %collective-permute-start.16 = (f32[256,512]{1,0:T(8,128)S(1)}, f32[256,512]{1,0:T(8,128)S(1)}, u32[]{:S(2)}, u32[]{:S(2)}) collective-permute-start(f32[256,512]{1,0:T(8,128)S(1)} %get-tuple-element.39), channel_id=1, source_target_pairs={{0,6},{1,7},{2,0},{3,1},{4,2},{5,3},{6,4},{7,5},{8,14},{9,15},{10,... | collective-permute-start | bytes 1572872 | tf_op jit(solution)/shard_map/ppermute | solution.py:325
  181.9 23.4 %collective-permute-start.9 = (f32[256,512]{1,0:T(8,128)S(1)}, f32[256,512]{1,0:T(8,128)S(1)}, u32[]{:S(2)}, u32[]{:S(2)}) collective-permute-start(f32[256,512]{1,0:T(8,128)S(1)} %bitcast_add_fusion.8), channel_id=1, source_target_pairs={{0,6},{1,7},{2,0},{3,1},{4,2},{5,3},{6,4},{7,5},{8,14},{9,15},{10,... | collective-permute-start | bytes 1572872 | tf_op jit(solution)/shard_map/ppermute | solution.py:325
  187.5 16.1 %collective-permute-start.12 = (f32[256,512]{1,0:T(8,128)S(1)}, f32[256,512]{1,0:T(8,128)S(1)}, u32[]{:S(2)}, u32[]{:S(2)}) collective-permute-start(f32[256,512]{1,0:T(8,128)S(1)} %get-tuple-element.37), channel_id=1, source_target_pairs={{0,2},{1,3},{2,4},{3,5},{4,6},{5,7},{6,0},{7,1},{8,10},{9,11},{10,... | collective-permute-start | bytes 1572872 | tf_op jit(solution)/shard_map/ppermute | solution.py:325
  189.2 35.9 %collective-permute-start.7 = (f32[256,512]{1,0:T(8,128)S(1)}, f32[256,512]{1,0:T(8,128)S(1)}, u32[]{:S(2)}, u32[]{:S(2)}) collective-permute-start(f32[256,512]{1,0:T(8,128)S(1)} %bitcast_add_fusion.10), channel_id=1, source_target_pairs={{0,2},{1,3},{2,4},{3,5},{4,6},{5,7},{6,0},{7,1},{8,10},{9,11},{10,... | collective-permute-start | bytes 1572872 | tf_op jit(solution)/shard_map/ppermute | solution.py:325
  194.2 22.4 %collective-permute-start.17 = (f32[256,512]{1,0:T(8,128)S(1)}, f32[256,512]{1,0:T(8,128)S(1)}, u32[]{:S(2)}, u32[]{:S(2)}) collective-permute-start(f32[256,512]{1,0:T(8,128)S(1)} %bitcast_add_fusion.2), channel_id=1, source_target_pairs={{0,6},{1,7},{2,0},{3,1},{4,2},{5,3},{6,4},{7,5},{8,14},{9,15},{10,... | collective-permute-start | bytes 1572872 | tf_op jit(solution)/shard_map/ppermute | solution.py:325
  203.7 21.0 %collective-permute-start.13 = (f32[256,512]{1,0:T(8,128)S(1)}, f32[256,512]{1,0:T(8,128)S(1)}, u32[]{:S(2)}, u32[]{:S(2)}) collective-permute-start(f32[256,512]{1,0:T(8,128)S(1)} %bitcast_add_fusion.5), channel_id=1, source_target_pairs={{0,2},{1,3},{2,4},{3,5},{4,6},{5,7},{6,0},{7,1},{8,10},{9,11},{10,... | collective-permute-start | bytes 1572872 | tf_op jit(solution)/shard_map/ppermute | solution.py:325
  205.4 22.4 %collective-permute-start.10 = (f32[256,512]{1,0:T(8,128)S(1)}, f32[256,512]{1,0:T(8,128)S(1)}, u32[]{:S(2)}, u32[]{:S(2)}) collective-permute-start(f32[256,512]{1,0:T(8,128)S(1)} %bitcast_add_fusion.7), channel_id=1, source_target_pairs={{0,6},{1,7},{2,0},{3,1},{4,2},{5,3},{6,4},{7,5},{8,14},{9,15},{10,... | collective-permute-start | bytes 1572872 | tf_op jit(solution)/shard_map/ppermute | solution.py:325
  216.7 21.7 %collective-permute-start.18 = (f32[256,512]{1,0:T(8,128)S(1)}, f32[256,512]{1,0:T(8,128)S(1)}, u32[]{:S(2)}, u32[]{:S(2)}) collective-permute-start(f32[256,512]{1,0:T(8,128)S(1)} %bitcast_add_fusion.1), channel_id=1, source_target_pairs={{0,6},{1,7},{2,0},{3,1},{4,2},{5,3},{6,4},{7,5},{8,14},{9,15},{10,... | collective-permute-start | bytes 1572872 | tf_op jit(solution)/shard_map/ppermute | solution.py:325
  224.8 13.9 %collective-permute-start.14 = (f32[256,512]{1,0:T(8,128)S(1)}, f32[256,512]{1,0:T(8,128)S(1)}, u32[]{:S(2)}, u32[]{:S(2)}) collective-permute-start(f32[256,512]{1,0:T(8,128)S(1)} %bitcast_add_fusion.4), channel_id=1, source_target_pairs={{0,2},{1,3},{2,4},{3,5},{4,6},{5,7},{6,0},{7,1},{8,10},{9,11},{10,... | collective-permute-start | bytes 1572872 | tf_op jit(solution)/shard_map/ppermute | solution.py:325
  238.7 1.6 copy-start.1

commit v2 on v0

v2 whole, which is shorter than its diff:
```python
import functools
import math

import jax
import jax.numpy as jnp
from jax import lax
from jax.experimental import pallas as pl
from jax.experimental.pallas import tpu as pltpu
from jax.sharding import PartitionSpec as P

HEAD_SIZE = 128
BLOCK = 64
TILE = 256
FAR = 1 << 30
LOW = -1e30
SMALL = pl.CostEstimate(flops=1024, bytes_accessed=1024, transcendentals=0)


def pick_kernel(place, held, *refs):
    *pieces, first, second, rows = refs
    size = pieces[0].shape[0]
    for at, piece in enumerate(pieces):
        rows[at * size : (at + 1) * size, :] = piece[...]
    slots = first.shape[0] // BLOCK
    for slot in range(2 * slots):
        out = first if slot < slots else second
        target = pl.ds(slot % slots * BLOCK, BLOCK)

        @pl.when(held[slot] == 1)
        def _():
            start = pl.multiple_of(place[slot] * BLOCK, BLOCK)
            out[target, :] = rows[pl.ds(start, BLOCK), :]

        @pl.when(held[slot] == 0)
        def _():
            out[target, :] = jnp.zeros((BLOCK, HEAD_SIZE), jnp.float32)


def pick_blocks(place, held, pieces):
    half = place.shape[0] // 2 * BLOCK
    smem = pl.BlockSpec(memory_space=pltpu.SMEM)
    vmem = pl.BlockSpec(memory_space=pltpu.VMEM)
    out = jax.ShapeDtypeStruct((half, HEAD_SIZE), jnp.float32)
    size = pieces[0].shape[0]
    return pl.pallas_call(
        pick_kernel,
        out_shape=[out, out],
        in_specs=[smem, smem] + [vmem] * len(pieces),
        out_specs=[vmem] * 2,
        scratch_shapes=[pltpu.VMEM((len(pieces) * size, HEAD_SIZE), jnp.float32)],
        compiler_params=pltpu.CompilerParams(vmem_limit_bytes=16 << 20),
        cost_estimate=SMALL,
    )(place, held, *pieces)


def split(x):
    high = x.astype(jnp.bfloat16)
    return high, (x - high.astype(jnp.float32)).astype(jnp.bfloat16)


def fold(x):
    half = x.shape[0] // 2
    return x[:half] + x[half:]


def attend_kernel(
    start, first_row, back, wraps, q, k_far, k_far_wrap, k_left, k_left_wrap, k_own,
    v_far_a, v_far_b, v_left, v_own, k_a, k_b, v_a, v_b, vert_pos, slash_pos, out,
    near_k, near_v, vert_k, vert_v,
):
    turn = pl.program_id(0)
    scale = 1.0 / math.sqrt(HEAD_SIZE)

    def put(target, first, pieces):
        for piece in pieces:
            count = piece.shape[0]
            high, low = split(piece[...])
            target[first : first + count, 0:HEAD_SIZE] = high
            target[first : first + count, HEAD_SIZE:] = low
            first += count

    @pl.when((turn == 0) & (pl.program_id(1) == 0))
    def _():
        rows = k_own.shape[0]
        for at, (plain, wrapped) in enumerate(((k_far, k_far_wrap), (k_left, k_left_wrap))):

            @pl.when(wraps[at] == 0)
            def _():
                put(near_k, at * rows, (plain,))

            @pl.when(wraps[at] == 1)
            def _():
                put(near_k, at * rows, (wrapped,))

        put(near_k, 2 * rows, (k_own,))
        put(near_v, 0, (v_far_a, v_far_b, v_left, v_own))
        put(vert_k, 0, (k_a, k_b))
        put(vert_v, 0, (v_a, v_b))

    dot = functools.partial(lax.dot_general, preferred_element_type=jnp.float32)
    across = (((1,), (1,)), ((), ()))
    down = (((1,), (0,)), ((), ()))
    q_pos = first_row[0] + start + turn * TILE + lax.broadcasted_iota(jnp.int32, (TILE, 1), 0)
    local = start // BLOCK + turn * (TILE // BLOCK)
    per_block = TILE // BLOCK
    vert = vert_pos.shape[2]
    pair = q.shape[1] // HEAD_SIZE
    for part in range(pair):
        head = pl.program_id(1) * pair + part
        columns = slice(part * HEAD_SIZE, (part + 1) * HEAD_SIZE)
        high, low = split(q[:, columns] * scale)
        high, low = (jnp.concatenate([x, x], axis=1) for x in (high, low))
        rows = pl.ds(pl.multiple_of(head * vert, vert), vert)
        both = jnp.concatenate([high, low], axis=0)
        vert_scores = fold(dot(both, vert_k[rows, :], across))
        vert_scores = jnp.where(vert_pos[head] <= q_pos, vert_scores, LOW)

        slash_scores, near = [], []
        for j in range(per_block):
            spots = [
                pl.ds(pl.multiple_of((local + j + back[head, n]) * BLOCK, BLOCK), BLOCK)
                for n in range(4)
            ]
            near.append(spots)
            keys = jnp.concatenate([near_k[s, :] for s in spots], axis=0)
            mine = slice(j * BLOCK, (j + 1) * BLOCK)
            score = fold(dot(jnp.concatenate([high[mine], low[mine]], axis=0), keys, across))
            slash_scores.append(jnp.where(slash_pos[head, local + j] <= q_pos[mine], score, LOW))
        slash_scores = jnp.concatenate(slash_scores, axis=0)

        top = jnp.maximum(
            jnp.max(vert_scores, axis=1, keepdims=True),
            jnp.max(slash_scores, axis=1, keepdims=True),
        )
        vert_w = jnp.exp(vert_scores - top)
        slash_w = jnp.exp(slash_scores - top)
        total = jnp.sum(vert_w, axis=1, keepdims=True) + jnp.sum(slash_w, axis=1, keepdims=True)
        mixed = fold(dot(jnp.concatenate(split(vert_w), axis=0), vert_v[rows, :], down))
        slash_high, slash_low = split(slash_w)
        parts = []
        for j in range(per_block):
            values = jnp.concatenate([near_v[s, :] for s in near[j]], axis=0)
            mine = slice(j * BLOCK, (j + 1) * BLOCK)
            weights = jnp.concatenate([slash_high[mine], slash_low[mine]], axis=0)
            parts.append(fold(dot(weights, values, down)))
        mixed = mixed + jnp.concatenate(parts, axis=0)
        out[:, columns] = (mixed[:, :HEAD_SIZE] + mixed[:, HEAD_SIZE:]) / total


def attend(q, start, rows, first_row, back, wraps, arrays):
    heads = q.shape[1] // HEAD_SIZE
    pair = 2
    smem = pl.BlockSpec(memory_space=pltpu.SMEM)
    vmem = pl.BlockSpec(memory_space=pltpu.VMEM)
    near, vert = 3 * q.shape[0], heads * 8 * BLOCK
    base = start // TILE
    return pl.pallas_call(
        functools.partial(attend_kernel, start),
        grid=(rows // TILE, heads // pair),
        out_shape=jax.ShapeDtypeStruct((rows, heads * HEAD_SIZE), jnp.float32),
        in_specs=[smem, smem, smem]
        + [pl.BlockSpec((TILE, pair * HEAD_SIZE), lambda t, h: (base + t, h))]
        + [vmem] * len(arrays),
        out_specs=pl.BlockSpec((TILE, pair * HEAD_SIZE), lambda t, h: (t, h)),
        scratch_shapes=[
            pltpu.VMEM((n, 2 * HEAD_SIZE), jnp.bfloat16) for n in (near, near, vert, vert)
        ],
        compiler_params=pltpu.CompilerParams(vmem_limit_bytes=40 << 20),
        cost_estimate=SMALL,
    )(first_row, back, wraps, q, *arrays)


def project_kernel(order, own, other, w_own, w_other, first_a, rest_a, first_b, rest_b, x, w):
    rows, depth = own.shape
    half = first_a.shape[0]
    step = pl.program_id(0)

    @pl.when(step == 0)
    def _():
        for at, ref in ((0, own), (depth, other)):
            x[0:rows, at : at + depth], x[rows:, at : at + depth] = split(ref[...])

    for at, ref in ((0, w_own), (depth, w_other)):
        w[0, at : at + depth, :], w[1, at : at + depth, :] = split(ref[...])
    dot = functools.partial(jnp.dot, preferred_element_type=jnp.float32)
    term = fold(dot(x[...], w[0])) + dot(x[0:rows, :], w[1])

    @pl.when(step == 0)
    def _():
        first_a[...] = term[:half]

    @pl.when(step > 0)
    def _():
        rest_a[0] = term[:half]

    @pl.when(step == 2)
    def _():
        first_b[...] = term[half:]

    @pl.when(step != 2)
    def _():
        rest_b[0] = term[half:]


def project(own, other, part, rows, w_own, w_other, order):
    depth = own.shape[1]
    half = rows // 2
    count = order.shape[0]
    width = w_own.shape[1] // (2 * count)
    x_spec = pl.BlockSpec((rows, depth), lambda i, o: (part, 0))
    w_spec = pl.BlockSpec((depth, width), lambda i, o: (0, o[i]))
    first = jax.ShapeDtypeStruct((half, width), jnp.float32)
    rest = jax.ShapeDtypeStruct((count - 1, half, width), jnp.float32)
    first_spec = pl.BlockSpec((half, width), lambda i, o: (0, 0))
    back_step = lambda i: jnp.where(i == 0, 1, jnp.where(i == 3, 2, 0))
    return pl.pallas_call(
        project_kernel,
        out_shape=[first, rest, first, rest],
        grid_spec=pltpu.PrefetchScalarGridSpec(
            num_scalar_prefetch=1,
            grid=(count,),
            in_specs=[x_spec, x_spec, w_spec, w_spec],
            out_specs=[
                first_spec,
                pl.BlockSpec((1, half, width), lambda i, o: (jnp.maximum(i - 1, 0), 0, 0)),
                first_spec,
                pl.BlockSpec((1, half, width), lambda i, o: (back_step(i), 0, 0)),
            ],
            scratch_shapes=[
                pltpu.VMEM((2 * rows, 2 * depth), jnp.bfloat16),
                pltpu.VMEM((2, 2 * depth, width), jnp.bfloat16),
            ],
        ),
        compiler_params=pltpu.CompilerParams(vmem_limit_bytes=48 << 20),
        cost_estimate=SMALL,
    )(order, own, other, w_own, w_other)


def body(
    queries, key_rows, value_vectors, vertical_blocks, slash_offsets, prompt_length, out_weight
):
    rows = queries.shape[0]
    blocks = rows // BLOCK
    heads = queries.shape[1] // HEAD_SIZE
    seq_index = lax.axis_index("seq")
    head_index = lax.axis_index("head")
    head_size = lax.axis_size("head")
    core = head_index % 2
    chips = head_size // 2

    x, z = seq_index % 4, seq_index // 4
    ids = range(lax.axis_size("seq"))
    right = [(i, i // 4 * 4 + (i + 1) % 4) for i in ids]
    left = [(i, i // 4 * 4 + (i + 3) % 4) for i in ids]
    over = [(i, i // 4 * 4 + (i + 2) % 4) for i in ids]
    up = [(i, (i + 4) % 16) for i in ids]
    down = [(i, (i + 12) % 16) for i in ids]
    send = lambda a, pairs: lax.ppermute(a, "seq", pairs)
    swapped = lambda a, bits: send(a, [(i, i ^ bits) for i in ids])

    k_left = send(key_rows, right)
    k_right = send(key_rows, left)
    v_below = send(value_vectors, up)
    v_above = send(value_vectors, down)
    swap = [(i, i ^ 1) for i in range(head_size)]
    w_other = lax.ppermute(out_weight, "head", swap)

    vert = lax.dynamic_slice_in_dim(vertical_blocks, head_index * heads, heads, 0)
    slash = lax.dynamic_slice_in_dim(slash_offsets, head_index * heads, heads, 0)
    prompt = prompt_length[0]
    named = vert.reshape(-1)
    inside = jnp.arange(BLOCK, dtype=jnp.int32)
    vert_pos = vert[:, :, None] * BLOCK + inside
    vert_pos = jnp.where(vert_pos < prompt, -1, vert_pos).reshape(heads, 1, -1)
    offsets = jnp.concatenate([jnp.zeros((heads, 1), jnp.int32), slash + 1], axis=1)
    block_ids = seq_index * blocks + jnp.arange(blocks, dtype=jnp.int32)
    slash_block = block_ids[None, :, None] - offsets[:, None, :]
    repeated = jnp.any(slash_block[:, :, :, None] == vert[:, None, None, :], axis=-1)
    usable = (slash_block >= 0) & jnp.logical_not(repeated)
    slash_pos = slash_block[..., None] * BLOCK + inside
    slash_pos = jnp.where(slash_pos < prompt, -1, slash_pos)
    slash_pos = jnp.where(usable[..., None], slash_pos, FAR).reshape(heads, blocks, 1, -1)
    first_row = (seq_index * rows).reshape(1)
    back = 2 * blocks - offsets
    wraps = jnp.stack([x < 2, x == 0]).astype(jnp.int32)
    order = (head_index // 2 + 2 * chips - 1 - jnp.arange(chips, dtype=jnp.int32)) % chips
    order = 2 * order + core
    owner = named // blocks
    at = named % blocks
    k_place, k_held = (owner % 4 - x) % 4 * blocks + at, (owner // 4 == z).astype(jnp.int32)
    v_place, v_held = (owner // 4 - z) % 4 * blocks + at, (owner % 4 == x).astype(jnp.int32)
    small = (vert_pos, slash_pos, first_row, back, wraps, order, k_place, k_held, v_place, v_held)

    (k_left, k_right, v_below, v_above), small = lax.optimization_barrier(
        ((k_left, k_right, v_below, v_above), small)
    )
    vert_pos, slash_pos, first_row, back, wraps, order, k_place, k_held, v_place, v_held = small
    k_far = send(k_right, left)
    v_beyond = send(v_above, down)
    v_left = send(jnp.where(x == 3, v_below, value_vectors), right)
    source = jnp.where(x >= 2, v_below, value_vectors)
    half = rows // 2
    k_far, v_beyond, v_left = lax.optimization_barrier((k_far, v_beyond, v_left))
    v_far_a = send(source[:half], over)
    v_far_b = send(source[half:], left)
    k_left_wrap = send(k_left, [(i, i + 4) for i in ids if i % 4 == 0 and i + 4 in ids])

    k_named = pick_blocks(k_place, k_held, (key_rows, k_right, k_far, k_left))
    v_named = pick_blocks(v_place, v_held, (value_vectors, v_above, v_beyond, v_below))
    named = [*k_named, *v_named]
    one, two = (4, 12, 1, 3), (12, 4, 3, 1)
    named = [a + swapped(a, bits) for a, bits in zip(named, one)]
    v_far_a, v_far_b, k_left_wrap, *named = lax.optimization_barrier(
        (v_far_a, v_far_b, k_left_wrap, *named)
    )
    v_far_b = send(v_far_b, left)
    k_far_wrap = send(k_far, [(i, i + 4) for i in ids if i % 4 < 2 and i + 4 in ids])
    more = [swapped(a, bits) for a, bits in zip(named, two)]
    v_far_b, k_far_wrap, *more = lax.optimization_barrier((v_far_b, k_far_wrap, *more))
    named = [a + b for a, b in zip(named, more)]

    arrays = (k_far, k_far_wrap, k_left, k_left_wrap, key_rows, v_far_a, v_far_b, v_left)
    arrays = (*arrays, value_vectors, *named, vert_pos, slash_pos)

    rings = [[(i, (i + d) % head_size) for i in range(head_size)] for d in (2, head_size - 2)]
    q = queries
    pairs = []
    for start in (0, half):
        own = attend(q, start, half, first_row, back, wraps, arrays)
        q, own = lax.optimization_barrier((q, own))
        pairs.append((own, lax.ppermute(own, "head", swap)))
    sums, terms = [], []
    for which, part, count in ((0, 0, half // 2), (0, 1, half // 2), (1, 0, half)):
        own, other = pairs[which]
        first_a, rest_a, first_b, rest_b = project(
            own, other, part, count, out_weight, w_other, order
        )
        order, first_a, first_b = lax.optimization_barrier((order, first_a, first_b))
        sums.append([first_a, first_b])
        terms.append([rest_a, rest_b])
    for step in range(chips - 1):
        for part in range(len(sums)):
            for way in range(2):
                moved = lax.ppermute(sums[part][way], "head", rings[way])
                sums[part][way] = moved + terms[part][way][step]
    return jnp.concatenate(sums[0] + sums[1] + sums[2], axis=0)


def solution(mesh):
    placed = (P("seq", "head"), P("seq", "head"), P("seq", "head"), P(), P(), P(), P("head", None))
    return jax.shard_map(
        body, mesh=mesh, in_specs=placed, out_specs=P("seq", "head"), check_vma=False
    )
```

time: 385 us -> 210 us (0.55)
  waiting for transfers between devices: 233 us -> 99 us
  matrix products: 80.6 us -> 0 us
  starting transfers between devices: 0.08 us -> 50.8 us
  Pallas kernels: 0 us -> 46.3 us
  local copies, waits for them, and re-layouts: 32 us -> 4.2 us
  other arithmetic: 24.4 us -> 4.68 us
  between operations: 14 us -> 1.1 us
    all_gather x2 -> x0, waiting for transfers between devices: 140 us -> none  [the longest x1 72.6 us: body(): lax.all_gather(key_rows, 'seq', axis=0, tiled=True)]
    ppermute x0 -> x41, waiting for transfers between devices: none -> 99 us  [the longest x20 49.7 us: body(): send = lambda a, pairs: lax.ppermute(a, 'seq', pairs)]
    reduce_scatter x1 -> x0, waiting for transfers between devices: 91.7 us -> none  [body(): lax.psum_scatter(partial_value, 'head', scatter_dimension=1, tiled=True)]
    dot_general x5 -> x0, matrix products: 80.6 us -> none  [the longest x1 29.4 us: body(): jnp.dot(attended, out_weight, precision=lax.Precision.HIGHEST, preferred_...]
    ppermute x0 -> x41, starting transfers between devices: none -> 50.8 us  [the longest x20 29.7 us: body(): send = lambda a, pairs: lax.ppermute(a, 'seq', pairs)]
    pallas_call x0 -> x7, Pallas kernels: none -> 46.3 us  [the longest x3 25 us: project(): pl.pallas_call(project_kernel, out_shape=[first, rest, first, rest], grid...]
    gather x4 -> x0, local copies, waits for them, and re-layouts: 21.8 us -> none  [the longest x2 15.1 us: body(): slash_pairs = near_rows[kv_of_head[:, None, None], near_index]]
    transpose x2 -> x0, other arithmetic: 12.2 us -> none  [arrange(): return stacked.transpose(3, 1, 0, 2, 4)]
  transfers between devices with their start and end apart: 3 -> 41, of which waited for: 3 -> 25; matrix products, arithmetic and copies ran while one was open for 2% -> 3% of each run, Pallas kernels for 0% -> 22%
where the time goes in v2:
time: 210 us; the launch traced here: 206 us
  waiting for transfers between devices  99 us (47%)
  starting transfers between devices  50.8 us (24%)
  Pallas kernels  46.3 us (22%)
  other arithmetic  4.68 us (2%)
  local copies, waits for them, and re-layouts  4.2 us (2%)
    ppermute x20, waiting for transfers between devices, body(): send = lambda a, pairs: lax.ppermute(a, 'seq', pairs)  49.7 us
    ppermute x18, waiting for transfers between devices, body(): moved = lax.ppermute(sums[part][way], 'head', rings[way])  49.4 us
    ppermute x20, starting transfers between devices, body(): send = lambda a, pairs: lax.ppermute(a, 'seq', pairs)  29.7 us
    pallas_call x3, Pallas kernels, project(): pl.pallas_call(project_kernel, out_shape=[first, rest, first, rest], grid...  25 us
    ppermute x18, starting transfers between devices, body(): moved = lax.ppermute(sums[part][way], 'head', rings[way])  20.4 us
    pallas_call x2, Pallas kernels, attend(): pl.pallas_call(functools.partial(attend_kernel, start), grid=(rows // TIL...  19 us
  transfers between devices with their start and end apart: 41, of which 25 were waited for; matrix products, arithmetic and copies ran while one was open for 3% of the time, Pallas kernels for 22%

profile of v2, /device:TPU:2, one launch (start us, length us, event | category | flops | bytes accessed | tf_op | source)
XLA Modules:
  0.0 206.1 jit_solution(15462907123016049910)
XLA Ops:
  0.5 1.7 collective-permute-start
  2.1 4.0 %collective-permute-start.3 = (f32[1024,128]{1,0:T(8,128)}, f32[1024,128]{1,0:T(8,128)S(1)}, u32[]{:S(2)}, u32[]{:S(2)}) collective-permute-start(f32[1024,128]{1,0:T(8,128)} %v_own.3), channel_id=1, source_target_pairs={{0,96},{8,104},{16,112},{24,120},{32,0},{40,8},{48,16},{56,24},{64... | collective-permute-start | bytes 1572872 | tf_op jit(solution)/shard_map/ppermute | solution.py:258
  9.7 4.8 %collective-permute-done.1.refs_1_ = f32[1024,128]{1,0:T(8,128)S(1)} collective-permute-done((f32[1024,128]{1,0:T(8,128)}, f32[1024,128]{1,0:T(8,128)S(1)}, u32[]{:S(2)}, u32[]{:S(2)}) %collective-permute-start.1) | collective-permute-done | bytes 524320 | tf_op jit(solution)/shard_map/ppermute | solution.py:258
  14.6 1.3 collective-permute-done.refs_3_.k_left
  15.9 1.8 collective-permute-done.3.refs_1_
  17.7 3.3 %collective-permute-done.2.refs_3_ = f32[1024,128]{1,0:T(8,128)S(1)} collective-permute-done((f32[1024,128]{1,0:T(8,128)}, f32[1024,128]{1,0:T(8,128)S(1)}, u32[]{:S(2)}, u32[]{:S(2)}) %collective-permute-start.2) | collective-permute-done | bytes 524320 | tf_op jit(solution)/shard_map/ppermute | solution.py:258
  21.0 1.6 collective-permute-start.4
  24.5 9.0 %collective-permute-done.4.refs_2_.k_far = f32[1024,128]{1,0:T(8,128)S(1)} collective-permute-done((f32[1024,128]{1,0:T(8,128)S(1)}, f32[1024,128]{1,0:T(8,128)S(1)}, u32[]{:S(2)}, u32[]{:S(2)}) %collective-permute-start.4) | collective-permute-done | bytes 524320 | tf_op jit(solution)/shard_map/ppermute | solution.py:258
  33.5 1.6 collective-permute-done.5.refs_2_
  35.1 2.4 %collective-permute-done.6.v_left = f32[1024,128]{1,0:T(8,128)S(1)} collective-permute-done((f32[1024,128]{1,0:T(8,128)S(1)}, f32[1024,128]{1,0:T(8,128)S(1)}, u32[]{:S(2)}, u32[]{:S(2)}) %collective-permute-start.6) | collective-permute-done | bytes 524320 | tf_op jit(solution)/shard_map/ppermute | solution.py:258
  37.5 1.2 shard_map.73
  38.7 1.5 collective-permute-start.10
  40.3 1.2 shard_map.74
  41.5 3.0 %collective-permute-start.12 = (f32[1024,128]{1,0:T(8,128)S(1)}, f32[1024,128]{1,0:T(8,128)S(1)}, u32[]{:S(2)}, u32[]{:S(2)}) collective-permute-start(f32[1024,128]{1,0:T(8,128)S(1)} %get-tuple-element.78), channel_id=1, source_target_pairs={{0,8},{8,0},{16,24},{24,16},{32,40},{40,32},{48,56},{56,48},{64,72... | collective-permute-start | bytes 1572872 | tf_op jit(solution)/shard_map/ppermute | solution.py:258
  44.5 6.0 %collective-permute-done.10 = f32[1024,128]{1,0:T(8,128)S(1)} collective-permute-done((f32[1024,128]{1,0:T(8,128)S(1)}, f32[1024,128]{1,0:T(8,128)S(1)}, u32[]{:S(2)}, u32[]{:S(2)}) %collective-permute-start.10) | collective-permute-done | bytes 524320 | tf_op jit(solution)/shard_map/ppermute | solution.py:258
  51.2 1.3 collective-permute-done.11
  52.5 3.8 %collective-permute-start.8 = (f32[512,128]{1,0:T(8,128)S(1)}, f32[512,128]{1,0:T(8,128)S(1)}, u32[]{:S(2)}, u32[]{:S(2)}) collective-permute-start(f32[512,128]{1,0:T(8,128)S(1)} %get-tuple-element.129), channel_id=1, source_target_pairs={{0,24},{8,0},{16,8},{24,16},{32,56},{40,32},{48,40},{56,48},{64,88... | collective-permute-start | bytes 786440 | tf_op jit(solution)/shard_map/ppermute | solution.py:258
  56.3 3.2 %collective-permute-done.13 = f32[1024,128]{1,0:T(8,128)S(1)} collective-permute-done((f32[1024,128]{1,0:T(8,128)S(1)}, f32[1024,128]{1,0:T(8,128)S(1)}, u32[]{:S(2)}, u32[]{:S(2)}) %collective-permute-start.13) | collective-permute-done | bytes 524320 | tf_op jit(solution)/shard_map/ppermute | solution.py:258
  59.5 6.7 %collective-permute-start.15 = (f32[1024,128]{1,0:T(8,128)S(1)}, f32[1024,128]{1,0:T(8,128)S(1)}, u32[]{:S(2)}, u32[]{:S(2)}) collective-permute-start(f32[1024,128]{1,0:T(8,128)S(1)} %collective-permute-done.4.refs_2_.k_far), channel_id=1, source_target_pairs={{0,32},{8,40},{32,64},{40,72},{64,96},{72,104},{1,33},{9,41},{33,6... | collective-permute-start | bytes 1572872 | tf_op jit(solution)/shard_map/ppermute | solution.py:258
  66.5 1.6 collective-permute-done.8
  68.5 2.6 %collective-permute-start.16 = (f32[1024,128]{1,0:T(8,128)S(1)}, f32[1024,128]{1,0:T(8,128)S(1)}, u32[]{:S(2)}, u32[]{:S(2)}) collective-permute-start(f32[1024,128]{1,0:T(8,128)S(1)} %add.229), channel_id=1, source_target_pairs={{0,96},{8,104},{16,112},{24,120},{32,64},{40,72},{48,80},{56,88},{... | collective-permute-start | bytes 1572872 | tf_op jit(solution)/shard_map/ppermute | solution.py:258
  71.2 3.7 %collective-permute-done.15.k_far_wrap = f32[1024,128]{1,0:T(8,128)S(1)} collective-permute-done((f32[1024,128]{1,0:T(8,128)S(1)}, f32[1024,128]{1,0:T(8,128)S(1)}, u32[]{:S(2)}, u32[]{:S(2)}) %collective-permute-start.15) | collective-permute-done | bytes 524320 | tf_op jit(solution)/shard_map/ppermute | solution.py:258
  74.9 2.5 %collective-permute-done.14.v_far_b = f32[512,128]{1,0:T(8,128)S(1)} collective-permute-done((f32[512,128]{1,0:T(8,128)S(1)}, f32[512,128]{1,0:T(8,128)S(1)}, u32[]{:S(2)}, u32[]{:S(2)}) %collective-permute-start.14) | collective-permute-done | bytes 262176 | tf_op jit(solution)/shard_map/ppermute | solution.py:258
  77.4 2.3 %collective-permute-start.19 = (f32[1024,128]{1,0:T(8,128)S(1)}, f32[1024,128]{1,0:T(8,128)S(1)}, u32[]{:S(2)}, u32[]{:S(2)}) collective-permute-start(f32[1024,128]{1,0:T(8,128)S(1)} %add.232), channel_id=1, source_target_pairs={{0,8},{8,0},{16,24},{24,16},{32,40},{40,32},{48,56},{56,48},{64,72... | collective-permute-start | bytes 1572872 | tf_op jit(solution)/shard_map/ppermute | solution.py:258
  80.5 3.6 %collective-permute-done.18 = f32[1024,128]{1,0:T(8,128)S(1)} collective-permute-done((f32[1024,128]{1,0:T(8,128)S(1)}, f32[1024,128]{1,0:T(8,128)S(1)}, u32[]{:S(2)}, u32[]{:S(2)}) %collective-permute-start.18) | collective-permute-done | bytes 524320 | tf_op jit(solution)/shard_map/ppermute | solution.py:258
  84.1 2.8 %collective-permute-done.19 = f32[1024,128]{1,0:T(8,128)S(1)} collective-permute-done((f32[1024,128]{1,0:T(8,128)S(1)}, f32[1024,128]{1,0:T(8,128)S(1)}, u32[]{:S(2)}, u32[]{:S(2)}) %collective-permute-start.19) | collective-permute-done | bytes 524320 | tf_op jit(solution)/shard_map/ppermute | solution.py:258
  87.2 1.4 copy-done.1
  88.5 9.5 %shard_map.75.own = f32[512,512]{1,0:T(8,128)S(1)} custom-call(s32[1]{0:T(128)} %bitcast.1.first_row, s32[4,4]{1,0:T(4,128)S(1)} %get-tuple-element.64.back, s32[2]{0:T(128)S(1)} %add_convert_fusion.wraps, f32[1024,512]{1,0:T(8,128)S(1)} %copy-done.1, f32[1024,128]{1,0:T(8,128)S(1)} %collective-permute-done.4.refs_2_.k_far, ...), custom_call_target="tpu_custom_call" | custom-call | flops 1024 | bytes 1024 | tf_op jit(solution)/shard_map/pallas_call | solution.py:157
  98.1 9.5 %shard_map.78.own = f32[512,512]{1,0:T(8,128)S(1)} custom-call(s32[1]{0:T(128)} %bitcast.1.first_row, s32[4,4]{1,0:T(4,128)S(1)} %get-tuple-element.64.back, s32[2]{0:T(128)S(1)} %add_convert_fusion.wraps, f32[1024,512]{1,0:T(8,128)S(1)} %copy-done.1, f32[1024,128]{1,0:T(8,128)S(1)} %collective-permute-done.4.refs_2_.k_far, ...), custom_call_target="tpu_custom_call" | custom-call | flops 1024 | bytes 1024 | tf_op jit(solution)/shard_map/pallas_call | solution.py:157
  108.1 7.1 %shard_map.76 = (f32[128,512]{1,0:T(8,128)S(1)}, f32[3,128,512]{2,1,0:T(8,128)S(1)}, f32[128,512]{1,0:T(8,128)S(1)}, f32[3,128,512]{2,1,0:T(8,128)S(1)}) custom-call(s32[4]{0:T(128)S(1)} %fusion.8.order, f32[512,512]{1,0:T(8,128)S(1)} %shard_map.75.own, f32[512,512]{1,0:T(8,128)S(1)} %collective-permute-done.20.other, f32[512,4096]{1,0:T(8,128)} %w_own.5, ...), custom_call_target="tpu_custom_call" | custom-call | flops 1024 | bytes 1024 | tf_op jit(solution)/shard_map/pallas_call | solution.py:216
  115.2 7.1 %shard_map.77 = (f32[128,512]{1,0:T(8,128)S(1)}, f32[3,128,512]{2,1,0:T(8,128)S(1)}, f32[128,512]{1,0:T(8,128)S(1)}, f32[3,128,512]{2,1,0:T(8,128)S(1)}) custom-call(s32[4]{0:T(128)S(1)} %fusion.8.order, f32[512,512]{1,0:T(8,128)S(1)} %shard_map.75.own, f32[512,512]{1,0:T(8,128)S(1)} %collective-permute-done.20.other, f32[512,4096]{1,0:T(8,128)} %w_own.5, ...), custom_call_target="tpu_custom_call" | custom-call | flops 1024 | bytes 1024 | tf_op jit(solution)/shard_map/pallas_call | solution.py:216
  122.3 1.6 collective-permute-start.28
  124.0 1.7 collective-permute-start.31
  125.7 10.8 %shard_map.79 = (f32[256,512]{1,0:T(8,128)S(1)}, f32[3,256,512]{2,1,0:T(8,128)S(1)}, f32[256,512]{1,0:T(8,128)S(1)}, f32[3,256,512]{2,1,0:T(8,128)}) custom-call(s32[4]{0:T(128)S(1)} %fusion.8.order, f32[512,512]{1,0:T(8,128)S(1)} %shard_map.78.own, f32[512,512]{1,0:T(8,128)S(1)} %collective-permute-done.34.other, f32[512,4096]{1,0:T(8,128)} %w_own.5, ...), custom_call_target="tpu_custom_call" | custom-call | flops 1024 | bytes 1024 | tf_op jit(solution)/shard_map/pallas_call | solution.py:216
  136.8 2.9 %collective-permute-start.25 = (f32[128,512]{1,0:T(8,128)S(1)}, f32[128,512]{1,0:T(8,128)S(1)}, u32[]{:S(2)}, u32[]{:S(2)}) collective-permute-start(f32[128,512]{1,0:T(8,128)S(1)} %get-tuple-element.101), channel_id=1, source_target_pairs={{0,6},{1,7},{2,0},{3,1},{4,2},{5,3},{6,4},{7,5},{8,14},{9,15},{10,... | collective-permute-start | bytes 786440 | tf_op jit(solution)/shard_map/ppermute | solution.py:344
  139.7 3.2 %collective-permute-start.38 = (f32[256,512]{1,0:T(8,128)S(1)}, f32[256,512]{1,0:T(8,128)S(1)}, u32[]{:S(2)}, u32[]{:S(2)}) collective-permute-start(f32[256,512]{1,0:T(8,128)S(1)} %get-tuple-element.117), channel_id=1, source_target_pairs={{0,6},{1,7},{2,0},{3,1},{4,2},{5,3},{6,4},{7,5},{8,14},{9,15},{10,... | collective-permute-start | bytes 1572872 | tf_op jit(solution)/shard_map/ppermute | solution.py:344
  143.1 3.8 %collective-permute-done.22 = f32[128,512]{1,0:T(8,128)S(1)} collective-permute-done((f32[128,512]{1,0:T(8,128)S(1)}, f32[128,512]{1,0:T(8,128)S(1)}, u32[]{:S(2)}, u32[]{:S(2)}) %collective-permute-start.22) | collective-permute-done | bytes 262176 | tf_op jit(solution)/shard_map/ppermute | solution.py:344
  147.5 1.5 collective-permute-start.23
  149.1 14.7 %collective-permute-done.29 = f32[128,512]{1,0:T(8,128)S(1)} collective-permute-done((f32[128,512]{1,0:T(8,128)S(1)}, f32[128,512]{1,0:T(8,128)S(1)}, u32[]{:S(2)}, u32[]{:S(2)}) %collective-permute-start.29) | collective-permute-done | bytes 262176 | tf_op jit(solution)/shard_map/ppermute | solution.py:344
  164.4 1.5 collective-permute-start.30
  165.9 3.4 %collective-permute-done.23 = f32[128,512]{1,0:T(8,128)S(1)} collective-permute-done((f32[128,512]{1,0:T(8,128)S(1)}, f32[128,512]{1,0:T(8,128)S(1)}, u32[]{:S(2)}, u32[]{:S(2)}) %collective-permute-start.23) | collective-permute-done | bytes 262176 | tf_op jit(solution)/shard_map/ppermute | solution.py:344
  171.5 2.6 %collective-permute-start.27 = (f32[128,512]{1,0:T(8,128)S(1)}, f32[128,512]{1,0:T(8,128)S(1)}, u32[]{:S(2)}, u32[]{:S(2)}) collective-permute-start(f32[128,512]{1,0:T(8,128)S(1)} %bitcast_add_fusion.13), channel_id=1, source_target_pairs={{0,6},{1,7},{2,0},{3,1},{4,2},{5,3},{6,4},{7,5},{8,14},{9,15},{10,... | collective-permute-start | bytes 786440 | tf_op jit(solution)/shard_map/ppermute | solution.py:344
  174.4 6.8 %collective-permute-done.24 = f32[128,512]{1,0:T(8,128)S(1)} collective-permute-done((f32[128,512]{1,0:T(8,128)S(1)}, f32[128,512]{1,0:T(8,128)S(1)}, u32[]{:S(2)}, u32[]{:S(2)}) %collective-permute-start.24) | collective-permute-done | bytes 262176 | tf_op jit(solution)/shard_map/ppermute | solution.py:344
  182.7 7.8 %collective-permute-done.36 = f32[256,512]{1,0:T(8,128)S(1)} collective-permute-done((f32[256,512]{1,0:T(8,128)S(1)}, f32[256,512]{1,0:T(8,128)S(1)}, u32[]{:S(2)}, u32[]{:S(2)}) %collective-permute-start.36) | collective-permute-done | bytes 524320 | tf_op jit(solution)/shard_map/ppermute | solution.py:344
  190.6 2.5 %collective-permute-done.39 = f32[256,512]{1,0:T(8,128)S(1)} collective-permute-done((f32[256,512]{1,0:T(8,128)S(1)}, f32[256,512]{1,0:T(8,128)S(1)}, u32[]{:S(2)}, u32[]{:S(2)}) %collective-permute-start.39) | collective-permute-done | bytes 524320 | tf_op jit(solution)/shard_map/ppermute | solution.py:344
  193.2 1.3 collective-permute-start.40
  194.6 9.2 %collective-permute-done.37 = f32[256,512]{1,0:T(8,128)S(1)} collective-permute-done((f32[256,512]{1,0:T(8,128)S(1)}, f32[256,512]{1,0:T(8,128)S(1)}, u32[]{:S(2)}, u32[]{:S(2)}) %collective-permute-start.37) | collective-permute-done | bytes 524320 | tf_op jit(solution)/shard_map/ppermute | solution.py:344
  203.9 1.3 copy-done.5
  (112 shorter events, 15.5 us)
Async XLA Ops:
  0.0 6.8 %copy-start = (s32[32,3]{0,1:T(4,128)S(1)}, s32[32,3]{0,1:T(4,128)}, u32[]{:S(2)}) copy-start(s32[32,3]{0,1:T(4,128)} %param.11) | copy-start | bytes 1156
  0.0 37.5 %copy-start.3 = (f32[1024,128]{1,0:T(8,128)S(1)}, f32[1024,128]{1,0:T(8,128)}, u32[]{:S(2)}) copy-start(f32[1024,128]{1,0:T(8,128)} %k_own.3) | copy-start | bytes 1572868
  0.0 108.1 %collective-permute-start.21 = (f32[512,4096]{1,0:T(8,128)}, f32[512,4096]{1,0:T(8,128)}, u32[]{:S(2)}, u32[]{:S(2)}) collective-permute-start(f32[512,4096]{1,0:T(8,128)} %w_own.5), channel_id=1, source_target_pairs={{0,1},{1,0},{2,3},{3,2},{4,5},{5,4},{6,7},{7,6},{8,9},{9,8},{10,11... | collective-permute-start | bytes 25165832 | tf_op jit(solution)/shard_map/ppermute | solution.py:266
  0.0 14.6 %collective-permute-start.1 = (f32[1024,128]{1,0:T(8,128)}, f32[1024,128]{1,0:T(8,128)S(1)}, u32[]{:S(2)}, u32[]{:S(2)}) collective-permute-start(f32[1024,128]{1,0:T(8,128)} %k_own.3), channel_id=1, source_target_pairs={{0,24},{8,0},{16,8},{24,16},{32,56},{40,32},{48,40},{56,48},{64,88... | collective-permute-start | bytes 1572872 | tf_op jit(solution)/shard_map/ppermute | solution.py:258
  0.5 15.4 %collective-permute-start = (f32[1024,128]{1,0:T(8,128)}, f32[1024,128]{1,0:T(8,128)S(1)}, u32[]{:S(2)}, u32[]{:S(2)}) collective-permute-start(f32[1024,128]{1,0:T(8,128)} %k_own.3), channel_id=1, source_target_pairs={{0,8},{8,16},{16,24},{24,0},{32,40},{40,48},{48,56},{56,32},{64,72... | collective-permute-start | bytes 1572872 | tf_op jit(solution)/shard_map/ppermute | solution.py:258
  2.1 15.6 %collective-permute-start.3 = (f32[1024,128]{1,0:T(8,128)}, f32[1024,128]{1,0:T(8,128)S(1)}, u32[]{:S(2)}, u32[]{:S(2)}) collective-permute-start(f32[1024,128]{1,0:T(8,128)} %v_own.3), channel_id=1, source_target_pairs={{0,96},{8,104},{16,112},{24,120},{32,0},{40,8},{48,16},{56,24},{64... | collective-permute-start | bytes 1572872 | tf_op jit(solution)/shard_map/ppermute | solution.py:258
  6.2 14.9 %collective-permute-start.2 = (f32[1024,128]{1,0:T(8,128)}, f32[1024,128]{1,0:T(8,128)S(1)}, u32[]{:S(2)}, u32[]{:S(2)}) collective-permute-start(f32[1024,128]{1,0:T(8,128)} %v_own.3), channel_id=1, source_target_pairs={{0,32},{8,40},{16,48},{24,56},{32,64},{40,72},{48,80},{56,88},{64,... | collective-permute-start | bytes 1572872 | tf_op jit(solution)/shard_map/ppermute | solution.py:258
  21.0 19.3 %copy-start.2 = (f32[1024,128]{1,0:T(8,128)S(1)}, f32[1024,128]{1,0:T(8,128)}, u32[]{:S(2)}) copy-start(f32[1024,128]{1,0:T(8,128)} %v_own.3) | copy-start | bytes 1572868
  21.0 12.5 %collective-permute-start.4 = (f32[1024,128]{1,0:T(8,128)S(1)}, f32[1024,128]{1,0:T(8,128)S(1)}, u32[]{:S(2)}, u32[]{:S(2)}) collective-permute-start(f32[1024,128]{1,0:T(8,128)S(1)} %collective-permute-done.1.refs_1_), channel_id=1, source_target_pairs={{0,24},{8,0},{16,8},{24,16},{32,56},{40,32},{48,40},{56,48},{64,88... | collective-permute-start | bytes 1572872 | tf_op jit(solution)/shard_map/ppermute | solution.py:258
  22.6 12.6 %collective-permute-start.5 = (f32[1024,128]{1,0:T(8,128)S(1)}, f32[1024,128]{1,0:T(8,128)S(1)}, u32[]{:S(2)}, u32[]{:S(2)}) collective-permute-start(f32[1024,128]{1,0:T(8,128)S(1)} %collective-permute-done.3.refs_1_), channel_id=1, source_target_pairs={{0,96},{8,104},{16,112},{24,120},{32,0},{40,8},{48,16},{56,24},{64... | collective-permute-start | bytes 1572872 | tf_op jit(solution)/shard_map/ppermute | solution.py:258
  24.0 13.5 %collective-permute-start.6 = (f32[1024,128]{1,0:T(8,128)S(1)}, f32[1024,128]{1,0:T(8,128)S(1)}, u32[]{:S(2)}, u32[]{:S(2)}) collective-permute-start(f32[1024,128]{1,0:T(8,128)S(1)} %get-tuple-element.128), channel_id=1, source_target_pairs={{0,8},{8,16},{16,24},{24,0},{32,40},{40,48},{48,56},{56,32},{64,72... | collective-permute-start | bytes 1572872 | tf_op jit(solution)/shard_map/ppermute | solution.py:258
  38.7 11.7 %collective-permute-start.10 = (f32[1024,128]{1,0:T(8,128)S(1)}, f32[1024,128]{1,0:T(8,128)S(1)}, u32[]{:S(2)}, u32[]{:S(2)}) collective-permute-start(f32[1024,128]{1,0:T(8,128)S(1)} %get-tuple-element.73), channel_id=1, source_target_pairs={{0,32},{8,40},{16,48},{24,56},{32,0},{40,8},{48,16},{56,24},{64,96... | collective-permute-start | bytes 1572872 | tf_op jit(solution)/shard_map/ppermute | solution.py:258
  40.2 12.3 %collective-permute-start.11 = (f32[1024,128]{1,0:T(8,128)S(1)}, f32[1024,128]{1,0:T(8,128)S(1)}, u32[]{:S(2)}, u32[]{:S(2)}) collective-permute-start(f32[1024,128]{1,0:T(8,128)S(1)} %get-tuple-element.74), channel_id=1, source_target_pairs={{0,96},{8,104},{16,112},{24,120},{32,64},{40,72},{48,80},{56,88},{... | collective-permute-start | bytes 1572872 | tf_op jit(solution)/shard_map/ppermute | solution.py:258
  41.5 14.8 %collective-permute-start.12 = (f32[1024,128]{1,0:T(8,128)S(1)}, f32[1024,128]{1,0:T(8,128)S(1)}, u32[]{:S(2)}, u32[]{:S(2)}) collective-permute-start(f32[1024,128]{1,0:T(8,128)S(1)} %get-tuple-element.78), channel_id=1, source_target_pairs={{0,8},{8,0},{16,24},{24,16},{32,40},{40,32},{48,56},{56,48},{64,72... | collective-permute-start | bytes 1572872 | tf_op jit(solution)/shard_map/ppermute | solution.py:258
  44.5 15.0 %collective-permute-start.13 = (f32[1024,128]{1,0:T(8,128)S(1)}, f32[1024,128]{1,0:T(8,128)S(1)}, u32[]{:S(2)}, u32[]{:S(2)}) collective-permute-start(f32[1024,128]{1,0:T(8,128)S(1)} %get-tuple-element.79), channel_id=1, source_target_pairs={{0,24},{8,16},{16,8},{24,0},{32,56},{40,48},{48,40},{56,32},{64,88... | collective-permute-start | bytes 1572872 | tf_op jit(solution)/shard_map/ppermute | solution.py:258
  50.4 17.7 %collective-permute-start.9 = (f32[1024,128]{1,0:T(8,128)S(1)}, f32[1024,128]{1,0:T(8,128)S(1)}, u32[]{:S(2)}, u32[]{:S(2)}) collective-permute-start(f32[1024,128]{1,0:T(8,128)S(1)} %collective-permute-done.refs_3_.k_left), channel_id=1, source_target_pairs={{0,32},{32,64},{64,96},{1,33},{33,65},{65,97},{2,34},{34,66},{66,9... | collective-permute-start | bytes 1572872 | tf_op jit(solution)/shard_map/ppermute | solution.py:258
  52.5 15.7 %collective-permute-start.8 = (f32[512,128]{1,0:T(8,128)S(1)}, f32[512,128]{1,0:T(8,128)S(1)}, u32[]{:S(2)}, u32[]{:S(2)}) collective-permute-start(f32[512,128]{1,0:T(8,128)S(1)} %get-tuple-element.129), channel_id=1, source_target_pairs={{0,24},{8,0},{16,8},{24,16},{32,56},{40,32},{48,40},{56,48},{64,88... | collective-permute-start | bytes 786440 | tf_op jit(solution)/shard_map/ppermute | solution.py:258
  56.3 11.9 %collective-permute-start.7 = (f32[512,128]{1,0:T(8,128)S(1)}, f32[512,128]{1,0:T(8,128)S(1)}, u32[]{:S(2)}, u32[]{:S(2)}) collective-permute-start(f32[512,128]{1,0:T(8,128)S(1)} %get-tuple-element.130), channel_id=1, source_target_pairs={{0,16},{8,24},{16,0},{24,8},{32,48},{40,56},{48,32},{56,40},{64,80... | collective-permute-start | bytes 786440 | tf_op jit(solution)/shard_map/ppermute | solution.py:258
  59.5 15.4 %collective-permute-start.15 = (f32[1024,128]{1,0:T(8,128)S(1)}, f32[1024,128]{1,0:T(8,128)S(1)}, u32[]{:S(2)}, u32[]{:S(2)}) collective-permute-start(f32[1024,128]{1,0:T(8,128)S(1)} %collective-permute-done.4.refs_2_.k_far), channel_id=1, source_target_pairs={{0,32},{8,40},{32,64},{40,72},{64,96},{72,104},{1,33},{9,41},{33,6... | collective-permute-start | bytes 1572872 | tf_op jit(solution)/shard_map/ppermute | solution.py:258
  68.1 9.2 %collective-permute-start.14 = (f32[512,128]{1,0:T(8,128)S(1)}, f32[512,128]{1,0:T(8,128)S(1)}, u32[]{:S(2)}, u32[]{:S(2)}) collective-permute-start(f32[512,128]{1,0:T(8,128)S(1)} %collective-permute-done.8), channel_id=1, source_target_pairs={{0,24},{8,0},{16,8},{24,16},{32,56},{40,32},{48,40},{56,48},{64,88... | collective-permute-start | bytes 786440 | tf_op jit(solution)/shard_map/ppermute | solution.py:258
  68.5 11.2 %collective-permute-start.16 = (f32[1024,128]{1,0:T(8,128)S(1)}, f32[1024,128]{1,0:T(8,128)S(1)}, u32[]{:S(2)}, u32[]{:S(2)}) collective-permute-start(f32[1024,128]{1,0:T(8,128)S(1)} %add.229), channel_id=1, source_target_pairs={{0,96},{8,104},{16,112},{24,120},{32,64},{40,72},{48,80},{56,88},{... | collective-permute-start | bytes 1572872 | tf_op jit(solution)/shard_map/ppermute | solution.py:258
  71.1 9.5 %collective-permute-start.17 = (f32[1024,128]{1,0:T(8,128)S(1)}, f32[1024,128]{1,0:T(8,128)S(1)}, u32[]{:S(2)}, u32[]{:S(2)}) collective-permute-start(f32[1024,128]{1,0:T(8,128)S(1)} %add.230), channel_id=1, source_target_pairs={{0,32},{8,40},{16,48},{24,56},{32,0},{40,8},{48,16},{56,24},{64,96... | collective-permute-start | bytes 1572872 | tf_op jit(solution)/shard_map/ppermute | solution.py:258
  74.9 9.2 %collective-permute-start.18 = (f32[1024,128]{1,0:T(8,128)S(1)}, f32[1024,128]{1,0:T(8,128)S(1)}, u32[]{:S(2)}, u32[]{:S(2)}) collective-permute-start(f32[1024,128]{1,0:T(8,128)S(1)} %add.231), channel_id=1, source_target_pairs={{0,24},{8,16},{16,8},{24,0},{32,56},{40,48},{48,40},{56,32},{64,88... | collective-permute-start | bytes 1572872 | tf_op jit(solution)/shard_map/ppermute | solution.py:258
  77.4 9.5 %collective-permute-start.19 = (f32[1024,128]{1,0:T(8,128)S(1)}, f32[1024,128]{1,0:T(8,128)S(1)}, u32[]{:S(2)}, u32[]{:S(2)}) collective-permute-start(f32[1024,128]{1,0:T(8,128)S(1)} %add.232), channel_id=1, source_target_pairs={{0,8},{8,0},{16,24},{24,16},{32,40},{40,32},{48,56},{56,48},{64,72... | collective-permute-start | bytes 1572872 | tf_op jit(solution)/shard_map/ppermute | solution.py:258
  86.9 1.6 copy-start.1
  98.0 10.2 %collective-permute-start.20 = (f32[512,512]{1,0:T(8,128)S(1)}, f32[512,512]{1,0:T(8,128)S(1)}, u32[]{:S(2)}, u32[]{:S(2)}) collective-permute-start(f32[512,512]{1,0:T(8,128)S(1)} %shard_map.75.own), channel_id=1, source_target_pairs={{0,1},{1,0},{2,3},{3,2},{4,5},{5,4},{6,7},{7,6},{8,9},{9,8},{10,11... | collective-permute-start | bytes 3145736 | tf_op jit(solution)/shard_map/ppermute | solution.py:331
  107.6 18.0 %collective-permute-start.34 = (f32[512,512]{1,0:T(8,128)S(1)}, f32[512,512]{1,0:T(8,128)S(1)}, u32[]{:S(2)}, u32[]{:S(2)}) collective-permute-start(f32[512,512]{1,0:T(8,128)S(1)} %shard_map.78.own), channel_id=1, source_target_pairs={{0,1},{1,0},{2,3},{3,2},{4,5},{5,4},{6,7},{7,6},{8,9},{9,8},{10,11... | collective-permute-start | bytes 3145736 | tf_op jit(solution)/shard_map/ppermute | solution.py:331
  122.3 17.3 %collective-permute-start.28 = (f32[128,512]{1,0:T(8,128)S(1)}, f32[128,512]{1,0:T(8,128)S(1)}, u32[]{:S(2)}, u32[]{:S(2)}) collective-permute-start(f32[128,512]{1,0:T(8,128)S(1)} %get-tuple-element.106), channel_id=1, source_target_pairs={{0,2},{1,3},{2,4},{3,5},{4,6},{5,7},{6,0},{7,1},{8,10},{9,11},{10,... | collective-permute-start | bytes 786440 | tf_op jit(solution)/shard_map/ppermute | solution.py:344
  124.0 19.0 %collective-permute-start.31 = (f32[128,512]{1,0:T(8,128)S(1)}, f32[128,512]{1,0:T(8,128)S(1)}, u32[]{:S(2)}, u32[]{:S(2)}) collective-permute-start(f32[128,512]{1,0:T(8,128)S(1)} %get-tuple-element.108), channel_id=1, source_target_pairs={{0,6},{1,7},{2,0},{3,1},{4,2},{5,3},{6,4},{7,5},{8,14},{9,15},{10,... | collective-permute-start | bytes 786440 | tf_op jit(solution)/shard_map/ppermute | solution.py:344
  136.4 10.4 %collective-permute-start.22 = (f32[128,512]{1,0:T(8,128)S(1)}, f32[128,512]{1,0:T(8,128)S(1)}, u32[]{:S(2)}, u32[]{:S(2)}) collective-permute-start(f32[128,512]{1,0:T(8,128)S(1)} %get-tuple-element.99), channel_id=1, source_target_pairs={{0,2},{1,3},{2,4},{3,5},{4,6},{5,7},{6,0},{7,1},{8,10},{9,11},{10,... | collective-permute-start | bytes 786440 | tf_op jit(solution)/shard_map/ppermute | solution.py:344
  136.8 10.7 %collective-permute-start.25 = (f32[128,512]{1,0:T(8,128)S(1)}, f32[128,512]{1,0:T(8,128)S(1)}, u32[]{:S(2)}, u32[]{:S(2)}) collective-permute-start(f32[128,512]{1,0:T(8,128)S(1)} %get-tuple-element.101), channel_id=1, source_target_pairs={{0,6},{1,7},{2,0},{3,1},{4,2},{5,3},{6,4},{7,5},{8,14},{9,15},{10,... | collective-permute-start | bytes 786440 | tf_op jit(solution)/shard_map/ppermute | solution.py:344
  139.7 31.8 %collective-permute-start.35 = (f32[256,512]{1,0:T(8,128)S(1)}, f32[256,512]{1,0:T(8,128)S(1)}, u32[]{:S(2)}, u32[]{:S(2)}) collective-permute-start(f32[256,512]{1,0:T(8,128)S(1)} %get-tuple-element.115), channel_id=1, source_target_pairs={{0,2},{1,3},{2,4},{3,5},{4,6},{5,7},{6,0},{7,1},{8,10},{9,11},{10,... | collective-permute-start | bytes 1572872 | tf_op jit(solution)/shard_map/ppermute | solution.py:344
  139.7 34.5 %collective-permute-start.38 = (f32[256,512]{1,0:T(8,128)S(1)}, f32[256,512]{1,0:T(8,128)S(1)}, u32[]{:S(2)}, u32[]{:S(2)}) collective-permute-start(f32[256,512]{1,0:T(8,128)S(1)} %get-tuple-element.117), channel_id=1, source_target_pairs={{0,6},{1,7},{2,0},{3,1},{4,2},{5,3},{6,4},{7,5},{8,14},{9,15},{10,... | collective-permute-start | bytes 1572872 | tf_op jit(solution)/shard_map/ppermute | solution.py:344
  143.0 20.8 %collective-permute-start.29 = (f32[128,512]{1,0:T(8,128)S(1)}, f32[128,512]{1,0:T(8,128)S(1)}, u32[]{:S(2)}, u32[]{:S(2)}) collective-permute-start(f32[128,512]{1,0:T(8,128)S(1)} %bitcast_add_fusion.11), channel_id=1, source_target_pairs={{0,2},{1,3},{2,4},{3,5},{4,6},{5,7},{6,0},{7,1},{8,10},{9,11},{10,... | collective-permute-start | bytes 786440 | tf_op jit(solution)/shard_map/ppermute | solution.py:344
  146.9 17.5 %collective-permute-start.32 = (f32[128,512]{1,0:T(8,128)S(1)}, f32[128,512]{1,0:T(8,128)S(1)}, u32[]{:S(2)}, u32[]{:S(2)}) collective-permute-start(f32[128,512]{1,0:T(8,128)S(1)} %bitcast_add_fusion.8), channel_id=1, source_target_pairs={{0,6},{1,7},{2,0},{3,1},{4,2},{5,3},{6,4},{7,5},{8,14},{9,15},{10,... | collective-permute-start | bytes 786440 | tf_op jit(solution)/shard_map/ppermute | solution.py:344
  147.5 21.8 %collective-permute-start.23 = (f32[128,512]{1,0:T(8,128)S(1)}, f32[128,512]{1,0:T(8,128)S(1)}, u32[]{:S(2)}, u32[]{:S(2)}) collective-permute-start(f32[128,512]{1,0:T(8,128)S(1)} %bitcast_add_fusion.17), channel_id=1, source_target_pairs={{0,2},{1,3},{2,4},{3,5},{4,6},{5,7},{6,0},{7,1},{8,10},{9,11},{10,... | collective-permute-start | bytes 786440 | tf_op jit(solution)/shard_map/ppermute | solution.py:344
  163.7 7.0 %collective-permute-start.26 = (f32[128,512]{1,0:T(8,128)S(1)}, f32[128,512]{1,0:T(8,128)S(1)}, u32[]{:S(2)}, u32[]{:S(2)}) collective-permute-start(f32[128,512]{1,0:T(8,128)S(1)} %bitcast_add_fusion.14), channel_id=1, source_target_pairs={{0,6},{1,7},{2,0},{3,1},{4,2},{5,3},{6,4},{7,5},{8,14},{9,15},{10,... | collective-permute-start | bytes 786440 | tf_op jit(solution)/shard_map/ppermute | solution.py:344
  164.4 9.9 %copy-start.4 = (f32[3,256,512]{2,1,0:T(8,128)S(1)}, f32[3,256,512]{2,1,0:T(8,128)}, u32[]{:S(2)}) copy-start(f32[3,256,512]{2,1,0:T(8,128)} %get-tuple-element.118) | copy-start | bytes 4718596
  164.4 30.1 %collective-permute-start.30 = (f32[128,512]{1,0:T(8,128)S(1)}, f32[128,512]{1,0:T(8,128)S(1)}, u32[]{:S(2)}, u32[]{:S(2)}) collective-permute-start(f32[128,512]{1,0:T(8,128)S(1)} %bitcast_add_fusion.10), channel_id=1, source_target_pairs={{0,2},{1,3},{2,4},{3,5},{4,6},{5,7},{6,0},{7,1},{8,10},{9,11},{10,... | collective-permute-start | bytes 786440 | tf_op jit(solution)/shard_map/ppermute | solution.py:344
  169.3 25.3 %collective-permute-start.33 = (f32[128,512]{1,0:T(8,128)S(1)}, f32[128,512]{1,0:T(8,128)S(1)}, u32[]{:S(2)}, u32[]{:S(2)}) collective-permute-start(f32[128,512]{1,0:T(8,128)S(1)} %bitcast_add_fusion.7), channel_id=1, source_target_pairs={{0,6},{1,7},{2,0},{3,1},{4,2},{5,3},{6,4},{7,5},{8,14},{9,15},{10,... | collective-permute-start | bytes 786440 | tf_op jit(solution)/shard_map/ppermute | solution.py:344
  170.8 10.5 %collective-permute-start.24 = (f32[128,512]{1,0:T(8,128)S(1)}, f32[128,512]{1,0:T(8,128)S(1)}, u32[]{:S(2)}, u32[]{:S(2)}) collective-permute-start(f32[128,512]{1,0:T(8,128)S(1)} %bitcast_add_fusion.16), channel_id=1, source_target_pairs={{0,2},{1,3},{2,4},{3,5},{4,6},{5,7},{6,0},{7,1},{8,10},{9,11},{10,... | collective-permute-start | bytes 786440 | tf_op jit(solution)/shard_map/ppermute | solution.py:344
  171.5 11.1 %collective-permute-start.27 = (f32[128,512]{1,0:T(8,128)S(1)}, f32[128,512]{1,0:T(8,128)S(1)}, u32[]{:S(2)}, u32[]{:S(2)}) collective-permute-start(f32[128,512]{1,0:T(8,128)S(1)} %bitcast_add_fusion.13), channel_id=1, source_target_pairs={{0,6},{1,7},{2,0},{3,1},{4,2},{5,3},{6,4},{7,5},{8,14},{9,15},{10,... | collective-permute-start | bytes 786440 | tf_op jit(solution)/shard_map/ppermute | solution.py:344
  174.2 16.3 %collective-permute-start.36 = (f32[256,512]{1,0:T(8,128)S(1)}, f32[256,512]{1,0:T(8,128)S(1)}, u32[]{:S(2)}, u32[]{:S(2)}) collective-permute-start(f32[256,512]{1,0:T(8,128)S(1)} %bitcast_add_fusion.5), channel_id=1, source_target_pairs={{0,2},{1,3},{2,4},{3,5},{4,6},{5,7},{6,0},{7,1},{8,10},{9,11},{10,... | collective-permute-start | bytes 1572872 | tf_op jit(solution)/shard_map/ppermute | solution.py:344
  181.2 11.9 %collective-permute-start.39 = (f32[256,512]{1,0:T(8,128)S(1)}, f32[256,512]{1,0:T(8,128)S(1)}, u32[]{:S(2)}, u32[]{:S(2)}) collective-permute-start(f32[256,512]{1,0:T(8,128)S(1)} %bitcast_add_fusion.2), channel_id=1, source_target_pairs={{0,6},{1,7},{2,0},{3,1},{4,2},{5,3},{6,4},{7,5},{8,14},{9,15},{10,... | collective-permute-start | bytes 1572872 | tf_op jit(solution)/shard_map/ppermute | solution.py:344
  190.6 13.2 %collective-permute-start.37 = (f32[256,512]{1,0:T(8,128)S(1)}, f32[256,512]{1,0:T(8,128)S(1)}, u32[]{:S(2)}, u32[]{:S(2)}) collective-permute-start(f32[256,512]{1,0:T(8,128)S(1)} %bitcast_add_fusion.4), channel_id=1, source_target_pairs={{0,2},{1,3},{2,4},{3,5},{4,6},{5,7},{6,0},{7,1},{8,10},{9,11},{10,... | collective-permute-start | bytes 1572872 | tf_op jit(solution)/shard_map/ppermute | solution.py:344
  193.2 10.7 %collective-permute-start.40 = (f32[256,512]{1,0:T(8,128)S(1)}, f32[256,512]{1,0:T(8,128)S(1)}, u32[]{:S(2)}, u32[]{:S(2)}) collective-permute-start(f32[256,512]{1,0:T(8,128)S(1)} %bitcast_add_fusion.1), channel_id=1, source_target_pairs={{0,6},{1,7},{2,0},{3,1},{4,2},{5,3},{6,4},{7,5},{8,14},{9,15},{10,... | collective-permute-start | bytes 1572872 | tf_op jit(solution)/shard_map/ppermute | solution.py:344
  203.9 1.3 copy-start.5

commit v3 on v2

--- a/solution.py
+++ b/solution.py
@@ -13,6 +13,7 @@
 TILE = 256
 FAR = 1 << 30
 LOW = -1e30
+LARGE = pl.CostEstimate(flops=12 << 30, bytes_accessed=16 << 20, transcendentals=0)
 SMALL = pl.CostEstimate(flops=1024, bytes_accessed=1024, transcendentals=0)
 
 
@@ -166,7 +167,7 @@
             pltpu.VMEM((n, 2 * HEAD_SIZE), jnp.bfloat16) for n in (near, near, vert, vert)
         ],
         compiler_params=pltpu.CompilerParams(vmem_limit_bytes=40 << 20),
-        cost_estimate=SMALL,
+        cost_estimate=LARGE,
     )(first_row, back, wraps, q, *arrays)
 
 
@@ -202,18 +203,18 @@
         rest_b[0] = term[half:]
 
 
-def project(own, other, part, rows, w_own, w_other, order):
-    depth = own.shape[1]
+def project(own, other, w_own, w_other, order):
+    rows, depth = own.shape
     half = rows // 2
     count = order.shape[0]
     width = w_own.shape[1] // (2 * count)
-    x_spec = pl.BlockSpec((rows, depth), lambda i, o: (part, 0))
+    x_spec = pl.BlockSpec((rows, depth), lambda i, o: (0, 0))
     w_spec = pl.BlockSpec((depth, width), lambda i, o: (0, o[i]))
     first = jax.ShapeDtypeStruct((half, width), jnp.float32)
     rest = jax.ShapeDtypeStruct((count - 1, half, width), jnp.float32)
     first_spec = pl.BlockSpec((half, width), lambda i, o: (0, 0))
     back_step = lambda i: jnp.where(i == 0, 1, jnp.where(i == 3, 2, 0))
-    return pl.pallas_call(
+    first_a, rest_a, first_b, rest_b = pl.pallas_call(
         project_kernel,
         out_shape=[first, rest, first, rest],
         grid_spec=pltpu.PrefetchScalarGridSpec(
@@ -232,8 +233,9 @@
             ],
         ),
         compiler_params=pltpu.CompilerParams(vmem_limit_bytes=48 << 20),
-        cost_estimate=SMALL,
+        cost_estimate=LARGE,
     )(order, own, other, w_own, w_other)
+    return (first_a, first_b), (rest_a, rest_b)
 
 
 def body(
@@ -295,55 +297,57 @@
         ((k_left, k_right, v_below, v_above), small)
     )
     vert_pos, slash_pos, first_row, back, wraps, order, k_place, k_held, v_place, v_held = small
-    k_far = send(k_right, left)
+    half = rows // 2
+    source = jnp.where(x >= 2, v_below, value_vectors)
+    v_left = jnp.where(x == 3, v_below, value_vectors)
+    moved_left = send(jnp.concatenate([k_right, source[half:]]), left)
     v_beyond = send(v_above, down)
-    v_left = send(jnp.where(x == 3, v_below, value_vectors), right)
-    source = jnp.where(x >= 2, v_below, value_vectors)
-    half = rows // 2
-    k_far, v_beyond, v_left = lax.optimization_barrier((k_far, v_beyond, v_left))
-    v_far_a = send(source[:half], over)
-    v_far_b = send(source[half:], left)
+    moved_right = send(jnp.concatenate([v_left, source[:half]]), right)
     k_left_wrap = send(k_left, [(i, i + 4) for i in ids if i % 4 == 0 and i + 4 in ids])
+    moved_left, v_beyond, moved_right, k_left_wrap = lax.optimization_barrier(
+        (moved_left, v_beyond, moved_right, k_left_wrap)
+    )
+    k_far, v_far_b = moved_left[:rows], moved_left[rows:]
+    v_left, v_far_a = moved_right[:rows], moved_right[rows:]
 
     k_named = pick_blocks(k_place, k_held, (key_rows, k_right, k_far, k_left))
     v_named = pick_blocks(v_place, v_held, (value_vectors, v_above, v_beyond, v_below))
+    v_far_a = send(v_far_a, right)
+    v_far_b = send(v_far_b, left)
+    k_far_wrap = send(k_far, [(i, i + 4) for i in ids if i % 4 < 2 and i + 4 in ids])
     named = [*k_named, *v_named]
     one, two = (4, 12, 1, 3), (12, 4, 3, 1)
     named = [a + swapped(a, bits) for a, bits in zip(named, one)]
-    v_far_a, v_far_b, k_left_wrap, *named = lax.optimization_barrier(
-        (v_far_a, v_far_b, k_left_wrap, *named)
+    v_far_a, v_far_b, k_far_wrap, *named = lax.optimization_barrier(
+        (v_far_a, v_far_b, k_far_wrap, *named)
     )
-    v_far_b = send(v_far_b, left)
-    k_far_wrap = send(k_far, [(i, i + 4) for i in ids if i % 4 < 2 and i + 4 in ids])
-    more = [swapped(a, bits) for a, bits in zip(named, two)]
-    v_far_b, k_far_wrap, *more = lax.optimization_barrier((v_far_b, k_far_wrap, *more))
-    named = [a + b for a, b in zip(named, more)]
+    named = [a + swapped(a, bits) for a, bits in zip(named, two)]
 
     arrays = (k_far, k_far_wrap, k_left, k_left_wrap, key_rows, v_far_a, v_far_b, v_left)
     arrays = (*arrays, value_vectors, *named, vert_pos, slash_pos)
 
     rings = [[(i, (i + d) % head_size) for i in range(head_size)] for d in (2, head_size - 2)]
-    q = queries
-    pairs = []
-    for start in (0, half):
-        own = attend(q, start, half, first_row, back, wraps, arrays)
-        q, own = lax.optimization_barrier((q, own))
-        pairs.append((own, lax.ppermute(own, "head", swap)))
-    sums, terms = [], []
-    for which, part, count in ((0, 0, half // 2), (0, 1, half // 2), (1, 0, half)):
-        own, other = pairs[which]
-        first_a, rest_a, first_b, rest_b = project(
-            own, other, part, count, out_weight, w_other, order
-        )
-        order, first_a, first_b = lax.optimization_barrier((order, first_a, first_b))
-        sums.append([first_a, first_b])
-        terms.append([rest_a, rest_b])
-    for step in range(chips - 1):
-        for part in range(len(sums)):
-            for way in range(2):
-                moved = lax.ppermute(sums[part][way], "head", rings[way])
-                sums[part][way] = moved + terms[part][way][step]
-    return jnp.concatenate(sums[0] + sums[1] + sums[2], axis=0)
+    ring = lambda parts: [lax.ppermute(p, "head", r) for p, r in zip(parts, rings)]
+    add = lambda parts, terms, step: [p + t[step] for p, t in zip(parts, terms)]
+
+    own = attend(queries, 0, half, first_row, back, wraps, arrays)
+    other = lax.ppermute(own, "head", swap)
+    first, terms = project(own, other, out_weight, w_other, order)
+    q, *first = lax.optimization_barrier((queries, *first))
+    moved = ring(first)
+    own = attend(q, half, half, first_row, back, wraps, arrays)
+    own, *moved = lax.optimization_barrier((own, *moved))
+    other = lax.ppermute(own, "head", swap)
+    sums = add(moved, terms, 0)
+    order, *sums = lax.optimization_barrier((order, *sums))
+    moved = ring(sums)
+    later, later_terms = project(own, other, out_weight, w_other, order)
+    *moved, later_a, later_b = lax.optimization_barrier((*moved, *later))
+    sums, later = add(moved, terms, 1), (later_a, later_b)
+    sums, later = add(ring(sums), terms, 2), add(ring(later), later_terms, 0)
+    later = add(ring(later), later_terms, 1)
+    later = add(ring(later), later_terms, 2)
+    return jnp.concatenate([*sums, *later], axis=0)
 
 
 def solution(mesh):

time: 210 us -> 192 us (0.914)
  starting transfers between devices: 50.8 us -> 43.9 us
  waiting for transfers between devices: 99 us -> 94.2 us
  Pallas kernels: 46.3 us -> 42.9 us
  local copies, waits for them, and re-layouts: 4.2 us -> 1.65 us
    ppermute x20 -> x19, starting transfers between devices: 29.7 us -> 24.3 us  [body(): send = lambda a, pairs: lax.ppermute(a, 'seq', pairs)]
    ppermute x20 -> x14, waiting for transfers between devices: 49.4 us -> 45 us  [the longest x12 42.4 us: body(): lax.ppermute(p, 'head', r)]
    pallas_call x3 -> x2, Pallas kernels: 25 us -> 21.6 us  [project(): pl.pallas_call(project_kernel, out_shape=[first, rest, first, rest], grid...]
    unnamed x13 -> x15, local copies, waits for them, and re-layouts: 2.79 us -> 0.13 us
    ppermute x20 -> x14, starting transfers between devices: 21 us -> 19.6 us  [the longest x12 19.5 us: body(): lax.ppermute(p, 'head', r)]
    ppermute x20 -> x19, waiting for transfers between devices: 49.7 us -> 49.2 us  [body(): send = lambda a, pairs: lax.ppermute(a, 'seq', pairs)]
  transfers between devices with their start and end apart: 41 -> 34, of which waited for: 25 -> 26; matrix products, arithmetic and copies ran while one was open for 3% -> 3% of each run, Pallas kernels for 22% -> 17%
where the time goes in v3:
time: 192 us; the launch traced here: 189 us
  waiting for transfers between devices  94.2 us (49%)
  starting transfers between devices  43.9 us (23%)
  Pallas kernels  42.9 us (22%)
  other arithmetic  5.52 us (3%)
    ppermute x19, waiting for transfers between devices, body(): send = lambda a, pairs: lax.ppermute(a, 'seq', pairs)  49.2 us
    ppermute x12, waiting for transfers between devices, body(): lax.ppermute(p, 'head', r)  42.4 us
    ppermute x19, starting transfers between devices, body(): send = lambda a, pairs: lax.ppermute(a, 'seq', pairs)  24.3 us
    pallas_call x2, Pallas kernels, project(): pl.pallas_call(project_kernel, out_shape=[first, rest, first, rest], grid...  21.6 us
    ppermute x12, starting transfers between devices, body(): lax.ppermute(p, 'head', r)  19.5 us
    pallas_call x2, Pallas kernels, attend(): pl.pallas_call(functools.partial(attend_kernel, start), grid=(rows // TIL...  19 us
  transfers between devices with their start and end apart: 34, of which 26 were waited for; matrix products, arithmetic and copies ran while one was open for 3% of the time, Pallas kernels for 17%

profile of v3, /device:TPU:2, one launch (start us, length us, event | category | flops | bytes accessed | tf_op | source)
XLA Modules:
  0.0 189.2 jit_solution(6544060063791766043)
XLA Ops:
  0.5 1.6 collective-permute-start
  2.1 4.0 %collective-permute-start.3 = (f32[1024,128]{1,0:T(8,128)}, f32[1024,128]{1,0:T(8,128)S(1)}, u32[]{:S(2)}, u32[]{:S(2)}) collective-permute-start(f32[1024,128]{1,0:T(8,128)} %v_own.3), channel_id=1, source_target_pairs={{0,96},{8,104},{16,112},{24,120},{32,0},{40,8},{48,16},{56,24},{64... | collective-permute-start | bytes 1572872 | tf_op jit(solution)/shard_map/ppermute | solution.py:260
  9.7 4.8 %collective-permute-done.1.refs_1_ = f32[1024,128]{1,0:T(8,128)S(1)} collective-permute-done((f32[1024,128]{1,0:T(8,128)}, f32[1024,128]{1,0:T(8,128)S(1)}, u32[]{:S(2)}, u32[]{:S(2)}) %collective-permute-start.1) | collective-permute-done | bytes 524320 | tf_op jit(solution)/shard_map/ppermute | solution.py:260
  14.6 1.3 collective-permute-done.refs_3_.k_left
  15.9 1.8 collective-permute-done.3.refs_1_
  17.7 3.3 %collective-permute-done.2.refs_3_ = f32[1024,128]{1,0:T(8,128)S(1)} collective-permute-done((f32[1024,128]{1,0:T(8,128)}, f32[1024,128]{1,0:T(8,128)S(1)}, u32[]{:S(2)}, u32[]{:S(2)}) %collective-permute-start.2) | collective-permute-done | bytes 524320 | tf_op jit(solution)/shard_map/ppermute | solution.py:260
  21.0 1.1 broadcast_select_fusion
  22.2 1.6 collective-permute-start.4
  25.4 11.2 %collective-permute-done.5.refs_2_ = f32[1024,128]{1,0:T(8,128)S(1)} collective-permute-done((f32[1024,128]{1,0:T(8,128)S(1)}, f32[1024,128]{1,0:T(8,128)S(1)}, u32[]{:S(2)}, u32[]{:S(2)}) %collective-permute-start.5) | collective-permute-done | bytes 524320 | tf_op jit(solution)/shard_map/ppermute | solution.py:260
  36.6 3.8 %collective-permute-done.4 = f32[1536,128]{1,0:T(8,128)S(1)} collective-permute-done((f32[1536,128]{1,0:T(8,128)S(1)}, f32[1536,128]{1,0:T(8,128)S(1)}, u32[]{:S(2)}, u32[]{:S(2)}) %collective-permute-start.4) | collective-permute-done | bytes 786464 | tf_op jit(solution)/shard_map/ppermute | solution.py:260
  40.4 2.6 %collective-permute-done.6 = f32[1536,128]{1,0:T(8,128)S(1)} collective-permute-done((f32[1536,128]{1,0:T(8,128)S(1)}, f32[1536,128]{1,0:T(8,128)S(1)}, u32[]{:S(2)}, u32[]{:S(2)}) %collective-permute-start.6) | collective-permute-done | bytes 786464 | tf_op jit(solution)/shard_map/ppermute | solution.py:260
  43.1 1.2 shard_map.73
  45.1 1.2 shard_map.74
  46.3 3.1 %collective-permute-start.13 = (f32[1024,128]{1,0:T(8,128)S(1)}, f32[1024,128]{1,0:T(8,128)S(1)}, u32[]{:S(2)}, u32[]{:S(2)}) collective-permute-start(f32[1024,128]{1,0:T(8,128)S(1)} %get-tuple-element.72), channel_id=1, source_target_pairs={{0,8},{8,0},{16,24},{24,16},{32,40},{40,32},{48,56},{56,48},{64,72... | collective-permute-start | bytes 1572872 | tf_op jit(solution)/shard_map/ppermute | solution.py:260
  49.3 6.7 %collective-permute-done.11 = f32[1024,128]{1,0:T(8,128)S(1)} collective-permute-done((f32[1024,128]{1,0:T(8,128)S(1)}, f32[1024,128]{1,0:T(8,128)S(1)}, u32[]{:S(2)}, u32[]{:S(2)}) %collective-permute-start.11) | collective-permute-done | bytes 524320 | tf_op jit(solution)/shard_map/ppermute | solution.py:260
  56.0 2.2 %collective-permute-start.10 = (f32[1024,128]{1,0:T(8,128)S(1)}, f32[1024,128]{1,0:T(8,128)S(1)}, u32[]{:S(2)}, u32[]{:S(2)}) collective-permute-start(f32[1024,128]{1,0:T(8,128)S(1)} %slice.56.refs_2_.k_far), channel_id=1, source_target_pairs={{0,32},{8,40},{32,64},{40,72},{64,96},{72,104},{1,33},{9,41},{33,6... | collective-permute-start | bytes 1572872 | tf_op jit(solution)/shard_map/ppermute | solution.py:260
  58.3 1.0 collective-permute-done.13
  59.3 1.7 collective-permute-start.9
  61.3 1.0 collective-permute-done.14
  62.4 3.0 %collective-permute-done.8.v_far_a = f32[512,128]{1,0:T(8,128)S(1)} collective-permute-done((f32[512,128]{1,0:T(8,128)S(1)}, f32[512,128]{1,0:T(8,128)S(1)}, u32[]{:S(2)}, u32[]{:S(2)}) %collective-permute-start.8) | collective-permute-done | bytes 262176 | tf_op jit(solution)/shard_map/ppermute | solution.py:260
  66.0 1.0 collective-permute-done.10.k_far_wrap
  67.0 3.4 %collective-permute-start.15 = (f32[1024,128]{1,0:T(8,128)S(1)}, f32[1024,128]{1,0:T(8,128)S(1)}, u32[]{:S(2)}, u32[]{:S(2)}) collective-permute-start(f32[1024,128]{1,0:T(8,128)S(1)} %add.211), channel_id=1, source_target_pairs={{0,96},{8,104},{16,112},{24,120},{32,64},{40,72},{48,80},{56,88},{... | collective-permute-start | bytes 1572872 | tf_op jit(solution)/shard_map/ppermute | solution.py:260
  70.5 3.7 %collective-permute-start.18 = (f32[1024,128]{1,0:T(8,128)S(1)}, f32[1024,128]{1,0:T(8,128)S(1)}, u32[]{:S(2)}, u32[]{:S(2)}) collective-permute-start(f32[1024,128]{1,0:T(8,128)S(1)} %add.214), channel_id=1, source_target_pairs={{0,8},{8,0},{16,24},{24,16},{32,40},{40,32},{48,56},{56,48},{64,72... | collective-permute-start | bytes 1572872 | tf_op jit(solution)/shard_map/ppermute | solution.py:260
  74.3 4.3 %collective-permute-done.15 = f32[1024,128]{1,0:T(8,128)S(1)} collective-permute-done((f32[1024,128]{1,0:T(8,128)S(1)}, f32[1024,128]{1,0:T(8,128)S(1)}, u32[]{:S(2)}, u32[]{:S(2)}) %collective-permute-start.15) | collective-permute-done | bytes 524320 | tf_op jit(solution)/shard_map/ppermute | solution.py:260
  78.6 1.0 collective-permute-done.16
  79.8 1.6 collective-permute-done.18
  81.5 9.5 %shard_map.75.own = f32[512,512]{1,0:T(8,128)S(1)} custom-call(s32[1]{0:T(128)} %bitcast.1.first_row, s32[4,4]{1,0:T(4,128)S(1)} %get-tuple-element.57.back, s32[2]{0:T(128)S(1)} %add_convert_fusion.wraps, f32[1024,512]{1,0:T(8,128)S(1)} %copy-done.4, f32[1024,128]{1,0:T(8,128)S(1)} %slice.56.refs_2_.k_far, ...), custom_call_target="tpu_custom_call" | custom-call | flops 12884901888 | bytes 16777216 | tf_op jit(solution)/shard_map/pallas_call | solution.py:158
  91.1 2.6 %collective-permute-done.19.other = f32[512,512]{1,0:T(8,128)S(1)} collective-permute-done((f32[512,512]{1,0:T(8,128)S(1)}, f32[512,512]{1,0:T(8,128)S(1)}, u32[]{:S(2)}, u32[]{:S(2)}) %collective-permute-start.19) | collective-permute-done | bytes 1048608 | tf_op jit(solution)/shard_map/ppermute | solution.py:334
  93.7 10.8 %shard_map.76 = (f32[256,512]{1,0:T(8,128)S(1)}, f32[3,256,512]{2,1,0:T(8,128)S(1)}, f32[256,512]{1,0:T(8,128)S(1)}, f32[3,256,512]{2,1,0:T(8,128)}) custom-call(s32[4]{0:T(128)S(1)} %fusion.2.order, f32[512,512]{1,0:T(8,128)S(1)} %shard_map.75.own, f32[512,512]{1,0:T(8,128)S(1)} %collective-permute-done.19.other, f32[512,4096]{1,0:T(8,128)} %w_own.3, ...), custom_call_target="tpu_custom_call" | custom-call | flops 12884901888 | bytes 16777216 | tf_op jit(solution)/shard_map/pallas_call | solution.py:217
  104.5 1.6 collective-permute-start.21
  106.1 1.6 collective-permute-start.22
  107.7 9.5 %shard_map.77.own = f32[512,512]{1,0:T(8,128)S(1)} custom-call(s32[1]{0:T(128)} %bitcast.1.first_row, s32[4,4]{1,0:T(4,128)S(1)} %get-tuple-element.57.back, s32[2]{0:T(128)S(1)} %add_convert_fusion.wraps, f32[1024,512]{1,0:T(8,128)S(1)} %copy-done.4, f32[1024,128]{1,0:T(8,128)S(1)} %slice.56.refs_2_.k_far, ...), custom_call_target="tpu_custom_call" | custom-call | flops 12884901888 | bytes 16777216 | tf_op jit(solution)/shard_map/pallas_call | solution.py:158
  117.2 2.5 %collective-permute-done.21 = f32[256,512]{1,0:T(8,128)S(1)} collective-permute-done((f32[256,512]{1,0:T(8,128)S(1)}, f32[256,512]{1,0:T(8,128)S(1)}, u32[]{:S(2)}, u32[]{:S(2)}) %collective-permute-start.21) | collective-permute-done | bytes 524320 | tf_op jit(solution)/shard_map/ppermute | solution.py:330
  120.0 1.6 collective-permute-start.23
  121.7 1.7 collective-permute-start.24
  123.3 10.8 %shard_map.78 = (f32[256,512]{1,0:T(8,128)S(1)}, f32[3,256,512]{2,1,0:T(8,128)S(1)}, f32[256,512]{1,0:T(8,128)S(1)}, f32[3,256,512]{2,1,0:T(8,128)}) custom-call(s32[4]{0:T(128)S(1)} %fusion.2.order, f32[512,512]{1,0:T(8,128)S(1)} %shard_map.77.own, f32[512,512]{1,0:T(8,128)S(1)} %collective-permute-done.25.other, f32[512,4096]{1,0:T(8,128)} %w_own.3, ...), custom_call_target="tpu_custom_call" | custom-call | flops 12884901888 | bytes 16777216 | tf_op jit(solution)/shard_map/pallas_call | solution.py:217
  134.1 1.6 collective-permute-done.23
  135.7 1.3 collective-permute-start.28
  137.1 2.0 %collective-permute-start.27 = (f32[256,512]{1,0:T(8,128)S(1)}, f32[256,512]{1,0:T(8,128)S(1)}, u32[]{:S(2)}, u32[]{:S(2)}) collective-permute-start(f32[256,512]{1,0:T(8,128)S(1)} %bitcast_add_fusion.7), channel_id=1, source_target_pairs={{0,6},{1,7},{2,0},{3,1},{4,2},{5,3},{6,4},{7,5},{8,14},{9,15},{10,... | collective-permute-start | bytes 1572872 | tf_op jit(solution)/shard_map/ppermute | solution.py:330
  139.1 1.8 collective-permute-start.31
  141.3 10.5 %collective-permute-done.28 = f32[256,512]{1,0:T(8,128)S(1)} collective-permute-done((f32[256,512]{1,0:T(8,128)S(1)}, f32[256,512]{1,0:T(8,128)S(1)}, u32[]{:S(2)}, u32[]{:S(2)}) %collective-permute-start.28) | collective-permute-done | bytes 524320 | tf_op jit(solution)/shard_map/ppermute | solution.py:330
  152.0 9.3 %collective-permute-done.31 = f32[256,512]{1,0:T(8,128)S(1)} collective-permute-done((f32[256,512]{1,0:T(8,128)S(1)}, f32[256,512]{1,0:T(8,128)S(1)}, u32[]{:S(2)}, u32[]{:S(2)}) %collective-permute-start.31) | collective-permute-done | bytes 524320 | tf_op jit(solution)/shard_map/ppermute | solution.py:330
  161.4 3.6 %collective-permute-start.32 = (f32[256,512]{1,0:T(8,128)S(1)}, f32[256,512]{1,0:T(8,128)S(1)}, u32[]{:S(2)}, u32[]{:S(2)}) collective-permute-start(f32[256,512]{1,0:T(8,128)S(1)} %bitcast_add_fusion.2), channel_id=1, source_target_pairs={{0,6},{1,7},{2,0},{3,1},{4,2},{5,3},{6,4},{7,5},{8,14},{9,15},{10,... | collective-permute-start | bytes 1572872 | tf_op jit(solution)/shard_map/ppermute | solution.py:330
  165.1 7.9 %collective-permute-done.29 = f32[256,512]{1,0:T(8,128)S(1)} collective-permute-done((f32[256,512]{1,0:T(8,128)S(1)}, f32[256,512]{1,0:T(8,128)S(1)}, u32[]{:S(2)}, u32[]{:S(2)}) %collective-permute-start.29) | collective-permute-done | bytes 524320 | tf_op jit(solution)/shard_map/ppermute | solution.py:330
  173.1 1.7 collective-permute-done.32
  174.9 3.8 %collective-permute-start.33 = (f32[256,512]{1,0:T(8,128)S(1)}, f32[256,512]{1,0:T(8,128)S(1)}, u32[]{:S(2)}, u32[]{:S(2)}) collective-permute-start(f32[256,512]{1,0:T(8,128)S(1)} %bitcast_add_fusion.1), channel_id=1, source_target_pairs={{0,6},{1,7},{2,0},{3,1},{4,2},{5,3},{6,4},{7,5},{8,14},{9,15},{10,... | collective-permute-start | bytes 1572872 | tf_op jit(solution)/shard_map/ppermute | solution.py:330
  178.8 8.2 %collective-permute-done.30 = f32[256,512]{1,0:T(8,128)S(1)} collective-permute-done((f32[256,512]{1,0:T(8,128)S(1)}, f32[256,512]{1,0:T(8,128)S(1)}, u32[]{:S(2)}, u32[]{:S(2)}) %collective-permute-start.30) | collective-permute-done | bytes 524320 | tf_op jit(solution)/shard_map/ppermute | solution.py:330
  187.7 1.5 pad_maximum_fusion
  (99 shorter events, 9.6 us)
Async XLA Ops:
  0.0 6.8 %copy-start = (s32[32,3]{0,1:T(4,128)S(1)}, s32[32,3]{0,1:T(4,128)}, u32[]{:S(2)}) copy-start(s32[32,3]{0,1:T(4,128)} %param.11) | copy-start | bytes 1156
  0.0 93.7 %collective-permute-start.20 = (f32[512,4096]{1,0:T(8,128)}, f32[512,4096]{1,0:T(8,128)}, u32[]{:S(2)}, u32[]{:S(2)}) collective-permute-start(f32[512,4096]{1,0:T(8,128)} %w_own.3), channel_id=1, source_target_pairs={{0,1},{1,0},{2,3},{3,2},{4,5},{5,4},{6,7},{7,6},{8,9},{9,8},{10,11... | collective-permute-start | bytes 25165832 | tf_op jit(solution)/shard_map/ppermute | solution.py:268
  0.0 14.5 %collective-permute-start.1 = (f32[1024,128]{1,0:T(8,128)}, f32[1024,128]{1,0:T(8,128)S(1)}, u32[]{:S(2)}, u32[]{:S(2)}) collective-permute-start(f32[1024,128]{1,0:T(8,128)} %k_own.3), channel_id=1, source_target_pairs={{0,24},{8,0},{16,8},{24,16},{32,56},{40,32},{48,40},{56,48},{64,88... | collective-permute-start | bytes 1572872 | tf_op jit(solution)/shard_map/ppermute | solution.py:260
  0.5 15.4 %collective-permute-start = (f32[1024,128]{1,0:T(8,128)}, f32[1024,128]{1,0:T(8,128)S(1)}, u32[]{:S(2)}, u32[]{:S(2)}) collective-permute-start(f32[1024,128]{1,0:T(8,128)} %k_own.3), channel_id=1, source_target_pairs={{0,8},{8,16},{16,24},{24,0},{32,40},{40,48},{48,56},{56,32},{64,72... | collective-permute-start | bytes 1572872 | tf_op jit(solution)/shard_map/ppermute | solution.py:260
  2.1 15.6 %collective-permute-start.3 = (f32[1024,128]{1,0:T(8,128)}, f32[1024,128]{1,0:T(8,128)S(1)}, u32[]{:S(2)}, u32[]{:S(2)}) collective-permute-start(f32[1024,128]{1,0:T(8,128)} %v_own.3), channel_id=1, source_target_pairs={{0,96},{8,104},{16,112},{24,120},{32,0},{40,8},{48,16},{56,24},{64... | collective-permute-start | bytes 1572872 | tf_op jit(solution)/shard_map/ppermute | solution.py:260
  6.1 14.8 %collective-permute-start.2 = (f32[1024,128]{1,0:T(8,128)}, f32[1024,128]{1,0:T(8,128)S(1)}, u32[]{:S(2)}, u32[]{:S(2)}) collective-permute-start(f32[1024,128]{1,0:T(8,128)} %v_own.3), channel_id=1, source_target_pairs={{0,32},{8,40},{16,48},{24,56},{32,64},{40,72},{48,80},{56,88},{64,... | collective-permute-start | bytes 1572872 | tf_op jit(solution)/shard_map/ppermute | solution.py:260
  22.2 20.9 %copy-start.3 = (f32[1024,128]{1,0:T(8,128)S(1)}, f32[1024,128]{1,0:T(8,128)}, u32[]{:S(2)}) copy-start(f32[1024,128]{1,0:T(8,128)} %k_own.3) | copy-start | bytes 1572868
  22.2 18.2 %collective-permute-start.4 = (f32[1536,128]{1,0:T(8,128)S(1)}, f32[1536,128]{1,0:T(8,128)S(1)}, u32[]{:S(2)}, u32[]{:S(2)}) collective-permute-start(f32[1536,128]{1,0:T(8,128)S(1)} %pad_maximum_fusion.1), channel_id=1, source_target_pairs={{0,24},{8,0},{16,8},{24,16},{32,56},{40,32},{48,40},{56,48},{64,88... | collective-permute-start | bytes 2359304 | tf_op jit(solution)/shard_map/ppermute | solution.py:260
  23.9 21.2 %copy-start.2 = (f32[1024,128]{1,0:T(8,128)S(1)}, f32[1024,128]{1,0:T(8,128)}, u32[]{:S(2)}) copy-start(f32[1024,128]{1,0:T(8,128)} %v_own.3) | copy-start | bytes 1572868
  23.9 19.1 %collective-permute-start.6 = (f32[1536,128]{1,0:T(8,128)S(1)}, f32[1536,128]{1,0:T(8,128)S(1)}, u32[]{:S(2)}, u32[]{:S(2)}) collective-permute-start(f32[1536,128]{1,0:T(8,128)S(1)} %pad_maximum_fusion.2), channel_id=1, source_target_pairs={{0,8},{8,16},{16,24},{24,0},{32,40},{40,48},{48,56},{56,32},{64,72... | collective-permute-start | bytes 2359304 | tf_op jit(solution)/shard_map/ppermute | solution.py:260
  24.5 12.2 %collective-permute-start.5 = (f32[1024,128]{1,0:T(8,128)S(1)}, f32[1024,128]{1,0:T(8,128)S(1)}, u32[]{:S(2)}, u32[]{:S(2)}) collective-permute-start(f32[1024,128]{1,0:T(8,128)S(1)} %collective-permute-done.3.refs_1_), channel_id=1, source_target_pairs={{0,96},{8,104},{16,112},{24,120},{32,0},{40,8},{48,16},{56,24},{64... | collective-permute-start | bytes 1572872 | tf_op jit(solution)/shard_map/ppermute | solution.py:260
  24.7 11.9 %collective-permute-start.7 = (f32[1024,128]{1,0:T(8,128)S(1)}, f32[1024,128]{1,0:T(8,128)S(1)}, u32[]{:S(2)}, u32[]{:S(2)}) collective-permute-start(f32[1024,128]{1,0:T(8,128)S(1)} %collective-permute-done.refs_3_.k_left), channel_id=1, source_target_pairs={{0,32},{32,64},{64,96},{1,33},{33,65},{65,97},{2,34},{34,66},{66,9... | collective-permute-start | bytes 1572872 | tf_op jit(solution)/shard_map/ppermute | solution.py:260
  44.3 11.7 %collective-permute-start.11 = (f32[1024,128]{1,0:T(8,128)S(1)}, f32[1024,128]{1,0:T(8,128)S(1)}, u32[]{:S(2)}, u32[]{:S(2)}) collective-permute-start(f32[1024,128]{1,0:T(8,128)S(1)} %get-tuple-element.67), channel_id=1, source_target_pairs={{0,32},{8,40},{16,48},{24,56},{32,0},{40,8},{48,16},{56,24},{64,96... | collective-permute-start | bytes 1572872 | tf_op jit(solution)/shard_map/ppermute | solution.py:260
  44.4 13.9 %collective-permute-start.12 = (f32[1024,128]{1,0:T(8,128)S(1)}, f32[1024,128]{1,0:T(8,128)S(1)}, u32[]{:S(2)}, u32[]{:S(2)}) collective-permute-start(f32[1024,128]{1,0:T(8,128)S(1)} %get-tuple-element.68), channel_id=1, source_target_pairs={{0,96},{8,104},{16,112},{24,120},{32,64},{40,72},{48,80},{56,88},{... | collective-permute-start | bytes 1572872 | tf_op jit(solution)/shard_map/ppermute | solution.py:260
  46.3 13.1 %collective-permute-start.13 = (f32[1024,128]{1,0:T(8,128)S(1)}, f32[1024,128]{1,0:T(8,128)S(1)}, u32[]{:S(2)}, u32[]{:S(2)}) collective-permute-start(f32[1024,128]{1,0:T(8,128)S(1)} %get-tuple-element.72), channel_id=1, source_target_pairs={{0,8},{8,0},{16,24},{24,16},{32,40},{40,32},{48,56},{56,48},{64,72... | collective-permute-start | bytes 1572872 | tf_op jit(solution)/shard_map/ppermute | solution.py:260
  49.3 13.0 %collective-permute-start.14 = (f32[1024,128]{1,0:T(8,128)S(1)}, f32[1024,128]{1,0:T(8,128)S(1)}, u32[]{:S(2)}, u32[]{:S(2)}) collective-permute-start(f32[1024,128]{1,0:T(8,128)S(1)} %get-tuple-element.73), channel_id=1, source_target_pairs={{0,24},{8,16},{16,8},{24,0},{32,56},{40,48},{48,40},{56,32},{64,88... | collective-permute-start | bytes 1572872 | tf_op jit(solution)/shard_map/ppermute | solution.py:260
  56.0 11.1 %collective-permute-start.10 = (f32[1024,128]{1,0:T(8,128)S(1)}, f32[1024,128]{1,0:T(8,128)S(1)}, u32[]{:S(2)}, u32[]{:S(2)}) collective-permute-start(f32[1024,128]{1,0:T(8,128)S(1)} %slice.56.refs_2_.k_far), channel_id=1, source_target_pairs={{0,32},{8,40},{32,64},{40,72},{64,96},{72,104},{1,33},{9,41},{33,6... | collective-permute-start | bytes 1572872 | tf_op jit(solution)/shard_map/ppermute | solution.py:260
  58.3 7.1 %collective-permute-start.8 = (f32[512,128]{1,0:T(8,128)S(1)}, f32[512,128]{1,0:T(8,128)S(1)}, u32[]{:S(2)}, u32[]{:S(2)}) collective-permute-start(f32[512,128]{1,0:T(8,128)S(1)} %slice.57), channel_id=1, source_target_pairs={{0,8},{8,16},{16,24},{24,0},{32,40},{40,48},{48,56},{56,32},{64,72... | collective-permute-start | bytes 786440 | tf_op jit(solution)/shard_map/ppermute | solution.py:260
  59.3 6.6 %collective-permute-start.9 = (f32[512,128]{1,0:T(8,128)S(1)}, f32[512,128]{1,0:T(8,128)S(1)}, u32[]{:S(2)}, u32[]{:S(2)}) collective-permute-start(f32[512,128]{1,0:T(8,128)S(1)} %slice.58), channel_id=1, source_target_pairs={{0,24},{8,0},{16,8},{24,16},{32,56},{40,32},{48,40},{56,48},{64,88... | collective-permute-start | bytes 786440 | tf_op jit(solution)/shard_map/ppermute | solution.py:260
  67.0 11.5 %collective-permute-start.15 = (f32[1024,128]{1,0:T(8,128)S(1)}, f32[1024,128]{1,0:T(8,128)S(1)}, u32[]{:S(2)}, u32[]{:S(2)}) collective-permute-start(f32[1024,128]{1,0:T(8,128)S(1)} %add.211), channel_id=1, source_target_pairs={{0,96},{8,104},{16,112},{24,120},{32,64},{40,72},{48,80},{56,88},{... | collective-permute-start | bytes 1572872 | tf_op jit(solution)/shard_map/ppermute | solution.py:260
  70.4 9.2 %collective-permute-start.16 = (f32[1024,128]{1,0:T(8,128)S(1)}, f32[1024,128]{1,0:T(8,128)S(1)}, u32[]{:S(2)}, u32[]{:S(2)}) collective-permute-start(f32[1024,128]{1,0:T(8,128)S(1)} %add.212), channel_id=1, source_target_pairs={{0,32},{8,40},{16,48},{24,56},{32,0},{40,8},{48,16},{56,24},{64,96... | collective-permute-start | bytes 1572872 | tf_op jit(solution)/shard_map/ppermute | solution.py:260
  70.5 9.2 %collective-permute-start.17 = (f32[1024,128]{1,0:T(8,128)S(1)}, f32[1024,128]{1,0:T(8,128)S(1)}, u32[]{:S(2)}, u32[]{:S(2)}) collective-permute-start(f32[1024,128]{1,0:T(8,128)S(1)} %add.213), channel_id=1, source_target_pairs={{0,24},{8,16},{16,8},{24,0},{32,56},{40,48},{48,40},{56,32},{64,88... | collective-permute-start | bytes 1572872 | tf_op jit(solution)/shard_map/ppermute | solution.py:260
  70.5 10.8 %collective-permute-start.18 = (f32[1024,128]{1,0:T(8,128)S(1)}, f32[1024,128]{1,0:T(8,128)S(1)}, u32[]{:S(2)}, u32[]{:S(2)}) collective-permute-start(f32[1024,128]{1,0:T(8,128)S(1)} %add.214), channel_id=1, source_target_pairs={{0,8},{8,0},{16,24},{24,16},{32,40},{40,32},{48,56},{56,48},{64,72... | collective-permute-start | bytes 1572872 | tf_op jit(solution)/shard_map/ppermute | solution.py:260
  79.6 1.8 copy-start.4
  91.0 2.7 %collective-permute-start.19 = (f32[512,512]{1,0:T(8,128)S(1)}, f32[512,512]{1,0:T(8,128)S(1)}, u32[]{:S(2)}, u32[]{:S(2)}) collective-permute-start(f32[512,512]{1,0:T(8,128)S(1)} %shard_map.75.own), channel_id=1, source_target_pairs={{0,1},{1,0},{2,3},{3,2},{4,5},{5,4},{6,7},{7,6},{8,9},{9,8},{10,11... | collective-permute-start | bytes 3145736 | tf_op jit(solution)/shard_map/ppermute | solution.py:334
  104.5 15.3 %copy-start.6 = (f32[3,256,512]{2,1,0:T(8,128)S(1)}, f32[3,256,512]{2,1,0:T(8,128)}, u32[]{:S(2)}) copy-start(f32[3,256,512]{2,1,0:T(8,128)} %get-tuple-element.92) | copy-start | bytes 4718596
  104.5 15.3 %collective-permute-start.21 = (f32[256,512]{1,0:T(8,128)S(1)}, f32[256,512]{1,0:T(8,128)S(1)}, u32[]{:S(2)}, u32[]{:S(2)}) collective-permute-start(f32[256,512]{1,0:T(8,128)S(1)} %get-tuple-element.87), channel_id=1, source_target_pairs={{0,2},{1,3},{2,4},{3,5},{4,6},{5,7},{6,0},{7,1},{8,10},{9,11},{10,... | collective-permute-start | bytes 1572872 | tf_op jit(solution)/shard_map/ppermute | solution.py:330
  106.1 13.7 %collective-permute-start.22 = (f32[256,512]{1,0:T(8,128)S(1)}, f32[256,512]{1,0:T(8,128)S(1)}, u32[]{:S(2)}, u32[]{:S(2)}) collective-permute-start(f32[256,512]{1,0:T(8,128)S(1)} %get-tuple-element.88), channel_id=1, source_target_pairs={{0,6},{1,7},{2,0},{3,1},{4,2},{5,3},{6,4},{7,5},{8,14},{9,15},{10,... | collective-permute-start | bytes 1572872 | tf_op jit(solution)/shard_map/ppermute | solution.py:330
  119.8 3.5 %collective-permute-start.25 = (f32[512,512]{1,0:T(8,128)S(1)}, f32[512,512]{1,0:T(8,128)S(1)}, u32[]{:S(2)}, u32[]{:S(2)}) collective-permute-start(f32[512,512]{1,0:T(8,128)S(1)} %shard_map.77.own), channel_id=1, source_target_pairs={{0,1},{1,0},{2,3},{3,2},{4,5},{5,4},{6,7},{7,6},{8,9},{9,8},{10,11... | collective-permute-start | bytes 3145736 | tf_op jit(solution)/shard_map/ppermute | solution.py:340
  120.0 15.6 %collective-permute-start.23 = (f32[256,512]{1,0:T(8,128)S(1)}, f32[256,512]{1,0:T(8,128)S(1)}, u32[]{:S(2)}, u32[]{:S(2)}) collective-permute-start(f32[256,512]{1,0:T(8,128)S(1)} %get-tuple-element.93), channel_id=1, source_target_pairs={{0,2},{1,3},{2,4},{3,5},{4,6},{5,7},{6,0},{7,1},{8,10},{9,11},{10,... | collective-permute-start | bytes 1572872 | tf_op jit(solution)/shard_map/ppermute | solution.py:330
  121.7 14.1 %collective-permute-start.24 = (f32[256,512]{1,0:T(8,128)S(1)}, f32[256,512]{1,0:T(8,128)S(1)}, u32[]{:S(2)}, u32[]{:S(2)}) collective-permute-start(f32[256,512]{1,0:T(8,128)S(1)} %get-tuple-element.94), channel_id=1, source_target_pairs={{0,6},{1,7},{2,0},{3,1},{4,2},{5,3},{6,4},{7,5},{8,14},{9,15},{10,... | collective-permute-start | bytes 1572872 | tf_op jit(solution)/shard_map/ppermute | solution.py:330
  135.7 16.0 %collective-permute-start.28 = (f32[256,512]{1,0:T(8,128)S(1)}, f32[256,512]{1,0:T(8,128)S(1)}, u32[]{:S(2)}, u32[]{:S(2)}) collective-permute-start(f32[256,512]{1,0:T(8,128)S(1)} %get-tuple-element.101), channel_id=1, source_target_pairs={{0,2},{1,3},{2,4},{3,5},{4,6},{5,7},{6,0},{7,1},{8,10},{9,11},{10,... | collective-permute-start | bytes 1572872 | tf_op jit(solution)/shard_map/ppermute | solution.py:330
  137.1 24.3 %copy-start.5 = (f32[3,256,512]{2,1,0:T(8,128)S(1)}, f32[3,256,512]{2,1,0:T(8,128)}, u32[]{:S(2)}) copy-start(f32[3,256,512]{2,1,0:T(8,128)} %get-tuple-element.104) | copy-start | bytes 4718596
  137.1 27.9 %collective-permute-start.27 = (f32[256,512]{1,0:T(8,128)S(1)}, f32[256,512]{1,0:T(8,128)S(1)}, u32[]{:S(2)}, u32[]{:S(2)}) collective-permute-start(f32[256,512]{1,0:T(8,128)S(1)} %bitcast_add_fusion.7), channel_id=1, source_target_pairs={{0,6},{1,7},{2,0},{3,1},{4,2},{5,3},{6,4},{7,5},{8,14},{9,15},{10,... | collective-permute-start | bytes 1572872 | tf_op jit(solution)/shard_map/ppermute | solution.py:330
  139.1 22.2 %collective-permute-start.31 = (f32[256,512]{1,0:T(8,128)S(1)}, f32[256,512]{1,0:T(8,128)S(1)}, u32[]{:S(2)}, u32[]{:S(2)}) collective-permute-start(f32[256,512]{1,0:T(8,128)S(1)} %get-tuple-element.103), channel_id=1, source_target_pairs={{0,6},{1,7},{2,0},{3,1},{4,2},{5,3},{6,4},{7,5},{8,14},{9,15},{10,... | collective-permute-start | bytes 1572872 | tf_op jit(solution)/shard_map/ppermute | solution.py:330
  141.0 37.7 %collective-permute-start.26 = (f32[256,512]{1,0:T(8,128)S(1)}, f32[256,512]{1,0:T(8,128)S(1)}, u32[]{:S(2)}, u32[]{:S(2)}) collective-permute-start(f32[256,512]{1,0:T(8,128)S(1)} %bitcast_add_fusion.9), channel_id=1, source_target_pairs={{0,2},{1,3},{2,4},{3,5},{4,6},{5,7},{6,0},{7,1},{8,10},{9,11},{10,... | collective-permute-start | bytes 1572872 | tf_op jit(solution)/shard_map/ppermute | solution.py:330
  151.8 21.1 %collective-permute-start.29 = (f32[256,512]{1,0:T(8,128)S(1)}, f32[256,512]{1,0:T(8,128)S(1)}, u32[]{:S(2)}, u32[]{:S(2)}) collective-permute-start(f32[256,512]{1,0:T(8,128)S(1)} %bitcast_add_fusion.5), channel_id=1, source_target_pairs={{0,2},{1,3},{2,4},{3,5},{4,6},{5,7},{6,0},{7,1},{8,10},{9,11},{10,... | collective-permute-start | bytes 1572872 | tf_op jit(solution)/shard_map/ppermute | solution.py:330
  161.4 13.4 %collective-permute-start.32 = (f32[256,512]{1,0:T(8,128)S(1)}, f32[256,512]{1,0:T(8,128)S(1)}, u32[]{:S(2)}, u32[]{:S(2)}) collective-permute-start(f32[256,512]{1,0:T(8,128)S(1)} %bitcast_add_fusion.2), channel_id=1, source_target_pairs={{0,6},{1,7},{2,0},{3,1},{4,2},{5,3},{6,4},{7,5},{8,14},{9,15},{10,... | collective-permute-start | bytes 1572872 | tf_op jit(solution)/shard_map/ppermute | solution.py:330
  173.0 13.9 %collective-permute-start.30 = (f32[256,512]{1,0:T(8,128)S(1)}, f32[256,512]{1,0:T(8,128)S(1)}, u32[]{:S(2)}, u32[]{:S(2)}) collective-permute-start(f32[256,512]{1,0:T(8,128)S(1)} %bitcast_add_fusion.4), channel_id=1, source_target_pairs={{0,2},{1,3},{2,4},{3,5},{4,6},{5,7},{6,0},{7,1},{8,10},{9,11},{10,... | collective-permute-start | bytes 1572872 | tf_op jit(solution)/shard_map/ppermute | solution.py:330
  174.9 12.7 %collective-permute-start.33 = (f32[256,512]{1,0:T(8,128)S(1)}, f32[256,512]{1,0:T(8,128)S(1)}, u32[]{:S(2)}, u32[]{:S(2)}) collective-permute-start(f32[256,512]{1,0:T(8,128)S(1)} %bitcast_add_fusion.1), channel_id=1, source_target_pairs={{0,6},{1,7},{2,0},{3,1},{4,2},{5,3},{6,4},{7,5},{8,14},{9,15},{10,... | collective-permute-start | bytes 1572872 | tf_op jit(solution)/shard_map/ppermute | solution.py:330
  187.7 1.6 copy-start.1

commit v4 on v3

--- a/solution.py
+++ b/solution.py
@@ -64,21 +64,35 @@
     return x[:half] + x[half:]
 
 
-def attend_kernel(
-    start, first_row, back, wraps, q, k_far, k_far_wrap, k_left, k_left_wrap, k_own,
-    v_far_a, v_far_b, v_left, v_own, k_a, k_b, v_a, v_b, vert_pos, slash_pos, out,
-    near_k, near_v, vert_k, vert_v,
+def put_parts(target, first, pieces):
+    for piece in pieces:
+        count = piece.shape[0]
+        high, low = split(piece[...])
+        target[first : first + count, 0:HEAD_SIZE] = high
+        target[first : first + count, HEAD_SIZE:] = low
+        first += count
+
+
+dot = functools.partial(lax.dot_general, preferred_element_type=jnp.float32)
+ACROSS = (((1,), (1,)), ((), ()))
+DOWN = (((1,), (0,)), ((), ()))
+SCALE = math.log2(math.e) / math.sqrt(HEAD_SIZE)
+
+
+def query_parts(q):
+    return (jnp.concatenate([x, x], axis=1) for x in split(q * SCALE))
+
+
+def weights_of(scores, top):
+    weights = jnp.exp2(scores - top)
+    return weights, jnp.sum(weights, axis=1, keepdims=True)
+
+
+def near_kernel(
+    first_row, back, wraps, q, k_far, k_far_wrap, k_left, k_left_wrap, k_own,
+    v_far_a, v_far_b, v_left, v_own, slash_pos, out, stats, near_k, near_v,
 ):
     turn = pl.program_id(0)
-    scale = 1.0 / math.sqrt(HEAD_SIZE)
-
-    def put(target, first, pieces):
-        for piece in pieces:
-            count = piece.shape[0]
-            high, low = split(piece[...])
-            target[first : first + count, 0:HEAD_SIZE] = high
-            target[first : first + count, HEAD_SIZE:] = low
-            first += count
 
     @pl.when((turn == 0) & (pl.program_id(1) == 0))
     def _():
@@ -87,104 +101,167 @@
 
             @pl.when(wraps[at] == 0)
             def _():
-                put(near_k, at * rows, (plain,))
+                put_parts(near_k, at * rows, (plain,))
 
             @pl.when(wraps[at] == 1)
             def _():
-                put(near_k, at * rows, (wrapped,))
-
-        put(near_k, 2 * rows, (k_own,))
-        put(near_v, 0, (v_far_a, v_far_b, v_left, v_own))
-        put(vert_k, 0, (k_a, k_b))
-        put(vert_v, 0, (v_a, v_b))
-
-    dot = functools.partial(lax.dot_general, preferred_element_type=jnp.float32)
-    across = (((1,), (1,)), ((), ()))
-    down = (((1,), (0,)), ((), ()))
+                put_parts(near_k, at * rows, (wrapped,))
+
+        put_parts(near_k, 2 * rows, (k_own,))
+        put_parts(near_v, 0, (v_far_a, v_far_b, v_left, v_own))
+
+    q_pos = first_row[0] + turn * TILE + lax.broadcasted_iota(jnp.int32, (TILE, 1), 0)
+    per_block = TILE // BLOCK
+    pair = q.shape[1] // HEAD_SIZE
+    lane = lax.broadcasted_iota(jnp.int32, (TILE, HEAD_SIZE), 1)
+    known = jnp.zeros((TILE, HEAD_SIZE), jnp.float32)
+    for part in range(pair):
+        head = pl.program_id(1) * pair + part
+        columns = slice(part * HEAD_SIZE, (part + 1) * HEAD_SIZE)
+        high, low = query_parts(q[:, columns])
+        scores, near = [], []
+        for j in range(per_block):
+            block = turn * per_block + j
+            spots = [
+                pl.ds(pl.multiple_of((block + back[head, n]) * BLOCK, BLOCK), BLOCK)
+                for n in range(4)
+            ]
+            near.append(spots)
+            keys = jnp.concatenate([near_k[s, :] for s in spots], axis=0)
+            mine = slice(j * BLOCK, (j + 1) * BLOCK)
+            score = fold(dot(jnp.concatenate([high[mine], low[mine]], axis=0), keys, ACROSS))
+            scores.append(jnp.where(slash_pos[head, block] <= q_pos[mine], score, LOW))
+        scores = jnp.concatenate(scores, axis=0)
+        top = jnp.max(scores, axis=1, keepdims=True)
+        weights, total = weights_of(scores, top)
+        w_high, w_low = split(weights)
+        parts = []
+        for j in range(per_block):
+            values = jnp.concatenate([near_v[s, :] for s in near[j]], axis=0)
+            mine = slice(j * BLOCK, (j + 1) * BLOCK)
+            stacked = jnp.concatenate([w_high[mine], w_low[mine]], axis=0)
+            parts.append(fold(dot(stacked, values, DOWN)))
+        mixed = jnp.concatenate(parts, axis=0)
+        out[:, columns] = mixed[:, :HEAD_SIZE] + mixed[:, HEAD_SIZE:]
+        known = jnp.where(lane == 2 * part, top, known)
+        known = jnp.where(lane == 2 * part + 1, total, known)
+    stats[...] = known
+
+
+def attend_near(q, first_row, back, wraps, arrays):
+    rows, width = q.shape
+    pair = 2
+    count = width // (pair * HEAD_SIZE)
+    smem = pl.BlockSpec(memory_space=pltpu.SMEM)
+    vmem = pl.BlockSpec(memory_space=pltpu.VMEM)
+    wide = pl.BlockSpec((TILE, pair * HEAD_SIZE), lambda t, h: (t, h))
+    return pl.pallas_call(
+        near_kernel,
+        grid=(rows // TILE, count),
+        out_shape=[
+            jax.ShapeDtypeStruct((rows, width), jnp.float32),
+            jax.ShapeDtypeStruct((rows, count * HEAD_SIZE), jnp.float32),
+        ],
+        in_specs=[smem, smem, smem, wide] + [vmem] * len(arrays),
+        out_specs=[wide, pl.BlockSpec((TILE, HEAD_SIZE), lambda t, h: (t, h))],
+        scratch_shapes=[pltpu.VMEM((3 * rows, 2 * HEAD_SIZE), jnp.bfloat16)] * 2,
+        compiler_params=pltpu.CompilerParams(vmem_limit_bytes=40 << 20),
+        cost_estimate=LARGE,
+    )(first_row, back, wraps, q, *arrays)
+
+
+def attend_kernel(
+    start, first_row, q, near, stats, k_a, k_b, v_a, v_b, vert_pos, out, vert_k, vert_v
+):
+    turn = pl.program_id(0)
+
+    @pl.when((turn == 0) & (pl.program_id(1) == 0))
+    def _():
+        put_parts(vert_k, 0, (k_a, k_b))
+        put_parts(vert_v, 0, (v_a, v_b))
+
     q_pos = first_row[0] + start + turn * TILE + lax.broadcasted_iota(jnp.int32, (TILE, 1), 0)
-    local = start // BLOCK + turn * (TILE // BLOCK)
-    per_block = TILE // BLOCK
     vert = vert_pos.shape[2]
     pair = q.shape[1] // HEAD_SIZE
     for part in range(pair):
         head = pl.program_id(1) * pair + part
         columns = slice(part * HEAD_SIZE, (part + 1) * HEAD_SIZE)
-        high, low = split(q[:, columns] * scale)
-        high, low = (jnp.concatenate([x, x], axis=1) for x in (high, low))
         rows = pl.ds(pl.multiple_of(head * vert, vert), vert)
-        both = jnp.concatenate([high, low], axis=0)
-        vert_scores = fold(dot(both, vert_k[rows, :], across))
-        vert_scores = jnp.where(vert_pos[head] <= q_pos, vert_scores, LOW)
-
-        slash_scores, near = [], []
-        for j in range(per_block):
-            spots = [
-                pl.ds(pl.multiple_of((local + j + back[head, n]) * BLOCK, BLOCK), BLOCK)
-                for n in range(4)
-            ]
-            near.append(spots)
-            keys = jnp.concatenate([near_k[s, :] for s in spots], axis=0)
-            mine = slice(j * BLOCK, (j + 1) * BLOCK)
-            score = fold(dot(jnp.concatenate([high[mine], low[mine]], axis=0), keys, across))
-            slash_scores.append(jnp.where(slash_pos[head, local + j] <= q_pos[mine], score, LOW))
-        slash_scores = jnp.concatenate(slash_scores, axis=0)
-
-        top = jnp.maximum(
-            jnp.max(vert_scores, axis=1, keepdims=True),
-            jnp.max(slash_scores, axis=1, keepdims=True),
-        )
-        vert_w = jnp.exp(vert_scores - top)
-        slash_w = jnp.exp(slash_scores - top)
-        total = jnp.sum(vert_w, axis=1, keepdims=True) + jnp.sum(slash_w, axis=1, keepdims=True)
-        mixed = fold(dot(jnp.concatenate(split(vert_w), axis=0), vert_v[rows, :], down))
-        slash_high, slash_low = split(slash_w)
-        parts = []
-        for j in range(per_block):
-            values = jnp.concatenate([near_v[s, :] for s in near[j]], axis=0)
-            mine = slice(j * BLOCK, (j + 1) * BLOCK)
-            weights = jnp.concatenate([slash_high[mine], slash_low[mine]], axis=0)
-            parts.append(fold(dot(weights, values, down)))
-        mixed = mixed + jnp.concatenate(parts, axis=0)
-        out[:, columns] = (mixed[:, :HEAD_SIZE] + mixed[:, HEAD_SIZE:]) / total
-
-
-def attend(q, start, rows, first_row, back, wraps, arrays):
-    heads = q.shape[1] // HEAD_SIZE
+        both = jnp.concatenate(list(query_parts(q[:, columns])), axis=0)
+        scores = fold(dot(both, vert_k[rows, :], ACROSS))
+        scores = jnp.where(vert_pos[head] <= q_pos, scores, LOW)
+        near_top = stats[:, 2 * part : 2 * part + 1]
+        top = jnp.maximum(jnp.max(scores, axis=1, keepdims=True), near_top)
+        weights, total = weights_of(scores, top)
+        keep = jnp.exp2(near_top - top)
+        total = total + keep * stats[:, 2 * part + 1 : 2 * part + 2]
+        mixed = fold(dot(jnp.concatenate(split(weights), axis=0), vert_v[rows, :], DOWN))
+        mixed = mixed[:, :HEAD_SIZE] + mixed[:, HEAD_SIZE:] + keep * near[:, columns]
+        out[:, columns] = mixed / total
+
+
+def attend(q, near, stats, start, rows, first_row, arrays):
+    width = q.shape[1]
+    heads = width // HEAD_SIZE
     pair = 2
     smem = pl.BlockSpec(memory_space=pltpu.SMEM)
     vmem = pl.BlockSpec(memory_space=pltpu.VMEM)
-    near, vert = 3 * q.shape[0], heads * 8 * BLOCK
     base = start // TILE
+    wide = pl.BlockSpec((TILE, pair * HEAD_SIZE), lambda t, h: (base + t, h))
     return pl.pallas_call(
         functools.partial(attend_kernel, start),
         grid=(rows // TILE, heads // pair),
-        out_shape=jax.ShapeDtypeStruct((rows, heads * HEAD_SIZE), jnp.float32),
-        in_specs=[smem, smem, smem]
-        + [pl.BlockSpec((TILE, pair * HEAD_SIZE), lambda t, h: (base + t, h))]
+        out_shape=jax.ShapeDtypeStruct((rows, width), jnp.float32),
+        in_specs=[smem, wide, wide, pl.BlockSpec((TILE, HEAD_SIZE), lambda t, h: (base + t, h))]
         + [vmem] * len(arrays),
         out_specs=pl.BlockSpec((TILE, pair * HEAD_SIZE), lambda t, h: (t, h)),
-        scratch_shapes=[
-            pltpu.VMEM((n, 2 * HEAD_SIZE), jnp.bfloat16) for n in (near, near, vert, vert)
-        ],
+        scratch_shapes=[pltpu.VMEM((heads * 8 * BLOCK, 2 * HEAD_SIZE), jnp.bfloat16)] * 2,
         compiler_params=pltpu.CompilerParams(vmem_limit_bytes=40 << 20),
         cost_estimate=LARGE,
-    )(first_row, back, wraps, q, *arrays)
-
-
-def project_kernel(order, own, other, w_own, w_other, first_a, rest_a, first_b, rest_b, x, w):
-    rows, depth = own.shape
+    )(first_row, q, near, stats, *arrays)
+
+
+def halves_kernel(order, own, other, out):
+    rows = own.shape[0]
+    for first, ref in ((0, own), (rows, other)):
+        high, low = split(ref[...])
+        out[0, first : first + rows] = high
+        out[0, first + 2 * rows : first + 3 * rows] = low
+
+
+def weight_halves(own, other, order):
+    rows = own.shape[0]
+    count = order.shape[0]
+    width = own.shape[1] // (2 * count)
+    w_spec = pl.BlockSpec((rows, width), lambda i, o: (0, o[i]))
+    return pl.pallas_call(
+        halves_kernel,
+        out_shape=jax.ShapeDtypeStruct((count, 4 * rows, width), jnp.bfloat16),
+        grid_spec=pltpu.PrefetchScalarGridSpec(
+            num_scalar_prefetch=1,
+            grid=(count,),
+            in_specs=[w_spec, w_spec],
+            out_specs=pl.BlockSpec((1, 4 * rows, width), lambda i, o: (i, 0, 0)),
+        ),
+        compiler_params=pltpu.CompilerParams(vmem_limit_bytes=24 << 20),
+        cost_estimate=LARGE,
+    )(order, own, other)
+
+
+def project_kernel(own, other, w, first_a, rest_a, first_b, rest_b, x):
+    depth = own.shape[1]
     half = first_a.shape[0]
     step = pl.program_id(0)
 
     @pl.when(step == 0)
     def _():
         for at, ref in ((0, own), (depth, other)):
-            x[0:rows, at : at + depth], x[rows:, at : at + depth] = split(ref[...])
-
-    for at, ref in ((0, w_own), (depth, w_other)):
-        w[0, at : at + depth, :], w[1, at : at + depth, :] = split(ref[...])
-    dot = functools.partial(jnp.dot, preferred_element_type=jnp.float32)
-    term = fold(dot(x[...], w[0])) + dot(x[0:rows, :], w[1])
+            high, low = split(ref[...])
+            x[:, at : at + depth] = high
+            x[:, at + 2 * depth : at + 3 * depth] = high
+            x[:, at + 4 * depth : at + 5 * depth] = low
+
+    term = dot(x[:, : 4 * depth], w[0], DOWN) + dot(x[:, 4 * depth :], w[0, : 2 * depth], DOWN)
 
     @pl.when(step == 0)
     def _():
@@ -203,38 +280,30 @@
         rest_b[0] = term[half:]
 
 
-def project(own, other, w_own, w_other, order):
+def project(own, other, weights):
     rows, depth = own.shape
     half = rows // 2
-    count = order.shape[0]
-    width = w_own.shape[1] // (2 * count)
-    x_spec = pl.BlockSpec((rows, depth), lambda i, o: (0, 0))
-    w_spec = pl.BlockSpec((depth, width), lambda i, o: (0, o[i]))
+    count, _, width = weights.shape
+    x_spec = pl.BlockSpec((rows, depth), lambda i: (0, 0))
     first = jax.ShapeDtypeStruct((half, width), jnp.float32)
     rest = jax.ShapeDtypeStruct((count - 1, half, width), jnp.float32)
-    first_spec = pl.BlockSpec((half, width), lambda i, o: (0, 0))
+    first_spec = pl.BlockSpec((half, width), lambda i: (0, 0))
     back_step = lambda i: jnp.where(i == 0, 1, jnp.where(i == 3, 2, 0))
     first_a, rest_a, first_b, rest_b = pl.pallas_call(
         project_kernel,
+        grid=(count,),
         out_shape=[first, rest, first, rest],
-        grid_spec=pltpu.PrefetchScalarGridSpec(
-            num_scalar_prefetch=1,
-            grid=(count,),
-            in_specs=[x_spec, x_spec, w_spec, w_spec],
-            out_specs=[
-                first_spec,
-                pl.BlockSpec((1, half, width), lambda i, o: (jnp.maximum(i - 1, 0), 0, 0)),
-                first_spec,
-                pl.BlockSpec((1, half, width), lambda i, o: (back_step(i), 0, 0)),
-            ],
-            scratch_shapes=[
-                pltpu.VMEM((2 * rows, 2 * depth), jnp.bfloat16),
-                pltpu.VMEM((2, 2 * depth, width), jnp.bfloat16),
-            ],
-        ),
+        in_specs=[x_spec, x_spec, pl.BlockSpec((1, 4 * depth, width), lambda i: (i, 0, 0))],
+        out_specs=[
+            first_spec,
+            pl.BlockSpec((1, half, width), lambda i: (jnp.maximum(i - 1, 0), 0, 0)),
+            first_spec,
+            pl.BlockSpec((1, half, width), lambda i: (back_step(i), 0, 0)),
+        ],
+        scratch_shapes=[pltpu.VMEM((rows, 6 * depth), jnp.bfloat16)],
         compiler_params=pltpu.CompilerParams(vmem_limit_bytes=48 << 20),
         cost_estimate=LARGE,
-    )(order, own, other, w_own, w_other)
+    )(own, other, weights)
     return (first_a, first_b), (rest_a, rest_b)
 
 
@@ -317,31 +386,35 @@
     k_far_wrap = send(k_far, [(i, i + 4) for i in ids if i % 4 < 2 and i + 4 in ids])
     named = [*k_named, *v_named]
     one, two = (4, 12, 1, 3), (12, 4, 3, 1)
-    named = [a + swapped(a, bits) for a, bits in zip(named, one)]
-    v_far_a, v_far_b, k_far_wrap, *named = lax.optimization_barrier(
-        (v_far_a, v_far_b, k_far_wrap, *named)
+    more = [swapped(a, bits) for a, bits in zip(named, one)]
+    weights = weight_halves(out_weight, w_other, order)
+    weights, v_far_a, v_far_b, k_far_wrap, *more = lax.optimization_barrier(
+        (weights, v_far_a, v_far_b, k_far_wrap, *more)
     )
-    named = [a + swapped(a, bits) for a, bits in zip(named, two)]
-
+    named = [a + b for a, b in zip(named, more)]
     arrays = (k_far, k_far_wrap, k_left, k_left_wrap, key_rows, v_far_a, v_far_b, v_left)
-    arrays = (*arrays, value_vectors, *named, vert_pos, slash_pos)
+    arrays = (*arrays, value_vectors, slash_pos)
+    near, stats = attend_near(queries, first_row, back, wraps, arrays)
+    more = [swapped(a, bits) for a, bits in zip(named, two)]
+    near, stats, *more = lax.optimization_barrier((near, stats, *more))
+    arrays = (*(a + b for a, b in zip(named, more)), vert_pos)
 
     rings = [[(i, (i + d) % head_size) for i in range(head_size)] for d in (2, head_size - 2)]
     ring = lambda parts: [lax.ppermute(p, "head", r) for p, r in zip(parts, rings)]
     add = lambda parts, terms, step: [p + t[step] for p, t in zip(parts, terms)]
 
-    own = attend(queries, 0, half, first_row, back, wraps, arrays)
+    own = attend(queries, near, stats, 0, half, first_row, arrays)
     other = lax.ppermute(own, "head", swap)
-    first, terms = project(own, other, out_weight, w_other, order)
+    first, terms = project(own, other, weights)
     q, *first = lax.optimization_barrier((queries, *first))
     moved = ring(first)
-    own = attend(q, half, half, first_row, back, wraps, arrays)
+    own = attend(q, near, stats, half, half, first_row, arrays)
     own, *moved = lax.optimization_barrier((own, *moved))
     other = lax.ppermute(own, "head", swap)
     sums = add(moved, terms, 0)
-    order, *sums = lax.optimization_barrier((order, *sums))
+    weights, *sums = lax.optimization_barrier((weights, *sums))
     moved = ring(sums)
-    later, later_terms = project(own, other, out_weight, w_other, order)
+    later, later_terms = project(own, other, weights)
     *moved, later_a, later_b = lax.optimization_barrier((*moved, *later))
     sums, later = add(moved, terms, 1), (later_a, later_b)
     sums, later = add(ring(sums), terms, 2), add(ring(later), later_terms, 0)

time: 192 us -> 192 us (level)
  waiting for transfers between devices: 94.2 us -> 72.5 us
  starting transfers between devices: 43.9 us -> 53.3 us
  local copies, waits for them, and re-layouts: 1.65 us -> 8.31 us
  Pallas kernels: 42.9 us -> 49.1 us
    ppermute x19, waiting for transfers between devices: 49.2 us -> 23.2 us  [body(): send = lambda a, pairs: lax.ppermute(a, 'seq', pairs)]
    pallas_call x2 -> x4, Pallas kernels: 21.6 us -> 34.3 us  [the longest x2 20.5 us: project(): pl.pallas_call(project_kernel, grid=(count,), out_shape=[first, rest, fir...]
    ppermute x19, starting transfers between devices: 24.3 us -> 32.7 us  [body(): send = lambda a, pairs: lax.ppermute(a, 'seq', pairs)]
    unnamed x15 -> x19, local copies, waits for them, and re-layouts: 0.13 us -> 6.81 us
    pallas_call x2, Pallas kernels: 19 us -> 12.5 us  [attend(): pl.pallas_call(functools.partial(attend_kernel, start), grid=(rows // TIL...]
    ppermute x12, waiting for transfers between devices: 42.4 us -> 46.7 us  [body(): lax.ppermute(p, 'head', r)]
  transfers between devices with their start and end apart: 34 -> 34, of which waited for: 26 -> 15; matrix products, arithmetic and copies ran while one was open for 3% -> 3% of each run, Pallas kernels for 17% -> 17%
where the time goes in v4:
time: 192 us; the launch traced here: 190 us
  waiting for transfers between devices  72.5 us (38%)
  starting transfers between devices  53.3 us (28%)
  Pallas kernels  49.1 us (26%)
  local copies, waits for them, and re-layouts  8.31 us (4%)
  other arithmetic  5.62 us (3%)
    ppermute x12, waiting for transfers between devices, body(): lax.ppermute(p, 'head', r)  46.7 us
    ppermute x19, starting transfers between devices, body(): send = lambda a, pairs: lax.ppermute(a, 'seq', pairs)  32.7 us
    ppermute x19, waiting for transfers between devices, body(): send = lambda a, pairs: lax.ppermute(a, 'seq', pairs)  23.2 us
    ppermute x12, starting transfers between devices, body(): lax.ppermute(p, 'head', r)  20.5 us
    pallas_call x2, Pallas kernels, project(): pl.pallas_call(project_kernel, grid=(count,), out_shape=[first, rest, fir...  20.5 us
    pallas_call x2, Pallas kernels, attend(): pl.pallas_call(functools.partial(attend_kernel, start), grid=(rows // TIL...  12.5 us
    pallas_call x1, Pallas kernels, attend_near(): pl.pallas_call(near_kernel, grid=(rows // TILE, count), out_shape=[jax.Sh...  9.61 us
    unnamed x19, local copies, waits for them, and re-layouts  6.81 us
  transfers between devices with their start and end apart: 34, of which 15 were waited for; matrix products, arithmetic and copies ran while one was open for 3% of the time, Pallas kernels for 17%

profile of v4, /device:TPU:2, one launch (start us, length us, event | category | flops | bytes accessed | tf_op | source)
XLA Modules:
  0.0 190.0 jit_solution(11789028592598958813)
XLA Ops:
  0.0 1.6 collective-permute-start
  2.1 1.9 %collective-permute-start.2 = (f32[1024,128]{1,0:T(8,128)}, f32[1024,128]{1,0:T(8,128)S(1)}, u32[]{:S(2)}, u32[]{:S(2)}) collective-permute-start(f32[1024,128]{1,0:T(8,128)} %v_own.1), channel_id=1, source_target_pairs={{0,32},{8,40},{16,48},{24,56},{32,64},{40,72},{48,80},{56,88},{64,... | collective-permute-start | bytes 1572872 | tf_op jit(solution)/shard_map/ppermute | solution.py:329
  4.0 2.1 %collective-permute-start.3 = (f32[1024,128]{1,0:T(8,128)}, f32[1024,128]{1,0:T(8,128)S(1)}, u32[]{:S(2)}, u32[]{:S(2)}) collective-permute-start(f32[1024,128]{1,0:T(8,128)} %v_own.1), channel_id=1, source_target_pairs={{0,96},{8,104},{16,112},{24,120},{32,0},{40,8},{48,16},{56,24},{64... | collective-permute-start | bytes 1572872 | tf_op jit(solution)/shard_map/ppermute | solution.py:329
  6.1 0.8 broadcast_multiply_fusion
  9.7 4.8 %collective-permute-done.refs_3_.k_left = f32[1024,128]{1,0:T(8,128)S(1)} collective-permute-done((f32[1024,128]{1,0:T(8,128)}, f32[1024,128]{1,0:T(8,128)S(1)}, u32[]{:S(2)}, u32[]{:S(2)}) %collective-permute-start) | collective-permute-done | bytes 524320 | tf_op jit(solution)/shard_map/ppermute | solution.py:329
  14.6 1.2 collective-permute-done.1.refs_1_
  15.8 2.5 %collective-permute-done.2.refs_3_ = f32[1024,128]{1,0:T(8,128)S(1)} collective-permute-done((f32[1024,128]{1,0:T(8,128)}, f32[1024,128]{1,0:T(8,128)S(1)}, u32[]{:S(2)}, u32[]{:S(2)}) %collective-permute-start.2) | collective-permute-done | bytes 524320 | tf_op jit(solution)/shard_map/ppermute | solution.py:329
  18.3 1.1 broadcast_select_fusion
  19.5 1.8 collective-permute-start.5
  21.8 3.0 %collective-permute-start.6 = (f32[1024,128]{1,0:T(8,128)S(1)}, f32[1024,128]{1,0:T(8,128)S(1)}, u32[]{:S(2)}, u32[]{:S(2)}) collective-permute-start(f32[1024,128]{1,0:T(8,128)S(1)} %collective-permute-done.3.refs_1_), channel_id=1, source_target_pairs={{0,96},{8,104},{16,112},{24,120},{32,0},{40,8},{48,16},{56,24},{64... | collective-permute-start | bytes 1572872 | tf_op jit(solution)/shard_map/ppermute | solution.py:329
  24.7 0.7 collective-permute-start.8
  25.4 9.2 %collective-permute-done.6.refs_2_ = f32[1024,128]{1,0:T(8,128)S(1)} collective-permute-done((f32[1024,128]{1,0:T(8,128)S(1)}, f32[1024,128]{1,0:T(8,128)S(1)}, u32[]{:S(2)}, u32[]{:S(2)}) %collective-permute-start.6) | collective-permute-done | bytes 524320 | tf_op jit(solution)/shard_map/ppermute | solution.py:329
  34.6 3.8 %collective-permute-done.5 = f32[1536,128]{1,0:T(8,128)S(1)} collective-permute-done((f32[1536,128]{1,0:T(8,128)S(1)}, f32[1536,128]{1,0:T(8,128)S(1)}, u32[]{:S(2)}, u32[]{:S(2)}) %collective-permute-start.5) | collective-permute-done | bytes 786464 | tf_op jit(solution)/shard_map/ppermute | solution.py:329
  38.4 1.6 collective-permute-done.7
  40.4 2.6 %collective-permute-start.10 = (f32[512,128]{1,0:T(8,128)S(1)}, f32[512,128]{1,0:T(8,128)S(1)}, u32[]{:S(2)}, u32[]{:S(2)}) collective-permute-start(f32[512,128]{1,0:T(8,128)S(1)} %slice.57), channel_id=1, source_target_pairs={{0,24},{8,0},{16,8},{24,16},{32,56},{40,32},{48,40},{56,48},{64,88... | collective-permute-start | bytes 786440 | tf_op jit(solution)/shard_map/ppermute | solution.py:329
  43.0 2.6 %collective-permute-start.11 = (f32[1024,128]{1,0:T(8,128)S(1)}, f32[1024,128]{1,0:T(8,128)S(1)}, u32[]{:S(2)}, u32[]{:S(2)}) collective-permute-start(f32[1024,128]{1,0:T(8,128)S(1)} %slice.58.refs_2_.k_far), channel_id=1, source_target_pairs={{0,32},{8,40},{32,64},{40,72},{64,96},{72,104},{1,33},{9,41},{33,6... | collective-permute-start | bytes 1572872 | tf_op jit(solution)/shard_map/ppermute | solution.py:329
  45.6 1.2 shard_map.74
  46.8 1.2 shard_map.75
  48.0 1.7 collective-permute-start.12
  49.7 2.4 %collective-permute-start.13 = (f32[1024,128]{1,0:T(8,128)S(1)}, f32[1024,128]{1,0:T(8,128)S(1)}, u32[]{:S(2)}, u32[]{:S(2)}) collective-permute-start(f32[1024,128]{1,0:T(8,128)S(1)} %get-tuple-element.74), channel_id=1, source_target_pairs={{0,96},{8,104},{16,112},{24,120},{32,64},{40,72},{48,80},{56,88},{... | collective-permute-start | bytes 1572872 | tf_op jit(solution)/shard_map/ppermute | solution.py:329
  52.1 3.2 %collective-permute-start.14 = (f32[1024,128]{1,0:T(8,128)S(1)}, f32[1024,128]{1,0:T(8,128)S(1)}, u32[]{:S(2)}, u32[]{:S(2)}) collective-permute-start(f32[1024,128]{1,0:T(8,128)S(1)} %get-tuple-element.78), channel_id=1, source_target_pairs={{0,8},{8,0},{16,24},{24,16},{32,40},{40,32},{48,56},{56,48},{64,72... | collective-permute-start | bytes 1572872 | tf_op jit(solution)/shard_map/ppermute | solution.py:329
  55.3 3.4 %copy-done.4 = f32[512,4096]{1,0:T(8,128)S(1)} copy-done((f32[512,4096]{1,0:T(8,128)S(1)}, f32[512,4096]{1,0:T(8,128)}, u32[]{:S(2)}) %copy-start.4) | copy-done | bytes 8388632
  58.7 4.2 %shard_map.73.w = bf16[4,2048,512]{2,1,0:T(8,128)(2,1)S(1)} custom-call(s32[4]{0:T(128)S(1)} %fusion.2.order, f32[512,4096]{1,0:T(8,128)S(1)} %copy-done.4, f32[512,4096]{1,0:T(8,128)} %collective-permute-done.4.other), custom_call_target="tpu_custom_call" | custom-call | flops 12884901888 | bytes 16777216 | tf_op jit(solution)/shard_map/pallas_call | solution.py:237
  62.9 3.3 %copy-done.6 = bf16[4,2048,512]{2,1,0:T(8,128)(2,1)} copy-done((bf16[4,2048,512]{2,1,0:T(8,128)(2,1)}, bf16[4,2048,512]{2,1,0:T(8,128)(2,1)S(1)}, u32[]{:S(2)}) %copy-start.6) | copy-done | bytes 8388632
  66.3 4.3 %collective-permute-start.16 = (f32[1024,128]{1,0:T(8,128)S(1)}, f32[1024,128]{1,0:T(8,128)S(1)}, u32[]{:S(2)}, u32[]{:S(2)}) collective-permute-start(f32[1024,128]{1,0:T(8,128)S(1)} %add.211), channel_id=1, source_target_pairs={{0,96},{8,104},{16,112},{24,120},{32,64},{40,72},{48,80},{56,88},{... | collective-permute-start | bytes 1572872 | tf_op jit(solution)/shard_map/ppermute | solution.py:329
  71.1 3.5 %collective-permute-start.19 = (f32[1024,128]{1,0:T(8,128)S(1)}, f32[1024,128]{1,0:T(8,128)S(1)}, u32[]{:S(2)}, u32[]{:S(2)}) collective-permute-start(f32[1024,128]{1,0:T(8,128)S(1)} %add.214), channel_id=1, source_target_pairs={{0,8},{8,0},{16,24},{24,16},{32,40},{40,32},{48,56},{56,48},{64,72... | collective-permute-start | bytes 1572872 | tf_op jit(solution)/shard_map/ppermute | solution.py:329
  74.6 9.6 %shard_map.76 = (f32[1024,512]{1,0:T(8,128)S(1)}, f32[1024,256]{1,0:T(8,128)S(1)}) custom-call(s32[1]{0:T(128)} %bitcast.1.first_row, s32[4,4]{1,0:T(4,128)S(1)} %get-tuple-element.82.back, s32[2]{0:T(128)S(1)} %add_convert_fusion.wraps, f32[1024,512]{1,0:T(8,128)S(1)} %copy-done.5, f32[1024,128]{1,0:T(8,128)S(1)} %slice.58.refs_2_.k_far, ...), custom_call_target="tpu_custom_call" | custom-call | flops 12884901888 | bytes 16777216 | tf_op jit(solution)/shard_map/pallas_call | solution.py:158
  84.5 6.2 %shard_map.77.own = f32[512,512]{1,0:T(8,128)S(1)} custom-call(s32[1]{0:T(128)} %bitcast.1.first_row, f32[1024,512]{1,0:T(8,128)S(1)} %copy-done.5, f32[1024,512]{1,0:T(8,128)S(1)} %get-tuple-element.95.near, f32[1024,256]{1,0:T(8,128)S(1)} %get-tuple-element.96.stats, f32[1024,128]{1,0:T(8,128)S(1)} %add.215.k_a, f32[1024,128]{1,0:T(8,128)S(1)} %add.216.k_b, ...), custom_call_target="tpu_custom_call" | custom-call | flops 12884901888 | bytes 16777216 | tf_op jit(solution)/shard_map/pallas_call | solution.py:211
  90.8 2.6 %collective-permute-done.20.other = f32[512,512]{1,0:T(8,128)S(1)} collective-permute-done((f32[512,512]{1,0:T(8,128)S(1)}, f32[512,512]{1,0:T(8,128)S(1)}, u32[]{:S(2)}, u32[]{:S(2)}) %collective-permute-start.20) | collective-permute-done | bytes 1048608 | tf_op jit(solution)/shard_map/ppermute | solution.py:407
  93.5 10.2 %shard_map.78 = (f32[256,512]{1,0:T(8,128)S(1)}, f32[3,256,512]{2,1,0:T(8,128)S(1)}, f32[256,512]{1,0:T(8,128)S(1)}, f32[3,256,512]{2,1,0:T(8,128)}) custom-call(f32[512,512]{1,0:T(8,128)S(1)} %shard_map.77.own, f32[512,512]{1,0:T(8,128)S(1)} %collective-permute-done.20.other, bf16[4,2048,512]{2,1,0:T(8,128)(2,1)} %copy-done.6), custom_call_target="tpu_custom_call" | custom-call | flops 12884901888 | bytes 16777216 | tf_op jit(solution)/shard_map/pallas_call | solution.py:292
  103.7 1.6 collective-permute-start.21
  105.3 1.7 collective-permute-start.22
  106.9 6.2 %shard_map.79.own = f32[512,512]{1,0:T(8,128)S(1)} custom-call(s32[1]{0:T(128)} %bitcast.1.first_row, f32[1024,512]{1,0:T(8,128)S(1)} %copy-done.5, f32[1024,512]{1,0:T(8,128)S(1)} %get-tuple-element.95.near, f32[1024,256]{1,0:T(8,128)S(1)} %get-tuple-element.96.stats, f32[1024,128]{1,0:T(8,128)S(1)} %add.215.k_a, f32[1024,128]{1,0:T(8,128)S(1)} %add.216.k_b, ...), custom_call_target="tpu_custom_call" | custom-call | flops 12884901888 | bytes 16777216 | tf_op jit(solution)/shard_map/pallas_call | solution.py:211
  113.2 5.8 %collective-permute-done.21 = f32[256,512]{1,0:T(8,128)S(1)} collective-permute-done((f32[256,512]{1,0:T(8,128)S(1)}, f32[256,512]{1,0:T(8,128)S(1)}, u32[]{:S(2)}, u32[]{:S(2)}) %collective-permute-start.21) | collective-permute-done | bytes 524320 | tf_op jit(solution)/shard_map/ppermute | solution.py:403
  119.2 1.6 collective-permute-start.23
  120.8 1.7 collective-permute-start.24
  122.5 10.2 %shard_map.80 = (f32[256,512]{1,0:T(8,128)S(1)}, f32[3,256,512]{2,1,0:T(8,128)S(1)}, f32[256,512]{1,0:T(8,128)S(1)}, f32[3,256,512]{2,1,0:T(8,128)}) custom-call(f32[512,512]{1,0:T(8,128)S(1)} %shard_map.79.own, f32[512,512]{1,0:T(8,128)S(1)} %collective-permute-done.25.other, bf16[4,2048,512]{2,1,0:T(8,128)(2,1)} %copy-done.6), custom_call_target="tpu_custom_call" | custom-call | flops 12884901888 | bytes 16777216 | tf_op jit(solution)/shard_map/pallas_call | solution.py:292
  132.7 2.1 %collective-permute-done.23 = f32[256,512]{1,0:T(8,128)S(1)} collective-permute-done((f32[256,512]{1,0:T(8,128)S(1)}, f32[256,512]{1,0:T(8,128)S(1)}, u32[]{:S(2)}, u32[]{:S(2)}) %collective-permute-start.23) | collective-permute-done | bytes 524320 | tf_op jit(solution)/shard_map/ppermute | solution.py:403
  134.9 2.9 %collective-permute-start.31 = (f32[256,512]{1,0:T(8,128)S(1)}, f32[256,512]{1,0:T(8,128)S(1)}, u32[]{:S(2)}, u32[]{:S(2)}) collective-permute-start(f32[256,512]{1,0:T(8,128)S(1)} %get-tuple-element.121), channel_id=1, source_target_pairs={{0,6},{1,7},{2,0},{3,1},{4,2},{5,3},{6,4},{7,5},{8,14},{9,15},{10,... | collective-permute-start | bytes 1572872 | tf_op jit(solution)/shard_map/ppermute | solution.py:403
  137.9 3.3 %collective-permute-start.27 = (f32[256,512]{1,0:T(8,128)S(1)}, f32[256,512]{1,0:T(8,128)S(1)}, u32[]{:S(2)}, u32[]{:S(2)}) collective-permute-start(f32[256,512]{1,0:T(8,128)S(1)} %bitcast_add_fusion.7), channel_id=1, source_target_pairs={{0,6},{1,7},{2,0},{3,1},{4,2},{5,3},{6,4},{7,5},{8,14},{9,15},{10,... | collective-permute-start | bytes 1572872 | tf_op jit(solution)/shard_map/ppermute | solution.py:403
  141.4 8.8 %collective-permute-done.31 = f32[256,512]{1,0:T(8,128)S(1)} collective-permute-done((f32[256,512]{1,0:T(8,128)S(1)}, f32[256,512]{1,0:T(8,128)S(1)}, u32[]{:S(2)}, u32[]{:S(2)}) %collective-permute-start.31) | collective-permute-done | bytes 524320 | tf_op jit(solution)/shard_map/ppermute | solution.py:403
  150.3 3.8 %collective-permute-start.32 = (f32[256,512]{1,0:T(8,128)S(1)}, f32[256,512]{1,0:T(8,128)S(1)}, u32[]{:S(2)}, u32[]{:S(2)}) collective-permute-start(f32[256,512]{1,0:T(8,128)S(1)} %bitcast_add_fusion.2), channel_id=1, source_target_pairs={{0,6},{1,7},{2,0},{3,1},{4,2},{5,3},{6,4},{7,5},{8,14},{9,15},{10,... | collective-permute-start | bytes 1572872 | tf_op jit(solution)/shard_map/ppermute | solution.py:403
  154.2 7.2 %collective-permute-done.27 = f32[256,512]{1,0:T(8,128)S(1)} collective-permute-done((f32[256,512]{1,0:T(8,128)S(1)}, f32[256,512]{1,0:T(8,128)S(1)}, u32[]{:S(2)}, u32[]{:S(2)}) %collective-permute-start.27) | collective-permute-done | bytes 524320 | tf_op jit(solution)/shard_map/ppermute | solution.py:403
  161.5 9.6 %collective-permute-done.32 = f32[256,512]{1,0:T(8,128)S(1)} collective-permute-done((f32[256,512]{1,0:T(8,128)S(1)}, f32[256,512]{1,0:T(8,128)S(1)}, u32[]{:S(2)}, u32[]{:S(2)}) %collective-permute-start.32) | collective-permute-done | bytes 524320 | tf_op jit(solution)/shard_map/ppermute | solution.py:403
  171.2 3.8 %collective-permute-start.33 = (f32[256,512]{1,0:T(8,128)S(1)}, f32[256,512]{1,0:T(8,128)S(1)}, u32[]{:S(2)}, u32[]{:S(2)}) collective-permute-start(f32[256,512]{1,0:T(8,128)S(1)} %bitcast_add_fusion.1), channel_id=1, source_target_pairs={{0,6},{1,7},{2,0},{3,1},{4,2},{5,3},{6,4},{7,5},{8,14},{9,15},{10,... | collective-permute-start | bytes 1572872 | tf_op jit(solution)/shard_map/ppermute | solution.py:403
  175.2 9.6 %collective-permute-done.33 = f32[256,512]{1,0:T(8,128)S(1)} collective-permute-done((f32[256,512]{1,0:T(8,128)S(1)}, f32[256,512]{1,0:T(8,128)S(1)}, u32[]{:S(2)}, u32[]{:S(2)}) %collective-permute-start.33) | collective-permute-done | bytes 524320 | tf_op jit(solution)/shard_map/ppermute | solution.py:403
  184.9 3.5 %collective-permute-done.30 = f32[256,512]{1,0:T(8,128)S(1)} collective-permute-done((f32[256,512]{1,0:T(8,128)S(1)}, f32[256,512]{1,0:T(8,128)S(1)}, u32[]{:S(2)}, u32[]{:S(2)}) %collective-permute-start.30) | collective-permute-done | bytes 524320 | tf_op jit(solution)/shard_map/ppermute | solution.py:403
  188.5 1.5 pad_maximum_fusion
  (105 shorter events, 5.8 us)
Async XLA Ops:
  0.0 8.0 %copy-start = (s32[32,3]{0,1:T(4,128)S(1)}, s32[32,3]{0,1:T(4,128)}, u32[]{:S(2)}) copy-start(s32[32,3]{0,1:T(4,128)} %param.11) | copy-start | bytes 1156
  0.0 55.3 %collective-permute-start.4 = (f32[512,4096]{1,0:T(8,128)}, f32[512,4096]{1,0:T(8,128)}, u32[]{:S(2)}, u32[]{:S(2)}) collective-permute-start(f32[512,4096]{1,0:T(8,128)} %own.1), channel_id=1, source_target_pairs={{0,1},{1,0},{2,3},{3,2},{4,5},{5,4},{6,7},{7,6},{8,9},{9,8},{10,11... | collective-permute-start | bytes 25165832 | tf_op jit(solution)/shard_map/ppermute | solution.py:337
  0.0 14.5 %collective-permute-start = (f32[1024,128]{1,0:T(8,128)}, f32[1024,128]{1,0:T(8,128)S(1)}, u32[]{:S(2)}, u32[]{:S(2)}) collective-permute-start(f32[1024,128]{1,0:T(8,128)} %k_own.1), channel_id=1, source_target_pairs={{0,8},{8,16},{16,24},{24,0},{32,40},{40,48},{48,56},{56,32},{64,72... | collective-permute-start | bytes 1572872 | tf_op jit(solution)/shard_map/ppermute | solution.py:329
  1.6 14.2 %collective-permute-start.1 = (f32[1024,128]{1,0:T(8,128)}, f32[1024,128]{1,0:T(8,128)S(1)}, u32[]{:S(2)}, u32[]{:S(2)}) collective-permute-start(f32[1024,128]{1,0:T(8,128)} %k_own.1), channel_id=1, source_target_pairs={{0,24},{8,0},{16,8},{24,16},{32,56},{40,32},{48,40},{56,48},{64,88... | collective-permute-start | bytes 1572872 | tf_op jit(solution)/shard_map/ppermute | solution.py:329
  2.1 16.2 %collective-permute-start.2 = (f32[1024,128]{1,0:T(8,128)}, f32[1024,128]{1,0:T(8,128)S(1)}, u32[]{:S(2)}, u32[]{:S(2)}) collective-permute-start(f32[1024,128]{1,0:T(8,128)} %v_own.1), channel_id=1, source_target_pairs={{0,32},{8,40},{16,48},{24,56},{32,64},{40,72},{48,80},{56,88},{64,... | collective-permute-start | bytes 1572872 | tf_op jit(solution)/shard_map/ppermute | solution.py:329
  4.0 14.3 %collective-permute-start.3 = (f32[1024,128]{1,0:T(8,128)}, f32[1024,128]{1,0:T(8,128)S(1)}, u32[]{:S(2)}, u32[]{:S(2)}) collective-permute-start(f32[1024,128]{1,0:T(8,128)} %v_own.1), channel_id=1, source_target_pairs={{0,96},{8,104},{16,112},{24,120},{32,0},{40,8},{48,16},{56,24},{64... | collective-permute-start | bytes 1572872 | tf_op jit(solution)/shard_map/ppermute | solution.py:329
  19.5 18.8 %collective-permute-start.5 = (f32[1536,128]{1,0:T(8,128)S(1)}, f32[1536,128]{1,0:T(8,128)S(1)}, u32[]{:S(2)}, u32[]{:S(2)}) collective-permute-start(f32[1536,128]{1,0:T(8,128)S(1)} %pad_maximum_fusion.1), channel_id=1, source_target_pairs={{0,24},{8,0},{16,8},{24,16},{32,56},{40,32},{48,40},{56,48},{64,88... | collective-permute-start | bytes 2359304 | tf_op jit(solution)/shard_map/ppermute | solution.py:329
  21.4 24.2 %copy-start.3 = (f32[1024,128]{1,0:T(8,128)S(1)}, f32[1024,128]{1,0:T(8,128)}, u32[]{:S(2)}) copy-start(f32[1024,128]{1,0:T(8,128)} %k_own.1) | copy-start | bytes 1572868
  21.4 18.6 %collective-permute-start.7 = (f32[1536,128]{1,0:T(8,128)S(1)}, f32[1536,128]{1,0:T(8,128)S(1)}, u32[]{:S(2)}, u32[]{:S(2)}) collective-permute-start(f32[1536,128]{1,0:T(8,128)S(1)} %pad_maximum_fusion.2), channel_id=1, source_target_pairs={{0,8},{8,16},{16,24},{24,0},{32,40},{40,48},{48,56},{56,32},{64,72... | collective-permute-start | bytes 2359304 | tf_op jit(solution)/shard_map/ppermute | solution.py:329
  21.8 12.8 %collective-permute-start.6 = (f32[1024,128]{1,0:T(8,128)S(1)}, f32[1024,128]{1,0:T(8,128)S(1)}, u32[]{:S(2)}, u32[]{:S(2)}) collective-permute-start(f32[1024,128]{1,0:T(8,128)S(1)} %collective-permute-done.3.refs_1_), channel_id=1, source_target_pairs={{0,96},{8,104},{16,112},{24,120},{32,0},{40,8},{48,16},{56,24},{64... | collective-permute-start | bytes 1572872 | tf_op jit(solution)/shard_map/ppermute | solution.py:329
  24.7 9.9 %collective-permute-start.8 = (f32[1024,128]{1,0:T(8,128)S(1)}, f32[1024,128]{1,0:T(8,128)S(1)}, u32[]{:S(2)}, u32[]{:S(2)}) collective-permute-start(f32[1024,128]{1,0:T(8,128)S(1)} %collective-permute-done.refs_3_.k_left), channel_id=1, source_target_pairs={{0,32},{32,64},{64,96},{1,33},{33,65},{65,97},{2,34},{34,66},{66,9... | collective-permute-start | bytes 1572872 | tf_op jit(solution)/shard_map/ppermute | solution.py:329
  40.0 9.7 %collective-permute-start.9 = (f32[512,128]{1,0:T(8,128)S(1)}, f32[512,128]{1,0:T(8,128)S(1)}, u32[]{:S(2)}, u32[]{:S(2)}) collective-permute-start(f32[512,128]{1,0:T(8,128)S(1)} %slice.56), channel_id=1, source_target_pairs={{0,8},{8,16},{16,24},{24,0},{32,40},{40,48},{48,56},{56,32},{64,72... | collective-permute-start | bytes 786440 | tf_op jit(solution)/shard_map/ppermute | solution.py:329
  40.4 6.4 %copy-start.2 = (f32[1024,128]{1,0:T(8,128)S(1)}, f32[1024,128]{1,0:T(8,128)}, u32[]{:S(2)}) copy-start(f32[1024,128]{1,0:T(8,128)} %v_own.1) | copy-start | bytes 1572868
  40.4 11.7 %collective-permute-start.10 = (f32[512,128]{1,0:T(8,128)S(1)}, f32[512,128]{1,0:T(8,128)S(1)}, u32[]{:S(2)}, u32[]{:S(2)}) collective-permute-start(f32[512,128]{1,0:T(8,128)S(1)} %slice.57), channel_id=1, source_target_pairs={{0,24},{8,0},{16,8},{24,16},{32,56},{40,32},{48,40},{56,48},{64,88... | collective-permute-start | bytes 786440 | tf_op jit(solution)/shard_map/ppermute | solution.py:329
  43.0 23.3 %collective-permute-start.11 = (f32[1024,128]{1,0:T(8,128)S(1)}, f32[1024,128]{1,0:T(8,128)S(1)}, u32[]{:S(2)}, u32[]{:S(2)}) collective-permute-start(f32[1024,128]{1,0:T(8,128)S(1)} %slice.58.refs_2_.k_far), channel_id=1, source_target_pairs={{0,32},{8,40},{32,64},{40,72},{64,96},{72,104},{1,33},{9,41},{33,6... | collective-permute-start | bytes 1572872 | tf_op jit(solution)/shard_map/ppermute | solution.py:329
  48.0 18.2 %collective-permute-start.12 = (f32[1024,128]{1,0:T(8,128)S(1)}, f32[1024,128]{1,0:T(8,128)S(1)}, u32[]{:S(2)}, u32[]{:S(2)}) collective-permute-start(f32[1024,128]{1,0:T(8,128)S(1)} %get-tuple-element.73), channel_id=1, source_target_pairs={{0,32},{8,40},{16,48},{24,56},{32,0},{40,8},{48,16},{56,24},{64,96... | collective-permute-start | bytes 1572872 | tf_op jit(solution)/shard_map/ppermute | solution.py:329
  49.7 16.6 %collective-permute-start.13 = (f32[1024,128]{1,0:T(8,128)S(1)}, f32[1024,128]{1,0:T(8,128)S(1)}, u32[]{:S(2)}, u32[]{:S(2)}) collective-permute-start(f32[1024,128]{1,0:T(8,128)S(1)} %get-tuple-element.74), channel_id=1, source_target_pairs={{0,96},{8,104},{16,112},{24,120},{32,64},{40,72},{48,80},{56,88},{... | collective-permute-start | bytes 1572872 | tf_op jit(solution)/shard_map/ppermute | solution.py:329
  52.1 14.1 %collective-permute-start.14 = (f32[1024,128]{1,0:T(8,128)S(1)}, f32[1024,128]{1,0:T(8,128)S(1)}, u32[]{:S(2)}, u32[]{:S(2)}) collective-permute-start(f32[1024,128]{1,0:T(8,128)S(1)} %get-tuple-element.78), channel_id=1, source_target_pairs={{0,8},{8,0},{16,24},{24,16},{32,40},{40,32},{48,56},{56,48},{64,72... | collective-permute-start | bytes 1572872 | tf_op jit(solution)/shard_map/ppermute | solution.py:329
  55.3 10.9 %collective-permute-start.15 = (f32[1024,128]{1,0:T(8,128)S(1)}, f32[1024,128]{1,0:T(8,128)S(1)}, u32[]{:S(2)}, u32[]{:S(2)}) collective-permute-start(f32[1024,128]{1,0:T(8,128)S(1)} %get-tuple-element.79), channel_id=1, source_target_pairs={{0,24},{8,16},{16,8},{24,0},{32,56},{40,48},{48,40},{56,32},{64,88... | collective-permute-start | bytes 1572872 | tf_op jit(solution)/shard_map/ppermute | solution.py:329
  55.3 3.4 %copy-start.4 = (f32[512,4096]{1,0:T(8,128)S(1)}, f32[512,4096]{1,0:T(8,128)}, u32[]{:S(2)}) copy-start(f32[512,4096]{1,0:T(8,128)} %own.1) | copy-start | bytes 25165828
  62.9 3.3 %copy-start.6 = (bf16[4,2048,512]{2,1,0:T(8,128)(2,1)}, bf16[4,2048,512]{2,1,0:T(8,128)(2,1)S(1)}, u32[]{:S(2)}) copy-start(bf16[4,2048,512]{2,1,0:T(8,128)(2,1)S(1)} %shard_map.73.w) | copy-start | bytes 25165828
  66.3 17.8 %collective-permute-start.16 = (f32[1024,128]{1,0:T(8,128)S(1)}, f32[1024,128]{1,0:T(8,128)S(1)}, u32[]{:S(2)}, u32[]{:S(2)}) collective-permute-start(f32[1024,128]{1,0:T(8,128)S(1)} %add.211), channel_id=1, source_target_pairs={{0,96},{8,104},{16,112},{24,120},{32,64},{40,72},{48,80},{56,88},{... | collective-permute-start | bytes 1572872 | tf_op jit(solution)/shard_map/ppermute | solution.py:329
  70.7 3.8 %copy-start.5 = (f32[1024,512]{1,0:T(8,128)S(1)}, f32[1024,512]{1,0:T(8,128)}, u32[]{:S(2)}) copy-start(f32[1024,512]{1,0:T(8,128)} %q.4) | copy-start | bytes 6291460
  70.7 13.5 %collective-permute-start.17 = (f32[1024,128]{1,0:T(8,128)S(1)}, f32[1024,128]{1,0:T(8,128)S(1)}, u32[]{:S(2)}, u32[]{:S(2)}) collective-permute-start(f32[1024,128]{1,0:T(8,128)S(1)} %add.212), channel_id=1, source_target_pairs={{0,32},{8,40},{16,48},{24,56},{32,0},{40,8},{48,16},{56,24},{64,96... | collective-permute-start | bytes 1572872 | tf_op jit(solution)/shard_map/ppermute | solution.py:329
  70.9 13.3 %collective-permute-start.18 = (f32[1024,128]{1,0:T(8,128)S(1)}, f32[1024,128]{1,0:T(8,128)S(1)}, u32[]{:S(2)}, u32[]{:S(2)}) collective-permute-start(f32[1024,128]{1,0:T(8,128)S(1)} %add.213), channel_id=1, source_target_pairs={{0,24},{8,16},{16,8},{24,0},{32,56},{40,48},{48,40},{56,32},{64,88... | collective-permute-start | bytes 1572872 | tf_op jit(solution)/shard_map/ppermute | solution.py:329
  71.1 13.1 %collective-permute-start.19 = (f32[1024,128]{1,0:T(8,128)S(1)}, f32[1024,128]{1,0:T(8,128)S(1)}, u32[]{:S(2)}, u32[]{:S(2)}) collective-permute-start(f32[1024,128]{1,0:T(8,128)S(1)} %add.214), channel_id=1, source_target_pairs={{0,8},{8,0},{16,24},{24,16},{32,40},{40,32},{48,56},{56,48},{64,72... | collective-permute-start | bytes 1572872 | tf_op jit(solution)/shard_map/ppermute | solution.py:329
  90.7 2.7 %collective-permute-start.20 = (f32[512,512]{1,0:T(8,128)S(1)}, f32[512,512]{1,0:T(8,128)S(1)}, u32[]{:S(2)}, u32[]{:S(2)}) collective-permute-start(f32[512,512]{1,0:T(8,128)S(1)} %shard_map.77.own), channel_id=1, source_target_pairs={{0,1},{1,0},{2,3},{3,2},{4,5},{5,4},{6,7},{7,6},{8,9},{9,8},{10,11... | collective-permute-start | bytes 3145736 | tf_op jit(solution)/shard_map/ppermute | solution.py:407
  103.7 15.3 %copy-start.8 = (f32[3,256,512]{2,1,0:T(8,128)S(1)}, f32[3,256,512]{2,1,0:T(8,128)}, u32[]{:S(2)}) copy-start(f32[3,256,512]{2,1,0:T(8,128)} %get-tuple-element.110) | copy-start | bytes 4718596
  103.7 15.2 %collective-permute-start.21 = (f32[256,512]{1,0:T(8,128)S(1)}, f32[256,512]{1,0:T(8,128)S(1)}, u32[]{:S(2)}, u32[]{:S(2)}) collective-permute-start(f32[256,512]{1,0:T(8,128)S(1)} %get-tuple-element.105), channel_id=1, source_target_pairs={{0,2},{1,3},{2,4},{3,5},{4,6},{5,7},{6,0},{7,1},{8,10},{9,11},{10,... | collective-permute-start | bytes 1572872 | tf_op jit(solution)/shard_map/ppermute | solution.py:403
  105.3 13.7 %collective-permute-start.22 = (f32[256,512]{1,0:T(8,128)S(1)}, f32[256,512]{1,0:T(8,128)S(1)}, u32[]{:S(2)}, u32[]{:S(2)}) collective-permute-start(f32[256,512]{1,0:T(8,128)S(1)} %get-tuple-element.106), channel_id=1, source_target_pairs={{0,6},{1,7},{2,0},{3,1},{4,2},{5,3},{6,4},{7,5},{8,14},{9,15},{10,... | collective-permute-start | bytes 1572872 | tf_op jit(solution)/shard_map/ppermute | solution.py:403
  119.0 3.5 %collective-permute-start.25 = (f32[512,512]{1,0:T(8,128)S(1)}, f32[512,512]{1,0:T(8,128)S(1)}, u32[]{:S(2)}, u32[]{:S(2)}) collective-permute-start(f32[512,512]{1,0:T(8,128)S(1)} %shard_map.79.own), channel_id=1, source_target_pairs={{0,1},{1,0},{2,3},{3,2},{4,5},{5,4},{6,7},{7,6},{8,9},{9,8},{10,11... | collective-permute-start | bytes 3145736 | tf_op jit(solution)/shard_map/ppermute | solution.py:413
  119.2 15.6 %collective-permute-start.23 = (f32[256,512]{1,0:T(8,128)S(1)}, f32[256,512]{1,0:T(8,128)S(1)}, u32[]{:S(2)}, u32[]{:S(2)}) collective-permute-start(f32[256,512]{1,0:T(8,128)S(1)} %get-tuple-element.111), channel_id=1, source_target_pairs={{0,2},{1,3},{2,4},{3,5},{4,6},{5,7},{6,0},{7,1},{8,10},{9,11},{10,... | collective-permute-start | bytes 1572872 | tf_op jit(solution)/shard_map/ppermute | solution.py:403
  120.8 14.1 %collective-permute-start.24 = (f32[256,512]{1,0:T(8,128)S(1)}, f32[256,512]{1,0:T(8,128)S(1)}, u32[]{:S(2)}, u32[]{:S(2)}) collective-permute-start(f32[256,512]{1,0:T(8,128)S(1)} %get-tuple-element.112), channel_id=1, source_target_pairs={{0,6},{1,7},{2,0},{3,1},{4,2},{5,3},{6,4},{7,5},{8,14},{9,15},{10,... | collective-permute-start | bytes 1572872 | tf_op jit(solution)/shard_map/ppermute | solution.py:403
  134.9 15.3 %copy-start.7 = (f32[3,256,512]{2,1,0:T(8,128)S(1)}, f32[3,256,512]{2,1,0:T(8,128)}, u32[]{:S(2)}) copy-start(f32[3,256,512]{2,1,0:T(8,128)} %get-tuple-element.122) | copy-start | bytes 4718596
  134.9 15.3 %collective-permute-start.31 = (f32[256,512]{1,0:T(8,128)S(1)}, f32[256,512]{1,0:T(8,128)S(1)}, u32[]{:S(2)}, u32[]{:S(2)}) collective-permute-start(f32[256,512]{1,0:T(8,128)S(1)} %get-tuple-element.121), channel_id=1, source_target_pairs={{0,6},{1,7},{2,0},{3,1},{4,2},{5,3},{6,4},{7,5},{8,14},{9,15},{10,... | collective-permute-start | bytes 1572872 | tf_op jit(solution)/shard_map/ppermute | solution.py:403
  137.8 16.2 %collective-permute-start.28 = (f32[256,512]{1,0:T(8,128)S(1)}, f32[256,512]{1,0:T(8,128)S(1)}, u32[]{:S(2)}, u32[]{:S(2)}) collective-permute-start(f32[256,512]{1,0:T(8,128)S(1)} %get-tuple-element.119), channel_id=1, source_target_pairs={{0,2},{1,3},{2,4},{3,5},{4,6},{5,7},{6,0},{7,1},{8,10},{9,11},{10,... | collective-permute-start | bytes 1572872 | tf_op jit(solution)/shard_map/ppermute | solution.py:403
  137.9 23.5 %collective-permute-start.27 = (f32[256,512]{1,0:T(8,128)S(1)}, f32[256,512]{1,0:T(8,128)S(1)}, u32[]{:S(2)}, u32[]{:S(2)}) collective-permute-start(f32[256,512]{1,0:T(8,128)S(1)} %bitcast_add_fusion.7), channel_id=1, source_target_pairs={{0,6},{1,7},{2,0},{3,1},{4,2},{5,3},{6,4},{7,5},{8,14},{9,15},{10,... | collective-permute-start | bytes 1572872 | tf_op jit(solution)/shard_map/ppermute | solution.py:403
  141.3 33.8 %collective-permute-start.26 = (f32[256,512]{1,0:T(8,128)S(1)}, f32[256,512]{1,0:T(8,128)S(1)}, u32[]{:S(2)}, u32[]{:S(2)}) collective-permute-start(f32[256,512]{1,0:T(8,128)S(1)} %bitcast_add_fusion.9), channel_id=1, source_target_pairs={{0,2},{1,3},{2,4},{3,5},{4,6},{5,7},{6,0},{7,1},{8,10},{9,11},{10,... | collective-permute-start | bytes 1572872 | tf_op jit(solution)/shard_map/ppermute | solution.py:403
  150.3 20.8 %collective-permute-start.32 = (f32[256,512]{1,0:T(8,128)S(1)}, f32[256,512]{1,0:T(8,128)S(1)}, u32[]{:S(2)}, u32[]{:S(2)}) collective-permute-start(f32[256,512]{1,0:T(8,128)S(1)} %bitcast_add_fusion.2), channel_id=1, source_target_pairs={{0,6},{1,7},{2,0},{3,1},{4,2},{5,3},{6,4},{7,5},{8,14},{9,15},{10,... | collective-permute-start | bytes 1572872 | tf_op jit(solution)/shard_map/ppermute | solution.py:403
  154.1 20.8 %collective-permute-start.29 = (f32[256,512]{1,0:T(8,128)S(1)}, f32[256,512]{1,0:T(8,128)S(1)}, u32[]{:S(2)}, u32[]{:S(2)}) collective-permute-start(f32[256,512]{1,0:T(8,128)S(1)} %bitcast_add_fusion.5), channel_id=1, source_target_pairs={{0,2},{1,3},{2,4},{3,5},{4,6},{5,7},{6,0},{7,1},{8,10},{9,11},{10,... | collective-permute-start | bytes 1572872 | tf_op jit(solution)/shard_map/ppermute | solution.py:403
  171.2 13.7 %collective-permute-start.33 = (f32[256,512]{1,0:T(8,128)S(1)}, f32[256,512]{1,0:T(8,128)S(1)}, u32[]{:S(2)}, u32[]{:S(2)}) collective-permute-start(f32[256,512]{1,0:T(8,128)S(1)} %bitcast_add_fusion.1), channel_id=1, source_target_pairs={{0,6},{1,7},{2,0},{3,1},{4,2},{5,3},{6,4},{7,5},{8,14},{9,15},{10,... | collective-permute-start | bytes 1572872 | tf_op jit(solution)/shard_map/ppermute | solution.py:403
  175.0 13.4 %collective-permute-start.30 = (f32[256,512]{1,0:T(8,128)S(1)}, f32[256,512]{1,0:T(8,128)S(1)}, u32[]{:S(2)}, u32[]{:S(2)}) collective-permute-start(f32[256,512]{1,0:T(8,128)S(1)} %bitcast_add_fusion.4), channel_id=1, source_target_pairs={{0,2},{1,3},{2,4},{3,5},{4,6},{5,7},{6,0},{7,1},{8,10},{9,11},{10,... | collective-permute-start | bytes 1572872 | tf_op jit(solution)/shard_map/ppermute | solution.py:403
  188.4 1.6 copy-start.1

commit v5 on v4

--- a/solution.py
+++ b/solution.py
@@ -13,7 +13,7 @@
 TILE = 256
 FAR = 1 << 30
 LOW = -1e30
-LARGE = pl.CostEstimate(flops=12 << 30, bytes_accessed=16 << 20, transcendentals=0)
+LARGE = pl.CostEstimate(flops=4 << 30, bytes_accessed=4 << 20, transcendentals=0)
 SMALL = pl.CostEstimate(flops=1024, bytes_accessed=1024, transcendentals=0)
 
 
@@ -89,7 +89,7 @@
 
 
 def near_kernel(
-    first_row, back, wraps, q, k_far, k_far_wrap, k_left, k_left_wrap, k_own,
+    start, first_row, back, wraps, q, k_far, k_far_wrap, k_left, k_left_wrap, k_own,
     v_far_a, v_far_b, v_left, v_own, slash_pos, out, stats, near_k, near_v,
 ):
     turn = pl.program_id(0)
@@ -110,7 +110,7 @@
         put_parts(near_k, 2 * rows, (k_own,))
         put_parts(near_v, 0, (v_far_a, v_far_b, v_left, v_own))
 
-    q_pos = first_row[0] + turn * TILE + lax.broadcasted_iota(jnp.int32, (TILE, 1), 0)
+    q_pos = first_row[0] + start + turn * TILE + lax.broadcasted_iota(jnp.int32, (TILE, 1), 0)
     per_block = TILE // BLOCK
     pair = q.shape[1] // HEAD_SIZE
     lane = lax.broadcasted_iota(jnp.int32, (TILE, HEAD_SIZE), 1)
@@ -121,7 +121,7 @@
         high, low = query_parts(q[:, columns])
         scores, near = [], []
         for j in range(per_block):
-            block = turn * per_block + j
+            block = start // BLOCK + turn * per_block + j
             spots = [
                 pl.ds(pl.multiple_of((block + back[head, n]) * BLOCK, BLOCK), BLOCK)
                 for n in range(4)
@@ -148,30 +148,35 @@
     stats[...] = known
 
 
-def attend_near(q, first_row, back, wraps, arrays):
-    rows, width = q.shape
+def attend_near(q, start, rows, first_row, back, wraps, arrays):
+    width = q.shape[1]
     pair = 2
     count = width // (pair * HEAD_SIZE)
+    base = start // TILE
     smem = pl.BlockSpec(memory_space=pltpu.SMEM)
     vmem = pl.BlockSpec(memory_space=pltpu.VMEM)
-    wide = pl.BlockSpec((TILE, pair * HEAD_SIZE), lambda t, h: (t, h))
+    wide = (TILE, pair * HEAD_SIZE)
     return pl.pallas_call(
-        near_kernel,
+        functools.partial(near_kernel, start),
         grid=(rows // TILE, count),
         out_shape=[
             jax.ShapeDtypeStruct((rows, width), jnp.float32),
             jax.ShapeDtypeStruct((rows, count * HEAD_SIZE), jnp.float32),
         ],
-        in_specs=[smem, smem, smem, wide] + [vmem] * len(arrays),
-        out_specs=[wide, pl.BlockSpec((TILE, HEAD_SIZE), lambda t, h: (t, h))],
-        scratch_shapes=[pltpu.VMEM((3 * rows, 2 * HEAD_SIZE), jnp.bfloat16)] * 2,
+        in_specs=[smem, smem, smem, pl.BlockSpec(wide, lambda t, h: (base + t, h))]
+        + [vmem] * len(arrays),
+        out_specs=[
+            pl.BlockSpec(wide, lambda t, h: (t, h)),
+            pl.BlockSpec((TILE, HEAD_SIZE), lambda t, h: (t, h)),
+        ],
+        scratch_shapes=[pltpu.VMEM((3 * q.shape[0], 2 * HEAD_SIZE), jnp.bfloat16)] * 2,
         compiler_params=pltpu.CompilerParams(vmem_limit_bytes=40 << 20),
         cost_estimate=LARGE,
     )(first_row, back, wraps, q, *arrays)
 
 
 def attend_kernel(
-    start, first_row, q, near, stats, k_a, k_b, v_a, v_b, vert_pos, out, vert_k, vert_v
+    start, first_row, q, near, stats, k_a, k_b, v_a, v_b, vert_pos, out_a, out_b, vert_k, vert_v
 ):
     turn = pl.program_id(0)
 
@@ -197,114 +202,151 @@
         total = total + keep * stats[:, 2 * part + 1 : 2 * part + 2]
         mixed = fold(dot(jnp.concatenate(split(weights), axis=0), vert_v[rows, :], DOWN))
         mixed = mixed[:, :HEAD_SIZE] + mixed[:, HEAD_SIZE:] + keep * near[:, columns]
-        out[:, columns] = mixed / total
-
-
-def attend(q, near, stats, start, rows, first_row, arrays):
+        mixed = mixed / total
+
+        @pl.when(turn == 0)
+        def _():
+            out_a[:, columns] = mixed
+
+        @pl.when(turn == 1)
+        def _():
+            out_b[:, columns] = mixed
+
+
+def attend(q, near, stats, start, first_row, arrays):
     width = q.shape[1]
     heads = width // HEAD_SIZE
     pair = 2
+    last = heads // pair - 1
     smem = pl.BlockSpec(memory_space=pltpu.SMEM)
     vmem = pl.BlockSpec(memory_space=pltpu.VMEM)
     base = start // TILE
-    wide = pl.BlockSpec((TILE, pair * HEAD_SIZE), lambda t, h: (base + t, h))
+    wide = (TILE, pair * HEAD_SIZE)
+    out = jax.ShapeDtypeStruct((TILE, width), jnp.float32)
     return pl.pallas_call(
         functools.partial(attend_kernel, start),
-        grid=(rows // TILE, heads // pair),
-        out_shape=jax.ShapeDtypeStruct((rows, width), jnp.float32),
-        in_specs=[smem, wide, wide, pl.BlockSpec((TILE, HEAD_SIZE), lambda t, h: (base + t, h))]
+        grid=(2, heads // pair),
+        out_shape=[out, out],
+        in_specs=[
+            smem,
+            pl.BlockSpec(wide, lambda t, h: (base + t, h)),
+            pl.BlockSpec(wide, lambda t, h: (base + t, h)),
+            pl.BlockSpec((TILE, HEAD_SIZE), lambda t, h: (base + t, h)),
+        ]
         + [vmem] * len(arrays),
-        out_specs=pl.BlockSpec((TILE, pair * HEAD_SIZE), lambda t, h: (t, h)),
+        out_specs=[
+            pl.BlockSpec(wide, lambda t, h: (0, jnp.where(t == 0, h, last))),
+            pl.BlockSpec(wide, lambda t, h: (0, jnp.where(t == 0, 0, h))),
+        ],
         scratch_shapes=[pltpu.VMEM((heads * 8 * BLOCK, 2 * HEAD_SIZE), jnp.bfloat16)] * 2,
         compiler_params=pltpu.CompilerParams(vmem_limit_bytes=40 << 20),
         cost_estimate=LARGE,
     )(first_row, q, near, stats, *arrays)
 
 
-def halves_kernel(order, own, other, out):
-    rows = own.shape[0]
-    for first, ref in ((0, own), (rows, other)):
-        high, low = split(ref[...])
-        out[0, first : first + rows] = high
-        out[0, first + 2 * rows : first + 3 * rows] = low
-
-
-def weight_halves(own, other, order):
-    rows = own.shape[0]
-    count = order.shape[0]
-    width = own.shape[1] // (2 * count)
-    w_spec = pl.BlockSpec((rows, width), lambda i, o: (0, o[i]))
+def stack_split(x, at, ref):
+    rows, depth = ref.shape
+    high, low = split(ref[...])
+    x[:rows, at : at + depth] = high
+    x[rows:, at : at + depth] = low
+
+
+def times_weight(x, w, refs):
+    depth = refs[0].shape[0]
+    for at, ref in enumerate(refs):
+        rows = slice(at * depth, (at + 1) * depth)
+        w[0, rows, :], w[1, rows, :] = split(ref[...])
+    return fold(dot(x[...], w[0], DOWN)) + dot(x[: x.shape[0] // 2, :], w[1], DOWN)
+
+
+def chip_kernel(order, *refs):
+    own, mate = refs[0:2], refs[2:4]
+    w_own, w_mate, out, x, w = refs[4:]
+    for kind in range(2):
+
+        @pl.when((pl.program_id(0) == kind) & (pl.program_id(1) == 0))
+        def _():
+            stack_split(x, 0, own[kind])
+            stack_split(x, own[kind].shape[1], mate[kind])
+
+    out[0] = times_weight(x, w, (w_own, w_mate))
+
+
+def project_chip(own, mate, w_own, w_mate, order):
+    rows, depth = own[0].shape
+    width = depth
+    vmem = pl.BlockSpec(memory_space=pltpu.VMEM)
     return pl.pallas_call(
-        halves_kernel,
-        out_shape=jax.ShapeDtypeStruct((count, 4 * rows, width), jnp.bfloat16),
+        chip_kernel,
+        out_shape=jax.ShapeDtypeStruct((2, rows, 2 * width), jnp.float32),
         grid_spec=pltpu.PrefetchScalarGridSpec(
             num_scalar_prefetch=1,
-            grid=(count,),
-            in_specs=[w_spec, w_spec],
-            out_specs=pl.BlockSpec((1, 4 * rows, width), lambda i, o: (i, 0, 0)),
+            grid=(2, 2),
+            in_specs=[vmem] * 4
+            + [
+                pl.BlockSpec((depth, width), lambda k, d, o: (0, o[2 * k + d])),
+                pl.BlockSpec((depth, width), lambda k, d, o: (0, d * (k + 1))),
+            ],
+            out_specs=pl.BlockSpec((1, rows, width), lambda k, d, o: (k, 0, d)),
+            scratch_shapes=[
+                pltpu.VMEM((2 * rows, 2 * depth), jnp.bfloat16),
+                pltpu.VMEM((2, 2 * depth, width), jnp.bfloat16),
+            ],
         ),
-        compiler_params=pltpu.CompilerParams(vmem_limit_bytes=24 << 20),
-        cost_estimate=LARGE,
-    )(order, own, other)
-
-
-def project_kernel(own, other, w, first_a, rest_a, first_b, rest_b, x):
-    depth = own.shape[1]
-    half = first_a.shape[0]
-    step = pl.program_id(0)
-
-    @pl.when(step == 0)
-    def _():
-        for at, ref in ((0, own), (depth, other)):
-            high, low = split(ref[...])
-            x[:, at : at + depth] = high
-            x[:, at + 2 * depth : at + 3 * depth] = high
-            x[:, at + 4 * depth : at + 5 * depth] = low
-
-    term = dot(x[:, : 4 * depth], w[0], DOWN) + dot(x[:, 4 * depth :], w[0, : 2 * depth], DOWN)
-
-    @pl.when(step == 0)
-    def _():
-        first_a[...] = term[:half]
-
-    @pl.when(step > 0)
-    def _():
-        rest_a[0] = term[:half]
-
-    @pl.when(step == 2)
-    def _():
-        first_b[...] = term[half:]
-
-    @pl.when(step != 2)
-    def _():
-        rest_b[0] = term[half:]
-
-
-def project(own, other, weights):
-    rows, depth = own.shape
-    half = rows // 2
-    count, _, width = weights.shape
-    x_spec = pl.BlockSpec((rows, depth), lambda i: (0, 0))
-    first = jax.ShapeDtypeStruct((half, width), jnp.float32)
-    rest = jax.ShapeDtypeStruct((count - 1, half, width), jnp.float32)
-    first_spec = pl.BlockSpec((half, width), lambda i: (0, 0))
-    back_step = lambda i: jnp.where(i == 0, 1, jnp.where(i == 3, 2, 0))
-    first_a, rest_a, first_b, rest_b = pl.pallas_call(
-        project_kernel,
-        grid=(count,),
-        out_shape=[first, rest, first, rest],
-        in_specs=[x_spec, x_spec, pl.BlockSpec((1, 4 * depth, width), lambda i: (i, 0, 0))],
-        out_specs=[
-            first_spec,
-            pl.BlockSpec((1, half, width), lambda i: (jnp.maximum(i - 1, 0), 0, 0)),
-            first_spec,
-            pl.BlockSpec((1, half, width), lambda i: (back_step(i), 0, 0)),
-        ],
-        scratch_shapes=[pltpu.VMEM((rows, 6 * depth), jnp.bfloat16)],
         compiler_params=pltpu.CompilerParams(vmem_limit_bytes=48 << 20),
         cost_estimate=LARGE,
-    )(own, other, weights)
-    return (first_a, first_b), (rest_a, rest_b)
+    )(order, *own, *mate, w_own, w_mate)
+
+
+def pair_kernel(core, *refs):
+    got, mate = refs[0:2], refs[2:4]
+    weights = (refs[4:6], refs[6:8])
+    total, outs, x, w = refs[8], refs[9:13], refs[13], refs[14]
+    for kind in range(2):
+
+        @pl.when((pl.program_id(0) == kind) & (pl.program_id(1) == 0))
+        def _():
+            stack_split(x, 0, got[kind])
+            stack_split(x, got[kind].shape[1], mate[kind])
+
+        for chip in range(2):
+
+            @pl.when((pl.program_id(0) == kind) & (pl.program_id(1) == chip))
+            def _():
+                outs[2 * kind + chip][...] = total[0] + times_weight(x, w, weights[kind])
+
+
+def project_pair(got, mate, near, near_mate, far, far_mate, total, core):
+    rows, depth = got[0].shape
+    width = depth
+    vmem = pl.BlockSpec(memory_space=pltpu.VMEM)
+    out = jax.ShapeDtypeStruct((rows, width), jnp.float32)
+    even = lambda k, d: jnp.where(k == 0, d, 1)
+    odd = lambda k, d: jnp.where(k == 0, 0, d)
+    w_spec = lambda place: pl.BlockSpec((depth, width), place)
+    return pl.pallas_call(
+        pair_kernel,
+        out_shape=[out] * 4,
+        grid_spec=pltpu.PrefetchScalarGridSpec(
+            num_scalar_prefetch=1,
+            grid=(2, 2),
+            in_specs=[vmem] * 4
+            + [
+                w_spec(lambda k, d, c: (0, 2 * even(k, d) + c[0])),
+                w_spec(lambda k, d, c: (0, even(k, d))),
+                w_spec(lambda k, d, c: (0, 2 * odd(k, d) + c[0])),
+                w_spec(lambda k, d, c: (0, odd(k, d))),
+                pl.BlockSpec((1, rows, width), lambda k, d, c: (k, 0, d)),
+            ],
+            out_specs=[pl.BlockSpec((rows, width), lambda k, d, c: (0, 0))] * 4,
+            scratch_shapes=[
+                pltpu.VMEM((2 * rows, 2 * depth), jnp.bfloat16),
+                pltpu.VMEM((2, 2 * depth, width), jnp.bfloat16),
+            ],
+        ),
+        compiler_params=pltpu.CompilerParams(vmem_limit_bytes=48 << 20),
+        cost_estimate=LARGE,
+    )(core, *got, *mate, near, near_mate, far, far_mate, total)
 
 
 def body(
@@ -333,8 +375,18 @@
     k_right = send(key_rows, left)
     v_below = send(value_vectors, up)
     v_above = send(value_vectors, down)
-    swap = [(i, i ^ 1) for i in range(head_size)]
-    w_other = lax.ppermute(out_weight, "head", swap)
+
+    y = head_index // 2
+    over_head = lambda a, bits: lax.ppermute(a, "head", [(i, i ^ bits) for i in range(head_size)])
+    width = out_weight.shape[1] // head_size
+    cut = lambda a, first, count: lax.dynamic_slice_in_dim(a, first * width, count * width, 1)
+    beside = lambda *parts: jnp.concatenate(parts, axis=1)
+    chip_columns = lambda chip: cut(out_weight, 2 * chip, 2)
+    near_weight, far_weight = (
+        over_head(beside(chip_columns(y ^ chip), chip_columns(y ^ 2)), 2 * chip) for chip in (1, 3)
+    )
+    mate_columns = (cut(out_weight, 2 * chip + 1 - core, 1) for chip in (y, y ^ 3, y ^ 1))
+    mate_weight = over_head(beside(*mate_columns), 1)
 
     vert = lax.dynamic_slice_in_dim(vertical_blocks, head_index * heads, heads, 0)
     slash = lax.dynamic_slice_in_dim(slash_offsets, head_index * heads, heads, 0)
@@ -354,18 +406,19 @@
     first_row = (seq_index * rows).reshape(1)
     back = 2 * blocks - offsets
     wraps = jnp.stack([x < 2, x == 0]).astype(jnp.int32)
-    order = (head_index // 2 + 2 * chips - 1 - jnp.arange(chips, dtype=jnp.int32)) % chips
-    order = 2 * order + core
+    order = jnp.stack([2 * chip + core for chip in (y, y ^ 3, y, y ^ 1)])
+    my_core = core.reshape(1)
     owner = named // blocks
     at = named % blocks
     k_place, k_held = (owner % 4 - x) % 4 * blocks + at, (owner // 4 == z).astype(jnp.int32)
     v_place, v_held = (owner // 4 - z) % 4 * blocks + at, (owner % 4 == x).astype(jnp.int32)
-    small = (vert_pos, slash_pos, first_row, back, wraps, order, k_place, k_held, v_place, v_held)
+    orders = (order, my_core)
+    small = (vert_pos, slash_pos, first_row, back, wraps, orders, k_place, k_held, v_place, v_held)
 
     (k_left, k_right, v_below, v_above), small = lax.optimization_barrier(
         ((k_left, k_right, v_below, v_above), small)
     )
-    vert_pos, slash_pos, first_row, back, wraps, order, k_place, k_held, v_place, v_held = small
+    vert_pos, slash_pos, first_row, back, wraps, orders, k_place, k_held, v_place, v_held = small
     half = rows // 2
     source = jnp.where(x >= 2, v_below, value_vectors)
     v_left = jnp.where(x == 3, v_below, value_vectors)
@@ -387,40 +440,49 @@
     named = [*k_named, *v_named]
     one, two = (4, 12, 1, 3), (12, 4, 3, 1)
     more = [swapped(a, bits) for a, bits in zip(named, one)]
-    weights = weight_halves(out_weight, w_other, order)
-    weights, v_far_a, v_far_b, k_far_wrap, *more = lax.optimization_barrier(
-        (weights, v_far_a, v_far_b, k_far_wrap, *more)
+    v_far_a, v_far_b, k_far_wrap, *more = lax.optimization_barrier(
+        (v_far_a, v_far_b, k_far_wrap, *more)
     )
     named = [a + b for a, b in zip(named, more)]
     arrays = (k_far, k_far_wrap, k_left, k_left_wrap, key_rows, v_far_a, v_far_b, v_left)
-    arrays = (*arrays, value_vectors, slash_pos)
-    near, stats = attend_near(queries, first_row, back, wraps, arrays)
+    near_arrays = (*arrays, value_vectors, slash_pos)
+    near = attend_near(queries, 0, rows, first_row, back, wraps, near_arrays)
     more = [swapped(a, bits) for a, bits in zip(named, two)]
-    near, stats, *more = lax.optimization_barrier((near, stats, *more))
+    near, more = lax.optimization_barrier((near, more))
     arrays = (*(a + b for a, b in zip(named, more)), vert_pos)
 
-    rings = [[(i, (i + d) % head_size) for i in range(head_size)] for d in (2, head_size - 2)]
-    ring = lambda parts: [lax.ppermute(p, "head", r) for p, r in zip(parts, rings)]
-    add = lambda parts, terms, step: [p + t[step] for p, t in zip(parts, terms)]
-
-    own = attend(queries, near, stats, 0, half, first_row, arrays)
-    other = lax.ppermute(own, "head", swap)
-    first, terms = project(own, other, weights)
-    q, *first = lax.optimization_barrier((queries, *first))
-    moved = ring(first)
-    own = attend(q, near, stats, half, half, first_row, arrays)
-    own, *moved = lax.optimization_barrier((own, *moved))
-    other = lax.ppermute(own, "head", swap)
-    sums = add(moved, terms, 0)
-    weights, *sums = lax.optimization_barrier((weights, *sums))
-    moved = ring(sums)
-    later, later_terms = project(own, other, weights)
-    *moved, later_a, later_b = lax.optimization_barrier((*moved, *later))
-    sums, later = add(moved, terms, 1), (later_a, later_b)
-    sums, later = add(ring(sums), terms, 2), add(ring(later), later_terms, 0)
-    later = add(ring(later), later_terms, 1)
-    later = add(ring(later), later_terms, 2)
-    return jnp.concatenate([*sums, *later], axis=0)
+    order, my_core = orders
+    meet, end = (2, 6), (6, 2)
+    across_chip = lambda parts: [over_head(a, 1) for a in parts]
+    own = list(attend(queries, *near, 0, first_row, arrays))
+    q, *own = lax.optimization_barrier((queries, *own))
+    got_a = [over_head(a, bits) for a, bits in zip(own, meet)]
+    mate, near_weight, far_weight = lax.optimization_barrier(
+        (across_chip(own), near_weight, far_weight)
+    )
+    total = project_chip(own, mate, out_weight, mate_weight, order)
+    q, total = lax.optimization_barrier((q, total))
+    near_mate, far_mate = (
+        over_head(beside(cut(a, 1 - core, 1), cut(a, 3 - core, 1)), 1)
+        for a in (near_weight, far_weight)
+    )
+    own = attend(q, *near, half, first_row, arrays)
+    own, got_a = lax.optimization_barrier((own, got_a))
+    weights = (near_weight, near_mate, far_weight, far_mate)
+    got_b = [over_head(a, bits) for a, bits in zip(own, meet)]
+    mate = across_chip(own)
+    keep_0, pass_0, keep_1, pass_1 = project_pair(
+        got_a, across_chip(got_a), *weights, total, my_core
+    )
+    pass_0, pass_1, got_b, mate = lax.optimization_barrier((pass_0, pass_1, got_b, mate))
+    sent_a = [over_head(a, bits) for a, bits in zip((pass_0, pass_1), end)]
+    total = project_chip(own, mate, out_weight, mate_weight, order)
+    keep_2, pass_2, keep_3, pass_3 = project_pair(
+        got_b, across_chip(got_b), *weights, total, my_core
+    )
+    pass_2, pass_3, sent_a = lax.optimization_barrier((pass_2, pass_3, sent_a))
+    sent = sent_a + [over_head(a, bits) for a, bits in zip((pass_2, pass_3), end)]
+    return jnp.concatenate([a + b for a, b in zip((keep_0, keep_1, keep_2, keep_3), sent)], axis=0)
 
 
 def solution(mesh):

time: 192 us -> 201 us (1.047)
  waiting for transfers between devices: 72.5 us -> 56.7 us
  Pallas kernels: 49.1 us -> 60 us
  other arithmetic: 5.62 us -> 15.7 us
  local copies, waits for them, and re-layouts: 8.31 us -> 15.1 us
    ppermute x15 -> x21, waiting for transfers between devices: 49.3 us -> 22.1 us  [body(): lax.ppermute(a, 'head', [(i, i ^ bits) for i in range(head_size)])]
    ppermute x19, waiting for transfers between devices: 23.2 us -> 34.5 us  [body(): send = lambda a, pairs: lax.ppermute(a, 'seq', pairs)]
    pallas_call x6 -> x7, Pallas kernels: 46.7 us -> 57.6 us  [the longest x2 18.8 us: attend(): pl.pallas_call(functools.partial(attend_kernel, start), grid=(2, heads //...]
    concatenate x1 -> x5, other arithmetic: 1.49 us -> 10.7 us  [the longest x4 9.2 us: body(): beside = lambda *parts: jnp.concatenate(parts, axis=1)]
    dynamic_slice x0 -> x3, local copies, waits for them, and re-layouts: none -> 8.33 us  [body(): lax.dynamic_slice_in_dim(a, first * width, count * width, 1)]
    ppermute x15 -> x21, starting transfers between devices: 20.6 us -> 16.1 us  [body(): lax.ppermute(a, 'head', [(i, i ^ bits) for i in range(head_size)])]
    add x4, other arithmetic: 0.3 us -> 3.57 us  [body(): named = [a + b for a, b in zip(named, more)]]
    ppermute x19, starting transfers between devices: 32.7 us -> 35.4 us  [body(): send = lambda a, pairs: lax.ppermute(a, 'seq', pairs)]
  transfers between devices with their start and end apart: 34 -> 40, of which waited for: 15 -> 17; matrix products, arithmetic and copies ran while one was open for 3% -> 12% of each run, Pallas kernels for 17% -> 30%
where the time goes in v5:
time: 201 us; the launch traced here: 200 us
  Pallas kernels  60 us (30%)
  waiting for transfers between devices  56.7 us (28%)
  starting transfers between devices  51.4 us (26%)
  other arithmetic  15.7 us (8%)
  local copies, waits for them, and re-layouts  15.1 us (8%)
    ppermute x19, starting transfers between devices, body(): send = lambda a, pairs: lax.ppermute(a, 'seq', pairs)  35.4 us
    ppermute x19, waiting for transfers between devices, body(): send = lambda a, pairs: lax.ppermute(a, 'seq', pairs)  34.5 us
    ppermute x21, waiting for transfers between devices, body(): lax.ppermute(a, 'head', [(i, i ^ bits) for i in range(head_size)])  22.1 us
    pallas_call x2, Pallas kernels, attend(): pl.pallas_call(functools.partial(attend_kernel, start), grid=(2, heads //...  18.8 us
    ppermute x21, starting transfers between devices, body(): lax.ppermute(a, 'head', [(i, i ^ bits) for i in range(head_size)])  16.1 us
    pallas_call x2, Pallas kernels, project_chip(): pl.pallas_call(chip_kernel, out_shape=jax.ShapeDtypeStruct((2, rows, 2 *...  14.7 us
    pallas_call x2, Pallas kernels, project_pair(): pl.pallas_call(pair_kernel, out_shape=[out] * 4, grid_spec=pltpu.Prefetch...  14.5 us
    pallas_call x1, Pallas kernels, attend_near(): pl.pallas_call(functools.partial(near_kernel, start), grid=(rows // TILE,...  9.65 us
  transfers between devices with their start and end apart: 40, of which 17 were waited for; matrix products, arithmetic and copies ran while one was open for 12% of the time, Pallas kernels for 30%

profile of v5, /device:TPU:2, one launch (start us, length us, event | category | flops | bytes accessed | tf_op | source)
XLA Modules:
  0.0 200.3 jit_solution(1319621977470817472)
XLA Ops:
  0.0 1.5 collective-permute-start
  2.0 1.9 collective-permute-start.2
  3.9 2.1 %collective-permute-start.3 = (f32[1024,128]{1,0:T(8,128)}, f32[1024,128]{1,0:T(8,128)S(1)}, u32[]{:S(2)}, u32[]{:S(2)}) collective-permute-start(f32[1024,128]{1,0:T(8,128)} %v_own.1), channel_id=1, source_target_pairs={{0,96},{8,104},{16,112},{24,120},{32,0},{40,8},{48,16},{56,24},{64... | collective-permute-start | bytes 1572872 | tf_op jit(solution)/shard_map/ppermute | solution.py:371
  6.1 3.4 %constant_dynamic-slice_fusion.7 = (f32[512,1024]{1,0:T(8,128)S(1)}, f32[512,1024]{1,0:T(8,128)S(1)}, f32[512,1024]{1,0:T(8,128)S(1)}) fusion(f32[512,4096]{1,0:T(8,128)} %refs_4_.3, s32[]{:T(128)S(6)} %select_n.145, s32[]{:T(128)S(6)} %select_n.144, s32[]{:T(128)S(6)} %select_n.143), kind=kLoop, calls=%fused_computation.24 | loop fusion | bytes 12582924 | tf_op jit(solution)/shard_map/dynamic_slice | solution.py:382
  9.5 4.2 %pad_maximum_fusion = (f32[512,2048]{1,0:T(8,128)}, f32[512,2048]{1,0:T(8,128)}) fusion(f32[512,1024]{1,0:T(8,128)S(1)} %get-tuple-element.163, f32[512,1024]{1,0:T(8,128)S(1)} %get-tuple-element.162, f32[512,1024]{1,0:T(8,128)S(1)} %get-tuple-element.164), kind=kLoop, calls=%fused_computation | loop fusion | flops 2097152 | bytes 14680064 | tf_op jit(solution)/shard_map/concatenate | solution.py:383
  13.7 1.6 collective-permute-start.21
  18.3 2.3 %collective-permute-start.22 = (f32[512,2048]{1,0:T(8,128)}, f32[512,2048]{1,0:T(8,128)}, u32[]{:S(2)}, u32[]{:S(2)}) collective-permute-start(f32[512,2048]{1,0:T(8,128)} %get-tuple-element.169), channel_id=1, source_target_pairs={{0,6},{1,7},{2,4},{3,5},{4,2},{5,3},{6,0},{7,1},{8,14},{9,15},{10,... | collective-permute-start | bytes 12582920 | tf_op jit(solution)/shard_map/ppermute | solution.py:380
  20.7 2.1 %collective-permute-start.5 = (f32[1024,128]{1,0:T(8,128)S(1)}, f32[1024,128]{1,0:T(8,128)S(1)}, u32[]{:S(2)}, u32[]{:S(2)}) collective-permute-start(f32[1024,128]{1,0:T(8,128)S(1)} %collective-permute-done.3.refs_1_), channel_id=1, source_target_pairs={{0,96},{8,104},{16,112},{24,120},{32,0},{40,8},{48,16},{56,24},{64... | collective-permute-start | bytes 1572872 | tf_op jit(solution)/shard_map/ppermute | solution.py:371
  22.8 1.8 collective-permute-start.4
  25.1 7.9 %collective-permute-done.5.refs_2_ = f32[1024,128]{1,0:T(8,128)S(1)} collective-permute-done((f32[1024,128]{1,0:T(8,128)S(1)}, f32[1024,128]{1,0:T(8,128)S(1)}, u32[]{:S(2)}, u32[]{:S(2)}) %collective-permute-start.5) | collective-permute-done | bytes 524320 | tf_op jit(solution)/shard_map/ppermute | solution.py:371
  33.7 6.5 %collective-permute-done.4 = f32[1536,128]{1,0:T(8,128)S(1)} collective-permute-done((f32[1536,128]{1,0:T(8,128)S(1)}, f32[1536,128]{1,0:T(8,128)S(1)}, u32[]{:S(2)}, u32[]{:S(2)}) %collective-permute-start.4) | collective-permute-done | bytes 786464 | tf_op jit(solution)/shard_map/ppermute | solution.py:371
  40.2 1.6 collective-permute-done.6
  42.7 2.2 %collective-permute-start.10 = (f32[1024,128]{1,0:T(8,128)S(1)}, f32[1024,128]{1,0:T(8,128)S(1)}, u32[]{:S(2)}, u32[]{:S(2)}) collective-permute-start(f32[1024,128]{1,0:T(8,128)S(1)} %slice.20.refs_2_.k_far), channel_id=1, source_target_pairs={{0,32},{8,40},{32,64},{40,72},{64,96},{72,104},{1,33},{9,41},{33,6... | collective-permute-start | bytes 1572872 | tf_op jit(solution)/shard_map/ppermute | solution.py:371
  46.5 4.0 %collective-permute-done.8.v_far_a = f32[512,128]{1,0:T(8,128)S(1)} collective-permute-done((f32[512,128]{1,0:T(8,128)S(1)}, f32[512,128]{1,0:T(8,128)S(1)}, u32[]{:S(2)}, u32[]{:S(2)}) %collective-permute-start.8) | collective-permute-done | bytes 262176 | tf_op jit(solution)/shard_map/ppermute | solution.py:371
  50.5 3.6 %collective-permute-start.9 = (f32[512,128]{1,0:T(8,128)S(1)}, f32[512,128]{1,0:T(8,128)S(1)}, u32[]{:S(2)}, u32[]{:S(2)}) collective-permute-start(f32[512,128]{1,0:T(8,128)S(1)} %slice.22), channel_id=1, source_target_pairs={{0,24},{8,0},{16,8},{24,16},{32,56},{40,32},{48,40},{56,48},{64,88... | collective-permute-start | bytes 786440 | tf_op jit(solution)/shard_map/ppermute | solution.py:371
  55.2 2.7 %collective-permute-done.9.v_far_b = f32[512,128]{1,0:T(8,128)S(1)} collective-permute-done((f32[512,128]{1,0:T(8,128)S(1)}, f32[512,128]{1,0:T(8,128)S(1)}, u32[]{:S(2)}, u32[]{:S(2)}) %collective-permute-start.9) | collective-permute-done | bytes 262176 | tf_op jit(solution)/shard_map/ppermute | solution.py:371
  58.6 5.9 %collective-permute-start.12 = (f32[1024,128]{1,0:T(8,128)S(1)}, f32[1024,128]{1,0:T(8,128)}, u32[]{:S(2)}, u32[]{:S(2)}) collective-permute-start(f32[1024,128]{1,0:T(8,128)S(1)} %get-tuple-element.91), channel_id=1, source_target_pairs={{0,96},{8,104},{16,112},{24,120},{32,64},{40,72},{48,80},{56,88},{... | collective-permute-start | bytes 1572872 | tf_op jit(solution)/shard_map/ppermute | solution.py:371
  65.4 2.5 %collective-permute-start.13 = (f32[1024,128]{1,0:T(8,128)S(1)}, f32[1024,128]{1,0:T(8,128)}, u32[]{:S(2)}, u32[]{:S(2)}) collective-permute-start(f32[1024,128]{1,0:T(8,128)S(1)} %get-tuple-element.95), channel_id=1, source_target_pairs={{0,8},{8,0},{16,24},{24,16},{32,40},{40,32},{48,56},{56,48},{64,72... | collective-permute-start | bytes 1572872 | tf_op jit(solution)/shard_map/ppermute | solution.py:371
  68.7 2.3 %constant_dynamic-slice_fusion.6 = (f32[512,512]{1,0:T(8,128)S(1)}, f32[512,512]{1,0:T(8,128)S(1)}, f32[512,512]{1,0:T(8,128)S(1)}) fusion(f32[512,4096]{1,0:T(8,128)} %refs_4_.3, s32[]{:T(128)S(6)} %select_n.146, s32[]{:T(128)S(6)} %select_n.148, s32[]{:T(128)S(6)} %select_n.147), kind=kLoop, calls=%fused_computation.23 | loop fusion | bytes 6291468 | tf_op jit(solution)/shard_map/dynamic_slice | solution.py:382
  71.8 3.3 %collective-permute-done.13 = f32[1024,128]{1,0:T(8,128)} collective-permute-done((f32[1024,128]{1,0:T(8,128)S(1)}, f32[1024,128]{1,0:T(8,128)}, u32[]{:S(2)}, u32[]{:S(2)}) %collective-permute-start.13) | collective-permute-done | bytes 524320 | tf_op jit(solution)/shard_map/ppermute | solution.py:371
  75.1 2.8 %collective-permute-done.14 = f32[1024,128]{1,0:T(8,128)} collective-permute-done((f32[1024,128]{1,0:T(8,128)S(1)}, f32[1024,128]{1,0:T(8,128)}, u32[]{:S(2)}, u32[]{:S(2)}) %collective-permute-start.14) | collective-permute-done | bytes 524320 | tf_op jit(solution)/shard_map/ppermute | solution.py:371
  78.0 1.6 collective-permute-start.15
  80.9 1.9 pad_maximum_fusion.2
  85.3 3.2 %collective-permute-done.15 = f32[1024,128]{1,0:T(8,128)S(1)} collective-permute-done((f32[1024,128]{1,0:T(8,128)S(1)}, f32[1024,128]{1,0:T(8,128)S(1)}, u32[]{:S(2)}, u32[]{:S(2)}) %collective-permute-start.15) | collective-permute-done | bytes 524320 | tf_op jit(solution)/shard_map/ppermute | solution.py:371
  88.5 1.5 collective-permute-done.16
  90.0 7.4 %collective-permute-start.18 = (f32[1024,128]{1,0:T(8,128)S(1)}, f32[1024,128]{1,0:T(8,128)S(1)}, u32[]{:S(2)}, u32[]{:S(2)}) collective-permute-start(f32[1024,128]{1,0:T(8,128)S(1)} %add.220), channel_id=1, source_target_pairs={{0,8},{8,0},{16,24},{24,16},{32,40},{40,32},{48,56},{56,48},{64,72... | collective-permute-start | bytes 1572872 | tf_op jit(solution)/shard_map/ppermute | solution.py:371
  97.5 9.6 %shard_map.75 = (f32[1024,512]{1,0:T(8,128)S(1)}, f32[1024,256]{1,0:T(8,128)S(1)}) custom-call(s32[1]{0:T(128)} %bitcast.1.first_row, s32[4,4]{1,0:T(4,128)S(1)} %get-tuple-element.80.back, s32[2]{0:T(128)S(1)} %add_convert_fusion.wraps, f32[1024,512]{1,0:T(8,128)S(1)} %copy-done.13, f32[1024,128]{1,0:T(8,128)S(1)} %slice.20.refs_2_.k_far, ...), custom_call_target="tpu_custom_call" | custom-call | flops 4294967296 | bytes 4194304 | tf_op jit(solution)/shard_map/pallas_call | solution.py:159
  108.9 9.7 %shard_map.76 = (f32[256,512]{1,0:T(8,128)}, f32[256,512]{1,0:T(8,128)S(1)}) custom-call(s32[1]{0:T(128)} %bitcast.1.first_row, f32[1024,512]{1,0:T(8,128)S(1)} %copy-done.13, f32[1024,512]{1,0:T(8,128)S(1)} %get-tuple-element.108.near, f32[1024,256]{1,0:T(8,128)S(1)} %get-tuple-element.109.stats, f32[1024,128]{1,0:T(8,128)S(1)} %add.221.k_a, ...), custom_call_target="tpu_custom_call" | custom-call | flops 4294967296 | bytes 4194304 | tf_op jit(solution)/shard_map/pallas_call | solution.py:226
  119.2 2.3 %collective-permute-done.19.refs_2_ = f32[256,512]{1,0:T(8,128)S(1)} collective-permute-done((f32[256,512]{1,0:T(8,128)}, f32[256,512]{1,0:T(8,128)S(1)}, u32[]{:S(2)}, u32[]{:S(2)}) %collective-permute-start.19) | collective-permute-done | bytes 524320 | tf_op jit(solution)/shard_map/ppermute | solution.py:380
  121.5 2.6 %constant_dynamic-slice_fusion.1 = (f32[512,512]{1,0:T(8,128)S(1)}, f32[512,512]{1,0:T(8,128)S(1)}, f32[512,512]{1,0:T(8,128)S(1)}, f32[512,512]{1,0:T(8,128)S(1)}) fusion(f32[512,2048]{1,0:T(8,128)} %collective-permute-done.22.refs_6_, s32[]{:T(128)S(6)} %select_n.149, s32[]{:T(128)S(6)} %select_n.150, f32[512,2048]{1,0:T(8,128)} %collective-permute-done.21.refs_4_), kind=kLoop, calls=%fused_computation.18 | loop fusion | bytes 8388616 | tf_op jit(solution)/shard_map/dynamic_slice | solution.py:382
  124.1 1.5 pad_maximum_fusion.3
  125.8 1.6 pad_maximum_fusion.4
  128.2 1.9 collective-permute-start.25
  130.1 7.5 %shard_map.77.refs_8_ = f32[2,256,1024]{2,1,0:T(8,128)S(1)} custom-call(s32[4]{0:T(128)S(1)} %pad_add_fusion.order, f32[256,512]{1,0:T(8,128)} %get-tuple-element.119.refs_0_, f32[256,512]{1,0:T(8,128)S(1)} %get-tuple-element.120.refs_1_, f32[256,512]{1,0:T(8,128)S(1)} %collective-permute-done.19.refs_2_, f32[256,512]{1,0:T(8,128)} %collective-permute-done.20.refs_3_, ...), custom_call_target="tpu_custom_call" | custom-call | flops 4294967296 | bytes 4194304 | tf_op jit(solution)/shard_map/pallas_call | solution.py:279
  137.6 9.1 %shard_map.78 = (f32[256,512]{1,0:T(8,128)S(1)}, f32[256,512]{1,0:T(8,128)S(1)}) custom-call(s32[1]{0:T(128)} %bitcast.1.first_row, f32[1024,512]{1,0:T(8,128)S(1)} %copy-done.14, f32[1024,512]{1,0:T(8,128)S(1)} %copy-done.22, f32[1024,256]{1,0:T(8,128)S(1)} %copy-done.24, f32[1024,128]{1,0:T(8,128)S(1)} %add.221.k_a, f32[1024,128]{1,0:T(8,128)S(1)} %add.222.k_b, ...), custom_call_target="tpu_custom_call" | custom-call | flops 4294967296 | bytes 4194304 | tf_op jit(solution)/shard_map/pallas_call | solution.py:226
  149.5 1.3 collective-permute-start.31
  150.8 7.2 %shard_map.79 = (f32[256,512]{1,0:T(8,128)S(1)}, f32[256,512]{1,0:T(8,128)S(1)}, f32[256,512]{1,0:T(8,128)S(1)}, f32[256,512]{1,0:T(8,128)S(1)}) custom-call(s32[1]{0:T(128)} %bitcast.7.core, f32[256,512]{1,0:T(8,128)S(1)} %collective-permute-done.24.refs_0_, f32[256,512]{1,0:T(8,128)S(1)} %collective-permute-done.25.refs_1_, ...), custom_call_target="tpu_custom_call" | custom-call | flops 4294967296 | bytes 4194304 | tf_op jit(solution)/shard_map/pallas_call | solution.py:327
  158.1 3.2 %collective-permute-done.30.refs_0_ = f32[256,512]{1,0:T(8,128)S(1)} collective-permute-done((f32[256,512]{1,0:T(8,128)S(1)}, f32[256,512]{1,0:T(8,128)S(1)}, u32[]{:S(2)}, u32[]{:S(2)}) %collective-permute-start.30) | collective-permute-done | bytes 524320 | tf_op jit(solution)/shard_map/ppermute | solution.py:380
  161.2 3.4 %collective-permute-done.31.refs_1_ = f32[256,512]{1,0:T(8,128)S(1)} collective-permute-done((f32[256,512]{1,0:T(8,128)S(1)}, f32[256,512]{1,0:T(8,128)S(1)}, u32[]{:S(2)}, u32[]{:S(2)}) %collective-permute-start.31) | collective-permute-done | bytes 524320 | tf_op jit(solution)/shard_map/ppermute | solution.py:380
  165.2 1.3 collective-permute-start.36
  166.5 7.2 %shard_map.80.refs_8_ = f32[2,256,1024]{2,1,0:T(8,128)S(1)} custom-call(s32[4]{0:T(128)S(1)} %pad_add_fusion.order, f32[256,512]{1,0:T(8,128)S(1)} %get-tuple-element.134.refs_0_, f32[256,512]{1,0:T(8,128)S(1)} %get-tuple-element.135.refs_1_, f32[256,512]{1,0:T(8,128)S(1)} %collective-permute-done.32.refs_2_, ...), custom_call_target="tpu_custom_call" | custom-call | flops 4294967296 | bytes 4194304 | tf_op jit(solution)/shard_map/pallas_call | solution.py:279
  173.7 1.3 copy-done.3
  175.0 7.2 %shard_map.81 = (f32[256,512]{1,0:T(8,128)S(1)}, f32[256,512]{1,0:T(8,128)S(1)}, f32[256,512]{1,0:T(8,128)S(1)}, f32[256,512]{1,0:T(8,128)S(1)}) custom-call(s32[1]{0:T(128)} %bitcast.7.core, f32[256,512]{1,0:T(8,128)S(1)} %collective-permute-done.30.refs_0_, f32[256,512]{1,0:T(8,128)S(1)} %collective-permute-done.31.refs_1_, ...), custom_call_target="tpu_custom_call" | custom-call | flops 4294967296 | bytes 4194304 | tf_op jit(solution)/shard_map/pallas_call | solution.py:327
  182.3 2.1 %collective-permute-start.39 = (f32[256,512]{1,0:T(8,128)S(1)}, f32[256,512]{1,0:T(8,128)S(1)}, u32[]{:S(2)}, u32[]{:S(2)}) collective-permute-start(f32[256,512]{1,0:T(8,128)S(1)} %get-tuple-element.150), channel_id=1, source_target_pairs={{0,2},{1,3},{2,0},{3,1},{4,6},{5,7},{6,4},{7,5},{8,10},{9,11},{10,... | collective-permute-start | bytes 1572872 | tf_op jit(solution)/shard_map/ppermute | solution.py:380
  184.4 1.9 collective-permute-start.38
  186.5 9.6 %collective-permute-done.39 = f32[256,512]{1,0:T(8,128)S(1)} collective-permute-done((f32[256,512]{1,0:T(8,128)S(1)}, f32[256,512]{1,0:T(8,128)S(1)}, u32[]{:S(2)}, u32[]{:S(2)}) %collective-permute-start.39) | collective-permute-done | bytes 524320 | tf_op jit(solution)/shard_map/ppermute | solution.py:380
  196.1 2.6 %collective-permute-done.38 = f32[256,512]{1,0:T(8,128)S(1)} collective-permute-done((f32[256,512]{1,0:T(8,128)S(1)}, f32[256,512]{1,0:T(8,128)S(1)}, u32[]{:S(2)}, u32[]{:S(2)}) %collective-permute-start.38) | collective-permute-done | bytes 524320 | tf_op jit(solution)/shard_map/ppermute | solution.py:380
  198.8 1.5 pad_maximum_fusion.5
  (160 shorter events, 21.3 us)
Async XLA Ops:
  0.0 16.4 %copy-start = (s32[32,3]{0,1:T(4,128)S(1)}, s32[32,3]{0,1:T(4,128)}, u32[]{:S(2)}) copy-start(s32[32,3]{0,1:T(4,128)} %param.11) | copy-start | bytes 1156
  0.0 18.2 %collective-permute-start = (f32[1024,128]{1,0:T(8,128)}, f32[1024,128]{1,0:T(8,128)S(1)}, u32[]{:S(2)}, u32[]{:S(2)}) collective-permute-start(f32[1024,128]{1,0:T(8,128)} %k_own.1), channel_id=1, source_target_pairs={{0,8},{8,16},{16,24},{24,0},{32,40},{40,48},{48,56},{56,32},{64,72... | collective-permute-start | bytes 1572872 | tf_op jit(solution)/shard_map/ppermute | solution.py:371
  1.5 19.0 %collective-permute-start.1 = (f32[1024,128]{1,0:T(8,128)}, f32[1024,128]{1,0:T(8,128)S(1)}, u32[]{:S(2)}, u32[]{:S(2)}) collective-permute-start(f32[1024,128]{1,0:T(8,128)} %k_own.1), channel_id=1, source_target_pairs={{0,24},{8,0},{16,8},{24,16},{32,56},{40,32},{48,40},{56,48},{64,88... | collective-permute-start | bytes 1572872 | tf_op jit(solution)/shard_map/ppermute | solution.py:371
  2.0 18.5 %collective-permute-start.2 = (f32[1024,128]{1,0:T(8,128)}, f32[1024,128]{1,0:T(8,128)S(1)}, u32[]{:S(2)}, u32[]{:S(2)}) collective-permute-start(f32[1024,128]{1,0:T(8,128)} %v_own.1), channel_id=1, source_target_pairs={{0,32},{8,40},{16,48},{24,56},{32,64},{40,72},{48,80},{56,88},{64,... | collective-permute-start | bytes 1572872 | tf_op jit(solution)/shard_map/ppermute | solution.py:371
  3.9 16.6 %collective-permute-start.3 = (f32[1024,128]{1,0:T(8,128)}, f32[1024,128]{1,0:T(8,128)S(1)}, u32[]{:S(2)}, u32[]{:S(2)}) collective-permute-start(f32[1024,128]{1,0:T(8,128)} %v_own.1), channel_id=1, source_target_pairs={{0,96},{8,104},{16,112},{24,120},{32,0},{40,8},{48,16},{56,24},{64... | collective-permute-start | bytes 1572872 | tf_op jit(solution)/shard_map/ppermute | solution.py:371
  13.7 107.8 %collective-permute-start.21 = (f32[512,2048]{1,0:T(8,128)}, f32[512,2048]{1,0:T(8,128)}, u32[]{:S(2)}, u32[]{:S(2)}) collective-permute-start(f32[512,2048]{1,0:T(8,128)} %get-tuple-element.170), channel_id=1, source_target_pairs={{0,2},{1,3},{2,0},{3,1},{4,6},{5,7},{6,4},{7,5},{8,10},{9,11},{10,... | collective-permute-start | bytes 12582920 | tf_op jit(solution)/shard_map/ppermute | solution.py:380
  18.2 26.7 %copy-start.9 = (f32[1024,128]{1,0:T(8,128)}, f32[1024,128]{1,0:T(8,128)S(1)}, u32[]{:S(2)}) copy-start(f32[1024,128]{1,0:T(8,128)S(1)} %collective-permute-done.refs_3_.k_left) | copy-start | bytes 1572868
  18.3 103.2 %collective-permute-start.22 = (f32[512,2048]{1,0:T(8,128)}, f32[512,2048]{1,0:T(8,128)}, u32[]{:S(2)}, u32[]{:S(2)}) collective-permute-start(f32[512,2048]{1,0:T(8,128)} %get-tuple-element.169), channel_id=1, source_target_pairs={{0,6},{1,7},{2,4},{3,5},{4,2},{5,3},{6,0},{7,1},{8,14},{9,15},{10,... | collective-permute-start | bytes 12582920 | tf_op jit(solution)/shard_map/ppermute | solution.py:380
  20.7 12.3 %collective-permute-start.5 = (f32[1024,128]{1,0:T(8,128)S(1)}, f32[1024,128]{1,0:T(8,128)S(1)}, u32[]{:S(2)}, u32[]{:S(2)}) collective-permute-start(f32[1024,128]{1,0:T(8,128)S(1)} %collective-permute-done.3.refs_1_), channel_id=1, source_target_pairs={{0,96},{8,104},{16,112},{24,120},{32,0},{40,8},{48,16},{56,24},{64... | collective-permute-start | bytes 1572872 | tf_op jit(solution)/shard_map/ppermute | solution.py:371
  22.8 22.2 %copy-start.7 = (f32[1024,128]{1,0:T(8,128)S(1)}, f32[1024,128]{1,0:T(8,128)}, u32[]{:S(2)}) copy-start(f32[1024,128]{1,0:T(8,128)} %k_own.1) | copy-start | bytes 1572868
  22.8 17.4 %collective-permute-start.4 = (f32[1536,128]{1,0:T(8,128)S(1)}, f32[1536,128]{1,0:T(8,128)S(1)}, u32[]{:S(2)}, u32[]{:S(2)}) collective-permute-start(f32[1536,128]{1,0:T(8,128)S(1)} %pad_maximum_fusion.6), channel_id=1, source_target_pairs={{0,24},{8,0},{16,8},{24,16},{32,56},{40,32},{48,40},{56,48},{64,88... | collective-permute-start | bytes 2359304 | tf_op jit(solution)/shard_map/ppermute | solution.py:371
  24.7 29.4 %copy-start.12 = (f32[1024,128]{1,0:T(8,128)S(1)}, f32[1024,128]{1,0:T(8,128)}, u32[]{:S(2)}) copy-start(f32[1024,128]{1,0:T(8,128)} %copy-done.11) | copy-start | bytes 1572868
  24.7 17.1 %collective-permute-start.6 = (f32[1536,128]{1,0:T(8,128)S(1)}, f32[1536,128]{1,0:T(8,128)S(1)}, u32[]{:S(2)}, u32[]{:S(2)}) collective-permute-start(f32[1536,128]{1,0:T(8,128)S(1)} %pad_maximum_fusion.7), channel_id=1, source_target_pairs={{0,8},{8,16},{16,24},{24,0},{32,40},{40,48},{48,56},{56,32},{64,72... | collective-permute-start | bytes 2359304 | tf_op jit(solution)/shard_map/ppermute | solution.py:371
  33.0 0.7 collective-permute-start.7
  41.9 8.6 %collective-permute-start.8 = (f32[512,128]{1,0:T(8,128)S(1)}, f32[512,128]{1,0:T(8,128)S(1)}, u32[]{:S(2)}, u32[]{:S(2)}) collective-permute-start(f32[512,128]{1,0:T(8,128)S(1)} %slice.21), channel_id=1, source_target_pairs={{0,8},{8,16},{16,24},{24,0},{32,40},{40,48},{48,56},{56,32},{64,72... | collective-permute-start | bytes 786440 | tf_op jit(solution)/shard_map/ppermute | solution.py:371
  42.7 21.8 %collective-permute-start.10 = (f32[1024,128]{1,0:T(8,128)S(1)}, f32[1024,128]{1,0:T(8,128)S(1)}, u32[]{:S(2)}, u32[]{:S(2)}) collective-permute-start(f32[1024,128]{1,0:T(8,128)S(1)} %slice.20.refs_2_.k_far), channel_id=1, source_target_pairs={{0,32},{8,40},{32,64},{40,72},{64,96},{72,104},{1,33},{9,41},{33,6... | collective-permute-start | bytes 1572872 | tf_op jit(solution)/shard_map/ppermute | solution.py:371
  46.1 21.7 %copy-start.5 = (f32[1024,128]{1,0:T(8,128)}, f32[1024,128]{1,0:T(8,128)S(1)}, u32[]{:S(2)}) copy-start(f32[1024,128]{1,0:T(8,128)S(1)} %get-tuple-element.90) | copy-start | bytes 1572868
  46.1 21.7 %collective-permute-start.11 = (f32[1024,128]{1,0:T(8,128)S(1)}, f32[1024,128]{1,0:T(8,128)S(1)}, u32[]{:S(2)}, u32[]{:S(2)}) collective-permute-start(f32[1024,128]{1,0:T(8,128)S(1)} %get-tuple-element.90), channel_id=1, source_target_pairs={{0,32},{8,40},{16,48},{24,56},{32,0},{40,8},{48,16},{56,24},{64,96... | collective-permute-start | bytes 1572872 | tf_op jit(solution)/shard_map/ppermute | solution.py:371
  50.5 7.5 %collective-permute-start.9 = (f32[512,128]{1,0:T(8,128)S(1)}, f32[512,128]{1,0:T(8,128)S(1)}, u32[]{:S(2)}, u32[]{:S(2)}) collective-permute-start(f32[512,128]{1,0:T(8,128)S(1)} %slice.22), channel_id=1, source_target_pairs={{0,24},{8,0},{16,8},{24,16},{32,56},{40,32},{48,40},{56,48},{64,88... | collective-permute-start | bytes 786440 | tf_op jit(solution)/shard_map/ppermute | solution.py:371
  58.6 13.2 %collective-permute-start.12 = (f32[1024,128]{1,0:T(8,128)S(1)}, f32[1024,128]{1,0:T(8,128)}, u32[]{:S(2)}, u32[]{:S(2)}) collective-permute-start(f32[1024,128]{1,0:T(8,128)S(1)} %get-tuple-element.91), channel_id=1, source_target_pairs={{0,96},{8,104},{16,112},{24,120},{32,64},{40,72},{48,80},{56,88},{... | collective-permute-start | bytes 1572872 | tf_op jit(solution)/shard_map/ppermute | solution.py:371
  65.4 9.7 %collective-permute-start.13 = (f32[1024,128]{1,0:T(8,128)S(1)}, f32[1024,128]{1,0:T(8,128)}, u32[]{:S(2)}, u32[]{:S(2)}) collective-permute-start(f32[1024,128]{1,0:T(8,128)S(1)} %get-tuple-element.95), channel_id=1, source_target_pairs={{0,8},{8,0},{16,24},{24,16},{32,40},{40,32},{48,56},{56,48},{64,72... | collective-permute-start | bytes 1572872 | tf_op jit(solution)/shard_map/ppermute | solution.py:371
  68.7 9.3 %collective-permute-start.14 = (f32[1024,128]{1,0:T(8,128)S(1)}, f32[1024,128]{1,0:T(8,128)}, u32[]{:S(2)}, u32[]{:S(2)}) collective-permute-start(f32[1024,128]{1,0:T(8,128)S(1)} %get-tuple-element.96), channel_id=1, source_target_pairs={{0,24},{8,16},{16,8},{24,0},{32,56},{40,48},{48,40},{56,32},{64,88... | collective-permute-start | bytes 1572872 | tf_op jit(solution)/shard_map/ppermute | solution.py:371
  78.0 10.5 %collective-permute-start.15 = (f32[1024,128]{1,0:T(8,128)S(1)}, f32[1024,128]{1,0:T(8,128)S(1)}, u32[]{:S(2)}, u32[]{:S(2)}) collective-permute-start(f32[1024,128]{1,0:T(8,128)S(1)} %add.217), channel_id=1, source_target_pairs={{0,96},{8,104},{16,112},{24,120},{32,64},{40,72},{48,80},{56,88},{... | collective-permute-start | bytes 1572872 | tf_op jit(solution)/shard_map/ppermute | solution.py:371
  80.7 9.3 %collective-permute-start.16 = (f32[1024,128]{1,0:T(8,128)S(1)}, f32[1024,128]{1,0:T(8,128)S(1)}, u32[]{:S(2)}, u32[]{:S(2)}) collective-permute-start(f32[1024,128]{1,0:T(8,128)S(1)} %add.218), channel_id=1, source_target_pairs={{0,32},{8,40},{16,48},{24,56},{32,0},{40,8},{48,16},{56,24},{64,96... | collective-permute-start | bytes 1572872 | tf_op jit(solution)/shard_map/ppermute | solution.py:371
  80.8 16.6 %copy-start.26 = (f32[1536,128]{1,0:T(8,128)S(1)}, f32[1536,128]{1,0:T(8,128)}, u32[]{:S(2)}) copy-start(f32[1536,128]{1,0:T(8,128)} %copy-done.25) | copy-start | bytes 2359300
  80.9 16.6 %copy-start.20 = (f32[512,128]{1,0:T(8,128)S(1)}, f32[512,128]{1,0:T(8,128)}, u32[]{:S(2)}) copy-start(f32[512,128]{1,0:T(8,128)} %copy-done.19) | copy-start | bytes 786436
  82.8 14.8 %copy-start.18 = (f32[1024,128]{1,0:T(8,128)S(1)}, f32[1024,128]{1,0:T(8,128)}, u32[]{:S(2)}) copy-start(f32[1024,128]{1,0:T(8,128)} %copy-done.17) | copy-start | bytes 1572868
  82.8 47.3 %collective-permute-start.23 = (f32[512,1536]{1,0:T(8,128)}, f32[512,1536]{1,0:T(8,128)}, u32[]{:S(2)}, u32[]{:S(2)}) collective-permute-start(f32[512,1536]{1,0:T(8,128)} %pad_maximum_fusion.2), channel_id=1, source_target_pairs={{0,1},{1,0},{2,3},{3,2},{4,5},{5,4},{6,7},{7,6},{8,9},{9,8},{10,11... | collective-permute-start | bytes 9437192 | tf_op jit(solution)/shard_map/ppermute | solution.py:380
  88.5 18.7 %collective-permute-start.17 = (f32[1024,128]{1,0:T(8,128)S(1)}, f32[1024,128]{1,0:T(8,128)S(1)}, u32[]{:S(2)}, u32[]{:S(2)}) collective-permute-start(f32[1024,128]{1,0:T(8,128)S(1)} %add.219), channel_id=1, source_target_pairs={{0,24},{8,16},{16,8},{24,0},{32,56},{40,48},{48,40},{56,32},{64,88... | collective-permute-start | bytes 1572872 | tf_op jit(solution)/shard_map/ppermute | solution.py:371
  90.0 17.2 %collective-permute-start.18 = (f32[1024,128]{1,0:T(8,128)S(1)}, f32[1024,128]{1,0:T(8,128)S(1)}, u32[]{:S(2)}, u32[]{:S(2)}) collective-permute-start(f32[1024,128]{1,0:T(8,128)S(1)} %add.220), channel_id=1, source_target_pairs={{0,8},{8,0},{16,24},{24,16},{32,40},{40,32},{48,56},{56,48},{64,72... | collective-permute-start | bytes 1572872 | tf_op jit(solution)/shard_map/ppermute | solution.py:371
  118.7 2.8 %collective-permute-start.19 = (f32[256,512]{1,0:T(8,128)}, f32[256,512]{1,0:T(8,128)S(1)}, u32[]{:S(2)}, u32[]{:S(2)}) collective-permute-start(f32[256,512]{1,0:T(8,128)} %get-tuple-element.119.refs_0_), channel_id=1, source_target_pairs={{0,1},{1,0},{2,3},{3,2},{4,5},{5,4},{6,7},{7,6},{8,9},{9,8},{10,11... | collective-permute-start | bytes 1572872 | tf_op jit(solution)/shard_map/ppermute | solution.py:380
  118.7 2.8 %collective-permute-start.20 = (f32[256,512]{1,0:T(8,128)S(1)}, f32[256,512]{1,0:T(8,128)}, u32[]{:S(2)}, u32[]{:S(2)}) collective-permute-start(f32[256,512]{1,0:T(8,128)S(1)} %get-tuple-element.120.refs_1_), channel_id=1, source_target_pairs={{0,1},{1,0},{2,3},{3,2},{4,5},{5,4},{6,7},{7,6},{8,9},{9,8},{10,11... | collective-permute-start | bytes 1572872 | tf_op jit(solution)/shard_map/ppermute | solution.py:380
  125.6 25.2 %collective-permute-start.28 = (f32[512,1024]{1,0:T(8,128)}, f32[512,1024]{1,0:T(8,128)}, u32[]{:S(2)}, u32[]{:S(2)}) collective-permute-start(f32[512,1024]{1,0:T(8,128)} %pad_maximum_fusion.3), channel_id=1, source_target_pairs={{0,1},{1,0},{2,3},{3,2},{4,5},{5,4},{6,7},{7,6},{8,9},{9,8},{10,11... | collective-permute-start | bytes 6291464 | tf_op jit(solution)/shard_map/ppermute | solution.py:380
  127.4 23.4 %collective-permute-start.29 = (f32[512,1024]{1,0:T(8,128)}, f32[512,1024]{1,0:T(8,128)}, u32[]{:S(2)}, u32[]{:S(2)}) collective-permute-start(f32[512,1024]{1,0:T(8,128)} %pad_maximum_fusion.4), channel_id=1, source_target_pairs={{0,1},{1,0},{2,3},{3,2},{4,5},{5,4},{6,7},{7,6},{8,9},{9,8},{10,11... | collective-permute-start | bytes 6291464 | tf_op jit(solution)/shard_map/ppermute | solution.py:380
  127.8 18.9 %collective-permute-start.24 = (f32[256,512]{1,0:T(8,128)}, f32[256,512]{1,0:T(8,128)S(1)}, u32[]{:S(2)}, u32[]{:S(2)}) collective-permute-start(f32[256,512]{1,0:T(8,128)} %get-tuple-element.119.refs_0_), channel_id=1, source_target_pairs={{0,2},{1,3},{2,0},{3,1},{4,6},{5,7},{6,4},{7,5},{8,10},{9,11},{10,... | collective-permute-start | bytes 1572872 | tf_op jit(solution)/shard_map/ppermute | solution.py:380
  128.2 18.6 %collective-permute-start.25 = (f32[256,512]{1,0:T(8,128)S(1)}, f32[256,512]{1,0:T(8,128)S(1)}, u32[]{:S(2)}, u32[]{:S(2)}) collective-permute-start(f32[256,512]{1,0:T(8,128)S(1)} %get-tuple-element.120.refs_1_), channel_id=1, source_target_pairs={{0,6},{1,7},{2,4},{3,5},{4,2},{5,3},{6,0},{7,1},{8,14},{9,15},{10,... | collective-permute-start | bytes 1572872 | tf_op jit(solution)/shard_map/ppermute | solution.py:380
  146.7 2.0 collective-permute-start.26
  146.8 2.6 %collective-permute-start.27 = (f32[256,512]{1,0:T(8,128)S(1)}, f32[256,512]{1,0:T(8,128)S(1)}, u32[]{:S(2)}, u32[]{:S(2)}) collective-permute-start(f32[256,512]{1,0:T(8,128)S(1)} %collective-permute-done.25.refs_1_), channel_id=1, source_target_pairs={{0,1},{1,0},{2,3},{3,2},{4,5},{5,4},{6,7},{7,6},{8,9},{9,8},{10,11... | collective-permute-start | bytes 1572872 | tf_op jit(solution)/shard_map/ppermute | solution.py:380
  147.3 13.9 %collective-permute-start.30 = (f32[256,512]{1,0:T(8,128)S(1)}, f32[256,512]{1,0:T(8,128)S(1)}, u32[]{:S(2)}, u32[]{:S(2)}) collective-permute-start(f32[256,512]{1,0:T(8,128)S(1)} %get-tuple-element.134.refs_0_), channel_id=1, source_target_pairs={{0,2},{1,3},{2,0},{3,1},{4,6},{5,7},{6,4},{7,5},{8,10},{9,11},{10,... | collective-permute-start | bytes 1572872 | tf_op jit(solution)/shard_map/ppermute | solution.py:380
  148.7 15.9 %collective-permute-start.32 = (f32[256,512]{1,0:T(8,128)S(1)}, f32[256,512]{1,0:T(8,128)S(1)}, u32[]{:S(2)}, u32[]{:S(2)}) collective-permute-start(f32[256,512]{1,0:T(8,128)S(1)} %get-tuple-element.134.refs_0_), channel_id=1, source_target_pairs={{0,1},{1,0},{2,3},{3,2},{4,5},{5,4},{6,7},{7,6},{8,9},{9,8},{10,11... | collective-permute-start | bytes 1572872 | tf_op jit(solution)/shard_map/ppermute | solution.py:380
  149.5 15.2 %collective-permute-start.31 = (f32[256,512]{1,0:T(8,128)S(1)}, f32[256,512]{1,0:T(8,128)S(1)}, u32[]{:S(2)}, u32[]{:S(2)}) collective-permute-start(f32[256,512]{1,0:T(8,128)S(1)} %get-tuple-element.135.refs_1_), channel_id=1, source_target_pairs={{0,6},{1,7},{2,4},{3,5},{4,2},{5,3},{6,0},{7,1},{8,14},{9,15},{10,... | collective-permute-start | bytes 1572872 | tf_op jit(solution)/shard_map/ppermute | solution.py:380
  150.8 13.8 %collective-permute-start.33 = (f32[256,512]{1,0:T(8,128)S(1)}, f32[256,512]{1,0:T(8,128)S(1)}, u32[]{:S(2)}, u32[]{:S(2)}) collective-permute-start(f32[256,512]{1,0:T(8,128)S(1)} %get-tuple-element.135.refs_1_), channel_id=1, source_target_pairs={{0,1},{1,0},{2,3},{3,2},{4,5},{5,4},{6,7},{7,6},{8,9},{9,8},{10,11... | collective-permute-start | bytes 1572872 | tf_op jit(solution)/shard_map/ppermute | solution.py:380
  164.7 10.4 %collective-permute-start.34 = (f32[256,512]{1,0:T(8,128)S(1)}, f32[256,512]{1,0:T(8,128)S(1)}, u32[]{:S(2)}, u32[]{:S(2)}) collective-permute-start(f32[256,512]{1,0:T(8,128)S(1)} %collective-permute-done.30.refs_0_), channel_id=1, source_target_pairs={{0,1},{1,0},{2,3},{3,2},{4,5},{5,4},{6,7},{7,6},{8,9},{9,8},{10,11... | collective-permute-start | bytes 1572872 | tf_op jit(solution)/shard_map/ppermute | solution.py:380
  164.7 10.4 %collective-permute-start.35 = (f32[256,512]{1,0:T(8,128)S(1)}, f32[256,512]{1,0:T(8,128)S(1)}, u32[]{:S(2)}, u32[]{:S(2)}) collective-permute-start(f32[256,512]{1,0:T(8,128)S(1)} %collective-permute-done.31.refs_1_), channel_id=1, source_target_pairs={{0,1},{1,0},{2,3},{3,2},{4,5},{5,4},{6,7},{7,6},{8,9},{9,8},{10,11... | collective-permute-start | bytes 1572872 | tf_op jit(solution)/shard_map/ppermute | solution.py:380
  165.2 17.1 %collective-permute-start.36 = (f32[256,512]{1,0:T(8,128)S(1)}, f32[256,512]{1,0:T(8,128)S(1)}, u32[]{:S(2)}, u32[]{:S(2)}) collective-permute-start(f32[256,512]{1,0:T(8,128)S(1)} %get-tuple-element.142), channel_id=1, source_target_pairs={{0,6},{1,7},{2,4},{3,5},{4,2},{5,3},{6,0},{7,1},{8,14},{9,15},{10,... | collective-permute-start | bytes 1572872 | tf_op jit(solution)/shard_map/ppermute | solution.py:380
  166.5 15.8 %collective-permute-start.37 = (f32[256,512]{1,0:T(8,128)S(1)}, f32[256,512]{1,0:T(8,128)S(1)}, u32[]{:S(2)}, u32[]{:S(2)}) collective-permute-start(f32[256,512]{1,0:T(8,128)S(1)} %get-tuple-element.143), channel_id=1, source_target_pairs={{0,2},{1,3},{2,0},{3,1},{4,6},{5,7},{6,4},{7,5},{8,10},{9,11},{10,... | collective-permute-start | bytes 1572872 | tf_op jit(solution)/shard_map/ppermute | solution.py:380
  182.3 13.7 %collective-permute-start.39 = (f32[256,512]{1,0:T(8,128)S(1)}, f32[256,512]{1,0:T(8,128)S(1)}, u32[]{:S(2)}, u32[]{:S(2)}) collective-permute-start(f32[256,512]{1,0:T(8,128)S(1)} %get-tuple-element.150), channel_id=1, source_target_pairs={{0,2},{1,3},{2,0},{3,1},{4,6},{5,7},{6,4},{7,5},{8,10},{9,11},{10,... | collective-permute-start | bytes 1572872 | tf_op jit(solution)/shard_map/ppermute | solution.py:380
  184.4 14.3 %collective-permute-start.38 = (f32[256,512]{1,0:T(8,128)S(1)}, f32[256,512]{1,0:T(8,128)S(1)}, u32[]{:S(2)}, u32[]{:S(2)}) collective-permute-start(f32[256,512]{1,0:T(8,128)S(1)} %get-tuple-element.148), channel_id=1, source_target_pairs={{0,6},{1,7},{2,4},{3,5},{4,2},{5,3},{6,0},{7,1},{8,14},{9,15},{10,... | collective-permute-start | bytes 1572872 | tf_op jit(solution)/shard_map/ppermute | solution.py:380
  (22 other events, 153.5 us)

commit v6 on v5

--- a/solution.py
+++ b/solution.py
@@ -13,7 +13,7 @@
 TILE = 256
 FAR = 1 << 30
 LOW = -1e30
-LARGE = pl.CostEstimate(flops=4 << 30, bytes_accessed=4 << 20, transcendentals=0)
+LARGE = pl.CostEstimate(flops=1 << 30, bytes_accessed=1 << 20, transcendentals=0)
 SMALL = pl.CostEstimate(flops=1024, bytes_accessed=1024, transcendentals=0)
 
 
@@ -80,7 +80,25 @@
 
 
 def query_parts(q):
-    return (jnp.concatenate([x, x], axis=1) for x in split(q * SCALE))
+    return (jnp.concatenate([x, x], axis=1) for x in split(q))
+
+
+def scale_kernel(q, out):
+    out[...] = q[...] * SCALE
+
+
+def scaled(q):
+    rows, width = q.shape
+    spec = pl.BlockSpec((TILE, width), lambda i: (i, 0))
+    return pl.pallas_call(
+        scale_kernel,
+        grid=(rows // TILE,),
+        out_shape=jax.ShapeDtypeStruct(q.shape, jnp.float32),
+        in_specs=[spec],
+        out_specs=spec,
+        compiler_params=pltpu.CompilerParams(vmem_limit_bytes=8 << 20),
+        cost_estimate=LARGE,
+    )(q)
 
 
 def weights_of(scores, top):
@@ -170,13 +188,13 @@
             pl.BlockSpec((TILE, HEAD_SIZE), lambda t, h: (t, h)),
         ],
         scratch_shapes=[pltpu.VMEM((3 * q.shape[0], 2 * HEAD_SIZE), jnp.bfloat16)] * 2,
-        compiler_params=pltpu.CompilerParams(vmem_limit_bytes=40 << 20),
+        compiler_params=pltpu.CompilerParams(vmem_limit_bytes=24 << 20),
         cost_estimate=LARGE,
     )(first_row, back, wraps, q, *arrays)
 
 
 def attend_kernel(
-    start, first_row, q, near, stats, k_a, k_b, v_a, v_b, vert_pos, out_a, out_b, vert_k, vert_v
+    start, first_row, q, near, stats, k_a, k_b, v_a, v_b, vert_pos, out, vert_k, vert_v
 ):
     turn = pl.program_id(0)
 
@@ -202,31 +220,21 @@
         total = total + keep * stats[:, 2 * part + 1 : 2 * part + 2]
         mixed = fold(dot(jnp.concatenate(split(weights), axis=0), vert_v[rows, :], DOWN))
         mixed = mixed[:, :HEAD_SIZE] + mixed[:, HEAD_SIZE:] + keep * near[:, columns]
-        mixed = mixed / total
-
-        @pl.when(turn == 0)
-        def _():
-            out_a[:, columns] = mixed
-
-        @pl.when(turn == 1)
-        def _():
-            out_b[:, columns] = mixed
+        out[0, :, columns] = mixed / total
 
 
 def attend(q, near, stats, start, first_row, arrays):
     width = q.shape[1]
     heads = width // HEAD_SIZE
     pair = 2
-    last = heads // pair - 1
     smem = pl.BlockSpec(memory_space=pltpu.SMEM)
     vmem = pl.BlockSpec(memory_space=pltpu.VMEM)
     base = start // TILE
     wide = (TILE, pair * HEAD_SIZE)
-    out = jax.ShapeDtypeStruct((TILE, width), jnp.float32)
     return pl.pallas_call(
         functools.partial(attend_kernel, start),
         grid=(2, heads // pair),
-        out_shape=[out, out],
+        out_shape=jax.ShapeDtypeStruct((2, TILE, width), jnp.float32),
         in_specs=[
             smem,
             pl.BlockSpec(wide, lambda t, h: (base + t, h)),
@@ -234,119 +242,94 @@
             pl.BlockSpec((TILE, HEAD_SIZE), lambda t, h: (base + t, h)),
         ]
         + [vmem] * len(arrays),
-        out_specs=[
-            pl.BlockSpec(wide, lambda t, h: (0, jnp.where(t == 0, h, last))),
-            pl.BlockSpec(wide, lambda t, h: (0, jnp.where(t == 0, 0, h))),
-        ],
+        out_specs=pl.BlockSpec((1, TILE, pair * HEAD_SIZE), lambda t, h: (t, 0, h)),
         scratch_shapes=[pltpu.VMEM((heads * 8 * BLOCK, 2 * HEAD_SIZE), jnp.bfloat16)] * 2,
-        compiler_params=pltpu.CompilerParams(vmem_limit_bytes=40 << 20),
+        compiler_params=pltpu.CompilerParams(vmem_limit_bytes=20 << 20),
         cost_estimate=LARGE,
     )(first_row, q, near, stats, *arrays)
 
 
-def stack_split(x, at, ref):
-    rows, depth = ref.shape
-    high, low = split(ref[...])
-    x[:rows, at : at + depth] = high
-    x[rows:, at : at + depth] = low
-
-
-def times_weight(x, w, refs):
-    depth = refs[0].shape[0]
-    for at, ref in enumerate(refs):
-        rows = slice(at * depth, (at + 1) * depth)
-        w[0, rows, :], w[1, rows, :] = split(ref[...])
-    return fold(dot(x[...], w[0], DOWN)) + dot(x[: x.shape[0] // 2, :], w[1], DOWN)
-
-
-def chip_kernel(order, *refs):
-    own, mate = refs[0:2], refs[2:4]
-    w_own, w_mate, out, x, w = refs[4:]
+def weight_term(x, block):
+    high, low = split(block)
+    return fold(dot(x, high, DOWN)) + dot(x[: x.shape[0] // 2], low, DOWN)
+
+
+def stack(rows):
+    return jnp.concatenate(split(rows), axis=0)
+
+
+def chip_kernel(order, own_a, own_b, w, out, x):
     for kind in range(2):
 
         @pl.when((pl.program_id(0) == kind) & (pl.program_id(1) == 0))
         def _():
-            stack_split(x, 0, own[kind])
-            stack_split(x, own[kind].shape[1], mate[kind])
-
-    out[0] = times_weight(x, w, (w_own, w_mate))
-
-
-def project_chip(own, mate, w_own, w_mate, order):
-    rows, depth = own[0].shape
+            x[...] = stack(jnp.concatenate([own_a[kind], own_b[kind]], axis=0))
+
+    out[0] = weight_term(x[...], w[...])
+
+
+def project_chip(own_a, own_b, weight, order):
+    _, rows, depth = own_a.shape
     width = depth
     vmem = pl.BlockSpec(memory_space=pltpu.VMEM)
     return pl.pallas_call(
         chip_kernel,
-        out_shape=jax.ShapeDtypeStruct((2, rows, 2 * width), jnp.float32),
+        out_shape=jax.ShapeDtypeStruct((2, 2 * rows, 4 * width), jnp.float32),
+        grid_spec=pltpu.PrefetchScalarGridSpec(
+            num_scalar_prefetch=1,
+            grid=(2, 4),
+            in_specs=[vmem, vmem, pl.BlockSpec((depth, width), lambda k, j, o: (0, o[4 * k + j]))],
+            out_specs=pl.BlockSpec((1, 2 * rows, width), lambda k, j, o: (k, 0, j)),
+            scratch_shapes=[pltpu.VMEM((4 * rows, depth), jnp.bfloat16)],
+        ),
+        compiler_params=pltpu.CompilerParams(vmem_limit_bytes=20 << 20),
+        cost_estimate=LARGE,
+    )(order, own_a, own_b, weight)
+
+
+def pair_kernel(cores, got_a, got_b, near, far, total, there, here, x):
+    for kind, (got, weight) in enumerate(((got_a, near), (got_b, far))):
+
+        @pl.when((pl.program_id(0) == kind) & (pl.program_id(1) == 0))
+        def _():
+            x[...] = stack(got[...])
+
+        for side, out in enumerate((there, here)):
+
+            @pl.when((pl.program_id(0) == kind) & (pl.program_id(1) == side))
+            def _():
+                out[0] = total[0] + weight_term(x[...], weight[...])
+
+
+def project_pair(got, near, far, total, unit, keep, cores):
+    rows, depth = got[0].shape
+    width = depth
+    base = 0 if keep else 2
+    vmem = pl.BlockSpec(memory_space=pltpu.VMEM)
+    out = jax.ShapeDtypeStruct((2, rows, width), jnp.float32)
+    out_spec = pl.BlockSpec((1, rows, width), lambda k, s, c: (k, 0, 0))
+    w_spec = lambda side: pl.BlockSpec(
+        (depth, width), lambda k, s, c: (0, base + c[side(k, s)])
+    )
+    return pl.pallas_call(
+        pair_kernel,
+        out_shape=[out, out],
         grid_spec=pltpu.PrefetchScalarGridSpec(
             num_scalar_prefetch=1,
             grid=(2, 2),
-            in_specs=[vmem] * 4
-            + [
-                pl.BlockSpec((depth, width), lambda k, d, o: (0, o[2 * k + d])),
-                pl.BlockSpec((depth, width), lambda k, d, o: (0, d * (k + 1))),
+            in_specs=[
+                vmem,
+                vmem,
+                w_spec(lambda k, s: jnp.where(k == 0, s, 1)),
+                w_spec(lambda k, s: jnp.where(k == 0, 0, s)),
+                pl.BlockSpec((1, rows, width), lambda k, s, c: (k, unit, 2 - base + s)),
             ],
-            out_specs=pl.BlockSpec((1, rows, width), lambda k, d, o: (k, 0, d)),
-            scratch_shapes=[
-                pltpu.VMEM((2 * rows, 2 * depth), jnp.bfloat16),
-                pltpu.VMEM((2, 2 * depth, width), jnp.bfloat16),
-            ],
+            out_specs=[out_spec, out_spec],
+            scratch_shapes=[pltpu.VMEM((2 * rows, depth), jnp.bfloat16)],
         ),
-        compiler_params=pltpu.CompilerParams(vmem_limit_bytes=48 << 20),
+        compiler_params=pltpu.CompilerParams(vmem_limit_bytes=16 << 20),
         cost_estimate=LARGE,
-    )(order, *own, *mate, w_own, w_mate)
-
-
-def pair_kernel(core, *refs):
-    got, mate = refs[0:2], refs[2:4]
-    weights = (refs[4:6], refs[6:8])
-    total, outs, x, w = refs[8], refs[9:13], refs[13], refs[14]
-    for kind in range(2):
-
-        @pl.when((pl.program_id(0) == kind) & (pl.program_id(1) == 0))
-        def _():
-            stack_split(x, 0, got[kind])
-            stack_split(x, got[kind].shape[1], mate[kind])
-
-        for chip in range(2):
-
-            @pl.when((pl.program_id(0) == kind) & (pl.program_id(1) == chip))
-            def _():
-                outs[2 * kind + chip][...] = total[0] + times_weight(x, w, weights[kind])
-
-
-def project_pair(got, mate, near, near_mate, far, far_mate, total, core):
-    rows, depth = got[0].shape
-    width = depth
-    vmem = pl.BlockSpec(memory_space=pltpu.VMEM)
-    out = jax.ShapeDtypeStruct((rows, width), jnp.float32)
-    even = lambda k, d: jnp.where(k == 0, d, 1)
-    odd = lambda k, d: jnp.where(k == 0, 0, d)
-    w_spec = lambda place: pl.BlockSpec((depth, width), place)
-    return pl.pallas_call(
-        pair_kernel,
-        out_shape=[out] * 4,
-        grid_spec=pltpu.PrefetchScalarGridSpec(
-            num_scalar_prefetch=1,
-            grid=(2, 2),
-            in_specs=[vmem] * 4
-            + [
-                w_spec(lambda k, d, c: (0, 2 * even(k, d) + c[0])),
-                w_spec(lambda k, d, c: (0, even(k, d))),
-                w_spec(lambda k, d, c: (0, 2 * odd(k, d) + c[0])),
-                w_spec(lambda k, d, c: (0, odd(k, d))),
-                pl.BlockSpec((1, rows, width), lambda k, d, c: (k, 0, d)),
-            ],
-            out_specs=[pl.BlockSpec((rows, width), lambda k, d, c: (0, 0))] * 4,
-            scratch_shapes=[
-                pltpu.VMEM((2 * rows, 2 * depth), jnp.bfloat16),
-                pltpu.VMEM((2, 2 * depth, width), jnp.bfloat16),
-            ],
-        ),
-        compiler_params=pltpu.CompilerParams(vmem_limit_bytes=48 << 20),
-        cost_estimate=LARGE,
-    )(core, *got, *mate, near, near_mate, far, far_mate, total)
+    )(cores, *got, near, far, total)
 
 
 def body(
@@ -385,8 +368,6 @@
     near_weight, far_weight = (
         over_head(beside(chip_columns(y ^ chip), chip_columns(y ^ 2)), 2 * chip) for chip in (1, 3)
     )
-    mate_columns = (cut(out_weight, 2 * chip + 1 - core, 1) for chip in (y, y ^ 3, y ^ 1))
-    mate_weight = over_head(beside(*mate_columns), 1)
 
     vert = lax.dynamic_slice_in_dim(vertical_blocks, head_index * heads, heads, 0)
     slash = lax.dynamic_slice_in_dim(slash_offsets, head_index * heads, heads, 0)
@@ -406,13 +387,13 @@
     first_row = (seq_index * rows).reshape(1)
     back = 2 * blocks - offsets
     wraps = jnp.stack([x < 2, x == 0]).astype(jnp.int32)
-    order = jnp.stack([2 * chip + core for chip in (y, y ^ 3, y, y ^ 1)])
-    my_core = core.reshape(1)
+    cores = jnp.stack([1 - core, core])
+    order = jnp.concatenate([2 * chip + cores for chip in (y ^ 3, y, y ^ 1, y)])
     owner = named // blocks
     at = named % blocks
     k_place, k_held = (owner % 4 - x) % 4 * blocks + at, (owner // 4 == z).astype(jnp.int32)
     v_place, v_held = (owner // 4 - z) % 4 * blocks + at, (owner % 4 == x).astype(jnp.int32)
-    orders = (order, my_core)
+    orders = (order, cores)
     small = (vert_pos, slash_pos, first_row, back, wraps, orders, k_place, k_held, v_place, v_held)
 
     (k_left, k_right, v_below, v_above), small = lax.optimization_barrier(
@@ -440,49 +421,50 @@
     named = [*k_named, *v_named]
     one, two = (4, 12, 1, 3), (12, 4, 3, 1)
     more = [swapped(a, bits) for a, bits in zip(named, one)]
-    v_far_a, v_far_b, k_far_wrap, *more = lax.optimization_barrier(
-        (v_far_a, v_far_b, k_far_wrap, *more)
+    q = scaled(queries)
+    q, v_far_a, v_far_b, k_far_wrap, *more = lax.optimization_barrier(
+        (q, v_far_a, v_far_b, k_far_wrap, *more)
     )
     named = [a + b for a, b in zip(named, more)]
     arrays = (k_far, k_far_wrap, k_left, k_left_wrap, key_rows, v_far_a, v_far_b, v_left)
     near_arrays = (*arrays, value_vectors, slash_pos)
-    near = attend_near(queries, 0, rows, first_row, back, wraps, near_arrays)
+    near = attend_near(q, 0, rows, first_row, back, wraps, near_arrays)
     more = [swapped(a, bits) for a, bits in zip(named, two)]
     near, more = lax.optimization_barrier((near, more))
     arrays = (*(a + b for a, b in zip(named, more)), vert_pos)
 
-    order, my_core = orders
+    order, cores = orders
     meet, end = (2, 6), (6, 2)
-    across_chip = lambda parts: [over_head(a, 1) for a in parts]
-    own = list(attend(queries, *near, 0, first_row, arrays))
-    q, *own = lax.optimization_barrier((queries, *own))
-    got_a = [over_head(a, bits) for a, bits in zip(own, meet)]
-    mate, near_weight, far_weight = lax.optimization_barrier(
-        (across_chip(own), near_weight, far_weight)
-    )
-    total = project_chip(own, mate, out_weight, mate_weight, order)
-    q, total = lax.optimization_barrier((q, total))
-    near_mate, far_mate = (
-        over_head(beside(cut(a, 1 - core, 1), cut(a, 3 - core, 1)), 1)
-        for a in (near_weight, far_weight)
-    )
-    own = attend(q, *near, half, first_row, arrays)
-    own, got_a = lax.optimization_barrier((own, got_a))
-    weights = (near_weight, near_mate, far_weight, far_mate)
-    got_b = [over_head(a, bits) for a, bits in zip(own, meet)]
-    mate = across_chip(own)
-    keep_0, pass_0, keep_1, pass_1 = project_pair(
-        got_a, across_chip(got_a), *weights, total, my_core
-    )
-    pass_0, pass_1, got_b, mate = lax.optimization_barrier((pass_0, pass_1, got_b, mate))
-    sent_a = [over_head(a, bits) for a, bits in zip((pass_0, pass_1), end)]
-    total = project_chip(own, mate, out_weight, mate_weight, order)
-    keep_2, pass_2, keep_3, pass_3 = project_pair(
-        got_b, across_chip(got_b), *weights, total, my_core
-    )
-    pass_2, pass_3, sent_a = lax.optimization_barrier((pass_2, pass_3, sent_a))
-    sent = sent_a + [over_head(a, bits) for a, bits in zip((pass_2, pass_3), end)]
-    return jnp.concatenate([a + b for a, b in zip((keep_0, keep_1, keep_2, keep_3), sent)], axis=0)
+    own_a = attend(q, *near, 0, first_row, arrays)
+    q, own_a = lax.optimization_barrier((q, own_a))
+    meeting = lambda parts: [over_head(parts[i], bits) for i, bits in enumerate(meet)]
+    ending = lambda parts: [over_head(parts[i], bits) for i, bits in enumerate(end)]
+    got_a = meeting(own_a)
+    own_b = attend(q, *near, half, first_row, arrays)
+    total = project_chip(own_a, own_b, out_weight, order)
+    total, near_weight, far_weight, got_a = lax.optimization_barrier(
+        (total, near_weight, far_weight, got_a)
+    )
+    got_b = meeting(own_b)
+    product = lambda got, unit, keep: project_pair(
+        got, near_weight, far_weight, total, unit, keep, cores
+    )
+    there_a, here_a = product(got_a, 0, False)
+    there_a, here_a, got_a = lax.optimization_barrier((there_a, here_a, got_a))
+    pass_a = here_a + over_head(there_a, 1)
+    keep_there_a, keep_here_a = product(got_a, 0, True)
+    pass_a, got_b, keep_there_a = lax.optimization_barrier((pass_a, got_b, keep_there_a))
+    sent_a = ending(pass_a)
+    there_b, here_b = product(got_b, 1, False)
+    there_b, here_b, got_b = lax.optimization_barrier((there_b, here_b, got_b))
+    pass_b = here_b + over_head(there_b, 1)
+    keep_there_b, keep_here_b = product(got_b, 1, True)
+    kept_a = keep_here_a + over_head(keep_there_a, 1)
+    pass_b, sent_a, keep_there_b = lax.optimization_barrier((pass_b, sent_a, keep_there_b))
+    sent_b = ending(pass_b)
+    kept_b = keep_here_b + over_head(keep_there_b, 1)
+    kept = (kept_a[0], kept_a[1], kept_b[0], kept_b[1])
+    return jnp.concatenate([a + b for a, b in zip(kept, (*sent_a, *sent_b))], axis=0)
 
 
 def solution(mesh):

time: 201 us -> 184 us (0.915)
  waiting for transfers between devices: 56.7 us -> 68.3 us
  local copies, waits for them, and re-layouts: 15.1 us -> 5.39 us
  starting transfers between devices: 51.4 us -> 43.7 us
  other arithmetic: 15.7 us -> 8.3 us
  Pallas kernels: 60 us -> 54.9 us
    ppermute x21 -> x14, waiting for transfers between devices: 22.1 us -> 33.3 us  [body(): lax.ppermute(a, 'head', [(i, i ^ bits) for i in range(head_size)])]
    pallas_call x2, Pallas kernels: 18.8 us -> 12.6 us  [attend(): pl.pallas_call(functools.partial(attend_kernel, start), grid=(2, heads //...]
    ppermute x21 -> x14, starting transfers between devices: 16.1 us -> 9.96 us  [body(): lax.ppermute(a, 'head', [(i, i ^ bits) for i in range(head_size)])]
    unnamed x61 -> x17, local copies, waits for them, and re-layouts: 5.28 us -> 0.15 us
    concatenate x4 -> x1, other arithmetic: 9.2 us -> 4.11 us  [body(): beside = lambda *parts: jnp.concatenate(parts, axis=1)]
    dynamic_slice x3 -> x1, local copies, waits for them, and re-layouts: 8.33 us -> 3.44 us  [body(): lax.dynamic_slice_in_dim(a, first * width, count * width, 1)]
    add x4, other arithmetic: 3.57 us -> 0.22 us  [body(): named = [a + b for a, b in zip(named, more)]]
    pallas_call x4 -> x6, Pallas kernels: 29.1 us -> 30.4 us  [the longest x4 20.2 us: project_pair(): pl.pallas_call(pair_kernel, out_shape=[out, out], grid_spec=pltpu.Prefetc...]
  transfers between devices with their start and end apart: 40 -> 33, of which waited for: 17 -> 16; matrix products, arithmetic and copies ran while one was open for 12% -> 7% of each run, Pallas kernels for 30% -> 25%
where the time goes in v6:
time: 184 us; the launch traced here: 182 us
  waiting for transfers between devices  68.3 us (37%)
  Pallas kernels  54.9 us (30%)
  starting transfers between devices  43.7 us (24%)
  other arithmetic  8.3 us (5%)
  local copies, waits for them, and re-layouts  5.39 us (3%)
    ppermute x19, waiting for transfers between devices, body(): send = lambda a, pairs: lax.ppermute(a, 'seq', pairs)  35 us
    ppermute x19, starting transfers between devices, body(): send = lambda a, pairs: lax.ppermute(a, 'seq', pairs)  33.8 us
    ppermute x14, waiting for transfers between devices, body(): lax.ppermute(a, 'head', [(i, i ^ bits) for i in range(head_size)])  33.3 us
    pallas_call x4, Pallas kernels, project_pair(): pl.pallas_call(pair_kernel, out_shape=[out, out], grid_spec=pltpu.Prefetc...  20.2 us
    pallas_call x2, Pallas kernels, attend(): pl.pallas_call(functools.partial(attend_kernel, start), grid=(2, heads //...  12.6 us
    ppermute x14, starting transfers between devices, body(): lax.ppermute(a, 'head', [(i, i ^ bits) for i in range(head_size)])  9.96 us
    pallas_call x1, Pallas kernels, project_chip(): pl.pallas_call(chip_kernel, out_shape=jax.ShapeDtypeStruct((2, 2 * rows,...  9.94 us
    pallas_call x1, Pallas kernels, attend_near(): pl.pallas_call(functools.partial(near_kernel, start), grid=(rows // TILE,...  9.64 us
  transfers between devices with their start and end apart: 33, of which 16 were waited for; matrix products, arithmetic and copies ran while one was open for 7% of the time, Pallas kernels for 25%

profile of v6, /device:TPU:2, one launch (start us, length us, event | category | flops | bytes accessed | tf_op | source)
XLA Modules:
  0.0 181.9 jit_solution(13577083004765847327)
XLA Ops:
  0.0 0.5 collective-permute-start.1
  0.5 1.6 collective-permute-start
  2.0 4.0 %collective-permute-start.3 = (f32[1024,128]{1,0:T(8,128)}, f32[1024,128]{1,0:T(8,128)S(1)}, u32[]{:S(2)}, u32[]{:S(2)}) collective-permute-start(f32[1024,128]{1,0:T(8,128)} %v_own.1), channel_id=1, source_target_pairs={{0,96},{8,104},{16,112},{24,120},{32,0},{40,8},{48,16},{56,24},{64... | collective-permute-start | bytes 1572872 | tf_op jit(solution)/shard_map/ppermute | solution.py:354
  6.1 3.4 %constant_dynamic-slice_fusion = (f32[512,1024]{1,0:T(8,128)S(1)}, f32[512,1024]{1,0:T(8,128)S(1)}, f32[512,1024]{1,0:T(8,128)S(1)}) fusion(f32[512,4096]{1,0:T(8,128)} %w.1, s32[]{:T(128)S(6)} %select_n.128, s32[]{:T(128)S(6)} %select_n.126, s32[]{:T(128)S(6)} %select_n.127), kind=kLoop, calls=%fused_computation.44 | loop fusion | bytes 12582924 | tf_op jit(solution)/shard_map/dynamic_slice | solution.py:365
  9.5 4.1 %pad_maximum_fusion = (f32[512,2048]{1,0:T(8,128)}, f32[512,2048]{1,0:T(8,128)}) fusion(f32[512,1024]{1,0:T(8,128)S(1)} %get-tuple-element.157, f32[512,1024]{1,0:T(8,128)S(1)} %get-tuple-element.155, f32[512,1024]{1,0:T(8,128)S(1)} %get-tuple-element.156), kind=kLoop, calls=%fused_computation | loop fusion | flops 2097152 | bytes 14680064 | tf_op jit(solution)/shard_map/concatenate | solution.py:366
  13.7 3.0 %collective-permute-start.20 = (f32[512,2048]{1,0:T(8,128)}, f32[512,2048]{1,0:T(8,128)}, u32[]{:S(2)}, u32[]{:S(2)}) collective-permute-start(f32[512,2048]{1,0:T(8,128)} %get-tuple-element.158), channel_id=1, source_target_pairs={{0,6},{1,7},{2,4},{3,5},{4,2},{5,3},{6,0},{7,1},{8,14},{9,15},{10,... | collective-permute-start | bytes 12582920 | tf_op jit(solution)/shard_map/ppermute | solution.py:363
  19.9 0.4 collective-permute-done.2.refs_3_
  20.3 2.9 %collective-permute-start.5 = (f32[1024,128]{1,0:T(8,128)S(1)}, f32[1024,128]{1,0:T(8,128)S(1)}, u32[]{:S(2)}, u32[]{:S(2)}) collective-permute-start(f32[1024,128]{1,0:T(8,128)S(1)} %collective-permute-done.3.refs_1_), channel_id=1, source_target_pairs={{0,96},{8,104},{16,112},{24,120},{32,0},{40,8},{48,16},{56,24},{64... | collective-permute-start | bytes 1572872 | tf_op jit(solution)/shard_map/ppermute | solution.py:354
  23.5 1.3 collective-permute-start.4
  24.8 0.8 collective-permute-start.6
  25.7 7.3 %collective-permute-done.5.refs_2_ = f32[1024,128]{1,0:T(8,128)S(1)} collective-permute-done((f32[1024,128]{1,0:T(8,128)S(1)}, f32[1024,128]{1,0:T(8,128)S(1)}, u32[]{:S(2)}, u32[]{:S(2)}) %collective-permute-start.5) | collective-permute-done | bytes 524320 | tf_op jit(solution)/shard_map/ppermute | solution.py:354
  32.9 0.7 collective-permute-start.7
  33.6 7.4 %collective-permute-done.4 = f32[1536,128]{1,0:T(8,128)S(1)} collective-permute-done((f32[1536,128]{1,0:T(8,128)S(1)}, f32[1536,128]{1,0:T(8,128)S(1)}, u32[]{:S(2)}, u32[]{:S(2)}) %collective-permute-start.4) | collective-permute-done | bytes 786464 | tf_op jit(solution)/shard_map/ppermute | solution.py:354
  41.0 2.6 %collective-permute-done.6 = f32[1536,128]{1,0:T(8,128)S(1)} collective-permute-done((f32[1536,128]{1,0:T(8,128)S(1)}, f32[1536,128]{1,0:T(8,128)S(1)}, u32[]{:S(2)}, u32[]{:S(2)}) %collective-permute-start.6) | collective-permute-done | bytes 786464 | tf_op jit(solution)/shard_map/ppermute | solution.py:354
  43.7 3.0 %collective-permute-start.9 = (f32[512,128]{1,0:T(8,128)S(1)}, f32[512,128]{1,0:T(8,128)S(1)}, u32[]{:S(2)}, u32[]{:S(2)}) collective-permute-start(f32[512,128]{1,0:T(8,128)S(1)} %slice.57), channel_id=1, source_target_pairs={{0,24},{8,0},{16,8},{24,16},{32,56},{40,32},{48,40},{56,48},{64,88... | collective-permute-start | bytes 786440 | tf_op jit(solution)/shard_map/ppermute | solution.py:354
  46.7 1.2 shard_map.74
  47.9 1.5 collective-permute-start.11
  49.4 3.8 %collective-permute-start.12 = (f32[1024,128]{1,0:T(8,128)S(1)}, f32[1024,128]{1,0:T(8,128)S(1)}, u32[]{:S(2)}, u32[]{:S(2)}) collective-permute-start(f32[1024,128]{1,0:T(8,128)S(1)} %get-tuple-element.86), channel_id=1, source_target_pairs={{0,96},{8,104},{16,112},{24,120},{32,64},{40,72},{48,80},{56,88},{... | collective-permute-start | bytes 1572872 | tf_op jit(solution)/shard_map/ppermute | solution.py:354
  53.3 1.2 shard_map.75
  54.5 5.2 %collective-permute-done.8.v_far_a = f32[512,128]{1,0:T(8,128)S(1)} collective-permute-done((f32[512,128]{1,0:T(8,128)S(1)}, f32[512,128]{1,0:T(8,128)S(1)}, u32[]{:S(2)}, u32[]{:S(2)}) %collective-permute-start.8) | collective-permute-done | bytes 262176 | tf_op jit(solution)/shard_map/ppermute | solution.py:354
  59.7 3.3 %collective-permute-start.10 = (f32[1024,128]{1,0:T(8,128)S(1)}, f32[1024,128]{1,0:T(8,128)S(1)}, u32[]{:S(2)}, u32[]{:S(2)}) collective-permute-start(f32[1024,128]{1,0:T(8,128)S(1)} %slice.58.refs_2_.k_far), channel_id=1, source_target_pairs={{0,32},{8,40},{32,64},{40,72},{64,96},{72,104},{1,33},{9,41},{33,6... | collective-permute-start | bytes 1572872 | tf_op jit(solution)/shard_map/ppermute | solution.py:354
  63.0 1.3 collective-permute-start.13
  64.5 5.1 %collective-permute-done.10.k_far_wrap = f32[1024,128]{1,0:T(8,128)S(1)} collective-permute-done((f32[1024,128]{1,0:T(8,128)S(1)}, f32[1024,128]{1,0:T(8,128)S(1)}, u32[]{:S(2)}, u32[]{:S(2)}) %collective-permute-start.10) | collective-permute-done | bytes 524320 | tf_op jit(solution)/shard_map/ppermute | solution.py:354
  69.6 2.6 %collective-permute-done.13 = f32[1024,128]{1,0:T(8,128)S(1)} collective-permute-done((f32[1024,128]{1,0:T(8,128)S(1)}, f32[1024,128]{1,0:T(8,128)S(1)}, u32[]{:S(2)}, u32[]{:S(2)}) %collective-permute-start.13) | collective-permute-done | bytes 524320 | tf_op jit(solution)/shard_map/ppermute | solution.py:354
  72.2 1.2 collective-permute-done.14
  73.5 3.0 %collective-permute-start.15 = (f32[1024,128]{1,0:T(8,128)S(1)}, f32[1024,128]{1,0:T(8,128)S(1)}, u32[]{:S(2)}, u32[]{:S(2)}) collective-permute-start(f32[1024,128]{1,0:T(8,128)S(1)} %add.216), channel_id=1, source_target_pairs={{0,96},{8,104},{16,112},{24,120},{32,64},{40,72},{48,80},{56,88},{... | collective-permute-start | bytes 1572872 | tf_op jit(solution)/shard_map/ppermute | solution.py:354
  76.7 4.0 %collective-permute-start.16 = (f32[1024,128]{1,0:T(8,128)S(1)}, f32[1024,128]{1,0:T(8,128)S(1)}, u32[]{:S(2)}, u32[]{:S(2)}) collective-permute-start(f32[1024,128]{1,0:T(8,128)S(1)} %add.217), channel_id=1, source_target_pairs={{0,32},{8,40},{16,48},{24,56},{32,0},{40,8},{48,16},{56,24},{64,96... | collective-permute-start | bytes 1572872 | tf_op jit(solution)/shard_map/ppermute | solution.py:354
  80.7 3.3 %collective-permute-done.15 = f32[1024,128]{1,0:T(8,128)S(1)} collective-permute-done((f32[1024,128]{1,0:T(8,128)S(1)}, f32[1024,128]{1,0:T(8,128)S(1)}, u32[]{:S(2)}, u32[]{:S(2)}) %collective-permute-start.15) | collective-permute-done | bytes 524320 | tf_op jit(solution)/shard_map/ppermute | solution.py:354
  84.0 2.0 %collective-permute-start.18 = (f32[1024,128]{1,0:T(8,128)S(1)}, f32[1024,128]{1,0:T(8,128)S(1)}, u32[]{:S(2)}, u32[]{:S(2)}) collective-permute-start(f32[1024,128]{1,0:T(8,128)S(1)} %add.219), channel_id=1, source_target_pairs={{0,8},{8,0},{16,24},{24,16},{32,40},{40,32},{48,56},{56,48},{64,72... | collective-permute-start | bytes 1572872 | tf_op jit(solution)/shard_map/ppermute | solution.py:354
  86.0 9.6 %shard_map.76 = (f32[1024,512]{1,0:T(8,128)S(1)}, f32[1024,256]{1,0:T(8,128)S(1)}) custom-call(s32[1]{0:T(128)} %bitcast.1.first_row, s32[4,4]{1,0:T(4,128)S(1)} %get-tuple-element.94.back, s32[2]{0:T(128)S(1)} %add_convert_fusion.wraps, f32[1024,512]{1,0:T(8,128)S(1)} %shard_map.73.q, f32[1024,128]{1,0:T(8,128)S(1)} %slice.58.refs_2_.k_far, ...), custom_call_target="tpu_custom_call" | custom-call | flops 1073741824 | bytes 1048576 | tf_op jit(solution)/shard_map/pallas_call | solution.py:177
  96.0 6.3 %shard_map.77.own_a = f32[2,256,512]{2,1,0:T(8,128)S(1)} custom-call(s32[1]{0:T(128)} %bitcast.1.first_row, f32[1024,512]{1,0:T(8,128)S(1)} %shard_map.73.q, f32[1024,512]{1,0:T(8,128)S(1)} %get-tuple-element.107.near, f32[1024,256]{1,0:T(8,128)S(1)} %get-tuple-element.108.stats, f32[1024,128]{1,0:T(8,128)S(1)} %add.220.k_a, f32[1024,128]{1,0:T(8,128)S(1)} %add.221.k_b, ...), custom_call_target="tpu_custom_call" | custom-call | flops 1073741824 | bytes 1048576 | tf_op jit(solution)/shard_map/pallas_call | solution.py:234
  102.3 1.4 collective-permute-start.22
  104.0 6.3 %shard_map.78.own_b = f32[2,256,512]{2,1,0:T(8,128)S(1)} custom-call(s32[1]{0:T(128)} %bitcast.1.first_row, f32[1024,512]{1,0:T(8,128)S(1)} %shard_map.73.q, f32[1024,512]{1,0:T(8,128)S(1)} %get-tuple-element.107.near, f32[1024,256]{1,0:T(8,128)S(1)} %get-tuple-element.108.stats, f32[1024,128]{1,0:T(8,128)S(1)} %add.220.k_a, f32[1024,128]{1,0:T(8,128)S(1)} %add.221.k_b, ...), custom_call_target="tpu_custom_call" | custom-call | flops 1073741824 | bytes 1048576 | tf_op jit(solution)/shard_map/pallas_call | solution.py:234
  110.3 9.9 %shard_map.79.total = f32[2,512,2048]{2,1,0:T(8,128)S(1)} custom-call(s32[8]{0:T(128)S(1)} %pad_add_fusion.1.order, f32[2,256,512]{2,1,0:T(8,128)S(1)} %shard_map.77.own_a, f32[2,256,512]{2,1,0:T(8,128)S(1)} %shard_map.78.own_b, f32[512,4096]{1,0:T(8,128)S(1)} %bitcast.41), custom_call_target="tpu_custom_call" | custom-call | flops 1073741824 | bytes 1048576 | tf_op jit(solution)/shard_map/pallas_call | solution.py:275
  120.2 2.2 %collective-permute-done.21.got_a = f32[256,512]{1,0:T(8,128)S(1)} collective-permute-done((f32[256,512]{1,0:T(8,128)S(1)}, f32[256,512]{1,0:T(8,128)S(1)}, u32[]{:S(2)}, u32[]{:S(2)}) %collective-permute-start.21) | collective-permute-done | bytes 524320 | tf_op jit(solution)/shard_map/ppermute | solution.py:363
  122.4 5.0 %shard_map.80 = (f32[2,256,512]{2,1,0:T(8,128)S(1)}, f32[2,256,512]{2,1,0:T(8,128)S(1)}) custom-call(s32[2]{0:T(128)S(1)} %get-tuple-element.75.cores, f32[256,512]{1,0:T(8,128)S(1)} %collective-permute-done.21.got_a, f32[256,512]{1,0:T(8,128)S(1)} %collective-permute-done.22.got_b, f32[512,2048]{1,0:T(8,128)S(1)} %collective-permute-done.19.near, ...), custom_call_target="tpu_custom_call" | custom-call | flops 1073741824 | bytes 1048576 | tf_op jit(solution)/shard_map/pallas_call | solution.py:314
  127.7 0.4 collective-permute-start.25
  128.1 0.6 collective-permute-start.24
  128.7 5.0 %shard_map.81 = (f32[2,256,512]{2,1,0:T(8,128)S(1)}, f32[2,256,512]{2,1,0:T(8,128)S(1)}) custom-call(s32[2]{0:T(128)S(1)} %get-tuple-element.75.cores, f32[256,512]{1,0:T(8,128)S(1)} %collective-permute-done.21.got_a, f32[256,512]{1,0:T(8,128)S(1)} %collective-permute-done.22.got_b, f32[512,2048]{1,0:T(8,128)S(1)} %collective-permute-done.19.near, ...), custom_call_target="tpu_custom_call" | custom-call | flops 1073741824 | bytes 1048576 | tf_op jit(solution)/shard_map/pallas_call | solution.py:314
  134.0 9.3 %collective-permute-done.25.got_b = f32[256,512]{1,0:T(8,128)S(1)} collective-permute-done((f32[256,512]{1,0:T(8,128)S(1)}, f32[256,512]{1,0:T(8,128)S(1)}, u32[]{:S(2)}, u32[]{:S(2)}) %collective-permute-start.25) | collective-permute-done | bytes 524320 | tf_op jit(solution)/shard_map/ppermute | solution.py:363
  143.3 5.0 %shard_map.82 = (f32[2,256,512]{2,1,0:T(8,128)S(1)}, f32[2,256,512]{2,1,0:T(8,128)S(1)}) custom-call(s32[2]{0:T(128)S(1)} %get-tuple-element.75.cores, f32[256,512]{1,0:T(8,128)S(1)} %collective-permute-done.24.got_a, f32[256,512]{1,0:T(8,128)S(1)} %collective-permute-done.25.got_b, f32[512,2048]{1,0:T(8,128)S(1)} %collective-permute-done.19.near, ...), custom_call_target="tpu_custom_call" | custom-call | flops 1073741824 | bytes 1048576 | tf_op jit(solution)/shard_map/pallas_call | solution.py:314
  148.6 2.0 %collective-permute-start.28 = (f32[256,512]{1,0:T(8,128)S(1)}, f32[256,512]{1,0:T(8,128)S(1)}, u32[]{:S(2)}, u32[]{:S(2)}) collective-permute-start(f32[256,512]{1,0:T(8,128)S(1)} %get-tuple-element.167), channel_id=1, source_target_pairs={{0,6},{1,7},{2,4},{3,5},{4,2},{5,3},{6,0},{7,1},{8,14},{9,15},{10,... | collective-permute-start | bytes 1572872 | tf_op jit(solution)/shard_map/ppermute | solution.py:363
  150.6 5.0 %shard_map.83 = (f32[2,256,512]{2,1,0:T(8,128)S(1)}, f32[2,256,512]{2,1,0:T(8,128)S(1)}) custom-call(s32[2]{0:T(128)S(1)} %get-tuple-element.75.cores, f32[256,512]{1,0:T(8,128)S(1)} %collective-permute-done.24.got_a, f32[256,512]{1,0:T(8,128)S(1)} %collective-permute-done.25.got_b, f32[512,2048]{1,0:T(8,128)S(1)} %collective-permute-done.19.near, ...), custom_call_target="tpu_custom_call" | custom-call | flops 1073741824 | bytes 1048576 | tf_op jit(solution)/shard_map/pallas_call | solution.py:314
  155.9 7.0 %collective-permute-done.29 = f32[256,512]{1,0:T(8,128)S(1)} collective-permute-done((f32[256,512]{1,0:T(8,128)S(1)}, f32[256,512]{1,0:T(8,128)S(1)}, u32[]{:S(2)}, u32[]{:S(2)}) %collective-permute-start.29) | collective-permute-done | bytes 524320 | tf_op jit(solution)/shard_map/ppermute | solution.py:363
  162.9 1.3 collective-permute-done.28
  164.3 1.8 collective-permute-start.31
  167.1 12.8 %collective-permute-done.31 = f32[256,512]{1,0:T(8,128)S(1)} collective-permute-done((f32[256,512]{1,0:T(8,128)S(1)}, f32[256,512]{1,0:T(8,128)S(1)}, u32[]{:S(2)}, u32[]{:S(2)}) %collective-permute-start.31) | collective-permute-done | bytes 524320 | tf_op jit(solution)/shard_map/ppermute | solution.py:363
  180.4 1.5 pad_maximum_fusion.2
  (108 shorter events, 6.3 us)
Async XLA Ops:
  0.0 17.3 %copy-start = (s32[32,3]{0,1:T(4,128)S(1)}, s32[32,3]{0,1:T(4,128)}, u32[]{:S(2)}) copy-start(s32[32,3]{0,1:T(4,128)} %param.11) | copy-start | bytes 1156
  0.0 19.7 %collective-permute-start.1 = (f32[1024,128]{1,0:T(8,128)}, f32[1024,128]{1,0:T(8,128)S(1)}, u32[]{:S(2)}, u32[]{:S(2)}) collective-permute-start(f32[1024,128]{1,0:T(8,128)} %k_own.1), channel_id=1, source_target_pairs={{0,24},{8,0},{16,8},{24,16},{32,56},{40,32},{48,40},{56,48},{64,88... | collective-permute-start | bytes 1572872 | tf_op jit(solution)/shard_map/ppermute | solution.py:354
  0.5 19.5 %collective-permute-start = (f32[1024,128]{1,0:T(8,128)}, f32[1024,128]{1,0:T(8,128)S(1)}, u32[]{:S(2)}, u32[]{:S(2)}) collective-permute-start(f32[1024,128]{1,0:T(8,128)} %k_own.1), channel_id=1, source_target_pairs={{0,8},{8,16},{16,24},{24,0},{32,40},{40,48},{48,56},{56,32},{64,72... | collective-permute-start | bytes 1572872 | tf_op jit(solution)/shard_map/ppermute | solution.py:354
  2.0 17.9 %collective-permute-start.3 = (f32[1024,128]{1,0:T(8,128)}, f32[1024,128]{1,0:T(8,128)S(1)}, u32[]{:S(2)}, u32[]{:S(2)}) collective-permute-start(f32[1024,128]{1,0:T(8,128)} %v_own.1), channel_id=1, source_target_pairs={{0,96},{8,104},{16,112},{24,120},{32,0},{40,8},{48,16},{56,24},{64... | collective-permute-start | bytes 1572872 | tf_op jit(solution)/shard_map/ppermute | solution.py:354
  6.1 14.2 %collective-permute-start.2 = (f32[1024,128]{1,0:T(8,128)}, f32[1024,128]{1,0:T(8,128)S(1)}, u32[]{:S(2)}, u32[]{:S(2)}) collective-permute-start(f32[1024,128]{1,0:T(8,128)} %v_own.1), channel_id=1, source_target_pairs={{0,32},{8,40},{16,48},{24,56},{32,64},{40,72},{48,80},{56,88},{64,... | collective-permute-start | bytes 1572872 | tf_op jit(solution)/shard_map/ppermute | solution.py:354
  9.5 8.3 %copy-start.5 = (s32[32,8]{0,1:T(8,128)S(1)}, s32[32,8]{0,1:T(8,128)}, u32[]{:S(2)}) copy-start(s32[32,8]{0,1:T(8,128)} %param.10) | copy-start | bytes 3076
  9.5 13.7 %copy-start.2 = (f32[1024,128]{1,0:T(8,128)S(1)}, f32[1024,128]{1,0:T(8,128)}, u32[]{:S(2)}) copy-start(f32[1024,128]{1,0:T(8,128)} %v_own.1) | copy-start | bytes 1572868
  13.7 108.8 %collective-permute-start.20 = (f32[512,2048]{1,0:T(8,128)}, f32[512,2048]{1,0:T(8,128)}, u32[]{:S(2)}, u32[]{:S(2)}) collective-permute-start(f32[512,2048]{1,0:T(8,128)} %get-tuple-element.158), channel_id=1, source_target_pairs={{0,6},{1,7},{2,4},{3,5},{4,2},{5,3},{6,0},{7,1},{8,14},{9,15},{10,... | collective-permute-start | bytes 12582920 | tf_op jit(solution)/shard_map/ppermute | solution.py:363
  19.7 102.7 %collective-permute-start.19 = (f32[512,2048]{1,0:T(8,128)}, f32[512,2048]{1,0:T(8,128)S(1)}, u32[]{:S(2)}, u32[]{:S(2)}) collective-permute-start(f32[512,2048]{1,0:T(8,128)} %get-tuple-element.159), channel_id=1, source_target_pairs={{0,2},{1,3},{2,0},{3,1},{4,6},{5,7},{6,4},{7,5},{8,10},{9,11},{10,... | collective-permute-start | bytes 12582920 | tf_op jit(solution)/shard_map/ppermute | solution.py:363
  20.3 12.6 %collective-permute-start.5 = (f32[1024,128]{1,0:T(8,128)S(1)}, f32[1024,128]{1,0:T(8,128)S(1)}, u32[]{:S(2)}, u32[]{:S(2)}) collective-permute-start(f32[1024,128]{1,0:T(8,128)S(1)} %collective-permute-done.3.refs_1_), channel_id=1, source_target_pairs={{0,96},{8,104},{16,112},{24,120},{32,0},{40,8},{48,16},{56,24},{64... | collective-permute-start | bytes 1572872 | tf_op jit(solution)/shard_map/ppermute | solution.py:354
  23.4 23.3 %copy-start.4 = (f32[1024,128]{1,0:T(8,128)S(1)}, f32[1024,128]{1,0:T(8,128)}, u32[]{:S(2)}) copy-start(f32[1024,128]{1,0:T(8,128)} %k_own.1) | copy-start | bytes 1572868
  23.5 17.6 %collective-permute-start.4 = (f32[1536,128]{1,0:T(8,128)S(1)}, f32[1536,128]{1,0:T(8,128)S(1)}, u32[]{:S(2)}, u32[]{:S(2)}) collective-permute-start(f32[1536,128]{1,0:T(8,128)S(1)} %pad_maximum_fusion.3), channel_id=1, source_target_pairs={{0,24},{8,0},{16,8},{24,16},{32,56},{40,32},{48,40},{56,48},{64,88... | collective-permute-start | bytes 2359304 | tf_op jit(solution)/shard_map/ppermute | solution.py:354
  24.8 18.8 %collective-permute-start.6 = (f32[1536,128]{1,0:T(8,128)S(1)}, f32[1536,128]{1,0:T(8,128)S(1)}, u32[]{:S(2)}, u32[]{:S(2)}) collective-permute-start(f32[1536,128]{1,0:T(8,128)S(1)} %pad_maximum_fusion.4), channel_id=1, source_target_pairs={{0,8},{8,16},{16,24},{24,0},{32,40},{40,48},{48,56},{56,32},{64,72... | collective-permute-start | bytes 2359304 | tf_op jit(solution)/shard_map/ppermute | solution.py:354
  32.9 0.7 collective-permute-start.7
  43.7 20.6 %copy-start.3 = (f32[1024,512]{1,0:T(8,128)S(1)}, f32[1024,512]{1,0:T(8,128)}, u32[]{:S(2)}) copy-start(f32[1024,512]{1,0:T(8,128)} %q.1) | copy-start | bytes 6291460
  43.7 9.5 %collective-permute-start.9 = (f32[512,128]{1,0:T(8,128)S(1)}, f32[512,128]{1,0:T(8,128)S(1)}, u32[]{:S(2)}, u32[]{:S(2)}) collective-permute-start(f32[512,128]{1,0:T(8,128)S(1)} %slice.57), channel_id=1, source_target_pairs={{0,24},{8,0},{16,8},{24,16},{32,56},{40,32},{48,40},{56,48},{64,88... | collective-permute-start | bytes 786440 | tf_op jit(solution)/shard_map/ppermute | solution.py:354
  47.9 15.0 %collective-permute-start.11 = (f32[1024,128]{1,0:T(8,128)S(1)}, f32[1024,128]{1,0:T(8,128)S(1)}, u32[]{:S(2)}, u32[]{:S(2)}) collective-permute-start(f32[1024,128]{1,0:T(8,128)S(1)} %get-tuple-element.85), channel_id=1, source_target_pairs={{0,32},{8,40},{16,48},{24,56},{32,0},{40,8},{48,16},{56,24},{64,96... | collective-permute-start | bytes 1572872 | tf_op jit(solution)/shard_map/ppermute | solution.py:354
  49.4 14.9 %collective-permute-start.12 = (f32[1024,128]{1,0:T(8,128)S(1)}, f32[1024,128]{1,0:T(8,128)S(1)}, u32[]{:S(2)}, u32[]{:S(2)}) collective-permute-start(f32[1024,128]{1,0:T(8,128)S(1)} %get-tuple-element.86), channel_id=1, source_target_pairs={{0,96},{8,104},{16,112},{24,120},{32,64},{40,72},{48,80},{56,88},{... | collective-permute-start | bytes 1572872 | tf_op jit(solution)/shard_map/ppermute | solution.py:354
  53.2 6.4 %collective-permute-start.8 = (f32[512,128]{1,0:T(8,128)S(1)}, f32[512,128]{1,0:T(8,128)S(1)}, u32[]{:S(2)}, u32[]{:S(2)}) collective-permute-start(f32[512,128]{1,0:T(8,128)S(1)} %slice.56), channel_id=1, source_target_pairs={{0,8},{8,16},{16,24},{24,0},{32,40},{40,48},{48,56},{56,32},{64,72... | collective-permute-start | bytes 786440 | tf_op jit(solution)/shard_map/ppermute | solution.py:354
  59.7 9.9 %collective-permute-start.10 = (f32[1024,128]{1,0:T(8,128)S(1)}, f32[1024,128]{1,0:T(8,128)S(1)}, u32[]{:S(2)}, u32[]{:S(2)}) collective-permute-start(f32[1024,128]{1,0:T(8,128)S(1)} %slice.58.refs_2_.k_far), channel_id=1, source_target_pairs={{0,32},{8,40},{32,64},{40,72},{64,96},{72,104},{1,33},{9,41},{33,6... | collective-permute-start | bytes 1572872 | tf_op jit(solution)/shard_map/ppermute | solution.py:354
  63.0 9.3 %collective-permute-start.13 = (f32[1024,128]{1,0:T(8,128)S(1)}, f32[1024,128]{1,0:T(8,128)S(1)}, u32[]{:S(2)}, u32[]{:S(2)}) collective-permute-start(f32[1024,128]{1,0:T(8,128)S(1)} %get-tuple-element.90), channel_id=1, source_target_pairs={{0,8},{8,0},{16,24},{24,16},{32,40},{40,32},{48,56},{56,48},{64,72... | collective-permute-start | bytes 1572872 | tf_op jit(solution)/shard_map/ppermute | solution.py:354
  64.3 9.2 %collective-permute-start.14 = (f32[1024,128]{1,0:T(8,128)S(1)}, f32[1024,128]{1,0:T(8,128)S(1)}, u32[]{:S(2)}, u32[]{:S(2)}) collective-permute-start(f32[1024,128]{1,0:T(8,128)S(1)} %get-tuple-element.91), channel_id=1, source_target_pairs={{0,24},{8,16},{16,8},{24,0},{32,56},{40,48},{48,40},{56,32},{64,88... | collective-permute-start | bytes 1572872 | tf_op jit(solution)/shard_map/ppermute | solution.py:354
  73.5 10.5 %collective-permute-start.15 = (f32[1024,128]{1,0:T(8,128)S(1)}, f32[1024,128]{1,0:T(8,128)S(1)}, u32[]{:S(2)}, u32[]{:S(2)}) collective-permute-start(f32[1024,128]{1,0:T(8,128)S(1)} %add.216), channel_id=1, source_target_pairs={{0,96},{8,104},{16,112},{24,120},{32,64},{40,72},{48,80},{56,88},{... | collective-permute-start | bytes 1572872 | tf_op jit(solution)/shard_map/ppermute | solution.py:354
  76.7 19.0 %collective-permute-start.16 = (f32[1024,128]{1,0:T(8,128)S(1)}, f32[1024,128]{1,0:T(8,128)S(1)}, u32[]{:S(2)}, u32[]{:S(2)}) collective-permute-start(f32[1024,128]{1,0:T(8,128)S(1)} %add.217), channel_id=1, source_target_pairs={{0,32},{8,40},{16,48},{24,56},{32,0},{40,8},{48,16},{56,24},{64,96... | collective-permute-start | bytes 1572872 | tf_op jit(solution)/shard_map/ppermute | solution.py:354
  80.7 15.0 %collective-permute-start.17 = (f32[1024,128]{1,0:T(8,128)S(1)}, f32[1024,128]{1,0:T(8,128)S(1)}, u32[]{:S(2)}, u32[]{:S(2)}) collective-permute-start(f32[1024,128]{1,0:T(8,128)S(1)} %add.218), channel_id=1, source_target_pairs={{0,24},{8,16},{16,8},{24,0},{32,56},{40,48},{48,40},{56,32},{64,88... | collective-permute-start | bytes 1572872 | tf_op jit(solution)/shard_map/ppermute | solution.py:354
  84.0 11.7 %collective-permute-start.18 = (f32[1024,128]{1,0:T(8,128)S(1)}, f32[1024,128]{1,0:T(8,128)S(1)}, u32[]{:S(2)}, u32[]{:S(2)}) collective-permute-start(f32[1024,128]{1,0:T(8,128)S(1)} %add.219), channel_id=1, source_target_pairs={{0,8},{8,0},{16,24},{24,16},{32,40},{40,32},{48,56},{56,48},{64,72... | collective-permute-start | bytes 1572872 | tf_op jit(solution)/shard_map/ppermute | solution.py:354
  96.0 14.3 %slice-start = ((s8[8388608]{0:T(1024)(128)(4,1)}), s8[4194304]{0:T(1024)(128)(4,1)S(1)}, s32[]{:S(2)}) async-start(s8[8388608]{0:T(1024)(128)(4,1)} %bitcast.40), calls=%async_computation | async-start | bytes 8388608
  102.3 8.0 %slice-start.1 = ((s8[8388608]{0:T(1024)(128)(4,1)}), s8[4194304]{0:T(1024)(128)(4,1)S(1)}, s32[]{:S(2)}) async-start(s8[8388608]{0:T(1024)(128)(4,1)} %bitcast.40), calls=%async_computation.1 | async-start | bytes 8388608
  102.3 17.9 %collective-permute-start.22 = (f32[256,512]{1,0:T(8,128)S(1)}, f32[256,512]{1,0:T(8,128)S(1)}, u32[]{:S(2)}, u32[]{:S(2)}) collective-permute-start(f32[256,512]{1,0:T(8,128)S(1)} %get-tuple-element.170), channel_id=1, source_target_pairs={{0,6},{1,7},{2,4},{3,5},{4,2},{5,3},{6,0},{7,1},{8,14},{9,15},{10,... | collective-permute-start | bytes 1572872 | tf_op jit(solution)/shard_map/ppermute | solution.py:363
  103.8 18.7 %collective-permute-start.21 = (f32[256,512]{1,0:T(8,128)S(1)}, f32[256,512]{1,0:T(8,128)S(1)}, u32[]{:S(2)}, u32[]{:S(2)}) collective-permute-start(f32[256,512]{1,0:T(8,128)S(1)} %get-tuple-element.171), channel_id=1, source_target_pairs={{0,2},{1,3},{2,0},{3,1},{4,6},{5,7},{6,4},{7,5},{8,10},{9,11},{10,... | collective-permute-start | bytes 1572872 | tf_op jit(solution)/shard_map/ppermute | solution.py:363
  127.5 6.2 %collective-permute-start.23 = (f32[2,256,512]{2,1,0:T(8,128)S(1)}, f32[2,256,512]{2,1,0:T(8,128)S(1)}, u32[]{:S(2)}, u32[]{:S(2)}) collective-permute-start(f32[2,256,512]{2,1,0:T(8,128)S(1)} %get-tuple-element.127), channel_id=1, source_target_pairs={{0,1},{1,0},{2,3},{3,2},{4,5},{5,4},{6,7},{7,6},{8,9},{9,8},{10,11... | collective-permute-start | bytes 3145736 | tf_op jit(solution)/shard_map/ppermute | solution.py:363
  127.7 15.6 %collective-permute-start.25 = (f32[256,512]{1,0:T(8,128)S(1)}, f32[256,512]{1,0:T(8,128)S(1)}, u32[]{:S(2)}, u32[]{:S(2)}) collective-permute-start(f32[256,512]{1,0:T(8,128)S(1)} %get-tuple-element.168), channel_id=1, source_target_pairs={{0,6},{1,7},{2,4},{3,5},{4,2},{5,3},{6,0},{7,1},{8,14},{9,15},{10,... | collective-permute-start | bytes 1572872 | tf_op jit(solution)/shard_map/ppermute | solution.py:363
  128.1 15.2 %collective-permute-start.24 = (f32[256,512]{1,0:T(8,128)S(1)}, f32[256,512]{1,0:T(8,128)S(1)}, u32[]{:S(2)}, u32[]{:S(2)}) collective-permute-start(f32[256,512]{1,0:T(8,128)S(1)} %get-tuple-element.169), channel_id=1, source_target_pairs={{0,2},{1,3},{2,0},{3,1},{4,6},{5,7},{6,4},{7,5},{8,10},{9,11},{10,... | collective-permute-start | bytes 1572872 | tf_op jit(solution)/shard_map/ppermute | solution.py:363
  148.3 7.3 %collective-permute-start.27 = (f32[2,256,512]{2,1,0:T(8,128)S(1)}, f32[2,256,512]{2,1,0:T(8,128)S(1)}, u32[]{:S(2)}, u32[]{:S(2)}) collective-permute-start(f32[2,256,512]{2,1,0:T(8,128)S(1)} %get-tuple-element.135), channel_id=1, source_target_pairs={{0,1},{1,0},{2,3},{3,2},{4,5},{5,4},{6,7},{7,6},{8,9},{9,8},{10,11... | collective-permute-start | bytes 3145736 | tf_op jit(solution)/shard_map/ppermute | solution.py:363
  148.5 14.4 %collective-permute-start.29 = (f32[256,512]{1,0:T(8,128)S(1)}, f32[256,512]{1,0:T(8,128)S(1)}, u32[]{:S(2)}, u32[]{:S(2)}) collective-permute-start(f32[256,512]{1,0:T(8,128)S(1)} %get-tuple-element.166), channel_id=1, source_target_pairs={{0,2},{1,3},{2,0},{3,1},{4,6},{5,7},{6,4},{7,5},{8,10},{9,11},{10,... | collective-permute-start | bytes 1572872 | tf_op jit(solution)/shard_map/ppermute | solution.py:363
  148.6 15.6 %collective-permute-start.28 = (f32[256,512]{1,0:T(8,128)S(1)}, f32[256,512]{1,0:T(8,128)S(1)}, u32[]{:S(2)}, u32[]{:S(2)}) collective-permute-start(f32[256,512]{1,0:T(8,128)S(1)} %get-tuple-element.167), channel_id=1, source_target_pairs={{0,6},{1,7},{2,4},{3,5},{4,2},{5,3},{6,0},{7,1},{8,14},{9,15},{10,... | collective-permute-start | bytes 1572872 | tf_op jit(solution)/shard_map/ppermute | solution.py:363
  150.6 15.5 %collective-permute-start.26 = (f32[2,256,512]{2,1,0:T(8,128)S(1)}, f32[2,256,512]{2,1,0:T(8,128)S(1)}, u32[]{:S(2)}, u32[]{:S(2)}) collective-permute-start(f32[2,256,512]{2,1,0:T(8,128)S(1)} %get-tuple-element.129), channel_id=1, source_target_pairs={{0,1},{1,0},{2,3},{3,2},{4,5},{5,4},{6,7},{7,6},{8,9},{9,8},{10,11... | collective-permute-start | bytes 3145736 | tf_op jit(solution)/shard_map/ppermute | solution.py:363
  164.2 2.7 %collective-permute-start.30 = (f32[2,256,512]{2,1,0:T(8,128)S(1)}, f32[2,256,512]{2,1,0:T(8,128)S(1)}, u32[]{:S(2)}, u32[]{:S(2)}) collective-permute-start(f32[2,256,512]{2,1,0:T(8,128)S(1)} %get-tuple-element.143), channel_id=1, source_target_pairs={{0,1},{1,0},{2,3},{3,2},{4,5},{5,4},{6,7},{7,6},{8,9},{9,8},{10,11... | collective-permute-start | bytes 3145736 | tf_op jit(solution)/shard_map/ppermute | solution.py:363
  164.3 15.6 %collective-permute-start.31 = (f32[256,512]{1,0:T(8,128)S(1)}, f32[256,512]{1,0:T(8,128)S(1)}, u32[]{:S(2)}, u32[]{:S(2)}) collective-permute-start(f32[256,512]{1,0:T(8,128)S(1)} %get-tuple-element.164), channel_id=1, source_target_pairs={{0,6},{1,7},{2,4},{3,5},{4,2},{5,3},{6,0},{7,1},{8,14},{9,15},{10,... | collective-permute-start | bytes 1572872 | tf_op jit(solution)/shard_map/ppermute | solution.py:363
  166.1 14.1 %collective-permute-start.32 = (f32[256,512]{1,0:T(8,128)S(1)}, f32[256,512]{1,0:T(8,128)S(1)}, u32[]{:S(2)}, u32[]{:S(2)}) collective-permute-start(f32[256,512]{1,0:T(8,128)S(1)} %get-tuple-element.165), channel_id=1, source_target_pairs={{0,2},{1,3},{2,0},{3,1},{4,6},{5,7},{6,4},{7,5},{8,10},{9,11},{10,... | collective-permute-start | bytes 1572872 | tf_op jit(solution)/shard_map/ppermute | solution.py:363
  180.4 1.5 copy-start.1

commit v7 on v6

--- a/solution.py
+++ b/solution.py
@@ -249,6 +249,27 @@
     )(first_row, q, near, stats, *arrays)
 
 
+def take_kernel(order, source, out):
+    out[...] = source[...]
+
+
+def take_columns(weight, order, width):
+    rows = weight.shape[0]
+    count = order.shape[0]
+    return pl.pallas_call(
+        take_kernel,
+        out_shape=jax.ShapeDtypeStruct((rows, count * width), jnp.float32),
+        grid_spec=pltpu.PrefetchScalarGridSpec(
+            num_scalar_prefetch=1,
+            grid=(count,),
+            in_specs=[pl.BlockSpec((rows, width), lambda i, o: (0, o[i]))],
+            out_specs=pl.BlockSpec((rows, width), lambda i, o: (0, i)),
+        ),
+        compiler_params=pltpu.CompilerParams(vmem_limit_bytes=58 << 20),
+        cost_estimate=SMALL,
+    )(order, weight)
+
+
 def weight_term(x, block):
     high, low = split(block)
     return fold(dot(x, high, DOWN)) + dot(x[: x.shape[0] // 2], low, DOWN)
@@ -362,11 +383,9 @@
     y = head_index // 2
     over_head = lambda a, bits: lax.ppermute(a, "head", [(i, i ^ bits) for i in range(head_size)])
     width = out_weight.shape[1] // head_size
-    cut = lambda a, first, count: lax.dynamic_slice_in_dim(a, first * width, count * width, 1)
-    beside = lambda *parts: jnp.concatenate(parts, axis=1)
-    chip_columns = lambda chip: cut(out_weight, 2 * chip, 2)
     near_weight, far_weight = (
-        over_head(beside(chip_columns(y ^ chip), chip_columns(y ^ 2)), 2 * chip) for chip in (1, 3)
+        over_head(take_columns(out_weight, jnp.stack([y ^ chip, y ^ 2]), 2 * width), 2 * chip)
+        for chip in (1, 3)
     )
 
     vert = lax.dynamic_slice_in_dim(vertical_blocks, head_index * heads, heads, 0)
@@ -441,30 +460,31 @@
     ending = lambda parts: [over_head(parts[i], bits) for i, bits in enumerate(end)]
     got_a = meeting(own_a)
     own_b = attend(q, *near, half, first_row, arrays)
+    got_b = meeting(own_b)
+    own_b, near_weight, far_weight = lax.optimization_barrier((own_b, near_weight, far_weight))
     total = project_chip(own_a, own_b, out_weight, order)
-    total, near_weight, far_weight, got_a = lax.optimization_barrier(
-        (total, near_weight, far_weight, got_a)
-    )
-    got_b = meeting(own_b)
+    total, got_a = lax.optimization_barrier((total, got_a))
     product = lambda got, unit, keep: project_pair(
         got, near_weight, far_weight, total, unit, keep, cores
     )
     there_a, here_a = product(got_a, 0, False)
     there_a, here_a, got_a = lax.optimization_barrier((there_a, here_a, got_a))
-    pass_a = here_a + over_head(there_a, 1)
-    keep_there_a, keep_here_a = product(got_a, 0, True)
-    pass_a, got_b, keep_there_a = lax.optimization_barrier((pass_a, got_b, keep_there_a))
-    sent_a = ending(pass_a)
+    keep_a = product(got_a, 0, True)
+    there_a, keep_a, got_b = lax.optimization_barrier((there_a, keep_a, got_b))
+    moved_a, keep_moved_a = over_head(there_a, 1), over_head(keep_a[0], 1)
     there_b, here_b = product(got_b, 1, False)
-    there_b, here_b, got_b = lax.optimization_barrier((there_b, here_b, got_b))
-    pass_b = here_b + over_head(there_b, 1)
-    keep_there_b, keep_here_b = product(got_b, 1, True)
-    kept_a = keep_here_a + over_head(keep_there_a, 1)
-    pass_b, sent_a, keep_there_b = lax.optimization_barrier((pass_b, sent_a, keep_there_b))
-    sent_b = ending(pass_b)
-    kept_b = keep_here_b + over_head(keep_there_b, 1)
+    there_b, here_b, moved_a, keep_moved_a, got_b = lax.optimization_barrier(
+        (there_b, here_b, moved_a, keep_moved_a, got_b)
+    )
+    pass_a, pass_b = here_a + moved_a, here_b + over_head(there_b, 1)
+    pass_a, pass_b, got_b = lax.optimization_barrier((pass_a, pass_b, got_b))
+    sent = ending(pass_a) + ending(pass_b)
+    keep_b = product(got_b, 1, True)
+    keep_b, sent = lax.optimization_barrier((keep_b, sent))
+    keep_moved_b = over_head(keep_b[0], 1)
+    kept_a, kept_b = keep_a[1] + keep_moved_a, keep_b[1] + keep_moved_b
     kept = (kept_a[0], kept_a[1], kept_b[0], kept_b[1])
-    return jnp.concatenate([a + b for a, b in zip(kept, (*sent_a, *sent_b))], axis=0)
+    return jnp.concatenate([a + b for a, b in zip(kept, sent)], axis=0)
 
 
 def solution(mesh):

time: 184 us -> 180 us (0.978)
  waiting for transfers between devices: 68.3 us -> 57.1 us
  Pallas kernels: 54.9 us -> 64.2 us
  starting transfers between devices: 43.7 us -> 48 us
  local copies, waits for them, and re-layouts: 5.39 us -> 1.93 us
  other arithmetic: 8.3 us -> 5.36 us
    ppermute x14, waiting for transfers between devices: 33.3 us -> 22.5 us  [body(): lax.ppermute(a, 'head', [(i, i ^ bits) for i in range(head_size)])]
    pallas_call x0 -> x2, Pallas kernels: none -> 9.21 us  [take_columns(): pl.pallas_call(take_kernel, out_shape=jax.ShapeDtypeStruct((rows, count *...]
    concatenate x2 -> x1, other arithmetic: 5.6 us -> 1.49 us  [body(): return jnp.concatenate([a + b for a, b in zip(kept, sent)], axis=0)]
    ppermute x14, starting transfers between devices: 9.96 us -> 13.8 us  [body(): lax.ppermute(a, 'head', [(i, i ^ bits) for i in range(head_size)])]
    dynamic_slice x1 -> x0, local copies, waits for them, and re-layouts: 3.44 us -> none  [body(): lax.dynamic_slice_in_dim(a, first * width, count * width, 1)]
  transfers between devices with their start and end apart: 33 -> 33, of which waited for: 16 -> 15; matrix products, arithmetic and copies ran while one was open for 7% -> 3% of each run, Pallas kernels for 25% -> 36%
where the time goes in v7:
time: 180 us; the launch traced here: 178 us
  Pallas kernels  64.2 us (36%)
  waiting for transfers between devices  57.1 us (32%)
  starting transfers between devices  48 us (27%)
  other arithmetic  5.36 us (3%)
  local copies, waits for them, and re-layouts  1.93 us (1%)
    ppermute x19, waiting for transfers between devices, body(): send = lambda a, pairs: lax.ppermute(a, 'seq', pairs)  34.7 us
    ppermute x19, starting transfers between devices, body(): send = lambda a, pairs: lax.ppermute(a, 'seq', pairs)  34.1 us
    ppermute x14, waiting for transfers between devices, body(): lax.ppermute(a, 'head', [(i, i ^ bits) for i in range(head_size)])  22.5 us
    pallas_call x4, Pallas kernels, project_pair(): pl.pallas_call(pair_kernel, out_shape=[out, out], grid_spec=pltpu.Prefetc...  20.2 us
    ppermute x14, starting transfers between devices, body(): lax.ppermute(a, 'head', [(i, i ^ bits) for i in range(head_size)])  13.8 us
    pallas_call x2, Pallas kernels, attend(): pl.pallas_call(functools.partial(attend_kernel, start), grid=(2, heads //...  12.6 us
    pallas_call x1, Pallas kernels, project_chip(): pl.pallas_call(chip_kernel, out_shape=jax.ShapeDtypeStruct((2, 2 * rows,...  9.94 us
    pallas_call x1, Pallas kernels, attend_near(): pl.pallas_call(functools.partial(near_kernel, start), grid=(rows // TILE,...  9.64 us
  transfers between devices with their start and end apart: 33, of which 15 were waited for; matrix products, arithmetic and copies ran while one was open for 3% of the time, Pallas kernels for 36%

profile of v7, /device:TPU:2, one launch (start us, length us, event | category | flops | bytes accessed | tf_op | source)
XLA Modules:
  0.0 177.7 jit_solution(14987021148103754161)
XLA Ops:
  0.5 1.6 collective-permute-start
  2.0 4.0 %collective-permute-start.3 = (f32[1024,128]{1,0:T(8,128)}, f32[1024,128]{1,0:T(8,128)S(1)}, u32[]{:S(2)}, u32[]{:S(2)}) collective-permute-start(f32[1024,128]{1,0:T(8,128)} %v_own.1), channel_id=1, source_target_pairs={{0,96},{8,104},{16,112},{24,120},{32,0},{40,8},{48,16},{56,24},{64... | collective-permute-start | bytes 1572872 | tf_op jit(solution)/shard_map/ppermute | solution.py:375
  6.7 4.6 %shard_map.80 = f32[512,2048]{1,0:T(8,128)} custom-call(s32[2]{0:T(128)} %pad_add_fusion.3.order, f32[512,4096]{1,0:T(8,128)} %w.1), custom_call_target="tpu_custom_call" | custom-call | flops 1024 | bytes 1024 | tf_op jit(solution)/shard_map/pallas_call | solution.py:259
  11.3 3.0 %collective-permute-start.20 = (f32[512,2048]{1,0:T(8,128)}, f32[512,2048]{1,0:T(8,128)}, u32[]{:S(2)}, u32[]{:S(2)}) collective-permute-start(f32[512,2048]{1,0:T(8,128)} %shard_map.80), channel_id=1, source_target_pairs={{0,6},{1,7},{2,4},{3,5},{4,2},{5,3},{6,0},{7,1},{8,14},{9,15},{10,... | collective-permute-start | bytes 12582920 | tf_op jit(solution)/shard_map/ppermute | solution.py:384
  17.5 4.6 %shard_map.79 = f32[512,2048]{1,0:T(8,128)} custom-call(s32[2]{0:T(128)} %pad_add_fusion.2.order, f32[512,4096]{1,0:T(8,128)} %w.1), custom_call_target="tpu_custom_call" | custom-call | flops 1024 | bytes 1024 | tf_op jit(solution)/shard_map/pallas_call | solution.py:259
  22.7 3.3 %collective-permute-start.5 = (f32[1024,128]{1,0:T(8,128)S(1)}, f32[1024,128]{1,0:T(8,128)S(1)}, u32[]{:S(2)}, u32[]{:S(2)}) collective-permute-start(f32[1024,128]{1,0:T(8,128)S(1)} %collective-permute-done.3.refs_1_), channel_id=1, source_target_pairs={{0,96},{8,104},{16,112},{24,120},{32,0},{40,8},{48,16},{56,24},{64... | collective-permute-start | bytes 1572872 | tf_op jit(solution)/shard_map/ppermute | solution.py:375
  26.2 1.3 collective-permute-start.4
  27.6 0.8 collective-permute-start.6
  28.5 7.3 %collective-permute-done.5.refs_2_ = f32[1024,128]{1,0:T(8,128)S(1)} collective-permute-done((f32[1024,128]{1,0:T(8,128)S(1)}, f32[1024,128]{1,0:T(8,128)S(1)}, u32[]{:S(2)}, u32[]{:S(2)}) %collective-permute-start.5) | collective-permute-done | bytes 524320 | tf_op jit(solution)/shard_map/ppermute | solution.py:375
  36.4 7.4 %collective-permute-done.4 = f32[1536,128]{1,0:T(8,128)S(1)} collective-permute-done((f32[1536,128]{1,0:T(8,128)S(1)}, f32[1536,128]{1,0:T(8,128)S(1)}, u32[]{:S(2)}, u32[]{:S(2)}) %collective-permute-start.4) | collective-permute-done | bytes 786464 | tf_op jit(solution)/shard_map/ppermute | solution.py:375
  43.8 2.6 %collective-permute-done.6 = f32[1536,128]{1,0:T(8,128)S(1)} collective-permute-done((f32[1536,128]{1,0:T(8,128)S(1)}, f32[1536,128]{1,0:T(8,128)S(1)}, u32[]{:S(2)}, u32[]{:S(2)}) %collective-permute-start.6) | collective-permute-done | bytes 786464 | tf_op jit(solution)/shard_map/ppermute | solution.py:375
  46.5 3.0 %collective-permute-start.9 = (f32[512,128]{1,0:T(8,128)S(1)}, f32[512,128]{1,0:T(8,128)S(1)}, u32[]{:S(2)}, u32[]{:S(2)}) collective-permute-start(f32[512,128]{1,0:T(8,128)S(1)} %slice.57), channel_id=1, source_target_pairs={{0,24},{8,0},{16,8},{24,16},{32,56},{40,32},{48,40},{56,48},{64,88... | collective-permute-start | bytes 786440 | tf_op jit(solution)/shard_map/ppermute | solution.py:375
  49.5 1.2 shard_map.74
  50.7 1.5 collective-permute-start.11
  52.2 3.8 %collective-permute-start.12 = (f32[1024,128]{1,0:T(8,128)S(1)}, f32[1024,128]{1,0:T(8,128)S(1)}, u32[]{:S(2)}, u32[]{:S(2)}) collective-permute-start(f32[1024,128]{1,0:T(8,128)S(1)} %get-tuple-element.96), channel_id=1, source_target_pairs={{0,96},{8,104},{16,112},{24,120},{32,64},{40,72},{48,80},{56,88},{... | collective-permute-start | bytes 1572872 | tf_op jit(solution)/shard_map/ppermute | solution.py:375
  56.1 1.2 shard_map.75
  57.3 5.1 %collective-permute-done.8.v_far_a = f32[512,128]{1,0:T(8,128)S(1)} collective-permute-done((f32[512,128]{1,0:T(8,128)S(1)}, f32[512,128]{1,0:T(8,128)S(1)}, u32[]{:S(2)}, u32[]{:S(2)}) %collective-permute-start.8) | collective-permute-done | bytes 262176 | tf_op jit(solution)/shard_map/ppermute | solution.py:375
  62.5 3.3 %collective-permute-start.10 = (f32[1024,128]{1,0:T(8,128)S(1)}, f32[1024,128]{1,0:T(8,128)S(1)}, u32[]{:S(2)}, u32[]{:S(2)}) collective-permute-start(f32[1024,128]{1,0:T(8,128)S(1)} %slice.58.refs_2_.k_far), channel_id=1, source_target_pairs={{0,32},{8,40},{32,64},{40,72},{64,96},{72,104},{1,33},{9,41},{33,6... | collective-permute-start | bytes 1572872 | tf_op jit(solution)/shard_map/ppermute | solution.py:375
  65.7 1.3 collective-permute-start.13
  67.3 5.1 %collective-permute-done.10.k_far_wrap = f32[1024,128]{1,0:T(8,128)S(1)} collective-permute-done((f32[1024,128]{1,0:T(8,128)S(1)}, f32[1024,128]{1,0:T(8,128)S(1)}, u32[]{:S(2)}, u32[]{:S(2)}) %collective-permute-start.10) | collective-permute-done | bytes 524320 | tf_op jit(solution)/shard_map/ppermute | solution.py:375
  72.4 2.6 %collective-permute-done.13 = f32[1024,128]{1,0:T(8,128)S(1)} collective-permute-done((f32[1024,128]{1,0:T(8,128)S(1)}, f32[1024,128]{1,0:T(8,128)S(1)}, u32[]{:S(2)}, u32[]{:S(2)}) %collective-permute-start.13) | collective-permute-done | bytes 524320 | tf_op jit(solution)/shard_map/ppermute | solution.py:375
  75.0 1.2 collective-permute-done.14
  76.3 3.0 %collective-permute-start.15 = (f32[1024,128]{1,0:T(8,128)S(1)}, f32[1024,128]{1,0:T(8,128)S(1)}, u32[]{:S(2)}, u32[]{:S(2)}) collective-permute-start(f32[1024,128]{1,0:T(8,128)S(1)} %add.206), channel_id=1, source_target_pairs={{0,96},{8,104},{16,112},{24,120},{32,64},{40,72},{48,80},{56,88},{... | collective-permute-start | bytes 1572872 | tf_op jit(solution)/shard_map/ppermute | solution.py:375
  79.5 4.0 %collective-permute-start.16 = (f32[1024,128]{1,0:T(8,128)S(1)}, f32[1024,128]{1,0:T(8,128)S(1)}, u32[]{:S(2)}, u32[]{:S(2)}) collective-permute-start(f32[1024,128]{1,0:T(8,128)S(1)} %add.207), channel_id=1, source_target_pairs={{0,32},{8,40},{16,48},{24,56},{32,0},{40,8},{48,16},{56,24},{64,96... | collective-permute-start | bytes 1572872 | tf_op jit(solution)/shard_map/ppermute | solution.py:375
  83.5 3.3 %collective-permute-done.15 = f32[1024,128]{1,0:T(8,128)S(1)} collective-permute-done((f32[1024,128]{1,0:T(8,128)S(1)}, f32[1024,128]{1,0:T(8,128)S(1)}, u32[]{:S(2)}, u32[]{:S(2)}) %collective-permute-start.15) | collective-permute-done | bytes 524320 | tf_op jit(solution)/shard_map/ppermute | solution.py:375
  86.8 2.0 %collective-permute-start.18 = (f32[1024,128]{1,0:T(8,128)S(1)}, f32[1024,128]{1,0:T(8,128)S(1)}, u32[]{:S(2)}, u32[]{:S(2)}) collective-permute-start(f32[1024,128]{1,0:T(8,128)S(1)} %add.209), channel_id=1, source_target_pairs={{0,8},{8,0},{16,24},{24,16},{32,40},{40,32},{48,56},{56,48},{64,72... | collective-permute-start | bytes 1572872 | tf_op jit(solution)/shard_map/ppermute | solution.py:375
  88.8 9.6 %shard_map.76 = (f32[1024,512]{1,0:T(8,128)S(1)}, f32[1024,256]{1,0:T(8,128)S(1)}) custom-call(s32[1]{0:T(128)} %bitcast.1.first_row, s32[4,4]{1,0:T(4,128)S(1)} %get-tuple-element.104.back, s32[2]{0:T(128)S(1)} %add_convert_fusion.wraps, f32[1024,512]{1,0:T(8,128)S(1)} %shard_map.73.q, f32[1024,128]{1,0:T(8,128)S(1)} %slice.58.refs_2_.k_far, ...), custom_call_target="tpu_custom_call" | custom-call | flops 1073741824 | bytes 1048576 | tf_op jit(solution)/shard_map/pallas_call | solution.py:177
  98.8 6.3 %shard_map.77.own_a = f32[2,256,512]{2,1,0:T(8,128)S(1)} custom-call(s32[1]{0:T(128)} %bitcast.1.first_row, f32[1024,512]{1,0:T(8,128)S(1)} %shard_map.73.q, f32[1024,512]{1,0:T(8,128)S(1)} %get-tuple-element.117.near, f32[1024,256]{1,0:T(8,128)S(1)} %get-tuple-element.118.stats, f32[1024,128]{1,0:T(8,128)S(1)} %add.210.k_a, f32[1024,128]{1,0:T(8,128)S(1)} %add.211.k_b, ...), custom_call_target="tpu_custom_call" | custom-call | flops 1073741824 | bytes 1048576 | tf_op jit(solution)/shard_map/pallas_call | solution.py:234
  105.1 0.8 collective-permute-start.22
  105.9 0.8 collective-permute-start.21
  106.7 6.3 %shard_map.78.own_b = f32[2,256,512]{2,1,0:T(8,128)S(1)} custom-call(s32[1]{0:T(128)} %bitcast.1.first_row, f32[1024,512]{1,0:T(8,128)S(1)} %shard_map.73.q, f32[1024,512]{1,0:T(8,128)S(1)} %get-tuple-element.117.near, f32[1024,256]{1,0:T(8,128)S(1)} %get-tuple-element.118.stats, f32[1024,128]{1,0:T(8,128)S(1)} %add.210.k_a, f32[1024,128]{1,0:T(8,128)S(1)} %add.211.k_b, ...), custom_call_target="tpu_custom_call" | custom-call | flops 1073741824 | bytes 1048576 | tf_op jit(solution)/shard_map/pallas_call | solution.py:234
  113.1 2.6 %collective-permute-start.24 = (f32[256,512]{1,0:T(8,128)S(1)}, f32[256,512]{1,0:T(8,128)S(1)}, u32[]{:S(2)}, u32[]{:S(2)}) collective-permute-start(f32[256,512]{1,0:T(8,128)S(1)} %get-tuple-element.183), channel_id=1, source_target_pairs={{0,6},{1,7},{2,4},{3,5},{4,2},{5,3},{6,0},{7,1},{8,14},{9,15},{10,... | collective-permute-start | bytes 1572872 | tf_op jit(solution)/shard_map/ppermute | solution.py:384
  116.3 9.9 %shard_map.81.total = f32[2,512,2048]{2,1,0:T(8,128)S(1)} custom-call(s32[8]{0:T(128)S(1)} %pad_add_fusion.1.order, f32[2,256,512]{2,1,0:T(8,128)S(1)} %shard_map.77.own_a, f32[2,256,512]{2,1,0:T(8,128)S(1)} %shard_map.78.own_b, f32[512,4096]{1,0:T(8,128)S(1)} %bitcast.44), custom_call_target="tpu_custom_call" | custom-call | flops 1073741824 | bytes 1048576 | tf_op jit(solution)/shard_map/pallas_call | solution.py:296
  126.3 1.3 collective-permute-done.21.got_a
  127.6 5.0 %shard_map.82 = (f32[2,256,512]{2,1,0:T(8,128)S(1)}, f32[2,256,512]{2,1,0:T(8,128)S(1)}) custom-call(s32[2]{0:T(128)S(1)} %get-tuple-element.85.cores, f32[256,512]{1,0:T(8,128)S(1)} %collective-permute-done.21.got_a, f32[256,512]{1,0:T(8,128)S(1)} %collective-permute-done.22.got_b, f32[512,2048]{1,0:T(8,128)S(1)} %collective-permute-done.19.near, ...), custom_call_target="tpu_custom_call" | custom-call | flops 1073741824 | bytes 1048576 | tf_op jit(solution)/shard_map/pallas_call | solution.py:335
  132.6 5.0 %shard_map.83 = (f32[2,256,512]{2,1,0:T(8,128)S(1)}, f32[2,256,512]{2,1,0:T(8,128)S(1)}) custom-call(s32[2]{0:T(128)S(1)} %get-tuple-element.85.cores, f32[256,512]{1,0:T(8,128)S(1)} %collective-permute-done.21.got_a, f32[256,512]{1,0:T(8,128)S(1)} %collective-permute-done.22.got_b, f32[512,2048]{1,0:T(8,128)S(1)} %collective-permute-done.19.near, ...), custom_call_target="tpu_custom_call" | custom-call | flops 1073741824 | bytes 1048576 | tf_op jit(solution)/shard_map/pallas_call | solution.py:335
  138.3 5.0 %shard_map.84 = (f32[2,256,512]{2,1,0:T(8,128)S(1)}, f32[2,256,512]{2,1,0:T(8,128)S(1)}) custom-call(s32[2]{0:T(128)S(1)} %get-tuple-element.85.cores, f32[256,512]{1,0:T(8,128)S(1)} %collective-permute-done.23.got_a, f32[256,512]{1,0:T(8,128)S(1)} %collective-permute-done.24.got_b, f32[512,2048]{1,0:T(8,128)S(1)} %collective-permute-done.19.near, ...), custom_call_target="tpu_custom_call" | custom-call | flops 1073741824 | bytes 1048576 | tf_op jit(solution)/shard_map/pallas_call | solution.py:335
  143.9 2.1 %collective-permute-done.27 = f32[2,256,512]{2,1,0:T(8,128)S(1)} collective-permute-done((f32[2,256,512]{2,1,0:T(8,128)S(1)}, f32[2,256,512]{2,1,0:T(8,128)S(1)}, u32[]{:S(2)}, u32[]{:S(2)}) %collective-permute-start.27) | collective-permute-done | bytes 1048608 | tf_op jit(solution)/shard_map/ppermute | solution.py:384
  146.6 1.0 collective-permute-start.28
  147.7 0.9 collective-permute-start.31
  148.6 2.6 %collective-permute-start.30 = (f32[256,512]{1,0:T(8,128)S(1)}, f32[256,512]{1,0:T(8,128)S(1)}, u32[]{:S(2)}, u32[]{:S(2)}) collective-permute-start(f32[256,512]{1,0:T(8,128)S(1)} %get-tuple-element.180), channel_id=1, source_target_pairs={{0,6},{1,7},{2,4},{3,5},{4,2},{5,3},{6,0},{7,1},{8,14},{9,15},{10,... | collective-permute-start | bytes 1572872 | tf_op jit(solution)/shard_map/ppermute | solution.py:384
  151.3 5.0 %shard_map.85 = (f32[2,256,512]{2,1,0:T(8,128)S(1)}, f32[2,256,512]{2,1,0:T(8,128)S(1)}) custom-call(s32[2]{0:T(128)S(1)} %get-tuple-element.85.cores, f32[256,512]{1,0:T(8,128)S(1)} %collective-permute-done.23.got_a, f32[256,512]{1,0:T(8,128)S(1)} %collective-permute-done.24.got_b, f32[512,2048]{1,0:T(8,128)S(1)} %collective-permute-done.19.near, ...), custom_call_target="tpu_custom_call" | custom-call | flops 1073741824 | bytes 1048576 | tf_op jit(solution)/shard_map/pallas_call | solution.py:335
  156.3 4.9 %collective-permute-done.29 = f32[256,512]{1,0:T(8,128)S(1)} collective-permute-done((f32[256,512]{1,0:T(8,128)S(1)}, f32[256,512]{1,0:T(8,128)S(1)}, u32[]{:S(2)}, u32[]{:S(2)}) %collective-permute-start.29) | collective-permute-done | bytes 524320 | tf_op jit(solution)/shard_map/ppermute | solution.py:384
  161.2 1.4 collective-permute-done.28
  162.6 9.2 %collective-permute-done.31 = f32[256,512]{1,0:T(8,128)S(1)} collective-permute-done((f32[256,512]{1,0:T(8,128)S(1)}, f32[256,512]{1,0:T(8,128)S(1)}, u32[]{:S(2)}, u32[]{:S(2)}) %collective-permute-start.31) | collective-permute-done | bytes 524320 | tf_op jit(solution)/shard_map/ppermute | solution.py:384
  171.8 1.3 collective-permute-done.30
  173.6 2.2 %collective-permute-done.32 = f32[2,256,512]{2,1,0:T(8,128)S(1)} collective-permute-done((f32[2,256,512]{2,1,0:T(8,128)S(1)}, f32[2,256,512]{2,1,0:T(8,128)S(1)}, u32[]{:S(2)}, u32[]{:S(2)}) %collective-permute-start.32) | collective-permute-done | bytes 1048608 | tf_op jit(solution)/shard_map/ppermute | solution.py:384
  176.2 1.5 pad_maximum_fusion
  (110 shorter events, 9.4 us)
Async XLA Ops:
  0.0 15.5 %copy-start = (s32[32,3]{0,1:T(4,128)S(1)}, s32[32,3]{0,1:T(4,128)}, u32[]{:S(2)}) copy-start(s32[32,3]{0,1:T(4,128)} %param.11) | copy-start | bytes 1156
  0.0 22.5 %collective-permute-start.1 = (f32[1024,128]{1,0:T(8,128)}, f32[1024,128]{1,0:T(8,128)S(1)}, u32[]{:S(2)}, u32[]{:S(2)}) collective-permute-start(f32[1024,128]{1,0:T(8,128)} %k_own.1), channel_id=1, source_target_pairs={{0,24},{8,0},{16,8},{24,16},{32,56},{40,32},{48,40},{56,48},{64,88... | collective-permute-start | bytes 1572872 | tf_op jit(solution)/shard_map/ppermute | solution.py:375
  0.5 22.3 %collective-permute-start = (f32[1024,128]{1,0:T(8,128)}, f32[1024,128]{1,0:T(8,128)S(1)}, u32[]{:S(2)}, u32[]{:S(2)}) collective-permute-start(f32[1024,128]{1,0:T(8,128)} %k_own.1), channel_id=1, source_target_pairs={{0,8},{8,16},{16,24},{24,0},{32,40},{40,48},{48,56},{56,32},{64,72... | collective-permute-start | bytes 1572872 | tf_op jit(solution)/shard_map/ppermute | solution.py:375
  2.0 20.7 %collective-permute-start.3 = (f32[1024,128]{1,0:T(8,128)}, f32[1024,128]{1,0:T(8,128)S(1)}, u32[]{:S(2)}, u32[]{:S(2)}) collective-permute-start(f32[1024,128]{1,0:T(8,128)} %v_own.1), channel_id=1, source_target_pairs={{0,96},{8,104},{16,112},{24,120},{32,0},{40,8},{48,16},{56,24},{64... | collective-permute-start | bytes 1572872 | tf_op jit(solution)/shard_map/ppermute | solution.py:375
  6.1 16.7 %collective-permute-start.2 = (f32[1024,128]{1,0:T(8,128)}, f32[1024,128]{1,0:T(8,128)S(1)}, u32[]{:S(2)}, u32[]{:S(2)}) collective-permute-start(f32[1024,128]{1,0:T(8,128)} %v_own.1), channel_id=1, source_target_pairs={{0,32},{8,40},{16,48},{24,56},{32,64},{40,72},{48,80},{56,88},{64,... | collective-permute-start | bytes 1572872 | tf_op jit(solution)/shard_map/ppermute | solution.py:375
  6.7 9.2 %copy-start.5 = (s32[32,8]{0,1:T(8,128)S(1)}, s32[32,8]{0,1:T(8,128)}, u32[]{:S(2)}) copy-start(s32[32,8]{0,1:T(8,128)} %param.10) | copy-start | bytes 3076
  11.3 104.5 %collective-permute-start.20 = (f32[512,2048]{1,0:T(8,128)}, f32[512,2048]{1,0:T(8,128)}, u32[]{:S(2)}, u32[]{:S(2)}) collective-permute-start(f32[512,2048]{1,0:T(8,128)} %shard_map.80), channel_id=1, source_target_pairs={{0,6},{1,7},{2,4},{3,5},{4,2},{5,3},{6,0},{7,1},{8,14},{9,15},{10,... | collective-permute-start | bytes 12582920 | tf_op jit(solution)/shard_map/ppermute | solution.py:384
  17.5 8.6 %copy-start.2 = (f32[1024,128]{1,0:T(8,128)S(1)}, f32[1024,128]{1,0:T(8,128)}, u32[]{:S(2)}) copy-start(f32[1024,128]{1,0:T(8,128)} %v_own.1) | copy-start | bytes 1572868
  22.5 93.8 %collective-permute-start.19 = (f32[512,2048]{1,0:T(8,128)}, f32[512,2048]{1,0:T(8,128)S(1)}, u32[]{:S(2)}, u32[]{:S(2)}) collective-permute-start(f32[512,2048]{1,0:T(8,128)} %shard_map.79), channel_id=1, source_target_pairs={{0,2},{1,3},{2,0},{3,1},{4,6},{5,7},{6,4},{7,5},{8,10},{9,11},{10,... | collective-permute-start | bytes 12582920 | tf_op jit(solution)/shard_map/ppermute | solution.py:384
  22.7 13.0 %collective-permute-start.5 = (f32[1024,128]{1,0:T(8,128)S(1)}, f32[1024,128]{1,0:T(8,128)S(1)}, u32[]{:S(2)}, u32[]{:S(2)}) collective-permute-start(f32[1024,128]{1,0:T(8,128)S(1)} %collective-permute-done.3.refs_1_), channel_id=1, source_target_pairs={{0,96},{8,104},{16,112},{24,120},{32,0},{40,8},{48,16},{56,24},{64... | collective-permute-start | bytes 1572872 | tf_op jit(solution)/shard_map/ppermute | solution.py:375
  26.2 23.3 %copy-start.4 = (f32[1024,128]{1,0:T(8,128)S(1)}, f32[1024,128]{1,0:T(8,128)}, u32[]{:S(2)}) copy-start(f32[1024,128]{1,0:T(8,128)} %k_own.1) | copy-start | bytes 1572868
  26.2 17.6 %collective-permute-start.4 = (f32[1536,128]{1,0:T(8,128)S(1)}, f32[1536,128]{1,0:T(8,128)S(1)}, u32[]{:S(2)}, u32[]{:S(2)}) collective-permute-start(f32[1536,128]{1,0:T(8,128)S(1)} %pad_maximum_fusion.1), channel_id=1, source_target_pairs={{0,24},{8,0},{16,8},{24,16},{32,56},{40,32},{48,40},{56,48},{64,88... | collective-permute-start | bytes 2359304 | tf_op jit(solution)/shard_map/ppermute | solution.py:375
  27.6 18.8 %collective-permute-start.6 = (f32[1536,128]{1,0:T(8,128)S(1)}, f32[1536,128]{1,0:T(8,128)S(1)}, u32[]{:S(2)}, u32[]{:S(2)}) collective-permute-start(f32[1536,128]{1,0:T(8,128)S(1)} %pad_maximum_fusion.2), channel_id=1, source_target_pairs={{0,8},{8,16},{16,24},{24,0},{32,40},{40,48},{48,56},{56,32},{64,72... | collective-permute-start | bytes 2359304 | tf_op jit(solution)/shard_map/ppermute | solution.py:375
  35.7 0.7 collective-permute-start.7
  46.5 20.6 %copy-start.3 = (f32[1024,512]{1,0:T(8,128)S(1)}, f32[1024,512]{1,0:T(8,128)}, u32[]{:S(2)}) copy-start(f32[1024,512]{1,0:T(8,128)} %q.1) | copy-start | bytes 6291460
  46.5 9.5 %collective-permute-start.9 = (f32[512,128]{1,0:T(8,128)S(1)}, f32[512,128]{1,0:T(8,128)S(1)}, u32[]{:S(2)}, u32[]{:S(2)}) collective-permute-start(f32[512,128]{1,0:T(8,128)S(1)} %slice.57), channel_id=1, source_target_pairs={{0,24},{8,0},{16,8},{24,16},{32,56},{40,32},{48,40},{56,48},{64,88... | collective-permute-start | bytes 786440 | tf_op jit(solution)/shard_map/ppermute | solution.py:375
  50.7 15.0 %collective-permute-start.11 = (f32[1024,128]{1,0:T(8,128)S(1)}, f32[1024,128]{1,0:T(8,128)S(1)}, u32[]{:S(2)}, u32[]{:S(2)}) collective-permute-start(f32[1024,128]{1,0:T(8,128)S(1)} %get-tuple-element.95), channel_id=1, source_target_pairs={{0,32},{8,40},{16,48},{24,56},{32,0},{40,8},{48,16},{56,24},{64,96... | collective-permute-start | bytes 1572872 | tf_op jit(solution)/shard_map/ppermute | solution.py:375
  52.2 14.9 %collective-permute-start.12 = (f32[1024,128]{1,0:T(8,128)S(1)}, f32[1024,128]{1,0:T(8,128)S(1)}, u32[]{:S(2)}, u32[]{:S(2)}) collective-permute-start(f32[1024,128]{1,0:T(8,128)S(1)} %get-tuple-element.96), channel_id=1, source_target_pairs={{0,96},{8,104},{16,112},{24,120},{32,64},{40,72},{48,80},{56,88},{... | collective-permute-start | bytes 1572872 | tf_op jit(solution)/shard_map/ppermute | solution.py:375
  56.0 6.4 %collective-permute-start.8 = (f32[512,128]{1,0:T(8,128)S(1)}, f32[512,128]{1,0:T(8,128)S(1)}, u32[]{:S(2)}, u32[]{:S(2)}) collective-permute-start(f32[512,128]{1,0:T(8,128)S(1)} %slice.56), channel_id=1, source_target_pairs={{0,8},{8,16},{16,24},{24,0},{32,40},{40,48},{48,56},{56,32},{64,72... | collective-permute-start | bytes 786440 | tf_op jit(solution)/shard_map/ppermute | solution.py:375
  62.5 9.9 %collective-permute-start.10 = (f32[1024,128]{1,0:T(8,128)S(1)}, f32[1024,128]{1,0:T(8,128)S(1)}, u32[]{:S(2)}, u32[]{:S(2)}) collective-permute-start(f32[1024,128]{1,0:T(8,128)S(1)} %slice.58.refs_2_.k_far), channel_id=1, source_target_pairs={{0,32},{8,40},{32,64},{40,72},{64,96},{72,104},{1,33},{9,41},{33,6... | collective-permute-start | bytes 1572872 | tf_op jit(solution)/shard_map/ppermute | solution.py:375
  65.7 9.3 %collective-permute-start.13 = (f32[1024,128]{1,0:T(8,128)S(1)}, f32[1024,128]{1,0:T(8,128)S(1)}, u32[]{:S(2)}, u32[]{:S(2)}) collective-permute-start(f32[1024,128]{1,0:T(8,128)S(1)} %get-tuple-element.100), channel_id=1, source_target_pairs={{0,8},{8,0},{16,24},{24,16},{32,40},{40,32},{48,56},{56,48},{64,72... | collective-permute-start | bytes 1572872 | tf_op jit(solution)/shard_map/ppermute | solution.py:375
  67.1 9.2 %collective-permute-start.14 = (f32[1024,128]{1,0:T(8,128)S(1)}, f32[1024,128]{1,0:T(8,128)S(1)}, u32[]{:S(2)}, u32[]{:S(2)}) collective-permute-start(f32[1024,128]{1,0:T(8,128)S(1)} %get-tuple-element.101), channel_id=1, source_target_pairs={{0,24},{8,16},{16,8},{24,0},{32,56},{40,48},{48,40},{56,32},{64,88... | collective-permute-start | bytes 1572872 | tf_op jit(solution)/shard_map/ppermute | solution.py:375
  76.3 10.5 %collective-permute-start.15 = (f32[1024,128]{1,0:T(8,128)S(1)}, f32[1024,128]{1,0:T(8,128)S(1)}, u32[]{:S(2)}, u32[]{:S(2)}) collective-permute-start(f32[1024,128]{1,0:T(8,128)S(1)} %add.206), channel_id=1, source_target_pairs={{0,96},{8,104},{16,112},{24,120},{32,64},{40,72},{48,80},{56,88},{... | collective-permute-start | bytes 1572872 | tf_op jit(solution)/shard_map/ppermute | solution.py:375
  79.5 19.0 %collective-permute-start.16 = (f32[1024,128]{1,0:T(8,128)S(1)}, f32[1024,128]{1,0:T(8,128)S(1)}, u32[]{:S(2)}, u32[]{:S(2)}) collective-permute-start(f32[1024,128]{1,0:T(8,128)S(1)} %add.207), channel_id=1, source_target_pairs={{0,32},{8,40},{16,48},{24,56},{32,0},{40,8},{48,16},{56,24},{64,96... | collective-permute-start | bytes 1572872 | tf_op jit(solution)/shard_map/ppermute | solution.py:375
  83.5 15.0 %collective-permute-start.17 = (f32[1024,128]{1,0:T(8,128)S(1)}, f32[1024,128]{1,0:T(8,128)S(1)}, u32[]{:S(2)}, u32[]{:S(2)}) collective-permute-start(f32[1024,128]{1,0:T(8,128)S(1)} %add.208), channel_id=1, source_target_pairs={{0,24},{8,16},{16,8},{24,0},{32,56},{40,48},{48,40},{56,32},{64,88... | collective-permute-start | bytes 1572872 | tf_op jit(solution)/shard_map/ppermute | solution.py:375
  86.8 11.7 %collective-permute-start.18 = (f32[1024,128]{1,0:T(8,128)S(1)}, f32[1024,128]{1,0:T(8,128)S(1)}, u32[]{:S(2)}, u32[]{:S(2)}) collective-permute-start(f32[1024,128]{1,0:T(8,128)S(1)} %add.209), channel_id=1, source_target_pairs={{0,8},{8,0},{16,24},{24,16},{32,40},{40,32},{48,56},{56,48},{64,72... | collective-permute-start | bytes 1572872 | tf_op jit(solution)/shard_map/ppermute | solution.py:375
  98.7 17.6 %slice-start = ((s8[8388608]{0:T(1024)(128)(4,1)}), s8[4194304]{0:T(1024)(128)(4,1)S(1)}, s32[]{:S(2)}) async-start(s8[8388608]{0:T(1024)(128)(4,1)} %bitcast.43), calls=%async_computation | async-start | bytes 8388608
  105.1 21.2 %collective-permute-start.22 = (f32[256,512]{1,0:T(8,128)S(1)}, f32[256,512]{1,0:T(8,128)S(1)}, u32[]{:S(2)}, u32[]{:S(2)}) collective-permute-start(f32[256,512]{1,0:T(8,128)S(1)} %get-tuple-element.185), channel_id=1, source_target_pairs={{0,6},{1,7},{2,4},{3,5},{4,2},{5,3},{6,0},{7,1},{8,14},{9,15},{10,... | collective-permute-start | bytes 1572872 | tf_op jit(solution)/shard_map/ppermute | solution.py:384
  105.9 10.4 %slice-start.1 = ((s8[8388608]{0:T(1024)(128)(4,1)}), s8[4194304]{0:T(1024)(128)(4,1)S(1)}, s32[]{:S(2)}) async-start(s8[8388608]{0:T(1024)(128)(4,1)} %bitcast.43), calls=%async_computation.1 | async-start | bytes 8388608
  105.9 21.6 %collective-permute-start.21 = (f32[256,512]{1,0:T(8,128)S(1)}, f32[256,512]{1,0:T(8,128)S(1)}, u32[]{:S(2)}, u32[]{:S(2)}) collective-permute-start(f32[256,512]{1,0:T(8,128)S(1)} %get-tuple-element.186), channel_id=1, source_target_pairs={{0,2},{1,3},{2,0},{3,1},{4,6},{5,7},{6,4},{7,5},{8,10},{9,11},{10,... | collective-permute-start | bytes 1572872 | tf_op jit(solution)/shard_map/ppermute | solution.py:384
  113.1 24.5 %collective-permute-start.24 = (f32[256,512]{1,0:T(8,128)S(1)}, f32[256,512]{1,0:T(8,128)S(1)}, u32[]{:S(2)}, u32[]{:S(2)}) collective-permute-start(f32[256,512]{1,0:T(8,128)S(1)} %get-tuple-element.183), channel_id=1, source_target_pairs={{0,6},{1,7},{2,4},{3,5},{4,2},{5,3},{6,0},{7,1},{8,14},{9,15},{10,... | collective-permute-start | bytes 1572872 | tf_op jit(solution)/shard_map/ppermute | solution.py:384
  115.7 22.0 %collective-permute-start.23 = (f32[256,512]{1,0:T(8,128)S(1)}, f32[256,512]{1,0:T(8,128)S(1)}, u32[]{:S(2)}, u32[]{:S(2)}) collective-permute-start(f32[256,512]{1,0:T(8,128)S(1)} %get-tuple-element.184), channel_id=1, source_target_pairs={{0,2},{1,3},{2,0},{3,1},{4,6},{5,7},{6,4},{7,5},{8,10},{9,11},{10,... | collective-permute-start | bytes 1572872 | tf_op jit(solution)/shard_map/ppermute | solution.py:384
  137.7 5.6 %collective-permute-start.25 = (f32[2,256,512]{2,1,0:T(8,128)S(1)}, f32[2,256,512]{2,1,0:T(8,128)S(1)}, u32[]{:S(2)}, u32[]{:S(2)}) collective-permute-start(f32[2,256,512]{2,1,0:T(8,128)S(1)} %get-tuple-element.144), channel_id=1, source_target_pairs={{0,1},{1,0},{2,3},{3,2},{4,5},{5,4},{6,7},{7,6},{8,9},{9,8},{10,11... | collective-permute-start | bytes 3145736 | tf_op jit(solution)/shard_map/ppermute | solution.py:384
  137.8 5.6 %collective-permute-start.26 = (f32[2,256,512]{2,1,0:T(8,128)S(1)}, f32[2,256,512]{2,1,0:T(8,128)S(1)}, u32[]{:S(2)}, u32[]{:S(2)}) collective-permute-start(f32[2,256,512]{2,1,0:T(8,128)S(1)} %get-tuple-element.145), channel_id=1, source_target_pairs={{0,1},{1,0},{2,3},{3,2},{4,5},{5,4},{6,7},{7,6},{8,9},{9,8},{10,11... | collective-permute-start | bytes 3145736 | tf_op jit(solution)/shard_map/ppermute | solution.py:384
  143.3 2.7 %collective-permute-start.27 = (f32[2,256,512]{2,1,0:T(8,128)S(1)}, f32[2,256,512]{2,1,0:T(8,128)S(1)}, u32[]{:S(2)}, u32[]{:S(2)}) collective-permute-start(f32[2,256,512]{2,1,0:T(8,128)S(1)} %get-tuple-element.150), channel_id=1, source_target_pairs={{0,1},{1,0},{2,3},{3,2},{4,5},{5,4},{6,7},{7,6},{8,9},{9,8},{10,11... | collective-permute-start | bytes 3145736 | tf_op jit(solution)/shard_map/ppermute | solution.py:384
  146.4 14.8 %collective-permute-start.29 = (f32[256,512]{1,0:T(8,128)S(1)}, f32[256,512]{1,0:T(8,128)S(1)}, u32[]{:S(2)}, u32[]{:S(2)}) collective-permute-start(f32[256,512]{1,0:T(8,128)S(1)} %get-tuple-element.181), channel_id=1, source_target_pairs={{0,2},{1,3},{2,0},{3,1},{4,6},{5,7},{6,4},{7,5},{8,10},{9,11},{10,... | collective-permute-start | bytes 1572872 | tf_op jit(solution)/shard_map/ppermute | solution.py:384
  146.6 16.0 %collective-permute-start.28 = (f32[256,512]{1,0:T(8,128)S(1)}, f32[256,512]{1,0:T(8,128)S(1)}, u32[]{:S(2)}, u32[]{:S(2)}) collective-permute-start(f32[256,512]{1,0:T(8,128)S(1)} %get-tuple-element.182), channel_id=1, source_target_pairs={{0,6},{1,7},{2,4},{3,5},{4,2},{5,3},{6,0},{7,1},{8,14},{9,15},{10,... | collective-permute-start | bytes 1572872 | tf_op jit(solution)/shard_map/ppermute | solution.py:384
  147.7 24.1 %collective-permute-start.31 = (f32[256,512]{1,0:T(8,128)S(1)}, f32[256,512]{1,0:T(8,128)S(1)}, u32[]{:S(2)}, u32[]{:S(2)}) collective-permute-start(f32[256,512]{1,0:T(8,128)S(1)} %get-tuple-element.179), channel_id=1, source_target_pairs={{0,2},{1,3},{2,0},{3,1},{4,6},{5,7},{6,4},{7,5},{8,10},{9,11},{10,... | collective-permute-start | bytes 1572872 | tf_op jit(solution)/shard_map/ppermute | solution.py:384
  148.6 24.5 %collective-permute-start.30 = (f32[256,512]{1,0:T(8,128)S(1)}, f32[256,512]{1,0:T(8,128)S(1)}, u32[]{:S(2)}, u32[]{:S(2)}) collective-permute-start(f32[256,512]{1,0:T(8,128)S(1)} %get-tuple-element.180), channel_id=1, source_target_pairs={{0,6},{1,7},{2,4},{3,5},{4,2},{5,3},{6,0},{7,1},{8,14},{9,15},{10,... | collective-permute-start | bytes 1572872 | tf_op jit(solution)/shard_map/ppermute | solution.py:384
  173.1 2.7 %collective-permute-start.32 = (f32[2,256,512]{2,1,0:T(8,128)S(1)}, f32[2,256,512]{2,1,0:T(8,128)S(1)}, u32[]{:S(2)}, u32[]{:S(2)}) collective-permute-start(f32[2,256,512]{2,1,0:T(8,128)S(1)} %get-tuple-element.162), channel_id=1, source_target_pairs={{0,1},{1,0},{2,3},{3,2},{4,5},{5,4},{6,7},{7,6},{8,9},{9,8},{10,11... | collective-permute-start | bytes 3145736 | tf_op jit(solution)/shard_map/ppermute | solution.py:384
  176.2 1.5 copy-start.1

commit v8 on v7

--- a/solution.py
+++ b/solution.py
@@ -13,45 +13,47 @@
 TILE = 256
 FAR = 1 << 30
 LOW = -1e30
-LARGE = pl.CostEstimate(flops=1 << 30, bytes_accessed=1 << 20, transcendentals=0)
+LARGE = pl.CostEstimate(flops=100000, bytes_accessed=1024, transcendentals=0)
+HUGE = pl.CostEstimate(flops=6 << 30, bytes_accessed=1024, transcendentals=0)
 SMALL = pl.CostEstimate(flops=1024, bytes_accessed=1024, transcendentals=0)
 
 
-def pick_kernel(place, held, *refs):
-    *pieces, first, second, rows = refs
+def pick_kernel(k_place, k_held, v_place, v_held, *refs):
+    pieces, outs, rows = refs[:8], refs[8:12], refs[12:]
     size = pieces[0].shape[0]
-    for at, piece in enumerate(pieces):
-        rows[at * size : (at + 1) * size, :] = piece[...]
-    slots = first.shape[0] // BLOCK
-    for slot in range(2 * slots):
-        out = first if slot < slots else second
-        target = pl.ds(slot % slots * BLOCK, BLOCK)
-
-        @pl.when(held[slot] == 1)
-        def _():
-            start = pl.multiple_of(place[slot] * BLOCK, BLOCK)
-            out[target, :] = rows[pl.ds(start, BLOCK), :]
-
-        @pl.when(held[slot] == 0)
-        def _():
-            out[target, :] = jnp.zeros((BLOCK, HEAD_SIZE), jnp.float32)
-
-
-def pick_blocks(place, held, pieces):
-    half = place.shape[0] // 2 * BLOCK
+    slots = outs[0].shape[0] // BLOCK
+    for which, (place, held) in enumerate(((k_place, k_held), (v_place, v_held))):
+        for at in range(4):
+            rows[which][at * size : (at + 1) * size, :] = pieces[4 * which + at][...]
+        for slot in range(2 * slots):
+            out = outs[2 * which + slot // slots]
+            target = pl.ds(slot % slots * BLOCK, BLOCK)
+
+            @pl.when(held[slot] == 1)
+            def _():
+                start = pl.multiple_of(place[slot] * BLOCK, BLOCK)
+                out[target, :] = rows[which][pl.ds(start, BLOCK), :]
+
+            @pl.when(held[slot] == 0)
+            def _():
+                out[target, :] = jnp.zeros((BLOCK, HEAD_SIZE), jnp.float32)
+
+
+def pick_blocks(k_place, k_held, v_place, v_held, k_pieces, v_pieces):
+    half = k_place.shape[0] // 2 * BLOCK
     smem = pl.BlockSpec(memory_space=pltpu.SMEM)
     vmem = pl.BlockSpec(memory_space=pltpu.VMEM)
     out = jax.ShapeDtypeStruct((half, HEAD_SIZE), jnp.float32)
-    size = pieces[0].shape[0]
+    size = k_pieces[0].shape[0]
     return pl.pallas_call(
         pick_kernel,
-        out_shape=[out, out],
-        in_specs=[smem, smem] + [vmem] * len(pieces),
-        out_specs=[vmem] * 2,
-        scratch_shapes=[pltpu.VMEM((len(pieces) * size, HEAD_SIZE), jnp.float32)],
+        out_shape=[out] * 4,
+        in_specs=[smem] * 4 + [vmem] * 8,
+        out_specs=[vmem] * 4,
+        scratch_shapes=[pltpu.VMEM((4 * size, HEAD_SIZE), jnp.float32)] * 2,
         compiler_params=pltpu.CompilerParams(vmem_limit_bytes=16 << 20),
         cost_estimate=SMALL,
-    )(place, held, *pieces)
+    )(k_place, k_held, v_place, v_held, *k_pieces, *v_pieces)
 
 
 def split(x):
@@ -97,7 +99,7 @@
         in_specs=[spec],
         out_specs=spec,
         compiler_params=pltpu.CompilerParams(vmem_limit_bytes=8 << 20),
-        cost_estimate=LARGE,
+        cost_estimate=HUGE,
     )(q)
 
 
@@ -238,8 +240,8 @@
         in_specs=[
             smem,
             pl.BlockSpec(wide, lambda t, h: (base + t, h)),
-            pl.BlockSpec(wide, lambda t, h: (base + t, h)),
-            pl.BlockSpec((TILE, HEAD_SIZE), lambda t, h: (base + t, h)),
+            pl.BlockSpec(wide, lambda t, h: (t, h)),
+            pl.BlockSpec((TILE, HEAD_SIZE), lambda t, h: (t, h)),
         ]
         + [vmem] * len(arrays),
         out_specs=pl.BlockSpec((1, TILE, pair * HEAD_SIZE), lambda t, h: (t, 0, h)),
@@ -249,25 +251,30 @@
     )(first_row, q, near, stats, *arrays)
 
 
-def take_kernel(order, source, out):
-    out[...] = source[...]
-
-
-def take_columns(weight, order, width):
+def take_kernel(chips, one, two, three, near, far):
+    width = one.shape[1]
+    near[:, :width], near[:, width:] = one[...], two[...]
+    far[:, :width], far[:, width:] = three[...], two[...]
+
+
+def take_columns(weight, chips, width):
     rows = weight.shape[0]
-    count = order.shape[0]
+    step = rows // 8
+    out = jax.ShapeDtypeStruct((rows, 2 * width), jnp.float32)
+    out_spec = pl.BlockSpec((step, 2 * width), lambda i, o: (i, 0))
+    w_spec = lambda at: pl.BlockSpec((step, width), lambda i, o: (i, o[at]))
     return pl.pallas_call(
         take_kernel,
-        out_shape=jax.ShapeDtypeStruct((rows, count * width), jnp.float32),
+        out_shape=[out, out],
         grid_spec=pltpu.PrefetchScalarGridSpec(
             num_scalar_prefetch=1,
-            grid=(count,),
-            in_specs=[pl.BlockSpec((rows, width), lambda i, o: (0, o[i]))],
-            out_specs=pl.BlockSpec((rows, width), lambda i, o: (0, i)),
+            grid=(rows // step,),
+            in_specs=[w_spec(0), w_spec(1), w_spec(2)],
+            out_specs=[out_spec, out_spec],
         ),
         compiler_params=pltpu.CompilerParams(vmem_limit_bytes=58 << 20),
         cost_estimate=SMALL,
-    )(order, weight)
+    )(chips, weight, weight, weight)
 
 
 def weight_term(x, block):
@@ -295,11 +302,11 @@
     vmem = pl.BlockSpec(memory_space=pltpu.VMEM)
     return pl.pallas_call(
         chip_kernel,
-        out_shape=jax.ShapeDtypeStruct((2, 2 * rows, 4 * width), jnp.float32),
+        out_shape=jax.ShapeDtypeStruct((2, 2 * rows, 2 * width), jnp.float32),
         grid_spec=pltpu.PrefetchScalarGridSpec(
             num_scalar_prefetch=1,
-            grid=(2, 4),
-            in_specs=[vmem, vmem, pl.BlockSpec((depth, width), lambda k, j, o: (0, o[4 * k + j]))],
+            grid=(2, 2),
+            in_specs=[vmem, vmem, pl.BlockSpec((depth, width), lambda k, j, o: (0, o[2 * k + j]))],
             out_specs=pl.BlockSpec((1, 2 * rows, width), lambda k, j, o: (k, 0, j)),
             scratch_shapes=[pltpu.VMEM((4 * rows, depth), jnp.bfloat16)],
         ),
@@ -343,7 +350,7 @@
                 vmem,
                 w_spec(lambda k, s: jnp.where(k == 0, s, 1)),
                 w_spec(lambda k, s: jnp.where(k == 0, 0, s)),
-                pl.BlockSpec((1, rows, width), lambda k, s, c: (k, unit, 2 - base + s)),
+                pl.BlockSpec((1, rows, width), lambda k, s, c: (k, unit, s)),
             ],
             out_specs=[out_spec, out_spec],
             scratch_shapes=[pltpu.VMEM((2 * rows, depth), jnp.bfloat16)],
@@ -383,10 +390,8 @@
     y = head_index // 2
     over_head = lambda a, bits: lax.ppermute(a, "head", [(i, i ^ bits) for i in range(head_size)])
     width = out_weight.shape[1] // head_size
-    near_weight, far_weight = (
-        over_head(take_columns(out_weight, jnp.stack([y ^ chip, y ^ 2]), 2 * width), 2 * chip)
-        for chip in (1, 3)
-    )
+    near_weight, far_weight = take_columns(out_weight, y ^ jnp.arange(1, 4), 2 * width)
+    near_weight, far_weight = over_head(near_weight, 2), over_head(far_weight, 6)
 
     vert = lax.dynamic_slice_in_dim(vertical_blocks, head_index * heads, heads, 0)
     slash = lax.dynamic_slice_in_dim(slash_offsets, head_index * heads, heads, 0)
@@ -407,12 +412,13 @@
     back = 2 * blocks - offsets
     wraps = jnp.stack([x < 2, x == 0]).astype(jnp.int32)
     cores = jnp.stack([1 - core, core])
-    order = jnp.concatenate([2 * chip + cores for chip in (y ^ 3, y, y ^ 1, y)])
+    pass_order = jnp.concatenate([2 * chip + cores for chip in (y ^ 3, y ^ 1)])
+    keep_order = jnp.concatenate([2 * y + cores] * 2)
     owner = named // blocks
     at = named % blocks
     k_place, k_held = (owner % 4 - x) % 4 * blocks + at, (owner // 4 == z).astype(jnp.int32)
     v_place, v_held = (owner // 4 - z) % 4 * blocks + at, (owner % 4 == x).astype(jnp.int32)
-    orders = (order, cores)
+    orders = (pass_order, keep_order, cores)
     small = (vert_pos, slash_pos, first_row, back, wraps, orders, k_place, k_held, v_place, v_held)
 
     (k_left, k_right, v_below, v_above), small = lax.optimization_barrier(
@@ -432,12 +438,12 @@
     k_far, v_far_b = moved_left[:rows], moved_left[rows:]
     v_left, v_far_a = moved_right[:rows], moved_right[rows:]
 
-    k_named = pick_blocks(k_place, k_held, (key_rows, k_right, k_far, k_left))
-    v_named = pick_blocks(v_place, v_held, (value_vectors, v_above, v_beyond, v_below))
+    k_pieces = (key_rows, k_right, k_far, k_left)
+    v_pieces = (value_vectors, v_above, v_beyond, v_below)
+    named = pick_blocks(k_place, k_held, v_place, v_held, k_pieces, v_pieces)
     v_far_a = send(v_far_a, right)
     v_far_b = send(v_far_b, left)
     k_far_wrap = send(k_far, [(i, i + 4) for i in ids if i % 4 < 2 and i + 4 in ids])
-    named = [*k_named, *v_named]
     one, two = (4, 12, 1, 3), (12, 4, 3, 1)
     more = [swapped(a, bits) for a, bits in zip(named, one)]
     q = scaled(queries)
@@ -447,42 +453,41 @@
     named = [a + b for a, b in zip(named, more)]
     arrays = (k_far, k_far_wrap, k_left, k_left_wrap, key_rows, v_far_a, v_far_b, v_left)
     near_arrays = (*arrays, value_vectors, slash_pos)
-    near = attend_near(q, 0, rows, first_row, back, wraps, near_arrays)
+    near = attend_near(q, 0, half, first_row, back, wraps, near_arrays)
     more = [swapped(a, bits) for a, bits in zip(named, two)]
     near, more = lax.optimization_barrier((near, more))
     arrays = (*(a + b for a, b in zip(named, more)), vert_pos)
 
-    order, cores = orders
+    pass_order, keep_order, cores = orders
     meet, end = (2, 6), (6, 2)
     own_a = attend(q, *near, 0, first_row, arrays)
     q, own_a = lax.optimization_barrier((q, own_a))
     meeting = lambda parts: [over_head(parts[i], bits) for i, bits in enumerate(meet)]
     ending = lambda parts: [over_head(parts[i], bits) for i, bits in enumerate(end)]
     got_a = meeting(own_a)
+    near = attend_near(q, half, half, first_row, back, wraps, near_arrays)
     own_b = attend(q, *near, half, first_row, arrays)
     got_b = meeting(own_b)
     own_b, near_weight, far_weight = lax.optimization_barrier((own_b, near_weight, far_weight))
-    total = project_chip(own_a, own_b, out_weight, order)
+    total = project_chip(own_a, own_b, out_weight, pass_order)
     total, got_a = lax.optimization_barrier((total, got_a))
-    product = lambda got, unit, keep: project_pair(
+    product = lambda got, total, unit, keep: project_pair(
         got, near_weight, far_weight, total, unit, keep, cores
     )
-    there_a, here_a = product(got_a, 0, False)
-    there_a, here_a, got_a = lax.optimization_barrier((there_a, here_a, got_a))
-    keep_a = product(got_a, 0, True)
-    there_a, keep_a, got_b = lax.optimization_barrier((there_a, keep_a, got_b))
-    moved_a, keep_moved_a = over_head(there_a, 1), over_head(keep_a[0], 1)
-    there_b, here_b = product(got_b, 1, False)
-    there_b, here_b, moved_a, keep_moved_a, got_b = lax.optimization_barrier(
-        (there_b, here_b, moved_a, keep_moved_a, got_b)
-    )
+    there_a, here_a = product(got_a, total, 0, False)
+    own_b, there_a, here_a, got_a = lax.optimization_barrier((own_b, there_a, here_a, got_a))
+    kept_total = project_chip(own_a, own_b, out_weight, keep_order)
+    kept_total, there_a, got_b = lax.optimization_barrier((kept_total, there_a, got_b))
+    moved_a = over_head(there_a, 1)
+    there_b, here_b = product(got_b, total, 1, False)
+    there_b, here_b, moved_a, got_b = lax.optimization_barrier((there_b, here_b, moved_a, got_b))
     pass_a, pass_b = here_a + moved_a, here_b + over_head(there_b, 1)
-    pass_a, pass_b, got_b = lax.optimization_barrier((pass_a, pass_b, got_b))
+    pass_a, pass_b, got_a, got_b = lax.optimization_barrier((pass_a, pass_b, got_a, got_b))
     sent = ending(pass_a) + ending(pass_b)
-    keep_b = product(got_b, 1, True)
-    keep_b, sent = lax.optimization_barrier((keep_b, sent))
-    keep_moved_b = over_head(keep_b[0], 1)
-    kept_a, kept_b = keep_a[1] + keep_moved_a, keep_b[1] + keep_moved_b
+    keep_a = product(got_a, kept_total, 0, True)
+    keep_b = product(got_b, kept_total, 1, True)
+    keep_a, keep_b, sent = lax.optimization_barrier((keep_a, keep_b, sent))
+    kept_a, kept_b = (here + over_head(there, 1) for there, here in (keep_a, keep_b))
     kept = (kept_a[0], kept_a[1], kept_b[0], kept_b[1])
     return jnp.concatenate([a + b for a, b in zip(kept, sent)], axis=0)
 

time: 180 us -> 181 us (level)
  waiting for transfers between devices: 57.1 us -> 60.8 us
  starting transfers between devices: 48 us -> 46 us
    ppermute x19, waiting for transfers between devices: 34.7 us -> 42.2 us  [body(): send = lambda a, pairs: lax.ppermute(a, 'seq', pairs)]
    ppermute x14, waiting for transfers between devices: 22.5 us -> 18.6 us  [body(): lax.ppermute(a, 'head', [(i, i ^ bits) for i in range(head_size)])]
    ppermute x19, starting transfers between devices: 34.1 us -> 31.1 us  [body(): send = lambda a, pairs: lax.ppermute(a, 'seq', pairs)]
    pallas_call x4, Pallas kernels: 20.2 us -> 18.3 us  [project_pair(): pl.pallas_call(pair_kernel, out_shape=[out, out], grid_spec=pltpu.Prefetc...]
    pallas_call x1 -> x2, Pallas kernels: 9.64 us -> 10.9 us  [attend_near(): pl.pallas_call(functools.partial(near_kernel, start), grid=(rows // TILE,...]
    pallas_call x1 -> x2, Pallas kernels: 9.94 us -> 10.8 us  [project_chip(): pl.pallas_call(chip_kernel, out_shape=jax.ShapeDtypeStruct((2, 2 * rows,...]
    pallas_call x4 -> x2, Pallas kernels: 11.6 us -> 10.9 us  [the longest x1 9 us: take_columns(): pl.pallas_call(take_kernel, out_shape=[out, out], grid_spec=pltpu.Prefetc...]
  transfers between devices with their start and end apart: 33 -> 33, of which waited for: 15 -> 15; matrix products, arithmetic and copies ran while one was open for 3% -> 2% of each run, Pallas kernels for 36% -> 36%
where the time goes in v8:
time: 181 us; the launch traced here: 178 us
  Pallas kernels  63.7 us (35%)
  waiting for transfers between devices  60.8 us (34%)
  starting transfers between devices  46 us (25%)
  other arithmetic  4.72 us (3%)
  local copies, waits for them, and re-layouts  1.93 us (1%)
    ppermute x19, waiting for transfers between devices, body(): send = lambda a, pairs: lax.ppermute(a, 'seq', pairs)  42.2 us
    ppermute x19, starting transfers between devices, body(): send = lambda a, pairs: lax.ppermute(a, 'seq', pairs)  31.1 us
    ppermute x14, waiting for transfers between devices, body(): lax.ppermute(a, 'head', [(i, i ^ bits) for i in range(head_size)])  18.6 us
    pallas_call x4, Pallas kernels, project_pair(): pl.pallas_call(pair_kernel, out_shape=[out, out], grid_spec=pltpu.Prefetc...  18.3 us
    ppermute x14, starting transfers between devices, body(): lax.ppermute(a, 'head', [(i, i ^ bits) for i in range(head_size)])  14.8 us
    pallas_call x2, Pallas kernels, attend(): pl.pallas_call(functools.partial(attend_kernel, start), grid=(2, heads //...  12.5 us
    pallas_call x2, Pallas kernels, attend_near(): pl.pallas_call(functools.partial(near_kernel, start), grid=(rows // TILE,...  10.9 us
    pallas_call x2, Pallas kernels, project_chip(): pl.pallas_call(chip_kernel, out_shape=jax.ShapeDtypeStruct((2, 2 * rows,...  10.8 us
  transfers between devices with their start and end apart: 33, of which 15 were waited for; matrix products, arithmetic and copies ran while one was open for 2% of the time, Pallas kernels for 36%

profile of v8, /device:TPU:2, one launch (start us, length us, event | category | flops | bytes accessed | tf_op | source)
XLA Modules:
  0.0 178.3 jit_solution(10598030022681776471)
XLA Ops:
  0.0 1.5 collective-permute-start
  2.0 1.9 %collective-permute-start.2 = (f32[1024,128]{1,0:T(8,128)}, f32[1024,128]{1,0:T(8,128)S(1)}, u32[]{:S(2)}, u32[]{:S(2)}) collective-permute-start(f32[1024,128]{1,0:T(8,128)} %v_own.3), channel_id=1, source_target_pairs={{0,32},{8,40},{16,48},{24,56},{32,64},{40,72},{48,80},{56,88},{64,... | collective-permute-start | bytes 1572872 | tf_op jit(solution)/shard_map/ppermute | solution.py:382
  3.9 2.1 %collective-permute-start.3 = (f32[1024,128]{1,0:T(8,128)}, f32[1024,128]{1,0:T(8,128)S(1)}, u32[]{:S(2)}, u32[]{:S(2)}) collective-permute-start(f32[1024,128]{1,0:T(8,128)} %v_own.3), channel_id=1, source_target_pairs={{0,96},{8,104},{16,112},{24,120},{32,0},{40,8},{48,16},{56,24},{64... | collective-permute-start | bytes 1572872 | tf_op jit(solution)/shard_map/ppermute | solution.py:382
  6.6 9.0 %shard_map.79 = (f32[512,2048]{1,0:T(8,128)}, f32[512,2048]{1,0:T(8,128)}) custom-call(s32[3]{0:T(128)} %add_xor_fusion.chips, f32[512,4096]{1,0:T(8,128)} %w.3, f32[512,4096]{1,0:T(8,128)} %w.3, f32[512,4096]{1,0:T(8,128)} %w.3), custom_call_target="tpu_custom_call" | custom-call | flops 1024 | bytes 1024 | tf_op jit(solution)/shard_map/pallas_call | solution.py:266
  15.6 1.6 collective-permute-start.19
  20.2 2.3 %collective-permute-start.20 = (f32[512,2048]{1,0:T(8,128)}, f32[512,2048]{1,0:T(8,128)S(1)}, u32[]{:S(2)}, u32[]{:S(2)}) collective-permute-start(f32[512,2048]{1,0:T(8,128)} %get-tuple-element.135), channel_id=1, source_target_pairs={{0,6},{1,7},{2,4},{3,5},{4,2},{5,3},{6,0},{7,1},{8,14},{9,15},{10,... | collective-permute-start | bytes 12582920 | tf_op jit(solution)/shard_map/ppermute | solution.py:391
  22.5 2.1 %collective-permute-start.5 = (f32[1024,128]{1,0:T(8,128)S(1)}, f32[1024,128]{1,0:T(8,128)S(1)}, u32[]{:S(2)}, u32[]{:S(2)}) collective-permute-start(f32[1024,128]{1,0:T(8,128)S(1)} %collective-permute-done.3.refs_5_), channel_id=1, source_target_pairs={{0,96},{8,104},{16,112},{24,120},{32,0},{40,8},{48,16},{56,24},{64... | collective-permute-start | bytes 1572872 | tf_op jit(solution)/shard_map/ppermute | solution.py:382
  24.8 1.6 collective-permute-start.6
  27.0 7.8 %collective-permute-done.5.refs_6_ = f32[1024,128]{1,0:T(8,128)S(1)} collective-permute-done((f32[1024,128]{1,0:T(8,128)S(1)}, f32[1024,128]{1,0:T(8,128)S(1)}, u32[]{:S(2)}, u32[]{:S(2)}) %collective-permute-start.5) | collective-permute-done | bytes 524320 | tf_op jit(solution)/shard_map/ppermute | solution.py:382
  34.8 0.7 collective-permute-start.7
  35.5 6.6 %collective-permute-done.6 = f32[1536,128]{1,0:T(8,128)S(1)} collective-permute-done((f32[1536,128]{1,0:T(8,128)S(1)}, f32[1536,128]{1,0:T(8,128)S(1)}, u32[]{:S(2)}, u32[]{:S(2)}) %collective-permute-start.6) | collective-permute-done | bytes 786464 | tf_op jit(solution)/shard_map/ppermute | solution.py:382
  42.2 1.3 collective-permute-done.4
  43.6 1.3 collective-permute-start.8
  44.9 1.9 %shard_map.74 = (f32[1024,128]{1,0:T(8,128)S(1)}, f32[1024,128]{1,0:T(8,128)S(1)}, f32[1024,128]{1,0:T(8,128)S(1)}, f32[1024,128]{1,0:T(8,128)S(1)}) custom-call(s32[32]{0:T(128)S(1)} %get-tuple-element.101.k_place, s32[32]{0:T(128)S(1)} %compare_convert_fusion.1.k_held, s32[32]{0:T(128)S(1)} %get-tuple-element.103.v_place, ...), custom_call_target="tpu_custom_call" | custom-call | flops 1024 | bytes 1024 | tf_op jit(solution)/shard_map/pallas_call | solution.py:48
  47.6 4.1 %collective-permute-done.8.v_far_a = f32[512,128]{1,0:T(8,128)S(1)} collective-permute-done((f32[512,128]{1,0:T(8,128)S(1)}, f32[512,128]{1,0:T(8,128)S(1)}, u32[]{:S(2)}, u32[]{:S(2)}) %collective-permute-start.8) | collective-permute-done | bytes 262176 | tf_op jit(solution)/shard_map/ppermute | solution.py:382
  51.6 3.2 %collective-permute-start.9 = (f32[512,128]{1,0:T(8,128)S(1)}, f32[512,128]{1,0:T(8,128)S(1)}, u32[]{:S(2)}, u32[]{:S(2)}) collective-permute-start(f32[512,128]{1,0:T(8,128)S(1)} %slice.57), channel_id=1, source_target_pairs={{0,24},{8,0},{16,8},{24,16},{32,56},{40,32},{48,40},{56,48},{64,88... | collective-permute-start | bytes 786440 | tf_op jit(solution)/shard_map/ppermute | solution.py:382
  54.9 3.9 %collective-permute-done.9.v_far_b = f32[512,128]{1,0:T(8,128)S(1)} collective-permute-done((f32[512,128]{1,0:T(8,128)S(1)}, f32[512,128]{1,0:T(8,128)S(1)}, u32[]{:S(2)}, u32[]{:S(2)}) %collective-permute-start.9) | collective-permute-done | bytes 262176 | tf_op jit(solution)/shard_map/ppermute | solution.py:382
  58.8 4.4 %collective-permute-start.10 = (f32[1024,128]{1,0:T(8,128)S(1)}, f32[1024,128]{1,0:T(8,128)S(1)}, u32[]{:S(2)}, u32[]{:S(2)}) collective-permute-start(f32[1024,128]{1,0:T(8,128)S(1)} %slice.58.refs_2_.k_far), channel_id=1, source_target_pairs={{0,32},{8,40},{32,64},{40,72},{64,96},{72,104},{1,33},{9,41},{33,6... | collective-permute-start | bytes 1572872 | tf_op jit(solution)/shard_map/ppermute | solution.py:382
  63.2 2.6 %collective-permute-start.13 = (f32[1024,128]{1,0:T(8,128)S(1)}, f32[1024,128]{1,0:T(8,128)S(1)}, u32[]{:S(2)}, u32[]{:S(2)}) collective-permute-start(f32[1024,128]{1,0:T(8,128)S(1)} %get-tuple-element.108), channel_id=1, source_target_pairs={{0,8},{8,0},{16,24},{24,16},{32,40},{40,32},{48,56},{56,48},{64,72... | collective-permute-start | bytes 1572872 | tf_op jit(solution)/shard_map/ppermute | solution.py:382
  66.3 8.2 %collective-permute-done.13 = f32[1024,128]{1,0:T(8,128)S(1)} collective-permute-done((f32[1024,128]{1,0:T(8,128)S(1)}, f32[1024,128]{1,0:T(8,128)S(1)}, u32[]{:S(2)}, u32[]{:S(2)}) %collective-permute-start.13) | collective-permute-done | bytes 524320 | tf_op jit(solution)/shard_map/ppermute | solution.py:382
  74.5 2.6 %collective-permute-done.14 = f32[1024,128]{1,0:T(8,128)S(1)} collective-permute-done((f32[1024,128]{1,0:T(8,128)S(1)}, f32[1024,128]{1,0:T(8,128)S(1)}, u32[]{:S(2)}, u32[]{:S(2)}) %collective-permute-start.14) | collective-permute-done | bytes 524320 | tf_op jit(solution)/shard_map/ppermute | solution.py:382
  77.2 0.9 collective-permute-start.18
  78.5 2.0 %collective-permute-start.16 = (f32[1024,128]{1,0:T(8,128)S(1)}, f32[1024,128]{1,0:T(8,128)S(1)}, u32[]{:S(2)}, u32[]{:S(2)}) collective-permute-start(f32[1024,128]{1,0:T(8,128)S(1)} %add.208), channel_id=1, source_target_pairs={{0,32},{8,40},{16,48},{24,56},{32,0},{40,8},{48,16},{56,24},{64,96... | collective-permute-start | bytes 1572872 | tf_op jit(solution)/shard_map/ppermute | solution.py:382
  80.5 5.9 %collective-permute-done.18 = f32[1024,128]{1,0:T(8,128)S(1)} collective-permute-done((f32[1024,128]{1,0:T(8,128)S(1)}, f32[1024,128]{1,0:T(8,128)S(1)}, u32[]{:S(2)}, u32[]{:S(2)}) %collective-permute-start.18) | collective-permute-done | bytes 524320 | tf_op jit(solution)/shard_map/ppermute | solution.py:382
  86.4 4.4 %collective-permute-start.15 = (f32[1024,128]{1,0:T(8,128)S(1)}, f32[1024,128]{1,0:T(8,128)S(1)}, u32[]{:S(2)}, u32[]{:S(2)}) collective-permute-start(f32[1024,128]{1,0:T(8,128)S(1)} %add.207), channel_id=1, source_target_pairs={{0,96},{8,104},{16,112},{24,120},{32,64},{40,72},{48,80},{56,88},{... | collective-permute-start | bytes 1572872 | tf_op jit(solution)/shard_map/ppermute | solution.py:382
  90.9 5.5 %shard_map.75 = (f32[512,512]{1,0:T(8,128)S(1)}, f32[512,256]{1,0:T(8,128)S(1)}) custom-call(s32[1]{0:T(128)} %bitcast.1.first_row, s32[4,4]{1,0:T(4,128)S(1)} %get-tuple-element.111.back, s32[2]{0:T(128)S(1)} %add_convert_fusion.wraps, f32[1024,512]{1,0:T(8,128)S(1)} %shard_map.73.q, f32[1024,128]{1,0:T(8,128)S(1)} %slice.58.refs_2_.k_far, ...), custom_call_target="tpu_custom_call" | custom-call | flops 100000 | bytes 1024 | tf_op jit(solution)/shard_map/pallas_call | solution.py:179
  96.4 1.6 collective-permute-done.15
  98.3 6.3 %shard_map.76.own_a = f32[2,256,512]{2,1,0:T(8,128)S(1)} custom-call(s32[1]{0:T(128)} %bitcast.1.first_row, f32[1024,512]{1,0:T(8,128)S(1)} %shard_map.73.q, f32[512,512]{1,0:T(8,128)S(1)} %get-tuple-element.124.near, f32[512,256]{1,0:T(8,128)S(1)} %get-tuple-element.125.stats, f32[1024,128]{1,0:T(8,128)S(1)} %add.211.k_a, f32[1024,128]{1,0:T(8,128)S(1)} %add.212.k_b, ...), custom_call_target="tpu_custom_call" | custom-call | flops 100000 | bytes 1024 | tf_op jit(solution)/shard_map/pallas_call | solution.py:236
  104.5 5.5 %shard_map.77 = (f32[512,512]{1,0:T(8,128)S(1)}, f32[512,256]{1,0:T(8,128)S(1)}) custom-call(s32[1]{0:T(128)} %bitcast.1.first_row, s32[4,4]{1,0:T(4,128)S(1)} %get-tuple-element.111.back, s32[2]{0:T(128)S(1)} %add_convert_fusion.wraps, f32[1024,512]{1,0:T(8,128)S(1)} %shard_map.73.q, f32[1024,128]{1,0:T(8,128)S(1)} %slice.58.refs_2_.k_far, ...), custom_call_target="tpu_custom_call" | custom-call | flops 100000 | bytes 1024 | tf_op jit(solution)/shard_map/pallas_call | solution.py:179
  110.1 1.4 collective-permute-start.21
  112.1 6.3 %shard_map.78.own_b = f32[2,256,512]{2,1,0:T(8,128)S(1)} custom-call(s32[1]{0:T(128)} %bitcast.1.first_row, f32[1024,512]{1,0:T(8,128)S(1)} %shard_map.73.q, f32[512,512]{1,0:T(8,128)S(1)} %get-tuple-element.132.near, f32[512,256]{1,0:T(8,128)S(1)} %get-tuple-element.133.stats, f32[1024,128]{1,0:T(8,128)S(1)} %add.211.k_a, f32[1024,128]{1,0:T(8,128)S(1)} %add.212.k_b, ...), custom_call_target="tpu_custom_call" | custom-call | flops 100000 | bytes 1024 | tf_op jit(solution)/shard_map/pallas_call | solution.py:236
  118.4 0.7 collective-permute-start.23
  119.1 2.4 %collective-permute-start.24 = (f32[256,512]{1,0:T(8,128)S(1)}, f32[256,512]{1,0:T(8,128)S(1)}, u32[]{:S(2)}, u32[]{:S(2)}) collective-permute-start(f32[256,512]{1,0:T(8,128)S(1)} %get-tuple-element.199), channel_id=1, source_target_pairs={{0,6},{1,7},{2,4},{3,5},{4,2},{5,3},{6,0},{7,1},{8,14},{9,15},{10,... | collective-permute-start | bytes 1572872 | tf_op jit(solution)/shard_map/ppermute | solution.py:391
  121.5 5.4 %shard_map.80.total = f32[2,512,1024]{2,1,0:T(8,128)S(1)} custom-call(s32[4]{0:T(128)S(1)} %get-tuple-element.137.order, f32[2,256,512]{2,1,0:T(8,128)S(1)} %shard_map.76.own_a, f32[2,256,512]{2,1,0:T(8,128)S(1)} %shard_map.78.own_b, f32[512,4096]{1,0:T(8,128)S(1)} %bitcast.41), custom_call_target="tpu_custom_call" | custom-call | flops 100000 | bytes 1024 | tf_op jit(solution)/shard_map/pallas_call | solution.py:303
  127.6 4.6 %shard_map.81 = (f32[2,256,512]{2,1,0:T(8,128)S(1)}, f32[2,256,512]{2,1,0:T(8,128)S(1)}) custom-call(s32[2]{0:T(128)S(1)} %get-tuple-element.93.cores, f32[256,512]{1,0:T(8,128)S(1)} %collective-permute-done.21.got_a, f32[256,512]{1,0:T(8,128)S(1)} %collective-permute-done.22.got_b, f32[512,2048]{1,0:T(8,128)} %collective-permute-done.19.near, ...), custom_call_target="tpu_custom_call" | custom-call | flops 100000 | bytes 1024 | tf_op jit(solution)/shard_map/pallas_call | solution.py:342
  132.1 5.4 %shard_map.82.total = f32[2,512,1024]{2,1,0:T(8,128)S(1)} custom-call(s32[4]{0:T(128)S(1)} %get-tuple-element.147.order, f32[2,256,512]{2,1,0:T(8,128)S(1)} %shard_map.76.own_a, f32[2,256,512]{2,1,0:T(8,128)S(1)} %shard_map.78.own_b, f32[512,4096]{1,0:T(8,128)S(1)} %bitcast.41), custom_call_target="tpu_custom_call" | custom-call | flops 100000 | bytes 1024 | tf_op jit(solution)/shard_map/pallas_call | solution.py:303
  137.7 4.6 %shard_map.83 = (f32[2,256,512]{2,1,0:T(8,128)S(1)}, f32[2,256,512]{2,1,0:T(8,128)S(1)}) custom-call(s32[2]{0:T(128)S(1)} %get-tuple-element.93.cores, f32[256,512]{1,0:T(8,128)S(1)} %collective-permute-done.23.got_a, f32[256,512]{1,0:T(8,128)S(1)} %collective-permute-done.24.got_b, f32[512,2048]{1,0:T(8,128)} %collective-permute-done.19.near, ...), custom_call_target="tpu_custom_call" | custom-call | flops 100000 | bytes 1024 | tf_op jit(solution)/shard_map/pallas_call | solution.py:342
  143.1 2.1 %collective-permute-done.26 = f32[2,256,512]{2,1,0:T(8,128)S(1)} collective-permute-done((f32[2,256,512]{2,1,0:T(8,128)S(1)}, f32[2,256,512]{2,1,0:T(8,128)S(1)}, u32[]{:S(2)}, u32[]{:S(2)}) %collective-permute-start.26) | collective-permute-done | bytes 1048608 | tf_op jit(solution)/shard_map/ppermute | solution.py:391
  145.4 1.2 collective-permute-start.27
  146.7 2.2 %collective-permute-start.29 = (f32[256,512]{1,0:T(8,128)S(1)}, f32[256,512]{1,0:T(8,128)S(1)}, u32[]{:S(2)}, u32[]{:S(2)}) collective-permute-start(f32[256,512]{1,0:T(8,128)S(1)} %get-tuple-element.196), channel_id=1, source_target_pairs={{0,6},{1,7},{2,4},{3,5},{4,2},{5,3},{6,0},{7,1},{8,14},{9,15},{10,... | collective-permute-start | bytes 1572872 | tf_op jit(solution)/shard_map/ppermute | solution.py:391
  148.9 1.4 collective-permute-start.30
  150.3 4.6 %shard_map.85 = (f32[2,256,512]{2,1,0:T(8,128)S(1)}, f32[2,256,512]{2,1,0:T(8,128)S(1)}) custom-call(s32[2]{0:T(128)S(1)} %get-tuple-element.93.cores, f32[256,512]{1,0:T(8,128)S(1)} %collective-permute-done.23.got_a, f32[256,512]{1,0:T(8,128)S(1)} %collective-permute-done.24.got_b, f32[512,2048]{1,0:T(8,128)} %collective-permute-done.19.near, ...), custom_call_target="tpu_custom_call" | custom-call | flops 100000 | bytes 1024 | tf_op jit(solution)/shard_map/pallas_call | solution.py:342
  154.9 4.6 %shard_map.84 = (f32[2,256,512]{2,1,0:T(8,128)S(1)}, f32[2,256,512]{2,1,0:T(8,128)S(1)}) custom-call(s32[2]{0:T(128)S(1)} %get-tuple-element.93.cores, f32[256,512]{1,0:T(8,128)S(1)} %collective-permute-done.21.got_a, f32[256,512]{1,0:T(8,128)S(1)} %collective-permute-done.22.got_b, f32[512,2048]{1,0:T(8,128)} %collective-permute-done.19.near, ...), custom_call_target="tpu_custom_call" | custom-call | flops 100000 | bytes 1024 | tf_op jit(solution)/shard_map/pallas_call | solution.py:342
  159.5 2.0 %collective-permute-done.27 = f32[256,512]{1,0:T(8,128)S(1)} collective-permute-done((f32[256,512]{1,0:T(8,128)S(1)}, f32[256,512]{1,0:T(8,128)S(1)}, u32[]{:S(2)}, u32[]{:S(2)}) %collective-permute-start.27) | collective-permute-done | bytes 524320 | tf_op jit(solution)/shard_map/ppermute | solution.py:391
  161.5 10.7 %collective-permute-done.29 = f32[256,512]{1,0:T(8,128)S(1)} collective-permute-done((f32[256,512]{1,0:T(8,128)S(1)}, f32[256,512]{1,0:T(8,128)S(1)}, u32[]{:S(2)}, u32[]{:S(2)}) %collective-permute-start.29) | collective-permute-done | bytes 524320 | tf_op jit(solution)/shard_map/ppermute | solution.py:391
  172.7 2.1 %collective-permute-done.31 = f32[2,256,512]{2,1,0:T(8,128)S(1)} collective-permute-done((f32[2,256,512]{2,1,0:T(8,128)S(1)}, f32[2,256,512]{2,1,0:T(8,128)S(1)}, u32[]{:S(2)}, u32[]{:S(2)}) %collective-permute-start.31) | collective-permute-done | bytes 1048608 | tf_op jit(solution)/shard_map/ppermute | solution.py:391
  175.3 1.1 collective-permute-done.32
  176.8 1.5 pad_maximum_fusion
  (109 shorter events, 10.3 us)
Async XLA Ops:
  0.0 17.5 %copy-start = (s32[32,3]{0,1:T(4,128)S(1)}, s32[32,3]{0,1:T(4,128)}, u32[]{:S(2)}) copy-start(s32[32,3]{0,1:T(4,128)} %param.11) | copy-start | bytes 1156
  0.0 20.2 %collective-permute-start = (f32[1024,128]{1,0:T(8,128)}, f32[1024,128]{1,0:T(8,128)S(1)}, u32[]{:S(2)}, u32[]{:S(2)}) collective-permute-start(f32[1024,128]{1,0:T(8,128)} %k_own.3), channel_id=1, source_target_pairs={{0,8},{8,16},{16,24},{24,0},{32,40},{40,48},{48,56},{56,32},{64,72... | collective-permute-start | bytes 1572872 | tf_op jit(solution)/shard_map/ppermute | solution.py:382
  1.5 21.0 %collective-permute-start.1 = (f32[1024,128]{1,0:T(8,128)}, f32[1024,128]{1,0:T(8,128)S(1)}, u32[]{:S(2)}, u32[]{:S(2)}) collective-permute-start(f32[1024,128]{1,0:T(8,128)} %k_own.3), channel_id=1, source_target_pairs={{0,24},{8,0},{16,8},{24,16},{32,56},{40,32},{48,40},{56,48},{64,88... | collective-permute-start | bytes 1572872 | tf_op jit(solution)/shard_map/ppermute | solution.py:382
  2.0 20.5 %collective-permute-start.2 = (f32[1024,128]{1,0:T(8,128)}, f32[1024,128]{1,0:T(8,128)S(1)}, u32[]{:S(2)}, u32[]{:S(2)}) collective-permute-start(f32[1024,128]{1,0:T(8,128)} %v_own.3), channel_id=1, source_target_pairs={{0,32},{8,40},{16,48},{24,56},{32,64},{40,72},{48,80},{56,88},{64,... | collective-permute-start | bytes 1572872 | tf_op jit(solution)/shard_map/ppermute | solution.py:382
  3.9 18.6 %collective-permute-start.3 = (f32[1024,128]{1,0:T(8,128)}, f32[1024,128]{1,0:T(8,128)S(1)}, u32[]{:S(2)}, u32[]{:S(2)}) collective-permute-start(f32[1024,128]{1,0:T(8,128)} %v_own.3), channel_id=1, source_target_pairs={{0,96},{8,104},{16,112},{24,120},{32,0},{40,8},{48,16},{56,24},{64... | collective-permute-start | bytes 1572872 | tf_op jit(solution)/shard_map/ppermute | solution.py:382
  6.6 10.6 %copy-start.5 = (s32[32,8]{0,1:T(8,128)S(1)}, s32[32,8]{0,1:T(8,128)}, u32[]{:S(2)}) copy-start(s32[32,8]{0,1:T(8,128)} %param.10) | copy-start | bytes 3076
  6.6 18.0 %copy-start.2 = (f32[1024,128]{1,0:T(8,128)S(1)}, f32[1024,128]{1,0:T(8,128)}, u32[]{:S(2)}) copy-start(f32[1024,128]{1,0:T(8,128)} %v_own.3) | copy-start | bytes 1572868
  15.6 103.5 %collective-permute-start.19 = (f32[512,2048]{1,0:T(8,128)}, f32[512,2048]{1,0:T(8,128)}, u32[]{:S(2)}, u32[]{:S(2)}) collective-permute-start(f32[512,2048]{1,0:T(8,128)} %get-tuple-element.134), channel_id=1, source_target_pairs={{0,2},{1,3},{2,0},{3,1},{4,6},{5,7},{6,4},{7,5},{8,10},{9,11},{10,... | collective-permute-start | bytes 12582920 | tf_op jit(solution)/shard_map/ppermute | solution.py:391
  20.2 101.3 %collective-permute-start.20 = (f32[512,2048]{1,0:T(8,128)}, f32[512,2048]{1,0:T(8,128)S(1)}, u32[]{:S(2)}, u32[]{:S(2)}) collective-permute-start(f32[512,2048]{1,0:T(8,128)} %get-tuple-element.135), channel_id=1, source_target_pairs={{0,6},{1,7},{2,4},{3,5},{4,2},{5,3},{6,0},{7,1},{8,14},{9,15},{10,... | collective-permute-start | bytes 12582920 | tf_op jit(solution)/shard_map/ppermute | solution.py:391
  22.5 12.3 %collective-permute-start.5 = (f32[1024,128]{1,0:T(8,128)S(1)}, f32[1024,128]{1,0:T(8,128)S(1)}, u32[]{:S(2)}, u32[]{:S(2)}) collective-permute-start(f32[1024,128]{1,0:T(8,128)S(1)} %collective-permute-done.3.refs_5_), channel_id=1, source_target_pairs={{0,96},{8,104},{16,112},{24,120},{32,0},{40,8},{48,16},{56,24},{64... | collective-permute-start | bytes 1572872 | tf_op jit(solution)/shard_map/ppermute | solution.py:382
  24.7 20.1 %copy-start.3 = (f32[1024,128]{1,0:T(8,128)S(1)}, f32[1024,128]{1,0:T(8,128)}, u32[]{:S(2)}) copy-start(f32[1024,128]{1,0:T(8,128)} %k_own.3) | copy-start | bytes 1572868
  24.8 17.4 %collective-permute-start.6 = (f32[1536,128]{1,0:T(8,128)S(1)}, f32[1536,128]{1,0:T(8,128)S(1)}, u32[]{:S(2)}, u32[]{:S(2)}) collective-permute-start(f32[1536,128]{1,0:T(8,128)S(1)} %pad_maximum_fusion.2), channel_id=1, source_target_pairs={{0,8},{8,16},{16,24},{24,0},{32,40},{40,48},{48,56},{56,32},{64,72... | collective-permute-start | bytes 2359304 | tf_op jit(solution)/shard_map/ppermute | solution.py:382
  26.4 17.1 %collective-permute-start.4 = (f32[1536,128]{1,0:T(8,128)S(1)}, f32[1536,128]{1,0:T(8,128)S(1)}, u32[]{:S(2)}, u32[]{:S(2)}) collective-permute-start(f32[1536,128]{1,0:T(8,128)S(1)} %pad_maximum_fusion.1), channel_id=1, source_target_pairs={{0,24},{8,0},{16,8},{24,16},{32,56},{40,32},{48,40},{56,48},{64,88... | collective-permute-start | bytes 2359304 | tf_op jit(solution)/shard_map/ppermute | solution.py:382
  34.8 0.7 collective-permute-start.7
  43.6 22.5 %copy-start.4 = (f32[1024,512]{1,0:T(8,128)S(1)}, f32[1024,512]{1,0:T(8,128)}, u32[]{:S(2)}) copy-start(f32[1024,512]{1,0:T(8,128)} %q.1) | copy-start | bytes 6291460
  43.6 8.0 %collective-permute-start.8 = (f32[512,128]{1,0:T(8,128)S(1)}, f32[512,128]{1,0:T(8,128)S(1)}, u32[]{:S(2)}, u32[]{:S(2)}) collective-permute-start(f32[512,128]{1,0:T(8,128)S(1)} %slice.56), channel_id=1, source_target_pairs={{0,8},{8,16},{16,24},{24,0},{32,40},{40,48},{48,56},{56,32},{64,72... | collective-permute-start | bytes 786440 | tf_op jit(solution)/shard_map/ppermute | solution.py:382
  46.7 16.4 %collective-permute-start.11 = (f32[1024,128]{1,0:T(8,128)S(1)}, f32[1024,128]{1,0:T(8,128)S(1)}, u32[]{:S(2)}, u32[]{:S(2)}) collective-permute-start(f32[1024,128]{1,0:T(8,128)S(1)} %get-tuple-element.106), channel_id=1, source_target_pairs={{0,32},{8,40},{16,48},{24,56},{32,0},{40,8},{48,16},{56,24},{64,96... | collective-permute-start | bytes 1572872 | tf_op jit(solution)/shard_map/ppermute | solution.py:382
  47.1 18.7 %collective-permute-start.12 = (f32[1024,128]{1,0:T(8,128)S(1)}, f32[1024,128]{1,0:T(8,128)S(1)}, u32[]{:S(2)}, u32[]{:S(2)}) collective-permute-start(f32[1024,128]{1,0:T(8,128)S(1)} %get-tuple-element.107), channel_id=1, source_target_pairs={{0,96},{8,104},{16,112},{24,120},{32,64},{40,72},{48,80},{56,88},{... | collective-permute-start | bytes 1572872 | tf_op jit(solution)/shard_map/ppermute | solution.py:382
  51.6 7.1 %collective-permute-start.9 = (f32[512,128]{1,0:T(8,128)S(1)}, f32[512,128]{1,0:T(8,128)S(1)}, u32[]{:S(2)}, u32[]{:S(2)}) collective-permute-start(f32[512,128]{1,0:T(8,128)S(1)} %slice.57), channel_id=1, source_target_pairs={{0,24},{8,0},{16,8},{24,16},{32,56},{40,32},{48,40},{56,48},{64,88... | collective-permute-start | bytes 786440 | tf_op jit(solution)/shard_map/ppermute | solution.py:382
  58.8 18.4 %collective-permute-start.10 = (f32[1024,128]{1,0:T(8,128)S(1)}, f32[1024,128]{1,0:T(8,128)S(1)}, u32[]{:S(2)}, u32[]{:S(2)}) collective-permute-start(f32[1024,128]{1,0:T(8,128)S(1)} %slice.58.refs_2_.k_far), channel_id=1, source_target_pairs={{0,32},{8,40},{32,64},{40,72},{64,96},{72,104},{1,33},{9,41},{33,6... | collective-permute-start | bytes 1572872 | tf_op jit(solution)/shard_map/ppermute | solution.py:382
  63.2 11.3 %collective-permute-start.13 = (f32[1024,128]{1,0:T(8,128)S(1)}, f32[1024,128]{1,0:T(8,128)S(1)}, u32[]{:S(2)}, u32[]{:S(2)}) collective-permute-start(f32[1024,128]{1,0:T(8,128)S(1)} %get-tuple-element.108), channel_id=1, source_target_pairs={{0,8},{8,0},{16,24},{24,16},{32,40},{40,32},{48,56},{56,48},{64,72... | collective-permute-start | bytes 1572872 | tf_op jit(solution)/shard_map/ppermute | solution.py:382
  65.8 11.3 %collective-permute-start.14 = (f32[1024,128]{1,0:T(8,128)S(1)}, f32[1024,128]{1,0:T(8,128)S(1)}, u32[]{:S(2)}, u32[]{:S(2)}) collective-permute-start(f32[1024,128]{1,0:T(8,128)S(1)} %get-tuple-element.109), channel_id=1, source_target_pairs={{0,24},{8,16},{16,8},{24,0},{32,56},{40,48},{48,40},{56,32},{64,88... | collective-permute-start | bytes 1572872 | tf_op jit(solution)/shard_map/ppermute | solution.py:382
  77.2 9.3 %collective-permute-start.18 = (f32[1024,128]{1,0:T(8,128)S(1)}, f32[1024,128]{1,0:T(8,128)S(1)}, u32[]{:S(2)}, u32[]{:S(2)}) collective-permute-start(f32[1024,128]{1,0:T(8,128)S(1)} %add.210), channel_id=1, source_target_pairs={{0,8},{8,0},{16,24},{24,16},{32,40},{40,32},{48,56},{56,48},{64,72... | collective-permute-start | bytes 1572872 | tf_op jit(solution)/shard_map/ppermute | solution.py:382
  78.2 18.2 %collective-permute-start.17 = (f32[1024,128]{1,0:T(8,128)S(1)}, f32[1024,128]{1,0:T(8,128)S(1)}, u32[]{:S(2)}, u32[]{:S(2)}) collective-permute-start(f32[1024,128]{1,0:T(8,128)S(1)} %add.209), channel_id=1, source_target_pairs={{0,24},{8,16},{16,8},{24,0},{32,56},{40,48},{48,40},{56,32},{64,88... | collective-permute-start | bytes 1572872 | tf_op jit(solution)/shard_map/ppermute | solution.py:382
  78.5 17.8 %collective-permute-start.16 = (f32[1024,128]{1,0:T(8,128)S(1)}, f32[1024,128]{1,0:T(8,128)S(1)}, u32[]{:S(2)}, u32[]{:S(2)}) collective-permute-start(f32[1024,128]{1,0:T(8,128)S(1)} %add.208), channel_id=1, source_target_pairs={{0,32},{8,40},{16,48},{24,56},{32,0},{40,8},{48,16},{56,24},{64,96... | collective-permute-start | bytes 1572872 | tf_op jit(solution)/shard_map/ppermute | solution.py:382
  86.4 11.6 %collective-permute-start.15 = (f32[1024,128]{1,0:T(8,128)S(1)}, f32[1024,128]{1,0:T(8,128)S(1)}, u32[]{:S(2)}, u32[]{:S(2)}) collective-permute-start(f32[1024,128]{1,0:T(8,128)S(1)} %add.207), channel_id=1, source_target_pairs={{0,96},{8,104},{16,112},{24,120},{32,64},{40,72},{48,80},{56,88},{... | collective-permute-start | bytes 1572872 | tf_op jit(solution)/shard_map/ppermute | solution.py:382
  104.5 17.0 %slice-start = ((s8[8388608]{0:T(1024)(128)(4,1)}), s8[4194304]{0:T(1024)(128)(4,1)S(1)}, s32[]{:S(2)}) async-start(s8[8388608]{0:T(1024)(128)(4,1)} %bitcast.40), calls=%async_computation | async-start | bytes 8388608
  110.1 16.8 %collective-permute-start.21 = (f32[256,512]{1,0:T(8,128)S(1)}, f32[256,512]{1,0:T(8,128)S(1)}, u32[]{:S(2)}, u32[]{:S(2)}) collective-permute-start(f32[256,512]{1,0:T(8,128)S(1)} %get-tuple-element.202), channel_id=1, source_target_pairs={{0,2},{1,3},{2,0},{3,1},{4,6},{5,7},{6,4},{7,5},{8,10},{9,11},{10,... | collective-permute-start | bytes 1572872 | tf_op jit(solution)/shard_map/ppermute | solution.py:391
  111.5 16.1 %collective-permute-start.22 = (f32[256,512]{1,0:T(8,128)S(1)}, f32[256,512]{1,0:T(8,128)S(1)}, u32[]{:S(2)}, u32[]{:S(2)}) collective-permute-start(f32[256,512]{1,0:T(8,128)S(1)} %get-tuple-element.201), channel_id=1, source_target_pairs={{0,6},{1,7},{2,4},{3,5},{4,2},{5,3},{6,0},{7,1},{8,14},{9,15},{10,... | collective-permute-start | bytes 1572872 | tf_op jit(solution)/shard_map/ppermute | solution.py:391
  112.1 9.4 %slice-start.1 = ((s8[8388608]{0:T(1024)(128)(4,1)}), s8[4194304]{0:T(1024)(128)(4,1)S(1)}, s32[]{:S(2)}) async-start(s8[8388608]{0:T(1024)(128)(4,1)} %bitcast.40), calls=%async_computation.1 | async-start | bytes 8388608
  118.4 19.1 %collective-permute-start.23 = (f32[256,512]{1,0:T(8,128)S(1)}, f32[256,512]{1,0:T(8,128)S(1)}, u32[]{:S(2)}, u32[]{:S(2)}) collective-permute-start(f32[256,512]{1,0:T(8,128)S(1)} %get-tuple-element.200), channel_id=1, source_target_pairs={{0,2},{1,3},{2,0},{3,1},{4,6},{5,7},{6,4},{7,5},{8,10},{9,11},{10,... | collective-permute-start | bytes 1572872 | tf_op jit(solution)/shard_map/ppermute | solution.py:391
  119.1 18.5 %collective-permute-start.24 = (f32[256,512]{1,0:T(8,128)S(1)}, f32[256,512]{1,0:T(8,128)S(1)}, u32[]{:S(2)}, u32[]{:S(2)}) collective-permute-start(f32[256,512]{1,0:T(8,128)S(1)} %get-tuple-element.199), channel_id=1, source_target_pairs={{0,6},{1,7},{2,4},{3,5},{4,2},{5,3},{6,0},{7,1},{8,14},{9,15},{10,... | collective-permute-start | bytes 1572872 | tf_op jit(solution)/shard_map/ppermute | solution.py:391
  137.6 4.7 %collective-permute-start.25 = (f32[2,256,512]{2,1,0:T(8,128)S(1)}, f32[2,256,512]{2,1,0:T(8,128)S(1)}, u32[]{:S(2)}, u32[]{:S(2)}) collective-permute-start(f32[2,256,512]{2,1,0:T(8,128)S(1)} %get-tuple-element.154), channel_id=1, source_target_pairs={{0,1},{1,0},{2,3},{3,2},{4,5},{5,4},{6,7},{7,6},{8,9},{9,8},{10,11... | collective-permute-start | bytes 3145736 | tf_op jit(solution)/shard_map/ppermute | solution.py:391
  142.3 2.9 %collective-permute-start.26 = (f32[2,256,512]{2,1,0:T(8,128)S(1)}, f32[2,256,512]{2,1,0:T(8,128)S(1)}, u32[]{:S(2)}, u32[]{:S(2)}) collective-permute-start(f32[2,256,512]{2,1,0:T(8,128)S(1)} %get-tuple-element.157), channel_id=1, source_target_pairs={{0,1},{1,0},{2,3},{3,2},{4,5},{5,4},{6,7},{7,6},{8,9},{9,8},{10,11... | collective-permute-start | bytes 3145736 | tf_op jit(solution)/shard_map/ppermute | solution.py:391
  145.4 16.0 %collective-permute-start.27 = (f32[256,512]{1,0:T(8,128)S(1)}, f32[256,512]{1,0:T(8,128)S(1)}, u32[]{:S(2)}, u32[]{:S(2)}) collective-permute-start(f32[256,512]{1,0:T(8,128)S(1)} %get-tuple-element.198), channel_id=1, source_target_pairs={{0,6},{1,7},{2,4},{3,5},{4,2},{5,3},{6,0},{7,1},{8,14},{9,15},{10,... | collective-permute-start | bytes 1572872 | tf_op jit(solution)/shard_map/ppermute | solution.py:391
  146.6 14.9 %collective-permute-start.28 = (f32[256,512]{1,0:T(8,128)S(1)}, f32[256,512]{1,0:T(8,128)S(1)}, u32[]{:S(2)}, u32[]{:S(2)}) collective-permute-start(f32[256,512]{1,0:T(8,128)S(1)} %get-tuple-element.197), channel_id=1, source_target_pairs={{0,2},{1,3},{2,0},{3,1},{4,6},{5,7},{6,4},{7,5},{8,10},{9,11},{10,... | collective-permute-start | bytes 1572872 | tf_op jit(solution)/shard_map/ppermute | solution.py:391
  146.7 25.5 %collective-permute-start.29 = (f32[256,512]{1,0:T(8,128)S(1)}, f32[256,512]{1,0:T(8,128)S(1)}, u32[]{:S(2)}, u32[]{:S(2)}) collective-permute-start(f32[256,512]{1,0:T(8,128)S(1)} %get-tuple-element.196), channel_id=1, source_target_pairs={{0,6},{1,7},{2,4},{3,5},{4,2},{5,3},{6,0},{7,1},{8,14},{9,15},{10,... | collective-permute-start | bytes 1572872 | tf_op jit(solution)/shard_map/ppermute | solution.py:391
  148.9 23.2 %collective-permute-start.30 = (f32[256,512]{1,0:T(8,128)S(1)}, f32[256,512]{1,0:T(8,128)S(1)}, u32[]{:S(2)}, u32[]{:S(2)}) collective-permute-start(f32[256,512]{1,0:T(8,128)S(1)} %get-tuple-element.195), channel_id=1, source_target_pairs={{0,2},{1,3},{2,0},{3,1},{4,6},{5,7},{6,4},{7,5},{8,10},{9,11},{10,... | collective-permute-start | bytes 1572872 | tf_op jit(solution)/shard_map/ppermute | solution.py:391
  172.2 2.7 %collective-permute-start.31 = (f32[2,256,512]{2,1,0:T(8,128)S(1)}, f32[2,256,512]{2,1,0:T(8,128)S(1)}, u32[]{:S(2)}, u32[]{:S(2)}) collective-permute-start(f32[2,256,512]{2,1,0:T(8,128)S(1)} %get-tuple-element.174), channel_id=1, source_target_pairs={{0,1},{1,0},{2,3},{3,2},{4,5},{5,4},{6,7},{7,6},{8,9},{9,8},{10,11... | collective-permute-start | bytes 3145736 | tf_op jit(solution)/shard_map/ppermute | solution.py:391
  172.2 4.2 %collective-permute-start.32 = (f32[2,256,512]{2,1,0:T(8,128)S(1)}, f32[2,256,512]{2,1,0:T(8,128)S(1)}, u32[]{:S(2)}, u32[]{:S(2)}) collective-permute-start(f32[2,256,512]{2,1,0:T(8,128)S(1)} %get-tuple-element.178), channel_id=1, source_target_pairs={{0,1},{1,0},{2,3},{3,2},{4,5},{5,4},{6,7},{7,6},{8,9},{9,8},{10,11... | collective-permute-start | bytes 3145736 | tf_op jit(solution)/shard_map/ppermute | solution.py:391
  176.7 1.5 copy-start.1

commit v9 on v8

--- a/solution.py
+++ b/solution.py
@@ -240,8 +240,8 @@
         in_specs=[
             smem,
             pl.BlockSpec(wide, lambda t, h: (base + t, h)),
-            pl.BlockSpec(wide, lambda t, h: (t, h)),
-            pl.BlockSpec((TILE, HEAD_SIZE), lambda t, h: (t, h)),
+            pl.BlockSpec(wide, lambda t, h: (base + t, h)),
+            pl.BlockSpec((TILE, HEAD_SIZE), lambda t, h: (base + t, h)),
         ]
         + [vmem] * len(arrays),
         out_specs=pl.BlockSpec((1, TILE, pair * HEAD_SIZE), lambda t, h: (t, 0, h)),
@@ -251,26 +251,32 @@
     )(first_row, q, near, stats, *arrays)
 
 
-def take_kernel(chips, one, two, three, near, far):
-    width = one.shape[1]
-    near[:, :width], near[:, width:] = one[...], two[...]
-    far[:, :width], far[:, width:] = three[...], two[...]
-
-
-def take_columns(weight, chips, width):
+def take_kernel(chips, one, two, three, near, far, near_late, far_late):
+    rows = one.shape[0]
+    early = near.shape[0] - rows
+    near[:rows, :] = two[...]
+    far[:rows, :] = two[...]
+    near[rows:, :] = one[:early, :]
+    far[rows:, :] = three[:early, :]
+    near_late[...] = one[early:, :]
+    far_late[...] = three[early:, :]
+
+
+def take_columns(weight, chips, width, late):
     rows = weight.shape[0]
-    step = rows // 8
-    out = jax.ShapeDtypeStruct((rows, 2 * width), jnp.float32)
-    out_spec = pl.BlockSpec((step, 2 * width), lambda i, o: (i, 0))
-    w_spec = lambda at: pl.BlockSpec((step, width), lambda i, o: (i, o[at]))
+    part = width // 4
+    shape = lambda n: jax.ShapeDtypeStruct((n, width), jnp.float32)
+    out_spec = lambda n: pl.BlockSpec((n, part), lambda i, o: (0, i))
+    w_spec = lambda at: pl.BlockSpec((rows, part), lambda i, o: (0, 4 * o[at] + i))
+    sizes = (2 * rows - late, 2 * rows - late, late, late)
     return pl.pallas_call(
         take_kernel,
-        out_shape=[out, out],
+        out_shape=[shape(n) for n in sizes],
         grid_spec=pltpu.PrefetchScalarGridSpec(
             num_scalar_prefetch=1,
-            grid=(rows // step,),
+            grid=(4,),
             in_specs=[w_spec(0), w_spec(1), w_spec(2)],
-            out_specs=[out_spec, out_spec],
+            out_specs=[out_spec(n) for n in sizes],
         ),
         compiler_params=pltpu.CompilerParams(vmem_limit_bytes=58 << 20),
         cost_estimate=SMALL,
@@ -329,15 +335,14 @@
                 out[0] = total[0] + weight_term(x[...], weight[...])
 
 
-def project_pair(got, near, far, total, unit, keep, cores):
+def project_pair(got, near, far, total, unit, cores):
     rows, depth = got[0].shape
     width = depth
-    base = 0 if keep else 2
     vmem = pl.BlockSpec(memory_space=pltpu.VMEM)
     out = jax.ShapeDtypeStruct((2, rows, width), jnp.float32)
     out_spec = pl.BlockSpec((1, rows, width), lambda k, s, c: (k, 0, 0))
     w_spec = lambda side: pl.BlockSpec(
-        (depth, width), lambda k, s, c: (0, base + c[side(k, s)])
+        (depth, width), lambda k, s, c: (0, c[side(k, s)])
     )
     return pl.pallas_call(
         pair_kernel,
@@ -390,7 +395,10 @@
     y = head_index // 2
     over_head = lambda a, bits: lax.ppermute(a, "head", [(i, i ^ bits) for i in range(head_size)])
     width = out_weight.shape[1] // head_size
-    near_weight, far_weight = take_columns(out_weight, y ^ jnp.arange(1, 4), 2 * width)
+    late = out_weight.shape[0] // 8
+    near_weight, far_weight, *late_weights = take_columns(
+        out_weight, y ^ jnp.arange(1, 4), 2 * width, late
+    )
     near_weight, far_weight = over_head(near_weight, 2), over_head(far_weight, 6)
 
     vert = lax.dynamic_slice_in_dim(vertical_blocks, head_index * heads, heads, 0)
@@ -453,7 +461,7 @@
     named = [a + b for a, b in zip(named, more)]
     arrays = (k_far, k_far_wrap, k_left, k_left_wrap, key_rows, v_far_a, v_far_b, v_left)
     near_arrays = (*arrays, value_vectors, slash_pos)
-    near = attend_near(q, 0, half, first_row, back, wraps, near_arrays)
+    near = attend_near(q, 0, rows, first_row, back, wraps, near_arrays)
     more = [swapped(a, bits) for a, bits in zip(named, two)]
     near, more = lax.optimization_barrier((near, more))
     arrays = (*(a + b for a, b in zip(named, more)), vert_pos)
@@ -461,31 +469,36 @@
     pass_order, keep_order, cores = orders
     meet, end = (2, 6), (6, 2)
     own_a = attend(q, *near, 0, first_row, arrays)
-    q, own_a = lax.optimization_barrier((q, own_a))
+    q, own_a, near_weight, far_weight = lax.optimization_barrier(
+        (q, own_a, near_weight, far_weight)
+    )
     meeting = lambda parts: [over_head(parts[i], bits) for i, bits in enumerate(meet)]
     ending = lambda parts: [over_head(parts[i], bits) for i, bits in enumerate(end)]
     got_a = meeting(own_a)
-    near = attend_near(q, half, half, first_row, back, wraps, near_arrays)
     own_b = attend(q, *near, half, first_row, arrays)
     got_b = meeting(own_b)
-    own_b, near_weight, far_weight = lax.optimization_barrier((own_b, near_weight, far_weight))
+    own_b, got_a = lax.optimization_barrier((own_b, got_a))
     total = project_chip(own_a, own_b, out_weight, pass_order)
-    total, got_a = lax.optimization_barrier((total, got_a))
-    product = lambda got, total, unit, keep: project_pair(
-        got, near_weight, far_weight, total, unit, keep, cores
-    )
-    there_a, here_a = product(got_a, total, 0, False)
-    own_b, there_a, here_a, got_a = lax.optimization_barrier((own_b, there_a, here_a, got_a))
-    kept_total = project_chip(own_a, own_b, out_weight, keep_order)
-    kept_total, there_a, got_b = lax.optimization_barrier((kept_total, there_a, got_b))
+    product = lambda got, weights, total, unit: project_pair(got, *weights, total, unit, cores)
+    weights = (near_weight, far_weight)
+    there_a, here_a = product(got_a, weights, total, 0)
+    there_a, here_a, got_a, got_b = lax.optimization_barrier((there_a, here_a, got_a, got_b))
     moved_a = over_head(there_a, 1)
-    there_b, here_b = product(got_b, total, 1, False)
-    there_b, here_b, moved_a, got_b = lax.optimization_barrier((there_b, here_b, moved_a, got_b))
+    there_b, here_b = product(got_b, weights, total, 1)
+    late_weights = [over_head(a, bits) for a, bits in zip(late_weights, meet)]
+    there_b, here_b, moved_a, late_weights = lax.optimization_barrier(
+        (there_b, here_b, moved_a, late_weights)
+    )
     pass_a, pass_b = here_a + moved_a, here_b + over_head(there_b, 1)
-    pass_a, pass_b, got_a, got_b = lax.optimization_barrier((pass_a, pass_b, got_a, got_b))
+    pass_a, pass_b, got_a, got_b, own_b = lax.optimization_barrier(
+        (pass_a, pass_b, got_a, got_b, own_b)
+    )
     sent = ending(pass_a) + ending(pass_b)
-    keep_a = product(got_a, kept_total, 0, True)
-    keep_b = product(got_b, kept_total, 1, True)
+    rows = out_weight.shape[0]
+    weights = [jnp.concatenate([a[rows:], b]) for a, b in zip(weights, late_weights)]
+    total = project_chip(own_a, own_b, out_weight, keep_order)
+    keep_a = product(got_a, weights, total, 0)
+    keep_b = product(got_b, weights, total, 1)
     keep_a, keep_b, sent = lax.optimization_barrier((keep_a, keep_b, sent))
     kept_a, kept_b = (here + over_head(there, 1) for there, here in (keep_a, keep_b))
     kept = (kept_a[0], kept_a[1], kept_b[0], kept_b[1])

time: 181 us -> 181 us (level)
  Pallas kernels: 63.7 us -> 58.8 us
  starting transfers between devices: 46 us -> 49.7 us
  local copies, waits for them, and re-layouts: 1.93 us -> 3.99 us
    ppermute x14 -> x16, starting transfers between devices: 14.8 us -> 18.7 us  [body(): lax.ppermute(a, 'head', [(i, i ^ bits) for i in range(head_size)])]
    slice x0 -> x3, local copies, waits for them, and re-layouts: none -> 2.04 us  [body(): a[rows:]]
    pallas_call x4, Pallas kernels: 18.3 us -> 16.4 us  [project_pair(): pl.pallas_call(pair_kernel, out_shape=[out, out], grid_spec=pltpu.Prefetc...]
    pallas_call x2 -> x1, Pallas kernels: 10.9 us -> 9.65 us  [attend_near(): pl.pallas_call(functools.partial(near_kernel, start), grid=(rows // TILE,...]
    ppermute x14 -> x16, waiting for transfers between devices: 18.6 us -> 19.2 us  [body(): lax.ppermute(a, 'head', [(i, i ^ bits) for i in range(head_size)])]
  transfers between devices with their start and end apart: 33 -> 35, of which waited for: 15 -> 17; matrix products, arithmetic and copies ran while one was open for 2% -> 4% of each run, Pallas kernels for 36% -> 33%
where the time goes in v9:
time: 181 us; the launch traced here: 179 us
  waiting for transfers between devices  59.9 us (33%)
  Pallas kernels  58.8 us (32%)
  starting transfers between devices  49.7 us (27%)
  other arithmetic  5.24 us (3%)
  local copies, waits for them, and re-layouts  3.99 us (2%)
    ppermute x19, waiting for transfers between devices, body(): send = lambda a, pairs: lax.ppermute(a, 'seq', pairs)  40.6 us
    ppermute x19, starting transfers between devices, body(): send = lambda a, pairs: lax.ppermute(a, 'seq', pairs)  31 us
    ppermute x16, waiting for transfers between devices, body(): lax.ppermute(a, 'head', [(i, i ^ bits) for i in range(head_size)])  19.2 us
    ppermute x16, starting transfers between devices, body(): lax.ppermute(a, 'head', [(i, i ^ bits) for i in range(head_size)])  18.7 us
    pallas_call x4, Pallas kernels, project_pair(): pl.pallas_call(pair_kernel, out_shape=[out, out], grid_spec=pltpu.Prefetc...  16.4 us
    pallas_call x2, Pallas kernels, attend(): pl.pallas_call(functools.partial(attend_kernel, start), grid=(2, heads //...  12.5 us
    pallas_call x2, Pallas kernels, project_chip(): pl.pallas_call(chip_kernel, out_shape=jax.ShapeDtypeStruct((2, 2 * rows,...  10.8 us
    pallas_call x1, Pallas kernels, attend_near(): pl.pallas_call(functools.partial(near_kernel, start), grid=(rows // TILE,...  9.65 us
  transfers between devices with their start and end apart: 35, of which 17 were waited for; matrix products, arithmetic and copies ran while one was open for 4% of the time, Pallas kernels for 33%

profile of v9, /device:TPU:2, one launch (start us, length us, event | category | flops | bytes accessed | tf_op | source)
XLA Modules:
  0.0 178.8 jit_solution(15180881371868461377)
XLA Ops:
  0.0 1.5 collective-permute-start
  2.0 1.9 %collective-permute-start.2 = (f32[1024,128]{1,0:T(8,128)}, f32[1024,128]{1,0:T(8,128)S(1)}, u32[]{:S(2)}, u32[]{:S(2)}) collective-permute-start(f32[1024,128]{1,0:T(8,128)} %v_own.1), channel_id=1, source_target_pairs={{0,32},{8,40},{16,48},{24,56},{32,64},{40,72},{48,80},{56,88},{64,... | collective-permute-start | bytes 1572872 | tf_op jit(solution)/shard_map/ppermute | solution.py:387
  3.9 2.1 %collective-permute-start.3 = (f32[1024,128]{1,0:T(8,128)}, f32[1024,128]{1,0:T(8,128)S(1)}, u32[]{:S(2)}, u32[]{:S(2)}) collective-permute-start(f32[1024,128]{1,0:T(8,128)} %v_own.1), channel_id=1, source_target_pairs={{0,96},{8,104},{16,112},{24,120},{32,0},{40,8},{48,16},{56,24},{64... | collective-permute-start | bytes 1572872 | tf_op jit(solution)/shard_map/ppermute | solution.py:387
  6.6 7.3 %shard_map.77 = (f32[960,1024]{1,0:T(8,128)}, f32[960,1024]{1,0:T(8,128)}, f32[64,1024]{1,0:T(8,128)}, f32[64,1024]{1,0:T(8,128)}) custom-call(s32[3]{0:T(128)} %add_xor_fusion.chips, f32[512,4096]{1,0:T(8,128)} %w.3, f32[512,4096]{1,0:T(8,128)} %w.3, f32[512,4096]{1,0:T(8,128)} %w.3), custom_call_target="tpu_custom_call" | custom-call | flops 1024 | bytes 1024 | tf_op jit(solution)/shard_map/pallas_call | solution.py:272
  13.9 1.7 collective-permute-start.19
  18.6 2.3 %collective-permute-start.20 = (f32[960,1024]{1,0:T(8,128)}, f32[960,1024]{1,0:T(8,128)S(1)}, u32[]{:S(2)}, u32[]{:S(2)}) collective-permute-start(f32[960,1024]{1,0:T(8,128)} %get-tuple-element.129), channel_id=1, source_target_pairs={{0,6},{1,7},{2,4},{3,5},{4,2},{5,3},{6,0},{7,1},{8,14},{9,15},{10,... | collective-permute-start | bytes 11796488 | tf_op jit(solution)/shard_map/ppermute | solution.py:396
  20.9 2.1 %collective-permute-start.5 = (f32[1024,128]{1,0:T(8,128)S(1)}, f32[1024,128]{1,0:T(8,128)S(1)}, u32[]{:S(2)}, u32[]{:S(2)}) collective-permute-start(f32[1024,128]{1,0:T(8,128)S(1)} %collective-permute-done.3.refs_5_), channel_id=1, source_target_pairs={{0,96},{8,104},{16,112},{24,120},{32,0},{40,8},{48,16},{56,24},{64... | collective-permute-start | bytes 1572872 | tf_op jit(solution)/shard_map/ppermute | solution.py:387
  23.2 1.6 collective-permute-start.6
  25.4 7.8 %collective-permute-done.5.refs_6_ = f32[1024,128]{1,0:T(8,128)S(1)} collective-permute-done((f32[1024,128]{1,0:T(8,128)S(1)}, f32[1024,128]{1,0:T(8,128)S(1)}, u32[]{:S(2)}, u32[]{:S(2)}) %collective-permute-start.5) | collective-permute-done | bytes 524320 | tf_op jit(solution)/shard_map/ppermute | solution.py:387
  33.9 6.6 %collective-permute-done.6 = f32[1536,128]{1,0:T(8,128)S(1)} collective-permute-done((f32[1536,128]{1,0:T(8,128)S(1)}, f32[1536,128]{1,0:T(8,128)S(1)}, u32[]{:S(2)}, u32[]{:S(2)}) %collective-permute-start.6) | collective-permute-done | bytes 786464 | tf_op jit(solution)/shard_map/ppermute | solution.py:387
  40.6 1.3 collective-permute-done.4
  42.0 1.3 collective-permute-start.8
  43.2 1.9 %shard_map.74 = (f32[1024,128]{1,0:T(8,128)S(1)}, f32[1024,128]{1,0:T(8,128)S(1)}, f32[1024,128]{1,0:T(8,128)S(1)}, f32[1024,128]{1,0:T(8,128)S(1)}) custom-call(s32[32]{0:T(128)S(1)} %get-tuple-element.98.k_place, s32[32]{0:T(128)S(1)} %compare_convert_fusion.1.k_held, s32[32]{0:T(128)S(1)} %get-tuple-element.100.v_place, s32[32]{0:T(128)S(1)} %get-tuple-element.101.v_held, ...), custom_call_target="tpu_custom_call" | custom-call | flops 1024 | bytes 1024 | tf_op jit(solution)/shard_map/pallas_call | solution.py:48
  45.9 4.1 %collective-permute-done.8.v_far_a = f32[512,128]{1,0:T(8,128)S(1)} collective-permute-done((f32[512,128]{1,0:T(8,128)S(1)}, f32[512,128]{1,0:T(8,128)S(1)}, u32[]{:S(2)}, u32[]{:S(2)}) %collective-permute-start.8) | collective-permute-done | bytes 262176 | tf_op jit(solution)/shard_map/ppermute | solution.py:387
  50.0 3.2 %collective-permute-start.9 = (f32[512,128]{1,0:T(8,128)S(1)}, f32[512,128]{1,0:T(8,128)S(1)}, u32[]{:S(2)}, u32[]{:S(2)}) collective-permute-start(f32[512,128]{1,0:T(8,128)S(1)} %slice.63), channel_id=1, source_target_pairs={{0,24},{8,0},{16,8},{24,16},{32,56},{40,32},{48,40},{56,48},{64,88... | collective-permute-start | bytes 786440 | tf_op jit(solution)/shard_map/ppermute | solution.py:387
  53.3 3.9 %collective-permute-done.9.v_far_b = f32[512,128]{1,0:T(8,128)S(1)} collective-permute-done((f32[512,128]{1,0:T(8,128)S(1)}, f32[512,128]{1,0:T(8,128)S(1)}, u32[]{:S(2)}, u32[]{:S(2)}) %collective-permute-start.9) | collective-permute-done | bytes 262176 | tf_op jit(solution)/shard_map/ppermute | solution.py:387
  57.1 4.4 %collective-permute-start.10 = (f32[1024,128]{1,0:T(8,128)S(1)}, f32[1024,128]{1,0:T(8,128)S(1)}, u32[]{:S(2)}, u32[]{:S(2)}) collective-permute-start(f32[1024,128]{1,0:T(8,128)S(1)} %slice.64.refs_2_.k_far), channel_id=1, source_target_pairs={{0,32},{8,40},{32,64},{40,72},{64,96},{72,104},{1,33},{9,41},{33,6... | collective-permute-start | bytes 1572872 | tf_op jit(solution)/shard_map/ppermute | solution.py:387
  61.6 2.7 %collective-permute-start.13 = (f32[1024,128]{1,0:T(8,128)S(1)}, f32[1024,128]{1,0:T(8,128)S(1)}, u32[]{:S(2)}, u32[]{:S(2)}) collective-permute-start(f32[1024,128]{1,0:T(8,128)S(1)} %get-tuple-element.105), channel_id=1, source_target_pairs={{0,8},{8,0},{16,24},{24,16},{32,40},{40,32},{48,56},{56,48},{64,72... | collective-permute-start | bytes 1572872 | tf_op jit(solution)/shard_map/ppermute | solution.py:387
  64.7 8.2 %collective-permute-done.13 = f32[1024,128]{1,0:T(8,128)S(1)} collective-permute-done((f32[1024,128]{1,0:T(8,128)S(1)}, f32[1024,128]{1,0:T(8,128)S(1)}, u32[]{:S(2)}, u32[]{:S(2)}) %collective-permute-start.13) | collective-permute-done | bytes 524320 | tf_op jit(solution)/shard_map/ppermute | solution.py:387
  73.0 2.6 %collective-permute-done.14 = f32[1024,128]{1,0:T(8,128)S(1)} collective-permute-done((f32[1024,128]{1,0:T(8,128)S(1)}, f32[1024,128]{1,0:T(8,128)S(1)}, u32[]{:S(2)}, u32[]{:S(2)}) %collective-permute-start.14) | collective-permute-done | bytes 524320 | tf_op jit(solution)/shard_map/ppermute | solution.py:387
  77.0 1.9 %collective-permute-start.16 = (f32[1024,128]{1,0:T(8,128)S(1)}, f32[1024,128]{1,0:T(8,128)S(1)}, u32[]{:S(2)}, u32[]{:S(2)}) collective-permute-start(f32[1024,128]{1,0:T(8,128)S(1)} %add.208), channel_id=1, source_target_pairs={{0,32},{8,40},{16,48},{24,56},{32,0},{40,8},{48,16},{56,24},{64,96... | collective-permute-start | bytes 1572872 | tf_op jit(solution)/shard_map/ppermute | solution.py:387
  79.0 5.9 %collective-permute-done.18 = f32[1024,128]{1,0:T(8,128)S(1)} collective-permute-done((f32[1024,128]{1,0:T(8,128)S(1)}, f32[1024,128]{1,0:T(8,128)S(1)}, u32[]{:S(2)}, u32[]{:S(2)}) %collective-permute-start.18) | collective-permute-done | bytes 524320 | tf_op jit(solution)/shard_map/ppermute | solution.py:387
  84.9 4.3 %collective-permute-start.15 = (f32[1024,128]{1,0:T(8,128)S(1)}, f32[1024,128]{1,0:T(8,128)S(1)}, u32[]{:S(2)}, u32[]{:S(2)}) collective-permute-start(f32[1024,128]{1,0:T(8,128)S(1)} %add.207), channel_id=1, source_target_pairs={{0,96},{8,104},{16,112},{24,120},{32,64},{40,72},{48,80},{56,88},{... | collective-permute-start | bytes 1572872 | tf_op jit(solution)/shard_map/ppermute | solution.py:387
  89.3 9.6 %shard_map.75 = (f32[1024,512]{1,0:T(8,128)S(1)}, f32[1024,256]{1,0:T(8,128)S(1)}) custom-call(s32[1]{0:T(128)} %bitcast.1.first_row, s32[4,4]{1,0:T(4,128)S(1)} %get-tuple-element.108.back, s32[2]{0:T(128)S(1)} %add_convert_fusion.wraps, f32[1024,512]{1,0:T(8,128)S(1)} %shard_map.73.q, f32[1024,128]{1,0:T(8,128)S(1)} %slice.64.refs_2_.k_far, ...), custom_call_target="tpu_custom_call" | custom-call | flops 100000 | bytes 1024 | tf_op jit(solution)/shard_map/pallas_call | solution.py:179
  99.2 6.2 %shard_map.76.own_a = f32[2,256,512]{2,1,0:T(8,128)S(1)} custom-call(s32[1]{0:T(128)} %bitcast.1.first_row, f32[1024,512]{1,0:T(8,128)S(1)} %shard_map.73.q, f32[1024,512]{1,0:T(8,128)S(1)} %get-tuple-element.121.near, f32[1024,256]{1,0:T(8,128)S(1)} %get-tuple-element.122.stats, f32[1024,128]{1,0:T(8,128)S(1)} %add.211.k_a, f32[1024,128]{1,0:T(8,128)S(1)} %add.212.k_b, ...), custom_call_target="tpu_custom_call" | custom-call | flops 100000 | bytes 1024 | tf_op jit(solution)/shard_map/pallas_call | solution.py:236
  105.8 1.2 collective-permute-start.21
  107.0 1.1 collective-permute-start.22
  108.1 6.2 %shard_map.78.own_b = f32[2,256,512]{2,1,0:T(8,128)S(1)} custom-call(s32[1]{0:T(128)} %bitcast.1.first_row, f32[1024,512]{1,0:T(8,128)S(1)} %shard_map.73.q, f32[1024,512]{1,0:T(8,128)S(1)} %get-tuple-element.121.near, f32[1024,256]{1,0:T(8,128)S(1)} %get-tuple-element.122.stats, f32[1024,128]{1,0:T(8,128)S(1)} %add.211.k_a, f32[1024,128]{1,0:T(8,128)S(1)} %add.212.k_b, ...), custom_call_target="tpu_custom_call" | custom-call | flops 100000 | bytes 1024 | tf_op jit(solution)/shard_map/pallas_call | solution.py:236
  114.5 1.4 collective-permute-start.23
  116.9 3.3 %collective-permute-done.21.got_a = f32[256,512]{1,0:T(8,128)S(1)} collective-permute-done((f32[256,512]{1,0:T(8,128)S(1)}, f32[256,512]{1,0:T(8,128)S(1)}, u32[]{:S(2)}, u32[]{:S(2)}) %collective-permute-start.21) | collective-permute-done | bytes 524320 | tf_op jit(solution)/shard_map/ppermute | solution.py:396
  120.9 5.4 %shard_map.79.total = f32[2,512,1024]{2,1,0:T(8,128)S(1)} custom-call(s32[4]{0:T(128)S(1)} %get-tuple-element.136.order, f32[2,256,512]{2,1,0:T(8,128)S(1)} %shard_map.76.own_a, f32[2,256,512]{2,1,0:T(8,128)S(1)} %shard_map.78.own_b, f32[512,4096]{1,0:T(8,128)S(1)} %bitcast.41), custom_call_target="tpu_custom_call" | custom-call | flops 100000 | bytes 1024 | tf_op jit(solution)/shard_map/pallas_call | solution.py:309
  126.3 4.6 %shard_map.80 = (f32[2,256,512]{2,1,0:T(8,128)S(1)}, f32[2,256,512]{2,1,0:T(8,128)S(1)}) custom-call(s32[2]{0:T(128)S(1)} %get-tuple-element.90.cores, f32[256,512]{1,0:T(8,128)S(1)} %collective-permute-done.21.got_a, f32[256,512]{1,0:T(8,128)S(1)} %collective-permute-done.22.got_b, f32[960,1024]{1,0:T(8,128)} %collective-permute-done.19.near, ...), custom_call_target="tpu_custom_call" | custom-call | flops 100000 | bytes 1024 | tf_op jit(solution)/shard_map/pallas_call | solution.py:347
  131.0 1.2 collective-permute-start.26
  132.2 3.0 %collective-permute-start.27 = (f32[64,1024]{1,0:T(8,128)S(1)}, f32[64,1024]{1,0:T(8,128)S(1)}, u32[]{:S(2)}, u32[]{:S(2)}) collective-permute-start(f32[64,1024]{1,0:T(8,128)S(1)} %copy-done.7), channel_id=1, source_target_pairs={{0,6},{1,7},{2,4},{3,5},{4,2},{5,3},{6,0},{7,1},{8,14},{9,15},{10,... | collective-permute-start | bytes 786440 | tf_op jit(solution)/shard_map/ppermute | solution.py:396
  135.2 4.6 %shard_map.81 = (f32[2,256,512]{2,1,0:T(8,128)S(1)}, f32[2,256,512]{2,1,0:T(8,128)S(1)}) custom-call(s32[2]{0:T(128)S(1)} %get-tuple-element.90.cores, f32[256,512]{1,0:T(8,128)S(1)} %collective-permute-done.23.got_a, f32[256,512]{1,0:T(8,128)S(1)} %collective-permute-done.24.got_b, f32[960,1024]{1,0:T(8,128)} %collective-permute-done.19.near, ...), custom_call_target="tpu_custom_call" | custom-call | flops 100000 | bytes 1024 | tf_op jit(solution)/shard_map/pallas_call | solution.py:347
  139.7 2.0 %collective-permute-done.27 = f32[64,1024]{1,0:T(8,128)S(1)} collective-permute-done((f32[64,1024]{1,0:T(8,128)S(1)}, f32[64,1024]{1,0:T(8,128)S(1)}, u32[]{:S(2)}, u32[]{:S(2)}) %collective-permute-start.27) | collective-permute-done | bytes 262176 | tf_op jit(solution)/shard_map/ppermute | solution.py:396
  142.0 2.4 %collective-permute-done.28 = f32[2,256,512]{2,1,0:T(8,128)S(1)} collective-permute-done((f32[2,256,512]{2,1,0:T(8,128)S(1)}, f32[2,256,512]{2,1,0:T(8,128)S(1)}, u32[]{:S(2)}, u32[]{:S(2)}) %collective-permute-start.28) | collective-permute-done | bytes 1048608 | tf_op jit(solution)/shard_map/ppermute | solution.py:396
  144.7 3.0 %collective-permute-start.29 = (f32[256,512]{1,0:T(8,128)S(1)}, f32[256,512]{1,0:T(8,128)S(1)}, u32[]{:S(2)}, u32[]{:S(2)}) collective-permute-start(f32[256,512]{1,0:T(8,128)S(1)} %get-tuple-element.192), channel_id=1, source_target_pairs={{0,6},{1,7},{2,4},{3,5},{4,2},{5,3},{6,0},{7,1},{8,14},{9,15},{10,... | collective-permute-start | bytes 1572872 | tf_op jit(solution)/shard_map/ppermute | solution.py:396
  148.3 1.7 collective-permute-start.32
  150.0 1.8 %slice.70 = f32[448,1024]{1,0:T(8,128)S(1)} slice(f32[960,1024]{1,0:T(8,128)} %collective-permute-done.19.near), slice={[512:960], [0:1024]} | slice | bytes 3670016 | tf_op jit(solution)/shard_map/slice | solution.py:498
  152.6 5.4 %shard_map.82.total = f32[2,512,1024]{2,1,0:T(8,128)S(1)} custom-call(s32[4]{0:T(128)S(1)} %get-tuple-element.157.order, f32[2,256,512]{2,1,0:T(8,128)S(1)} %shard_map.76.own_a, f32[2,256,512]{2,1,0:T(8,128)S(1)} %shard_map.78.own_b, f32[512,4096]{1,0:T(8,128)S(1)} %bitcast.41), custom_call_target="tpu_custom_call" | custom-call | flops 100000 | bytes 1024 | tf_op jit(solution)/shard_map/pallas_call | solution.py:309
  158.0 3.6 %shard_map.84 = (f32[2,256,512]{2,1,0:T(8,128)S(1)}, f32[2,256,512]{2,1,0:T(8,128)S(1)}) custom-call(s32[2]{0:T(128)S(1)} %get-tuple-element.90.cores, f32[256,512]{1,0:T(8,128)S(1)} %collective-permute-done.23.got_a, f32[256,512]{1,0:T(8,128)S(1)} %collective-permute-done.24.got_b, f32[512,1024]{1,0:T(8,128)S(1)} %pad_maximum_fusion.near, ...), custom_call_target="tpu_custom_call" | custom-call | flops 100000 | bytes 1024 | tf_op jit(solution)/shard_map/pallas_call | solution.py:347
  161.6 3.6 %shard_map.83 = (f32[2,256,512]{2,1,0:T(8,128)S(1)}, f32[2,256,512]{2,1,0:T(8,128)S(1)}) custom-call(s32[2]{0:T(128)S(1)} %get-tuple-element.90.cores, f32[256,512]{1,0:T(8,128)S(1)} %collective-permute-done.21.got_a, f32[256,512]{1,0:T(8,128)S(1)} %collective-permute-done.22.got_b, f32[512,1024]{1,0:T(8,128)S(1)} %pad_maximum_fusion.near, ...), custom_call_target="tpu_custom_call" | custom-call | flops 100000 | bytes 1024 | tf_op jit(solution)/shard_map/pallas_call | solution.py:347
  165.3 5.9 %collective-permute-done.31 = f32[256,512]{1,0:T(8,128)S(1)} collective-permute-done((f32[256,512]{1,0:T(8,128)S(1)}, f32[256,512]{1,0:T(8,128)S(1)}, u32[]{:S(2)}, u32[]{:S(2)}) %collective-permute-start.31) | collective-permute-done | bytes 524320 | tf_op jit(solution)/shard_map/ppermute | solution.py:396
  171.2 1.5 collective-permute-done.32
  173.2 2.1 %collective-permute-done.33 = f32[2,256,512]{2,1,0:T(8,128)S(1)} collective-permute-done((f32[2,256,512]{2,1,0:T(8,128)S(1)}, f32[2,256,512]{2,1,0:T(8,128)S(1)}, u32[]{:S(2)}, u32[]{:S(2)}) %collective-permute-start.33) | collective-permute-done | bytes 1048608 | tf_op jit(solution)/shard_map/ppermute | solution.py:396
  175.8 1.1 collective-permute-done.34
  177.3 1.5 pad_maximum_fusion.2
  (123 shorter events, 13.2 us)
Async XLA Ops:
  0.0 15.9 %copy-start = (s32[32,3]{0,1:T(4,128)S(1)}, s32[32,3]{0,1:T(4,128)}, u32[]{:S(2)}) copy-start(s32[32,3]{0,1:T(4,128)} %param.11) | copy-start | bytes 1156
  0.0 18.6 %collective-permute-start = (f32[1024,128]{1,0:T(8,128)}, f32[1024,128]{1,0:T(8,128)S(1)}, u32[]{:S(2)}, u32[]{:S(2)}) collective-permute-start(f32[1024,128]{1,0:T(8,128)} %k_own.1), channel_id=1, source_target_pairs={{0,8},{8,16},{16,24},{24,0},{32,40},{40,48},{48,56},{56,32},{64,72... | collective-permute-start | bytes 1572872 | tf_op jit(solution)/shard_map/ppermute | solution.py:387
  1.5 19.4 %collective-permute-start.1 = (f32[1024,128]{1,0:T(8,128)}, f32[1024,128]{1,0:T(8,128)S(1)}, u32[]{:S(2)}, u32[]{:S(2)}) collective-permute-start(f32[1024,128]{1,0:T(8,128)} %k_own.1), channel_id=1, source_target_pairs={{0,24},{8,0},{16,8},{24,16},{32,56},{40,32},{48,40},{56,48},{64,88... | collective-permute-start | bytes 1572872 | tf_op jit(solution)/shard_map/ppermute | solution.py:387
  2.0 18.9 %collective-permute-start.2 = (f32[1024,128]{1,0:T(8,128)}, f32[1024,128]{1,0:T(8,128)S(1)}, u32[]{:S(2)}, u32[]{:S(2)}) collective-permute-start(f32[1024,128]{1,0:T(8,128)} %v_own.1), channel_id=1, source_target_pairs={{0,32},{8,40},{16,48},{24,56},{32,64},{40,72},{48,80},{56,88},{64,... | collective-permute-start | bytes 1572872 | tf_op jit(solution)/shard_map/ppermute | solution.py:387
  3.9 16.9 %collective-permute-start.3 = (f32[1024,128]{1,0:T(8,128)}, f32[1024,128]{1,0:T(8,128)S(1)}, u32[]{:S(2)}, u32[]{:S(2)}) collective-permute-start(f32[1024,128]{1,0:T(8,128)} %v_own.1), channel_id=1, source_target_pairs={{0,96},{8,104},{16,112},{24,120},{32,0},{40,8},{48,16},{56,24},{64... | collective-permute-start | bytes 1572872 | tf_op jit(solution)/shard_map/ppermute | solution.py:387
  6.6 8.9 %copy-start.6 = (s32[32,8]{0,1:T(8,128)S(1)}, s32[32,8]{0,1:T(8,128)}, u32[]{:S(2)}) copy-start(s32[32,8]{0,1:T(8,128)} %param.10) | copy-start | bytes 3076
  6.6 16.4 %copy-start.3 = (f32[1024,128]{1,0:T(8,128)S(1)}, f32[1024,128]{1,0:T(8,128)}, u32[]{:S(2)}) copy-start(f32[1024,128]{1,0:T(8,128)} %v_own.1) | copy-start | bytes 1572868
  13.9 91.6 %collective-permute-start.19 = (f32[960,1024]{1,0:T(8,128)}, f32[960,1024]{1,0:T(8,128)}, u32[]{:S(2)}, u32[]{:S(2)}) collective-permute-start(f32[960,1024]{1,0:T(8,128)} %get-tuple-element.128), channel_id=1, source_target_pairs={{0,2},{1,3},{2,0},{3,1},{4,6},{5,7},{6,4},{7,5},{8,10},{9,11},{10,... | collective-permute-start | bytes 11796488 | tf_op jit(solution)/shard_map/ppermute | solution.py:396
  18.6 87.1 %collective-permute-start.20 = (f32[960,1024]{1,0:T(8,128)}, f32[960,1024]{1,0:T(8,128)S(1)}, u32[]{:S(2)}, u32[]{:S(2)}) collective-permute-start(f32[960,1024]{1,0:T(8,128)} %get-tuple-element.129), channel_id=1, source_target_pairs={{0,6},{1,7},{2,4},{3,5},{4,2},{5,3},{6,0},{7,1},{8,14},{9,15},{10,... | collective-permute-start | bytes 11796488 | tf_op jit(solution)/shard_map/ppermute | solution.py:396
  20.9 12.3 %collective-permute-start.5 = (f32[1024,128]{1,0:T(8,128)S(1)}, f32[1024,128]{1,0:T(8,128)S(1)}, u32[]{:S(2)}, u32[]{:S(2)}) collective-permute-start(f32[1024,128]{1,0:T(8,128)S(1)} %collective-permute-done.3.refs_5_), channel_id=1, source_target_pairs={{0,96},{8,104},{16,112},{24,120},{32,0},{40,8},{48,16},{56,24},{64... | collective-permute-start | bytes 1572872 | tf_op jit(solution)/shard_map/ppermute | solution.py:387
  23.1 20.1 %copy-start.4 = (f32[1024,128]{1,0:T(8,128)S(1)}, f32[1024,128]{1,0:T(8,128)}, u32[]{:S(2)}) copy-start(f32[1024,128]{1,0:T(8,128)} %k_own.1) | copy-start | bytes 1572868
  23.2 17.4 %collective-permute-start.6 = (f32[1536,128]{1,0:T(8,128)S(1)}, f32[1536,128]{1,0:T(8,128)S(1)}, u32[]{:S(2)}, u32[]{:S(2)}) collective-permute-start(f32[1536,128]{1,0:T(8,128)S(1)} %pad_maximum_fusion.4), channel_id=1, source_target_pairs={{0,8},{8,16},{16,24},{24,0},{32,40},{40,48},{48,56},{56,32},{64,72... | collective-permute-start | bytes 2359304 | tf_op jit(solution)/shard_map/ppermute | solution.py:387
  24.8 17.1 %collective-permute-start.4 = (f32[1536,128]{1,0:T(8,128)S(1)}, f32[1536,128]{1,0:T(8,128)S(1)}, u32[]{:S(2)}, u32[]{:S(2)}) collective-permute-start(f32[1536,128]{1,0:T(8,128)S(1)} %pad_maximum_fusion.3), channel_id=1, source_target_pairs={{0,24},{8,0},{16,8},{24,16},{32,56},{40,32},{48,40},{56,48},{64,88... | collective-permute-start | bytes 2359304 | tf_op jit(solution)/shard_map/ppermute | solution.py:387
  33.2 0.7 collective-permute-start.7
  42.0 22.5 %copy-start.5 = (f32[1024,512]{1,0:T(8,128)S(1)}, f32[1024,512]{1,0:T(8,128)}, u32[]{:S(2)}) copy-start(f32[1024,512]{1,0:T(8,128)} %q.1) | copy-start | bytes 6291460
  42.0 8.0 %collective-permute-start.8 = (f32[512,128]{1,0:T(8,128)S(1)}, f32[512,128]{1,0:T(8,128)S(1)}, u32[]{:S(2)}, u32[]{:S(2)}) collective-permute-start(f32[512,128]{1,0:T(8,128)S(1)} %slice.62), channel_id=1, source_target_pairs={{0,8},{8,16},{16,24},{24,0},{32,40},{40,48},{48,56},{56,32},{64,72... | collective-permute-start | bytes 786440 | tf_op jit(solution)/shard_map/ppermute | solution.py:387
  45.1 16.4 %collective-permute-start.11 = (f32[1024,128]{1,0:T(8,128)S(1)}, f32[1024,128]{1,0:T(8,128)S(1)}, u32[]{:S(2)}, u32[]{:S(2)}) collective-permute-start(f32[1024,128]{1,0:T(8,128)S(1)} %get-tuple-element.103), channel_id=1, source_target_pairs={{0,32},{8,40},{16,48},{24,56},{32,0},{40,8},{48,16},{56,24},{64,96... | collective-permute-start | bytes 1572872 | tf_op jit(solution)/shard_map/ppermute | solution.py:387
  45.5 18.7 %collective-permute-start.12 = (f32[1024,128]{1,0:T(8,128)S(1)}, f32[1024,128]{1,0:T(8,128)S(1)}, u32[]{:S(2)}, u32[]{:S(2)}) collective-permute-start(f32[1024,128]{1,0:T(8,128)S(1)} %get-tuple-element.104), channel_id=1, source_target_pairs={{0,96},{8,104},{16,112},{24,120},{32,64},{40,72},{48,80},{56,88},{... | collective-permute-start | bytes 1572872 | tf_op jit(solution)/shard_map/ppermute | solution.py:387
  50.0 7.1 %collective-permute-start.9 = (f32[512,128]{1,0:T(8,128)S(1)}, f32[512,128]{1,0:T(8,128)S(1)}, u32[]{:S(2)}, u32[]{:S(2)}) collective-permute-start(f32[512,128]{1,0:T(8,128)S(1)} %slice.63), channel_id=1, source_target_pairs={{0,24},{8,0},{16,8},{24,16},{32,56},{40,32},{48,40},{56,48},{64,88... | collective-permute-start | bytes 786440 | tf_op jit(solution)/shard_map/ppermute | solution.py:387
  57.1 18.4 %collective-permute-start.10 = (f32[1024,128]{1,0:T(8,128)S(1)}, f32[1024,128]{1,0:T(8,128)S(1)}, u32[]{:S(2)}, u32[]{:S(2)}) collective-permute-start(f32[1024,128]{1,0:T(8,128)S(1)} %slice.64.refs_2_.k_far), channel_id=1, source_target_pairs={{0,32},{8,40},{32,64},{40,72},{64,96},{72,104},{1,33},{9,41},{33,6... | collective-permute-start | bytes 1572872 | tf_op jit(solution)/shard_map/ppermute | solution.py:387
  61.6 11.4 %collective-permute-start.13 = (f32[1024,128]{1,0:T(8,128)S(1)}, f32[1024,128]{1,0:T(8,128)S(1)}, u32[]{:S(2)}, u32[]{:S(2)}) collective-permute-start(f32[1024,128]{1,0:T(8,128)S(1)} %get-tuple-element.105), channel_id=1, source_target_pairs={{0,8},{8,0},{16,24},{24,16},{32,40},{40,32},{48,56},{56,48},{64,72... | collective-permute-start | bytes 1572872 | tf_op jit(solution)/shard_map/ppermute | solution.py:387
  64.2 11.3 %collective-permute-start.14 = (f32[1024,128]{1,0:T(8,128)S(1)}, f32[1024,128]{1,0:T(8,128)S(1)}, u32[]{:S(2)}, u32[]{:S(2)}) collective-permute-start(f32[1024,128]{1,0:T(8,128)S(1)} %get-tuple-element.106), channel_id=1, source_target_pairs={{0,24},{8,16},{16,8},{24,0},{32,56},{40,48},{48,40},{56,32},{64,88... | collective-permute-start | bytes 1572872 | tf_op jit(solution)/shard_map/ppermute | solution.py:387
  75.6 9.3 %collective-permute-start.18 = (f32[1024,128]{1,0:T(8,128)S(1)}, f32[1024,128]{1,0:T(8,128)S(1)}, u32[]{:S(2)}, u32[]{:S(2)}) collective-permute-start(f32[1024,128]{1,0:T(8,128)S(1)} %add.210), channel_id=1, source_target_pairs={{0,8},{8,0},{16,24},{24,16},{32,40},{40,32},{48,56},{56,48},{64,72... | collective-permute-start | bytes 1572872 | tf_op jit(solution)/shard_map/ppermute | solution.py:387
  76.7 22.3 %collective-permute-start.17 = (f32[1024,128]{1,0:T(8,128)S(1)}, f32[1024,128]{1,0:T(8,128)S(1)}, u32[]{:S(2)}, u32[]{:S(2)}) collective-permute-start(f32[1024,128]{1,0:T(8,128)S(1)} %add.209), channel_id=1, source_target_pairs={{0,24},{8,16},{16,8},{24,0},{32,56},{40,48},{48,40},{56,32},{64,88... | collective-permute-start | bytes 1572872 | tf_op jit(solution)/shard_map/ppermute | solution.py:387
  77.0 22.0 %collective-permute-start.16 = (f32[1024,128]{1,0:T(8,128)S(1)}, f32[1024,128]{1,0:T(8,128)S(1)}, u32[]{:S(2)}, u32[]{:S(2)}) collective-permute-start(f32[1024,128]{1,0:T(8,128)S(1)} %add.208), channel_id=1, source_target_pairs={{0,32},{8,40},{16,48},{24,56},{32,0},{40,8},{48,16},{56,24},{64,96... | collective-permute-start | bytes 1572872 | tf_op jit(solution)/shard_map/ppermute | solution.py:387
  84.9 14.0 %collective-permute-start.15 = (f32[1024,128]{1,0:T(8,128)S(1)}, f32[1024,128]{1,0:T(8,128)S(1)}, u32[]{:S(2)}, u32[]{:S(2)}) collective-permute-start(f32[1024,128]{1,0:T(8,128)S(1)} %add.207), channel_id=1, source_target_pairs={{0,96},{8,104},{16,112},{24,120},{32,64},{40,72},{48,80},{56,88},{... | collective-permute-start | bytes 1572872 | tf_op jit(solution)/shard_map/ppermute | solution.py:387
  99.2 21.7 %slice-start = ((s8[8388608]{0:T(1024)(128)(4,1)}), s8[4194304]{0:T(1024)(128)(4,1)S(1)}, s32[]{:S(2)}) async-start(s8[8388608]{0:T(1024)(128)(4,1)} %bitcast.40), calls=%async_computation | async-start | bytes 8388608
  105.7 44.3 %copy-start.2 = (f32[960,1024]{1,0:T(8,128)}, f32[960,1024]{1,0:T(8,128)S(1)}, u32[]{:S(2)}) copy-start(f32[960,1024]{1,0:T(8,128)S(1)} %collective-permute-done.20.far) | copy-start | bytes 11796484
  105.8 14.5 %collective-permute-start.21 = (f32[256,512]{1,0:T(8,128)S(1)}, f32[256,512]{1,0:T(8,128)S(1)}, u32[]{:S(2)}, u32[]{:S(2)}) collective-permute-start(f32[256,512]{1,0:T(8,128)S(1)} %get-tuple-element.196), channel_id=1, source_target_pairs={{0,2},{1,3},{2,0},{3,1},{4,6},{5,7},{6,4},{7,5},{8,10},{9,11},{10,... | collective-permute-start | bytes 1572872 | tf_op jit(solution)/shard_map/ppermute | solution.py:396
  107.0 13.9 %slice-start.1 = ((s8[8388608]{0:T(1024)(128)(4,1)}), s8[4194304]{0:T(1024)(128)(4,1)S(1)}, s32[]{:S(2)}) async-start(s8[8388608]{0:T(1024)(128)(4,1)} %bitcast.40), calls=%async_computation.1 | async-start | bytes 8388608
  107.0 13.9 %collective-permute-start.22 = (f32[256,512]{1,0:T(8,128)S(1)}, f32[256,512]{1,0:T(8,128)S(1)}, u32[]{:S(2)}, u32[]{:S(2)}) collective-permute-start(f32[256,512]{1,0:T(8,128)S(1)} %get-tuple-element.195), channel_id=1, source_target_pairs={{0,6},{1,7},{2,4},{3,5},{4,2},{5,3},{6,0},{7,1},{8,14},{9,15},{10,... | collective-permute-start | bytes 1572872 | tf_op jit(solution)/shard_map/ppermute | solution.py:396
  114.5 16.4 %collective-permute-start.23 = (f32[256,512]{1,0:T(8,128)S(1)}, f32[256,512]{1,0:T(8,128)S(1)}, u32[]{:S(2)}, u32[]{:S(2)}) collective-permute-start(f32[256,512]{1,0:T(8,128)S(1)} %get-tuple-element.194), channel_id=1, source_target_pairs={{0,2},{1,3},{2,0},{3,1},{4,6},{5,7},{6,4},{7,5},{8,10},{9,11},{10,... | collective-permute-start | bytes 1572872 | tf_op jit(solution)/shard_map/ppermute | solution.py:396
  115.9 15.1 %collective-permute-start.24 = (f32[256,512]{1,0:T(8,128)S(1)}, f32[256,512]{1,0:T(8,128)S(1)}, u32[]{:S(2)}, u32[]{:S(2)}) collective-permute-start(f32[256,512]{1,0:T(8,128)S(1)} %get-tuple-element.193), channel_id=1, source_target_pairs={{0,6},{1,7},{2,4},{3,5},{4,2},{5,3},{6,0},{7,1},{8,14},{9,15},{10,... | collective-permute-start | bytes 1572872 | tf_op jit(solution)/shard_map/ppermute | solution.py:396
  126.3 4.7 %copy-start.8 = (f32[64,1024]{1,0:T(8,128)S(1)}, f32[64,1024]{1,0:T(8,128)}, u32[]{:S(2)}) copy-start(f32[64,1024]{1,0:T(8,128)} %get-tuple-element.146) | copy-start | bytes 786436
  126.3 5.9 %copy-start.7 = (f32[64,1024]{1,0:T(8,128)S(1)}, f32[64,1024]{1,0:T(8,128)}, u32[]{:S(2)}) copy-start(f32[64,1024]{1,0:T(8,128)} %get-tuple-element.147) | copy-start | bytes 786436
  130.9 10.9 %collective-permute-start.25 = (f32[2,256,512]{2,1,0:T(8,128)S(1)}, f32[2,256,512]{2,1,0:T(8,128)S(1)}, u32[]{:S(2)}, u32[]{:S(2)}) collective-permute-start(f32[2,256,512]{2,1,0:T(8,128)S(1)} %get-tuple-element.145), channel_id=1, source_target_pairs={{0,1},{1,0},{2,3},{3,2},{4,5},{5,4},{6,7},{7,6},{8,9},{9,8},{10,11... | collective-permute-start | bytes 3145736 | tf_op jit(solution)/shard_map/ppermute | solution.py:396
  131.0 8.7 %collective-permute-start.26 = (f32[64,1024]{1,0:T(8,128)S(1)}, f32[64,1024]{1,0:T(8,128)S(1)}, u32[]{:S(2)}, u32[]{:S(2)}) collective-permute-start(f32[64,1024]{1,0:T(8,128)S(1)} %copy-done.8), channel_id=1, source_target_pairs={{0,2},{1,3},{2,0},{3,1},{4,6},{5,7},{6,4},{7,5},{8,10},{9,11},{10,... | collective-permute-start | bytes 786440 | tf_op jit(solution)/shard_map/ppermute | solution.py:396
  132.2 9.6 %collective-permute-start.27 = (f32[64,1024]{1,0:T(8,128)S(1)}, f32[64,1024]{1,0:T(8,128)S(1)}, u32[]{:S(2)}, u32[]{:S(2)}) collective-permute-start(f32[64,1024]{1,0:T(8,128)S(1)} %copy-done.7), channel_id=1, source_target_pairs={{0,6},{1,7},{2,4},{3,5},{4,2},{5,3},{6,0},{7,1},{8,14},{9,15},{10,... | collective-permute-start | bytes 786440 | tf_op jit(solution)/shard_map/ppermute | solution.py:396
  141.8 2.7 %collective-permute-start.28 = (f32[2,256,512]{2,1,0:T(8,128)S(1)}, f32[2,256,512]{2,1,0:T(8,128)S(1)}, u32[]{:S(2)}, u32[]{:S(2)}) collective-permute-start(f32[2,256,512]{2,1,0:T(8,128)S(1)} %get-tuple-element.150), channel_id=1, source_target_pairs={{0,1},{1,0},{2,3},{3,2},{4,5},{5,4},{6,7},{7,6},{8,9},{9,8},{10,11... | collective-permute-start | bytes 3145736 | tf_op jit(solution)/shard_map/ppermute | solution.py:396
  144.7 20.6 %collective-permute-start.29 = (f32[256,512]{1,0:T(8,128)S(1)}, f32[256,512]{1,0:T(8,128)S(1)}, u32[]{:S(2)}, u32[]{:S(2)}) collective-permute-start(f32[256,512]{1,0:T(8,128)S(1)} %get-tuple-element.192), channel_id=1, source_target_pairs={{0,6},{1,7},{2,4},{3,5},{4,2},{5,3},{6,0},{7,1},{8,14},{9,15},{10,... | collective-permute-start | bytes 1572872 | tf_op jit(solution)/shard_map/ppermute | solution.py:396
  147.8 17.6 %collective-permute-start.30 = (f32[256,512]{1,0:T(8,128)S(1)}, f32[256,512]{1,0:T(8,128)S(1)}, u32[]{:S(2)}, u32[]{:S(2)}) collective-permute-start(f32[256,512]{1,0:T(8,128)S(1)} %get-tuple-element.191), channel_id=1, source_target_pairs={{0,2},{1,3},{2,0},{3,1},{4,6},{5,7},{6,4},{7,5},{8,10},{9,11},{10,... | collective-permute-start | bytes 1572872 | tf_op jit(solution)/shard_map/ppermute | solution.py:396
  147.8 23.4 %collective-permute-start.31 = (f32[256,512]{1,0:T(8,128)S(1)}, f32[256,512]{1,0:T(8,128)S(1)}, u32[]{:S(2)}, u32[]{:S(2)}) collective-permute-start(f32[256,512]{1,0:T(8,128)S(1)} %get-tuple-element.190), channel_id=1, source_target_pairs={{0,6},{1,7},{2,4},{3,5},{4,2},{5,3},{6,0},{7,1},{8,14},{9,15},{10,... | collective-permute-start | bytes 1572872 | tf_op jit(solution)/shard_map/ppermute | solution.py:396
  148.3 24.4 %collective-permute-start.32 = (f32[256,512]{1,0:T(8,128)S(1)}, f32[256,512]{1,0:T(8,128)S(1)}, u32[]{:S(2)}, u32[]{:S(2)}) collective-permute-start(f32[256,512]{1,0:T(8,128)S(1)} %get-tuple-element.189), channel_id=1, source_target_pairs={{0,2},{1,3},{2,0},{3,1},{4,6},{5,7},{6,4},{7,5},{8,10},{9,11},{10,... | collective-permute-start | bytes 1572872 | tf_op jit(solution)/shard_map/ppermute | solution.py:396
  150.0 2.1 %slice-start.2 = ((f32[960,1024]{1,0:T(8,128)}), f32[448,1024]{1,0:T(8,128)S(1)}, s32[]{:S(2)}) async-start(f32[960,1024]{1,0:T(8,128)} %copy-done.2), calls=%async_computation.2 | async-start | bytes 3670016 | tf_op jit(solution)/shard_map/slice | solution.py:498
  172.7 2.7 %collective-permute-start.33 = (f32[2,256,512]{2,1,0:T(8,128)S(1)}, f32[2,256,512]{2,1,0:T(8,128)S(1)}, u32[]{:S(2)}, u32[]{:S(2)}) collective-permute-start(f32[2,256,512]{2,1,0:T(8,128)S(1)} %get-tuple-element.168), channel_id=1, source_target_pairs={{0,1},{1,0},{2,3},{3,2},{4,5},{5,4},{6,7},{7,6},{8,9},{9,8},{10,11... | collective-permute-start | bytes 3145736 | tf_op jit(solution)/shard_map/ppermute | solution.py:396
  172.7 4.2 %collective-permute-start.34 = (f32[2,256,512]{2,1,0:T(8,128)S(1)}, f32[2,256,512]{2,1,0:T(8,128)S(1)}, u32[]{:S(2)}, u32[]{:S(2)}) collective-permute-start(f32[2,256,512]{2,1,0:T(8,128)S(1)} %get-tuple-element.172), channel_id=1, source_target_pairs={{0,1},{1,0},{2,3},{3,2},{4,5},{5,4},{6,7},{7,6},{8,9},{9,8},{10,11... | collective-permute-start | bytes 3145736 | tf_op jit(solution)/shard_map/ppermute | solution.py:396
  177.3 1.5 copy-start.1

commit v10 on v8

--- a/solution.py
+++ b/solution.py
@@ -240,8 +240,8 @@
         in_specs=[
             smem,
             pl.BlockSpec(wide, lambda t, h: (base + t, h)),
-            pl.BlockSpec(wide, lambda t, h: (t, h)),
-            pl.BlockSpec((TILE, HEAD_SIZE), lambda t, h: (t, h)),
+            pl.BlockSpec(wide, lambda t, h: (base + t, h)),
+            pl.BlockSpec((TILE, HEAD_SIZE), lambda t, h: (base + t, h)),
         ]
         + [vmem] * len(arrays),
         out_specs=pl.BlockSpec((1, TILE, pair * HEAD_SIZE), lambda t, h: (t, 0, h)),
@@ -385,7 +385,6 @@
     k_left = send(key_rows, right)
     k_right = send(key_rows, left)
     v_below = send(value_vectors, up)
-    v_above = send(value_vectors, down)
 
     y = head_index // 2
     over_head = lambda a, bits: lax.ppermute(a, "head", [(i, i ^ bits) for i in range(head_size)])
@@ -421,8 +420,10 @@
     orders = (pass_order, keep_order, cores)
     small = (vert_pos, slash_pos, first_row, back, wraps, orders, k_place, k_held, v_place, v_held)
 
-    (k_left, k_right, v_below, v_above), small = lax.optimization_barrier(
-        ((k_left, k_right, v_below, v_above), small)
+    k_left, late_values = lax.optimization_barrier((k_left, value_vectors))
+    v_above = send(late_values, down)
+    (k_left, k_right, v_below), small = lax.optimization_barrier(
+        ((k_left, k_right, v_below), small)
     )
     vert_pos, slash_pos, first_row, back, wraps, orders, k_place, k_held, v_place, v_held = small
     half = rows // 2
@@ -453,7 +454,7 @@
     named = [a + b for a, b in zip(named, more)]
     arrays = (k_far, k_far_wrap, k_left, k_left_wrap, key_rows, v_far_a, v_far_b, v_left)
     near_arrays = (*arrays, value_vectors, slash_pos)
-    near = attend_near(q, 0, half, first_row, back, wraps, near_arrays)
+    near = attend_near(q, 0, rows, first_row, back, wraps, near_arrays)
     more = [swapped(a, bits) for a, bits in zip(named, two)]
     near, more = lax.optimization_barrier((near, more))
     arrays = (*(a + b for a, b in zip(named, more)), vert_pos)
@@ -465,7 +466,6 @@
     meeting = lambda parts: [over_head(parts[i], bits) for i, bits in enumerate(meet)]
     ending = lambda parts: [over_head(parts[i], bits) for i, bits in enumerate(end)]
     got_a = meeting(own_a)
-    near = attend_near(q, half, half, first_row, back, wraps, near_arrays)
     own_b = attend(q, *near, half, first_row, arrays)
     got_b = meeting(own_b)
     own_b, near_weight, far_weight = lax.optimization_barrier((own_b, near_weight, far_weight))
@@ -475,20 +475,23 @@
         got, near_weight, far_weight, total, unit, keep, cores
     )
     there_a, here_a = product(got_a, total, 0, False)
-    own_b, there_a, here_a, got_a = lax.optimization_barrier((own_b, there_a, here_a, got_a))
-    kept_total = project_chip(own_a, own_b, out_weight, keep_order)
-    kept_total, there_a, got_b = lax.optimization_barrier((kept_total, there_a, got_b))
+    there_a, here_a, got_a, got_b = lax.optimization_barrier((there_a, here_a, got_a, got_b))
     moved_a = over_head(there_a, 1)
     there_b, here_b = product(got_b, total, 1, False)
-    there_b, here_b, moved_a, got_b = lax.optimization_barrier((there_b, here_b, moved_a, got_b))
-    pass_a, pass_b = here_a + moved_a, here_b + over_head(there_b, 1)
-    pass_a, pass_b, got_a, got_b = lax.optimization_barrier((pass_a, pass_b, got_a, got_b))
-    sent = ending(pass_a) + ending(pass_b)
+    there_b, here_b, moved_a = lax.optimization_barrier((there_b, here_b, moved_a))
+    here = jnp.concatenate([here_a, here_b], axis=1)
+    passed = here + jnp.concatenate([moved_a, over_head(there_b, 1)], axis=1)
+    passed = [passed[0], passed[1]]
+    passed, got_a, got_b, own_b = lax.optimization_barrier((passed, got_a, got_b, own_b))
+    sent = ending(passed)
+    kept_total = project_chip(own_a, own_b, out_weight, keep_order)
     keep_a = product(got_a, kept_total, 0, True)
     keep_b = product(got_b, kept_total, 1, True)
     keep_a, keep_b, sent = lax.optimization_barrier((keep_a, keep_b, sent))
     kept_a, kept_b = (here + over_head(there, 1) for there, here in (keep_a, keep_b))
     kept = (kept_a[0], kept_a[1], kept_b[0], kept_b[1])
+    rows = kept_a.shape[1]
+    sent = (sent[0][:rows], sent[1][:rows], sent[0][rows:], sent[1][rows:])
     return jnp.concatenate([a + b for a, b in zip(kept, sent)], axis=0)
 
 

time: 181 us -> 179 us (0.989)
    ppermute x14 -> x12, starting transfers between devices: 14.8 us -> 11.7 us  [body(): lax.ppermute(a, 'head', [(i, i ^ bits) for i in range(head_size)])]
    pallas_call x4, Pallas kernels: 18.3 us -> 21.3 us  [project_pair(): pl.pallas_call(pair_kernel, out_shape=[out, out], grid_spec=pltpu.Prefetc...]
    pallas_call x2 -> x1, Pallas kernels: 10.9 us -> 9.63 us  [attend_near(): pl.pallas_call(functools.partial(near_kernel, start), grid=(rows // TILE,...]
    ppermute x14 -> x12, waiting for transfers between devices: 18.6 us -> 18.9 us  [body(): lax.ppermute(a, 'head', [(i, i ^ bits) for i in range(head_size)])]
  transfers between devices with their start and end apart: 33 -> 31, of which waited for: 15 -> 14; matrix products, arithmetic and copies ran while one was open for 2% -> 2% of each run, Pallas kernels for 36% -> 37%
where the time goes in v10:
time: 179 us; the launch traced here: 177 us
  Pallas kernels  65.4 us (37%)
  waiting for transfers between devices  59.5 us (33%)
  starting transfers between devices  44.4 us (25%)
  other arithmetic  4.88 us (3%)
  local copies, waits for them, and re-layouts  1.97 us (1%)
    ppermute x19, waiting for transfers between devices, body(): send = lambda a, pairs: lax.ppermute(a, 'seq', pairs)  40.6 us
    ppermute x19, starting transfers between devices, body(): send = lambda a, pairs: lax.ppermute(a, 'seq', pairs)  32.7 us
    pallas_call x4, Pallas kernels, project_pair(): pl.pallas_call(pair_kernel, out_shape=[out, out], grid_spec=pltpu.Prefetc...  21.3 us
    ppermute x12, waiting for transfers between devices, body(): lax.ppermute(a, 'head', [(i, i ^ bits) for i in range(head_size)])  18.9 us
    pallas_call x2, Pallas kernels, attend(): pl.pallas_call(functools.partial(attend_kernel, start), grid=(2, heads //...  12.6 us
    ppermute x12, starting transfers between devices, body(): lax.ppermute(a, 'head', [(i, i ^ bits) for i in range(head_size)])  11.7 us
    pallas_call x2, Pallas kernels, project_chip(): pl.pallas_call(chip_kernel, out_shape=jax.ShapeDtypeStruct((2, 2 * rows,...  10.8 us
    pallas_call x1, Pallas kernels, attend_near(): pl.pallas_call(functools.partial(near_kernel, start), grid=(rows // TILE,...  9.63 us
  transfers between devices with their start and end apart: 31, of which 14 were waited for; matrix products, arithmetic and copies ran while one was open for 2% of the time, Pallas kernels for 37%

profile of v10, /device:TPU:2, one launch (start us, length us, event | category | flops | bytes accessed | tf_op | source)
XLA Modules:
  0.0 177.3 jit_solution(17706830138634915259)
XLA Ops:
  0.5 1.6 collective-permute-start
  2.0 1.9 %collective-permute-start.2 = (f32[1024,128]{1,0:T(8,128)}, f32[1024,128]{1,0:T(8,128)S(1)}, u32[]{:S(2)}, u32[]{:S(2)}) collective-permute-start(f32[1024,128]{1,0:T(8,128)} %v_own.1), channel_id=1, source_target_pairs={{0,32},{8,40},{16,48},{24,56},{32,64},{40,72},{48,80},{56,88},{64,... | collective-permute-start | bytes 1572872 | tf_op jit(solution)/shard_map/ppermute | solution.py:382
  3.9 0.5 add_xor_fusion.chips
  4.5 9.0 %shard_map.78 = (f32[512,2048]{1,0:T(8,128)}, f32[512,2048]{1,0:T(8,128)}) custom-call(s32[3]{0:T(128)} %add_xor_fusion.chips, f32[512,4096]{1,0:T(8,128)} %w.3, f32[512,4096]{1,0:T(8,128)} %w.3, f32[512,4096]{1,0:T(8,128)} %w.3), custom_call_target="tpu_custom_call" | custom-call | flops 1024 | bytes 1024 | tf_op jit(solution)/shard_map/pallas_call | solution.py:266
  13.5 1.6 collective-permute-start.19
  15.0 2.2 %collective-permute-start.20 = (f32[512,2048]{1,0:T(8,128)}, f32[512,2048]{1,0:T(8,128)}, u32[]{:S(2)}, u32[]{:S(2)}) collective-permute-start(f32[512,2048]{1,0:T(8,128)} %get-tuple-element.129), channel_id=1, source_target_pairs={{0,6},{1,7},{2,4},{3,5},{4,2},{5,3},{6,0},{7,1},{8,14},{9,15},{10,... | collective-permute-start | bytes 12582920 | tf_op jit(solution)/shard_map/ppermute | solution.py:390
  20.3 2.2 %collective-permute-start.4 = (f32[1024,128]{1,0:T(8,128)S(1)}, f32[1024,128]{1,0:T(8,128)S(1)}, u32[]{:S(2)}, u32[]{:S(2)}) collective-permute-start(f32[1024,128]{1,0:T(8,128)S(1)} %copy-done.2), channel_id=1, source_target_pairs={{0,96},{8,104},{16,112},{24,120},{32,0},{40,8},{48,16},{56,24},{64... | collective-permute-start | bytes 1572872 | tf_op jit(solution)/shard_map/ppermute | solution.py:382
  22.5 0.7 collective-permute-start.7
  23.4 2.5 %collective-permute-start.3 = (f32[1536,128]{1,0:T(8,128)S(1)}, f32[1536,128]{1,0:T(8,128)S(1)}, u32[]{:S(2)}, u32[]{:S(2)}) collective-permute-start(f32[1536,128]{1,0:T(8,128)S(1)} %pad_maximum_fusion.1), channel_id=1, source_target_pairs={{0,24},{8,0},{16,8},{24,16},{32,56},{40,32},{48,40},{56,48},{64,88... | collective-permute-start | bytes 2359304 | tf_op jit(solution)/shard_map/ppermute | solution.py:382
  25.9 6.9 %collective-permute-done.4.refs_5_ = f32[1024,128]{1,0:T(8,128)S(1)} collective-permute-done((f32[1024,128]{1,0:T(8,128)S(1)}, f32[1024,128]{1,0:T(8,128)S(1)}, u32[]{:S(2)}, u32[]{:S(2)}) %collective-permute-start.4) | collective-permute-done | bytes 524320 | tf_op jit(solution)/shard_map/ppermute | solution.py:382
  32.8 1.5 collective-permute-start.6
  34.3 3.4 %collective-permute-start.5 = (f32[1024,128]{1,0:T(8,128)S(1)}, f32[1024,128]{1,0:T(8,128)S(1)}, u32[]{:S(2)}, u32[]{:S(2)}) collective-permute-start(f32[1024,128]{1,0:T(8,128)S(1)} %collective-permute-done.4.refs_5_), channel_id=1, source_target_pairs={{0,96},{8,104},{16,112},{24,120},{32,0},{40,8},{48,16},{56,24},{64... | collective-permute-start | bytes 1572872 | tf_op jit(solution)/shard_map/ppermute | solution.py:382
  37.7 3.6 %collective-permute-done.3 = f32[1536,128]{1,0:T(8,128)S(1)} collective-permute-done((f32[1536,128]{1,0:T(8,128)S(1)}, f32[1536,128]{1,0:T(8,128)S(1)}, u32[]{:S(2)}, u32[]{:S(2)}) %collective-permute-start.3) | collective-permute-done | bytes 786464 | tf_op jit(solution)/shard_map/ppermute | solution.py:382
  41.3 8.8 %collective-permute-done.6 = f32[1536,128]{1,0:T(8,128)S(1)} collective-permute-done((f32[1536,128]{1,0:T(8,128)S(1)}, f32[1536,128]{1,0:T(8,128)S(1)}, u32[]{:S(2)}, u32[]{:S(2)}) %collective-permute-start.6) | collective-permute-done | bytes 786464 | tf_op jit(solution)/shard_map/ppermute | solution.py:382
  50.2 3.0 %collective-permute-start.9 = (f32[512,128]{1,0:T(8,128)S(1)}, f32[512,128]{1,0:T(8,128)S(1)}, u32[]{:S(2)}, u32[]{:S(2)}) collective-permute-start(f32[512,128]{1,0:T(8,128)S(1)} %slice.63), channel_id=1, source_target_pairs={{0,24},{8,0},{16,8},{24,16},{32,56},{40,32},{48,40},{56,48},{64,88... | collective-permute-start | bytes 786440 | tf_op jit(solution)/shard_map/ppermute | solution.py:382
  53.2 1.8 %shard_map.74 = (f32[1024,128]{1,0:T(8,128)S(1)}, f32[1024,128]{1,0:T(8,128)S(1)}, f32[1024,128]{1,0:T(8,128)S(1)}, f32[1024,128]{1,0:T(8,128)S(1)}) custom-call(s32[32]{0:T(128)S(1)} %get-tuple-element.95.k_place, s32[32]{0:T(128)S(1)} %compare_convert_fusion.1.k_held, s32[32]{0:T(128)S(1)} %get-tuple-element.97.v_place, s32[32]{0:T(128)S(1)} %get-tuple-element.98.v_held, ...), custom_call_target="tpu_custom_call" | custom-call | flops 1024 | bytes 1024 | tf_op jit(solution)/shard_map/pallas_call | solution.py:48
  55.1 1.6 collective-permute-start.11
  56.7 2.2 %collective-permute-start.12 = (f32[1024,128]{1,0:T(8,128)S(1)}, f32[1024,128]{1,0:T(8,128)S(1)}, u32[]{:S(2)}, u32[]{:S(2)}) collective-permute-start(f32[1024,128]{1,0:T(8,128)S(1)} %get-tuple-element.101), channel_id=1, source_target_pairs={{0,96},{8,104},{16,112},{24,120},{32,64},{40,72},{48,80},{56,88},{... | collective-permute-start | bytes 1572872 | tf_op jit(solution)/shard_map/ppermute | solution.py:382
  59.1 6.4 %collective-permute-done.8.v_far_a = f32[512,128]{1,0:T(8,128)S(1)} collective-permute-done((f32[512,128]{1,0:T(8,128)S(1)}, f32[512,128]{1,0:T(8,128)S(1)}, u32[]{:S(2)}, u32[]{:S(2)}) %collective-permute-start.8) | collective-permute-done | bytes 262176 | tf_op jit(solution)/shard_map/ppermute | solution.py:382
  65.4 3.1 %collective-permute-start.10 = (f32[1024,128]{1,0:T(8,128)S(1)}, f32[1024,128]{1,0:T(8,128)S(1)}, u32[]{:S(2)}, u32[]{:S(2)}) collective-permute-start(f32[1024,128]{1,0:T(8,128)S(1)} %slice.64.refs_2_.k_far), channel_id=1, source_target_pairs={{0,32},{8,40},{32,64},{40,72},{64,96},{72,104},{1,33},{9,41},{33,6... | collective-permute-start | bytes 1572872 | tf_op jit(solution)/shard_map/ppermute | solution.py:382
  68.5 2.8 %collective-permute-start.13 = (f32[1024,128]{1,0:T(8,128)S(1)}, f32[1024,128]{1,0:T(8,128)S(1)}, u32[]{:S(2)}, u32[]{:S(2)}) collective-permute-start(f32[1024,128]{1,0:T(8,128)S(1)} %get-tuple-element.102), channel_id=1, source_target_pairs={{0,8},{8,0},{16,24},{24,16},{32,40},{40,32},{48,56},{56,48},{64,72... | collective-permute-start | bytes 1572872 | tf_op jit(solution)/shard_map/ppermute | solution.py:382
  71.6 7.0 %collective-permute-done.13 = f32[1024,128]{1,0:T(8,128)S(1)} collective-permute-done((f32[1024,128]{1,0:T(8,128)S(1)}, f32[1024,128]{1,0:T(8,128)S(1)}, u32[]{:S(2)}, u32[]{:S(2)}) %collective-permute-start.13) | collective-permute-done | bytes 524320 | tf_op jit(solution)/shard_map/ppermute | solution.py:382
  78.6 1.9 %collective-permute-done.14 = f32[1024,128]{1,0:T(8,128)S(1)} collective-permute-done((f32[1024,128]{1,0:T(8,128)S(1)}, f32[1024,128]{1,0:T(8,128)S(1)}, u32[]{:S(2)}, u32[]{:S(2)}) %collective-permute-start.14) | collective-permute-done | bytes 524320 | tf_op jit(solution)/shard_map/ppermute | solution.py:382
  80.6 1.1 collective-permute-start.15
  81.9 3.0 %collective-permute-start.16 = (f32[1024,128]{1,0:T(8,128)S(1)}, f32[1024,128]{1,0:T(8,128)S(1)}, u32[]{:S(2)}, u32[]{:S(2)}) collective-permute-start(f32[1024,128]{1,0:T(8,128)S(1)} %add.205), channel_id=1, source_target_pairs={{0,32},{8,40},{16,48},{24,56},{32,0},{40,8},{48,16},{56,24},{64,96... | collective-permute-start | bytes 1572872 | tf_op jit(solution)/shard_map/ppermute | solution.py:382
  85.1 6.0 %collective-permute-done.15 = f32[1024,128]{1,0:T(8,128)S(1)} collective-permute-done((f32[1024,128]{1,0:T(8,128)S(1)}, f32[1024,128]{1,0:T(8,128)S(1)}, u32[]{:S(2)}, u32[]{:S(2)}) %collective-permute-start.15) | collective-permute-done | bytes 524320 | tf_op jit(solution)/shard_map/ppermute | solution.py:382
  91.1 1.3 collective-permute-start.18
  92.4 9.6 %shard_map.75 = (f32[1024,512]{1,0:T(8,128)S(1)}, f32[1024,256]{1,0:T(8,128)S(1)}) custom-call(s32[1]{0:T(128)} %bitcast.1.first_row, s32[4,4]{1,0:T(4,128)S(1)} %get-tuple-element.106.back, s32[2]{0:T(128)S(1)} %add_convert_fusion.wraps, f32[1024,512]{1,0:T(8,128)S(1)} %shard_map.73.q, f32[1024,128]{1,0:T(8,128)S(1)} %slice.64.refs_2_.k_far, ...), custom_call_target="tpu_custom_call" | custom-call | flops 100000 | bytes 1024 | tf_op jit(solution)/shard_map/pallas_call | solution.py:179
  102.3 6.3 %shard_map.76.own_a = f32[2,256,512]{2,1,0:T(8,128)S(1)} custom-call(s32[1]{0:T(128)} %bitcast.1.first_row, f32[1024,512]{1,0:T(8,128)S(1)} %shard_map.73.q, f32[1024,512]{1,0:T(8,128)S(1)} %get-tuple-element.119.near, f32[1024,256]{1,0:T(8,128)S(1)} %get-tuple-element.120.stats, f32[1024,128]{1,0:T(8,128)S(1)} %add.208.k_a, f32[1024,128]{1,0:T(8,128)S(1)} %add.209.k_b, ...), custom_call_target="tpu_custom_call" | custom-call | flops 100000 | bytes 1024 | tf_op jit(solution)/shard_map/pallas_call | solution.py:236
  108.6 6.3 %shard_map.77.own_b = f32[2,256,512]{2,1,0:T(8,128)S(1)} custom-call(s32[1]{0:T(128)} %bitcast.1.first_row, f32[1024,512]{1,0:T(8,128)S(1)} %shard_map.73.q, f32[1024,512]{1,0:T(8,128)S(1)} %get-tuple-element.119.near, f32[1024,256]{1,0:T(8,128)S(1)} %get-tuple-element.120.stats, f32[1024,128]{1,0:T(8,128)S(1)} %add.208.k_a, f32[1024,128]{1,0:T(8,128)S(1)} %add.209.k_b, ...), custom_call_target="tpu_custom_call" | custom-call | flops 100000 | bytes 1024 | tf_op jit(solution)/shard_map/pallas_call | solution.py:236
  115.0 1.1 collective-permute-start.22
  116.3 2.2 %collective-permute-start.24 = (f32[256,512]{1,0:T(8,128)S(1)}, f32[256,512]{1,0:T(8,128)S(1)}, u32[]{:S(2)}, u32[]{:S(2)}) collective-permute-start(f32[256,512]{1,0:T(8,128)S(1)} %get-tuple-element.183), channel_id=1, source_target_pairs={{0,6},{1,7},{2,4},{3,5},{4,2},{5,3},{6,0},{7,1},{8,14},{9,15},{10,... | collective-permute-start | bytes 1572872 | tf_op jit(solution)/shard_map/ppermute | solution.py:390
  118.5 1.4 collective-permute-start.23
  119.9 5.4 %shard_map.79.total = f32[2,512,1024]{2,1,0:T(8,128)S(1)} custom-call(s32[4]{0:T(128)S(1)} %get-tuple-element.88.order, f32[2,256,512]{2,1,0:T(8,128)S(1)} %shard_map.76.own_a, f32[2,256,512]{2,1,0:T(8,128)S(1)} %shard_map.77.own_b, f32[512,4096]{1,0:T(8,128)S(1)} %bitcast.37), custom_call_target="tpu_custom_call" | custom-call | flops 100000 | bytes 1024 | tf_op jit(solution)/shard_map/pallas_call | solution.py:303
  125.4 3.8 %collective-permute-done.22.got_b = f32[256,512]{1,0:T(8,128)S(1)} collective-permute-done((f32[256,512]{1,0:T(8,128)S(1)}, f32[256,512]{1,0:T(8,128)S(1)}, u32[]{:S(2)}, u32[]{:S(2)}) %collective-permute-start.22) | collective-permute-done | bytes 524320 | tf_op jit(solution)/shard_map/ppermute | solution.py:390
  129.2 5.3 %shard_map.80 = (f32[2,256,512]{2,1,0:T(8,128)S(1)}, f32[2,256,512]{2,1,0:T(8,128)S(1)}) custom-call(s32[2]{0:T(128)S(1)} %get-tuple-element.87.cores, f32[256,512]{1,0:T(8,128)S(1)} %collective-permute-done.21.got_a, f32[256,512]{1,0:T(8,128)S(1)} %collective-permute-done.22.got_b, f32[512,2048]{1,0:T(8,128)} %collective-permute-done.19.near, ...), custom_call_target="tpu_custom_call" | custom-call | flops 100000 | bytes 1024 | tf_op jit(solution)/shard_map/pallas_call | solution.py:342
  134.8 5.3 %shard_map.81 = (f32[2,256,512]{2,1,0:T(8,128)S(1)}, f32[2,256,512]{2,1,0:T(8,128)S(1)}) custom-call(s32[2]{0:T(128)S(1)} %get-tuple-element.87.cores, f32[256,512]{1,0:T(8,128)S(1)} %collective-permute-done.23.got_a, f32[256,512]{1,0:T(8,128)S(1)} %collective-permute-done.24.got_b, f32[512,2048]{1,0:T(8,128)} %collective-permute-done.19.near, ...), custom_call_target="tpu_custom_call" | custom-call | flops 100000 | bytes 1024 | tf_op jit(solution)/shard_map/pallas_call | solution.py:342
  140.2 0.8 collective-permute-start.26
  141.0 2.3 %collective-permute-done.26 = f32[2,256,512]{2,1,0:T(8,128)S(1)} collective-permute-done((f32[2,256,512]{2,1,0:T(8,128)S(1)}, f32[2,256,512]{2,1,0:T(8,128)S(1)}, u32[]{:S(2)}, u32[]{:S(2)}) %collective-permute-start.26) | collective-permute-done | bytes 1048608 | tf_op jit(solution)/shard_map/ppermute | solution.py:390
  143.9 1.8 %collective-permute-start.27 = (f32[512,512]{1,0:T(8,128)S(1)}, f32[512,512]{1,0:T(8,128)S(1)}, u32[]{:S(2)}, u32[]{:S(2)}) collective-permute-start(f32[512,512]{1,0:T(8,128)S(1)} %get-tuple-element.159), channel_id=1, source_target_pairs={{0,6},{1,7},{2,4},{3,5},{4,2},{5,3},{6,0},{7,1},{8,14},{9,15},{10,... | collective-permute-start | bytes 3145736 | tf_op jit(solution)/shard_map/ppermute | solution.py:390
  145.8 5.4 %shard_map.82.total = f32[2,512,1024]{2,1,0:T(8,128)S(1)} custom-call(s32[4]{0:T(128)S(1)} %get-tuple-element.151.order, f32[2,256,512]{2,1,0:T(8,128)S(1)} %shard_map.76.own_a, f32[2,256,512]{2,1,0:T(8,128)S(1)} %shard_map.77.own_b, f32[512,4096]{1,0:T(8,128)S(1)} %bitcast.37), custom_call_target="tpu_custom_call" | custom-call | flops 100000 | bytes 1024 | tf_op jit(solution)/shard_map/pallas_call | solution.py:303
  151.2 5.3 %shard_map.84 = (f32[2,256,512]{2,1,0:T(8,128)S(1)}, f32[2,256,512]{2,1,0:T(8,128)S(1)}) custom-call(s32[2]{0:T(128)S(1)} %get-tuple-element.87.cores, f32[256,512]{1,0:T(8,128)S(1)} %collective-permute-done.23.got_a, f32[256,512]{1,0:T(8,128)S(1)} %collective-permute-done.24.got_b, f32[512,2048]{1,0:T(8,128)} %collective-permute-done.19.near, ...), custom_call_target="tpu_custom_call" | custom-call | flops 100000 | bytes 1024 | tf_op jit(solution)/shard_map/pallas_call | solution.py:342
  156.5 5.3 %shard_map.83 = (f32[2,256,512]{2,1,0:T(8,128)S(1)}, f32[2,256,512]{2,1,0:T(8,128)S(1)}) custom-call(s32[2]{0:T(128)S(1)} %get-tuple-element.87.cores, f32[256,512]{1,0:T(8,128)S(1)} %collective-permute-done.21.got_a, f32[256,512]{1,0:T(8,128)S(1)} %collective-permute-done.22.got_b, f32[512,2048]{1,0:T(8,128)} %collective-permute-done.19.near, ...), custom_call_target="tpu_custom_call" | custom-call | flops 100000 | bytes 1024 | tf_op jit(solution)/shard_map/pallas_call | solution.py:342
  161.8 8.8 %collective-permute-done.27 = f32[512,512]{1,0:T(8,128)S(1)} collective-permute-done((f32[512,512]{1,0:T(8,128)S(1)}, f32[512,512]{1,0:T(8,128)S(1)}, u32[]{:S(2)}, u32[]{:S(2)}) %collective-permute-start.27) | collective-permute-done | bytes 1048608 | tf_op jit(solution)/shard_map/ppermute | solution.py:390
  170.9 0.5 collective-permute-start.30
  171.4 2.1 %collective-permute-done.29 = f32[2,256,512]{2,1,0:T(8,128)S(1)} collective-permute-done((f32[2,256,512]{2,1,0:T(8,128)S(1)}, f32[2,256,512]{2,1,0:T(8,128)S(1)}, u32[]{:S(2)}, u32[]{:S(2)}) %collective-permute-start.29) | collective-permute-done | bytes 1048608 | tf_op jit(solution)/shard_map/ppermute | solution.py:390
  173.8 1.3 collective-permute-done.30
  175.8 1.5 pad_maximum_fusion
  (101 shorter events, 6.5 us)
Async XLA Ops:
  0.0 17.9 %copy-start = (s32[32,3]{0,1:T(4,128)S(1)}, s32[32,3]{0,1:T(4,128)}, u32[]{:S(2)}) copy-start(s32[32,3]{0,1:T(4,128)} %param.11) | copy-start | bytes 1156
  0.0 22.5 %collective-permute-start.1 = (f32[1024,128]{1,0:T(8,128)}, f32[1024,128]{1,0:T(8,128)S(1)}, u32[]{:S(2)}, u32[]{:S(2)}) collective-permute-start(f32[1024,128]{1,0:T(8,128)} %k_own.1), channel_id=1, source_target_pairs={{0,24},{8,0},{16,8},{24,16},{32,56},{40,32},{48,40},{56,48},{64,88... | collective-permute-start | bytes 1572872 | tf_op jit(solution)/shard_map/ppermute | solution.py:382
  0.5 19.8 %collective-permute-start = (f32[1024,128]{1,0:T(8,128)}, f32[1024,128]{1,0:T(8,128)S(1)}, u32[]{:S(2)}, u32[]{:S(2)}) collective-permute-start(f32[1024,128]{1,0:T(8,128)} %k_own.1), channel_id=1, source_target_pairs={{0,8},{8,16},{16,24},{24,0},{32,40},{40,48},{48,56},{56,32},{64,72... | collective-permute-start | bytes 1572872 | tf_op jit(solution)/shard_map/ppermute | solution.py:382
  2.0 20.5 %collective-permute-start.2 = (f32[1024,128]{1,0:T(8,128)}, f32[1024,128]{1,0:T(8,128)S(1)}, u32[]{:S(2)}, u32[]{:S(2)}) collective-permute-start(f32[1024,128]{1,0:T(8,128)} %v_own.1), channel_id=1, source_target_pairs={{0,32},{8,40},{16,48},{24,56},{32,64},{40,72},{48,80},{56,88},{64,... | collective-permute-start | bytes 1572872 | tf_op jit(solution)/shard_map/ppermute | solution.py:382
  4.5 13.9 %copy-start.5 = (s32[32,8]{0,1:T(8,128)S(1)}, s32[32,8]{0,1:T(8,128)}, u32[]{:S(2)}) copy-start(s32[32,8]{0,1:T(8,128)} %param.10) | copy-start | bytes 3076
  4.5 15.8 %copy-start.2 = (f32[1024,128]{1,0:T(8,128)S(1)}, f32[1024,128]{1,0:T(8,128)}, u32[]{:S(2)}) copy-start(f32[1024,128]{1,0:T(8,128)} %v_own.1) | copy-start | bytes 1572868
  13.5 105.0 %collective-permute-start.19 = (f32[512,2048]{1,0:T(8,128)}, f32[512,2048]{1,0:T(8,128)}, u32[]{:S(2)}, u32[]{:S(2)}) collective-permute-start(f32[512,2048]{1,0:T(8,128)} %get-tuple-element.128), channel_id=1, source_target_pairs={{0,2},{1,3},{2,0},{3,1},{4,6},{5,7},{6,4},{7,5},{8,10},{9,11},{10,... | collective-permute-start | bytes 12582920 | tf_op jit(solution)/shard_map/ppermute | solution.py:390
  15.0 104.9 %collective-permute-start.20 = (f32[512,2048]{1,0:T(8,128)}, f32[512,2048]{1,0:T(8,128)}, u32[]{:S(2)}, u32[]{:S(2)}) collective-permute-start(f32[512,2048]{1,0:T(8,128)} %get-tuple-element.129), channel_id=1, source_target_pairs={{0,6},{1,7},{2,4},{3,5},{4,2},{5,3},{6,0},{7,1},{8,14},{9,15},{10,... | collective-permute-start | bytes 12582920 | tf_op jit(solution)/shard_map/ppermute | solution.py:390
  20.3 12.5 %collective-permute-start.4 = (f32[1024,128]{1,0:T(8,128)S(1)}, f32[1024,128]{1,0:T(8,128)S(1)}, u32[]{:S(2)}, u32[]{:S(2)}) collective-permute-start(f32[1024,128]{1,0:T(8,128)S(1)} %copy-done.2), channel_id=1, source_target_pairs={{0,96},{8,104},{16,112},{24,120},{32,0},{40,8},{48,16},{56,24},{64... | collective-permute-start | bytes 1572872 | tf_op jit(solution)/shard_map/ppermute | solution.py:382
  22.5 11.8 %collective-permute-start.7 = (f32[1024,128]{1,0:T(8,128)S(1)}, f32[1024,128]{1,0:T(8,128)S(1)}, u32[]{:S(2)}, u32[]{:S(2)}) collective-permute-start(f32[1024,128]{1,0:T(8,128)S(1)} %collective-permute-done.refs_3_.k_left), channel_id=1, source_target_pairs={{0,32},{32,64},{64,96},{1,33},{33,65},{65,97},{2,34},{34,66},{66,9... | collective-permute-start | bytes 1572872 | tf_op jit(solution)/shard_map/ppermute | solution.py:382
  23.3 29.9 %copy-start.3 = (f32[1024,128]{1,0:T(8,128)S(1)}, f32[1024,128]{1,0:T(8,128)}, u32[]{:S(2)}) copy-start(f32[1024,128]{1,0:T(8,128)} %k_own.1) | copy-start | bytes 1572868
  23.4 17.9 %collective-permute-start.3 = (f32[1536,128]{1,0:T(8,128)S(1)}, f32[1536,128]{1,0:T(8,128)S(1)}, u32[]{:S(2)}, u32[]{:S(2)}) collective-permute-start(f32[1536,128]{1,0:T(8,128)S(1)} %pad_maximum_fusion.1), channel_id=1, source_target_pairs={{0,24},{8,0},{16,8},{24,16},{32,56},{40,32},{48,40},{56,48},{64,88... | collective-permute-start | bytes 2359304 | tf_op jit(solution)/shard_map/ppermute | solution.py:382
  32.8 17.3 %collective-permute-start.6 = (f32[1536,128]{1,0:T(8,128)S(1)}, f32[1536,128]{1,0:T(8,128)S(1)}, u32[]{:S(2)}, u32[]{:S(2)}) collective-permute-start(f32[1536,128]{1,0:T(8,128)S(1)} %pad_maximum_fusion.2), channel_id=1, source_target_pairs={{0,8},{8,16},{16,24},{24,0},{32,40},{40,48},{48,56},{56,32},{64,72... | collective-permute-start | bytes 2359304 | tf_op jit(solution)/shard_map/ppermute | solution.py:382
  34.3 15.8 %collective-permute-start.5 = (f32[1024,128]{1,0:T(8,128)S(1)}, f32[1024,128]{1,0:T(8,128)S(1)}, u32[]{:S(2)}, u32[]{:S(2)}) collective-permute-start(f32[1024,128]{1,0:T(8,128)S(1)} %collective-permute-done.4.refs_5_), channel_id=1, source_target_pairs={{0,96},{8,104},{16,112},{24,120},{32,0},{40,8},{48,16},{56,24},{64... | collective-permute-start | bytes 1572872 | tf_op jit(solution)/shard_map/ppermute | solution.py:382
  50.2 21.1 %copy-start.4 = (f32[1024,512]{1,0:T(8,128)S(1)}, f32[1024,512]{1,0:T(8,128)}, u32[]{:S(2)}) copy-start(f32[1024,512]{1,0:T(8,128)} %q.1) | copy-start | bytes 6291460
  50.2 8.8 %collective-permute-start.9 = (f32[512,128]{1,0:T(8,128)S(1)}, f32[512,128]{1,0:T(8,128)S(1)}, u32[]{:S(2)}, u32[]{:S(2)}) collective-permute-start(f32[512,128]{1,0:T(8,128)S(1)} %slice.63), channel_id=1, source_target_pairs={{0,24},{8,0},{16,8},{24,16},{32,56},{40,32},{48,40},{56,48},{64,88... | collective-permute-start | bytes 786440 | tf_op jit(solution)/shard_map/ppermute | solution.py:382
  55.1 13.4 %collective-permute-start.11 = (f32[1024,128]{1,0:T(8,128)S(1)}, f32[1024,128]{1,0:T(8,128)S(1)}, u32[]{:S(2)}, u32[]{:S(2)}) collective-permute-start(f32[1024,128]{1,0:T(8,128)S(1)} %get-tuple-element.100), channel_id=1, source_target_pairs={{0,32},{8,40},{16,48},{24,56},{32,0},{40,8},{48,16},{56,24},{64,96... | collective-permute-start | bytes 1572872 | tf_op jit(solution)/shard_map/ppermute | solution.py:382
  56.7 14.6 %collective-permute-start.12 = (f32[1024,128]{1,0:T(8,128)S(1)}, f32[1024,128]{1,0:T(8,128)S(1)}, u32[]{:S(2)}, u32[]{:S(2)}) collective-permute-start(f32[1024,128]{1,0:T(8,128)S(1)} %get-tuple-element.101), channel_id=1, source_target_pairs={{0,96},{8,104},{16,112},{24,120},{32,64},{40,72},{48,80},{56,88},{... | collective-permute-start | bytes 1572872 | tf_op jit(solution)/shard_map/ppermute | solution.py:382
  59.0 6.4 %collective-permute-start.8 = (f32[512,128]{1,0:T(8,128)S(1)}, f32[512,128]{1,0:T(8,128)S(1)}, u32[]{:S(2)}, u32[]{:S(2)}) collective-permute-start(f32[512,128]{1,0:T(8,128)S(1)} %slice.62), channel_id=1, source_target_pairs={{0,8},{8,16},{16,24},{24,0},{32,40},{40,48},{48,56},{56,32},{64,72... | collective-permute-start | bytes 786440 | tf_op jit(solution)/shard_map/ppermute | solution.py:382
  65.4 15.1 %collective-permute-start.10 = (f32[1024,128]{1,0:T(8,128)S(1)}, f32[1024,128]{1,0:T(8,128)S(1)}, u32[]{:S(2)}, u32[]{:S(2)}) collective-permute-start(f32[1024,128]{1,0:T(8,128)S(1)} %slice.64.refs_2_.k_far), channel_id=1, source_target_pairs={{0,32},{8,40},{32,64},{40,72},{64,96},{72,104},{1,33},{9,41},{33,6... | collective-permute-start | bytes 1572872 | tf_op jit(solution)/shard_map/ppermute | solution.py:382
  68.5 10.1 %collective-permute-start.13 = (f32[1024,128]{1,0:T(8,128)S(1)}, f32[1024,128]{1,0:T(8,128)S(1)}, u32[]{:S(2)}, u32[]{:S(2)}) collective-permute-start(f32[1024,128]{1,0:T(8,128)S(1)} %get-tuple-element.102), channel_id=1, source_target_pairs={{0,8},{8,0},{16,24},{24,16},{32,40},{40,32},{48,56},{56,48},{64,72... | collective-permute-start | bytes 1572872 | tf_op jit(solution)/shard_map/ppermute | solution.py:382
  71.3 9.2 %collective-permute-start.14 = (f32[1024,128]{1,0:T(8,128)S(1)}, f32[1024,128]{1,0:T(8,128)S(1)}, u32[]{:S(2)}, u32[]{:S(2)}) collective-permute-start(f32[1024,128]{1,0:T(8,128)S(1)} %get-tuple-element.103), channel_id=1, source_target_pairs={{0,24},{8,16},{16,8},{24,0},{32,56},{40,48},{48,40},{56,32},{64,88... | collective-permute-start | bytes 1572872 | tf_op jit(solution)/shard_map/ppermute | solution.py:382
  80.6 10.5 %collective-permute-start.15 = (f32[1024,128]{1,0:T(8,128)S(1)}, f32[1024,128]{1,0:T(8,128)S(1)}, u32[]{:S(2)}, u32[]{:S(2)}) collective-permute-start(f32[1024,128]{1,0:T(8,128)S(1)} %add.204), channel_id=1, source_target_pairs={{0,96},{8,104},{16,112},{24,120},{32,64},{40,72},{48,80},{56,88},{... | collective-permute-start | bytes 1572872 | tf_op jit(solution)/shard_map/ppermute | solution.py:382
  81.9 20.2 %collective-permute-start.16 = (f32[1024,128]{1,0:T(8,128)S(1)}, f32[1024,128]{1,0:T(8,128)S(1)}, u32[]{:S(2)}, u32[]{:S(2)}) collective-permute-start(f32[1024,128]{1,0:T(8,128)S(1)} %add.205), channel_id=1, source_target_pairs={{0,32},{8,40},{16,48},{24,56},{32,0},{40,8},{48,16},{56,24},{64,96... | collective-permute-start | bytes 1572872 | tf_op jit(solution)/shard_map/ppermute | solution.py:382
  84.9 17.2 %collective-permute-start.17 = (f32[1024,128]{1,0:T(8,128)S(1)}, f32[1024,128]{1,0:T(8,128)S(1)}, u32[]{:S(2)}, u32[]{:S(2)}) collective-permute-start(f32[1024,128]{1,0:T(8,128)S(1)} %add.206), channel_id=1, source_target_pairs={{0,24},{8,16},{16,8},{24,0},{32,56},{40,48},{48,40},{56,32},{64,88... | collective-permute-start | bytes 1572872 | tf_op jit(solution)/shard_map/ppermute | solution.py:382
  91.1 11.0 %collective-permute-start.18 = (f32[1024,128]{1,0:T(8,128)S(1)}, f32[1024,128]{1,0:T(8,128)S(1)}, u32[]{:S(2)}, u32[]{:S(2)}) collective-permute-start(f32[1024,128]{1,0:T(8,128)S(1)} %add.207), channel_id=1, source_target_pairs={{0,8},{8,0},{16,24},{24,16},{32,40},{40,32},{48,56},{56,48},{64,72... | collective-permute-start | bytes 1572872 | tf_op jit(solution)/shard_map/ppermute | solution.py:382
  102.3 17.6 %slice-start = ((s8[8388608]{0:T(1024)(128)(4,1)}), s8[4194304]{0:T(1024)(128)(4,1)S(1)}, s32[]{:S(2)}) async-start(s8[8388608]{0:T(1024)(128)(4,1)} %bitcast.36), calls=%async_computation | async-start | bytes 8388608
  108.6 11.3 %slice-start.1 = ((s8[8388608]{0:T(1024)(128)(4,1)}), s8[4194304]{0:T(1024)(128)(4,1)S(1)}, s32[]{:S(2)}) async-start(s8[8388608]{0:T(1024)(128)(4,1)} %bitcast.36), calls=%async_computation.1 | async-start | bytes 8388608
  115.0 14.2 %collective-permute-start.22 = (f32[256,512]{1,0:T(8,128)S(1)}, f32[256,512]{1,0:T(8,128)S(1)}, u32[]{:S(2)}, u32[]{:S(2)}) collective-permute-start(f32[256,512]{1,0:T(8,128)S(1)} %get-tuple-element.185), channel_id=1, source_target_pairs={{0,6},{1,7},{2,4},{3,5},{4,2},{5,3},{6,0},{7,1},{8,14},{9,15},{10,... | collective-permute-start | bytes 1572872 | tf_op jit(solution)/shard_map/ppermute | solution.py:390
  116.2 13.1 %collective-permute-start.21 = (f32[256,512]{1,0:T(8,128)S(1)}, f32[256,512]{1,0:T(8,128)S(1)}, u32[]{:S(2)}, u32[]{:S(2)}) collective-permute-start(f32[256,512]{1,0:T(8,128)S(1)} %get-tuple-element.186), channel_id=1, source_target_pairs={{0,2},{1,3},{2,0},{3,1},{4,6},{5,7},{6,4},{7,5},{8,10},{9,11},{10,... | collective-permute-start | bytes 1572872 | tf_op jit(solution)/shard_map/ppermute | solution.py:390
  116.3 18.5 %collective-permute-start.24 = (f32[256,512]{1,0:T(8,128)S(1)}, f32[256,512]{1,0:T(8,128)S(1)}, u32[]{:S(2)}, u32[]{:S(2)}) collective-permute-start(f32[256,512]{1,0:T(8,128)S(1)} %get-tuple-element.183), channel_id=1, source_target_pairs={{0,6},{1,7},{2,4},{3,5},{4,2},{5,3},{6,0},{7,1},{8,14},{9,15},{10,... | collective-permute-start | bytes 1572872 | tf_op jit(solution)/shard_map/ppermute | solution.py:390
  118.5 16.3 %collective-permute-start.23 = (f32[256,512]{1,0:T(8,128)S(1)}, f32[256,512]{1,0:T(8,128)S(1)}, u32[]{:S(2)}, u32[]{:S(2)}) collective-permute-start(f32[256,512]{1,0:T(8,128)S(1)} %get-tuple-element.184), channel_id=1, source_target_pairs={{0,2},{1,3},{2,0},{3,1},{4,6},{5,7},{6,4},{7,5},{8,10},{9,11},{10,... | collective-permute-start | bytes 1572872 | tf_op jit(solution)/shard_map/ppermute | solution.py:390
  134.8 5.3 %collective-permute-start.25 = (f32[2,256,512]{2,1,0:T(8,128)S(1)}, f32[2,256,512]{2,1,0:T(8,128)S(1)}, u32[]{:S(2)}, u32[]{:S(2)}) collective-permute-start(f32[2,256,512]{2,1,0:T(8,128)S(1)} %get-tuple-element.143), channel_id=1, source_target_pairs={{0,1},{1,0},{2,3},{3,2},{4,5},{5,4},{6,7},{7,6},{8,9},{9,8},{10,11... | collective-permute-start | bytes 3145736 | tf_op jit(solution)/shard_map/ppermute | solution.py:390
  140.2 3.1 %collective-permute-start.26 = (f32[2,256,512]{2,1,0:T(8,128)S(1)}, f32[2,256,512]{2,1,0:T(8,128)S(1)}, u32[]{:S(2)}, u32[]{:S(2)}) collective-permute-start(f32[2,256,512]{2,1,0:T(8,128)S(1)} %get-tuple-element.146), channel_id=1, source_target_pairs={{0,1},{1,0},{2,3},{3,2},{4,5},{5,4},{6,7},{7,6},{8,9},{9,8},{10,11... | collective-permute-start | bytes 3145736 | tf_op jit(solution)/shard_map/ppermute | solution.py:390
  143.9 26.7 %collective-permute-start.27 = (f32[512,512]{1,0:T(8,128)S(1)}, f32[512,512]{1,0:T(8,128)S(1)}, u32[]{:S(2)}, u32[]{:S(2)}) collective-permute-start(f32[512,512]{1,0:T(8,128)S(1)} %get-tuple-element.159), channel_id=1, source_target_pairs={{0,6},{1,7},{2,4},{3,5},{4,2},{5,3},{6,0},{7,1},{8,14},{9,15},{10,... | collective-permute-start | bytes 3145736 | tf_op jit(solution)/shard_map/ppermute | solution.py:390
  145.8 25.1 %collective-permute-start.28 = (f32[512,512]{1,0:T(8,128)S(1)}, f32[512,512]{1,0:T(8,128)S(1)}, u32[]{:S(2)}, u32[]{:S(2)}) collective-permute-start(f32[512,512]{1,0:T(8,128)S(1)} %get-tuple-element.160), channel_id=1, source_target_pairs={{0,2},{1,3},{2,0},{3,1},{4,6},{5,7},{6,4},{7,5},{8,10},{9,11},{10,... | collective-permute-start | bytes 3145736 | tf_op jit(solution)/shard_map/ppermute | solution.py:390
  170.9 2.7 %collective-permute-start.29 = (f32[2,256,512]{2,1,0:T(8,128)S(1)}, f32[2,256,512]{2,1,0:T(8,128)S(1)}, u32[]{:S(2)}, u32[]{:S(2)}) collective-permute-start(f32[2,256,512]{2,1,0:T(8,128)S(1)} %get-tuple-element.162), channel_id=1, source_target_pairs={{0,1},{1,0},{2,3},{3,2},{4,5},{5,4},{6,7},{7,6},{8,9},{9,8},{10,11... | collective-permute-start | bytes 3145736 | tf_op jit(solution)/shard_map/ppermute | solution.py:390
  170.9 4.2 %collective-permute-start.30 = (f32[2,256,512]{2,1,0:T(8,128)S(1)}, f32[2,256,512]{2,1,0:T(8,128)S(1)}, u32[]{:S(2)}, u32[]{:S(2)}) collective-permute-start(f32[2,256,512]{2,1,0:T(8,128)S(1)} %get-tuple-element.166), channel_id=1, source_target_pairs={{0,1},{1,0},{2,3},{3,2},{4,5},{5,4},{6,7},{7,6},{8,9},{9,8},{10,11... | collective-permute-start | bytes 3145736 | tf_op jit(solution)/shard_map/ppermute | solution.py:390
  175.8 1.5 copy-start.1

commit v11 on v10

--- a/solution.py
+++ b/solution.py
@@ -315,18 +315,25 @@
     )(order, own_a, own_b, weight)
 
 
-def pair_kernel(cores, got_a, got_b, near, far, total, there, here, x):
+def pair_kernel(cores, got_a, got_b, near, far, total, *refs):
+    *there, here, x = refs
+    width = here.shape[2] * 2 // len(there)
     for kind, (got, weight) in enumerate(((got_a, near), (got_b, far))):
 
         @pl.when((pl.program_id(0) == kind) & (pl.program_id(1) == 0))
         def _():
             x[...] = stack(got[...])
 
-        for side, out in enumerate((there, here)):
-
-            @pl.when((pl.program_id(0) == kind) & (pl.program_id(1) == side))
-            def _():
-                out[0] = total[0] + weight_term(x[...], weight[...])
+        @pl.when((pl.program_id(0) == kind) & (pl.program_id(1) == 0))
+        def _():
+            term = total[0] + weight_term(x[...], weight[...])
+            mine = there[kind * len(there) // 2 : (kind + 1) * len(there) // 2]
+            for at, out in enumerate(mine):
+                out[...] = term[:, at * width : (at + 1) * width]
+
+        @pl.when((pl.program_id(0) == kind) & (pl.program_id(1) == 1))
+        def _():
+            here[0] = total[0] + weight_term(x[...], weight[...])
 
 
 def project_pair(got, near, far, total, unit, keep, cores):
@@ -334,14 +341,15 @@
     width = depth
     base = 0 if keep else 2
     vmem = pl.BlockSpec(memory_space=pltpu.VMEM)
-    out = jax.ShapeDtypeStruct((2, rows, width), jnp.float32)
-    out_spec = pl.BlockSpec((1, rows, width), lambda k, s, c: (k, 0, 0))
+    pieces = 4 if keep else 2
+    here = jax.ShapeDtypeStruct((2, rows, width), jnp.float32)
+    there = jax.ShapeDtypeStruct((rows, 2 * width // pieces), jnp.float32)
     w_spec = lambda side: pl.BlockSpec(
         (depth, width), lambda k, s, c: (0, base + c[side(k, s)])
     )
-    return pl.pallas_call(
+    *there, here = pl.pallas_call(
         pair_kernel,
-        out_shape=[out, out],
+        out_shape=[there] * pieces + [here],
         grid_spec=pltpu.PrefetchScalarGridSpec(
             num_scalar_prefetch=1,
             grid=(2, 2),
@@ -352,12 +360,14 @@
                 w_spec(lambda k, s: jnp.where(k == 0, 0, s)),
                 pl.BlockSpec((1, rows, width), lambda k, s, c: (k, unit, s)),
             ],
-            out_specs=[out_spec, out_spec],
+            out_specs=[pl.BlockSpec(there.shape, lambda k, s, c: (0, 0))] * pieces
+            + [pl.BlockSpec((1, rows, width), lambda k, s, c: (k, 0, 0))],
             scratch_shapes=[pltpu.VMEM((2 * rows, depth), jnp.bfloat16)],
         ),
         compiler_params=pltpu.CompilerParams(vmem_limit_bytes=16 << 20),
         cost_estimate=LARGE,
     )(cores, *got, near, far, total)
+    return there, here
 
 
 def body(
@@ -476,21 +486,24 @@
     )
     there_a, here_a = product(got_a, total, 0, False)
     there_a, here_a, got_a, got_b = lax.optimization_barrier((there_a, here_a, got_a, got_b))
-    moved_a = over_head(there_a, 1)
+    across = lambda parts: [over_head(a, 1) for a in parts]
+    moved_a = across(there_a)
     there_b, here_b = product(got_b, total, 1, False)
     there_b, here_b, moved_a = lax.optimization_barrier((there_b, here_b, moved_a))
-    here = jnp.concatenate([here_a, here_b], axis=1)
-    passed = here + jnp.concatenate([moved_a, over_head(there_b, 1)], axis=1)
-    passed = [passed[0], passed[1]]
+    moved = zip(moved_a, across(there_b))
+    passed = [
+        jnp.concatenate([here_a[i] + a, here_b[i] + b]) for i, (a, b) in enumerate(moved)
+    ]
     passed, got_a, got_b, own_b = lax.optimization_barrier((passed, got_a, got_b, own_b))
     sent = ending(passed)
     kept_total = project_chip(own_a, own_b, out_weight, keep_order)
     keep_a = product(got_a, kept_total, 0, True)
     keep_b = product(got_b, kept_total, 1, True)
-    keep_a, keep_b, sent = lax.optimization_barrier((keep_a, keep_b, sent))
-    kept_a, kept_b = (here + over_head(there, 1) for there, here in (keep_a, keep_b))
-    kept = (kept_a[0], kept_a[1], kept_b[0], kept_b[1])
-    rows = kept_a.shape[1]
+    kept = []
+    for there, here in (keep_a, keep_b):
+        moved = across(there)
+        kept += [here[i] + jnp.concatenate(moved[2 * i : 2 * i + 2], axis=1) for i in range(2)]
+    rows = kept[0].shape[0]
     sent = (sent[0][:rows], sent[1][:rows], sent[0][rows:], sent[1][rows:])
     return jnp.concatenate([a + b for a, b in zip(kept, sent)], axis=0)
 

time: 179 us -> 173 us (0.966)
  waiting for transfers between devices: 59.5 us -> 53 us
  starting transfers between devices: 44.4 us -> 46.6 us
    ppermute x12 -> x20, waiting for transfers between devices: 18.9 us -> 12.5 us  [body(): lax.ppermute(a, 'head', [(i, i ^ bits) for i in range(head_size)])]
    ppermute x12 -> x20, starting transfers between devices: 11.7 us -> 13.9 us  [body(): lax.ppermute(a, 'head', [(i, i ^ bits) for i in range(head_size)])]
  transfers between devices with their start and end apart: 31 -> 39, of which waited for: 14 -> 16; matrix products, arithmetic and copies ran while one was open for 2% -> 2% of each run, Pallas kernels for 37% -> 38%
where the time goes in v11:
time: 173 us
  Pallas kernels  65.3 us (38%)
  waiting for transfers between devices  53 us (31%)
  starting transfers between devices  46.6 us (27%)
  other arithmetic  4.64 us (3%)
  local copies, waits for them, and re-layouts  1.8 us (1%)
    ppermute x19, waiting for transfers between devices, body(): send = lambda a, pairs: lax.ppermute(a, 'seq', pairs)  40.6 us
    ppermute x19, starting transfers between devices, body(): send = lambda a, pairs: lax.ppermute(a, 'seq', pairs)  32.7 us
    pallas_call x4, Pallas kernels, project_pair(): pl.pallas_call(pair_kernel, out_shape=[there] * pieces + [here], grid_spe...  21.3 us
    ppermute x20, starting transfers between devices, body(): lax.ppermute(a, 'head', [(i, i ^ bits) for i in range(head_size)])  13.9 us
    pallas_call x2, Pallas kernels, attend(): pl.pallas_call(functools.partial(attend_kernel, start), grid=(2, heads //...  12.6 us
    ppermute x20, waiting for transfers between devices, body(): lax.ppermute(a, 'head', [(i, i ^ bits) for i in range(head_size)])  12.5 us
    pallas_call x2, Pallas kernels, project_chip(): pl.pallas_call(chip_kernel, out_shape=jax.ShapeDtypeStruct((2, 2 * rows,...  10.8 us
    pallas_call x1, Pallas kernels, attend_near(): pl.pallas_call(functools.partial(near_kernel, start), grid=(rows // TILE,...  9.64 us
  transfers between devices with their start and end apart: 39, of which 16 were waited for; matrix products, arithmetic and copies ran while one was open for 2% of the time, Pallas kernels for 38%

profile of v11, /device:TPU:2, one launch (start us, length us, event | category | flops | bytes accessed | tf_op | source)
XLA Modules:
  0.0 172.6 jit_solution(10116684677227818457)
XLA Ops:
  0.5 1.6 collective-permute-start
  2.0 1.9 %collective-permute-start.2 = (f32[1024,128]{1,0:T(8,128)}, f32[1024,128]{1,0:T(8,128)S(1)}, u32[]{:S(2)}, u32[]{:S(2)}) collective-permute-start(f32[1024,128]{1,0:T(8,128)} %v_own.1), channel_id=1, source_target_pairs={{0,32},{8,40},{16,48},{24,56},{32,64},{40,72},{48,80},{56,88},{64,... | collective-permute-start | bytes 1572872 | tf_op jit(solution)/shard_map/ppermute | solution.py:392
  3.9 0.5 add_xor_fusion.chips
  4.5 8.9 %shard_map.78 = (f32[512,2048]{1,0:T(8,128)}, f32[512,2048]{1,0:T(8,128)}) custom-call(s32[3]{0:T(128)} %add_xor_fusion.chips, f32[512,4096]{1,0:T(8,128)} %w.3, f32[512,4096]{1,0:T(8,128)} %w.3, f32[512,4096]{1,0:T(8,128)} %w.3), custom_call_target="tpu_custom_call" | custom-call | flops 1024 | bytes 1024 | tf_op jit(solution)/shard_map/pallas_call | solution.py:266
  13.4 1.6 collective-permute-start.19
  15.0 2.2 %collective-permute-start.20 = (f32[512,2048]{1,0:T(8,128)}, f32[512,2048]{1,0:T(8,128)}, u32[]{:S(2)}, u32[]{:S(2)}) collective-permute-start(f32[512,2048]{1,0:T(8,128)} %get-tuple-element.134), channel_id=1, source_target_pairs={{0,6},{1,7},{2,4},{3,5},{4,2},{5,3},{6,0},{7,1},{8,14},{9,15},{10,... | collective-permute-start | bytes 12582920 | tf_op jit(solution)/shard_map/ppermute | solution.py:400
  20.2 2.2 %collective-permute-start.4 = (f32[1024,128]{1,0:T(8,128)S(1)}, f32[1024,128]{1,0:T(8,128)S(1)}, u32[]{:S(2)}, u32[]{:S(2)}) collective-permute-start(f32[1024,128]{1,0:T(8,128)S(1)} %copy-done.2), channel_id=1, source_target_pairs={{0,96},{8,104},{16,112},{24,120},{32,0},{40,8},{48,16},{56,24},{64... | collective-permute-start | bytes 1572872 | tf_op jit(solution)/shard_map/ppermute | solution.py:392
  22.4 0.7 collective-permute-start.7
  23.3 2.5 %collective-permute-start.3 = (f32[1536,128]{1,0:T(8,128)S(1)}, f32[1536,128]{1,0:T(8,128)S(1)}, u32[]{:S(2)}, u32[]{:S(2)}) collective-permute-start(f32[1536,128]{1,0:T(8,128)S(1)} %pad_maximum_fusion.3), channel_id=1, source_target_pairs={{0,24},{8,0},{16,8},{24,16},{32,56},{40,32},{48,40},{56,48},{64,88... | collective-permute-start | bytes 2359304 | tf_op jit(solution)/shard_map/ppermute | solution.py:392
  25.9 6.9 %collective-permute-done.4.refs_5_ = f32[1024,128]{1,0:T(8,128)S(1)} collective-permute-done((f32[1024,128]{1,0:T(8,128)S(1)}, f32[1024,128]{1,0:T(8,128)S(1)}, u32[]{:S(2)}, u32[]{:S(2)}) %collective-permute-start.4) | collective-permute-done | bytes 524320 | tf_op jit(solution)/shard_map/ppermute | solution.py:392
  32.8 1.5 collective-permute-start.6
  34.2 3.4 %collective-permute-start.5 = (f32[1024,128]{1,0:T(8,128)S(1)}, f32[1024,128]{1,0:T(8,128)S(1)}, u32[]{:S(2)}, u32[]{:S(2)}) collective-permute-start(f32[1024,128]{1,0:T(8,128)S(1)} %collective-permute-done.4.refs_5_), channel_id=1, source_target_pairs={{0,96},{8,104},{16,112},{24,120},{32,0},{40,8},{48,16},{56,24},{64... | collective-permute-start | bytes 1572872 | tf_op jit(solution)/shard_map/ppermute | solution.py:392
  37.7 3.6 %collective-permute-done.3 = f32[1536,128]{1,0:T(8,128)S(1)} collective-permute-done((f32[1536,128]{1,0:T(8,128)S(1)}, f32[1536,128]{1,0:T(8,128)S(1)}, u32[]{:S(2)}, u32[]{:S(2)}) %collective-permute-start.3) | collective-permute-done | bytes 786464 | tf_op jit(solution)/shard_map/ppermute | solution.py:392
  41.3 8.8 %collective-permute-done.6 = f32[1536,128]{1,0:T(8,128)S(1)} collective-permute-done((f32[1536,128]{1,0:T(8,128)S(1)}, f32[1536,128]{1,0:T(8,128)S(1)}, u32[]{:S(2)}, u32[]{:S(2)}) %collective-permute-start.6) | collective-permute-done | bytes 786464 | tf_op jit(solution)/shard_map/ppermute | solution.py:392
  50.2 3.0 %collective-permute-start.9 = (f32[512,128]{1,0:T(8,128)S(1)}, f32[512,128]{1,0:T(8,128)S(1)}, u32[]{:S(2)}, u32[]{:S(2)}) collective-permute-start(f32[512,128]{1,0:T(8,128)S(1)} %slice.69), channel_id=1, source_target_pairs={{0,24},{8,0},{16,8},{24,16},{32,56},{40,32},{48,40},{56,48},{64,88... | collective-permute-start | bytes 786440 | tf_op jit(solution)/shard_map/ppermute | solution.py:392
  53.2 1.8 %shard_map.74 = (f32[1024,128]{1,0:T(8,128)S(1)}, f32[1024,128]{1,0:T(8,128)S(1)}, f32[1024,128]{1,0:T(8,128)S(1)}, f32[1024,128]{1,0:T(8,128)S(1)}) custom-call(s32[32]{0:T(128)S(1)} %get-tuple-element.100.k_place, s32[32]{0:T(128)S(1)} %compare_convert_fusion.1.k_held, s32[32]{0:T(128)S(1)} %get-tuple-element.102.v_place, ...), custom_call_target="tpu_custom_call" | custom-call | flops 1024 | bytes 1024 | tf_op jit(solution)/shard_map/pallas_call | solution.py:48
  55.0 1.6 collective-permute-start.11
  56.7 2.2 %collective-permute-start.12 = (f32[1024,128]{1,0:T(8,128)S(1)}, f32[1024,128]{1,0:T(8,128)S(1)}, u32[]{:S(2)}, u32[]{:S(2)}) collective-permute-start(f32[1024,128]{1,0:T(8,128)S(1)} %get-tuple-element.106), channel_id=1, source_target_pairs={{0,96},{8,104},{16,112},{24,120},{32,64},{40,72},{48,80},{56,88},{... | collective-permute-start | bytes 1572872 | tf_op jit(solution)/shard_map/ppermute | solution.py:392
  59.0 6.4 %collective-permute-done.8.v_far_a = f32[512,128]{1,0:T(8,128)S(1)} collective-permute-done((f32[512,128]{1,0:T(8,128)S(1)}, f32[512,128]{1,0:T(8,128)S(1)}, u32[]{:S(2)}, u32[]{:S(2)}) %collective-permute-start.8) | collective-permute-done | bytes 262176 | tf_op jit(solution)/shard_map/ppermute | solution.py:392
  65.4 3.1 %collective-permute-start.10 = (f32[1024,128]{1,0:T(8,128)S(1)}, f32[1024,128]{1,0:T(8,128)S(1)}, u32[]{:S(2)}, u32[]{:S(2)}) collective-permute-start(f32[1024,128]{1,0:T(8,128)S(1)} %slice.70.refs_2_.k_far), channel_id=1, source_target_pairs={{0,32},{8,40},{32,64},{40,72},{64,96},{72,104},{1,33},{9,41},{33,6... | collective-permute-start | bytes 1572872 | tf_op jit(solution)/shard_map/ppermute | solution.py:392
  68.5 2.8 %collective-permute-start.13 = (f32[1024,128]{1,0:T(8,128)S(1)}, f32[1024,128]{1,0:T(8,128)S(1)}, u32[]{:S(2)}, u32[]{:S(2)}) collective-permute-start(f32[1024,128]{1,0:T(8,128)S(1)} %get-tuple-element.107), channel_id=1, source_target_pairs={{0,8},{8,0},{16,24},{24,16},{32,40},{40,32},{48,56},{56,48},{64,72... | collective-permute-start | bytes 1572872 | tf_op jit(solution)/shard_map/ppermute | solution.py:392
  71.5 7.0 %collective-permute-done.13 = f32[1024,128]{1,0:T(8,128)S(1)} collective-permute-done((f32[1024,128]{1,0:T(8,128)S(1)}, f32[1024,128]{1,0:T(8,128)S(1)}, u32[]{:S(2)}, u32[]{:S(2)}) %collective-permute-start.13) | collective-permute-done | bytes 524320 | tf_op jit(solution)/shard_map/ppermute | solution.py:392
  78.6 1.9 %collective-permute-done.14 = f32[1024,128]{1,0:T(8,128)S(1)} collective-permute-done((f32[1024,128]{1,0:T(8,128)S(1)}, f32[1024,128]{1,0:T(8,128)S(1)}, u32[]{:S(2)}, u32[]{:S(2)}) %collective-permute-start.14) | collective-permute-done | bytes 524320 | tf_op jit(solution)/shard_map/ppermute | solution.py:392
  80.5 1.1 collective-permute-start.15
  81.8 3.0 %collective-permute-start.16 = (f32[1024,128]{1,0:T(8,128)S(1)}, f32[1024,128]{1,0:T(8,128)S(1)}, u32[]{:S(2)}, u32[]{:S(2)}) collective-permute-start(f32[1024,128]{1,0:T(8,128)S(1)} %add.220), channel_id=1, source_target_pairs={{0,32},{8,40},{16,48},{24,56},{32,0},{40,8},{48,16},{56,24},{64,96... | collective-permute-start | bytes 1572872 | tf_op jit(solution)/shard_map/ppermute | solution.py:392
  85.0 6.0 %collective-permute-done.15 = f32[1024,128]{1,0:T(8,128)S(1)} collective-permute-done((f32[1024,128]{1,0:T(8,128)S(1)}, f32[1024,128]{1,0:T(8,128)S(1)}, u32[]{:S(2)}, u32[]{:S(2)}) %collective-permute-start.15) | collective-permute-done | bytes 524320 | tf_op jit(solution)/shard_map/ppermute | solution.py:392
  91.0 1.3 collective-permute-start.18
  92.3 9.6 %shard_map.75 = (f32[1024,512]{1,0:T(8,128)S(1)}, f32[1024,256]{1,0:T(8,128)S(1)}) custom-call(s32[1]{0:T(128)} %bitcast.1.first_row, s32[4,4]{1,0:T(4,128)S(1)} %get-tuple-element.111.back, s32[2]{0:T(128)S(1)} %add_convert_fusion.wraps, f32[1024,512]{1,0:T(8,128)S(1)} %shard_map.73.q, f32[1024,128]{1,0:T(8,128)S(1)} %slice.70.refs_2_.k_far, ...), custom_call_target="tpu_custom_call" | custom-call | flops 100000 | bytes 1024 | tf_op jit(solution)/shard_map/pallas_call | solution.py:179
  102.3 6.3 %shard_map.76.own_a = f32[2,256,512]{2,1,0:T(8,128)S(1)} custom-call(s32[1]{0:T(128)} %bitcast.1.first_row, f32[1024,512]{1,0:T(8,128)S(1)} %shard_map.73.q, f32[1024,512]{1,0:T(8,128)S(1)} %get-tuple-element.124.near, f32[1024,256]{1,0:T(8,128)S(1)} %get-tuple-element.125.stats, f32[1024,128]{1,0:T(8,128)S(1)} %add.223.k_a, f32[1024,128]{1,0:T(8,128)S(1)} %add.224.k_b, ...), custom_call_target="tpu_custom_call" | custom-call | flops 100000 | bytes 1024 | tf_op jit(solution)/shard_map/pallas_call | solution.py:236
  108.6 6.3 %shard_map.77.own_b = f32[2,256,512]{2,1,0:T(8,128)S(1)} custom-call(s32[1]{0:T(128)} %bitcast.1.first_row, f32[1024,512]{1,0:T(8,128)S(1)} %shard_map.73.q, f32[1024,512]{1,0:T(8,128)S(1)} %get-tuple-element.124.near, f32[1024,256]{1,0:T(8,128)S(1)} %get-tuple-element.125.stats, f32[1024,128]{1,0:T(8,128)S(1)} %add.223.k_a, f32[1024,128]{1,0:T(8,128)S(1)} %add.224.k_b, ...), custom_call_target="tpu_custom_call" | custom-call | flops 100000 | bytes 1024 | tf_op jit(solution)/shard_map/pallas_call | solution.py:236
  115.0 1.1 collective-permute-start.22
  116.2 2.2 %collective-permute-start.24 = (f32[256,512]{1,0:T(8,128)S(1)}, f32[256,512]{1,0:T(8,128)S(1)}, u32[]{:S(2)}, u32[]{:S(2)}) collective-permute-start(f32[256,512]{1,0:T(8,128)S(1)} %get-tuple-element.195), channel_id=1, source_target_pairs={{0,6},{1,7},{2,4},{3,5},{4,2},{5,3},{6,0},{7,1},{8,14},{9,15},{10,... | collective-permute-start | bytes 1572872 | tf_op jit(solution)/shard_map/ppermute | solution.py:400
  118.5 1.4 collective-permute-start.23
  119.9 5.4 %shard_map.79.total = f32[2,512,1024]{2,1,0:T(8,128)S(1)} custom-call(s32[4]{0:T(128)S(1)} %get-tuple-element.93.order, f32[2,256,512]{2,1,0:T(8,128)S(1)} %shard_map.76.own_a, f32[2,256,512]{2,1,0:T(8,128)S(1)} %shard_map.77.own_b, f32[512,4096]{1,0:T(8,128)S(1)} %bitcast.33), custom_call_target="tpu_custom_call" | custom-call | flops 100000 | bytes 1024 | tf_op jit(solution)/shard_map/pallas_call | solution.py:303
  125.3 3.8 %collective-permute-done.22.got_b = f32[256,512]{1,0:T(8,128)S(1)} collective-permute-done((f32[256,512]{1,0:T(8,128)S(1)}, f32[256,512]{1,0:T(8,128)S(1)}, u32[]{:S(2)}, u32[]{:S(2)}) %collective-permute-start.22) | collective-permute-done | bytes 524320 | tf_op jit(solution)/shard_map/ppermute | solution.py:400
  129.1 5.3 %shard_map.80 = (f32[256,512]{1,0:T(8,128)S(1)}, f32[256,512]{1,0:T(8,128)S(1)}, f32[2,256,512]{2,1,0:T(8,128)S(1)}) custom-call(s32[2]{0:T(128)S(1)} %get-tuple-element.92.cores, f32[256,512]{1,0:T(8,128)S(1)} %collective-permute-done.21.got_a, f32[256,512]{1,0:T(8,128)S(1)} %collective-permute-done.22.got_b, f32[512,2048]{1,0:T(8,128)} %collective-permute-done.19.near, ...), custom_call_target="tpu_custom_call" | custom-call | flops 100000 | bytes 1024 | tf_op jit(solution)/shard_map/pallas_call | solution.py:350
  135.3 5.3 %shard_map.81 = (f32[256,512]{1,0:T(8,128)S(1)}, f32[256,512]{1,0:T(8,128)S(1)}, f32[2,256,512]{2,1,0:T(8,128)S(1)}) custom-call(s32[2]{0:T(128)S(1)} %get-tuple-element.92.cores, f32[256,512]{1,0:T(8,128)S(1)} %collective-permute-done.23.got_a, f32[256,512]{1,0:T(8,128)S(1)} %collective-permute-done.24.got_b, f32[512,2048]{1,0:T(8,128)} %collective-permute-done.19.near, ...), custom_call_target="tpu_custom_call" | custom-call | flops 100000 | bytes 1024 | tf_op jit(solution)/shard_map/pallas_call | solution.py:350
  141.4 1.2 collective-permute-done.27
  142.6 0.7 collective-permute-done.28
  143.7 1.8 %collective-permute-start.31 = (f32[512,512]{1,0:T(8,128)S(1)}, f32[512,512]{1,0:T(8,128)S(1)}, u32[]{:S(2)}, u32[]{:S(2)}) collective-permute-start(f32[512,512]{1,0:T(8,128)S(1)} %pad_maximum_fusion.1), channel_id=1, source_target_pairs={{0,6},{1,7},{2,4},{3,5},{4,2},{5,3},{6,0},{7,1},{8,14},{9,15},{10,... | collective-permute-start | bytes 3145736 | tf_op jit(solution)/shard_map/ppermute | solution.py:400
  145.5 5.4 %shard_map.82.total = f32[2,512,1024]{2,1,0:T(8,128)S(1)} custom-call(s32[4]{0:T(128)S(1)} %get-tuple-element.161.order, f32[2,256,512]{2,1,0:T(8,128)S(1)} %shard_map.76.own_a, f32[2,256,512]{2,1,0:T(8,128)S(1)} %shard_map.77.own_b, f32[512,4096]{1,0:T(8,128)S(1)} %bitcast.33), custom_call_target="tpu_custom_call" | custom-call | flops 100000 | bytes 1024 | tf_op jit(solution)/shard_map/pallas_call | solution.py:303
  150.9 5.3 %shard_map.84 = (f32[256,256]{1,0:T(8,128)S(1)}, f32[256,256]{1,0:T(8,128)S(1)}, f32[256,256]{1,0:T(8,128)S(1)}, f32[256,256]{1,0:T(8,128)S(1)}, f32[2,256,512]{2,1,0:T(8,128)S(1)}) custom-call(s32[2]{0:T(128)S(1)} %get-tuple-element.92.cores, f32[256,512]{1,0:T(8,128)S(1)} %collective-permute-done.23.got_a, f32[256,512]{1,0:T(8,128)S(1)} %collective-permute-done.24.got_b, ...), custom_call_target="tpu_custom_call" | custom-call | flops 100000 | bytes 1024 | tf_op jit(solution)/shard_map/pallas_call | solution.py:350
  157.0 5.3 %shard_map.83 = (f32[256,256]{1,0:T(8,128)S(1)}, f32[256,256]{1,0:T(8,128)S(1)}, f32[256,256]{1,0:T(8,128)S(1)}, f32[256,256]{1,0:T(8,128)S(1)}, f32[2,256,512]{2,1,0:T(8,128)S(1)}) custom-call(s32[2]{0:T(128)S(1)} %get-tuple-element.92.cores, f32[256,512]{1,0:T(8,128)S(1)} %collective-permute-done.21.got_a, f32[256,512]{1,0:T(8,128)S(1)} %collective-permute-done.22.got_b, ...), custom_call_target="tpu_custom_call" | custom-call | flops 100000 | bytes 1024 | tf_op jit(solution)/shard_map/pallas_call | solution.py:350
  163.3 0.6 collective-permute-done.38
  164.7 0.8 collective-permute-done.32
  165.9 4.3 %collective-permute-done.31 = f32[512,512]{1,0:T(8,128)S(1)} collective-permute-done((f32[512,512]{1,0:T(8,128)S(1)}, f32[512,512]{1,0:T(8,128)S(1)}, u32[]{:S(2)}, u32[]{:S(2)}) %collective-permute-start.31) | collective-permute-done | bytes 1048608 | tf_op jit(solution)/shard_map/ppermute | solution.py:400
  170.4 0.6 slice_add_fusion.3
  171.1 1.5 pad_maximum_fusion
  (117 shorter events, 9.3 us)
Async XLA Ops:
  0.0 17.8 %copy-start = (s32[32,3]{0,1:T(4,128)S(1)}, s32[32,3]{0,1:T(4,128)}, u32[]{:S(2)}) copy-start(s32[32,3]{0,1:T(4,128)} %param.11) | copy-start | bytes 1156
  0.0 22.4 %collective-permute-start.1 = (f32[1024,128]{1,0:T(8,128)}, f32[1024,128]{1,0:T(8,128)S(1)}, u32[]{:S(2)}, u32[]{:S(2)}) collective-permute-start(f32[1024,128]{1,0:T(8,128)} %k_own.1), channel_id=1, source_target_pairs={{0,24},{8,0},{16,8},{24,16},{32,56},{40,32},{48,40},{56,48},{64,88... | collective-permute-start | bytes 1572872 | tf_op jit(solution)/shard_map/ppermute | solution.py:392
  0.5 19.8 %collective-permute-start = (f32[1024,128]{1,0:T(8,128)}, f32[1024,128]{1,0:T(8,128)S(1)}, u32[]{:S(2)}, u32[]{:S(2)}) collective-permute-start(f32[1024,128]{1,0:T(8,128)} %k_own.1), channel_id=1, source_target_pairs={{0,8},{8,16},{16,24},{24,0},{32,40},{40,48},{48,56},{56,32},{64,72... | collective-permute-start | bytes 1572872 | tf_op jit(solution)/shard_map/ppermute | solution.py:392
  2.0 20.4 %collective-permute-start.2 = (f32[1024,128]{1,0:T(8,128)}, f32[1024,128]{1,0:T(8,128)S(1)}, u32[]{:S(2)}, u32[]{:S(2)}) collective-permute-start(f32[1024,128]{1,0:T(8,128)} %v_own.1), channel_id=1, source_target_pairs={{0,32},{8,40},{16,48},{24,56},{32,64},{40,72},{48,80},{56,88},{64,... | collective-permute-start | bytes 1572872 | tf_op jit(solution)/shard_map/ppermute | solution.py:392
  4.5 13.8 %copy-start.5 = (s32[32,8]{0,1:T(8,128)S(1)}, s32[32,8]{0,1:T(8,128)}, u32[]{:S(2)}) copy-start(s32[32,8]{0,1:T(8,128)} %param.10) | copy-start | bytes 3076
  4.5 15.8 %copy-start.2 = (f32[1024,128]{1,0:T(8,128)S(1)}, f32[1024,128]{1,0:T(8,128)}, u32[]{:S(2)}) copy-start(f32[1024,128]{1,0:T(8,128)} %v_own.1) | copy-start | bytes 1572868
  13.4 105.0 %collective-permute-start.19 = (f32[512,2048]{1,0:T(8,128)}, f32[512,2048]{1,0:T(8,128)}, u32[]{:S(2)}, u32[]{:S(2)}) collective-permute-start(f32[512,2048]{1,0:T(8,128)} %get-tuple-element.133), channel_id=1, source_target_pairs={{0,2},{1,3},{2,0},{3,1},{4,6},{5,7},{6,4},{7,5},{8,10},{9,11},{10,... | collective-permute-start | bytes 12582920 | tf_op jit(solution)/shard_map/ppermute | solution.py:400
  15.0 104.9 %collective-permute-start.20 = (f32[512,2048]{1,0:T(8,128)}, f32[512,2048]{1,0:T(8,128)}, u32[]{:S(2)}, u32[]{:S(2)}) collective-permute-start(f32[512,2048]{1,0:T(8,128)} %get-tuple-element.134), channel_id=1, source_target_pairs={{0,6},{1,7},{2,4},{3,5},{4,2},{5,3},{6,0},{7,1},{8,14},{9,15},{10,... | collective-permute-start | bytes 12582920 | tf_op jit(solution)/shard_map/ppermute | solution.py:400
  20.2 12.5 %collective-permute-start.4 = (f32[1024,128]{1,0:T(8,128)S(1)}, f32[1024,128]{1,0:T(8,128)S(1)}, u32[]{:S(2)}, u32[]{:S(2)}) collective-permute-start(f32[1024,128]{1,0:T(8,128)S(1)} %copy-done.2), channel_id=1, source_target_pairs={{0,96},{8,104},{16,112},{24,120},{32,0},{40,8},{48,16},{56,24},{64... | collective-permute-start | bytes 1572872 | tf_op jit(solution)/shard_map/ppermute | solution.py:392
  22.4 11.8 %collective-permute-start.7 = (f32[1024,128]{1,0:T(8,128)S(1)}, f32[1024,128]{1,0:T(8,128)S(1)}, u32[]{:S(2)}, u32[]{:S(2)}) collective-permute-start(f32[1024,128]{1,0:T(8,128)S(1)} %collective-permute-done.refs_3_.k_left), channel_id=1, source_target_pairs={{0,32},{32,64},{64,96},{1,33},{33,65},{65,97},{2,34},{34,66},{66,9... | collective-permute-start | bytes 1572872 | tf_op jit(solution)/shard_map/ppermute | solution.py:392
  23.3 29.9 %copy-start.3 = (f32[1024,128]{1,0:T(8,128)S(1)}, f32[1024,128]{1,0:T(8,128)}, u32[]{:S(2)}) copy-start(f32[1024,128]{1,0:T(8,128)} %k_own.1) | copy-start | bytes 1572868
  23.3 17.9 %collective-permute-start.3 = (f32[1536,128]{1,0:T(8,128)S(1)}, f32[1536,128]{1,0:T(8,128)S(1)}, u32[]{:S(2)}, u32[]{:S(2)}) collective-permute-start(f32[1536,128]{1,0:T(8,128)S(1)} %pad_maximum_fusion.3), channel_id=1, source_target_pairs={{0,24},{8,0},{16,8},{24,16},{32,56},{40,32},{48,40},{56,48},{64,88... | collective-permute-start | bytes 2359304 | tf_op jit(solution)/shard_map/ppermute | solution.py:392
  32.8 17.3 %collective-permute-start.6 = (f32[1536,128]{1,0:T(8,128)S(1)}, f32[1536,128]{1,0:T(8,128)S(1)}, u32[]{:S(2)}, u32[]{:S(2)}) collective-permute-start(f32[1536,128]{1,0:T(8,128)S(1)} %pad_maximum_fusion.4), channel_id=1, source_target_pairs={{0,8},{8,16},{16,24},{24,0},{32,40},{40,48},{48,56},{56,32},{64,72... | collective-permute-start | bytes 2359304 | tf_op jit(solution)/shard_map/ppermute | solution.py:392
  34.2 15.8 %collective-permute-start.5 = (f32[1024,128]{1,0:T(8,128)S(1)}, f32[1024,128]{1,0:T(8,128)S(1)}, u32[]{:S(2)}, u32[]{:S(2)}) collective-permute-start(f32[1024,128]{1,0:T(8,128)S(1)} %collective-permute-done.4.refs_5_), channel_id=1, source_target_pairs={{0,96},{8,104},{16,112},{24,120},{32,0},{40,8},{48,16},{56,24},{64... | collective-permute-start | bytes 1572872 | tf_op jit(solution)/shard_map/ppermute | solution.py:392
  50.2 21.1 %copy-start.4 = (f32[1024,512]{1,0:T(8,128)S(1)}, f32[1024,512]{1,0:T(8,128)}, u32[]{:S(2)}) copy-start(f32[1024,512]{1,0:T(8,128)} %q.1) | copy-start | bytes 6291460
  50.2 8.8 %collective-permute-start.9 = (f32[512,128]{1,0:T(8,128)S(1)}, f32[512,128]{1,0:T(8,128)S(1)}, u32[]{:S(2)}, u32[]{:S(2)}) collective-permute-start(f32[512,128]{1,0:T(8,128)S(1)} %slice.69), channel_id=1, source_target_pairs={{0,24},{8,0},{16,8},{24,16},{32,56},{40,32},{48,40},{56,48},{64,88... | collective-permute-start | bytes 786440 | tf_op jit(solution)/shard_map/ppermute | solution.py:392
  55.0 13.4 %collective-permute-start.11 = (f32[1024,128]{1,0:T(8,128)S(1)}, f32[1024,128]{1,0:T(8,128)S(1)}, u32[]{:S(2)}, u32[]{:S(2)}) collective-permute-start(f32[1024,128]{1,0:T(8,128)S(1)} %get-tuple-element.105), channel_id=1, source_target_pairs={{0,32},{8,40},{16,48},{24,56},{32,0},{40,8},{48,16},{56,24},{64,96... | collective-permute-start | bytes 1572872 | tf_op jit(solution)/shard_map/ppermute | solution.py:392
  56.7 14.6 %collective-permute-start.12 = (f32[1024,128]{1,0:T(8,128)S(1)}, f32[1024,128]{1,0:T(8,128)S(1)}, u32[]{:S(2)}, u32[]{:S(2)}) collective-permute-start(f32[1024,128]{1,0:T(8,128)S(1)} %get-tuple-element.106), channel_id=1, source_target_pairs={{0,96},{8,104},{16,112},{24,120},{32,64},{40,72},{48,80},{56,88},{... | collective-permute-start | bytes 1572872 | tf_op jit(solution)/shard_map/ppermute | solution.py:392
  58.9 6.4 %collective-permute-start.8 = (f32[512,128]{1,0:T(8,128)S(1)}, f32[512,128]{1,0:T(8,128)S(1)}, u32[]{:S(2)}, u32[]{:S(2)}) collective-permute-start(f32[512,128]{1,0:T(8,128)S(1)} %slice.68), channel_id=1, source_target_pairs={{0,8},{8,16},{16,24},{24,0},{32,40},{40,48},{48,56},{56,32},{64,72... | collective-permute-start | bytes 786440 | tf_op jit(solution)/shard_map/ppermute | solution.py:392
  65.4 15.1 %collective-permute-start.10 = (f32[1024,128]{1,0:T(8,128)S(1)}, f32[1024,128]{1,0:T(8,128)S(1)}, u32[]{:S(2)}, u32[]{:S(2)}) collective-permute-start(f32[1024,128]{1,0:T(8,128)S(1)} %slice.70.refs_2_.k_far), channel_id=1, source_target_pairs={{0,32},{8,40},{32,64},{40,72},{64,96},{72,104},{1,33},{9,41},{33,6... | collective-permute-start | bytes 1572872 | tf_op jit(solution)/shard_map/ppermute | solution.py:392
  68.5 10.1 %collective-permute-start.13 = (f32[1024,128]{1,0:T(8,128)S(1)}, f32[1024,128]{1,0:T(8,128)S(1)}, u32[]{:S(2)}, u32[]{:S(2)}) collective-permute-start(f32[1024,128]{1,0:T(8,128)S(1)} %get-tuple-element.107), channel_id=1, source_target_pairs={{0,8},{8,0},{16,24},{24,16},{32,40},{40,32},{48,56},{56,48},{64,72... | collective-permute-start | bytes 1572872 | tf_op jit(solution)/shard_map/ppermute | solution.py:392
  71.3 9.2 %collective-permute-start.14 = (f32[1024,128]{1,0:T(8,128)S(1)}, f32[1024,128]{1,0:T(8,128)S(1)}, u32[]{:S(2)}, u32[]{:S(2)}) collective-permute-start(f32[1024,128]{1,0:T(8,128)S(1)} %get-tuple-element.108), channel_id=1, source_target_pairs={{0,24},{8,16},{16,8},{24,0},{32,56},{40,48},{48,40},{56,32},{64,88... | collective-permute-start | bytes 1572872 | tf_op jit(solution)/shard_map/ppermute | solution.py:392
  80.5 10.5 %collective-permute-start.15 = (f32[1024,128]{1,0:T(8,128)S(1)}, f32[1024,128]{1,0:T(8,128)S(1)}, u32[]{:S(2)}, u32[]{:S(2)}) collective-permute-start(f32[1024,128]{1,0:T(8,128)S(1)} %add.219), channel_id=1, source_target_pairs={{0,96},{8,104},{16,112},{24,120},{32,64},{40,72},{48,80},{56,88},{... | collective-permute-start | bytes 1572872 | tf_op jit(solution)/shard_map/ppermute | solution.py:392
  81.8 20.2 %collective-permute-start.16 = (f32[1024,128]{1,0:T(8,128)S(1)}, f32[1024,128]{1,0:T(8,128)S(1)}, u32[]{:S(2)}, u32[]{:S(2)}) collective-permute-start(f32[1024,128]{1,0:T(8,128)S(1)} %add.220), channel_id=1, source_target_pairs={{0,32},{8,40},{16,48},{24,56},{32,0},{40,8},{48,16},{56,24},{64,96... | collective-permute-start | bytes 1572872 | tf_op jit(solution)/shard_map/ppermute | solution.py:392
  84.8 17.2 %collective-permute-start.17 = (f32[1024,128]{1,0:T(8,128)S(1)}, f32[1024,128]{1,0:T(8,128)S(1)}, u32[]{:S(2)}, u32[]{:S(2)}) collective-permute-start(f32[1024,128]{1,0:T(8,128)S(1)} %add.221), channel_id=1, source_target_pairs={{0,24},{8,16},{16,8},{24,0},{32,56},{40,48},{48,40},{56,32},{64,88... | collective-permute-start | bytes 1572872 | tf_op jit(solution)/shard_map/ppermute | solution.py:392
  91.0 11.0 %collective-permute-start.18 = (f32[1024,128]{1,0:T(8,128)S(1)}, f32[1024,128]{1,0:T(8,128)S(1)}, u32[]{:S(2)}, u32[]{:S(2)}) collective-permute-start(f32[1024,128]{1,0:T(8,128)S(1)} %add.222), channel_id=1, source_target_pairs={{0,8},{8,0},{16,24},{24,16},{32,40},{40,32},{48,56},{56,48},{64,72... | collective-permute-start | bytes 1572872 | tf_op jit(solution)/shard_map/ppermute | solution.py:392
  102.3 17.6 %slice-start = ((s8[8388608]{0:T(1024)(128)(4,1)}), s8[4194304]{0:T(1024)(128)(4,1)S(1)}, s32[]{:S(2)}) async-start(s8[8388608]{0:T(1024)(128)(4,1)} %bitcast.32), calls=%async_computation | async-start | bytes 8388608
  108.6 11.3 %slice-start.1 = ((s8[8388608]{0:T(1024)(128)(4,1)}), s8[4194304]{0:T(1024)(128)(4,1)S(1)}, s32[]{:S(2)}) async-start(s8[8388608]{0:T(1024)(128)(4,1)} %bitcast.32), calls=%async_computation.1 | async-start | bytes 8388608
  115.0 14.1 %collective-permute-start.22 = (f32[256,512]{1,0:T(8,128)S(1)}, f32[256,512]{1,0:T(8,128)S(1)}, u32[]{:S(2)}, u32[]{:S(2)}) collective-permute-start(f32[256,512]{1,0:T(8,128)S(1)} %get-tuple-element.197), channel_id=1, source_target_pairs={{0,6},{1,7},{2,4},{3,5},{4,2},{5,3},{6,0},{7,1},{8,14},{9,15},{10,... | collective-permute-start | bytes 1572872 | tf_op jit(solution)/shard_map/ppermute | solution.py:400
  116.1 13.0 %collective-permute-start.21 = (f32[256,512]{1,0:T(8,128)S(1)}, f32[256,512]{1,0:T(8,128)S(1)}, u32[]{:S(2)}, u32[]{:S(2)}) collective-permute-start(f32[256,512]{1,0:T(8,128)S(1)} %get-tuple-element.198), channel_id=1, source_target_pairs={{0,2},{1,3},{2,0},{3,1},{4,6},{5,7},{6,4},{7,5},{8,10},{9,11},{10,... | collective-permute-start | bytes 1572872 | tf_op jit(solution)/shard_map/ppermute | solution.py:400
  116.2 18.5 %collective-permute-start.24 = (f32[256,512]{1,0:T(8,128)S(1)}, f32[256,512]{1,0:T(8,128)S(1)}, u32[]{:S(2)}, u32[]{:S(2)}) collective-permute-start(f32[256,512]{1,0:T(8,128)S(1)} %get-tuple-element.195), channel_id=1, source_target_pairs={{0,6},{1,7},{2,4},{3,5},{4,2},{5,3},{6,0},{7,1},{8,14},{9,15},{10,... | collective-permute-start | bytes 1572872 | tf_op jit(solution)/shard_map/ppermute | solution.py:400
  118.5 16.3 %collective-permute-start.23 = (f32[256,512]{1,0:T(8,128)S(1)}, f32[256,512]{1,0:T(8,128)S(1)}, u32[]{:S(2)}, u32[]{:S(2)}) collective-permute-start(f32[256,512]{1,0:T(8,128)S(1)} %get-tuple-element.196), channel_id=1, source_target_pairs={{0,2},{1,3},{2,0},{3,1},{4,6},{5,7},{6,4},{7,5},{8,10},{9,11},{10,... | collective-permute-start | bytes 1572872 | tf_op jit(solution)/shard_map/ppermute | solution.py:400
  134.7 5.8 %collective-permute-start.25 = (f32[256,512]{1,0:T(8,128)S(1)}, f32[256,512]{1,0:T(8,128)S(1)}, u32[]{:S(2)}, u32[]{:S(2)}) collective-permute-start(f32[256,512]{1,0:T(8,128)S(1)} %get-tuple-element.150), channel_id=1, source_target_pairs={{0,1},{1,0},{2,3},{3,2},{4,5},{5,4},{6,7},{7,6},{8,9},{9,8},{10,11... | collective-permute-start | bytes 1572872 | tf_op jit(solution)/shard_map/ppermute | solution.py:400
  134.7 5.8 %collective-permute-start.26 = (f32[256,512]{1,0:T(8,128)S(1)}, f32[256,512]{1,0:T(8,128)S(1)}, u32[]{:S(2)}, u32[]{:S(2)}) collective-permute-start(f32[256,512]{1,0:T(8,128)S(1)} %get-tuple-element.151), channel_id=1, source_target_pairs={{0,1},{1,0},{2,3},{3,2},{4,5},{5,4},{6,7},{7,6},{8,9},{9,8},{10,11... | collective-permute-start | bytes 1572872 | tf_op jit(solution)/shard_map/ppermute | solution.py:400
  140.6 2.0 %collective-permute-start.27 = (f32[256,512]{1,0:T(8,128)S(1)}, f32[256,512]{1,0:T(8,128)S(1)}, u32[]{:S(2)}, u32[]{:S(2)}) collective-permute-start(f32[256,512]{1,0:T(8,128)S(1)} %get-tuple-element.154), channel_id=1, source_target_pairs={{0,1},{1,0},{2,3},{3,2},{4,5},{5,4},{6,7},{7,6},{8,9},{9,8},{10,11... | collective-permute-start | bytes 1572872 | tf_op jit(solution)/shard_map/ppermute | solution.py:400
  140.7 2.6 %collective-permute-start.28 = (f32[256,512]{1,0:T(8,128)S(1)}, f32[256,512]{1,0:T(8,128)S(1)}, u32[]{:S(2)}, u32[]{:S(2)}) collective-permute-start(f32[256,512]{1,0:T(8,128)S(1)} %get-tuple-element.156), channel_id=1, source_target_pairs={{0,1},{1,0},{2,3},{3,2},{4,5},{5,4},{6,7},{7,6},{8,9},{9,8},{10,11... | collective-permute-start | bytes 1572872 | tf_op jit(solution)/shard_map/ppermute | solution.py:400
  143.7 26.5 %collective-permute-start.31 = (f32[512,512]{1,0:T(8,128)S(1)}, f32[512,512]{1,0:T(8,128)S(1)}, u32[]{:S(2)}, u32[]{:S(2)}) collective-permute-start(f32[512,512]{1,0:T(8,128)S(1)} %pad_maximum_fusion.1), channel_id=1, source_target_pairs={{0,6},{1,7},{2,4},{3,5},{4,2},{5,3},{6,0},{7,1},{8,14},{9,15},{10,... | collective-permute-start | bytes 3145736 | tf_op jit(solution)/shard_map/ppermute | solution.py:400
  145.5 24.9 %collective-permute-start.34 = (f32[512,512]{1,0:T(8,128)S(1)}, f32[512,512]{1,0:T(8,128)S(1)}, u32[]{:S(2)}, u32[]{:S(2)}) collective-permute-start(f32[512,512]{1,0:T(8,128)S(1)} %pad_maximum_fusion.2), channel_id=1, source_target_pairs={{0,2},{1,3},{2,0},{3,1},{4,6},{5,7},{6,4},{7,5},{8,10},{9,11},{10,... | collective-permute-start | bytes 3145736 | tf_op jit(solution)/shard_map/ppermute | solution.py:400
  156.3 6.0 %collective-permute-start.35 = (f32[256,256]{1,0:T(8,128)S(1)}, f32[256,256]{1,0:T(8,128)S(1)}, u32[]{:S(2)}, u32[]{:S(2)}) collective-permute-start(f32[256,256]{1,0:T(8,128)S(1)} %get-tuple-element.173), channel_id=1, source_target_pairs={{0,1},{1,0},{2,3},{3,2},{4,5},{5,4},{6,7},{7,6},{8,9},{9,8},{10,11... | collective-permute-start | bytes 786440 | tf_op jit(solution)/shard_map/ppermute | solution.py:400
  156.4 6.4 %collective-permute-start.36 = (f32[256,256]{1,0:T(8,128)S(1)}, f32[256,256]{1,0:T(8,128)S(1)}, u32[]{:S(2)}, u32[]{:S(2)}) collective-permute-start(f32[256,256]{1,0:T(8,128)S(1)} %get-tuple-element.174), channel_id=1, source_target_pairs={{0,1},{1,0},{2,3},{3,2},{4,5},{5,4},{6,7},{7,6},{8,9},{9,8},{10,11... | collective-permute-start | bytes 786440 | tf_op jit(solution)/shard_map/ppermute | solution.py:400
  156.9 6.0 %collective-permute-start.37 = (f32[256,256]{1,0:T(8,128)S(1)}, f32[256,256]{1,0:T(8,128)S(1)}, u32[]{:S(2)}, u32[]{:S(2)}) collective-permute-start(f32[256,256]{1,0:T(8,128)S(1)} %get-tuple-element.175), channel_id=1, source_target_pairs={{0,1},{1,0},{2,3},{3,2},{4,5},{5,4},{6,7},{7,6},{8,9},{9,8},{10,11... | collective-permute-start | bytes 786440 | tf_op jit(solution)/shard_map/ppermute | solution.py:400
  162.3 1.7 collective-permute-start.38
  162.8 1.5 collective-permute-start.29
  162.9 1.8 %collective-permute-start.30 = (f32[256,256]{1,0:T(8,128)S(1)}, f32[256,256]{1,0:T(8,128)S(1)}, u32[]{:S(2)}, u32[]{:S(2)}) collective-permute-start(f32[256,256]{1,0:T(8,128)S(1)} %get-tuple-element.165), channel_id=1, source_target_pairs={{0,1},{1,0},{2,3},{3,2},{4,5},{5,4},{6,7},{7,6},{8,9},{9,8},{10,11... | collective-permute-start | bytes 786440 | tf_op jit(solution)/shard_map/ppermute | solution.py:400
  163.9 1.5 collective-permute-start.32
  164.3 1.5 collective-permute-start.33
  171.1 1.5 copy-start.1

commit v12 on v11

--- a/solution.py
+++ b/solution.py
@@ -252,24 +252,33 @@
 
 
 def take_kernel(chips, one, two, three, near, far):
-    width = one.shape[1]
-    near[:, :width], near[:, width:] = one[...], two[...]
-    far[:, :width], far[:, width:] = three[...], two[...]
+    step = pl.program_id(0)
+
+    @pl.when(step < 4)
+    def _():
+        near[...], far[...] = one[...], three[...]
+
+    @pl.when(step >= 4)
+    def _():
+        near[...], far[...] = two[...], two[...]
 
 
 def take_columns(weight, chips, width):
     rows = weight.shape[0]
-    step = rows // 8
+    part = width // 4
     out = jax.ShapeDtypeStruct((rows, 2 * width), jnp.float32)
-    out_spec = pl.BlockSpec((step, 2 * width), lambda i, o: (i, 0))
-    w_spec = lambda at: pl.BlockSpec((step, width), lambda i, o: (i, o[at]))
+    out_spec = pl.BlockSpec((rows, part), lambda i, o: (0, i))
+    early = lambda at: pl.BlockSpec(
+        (rows, part), lambda i, o: (0, 4 * o[at] + jnp.minimum(i, 3))
+    )
+    late = pl.BlockSpec((rows, part), lambda i, o: (0, 4 * o[1] + jnp.maximum(i - 4, 0)))
     return pl.pallas_call(
         take_kernel,
         out_shape=[out, out],
         grid_spec=pltpu.PrefetchScalarGridSpec(
             num_scalar_prefetch=1,
-            grid=(rows // step,),
-            in_specs=[w_spec(0), w_spec(1), w_spec(2)],
+            grid=(8,),
+            in_specs=[early(0), late, early(2)],
             out_specs=[out_spec, out_spec],
         ),
         compiler_params=pltpu.CompilerParams(vmem_limit_bytes=58 << 20),
@@ -402,6 +411,12 @@
     near_weight, far_weight = take_columns(out_weight, y ^ jnp.arange(1, 4), 2 * width)
     near_weight, far_weight = over_head(near_weight, 2), over_head(far_weight, 6)
 
+    (k_left, late_values), (vertical_blocks, slash_offsets, prompt_length) = (
+        lax.optimization_barrier(
+            ((k_left, value_vectors), (vertical_blocks, slash_offsets, prompt_length))
+        )
+    )
+    v_above = send(late_values, down)
     vert = lax.dynamic_slice_in_dim(vertical_blocks, head_index * heads, heads, 0)
     slash = lax.dynamic_slice_in_dim(slash_offsets, head_index * heads, heads, 0)
     prompt = prompt_length[0]
@@ -430,12 +445,6 @@
     orders = (pass_order, keep_order, cores)
     small = (vert_pos, slash_pos, first_row, back, wraps, orders, k_place, k_held, v_place, v_held)
 
-    k_left, late_values = lax.optimization_barrier((k_left, value_vectors))
-    v_above = send(late_values, down)
-    (k_left, k_right, v_below), small = lax.optimization_barrier(
-        ((k_left, k_right, v_below), small)
-    )
-    vert_pos, slash_pos, first_row, back, wraps, orders, k_place, k_held, v_place, v_held = small
     half = rows // 2
     source = jnp.where(x >= 2, v_below, value_vectors)
     v_left = jnp.where(x == 3, v_below, value_vectors)
@@ -443,9 +452,10 @@
     v_beyond = send(v_above, down)
     moved_right = send(jnp.concatenate([v_left, source[:half]]), right)
     k_left_wrap = send(k_left, [(i, i + 4) for i in ids if i % 4 == 0 and i + 4 in ids])
-    moved_left, v_beyond, moved_right, k_left_wrap = lax.optimization_barrier(
-        (moved_left, v_beyond, moved_right, k_left_wrap)
-    )
+    (moved_left, v_beyond, moved_right, k_left_wrap), small = lax.optimization_barrier(
+        ((moved_left, v_beyond, moved_right, k_left_wrap), small)
+    )
+    vert_pos, slash_pos, first_row, back, wraps, orders, k_place, k_held, v_place, v_held = small
     k_far, v_far_b = moved_left[:rows], moved_left[rows:]
     v_left, v_far_a = moved_right[:rows], moved_right[rows:]
 

time: 173 us -> 176 us (1.017)
  local copies, waits for them, and re-layouts: 1.8 us -> 5.68 us
  waiting for transfers between devices: 53 us -> 50 us
  other arithmetic: 4.64 us -> 6.47 us
    ppermute x19, waiting for transfers between devices: 40.6 us -> 38.1 us  [body(): send = lambda a, pairs: lax.ppermute(a, 'seq', pairs)]
    slice x2, local copies, waits for them, and re-layouts: 0.05 us -> 2.05 us  [body(): k_far, v_far_b = (moved_left[:rows], moved_left[rows:])]
    slice x2, local copies, waits for them, and re-layouts: 0.05 us -> 2.04 us  [body(): v_left, v_far_a = (moved_right[:rows], moved_right[rows:])]
  transfers between devices with their start and end apart: 39 -> 39, of which waited for: 16 -> 16; matrix products, arithmetic and copies ran while one was open for 2% -> 5% of each run, Pallas kernels for 38% -> 38%
where the time goes in v12:
time: 176 us; the launch traced here: 175 us
  Pallas kernels  66.5 us (38%)
  waiting for transfers between devices  50 us (28%)
  starting transfers between devices  45.1 us (26%)
  other arithmetic  6.47 us (4%)
  local copies, waits for them, and re-layouts  5.68 us (3%)
    ppermute x19, waiting for transfers between devices, body(): send = lambda a, pairs: lax.ppermute(a, 'seq', pairs)  38.1 us
    ppermute x19, starting transfers between devices, body(): send = lambda a, pairs: lax.ppermute(a, 'seq', pairs)  31.2 us
    pallas_call x4, Pallas kernels, project_pair(): pl.pallas_call(pair_kernel, out_shape=[there] * pieces + [here], grid_spe...  21.3 us
    ppermute x20, starting transfers between devices, body(): lax.ppermute(a, 'head', [(i, i ^ bits) for i in range(head_size)])  13.9 us
    pallas_call x2, Pallas kernels, attend(): pl.pallas_call(functools.partial(attend_kernel, start), grid=(2, heads //...  12.7 us
    ppermute x20, waiting for transfers between devices, body(): lax.ppermute(a, 'head', [(i, i ^ bits) for i in range(head_size)])  11.9 us
    pallas_call x2, Pallas kernels, project_chip(): pl.pallas_call(chip_kernel, out_shape=jax.ShapeDtypeStruct((2, 2 * rows,...  10.8 us
    pallas_call x1, Pallas kernels, attend_near(): pl.pallas_call(functools.partial(near_kernel, start), grid=(rows // TILE,...  9.64 us
  transfers between devices with their start and end apart: 39, of which 16 were waited for; matrix products, arithmetic and copies ran while one was open for 5% of the time, Pallas kernels for 38%

profile of v12, /device:TPU:2, one launch (start us, length us, event | category | flops | bytes accessed | tf_op | source)
XLA Modules:
  0.0 174.9 jit_solution(2800893314697831535)
XLA Ops:
  0.0 1.5 collective-permute-start.3
  2.0 1.9 %collective-permute-start.1 = (f32[1024,128]{1,0:T(8,128)}, f32[1024,128]{1,0:T(8,128)S(1)}, u32[]{:S(2)}, u32[]{:S(2)}) collective-permute-start(f32[1024,128]{1,0:T(8,128)} %v_own.1), channel_id=1, source_target_pairs={{0,32},{8,40},{16,48},{24,56},{32,64},{40,72},{48,80},{56,88},{64,... | collective-permute-start | bytes 1572872 | tf_op jit(solution)/shard_map/ppermute | solution.py:401
  4.5 9.4 %shard_map.78 = (f32[512,2048]{1,0:T(8,128)}, f32[512,2048]{1,0:T(8,128)}) custom-call(s32[3]{0:T(128)} %add_xor_fusion.chips, f32[512,4096]{1,0:T(8,128)} %w.3, f32[512,4096]{1,0:T(8,128)} %w.3, f32[512,4096]{1,0:T(8,128)} %w.3), custom_call_target="tpu_custom_call" | custom-call | flops 1024 | bytes 1024 | tf_op jit(solution)/shard_map/pallas_call | solution.py:275
  13.8 1.6 collective-permute-start.19
  15.4 2.2 %collective-permute-start.20 = (f32[512,2048]{1,0:T(8,128)}, f32[512,2048]{1,0:T(8,128)}, u32[]{:S(2)}, u32[]{:S(2)}) collective-permute-start(f32[512,2048]{1,0:T(8,128)} %get-tuple-element.134), channel_id=1, source_target_pairs={{0,6},{1,7},{2,4},{3,5},{4,2},{5,3},{6,0},{7,1},{8,14},{9,15},{10,... | collective-permute-start | bytes 12582920 | tf_op jit(solution)/shard_map/ppermute | solution.py:409
  18.9 2.1 %collective-permute-start.4 = (f32[1024,128]{1,0:T(8,128)S(1)}, f32[1024,128]{1,0:T(8,128)}, u32[]{:S(2)}, u32[]{:S(2)}) collective-permute-start(f32[1024,128]{1,0:T(8,128)S(1)} %copy-done), channel_id=1, source_target_pairs={{0,96},{8,104},{16,112},{24,120},{32,0},{40,8},{48,16},{56,24},{64... | collective-permute-start | bytes 1572872 | tf_op jit(solution)/shard_map/ppermute | solution.py:401
  21.8 0.9 pad_maximum_fusion.3
  22.8 2.9 %collective-permute-start.2 = (f32[1536,128]{1,0:T(8,128)}, f32[1536,128]{1,0:T(8,128)}, u32[]{:S(2)}, u32[]{:S(2)}) collective-permute-start(f32[1536,128]{1,0:T(8,128)} %pad_maximum_fusion.3), channel_id=1, source_target_pairs={{0,24},{8,0},{16,8},{24,16},{32,56},{40,32},{48,40},{56,48},{64,88... | collective-permute-start | bytes 2359304 | tf_op jit(solution)/shard_map/ppermute | solution.py:401
  25.7 0.9 pad_maximum_fusion.4
  27.1 4.3 %collective-permute-done.4.refs_5_ = f32[1024,128]{1,0:T(8,128)} collective-permute-done((f32[1024,128]{1,0:T(8,128)S(1)}, f32[1024,128]{1,0:T(8,128)}, u32[]{:S(2)}, u32[]{:S(2)}) %collective-permute-start.4) | collective-permute-done | bytes 524320 | tf_op jit(solution)/shard_map/ppermute | solution.py:401
  31.4 1.5 collective-permute-start.6
  32.9 3.5 %collective-permute-start.5 = (f32[1024,128]{1,0:T(8,128)}, f32[1024,128]{1,0:T(8,128)}, u32[]{:S(2)}, u32[]{:S(2)}) collective-permute-start(f32[1024,128]{1,0:T(8,128)} %collective-permute-done.4.refs_5_), channel_id=1, source_target_pairs={{0,96},{8,104},{16,112},{24,120},{32,0},{40,8},{48,16},{56,24},{64... | collective-permute-start | bytes 1572872 | tf_op jit(solution)/shard_map/ppermute | solution.py:401
  37.6 3.4 %collective-permute-done.2 = f32[1536,128]{1,0:T(8,128)} collective-permute-done((f32[1536,128]{1,0:T(8,128)}, f32[1536,128]{1,0:T(8,128)}, u32[]{:S(2)}, u32[]{:S(2)}) %collective-permute-start.2) | collective-permute-done | bytes 786464 | tf_op jit(solution)/shard_map/ppermute | solution.py:401
  41.0 7.9 %collective-permute-done.6 = f32[1536,128]{1,0:T(8,128)} collective-permute-done((f32[1536,128]{1,0:T(8,128)}, f32[1536,128]{1,0:T(8,128)}, u32[]{:S(2)}, u32[]{:S(2)}) %collective-permute-start.6) | collective-permute-done | bytes 786464 | tf_op jit(solution)/shard_map/ppermute | solution.py:401
  48.9 1.0 slice.69
  49.8 1.1 slice.70.refs_2_.k_far
  50.9 3.0 %collective-permute-start.9 = (f32[512,128]{1,0:T(8,128)S(1)}, f32[512,128]{1,0:T(8,128)S(1)}, u32[]{:S(2)}, u32[]{:S(2)}) collective-permute-start(f32[512,128]{1,0:T(8,128)S(1)} %slice.69), channel_id=1, source_target_pairs={{0,24},{8,0},{16,8},{24,16},{32,56},{40,32},{48,40},{56,48},{64,88... | collective-permute-start | bytes 786440 | tf_op jit(solution)/shard_map/ppermute | solution.py:401
  54.0 2.5 %shard_map.74 = (f32[1024,128]{1,0:T(8,128)S(1)}, f32[1024,128]{1,0:T(8,128)S(1)}, f32[1024,128]{1,0:T(8,128)S(1)}, f32[1024,128]{1,0:T(8,128)S(1)}) custom-call(s32[32]{0:T(128)S(1)} %get-tuple-element.100.k_place, s32[32]{0:T(128)S(1)} %compare_convert_fusion.1.k_held, s32[32]{0:T(128)S(1)} %get-tuple-element.102.v_place, ...), custom_call_target="tpu_custom_call" | custom-call | flops 1024 | bytes 1024 | tf_op jit(solution)/shard_map/pallas_call | solution.py:48
  56.5 1.6 collective-permute-start.11
  58.1 2.2 %collective-permute-start.12 = (f32[1024,128]{1,0:T(8,128)S(1)}, f32[1024,128]{1,0:T(8,128)S(1)}, u32[]{:S(2)}, u32[]{:S(2)}) collective-permute-start(f32[1024,128]{1,0:T(8,128)S(1)} %get-tuple-element.106), channel_id=1, source_target_pairs={{0,96},{8,104},{16,112},{24,120},{32,64},{40,72},{48,80},{56,88},{... | collective-permute-start | bytes 1572872 | tf_op jit(solution)/shard_map/ppermute | solution.py:401
  60.3 1.0 slice.68
  61.4 6.4 %collective-permute-done.8.v_far_a = f32[512,128]{1,0:T(8,128)S(1)} collective-permute-done((f32[512,128]{1,0:T(8,128)S(1)}, f32[512,128]{1,0:T(8,128)S(1)}, u32[]{:S(2)}, u32[]{:S(2)}) %collective-permute-start.8) | collective-permute-done | bytes 262176 | tf_op jit(solution)/shard_map/ppermute | solution.py:401
  67.8 3.2 %collective-permute-start.10 = (f32[1024,128]{1,0:T(8,128)S(1)}, f32[1024,128]{1,0:T(8,128)S(1)}, u32[]{:S(2)}, u32[]{:S(2)}) collective-permute-start(f32[1024,128]{1,0:T(8,128)S(1)} %slice.70.refs_2_.k_far), channel_id=1, source_target_pairs={{0,32},{8,40},{32,64},{40,72},{64,96},{72,104},{1,33},{9,41},{33,6... | collective-permute-start | bytes 1572872 | tf_op jit(solution)/shard_map/ppermute | solution.py:401
  71.0 1.8 %collective-permute-start.13 = (f32[1024,128]{1,0:T(8,128)S(1)}, f32[1024,128]{1,0:T(8,128)S(1)}, u32[]{:S(2)}, u32[]{:S(2)}) collective-permute-start(f32[1024,128]{1,0:T(8,128)S(1)} %get-tuple-element.107), channel_id=1, source_target_pairs={{0,8},{8,0},{16,24},{24,16},{32,40},{40,32},{48,56},{56,48},{64,72... | collective-permute-start | bytes 1572872 | tf_op jit(solution)/shard_map/ppermute | solution.py:401
  73.0 7.2 %collective-permute-done.13 = f32[1024,128]{1,0:T(8,128)S(1)} collective-permute-done((f32[1024,128]{1,0:T(8,128)S(1)}, f32[1024,128]{1,0:T(8,128)S(1)}, u32[]{:S(2)}, u32[]{:S(2)}) %collective-permute-start.13) | collective-permute-done | bytes 524320 | tf_op jit(solution)/shard_map/ppermute | solution.py:401
  80.2 1.7 collective-permute-done.14
  82.3 2.8 %collective-permute-start.16 = (f32[1024,128]{1,0:T(8,128)S(1)}, f32[1024,128]{1,0:T(8,128)S(1)}, u32[]{:S(2)}, u32[]{:S(2)}) collective-permute-start(f32[1024,128]{1,0:T(8,128)S(1)} %add.220), channel_id=1, source_target_pairs={{0,32},{8,40},{16,48},{24,56},{32,0},{40,8},{48,16},{56,24},{64,96... | collective-permute-start | bytes 1572872 | tf_op jit(solution)/shard_map/ppermute | solution.py:401
  85.2 7.2 %collective-permute-done.15 = f32[1024,128]{1,0:T(8,128)S(1)} collective-permute-done((f32[1024,128]{1,0:T(8,128)S(1)}, f32[1024,128]{1,0:T(8,128)S(1)}, u32[]{:S(2)}, u32[]{:S(2)}) %collective-permute-start.15) | collective-permute-done | bytes 524320 | tf_op jit(solution)/shard_map/ppermute | solution.py:401
  92.4 1.6 collective-permute-start.18
  94.0 1.1 slice.71.v_left
  95.1 9.6 %shard_map.75 = (f32[1024,512]{1,0:T(8,128)S(1)}, f32[1024,256]{1,0:T(8,128)S(1)}) custom-call(s32[1]{0:T(128)} %bitcast.1.first_row, s32[4,4]{1,0:T(4,128)S(1)} %get-tuple-element.111.back, s32[2]{0:T(128)S(1)} %add_convert_fusion.wraps, f32[1024,512]{1,0:T(8,128)S(1)} %shard_map.73.q, f32[1024,128]{1,0:T(8,128)S(1)} %slice.70.refs_2_.k_far, ...), custom_call_target="tpu_custom_call" | custom-call | flops 100000 | bytes 1024 | tf_op jit(solution)/shard_map/pallas_call | solution.py:179
  105.1 6.3 %shard_map.76.own_a = f32[2,256,512]{2,1,0:T(8,128)S(1)} custom-call(s32[1]{0:T(128)} %bitcast.1.first_row, f32[1024,512]{1,0:T(8,128)S(1)} %shard_map.73.q, f32[1024,512]{1,0:T(8,128)S(1)} %get-tuple-element.124.near, f32[1024,256]{1,0:T(8,128)S(1)} %get-tuple-element.125.stats, f32[1024,128]{1,0:T(8,128)S(1)} %add.223.k_a, f32[1024,128]{1,0:T(8,128)S(1)} %add.224.k_b, ...), custom_call_target="tpu_custom_call" | custom-call | flops 100000 | bytes 1024 | tf_op jit(solution)/shard_map/pallas_call | solution.py:236
  111.4 6.3 %shard_map.77.own_b = f32[2,256,512]{2,1,0:T(8,128)S(1)} custom-call(s32[1]{0:T(128)} %bitcast.1.first_row, f32[1024,512]{1,0:T(8,128)S(1)} %shard_map.73.q, f32[1024,512]{1,0:T(8,128)S(1)} %get-tuple-element.124.near, f32[1024,256]{1,0:T(8,128)S(1)} %get-tuple-element.125.stats, f32[1024,128]{1,0:T(8,128)S(1)} %add.223.k_a, f32[1024,128]{1,0:T(8,128)S(1)} %add.224.k_b, ...), custom_call_target="tpu_custom_call" | custom-call | flops 100000 | bytes 1024 | tf_op jit(solution)/shard_map/pallas_call | solution.py:236
  117.8 1.1 collective-permute-start.22
  119.3 2.6 %collective-permute-start.24 = (f32[256,512]{1,0:T(8,128)S(1)}, f32[256,512]{1,0:T(8,128)S(1)}, u32[]{:S(2)}, u32[]{:S(2)}) collective-permute-start(f32[256,512]{1,0:T(8,128)S(1)} %get-tuple-element.195), channel_id=1, source_target_pairs={{0,6},{1,7},{2,4},{3,5},{4,2},{5,3},{6,0},{7,1},{8,14},{9,15},{10,... | collective-permute-start | bytes 1572872 | tf_op jit(solution)/shard_map/ppermute | solution.py:409
  121.9 0.8 collective-permute-start.23
  122.7 5.4 %shard_map.79.total = f32[2,512,1024]{2,1,0:T(8,128)S(1)} custom-call(s32[4]{0:T(128)S(1)} %get-tuple-element.97.order, f32[2,256,512]{2,1,0:T(8,128)S(1)} %shard_map.76.own_a, f32[2,256,512]{2,1,0:T(8,128)S(1)} %shard_map.77.own_b, f32[512,4096]{1,0:T(8,128)S(1)} %bitcast.33), custom_call_target="tpu_custom_call" | custom-call | flops 100000 | bytes 1024 | tf_op jit(solution)/shard_map/pallas_call | solution.py:312
  128.2 3.3 %collective-permute-done.22.got_b = f32[256,512]{1,0:T(8,128)S(1)} collective-permute-done((f32[256,512]{1,0:T(8,128)S(1)}, f32[256,512]{1,0:T(8,128)S(1)}, u32[]{:S(2)}, u32[]{:S(2)}) %collective-permute-start.22) | collective-permute-done | bytes 524320 | tf_op jit(solution)/shard_map/ppermute | solution.py:409
  131.4 5.3 %shard_map.80 = (f32[256,512]{1,0:T(8,128)S(1)}, f32[256,512]{1,0:T(8,128)S(1)}, f32[2,256,512]{2,1,0:T(8,128)S(1)}) custom-call(s32[2]{0:T(128)S(1)} %get-tuple-element.96.cores, f32[256,512]{1,0:T(8,128)S(1)} %collective-permute-done.21.got_a, f32[256,512]{1,0:T(8,128)S(1)} %collective-permute-done.22.got_b, f32[512,2048]{1,0:T(8,128)} %collective-permute-done.19.near, ...), custom_call_target="tpu_custom_call" | custom-call | flops 100000 | bytes 1024 | tf_op jit(solution)/shard_map/pallas_call | solution.py:359
  137.6 5.3 %shard_map.81 = (f32[256,512]{1,0:T(8,128)S(1)}, f32[256,512]{1,0:T(8,128)S(1)}, f32[2,256,512]{2,1,0:T(8,128)S(1)}) custom-call(s32[2]{0:T(128)S(1)} %get-tuple-element.96.cores, f32[256,512]{1,0:T(8,128)S(1)} %collective-permute-done.23.got_a, f32[256,512]{1,0:T(8,128)S(1)} %collective-permute-done.24.got_b, f32[512,2048]{1,0:T(8,128)} %collective-permute-done.19.near, ...), custom_call_target="tpu_custom_call" | custom-call | flops 100000 | bytes 1024 | tf_op jit(solution)/shard_map/pallas_call | solution.py:359
  143.7 1.2 collective-permute-done.27
  146.0 1.8 %collective-permute-start.31 = (f32[512,512]{1,0:T(8,128)S(1)}, f32[512,512]{1,0:T(8,128)S(1)}, u32[]{:S(2)}, u32[]{:S(2)}) collective-permute-start(f32[512,512]{1,0:T(8,128)S(1)} %pad_maximum_fusion.1), channel_id=1, source_target_pairs={{0,6},{1,7},{2,4},{3,5},{4,2},{5,3},{6,0},{7,1},{8,14},{9,15},{10,... | collective-permute-start | bytes 3145736 | tf_op jit(solution)/shard_map/ppermute | solution.py:409
  147.8 5.4 %shard_map.82.total = f32[2,512,1024]{2,1,0:T(8,128)S(1)} custom-call(s32[4]{0:T(128)S(1)} %get-tuple-element.161.order, f32[2,256,512]{2,1,0:T(8,128)S(1)} %shard_map.76.own_a, f32[2,256,512]{2,1,0:T(8,128)S(1)} %shard_map.77.own_b, f32[512,4096]{1,0:T(8,128)S(1)} %bitcast.33), custom_call_target="tpu_custom_call" | custom-call | flops 100000 | bytes 1024 | tf_op jit(solution)/shard_map/pallas_call | solution.py:312
  153.2 5.3 %shard_map.84 = (f32[256,256]{1,0:T(8,128)S(1)}, f32[256,256]{1,0:T(8,128)S(1)}, f32[256,256]{1,0:T(8,128)S(1)}, f32[256,256]{1,0:T(8,128)S(1)}, f32[2,256,512]{2,1,0:T(8,128)S(1)}) custom-call(s32[2]{0:T(128)S(1)} %get-tuple-element.96.cores, f32[256,512]{1,0:T(8,128)S(1)} %collective-permute-done.23.got_a, f32[256,512]{1,0:T(8,128)S(1)} %collective-permute-done.24.got_b, ...), custom_call_target="tpu_custom_call" | custom-call | flops 100000 | bytes 1024 | tf_op jit(solution)/shard_map/pallas_call | solution.py:359
  159.3 5.3 %shard_map.83 = (f32[256,256]{1,0:T(8,128)S(1)}, f32[256,256]{1,0:T(8,128)S(1)}, f32[256,256]{1,0:T(8,128)S(1)}, f32[256,256]{1,0:T(8,128)S(1)}, f32[2,256,512]{2,1,0:T(8,128)S(1)}) custom-call(s32[2]{0:T(128)S(1)} %get-tuple-element.96.cores, f32[256,512]{1,0:T(8,128)S(1)} %collective-permute-done.21.got_a, f32[256,512]{1,0:T(8,128)S(1)} %collective-permute-done.22.got_b, ...), custom_call_target="tpu_custom_call" | custom-call | flops 100000 | bytes 1024 | tf_op jit(solution)/shard_map/pallas_call | solution.py:359
  167.0 0.8 collective-permute-done.32
  168.2 4.3 %collective-permute-done.31 = f32[512,512]{1,0:T(8,128)S(1)} collective-permute-done((f32[512,512]{1,0:T(8,128)S(1)}, f32[512,512]{1,0:T(8,128)S(1)}, u32[]{:S(2)}, u32[]{:S(2)}) %collective-permute-start.31) | collective-permute-done | bytes 1048608 | tf_op jit(solution)/shard_map/ppermute | solution.py:409
  173.4 1.5 pad_maximum_fusion
  (114 shorter events, 12.6 us)
Async XLA Ops:
  0.0 18.7 %collective-permute-start.3 = (f32[1024,128]{1,0:T(8,128)}, f32[1024,128]{1,0:T(8,128)S(1)}, u32[]{:S(2)}, u32[]{:S(2)}) collective-permute-start(f32[1024,128]{1,0:T(8,128)} %k_own.1), channel_id=1, source_target_pairs={{0,8},{8,16},{16,24},{24,0},{32,40},{40,48},{48,56},{56,32},{64,72... | collective-permute-start | bytes 1572872 | tf_op jit(solution)/shard_map/ppermute | solution.py:401
  1.5 20.3 %collective-permute-start = (f32[1024,128]{1,0:T(8,128)}, f32[1024,128]{1,0:T(8,128)S(1)}, u32[]{:S(2)}, u32[]{:S(2)}) collective-permute-start(f32[1024,128]{1,0:T(8,128)} %k_own.1), channel_id=1, source_target_pairs={{0,24},{8,0},{16,8},{24,16},{32,56},{40,32},{48,40},{56,48},{64,88... | collective-permute-start | bytes 1572872 | tf_op jit(solution)/shard_map/ppermute | solution.py:401
  2.0 19.0 %collective-permute-start.1 = (f32[1024,128]{1,0:T(8,128)}, f32[1024,128]{1,0:T(8,128)S(1)}, u32[]{:S(2)}, u32[]{:S(2)}) collective-permute-start(f32[1024,128]{1,0:T(8,128)} %v_own.1), channel_id=1, source_target_pairs={{0,32},{8,40},{16,48},{24,56},{32,64},{40,72},{48,80},{56,88},{64,... | collective-permute-start | bytes 1572872 | tf_op jit(solution)/shard_map/ppermute | solution.py:401
  4.5 14.2 %copy-start.4 = (s32[32,3]{0,1:T(4,128)S(1)}, s32[32,3]{0,1:T(4,128)}, u32[]{:S(2)}) copy-start(s32[32,3]{0,1:T(4,128)} %param.11) | copy-start | bytes 1156
  4.5 14.4 %copy-start = (f32[1024,128]{1,0:T(8,128)S(1)}, f32[1024,128]{1,0:T(8,128)}, u32[]{:S(2)}) copy-start(f32[1024,128]{1,0:T(8,128)} %v_own.1) | copy-start | bytes 1572868
  13.8 108.1 %collective-permute-start.19 = (f32[512,2048]{1,0:T(8,128)}, f32[512,2048]{1,0:T(8,128)}, u32[]{:S(2)}, u32[]{:S(2)}) collective-permute-start(f32[512,2048]{1,0:T(8,128)} %get-tuple-element.133), channel_id=1, source_target_pairs={{0,2},{1,3},{2,0},{3,1},{4,6},{5,7},{6,4},{7,5},{8,10},{9,11},{10,... | collective-permute-start | bytes 12582920 | tf_op jit(solution)/shard_map/ppermute | solution.py:409
  15.4 107.3 %collective-permute-start.20 = (f32[512,2048]{1,0:T(8,128)}, f32[512,2048]{1,0:T(8,128)}, u32[]{:S(2)}, u32[]{:S(2)}) collective-permute-start(f32[512,2048]{1,0:T(8,128)} %get-tuple-element.134), channel_id=1, source_target_pairs={{0,6},{1,7},{2,4},{3,5},{4,2},{5,3},{6,0},{7,1},{8,14},{9,15},{10,... | collective-permute-start | bytes 12582920 | tf_op jit(solution)/shard_map/ppermute | solution.py:409
  18.9 12.6 %collective-permute-start.4 = (f32[1024,128]{1,0:T(8,128)S(1)}, f32[1024,128]{1,0:T(8,128)}, u32[]{:S(2)}, u32[]{:S(2)}) collective-permute-start(f32[1024,128]{1,0:T(8,128)S(1)} %copy-done), channel_id=1, source_target_pairs={{0,96},{8,104},{16,112},{24,120},{32,0},{40,8},{48,16},{56,24},{64... | collective-permute-start | bytes 1572872 | tf_op jit(solution)/shard_map/ppermute | solution.py:401
  21.0 11.9 %collective-permute-start.7 = (f32[1024,128]{1,0:T(8,128)S(1)}, f32[1024,128]{1,0:T(8,128)S(1)}, u32[]{:S(2)}, u32[]{:S(2)}) collective-permute-start(f32[1024,128]{1,0:T(8,128)S(1)} %collective-permute-done.3.refs_3_.k_left), channel_id=1, source_target_pairs={{0,32},{32,64},{64,96},{1,33},{33,65},{65,97},{2,34},{34,66},{66,9... | collective-permute-start | bytes 1572872 | tf_op jit(solution)/shard_map/ppermute | solution.py:401
  21.8 4.9 %copy-start.3 = (s32[32,8]{0,1:T(8,128)S(1)}, s32[32,8]{0,1:T(8,128)}, u32[]{:S(2)}) copy-start(s32[32,8]{0,1:T(8,128)} %param.10) | copy-start | bytes 3076
  22.8 31.2 %copy-start.1 = (f32[1024,128]{1,0:T(8,128)S(1)}, f32[1024,128]{1,0:T(8,128)}, u32[]{:S(2)}) copy-start(f32[1024,128]{1,0:T(8,128)} %k_own.1) | copy-start | bytes 1572868
  22.8 18.3 %collective-permute-start.2 = (f32[1536,128]{1,0:T(8,128)}, f32[1536,128]{1,0:T(8,128)}, u32[]{:S(2)}, u32[]{:S(2)}) collective-permute-start(f32[1536,128]{1,0:T(8,128)} %pad_maximum_fusion.3), channel_id=1, source_target_pairs={{0,24},{8,0},{16,8},{24,16},{32,56},{40,32},{48,40},{56,48},{64,88... | collective-permute-start | bytes 2359304 | tf_op jit(solution)/shard_map/ppermute | solution.py:401
  31.4 17.5 %collective-permute-start.6 = (f32[1536,128]{1,0:T(8,128)}, f32[1536,128]{1,0:T(8,128)}, u32[]{:S(2)}, u32[]{:S(2)}) collective-permute-start(f32[1536,128]{1,0:T(8,128)} %pad_maximum_fusion.4), channel_id=1, source_target_pairs={{0,8},{8,16},{16,24},{24,0},{32,40},{40,48},{48,56},{56,32},{64,72... | collective-permute-start | bytes 2359304 | tf_op jit(solution)/shard_map/ppermute | solution.py:401
  32.9 15.9 %collective-permute-start.5 = (f32[1024,128]{1,0:T(8,128)}, f32[1024,128]{1,0:T(8,128)}, u32[]{:S(2)}, u32[]{:S(2)}) collective-permute-start(f32[1024,128]{1,0:T(8,128)} %collective-permute-done.4.refs_5_), channel_id=1, source_target_pairs={{0,96},{8,104},{16,112},{24,120},{32,0},{40,8},{48,16},{56,24},{64... | collective-permute-start | bytes 1572872 | tf_op jit(solution)/shard_map/ppermute | solution.py:401
  50.9 21.8 %copy-start.2 = (f32[1024,512]{1,0:T(8,128)S(1)}, f32[1024,512]{1,0:T(8,128)}, u32[]{:S(2)}) copy-start(f32[1024,512]{1,0:T(8,128)} %q.1) | copy-start | bytes 6291460
  50.9 10.4 %collective-permute-start.9 = (f32[512,128]{1,0:T(8,128)S(1)}, f32[512,128]{1,0:T(8,128)S(1)}, u32[]{:S(2)}, u32[]{:S(2)}) collective-permute-start(f32[512,128]{1,0:T(8,128)S(1)} %slice.69), channel_id=1, source_target_pairs={{0,24},{8,0},{16,8},{24,16},{32,56},{40,32},{48,40},{56,48},{64,88... | collective-permute-start | bytes 786440 | tf_op jit(solution)/shard_map/ppermute | solution.py:401
  56.5 14.5 %collective-permute-start.11 = (f32[1024,128]{1,0:T(8,128)S(1)}, f32[1024,128]{1,0:T(8,128)S(1)}, u32[]{:S(2)}, u32[]{:S(2)}) collective-permute-start(f32[1024,128]{1,0:T(8,128)S(1)} %get-tuple-element.105), channel_id=1, source_target_pairs={{0,32},{8,40},{16,48},{24,56},{32,0},{40,8},{48,16},{56,24},{64,96... | collective-permute-start | bytes 1572872 | tf_op jit(solution)/shard_map/ppermute | solution.py:401
  58.1 14.6 %collective-permute-start.12 = (f32[1024,128]{1,0:T(8,128)S(1)}, f32[1024,128]{1,0:T(8,128)S(1)}, u32[]{:S(2)}, u32[]{:S(2)}) collective-permute-start(f32[1024,128]{1,0:T(8,128)S(1)} %get-tuple-element.106), channel_id=1, source_target_pairs={{0,96},{8,104},{16,112},{24,120},{32,64},{40,72},{48,80},{56,88},{... | collective-permute-start | bytes 1572872 | tf_op jit(solution)/shard_map/ppermute | solution.py:401
  61.3 6.4 %collective-permute-start.8 = (f32[512,128]{1,0:T(8,128)S(1)}, f32[512,128]{1,0:T(8,128)S(1)}, u32[]{:S(2)}, u32[]{:S(2)}) collective-permute-start(f32[512,128]{1,0:T(8,128)S(1)} %slice.68), channel_id=1, source_target_pairs={{0,8},{8,16},{16,24},{24,0},{32,40},{40,48},{48,56},{56,32},{64,72... | collective-permute-start | bytes 786440 | tf_op jit(solution)/shard_map/ppermute | solution.py:401
  67.8 14.1 %collective-permute-start.10 = (f32[1024,128]{1,0:T(8,128)S(1)}, f32[1024,128]{1,0:T(8,128)S(1)}, u32[]{:S(2)}, u32[]{:S(2)}) collective-permute-start(f32[1024,128]{1,0:T(8,128)S(1)} %slice.70.refs_2_.k_far), channel_id=1, source_target_pairs={{0,32},{8,40},{32,64},{40,72},{64,96},{72,104},{1,33},{9,41},{33,6... | collective-permute-start | bytes 1572872 | tf_op jit(solution)/shard_map/ppermute | solution.py:401
  71.0 9.3 %collective-permute-start.13 = (f32[1024,128]{1,0:T(8,128)S(1)}, f32[1024,128]{1,0:T(8,128)S(1)}, u32[]{:S(2)}, u32[]{:S(2)}) collective-permute-start(f32[1024,128]{1,0:T(8,128)S(1)} %get-tuple-element.107), channel_id=1, source_target_pairs={{0,8},{8,0},{16,24},{24,16},{32,40},{40,32},{48,56},{56,48},{64,72... | collective-permute-start | bytes 1572872 | tf_op jit(solution)/shard_map/ppermute | solution.py:401
  72.7 9.2 %collective-permute-start.14 = (f32[1024,128]{1,0:T(8,128)S(1)}, f32[1024,128]{1,0:T(8,128)S(1)}, u32[]{:S(2)}, u32[]{:S(2)}) collective-permute-start(f32[1024,128]{1,0:T(8,128)S(1)} %get-tuple-element.108), channel_id=1, source_target_pairs={{0,24},{8,16},{16,8},{24,0},{32,56},{40,48},{48,40},{56,32},{64,88... | collective-permute-start | bytes 1572872 | tf_op jit(solution)/shard_map/ppermute | solution.py:401
  82.0 10.5 %collective-permute-start.15 = (f32[1024,128]{1,0:T(8,128)S(1)}, f32[1024,128]{1,0:T(8,128)S(1)}, u32[]{:S(2)}, u32[]{:S(2)}) collective-permute-start(f32[1024,128]{1,0:T(8,128)S(1)} %add.219), channel_id=1, source_target_pairs={{0,96},{8,104},{16,112},{24,120},{32,64},{40,72},{48,80},{56,88},{... | collective-permute-start | bytes 1572872 | tf_op jit(solution)/shard_map/ppermute | solution.py:401
  82.3 22.4 %collective-permute-start.16 = (f32[1024,128]{1,0:T(8,128)S(1)}, f32[1024,128]{1,0:T(8,128)S(1)}, u32[]{:S(2)}, u32[]{:S(2)}) collective-permute-start(f32[1024,128]{1,0:T(8,128)S(1)} %add.220), channel_id=1, source_target_pairs={{0,32},{8,40},{16,48},{24,56},{32,0},{40,8},{48,16},{56,24},{64,96... | collective-permute-start | bytes 1572872 | tf_op jit(solution)/shard_map/ppermute | solution.py:401
  85.2 19.6 %collective-permute-start.17 = (f32[1024,128]{1,0:T(8,128)S(1)}, f32[1024,128]{1,0:T(8,128)S(1)}, u32[]{:S(2)}, u32[]{:S(2)}) collective-permute-start(f32[1024,128]{1,0:T(8,128)S(1)} %add.221), channel_id=1, source_target_pairs={{0,24},{8,16},{16,8},{24,0},{32,56},{40,48},{48,40},{56,32},{64,88... | collective-permute-start | bytes 1572872 | tf_op jit(solution)/shard_map/ppermute | solution.py:401
  92.4 12.4 %collective-permute-start.18 = (f32[1024,128]{1,0:T(8,128)S(1)}, f32[1024,128]{1,0:T(8,128)S(1)}, u32[]{:S(2)}, u32[]{:S(2)}) collective-permute-start(f32[1024,128]{1,0:T(8,128)S(1)} %add.222), channel_id=1, source_target_pairs={{0,8},{8,0},{16,24},{24,16},{32,40},{40,32},{48,56},{56,48},{64,72... | collective-permute-start | bytes 1572872 | tf_op jit(solution)/shard_map/ppermute | solution.py:401
  105.0 17.7 %slice-start = ((s8[8388608]{0:T(1024)(128)(4,1)}), s8[4194304]{0:T(1024)(128)(4,1)S(1)}, s32[]{:S(2)}) async-start(s8[8388608]{0:T(1024)(128)(4,1)} %bitcast.32), calls=%async_computation | async-start | bytes 8388608
  111.4 11.3 %slice-start.1 = ((s8[8388608]{0:T(1024)(128)(4,1)}), s8[4194304]{0:T(1024)(128)(4,1)S(1)}, s32[]{:S(2)}) async-start(s8[8388608]{0:T(1024)(128)(4,1)} %bitcast.32), calls=%async_computation.1 | async-start | bytes 8388608
  117.8 13.6 %collective-permute-start.22 = (f32[256,512]{1,0:T(8,128)S(1)}, f32[256,512]{1,0:T(8,128)S(1)}, u32[]{:S(2)}, u32[]{:S(2)}) collective-permute-start(f32[256,512]{1,0:T(8,128)S(1)} %get-tuple-element.197), channel_id=1, source_target_pairs={{0,6},{1,7},{2,4},{3,5},{4,2},{5,3},{6,0},{7,1},{8,14},{9,15},{10,... | collective-permute-start | bytes 1572872 | tf_op jit(solution)/shard_map/ppermute | solution.py:409
  119.0 12.5 %collective-permute-start.21 = (f32[256,512]{1,0:T(8,128)S(1)}, f32[256,512]{1,0:T(8,128)S(1)}, u32[]{:S(2)}, u32[]{:S(2)}) collective-permute-start(f32[256,512]{1,0:T(8,128)S(1)} %get-tuple-element.198), channel_id=1, source_target_pairs={{0,2},{1,3},{2,0},{3,1},{4,6},{5,7},{6,4},{7,5},{8,10},{9,11},{10,... | collective-permute-start | bytes 1572872 | tf_op jit(solution)/shard_map/ppermute | solution.py:409
  119.3 17.7 %collective-permute-start.24 = (f32[256,512]{1,0:T(8,128)S(1)}, f32[256,512]{1,0:T(8,128)S(1)}, u32[]{:S(2)}, u32[]{:S(2)}) collective-permute-start(f32[256,512]{1,0:T(8,128)S(1)} %get-tuple-element.195), channel_id=1, source_target_pairs={{0,6},{1,7},{2,4},{3,5},{4,2},{5,3},{6,0},{7,1},{8,14},{9,15},{10,... | collective-permute-start | bytes 1572872 | tf_op jit(solution)/shard_map/ppermute | solution.py:409
  121.9 15.1 %collective-permute-start.23 = (f32[256,512]{1,0:T(8,128)S(1)}, f32[256,512]{1,0:T(8,128)S(1)}, u32[]{:S(2)}, u32[]{:S(2)}) collective-permute-start(f32[256,512]{1,0:T(8,128)S(1)} %get-tuple-element.196), channel_id=1, source_target_pairs={{0,2},{1,3},{2,0},{3,1},{4,6},{5,7},{6,4},{7,5},{8,10},{9,11},{10,... | collective-permute-start | bytes 1572872 | tf_op jit(solution)/shard_map/ppermute | solution.py:409
  137.0 5.8 %collective-permute-start.25 = (f32[256,512]{1,0:T(8,128)S(1)}, f32[256,512]{1,0:T(8,128)S(1)}, u32[]{:S(2)}, u32[]{:S(2)}) collective-permute-start(f32[256,512]{1,0:T(8,128)S(1)} %get-tuple-element.150), channel_id=1, source_target_pairs={{0,1},{1,0},{2,3},{3,2},{4,5},{5,4},{6,7},{7,6},{8,9},{9,8},{10,11... | collective-permute-start | bytes 1572872 | tf_op jit(solution)/shard_map/ppermute | solution.py:409
  137.0 5.8 %collective-permute-start.26 = (f32[256,512]{1,0:T(8,128)S(1)}, f32[256,512]{1,0:T(8,128)S(1)}, u32[]{:S(2)}, u32[]{:S(2)}) collective-permute-start(f32[256,512]{1,0:T(8,128)S(1)} %get-tuple-element.151), channel_id=1, source_target_pairs={{0,1},{1,0},{2,3},{3,2},{4,5},{5,4},{6,7},{7,6},{8,9},{9,8},{10,11... | collective-permute-start | bytes 1572872 | tf_op jit(solution)/shard_map/ppermute | solution.py:409
  142.9 2.0 %collective-permute-start.27 = (f32[256,512]{1,0:T(8,128)S(1)}, f32[256,512]{1,0:T(8,128)S(1)}, u32[]{:S(2)}, u32[]{:S(2)}) collective-permute-start(f32[256,512]{1,0:T(8,128)S(1)} %get-tuple-element.154), channel_id=1, source_target_pairs={{0,1},{1,0},{2,3},{3,2},{4,5},{5,4},{6,7},{7,6},{8,9},{9,8},{10,11... | collective-permute-start | bytes 1572872 | tf_op jit(solution)/shard_map/ppermute | solution.py:409
  143.0 2.6 %collective-permute-start.28 = (f32[256,512]{1,0:T(8,128)S(1)}, f32[256,512]{1,0:T(8,128)S(1)}, u32[]{:S(2)}, u32[]{:S(2)}) collective-permute-start(f32[256,512]{1,0:T(8,128)S(1)} %get-tuple-element.156), channel_id=1, source_target_pairs={{0,1},{1,0},{2,3},{3,2},{4,5},{5,4},{6,7},{7,6},{8,9},{9,8},{10,11... | collective-permute-start | bytes 1572872 | tf_op jit(solution)/shard_map/ppermute | solution.py:409
  146.0 26.5 %collective-permute-start.31 = (f32[512,512]{1,0:T(8,128)S(1)}, f32[512,512]{1,0:T(8,128)S(1)}, u32[]{:S(2)}, u32[]{:S(2)}) collective-permute-start(f32[512,512]{1,0:T(8,128)S(1)} %pad_maximum_fusion.1), channel_id=1, source_target_pairs={{0,6},{1,7},{2,4},{3,5},{4,2},{5,3},{6,0},{7,1},{8,14},{9,15},{10,... | collective-permute-start | bytes 3145736 | tf_op jit(solution)/shard_map/ppermute | solution.py:409
  147.8 24.9 %collective-permute-start.34 = (f32[512,512]{1,0:T(8,128)S(1)}, f32[512,512]{1,0:T(8,128)S(1)}, u32[]{:S(2)}, u32[]{:S(2)}) collective-permute-start(f32[512,512]{1,0:T(8,128)S(1)} %pad_maximum_fusion.2), channel_id=1, source_target_pairs={{0,2},{1,3},{2,0},{3,1},{4,6},{5,7},{6,4},{7,5},{8,10},{9,11},{10,... | collective-permute-start | bytes 3145736 | tf_op jit(solution)/shard_map/ppermute | solution.py:409
  158.6 6.0 %collective-permute-start.35 = (f32[256,256]{1,0:T(8,128)S(1)}, f32[256,256]{1,0:T(8,128)S(1)}, u32[]{:S(2)}, u32[]{:S(2)}) collective-permute-start(f32[256,256]{1,0:T(8,128)S(1)} %get-tuple-element.173), channel_id=1, source_target_pairs={{0,1},{1,0},{2,3},{3,2},{4,5},{5,4},{6,7},{7,6},{8,9},{9,8},{10,11... | collective-permute-start | bytes 786440 | tf_op jit(solution)/shard_map/ppermute | solution.py:409
  158.7 6.4 %collective-permute-start.36 = (f32[256,256]{1,0:T(8,128)S(1)}, f32[256,256]{1,0:T(8,128)S(1)}, u32[]{:S(2)}, u32[]{:S(2)}) collective-permute-start(f32[256,256]{1,0:T(8,128)S(1)} %get-tuple-element.174), channel_id=1, source_target_pairs={{0,1},{1,0},{2,3},{3,2},{4,5},{5,4},{6,7},{7,6},{8,9},{9,8},{10,11... | collective-permute-start | bytes 786440 | tf_op jit(solution)/shard_map/ppermute | solution.py:409
  159.2 6.0 %collective-permute-start.37 = (f32[256,256]{1,0:T(8,128)S(1)}, f32[256,256]{1,0:T(8,128)S(1)}, u32[]{:S(2)}, u32[]{:S(2)}) collective-permute-start(f32[256,256]{1,0:T(8,128)S(1)} %get-tuple-element.175), channel_id=1, source_target_pairs={{0,1},{1,0},{2,3},{3,2},{4,5},{5,4},{6,7},{7,6},{8,9},{9,8},{10,11... | collective-permute-start | bytes 786440 | tf_op jit(solution)/shard_map/ppermute | solution.py:409
  164.6 1.7 collective-permute-start.38
  165.1 1.5 collective-permute-start.29
  165.2 1.8 %collective-permute-start.30 = (f32[256,256]{1,0:T(8,128)S(1)}, f32[256,256]{1,0:T(8,128)S(1)}, u32[]{:S(2)}, u32[]{:S(2)}) collective-permute-start(f32[256,256]{1,0:T(8,128)S(1)} %get-tuple-element.165), channel_id=1, source_target_pairs={{0,1},{1,0},{2,3},{3,2},{4,5},{5,4},{6,7},{7,6},{8,9},{9,8},{10,11... | collective-permute-start | bytes 786440 | tf_op jit(solution)/shard_map/ppermute | solution.py:409
  166.2 1.5 collective-permute-start.32
  166.6 1.5 collective-permute-start.33

commit v13 on v11

--- a/solution.py
+++ b/solution.py
@@ -315,59 +315,57 @@
     )(order, own_a, own_b, weight)
 
 
-def pair_kernel(cores, got_a, got_b, near, far, total, *refs):
-    *there, here, x = refs
-    width = here.shape[2] * 2 // len(there)
+def pair_kernel(pieces, cores, got_a, got_b, near, far, total, *refs):
+    *outs, x = refs
     for kind, (got, weight) in enumerate(((got_a, near), (got_b, far))):
-
-        @pl.when((pl.program_id(0) == kind) & (pl.program_id(1) == 0))
-        def _():
-            x[...] = stack(got[...])
-
-        @pl.when((pl.program_id(0) == kind) & (pl.program_id(1) == 0))
-        def _():
-            term = total[0] + weight_term(x[...], weight[...])
-            mine = there[kind * len(there) // 2 : (kind + 1) * len(there) // 2]
-            for at, out in enumerate(mine):
-                out[...] = term[:, at * width : (at + 1) * width]
-
-        @pl.when((pl.program_id(0) == kind) & (pl.program_id(1) == 1))
-        def _():
-            here[0] = total[0] + weight_term(x[...], weight[...])
-
-
-def project_pair(got, near, far, total, unit, keep, cores):
+        for turn, count in enumerate(pieces):
+            start = 2 * sum(pieces[:turn]) + kind * count
+
+            @pl.when((pl.program_id(0) == kind) & (pl.program_id(1) == turn))
+            def _():
+                if turn == 0:
+                    x[...] = stack(got[...])
+                term = total[0] + weight_term(x[...], weight[...])
+                for at, out in enumerate(outs[start : start + count]):
+                    width = out.shape[1]
+                    out[...] = term[:, at * width : (at + 1) * width]
+
+
+def project_pair(got, near, far, total, unit, keep, cores, first=0, pieces=(1, 1)):
     rows, depth = got[0].shape
     width = depth
     base = 0 if keep else 2
+    turns = len(pieces)
     vmem = pl.BlockSpec(memory_space=pltpu.VMEM)
-    pieces = 4 if keep else 2
-    here = jax.ShapeDtypeStruct((2, rows, width), jnp.float32)
-    there = jax.ShapeDtypeStruct((rows, 2 * width // pieces), jnp.float32)
-    w_spec = lambda side: pl.BlockSpec(
-        (depth, width), lambda k, s, c: (0, base + c[side(k, s)])
+    shapes = [
+        jax.ShapeDtypeStruct((rows, width // count), jnp.float32)
+        for count in pieces
+        for _ in range(2 * count)
+    ]
+    w_spec = lambda place: pl.BlockSpec(
+        (depth, width), lambda k, s, c: (0, base + c[first + place(k, s)])
     )
-    *there, here = pl.pallas_call(
-        pair_kernel,
-        out_shape=[there] * pieces + [here],
+    outs = pl.pallas_call(
+        functools.partial(pair_kernel, pieces),
+        out_shape=shapes,
         grid_spec=pltpu.PrefetchScalarGridSpec(
             num_scalar_prefetch=1,
-            grid=(2, 2),
+            grid=(2, turns),
             in_specs=[
                 vmem,
                 vmem,
-                w_spec(lambda k, s: jnp.where(k == 0, s, 1)),
+                w_spec(lambda k, s: jnp.where(k == 0, s, turns - 1)),
                 w_spec(lambda k, s: jnp.where(k == 0, 0, s)),
-                pl.BlockSpec((1, rows, width), lambda k, s, c: (k, unit, s)),
+                pl.BlockSpec((1, rows, width), lambda k, s, c: (k, unit, first + s)),
             ],
-            out_specs=[pl.BlockSpec(there.shape, lambda k, s, c: (0, 0))] * pieces
-            + [pl.BlockSpec((1, rows, width), lambda k, s, c: (k, 0, 0))],
+            out_specs=[pl.BlockSpec(x.shape, lambda k, s, c: (0, 0)) for x in shapes],
             scratch_shapes=[pltpu.VMEM((2 * rows, depth), jnp.bfloat16)],
         ),
         compiler_params=pltpu.CompilerParams(vmem_limit_bytes=16 << 20),
         cost_estimate=LARGE,
     )(cores, *got, near, far, total)
-    return there, here
+    cuts = [2 * sum(pieces[:turn]) for turn in range(turns + 1)]
+    return [outs[i:j] for i, j in zip(cuts, cuts[1:])]
 
 
 def body(
@@ -395,6 +393,7 @@
     k_left = send(key_rows, right)
     k_right = send(key_rows, left)
     v_below = send(value_vectors, up)
+    v_above = send(value_vectors, down)
 
     y = head_index // 2
     over_head = lambda a, bits: lax.ppermute(a, "head", [(i, i ^ bits) for i in range(head_size)])
@@ -430,10 +429,8 @@
     orders = (pass_order, keep_order, cores)
     small = (vert_pos, slash_pos, first_row, back, wraps, orders, k_place, k_held, v_place, v_held)
 
-    k_left, late_values = lax.optimization_barrier((k_left, value_vectors))
-    v_above = send(late_values, down)
-    (k_left, k_right, v_below), small = lax.optimization_barrier(
-        ((k_left, k_right, v_below), small)
+    (k_left, k_right, v_below, v_above), small = lax.optimization_barrier(
+        ((k_left, k_right, v_below, v_above), small)
     )
     vert_pos, slash_pos, first_row, back, wraps, orders, k_place, k_held, v_place, v_held = small
     half = rows // 2
@@ -479,26 +476,28 @@
     own_b = attend(q, *near, half, first_row, arrays)
     got_b = meeting(own_b)
     own_b, near_weight, far_weight = lax.optimization_barrier((own_b, near_weight, far_weight))
+    own_b, got_a = lax.optimization_barrier((own_b, got_a))
     total = project_chip(own_a, own_b, out_weight, pass_order)
-    total, got_a = lax.optimization_barrier((total, got_a))
-    product = lambda got, total, unit, keep: project_pair(
-        got, near_weight, far_weight, total, unit, keep, cores
+    product = lambda got, total, unit, keep, **kind: project_pair(
+        got, near_weight, far_weight, total, unit, keep, cores, **kind
     )
     there_a, here_a = product(got_a, total, 0, False)
     there_a, here_a, got_a, got_b = lax.optimization_barrier((there_a, here_a, got_a, got_b))
     across = lambda parts: [over_head(a, 1) for a in parts]
     moved_a = across(there_a)
-    there_b, here_b = product(got_b, total, 1, False)
-    there_b, here_b, moved_a = lax.optimization_barrier((there_b, here_b, moved_a))
-    moved = zip(moved_a, across(there_b))
+    (there_b,) = product(got_b, total, 1, False, pieces=(1,))
+    there_b, moved_a, got_b = lax.optimization_barrier((there_b, moved_a, got_b))
+    moved_b = across(there_b)
+    (here_b,) = product(got_b, total, 1, False, first=1, pieces=(1,))
+    here_b, moved_b = lax.optimization_barrier((here_b, moved_b))
     passed = [
-        jnp.concatenate([here_a[i] + a, here_b[i] + b]) for i, (a, b) in enumerate(moved)
+        jnp.concatenate([here_a[i] + moved_a[i], here_b[i] + moved_b[i]]) for i in range(2)
     ]
     passed, got_a, got_b, own_b = lax.optimization_barrier((passed, got_a, got_b, own_b))
     sent = ending(passed)
     kept_total = project_chip(own_a, own_b, out_weight, keep_order)
-    keep_a = product(got_a, kept_total, 0, True)
-    keep_b = product(got_b, kept_total, 1, True)
+    keep_a = product(got_a, kept_total, 0, True, pieces=(2, 1))
+    keep_b = product(got_b, kept_total, 1, True, pieces=(2, 1))
     kept = []
     for there, here in (keep_a, keep_b):
         moved = across(there)

time: 173 us -> 180 us (1.040); the launches traced: 173 us -> 178 us
  waiting for transfers between devices: 53 us -> 61.7 us
  starting transfers between devices: 46.6 us -> 44.5 us
    ppermute x20, waiting for transfers between devices: 12.5 us -> 21.3 us  [body(): lax.ppermute(a, 'head', [(i, i ^ bits) for i in range(head_size)])]
    pallas_call x4 -> x5, Pallas kernels: 21.3 us -> 19.7 us  [project_pair(): pl.pallas_call(functools.partial(pair_kernel, pieces), out_shape=shapes,...]
  transfers between devices with their start and end apart: 39 -> 39, of which waited for: 16 -> 14; matrix products, arithmetic and copies ran while one was open for 2% -> 2% of each run, Pallas kernels for 38% -> 36%
where the time goes in v13:
time: 180 us; the launch traced here: 178 us
  Pallas kernels  63.8 us (35%)
  waiting for transfers between devices  61.7 us (34%)
  starting transfers between devices  44.5 us (25%)
  other arithmetic  4.52 us (3%)
  local copies, waits for them, and re-layouts  1.8 us (1%)
    ppermute x19, waiting for transfers between devices, body(): send = lambda a, pairs: lax.ppermute(a, 'seq', pairs)  40.5 us
    ppermute x19, starting transfers between devices, body(): send = lambda a, pairs: lax.ppermute(a, 'seq', pairs)  31.3 us
    ppermute x20, waiting for transfers between devices, body(): lax.ppermute(a, 'head', [(i, i ^ bits) for i in range(head_size)])  21.3 us
    pallas_call x5, Pallas kernels, project_pair(): pl.pallas_call(functools.partial(pair_kernel, pieces), out_shape=shapes,...  19.7 us
    ppermute x20, starting transfers between devices, body(): lax.ppermute(a, 'head', [(i, i ^ bits) for i in range(head_size)])  13.2 us
    pallas_call x2, Pallas kernels, attend(): pl.pallas_call(functools.partial(attend_kernel, start), grid=(2, heads //...  12.6 us
    pallas_call x2, Pallas kernels, project_chip(): pl.pallas_call(chip_kernel, out_shape=jax.ShapeDtypeStruct((2, 2 * rows,...  10.8 us
    pallas_call x1, Pallas kernels, attend_near(): pl.pallas_call(functools.partial(near_kernel, start), grid=(rows // TILE,...  9.64 us
  transfers between devices with their start and end apart: 39, of which 14 were waited for; matrix products, arithmetic and copies ran while one was open for 2% of the time, Pallas kernels for 36%

profile of v13, /device:TPU:2, one launch (start us, length us, event | category | flops | bytes accessed | tf_op | source)
XLA Modules:
  0.0 177.5 jit_solution(7661625558293893595)
XLA Ops:
  0.0 1.5 collective-permute-start
  1.5 0.5 collective-permute-start.1
  2.0 1.9 %collective-permute-start.2 = (f32[1024,128]{1,0:T(8,128)}, f32[1024,128]{1,0:T(8,128)S(1)}, u32[]{:S(2)}, u32[]{:S(2)}) collective-permute-start(f32[1024,128]{1,0:T(8,128)} %v_own.1), channel_id=1, source_target_pairs={{0,32},{8,40},{16,48},{24,56},{32,64},{40,72},{48,80},{56,88},{64,... | collective-permute-start | bytes 1572872 | tf_op jit(solution)/shard_map/ppermute | solution.py:390
  3.9 2.1 %collective-permute-start.3 = (f32[1024,128]{1,0:T(8,128)}, f32[1024,128]{1,0:T(8,128)S(1)}, u32[]{:S(2)}, u32[]{:S(2)}) collective-permute-start(f32[1024,128]{1,0:T(8,128)} %v_own.1), channel_id=1, source_target_pairs={{0,96},{8,104},{16,112},{24,120},{32,0},{40,8},{48,16},{56,24},{64... | collective-permute-start | bytes 1572872 | tf_op jit(solution)/shard_map/ppermute | solution.py:390
  6.6 8.9 %shard_map.78 = (f32[512,2048]{1,0:T(8,128)}, f32[512,2048]{1,0:T(8,128)}) custom-call(s32[3]{0:T(128)} %add_xor_fusion.chips, f32[512,4096]{1,0:T(8,128)} %w.3, f32[512,4096]{1,0:T(8,128)} %w.3, f32[512,4096]{1,0:T(8,128)} %w.3), custom_call_target="tpu_custom_call" | custom-call | flops 1024 | bytes 1024 | tf_op jit(solution)/shard_map/pallas_call | solution.py:266
  15.5 1.6 collective-permute-start.19
  20.2 2.3 %collective-permute-start.20 = (f32[512,2048]{1,0:T(8,128)}, f32[512,2048]{1,0:T(8,128)S(1)}, u32[]{:S(2)}, u32[]{:S(2)}) collective-permute-start(f32[512,2048]{1,0:T(8,128)} %get-tuple-element.140), channel_id=1, source_target_pairs={{0,6},{1,7},{2,4},{3,5},{4,2},{5,3},{6,0},{7,1},{8,14},{9,15},{10,... | collective-permute-start | bytes 12582920 | tf_op jit(solution)/shard_map/ppermute | solution.py:399
  22.5 2.1 %collective-permute-start.5 = (f32[1024,128]{1,0:T(8,128)S(1)}, f32[1024,128]{1,0:T(8,128)S(1)}, u32[]{:S(2)}, u32[]{:S(2)}) collective-permute-start(f32[1024,128]{1,0:T(8,128)S(1)} %collective-permute-done.3.refs_5_), channel_id=1, source_target_pairs={{0,96},{8,104},{16,112},{24,120},{32,0},{40,8},{48,16},{56,24},{64... | collective-permute-start | bytes 1572872 | tf_op jit(solution)/shard_map/ppermute | solution.py:390
  24.7 1.6 collective-permute-start.6
  26.4 0.6 collective-permute-start.4
  27.0 7.8 %collective-permute-done.5.refs_6_ = f32[1024,128]{1,0:T(8,128)S(1)} collective-permute-done((f32[1024,128]{1,0:T(8,128)S(1)}, f32[1024,128]{1,0:T(8,128)S(1)}, u32[]{:S(2)}, u32[]{:S(2)}) %collective-permute-start.5) | collective-permute-done | bytes 524320 | tf_op jit(solution)/shard_map/ppermute | solution.py:390
  34.8 0.7 collective-permute-start.7
  35.5 6.6 %collective-permute-done.6 = f32[1536,128]{1,0:T(8,128)S(1)} collective-permute-done((f32[1536,128]{1,0:T(8,128)S(1)}, f32[1536,128]{1,0:T(8,128)S(1)}, u32[]{:S(2)}, u32[]{:S(2)}) %collective-permute-start.6) | collective-permute-done | bytes 786464 | tf_op jit(solution)/shard_map/ppermute | solution.py:390
  42.1 1.3 collective-permute-done.4
  43.5 1.3 collective-permute-start.8
  44.8 1.8 %shard_map.74 = (f32[1024,128]{1,0:T(8,128)S(1)}, f32[1024,128]{1,0:T(8,128)S(1)}, f32[1024,128]{1,0:T(8,128)S(1)}, f32[1024,128]{1,0:T(8,128)S(1)}) custom-call(s32[32]{0:T(128)S(1)} %get-tuple-element.108.k_place, s32[32]{0:T(128)S(1)} %compare_convert_fusion.1.k_held, s32[32]{0:T(128)S(1)} %get-tuple-element.110.v_place, ...), custom_call_target="tpu_custom_call" | custom-call | flops 1024 | bytes 1024 | tf_op jit(solution)/shard_map/pallas_call | solution.py:48
  47.5 4.1 %collective-permute-done.8.v_far_a = f32[512,128]{1,0:T(8,128)S(1)} collective-permute-done((f32[512,128]{1,0:T(8,128)S(1)}, f32[512,128]{1,0:T(8,128)S(1)}, u32[]{:S(2)}, u32[]{:S(2)}) %collective-permute-start.8) | collective-permute-done | bytes 262176 | tf_op jit(solution)/shard_map/ppermute | solution.py:390
  51.6 3.2 %collective-permute-start.9 = (f32[512,128]{1,0:T(8,128)S(1)}, f32[512,128]{1,0:T(8,128)S(1)}, u32[]{:S(2)}, u32[]{:S(2)}) collective-permute-start(f32[512,128]{1,0:T(8,128)S(1)} %slice.45), channel_id=1, source_target_pairs={{0,24},{8,0},{16,8},{24,16},{32,56},{40,32},{48,40},{56,48},{64,88... | collective-permute-start | bytes 786440 | tf_op jit(solution)/shard_map/ppermute | solution.py:390
  54.8 3.9 %collective-permute-done.9.v_far_b = f32[512,128]{1,0:T(8,128)S(1)} collective-permute-done((f32[512,128]{1,0:T(8,128)S(1)}, f32[512,128]{1,0:T(8,128)S(1)}, u32[]{:S(2)}, u32[]{:S(2)}) %collective-permute-start.9) | collective-permute-done | bytes 262176 | tf_op jit(solution)/shard_map/ppermute | solution.py:390
  58.7 4.4 %collective-permute-start.10 = (f32[1024,128]{1,0:T(8,128)S(1)}, f32[1024,128]{1,0:T(8,128)S(1)}, u32[]{:S(2)}, u32[]{:S(2)}) collective-permute-start(f32[1024,128]{1,0:T(8,128)S(1)} %slice.46.refs_2_.k_far), channel_id=1, source_target_pairs={{0,32},{8,40},{32,64},{40,72},{64,96},{72,104},{1,33},{9,41},{33,6... | collective-permute-start | bytes 1572872 | tf_op jit(solution)/shard_map/ppermute | solution.py:390
  63.1 2.6 %collective-permute-start.13 = (f32[1024,128]{1,0:T(8,128)S(1)}, f32[1024,128]{1,0:T(8,128)S(1)}, u32[]{:S(2)}, u32[]{:S(2)}) collective-permute-start(f32[1024,128]{1,0:T(8,128)S(1)} %get-tuple-element.115), channel_id=1, source_target_pairs={{0,8},{8,0},{16,24},{24,16},{32,40},{40,32},{48,56},{56,48},{64,72... | collective-permute-start | bytes 1572872 | tf_op jit(solution)/shard_map/ppermute | solution.py:390
  66.1 8.2 %collective-permute-done.13 = f32[1024,128]{1,0:T(8,128)S(1)} collective-permute-done((f32[1024,128]{1,0:T(8,128)S(1)}, f32[1024,128]{1,0:T(8,128)S(1)}, u32[]{:S(2)}, u32[]{:S(2)}) %collective-permute-start.13) | collective-permute-done | bytes 524320 | tf_op jit(solution)/shard_map/ppermute | solution.py:390
  74.3 2.6 %collective-permute-done.14 = f32[1024,128]{1,0:T(8,128)S(1)} collective-permute-done((f32[1024,128]{1,0:T(8,128)S(1)}, f32[1024,128]{1,0:T(8,128)S(1)}, u32[]{:S(2)}, u32[]{:S(2)}) %collective-permute-start.14) | collective-permute-done | bytes 524320 | tf_op jit(solution)/shard_map/ppermute | solution.py:390
  77.0 0.9 collective-permute-start.18
  78.3 2.1 %collective-permute-start.16 = (f32[1024,128]{1,0:T(8,128)S(1)}, f32[1024,128]{1,0:T(8,128)S(1)}, u32[]{:S(2)}, u32[]{:S(2)}) collective-permute-start(f32[1024,128]{1,0:T(8,128)S(1)} %add.220), channel_id=1, source_target_pairs={{0,32},{8,40},{16,48},{24,56},{32,0},{40,8},{48,16},{56,24},{64,96... | collective-permute-start | bytes 1572872 | tf_op jit(solution)/shard_map/ppermute | solution.py:390
  80.5 5.8 %collective-permute-done.18 = f32[1024,128]{1,0:T(8,128)S(1)} collective-permute-done((f32[1024,128]{1,0:T(8,128)S(1)}, f32[1024,128]{1,0:T(8,128)S(1)}, u32[]{:S(2)}, u32[]{:S(2)}) %collective-permute-start.18) | collective-permute-done | bytes 524320 | tf_op jit(solution)/shard_map/ppermute | solution.py:390
  86.3 4.5 %collective-permute-start.15 = (f32[1024,128]{1,0:T(8,128)S(1)}, f32[1024,128]{1,0:T(8,128)S(1)}, u32[]{:S(2)}, u32[]{:S(2)}) collective-permute-start(f32[1024,128]{1,0:T(8,128)S(1)} %add.219), channel_id=1, source_target_pairs={{0,96},{8,104},{16,112},{24,120},{32,64},{40,72},{48,80},{56,88},{... | collective-permute-start | bytes 1572872 | tf_op jit(solution)/shard_map/ppermute | solution.py:390
  90.8 9.6 %shard_map.75 = (f32[1024,512]{1,0:T(8,128)S(1)}, f32[1024,256]{1,0:T(8,128)S(1)}) custom-call(s32[1]{0:T(128)} %bitcast.1.first_row, s32[4,4]{1,0:T(4,128)S(1)} %get-tuple-element.118.back, s32[2]{0:T(128)S(1)} %add_convert_fusion.wraps, f32[1024,512]{1,0:T(8,128)S(1)} %shard_map.73.q, f32[1024,128]{1,0:T(8,128)S(1)} %slice.46.refs_2_.k_far, ...), custom_call_target="tpu_custom_call" | custom-call | flops 100000 | bytes 1024 | tf_op jit(solution)/shard_map/pallas_call | solution.py:179
  100.8 6.3 %shard_map.76.own_a = f32[2,256,512]{2,1,0:T(8,128)S(1)} custom-call(s32[1]{0:T(128)} %bitcast.1.first_row, f32[1024,512]{1,0:T(8,128)S(1)} %shard_map.73.q, f32[1024,512]{1,0:T(8,128)S(1)} %get-tuple-element.131.near, f32[1024,256]{1,0:T(8,128)S(1)} %get-tuple-element.132.stats, f32[1024,128]{1,0:T(8,128)S(1)} %add.223.k_a, f32[1024,128]{1,0:T(8,128)S(1)} %add.224.k_b, ...), custom_call_target="tpu_custom_call" | custom-call | flops 100000 | bytes 1024 | tf_op jit(solution)/shard_map/pallas_call | solution.py:236
  107.1 6.3 %shard_map.77.own_b = f32[2,256,512]{2,1,0:T(8,128)S(1)} custom-call(s32[1]{0:T(128)} %bitcast.1.first_row, f32[1024,512]{1,0:T(8,128)S(1)} %shard_map.73.q, f32[1024,512]{1,0:T(8,128)S(1)} %get-tuple-element.131.near, f32[1024,256]{1,0:T(8,128)S(1)} %get-tuple-element.132.stats, f32[1024,128]{1,0:T(8,128)S(1)} %add.223.k_a, f32[1024,128]{1,0:T(8,128)S(1)} %add.224.k_b, ...), custom_call_target="tpu_custom_call" | custom-call | flops 100000 | bytes 1024 | tf_op jit(solution)/shard_map/pallas_call | solution.py:236
  113.5 1.4 collective-permute-start.21
  114.8 0.6 collective-permute-start.22
  115.5 0.7 collective-permute-start.23
  116.2 2.2 %collective-permute-start.24 = (f32[256,512]{1,0:T(8,128)S(1)}, f32[256,512]{1,0:T(8,128)S(1)}, u32[]{:S(2)}, u32[]{:S(2)}) collective-permute-start(f32[256,512]{1,0:T(8,128)S(1)} %get-tuple-element.209), channel_id=1, source_target_pairs={{0,6},{1,7},{2,4},{3,5},{4,2},{5,3},{6,0},{7,1},{8,14},{9,15},{10,... | collective-permute-start | bytes 1572872 | tf_op jit(solution)/shard_map/ppermute | solution.py:399
  118.4 5.7 %collective-permute-done.21.got_a = f32[256,512]{1,0:T(8,128)S(1)} collective-permute-done((f32[256,512]{1,0:T(8,128)S(1)}, f32[256,512]{1,0:T(8,128)S(1)}, u32[]{:S(2)}, u32[]{:S(2)}) %collective-permute-start.21) | collective-permute-done | bytes 524320 | tf_op jit(solution)/shard_map/ppermute | solution.py:399
  124.1 5.7 %collective-permute-done.22.got_b = f32[256,512]{1,0:T(8,128)S(1)} collective-permute-done((f32[256,512]{1,0:T(8,128)S(1)}, f32[256,512]{1,0:T(8,128)S(1)}, u32[]{:S(2)}, u32[]{:S(2)}) %collective-permute-start.22) | collective-permute-done | bytes 524320 | tf_op jit(solution)/shard_map/ppermute | solution.py:399
  129.7 5.4 %shard_map.79.total = f32[2,512,1024]{2,1,0:T(8,128)S(1)} custom-call(s32[4]{0:T(128)S(1)} %get-tuple-element.147.order, f32[2,256,512]{2,1,0:T(8,128)S(1)} %shard_map.76.own_a, f32[2,256,512]{2,1,0:T(8,128)S(1)} %shard_map.77.own_b, f32[512,4096]{1,0:T(8,128)S(1)} %bitcast.17), custom_call_target="tpu_custom_call" | custom-call | flops 100000 | bytes 1024 | tf_op jit(solution)/shard_map/pallas_call | solution.py:303
  135.1 4.6 %shard_map.80 = (f32[256,512]{1,0:T(8,128)S(1)}, f32[256,512]{1,0:T(8,128)S(1)}, f32[256,512]{1,0:T(8,128)S(1)}, f32[256,512]{1,0:T(8,128)S(1)}) custom-call(s32[2]{0:T(128)S(1)} %get-tuple-element.100.cores, f32[256,512]{1,0:T(8,128)S(1)} %collective-permute-done.21.got_a, f32[256,512]{1,0:T(8,128)S(1)} %collective-permute-done.22.got_b, ...), custom_call_target="tpu_custom_call" | custom-call | flops 100000 | bytes 1024 | tf_op jit(solution)/shard_map/pallas_call | solution.py:348
  140.3 3.0 %shard_map.81 = (f32[256,512]{1,0:T(8,128)S(1)}, f32[256,512]{1,0:T(8,128)S(1)}) custom-call(s32[2]{0:T(128)S(1)} %get-tuple-element.100.cores, f32[256,512]{1,0:T(8,128)S(1)} %collective-permute-done.23.got_a, f32[256,512]{1,0:T(8,128)S(1)} %collective-permute-done.24.got_b, f32[512,2048]{1,0:T(8,128)} %collective-permute-done.19.near, ...), custom_call_target="tpu_custom_call" | custom-call | flops 100000 | bytes 1024 | tf_op jit(solution)/shard_map/pallas_call | solution.py:348
  144.0 3.0 %shard_map.82 = (f32[256,512]{1,0:T(8,128)S(1)}, f32[256,512]{1,0:T(8,128)S(1)}) custom-call(s32[2]{0:T(128)S(1)} %get-tuple-element.100.cores, f32[256,512]{1,0:T(8,128)S(1)} %collective-permute-done.23.got_a, f32[256,512]{1,0:T(8,128)S(1)} %collective-permute-done.24.got_b, f32[512,2048]{1,0:T(8,128)} %collective-permute-done.19.near, ...), custom_call_target="tpu_custom_call" | custom-call | flops 100000 | bytes 1024 | tf_op jit(solution)/shard_map/pallas_call | solution.py:348
  147.5 1.9 %collective-permute-start.31 = (f32[512,512]{1,0:T(8,128)S(1)}, f32[512,512]{1,0:T(8,128)S(1)}, u32[]{:S(2)}, u32[]{:S(2)}) collective-permute-start(f32[512,512]{1,0:T(8,128)S(1)} %pad_maximum_fusion.1), channel_id=1, source_target_pairs={{0,6},{1,7},{2,4},{3,5},{4,2},{5,3},{6,0},{7,1},{8,14},{9,15},{10,... | collective-permute-start | bytes 3145736 | tf_op jit(solution)/shard_map/ppermute | solution.py:399
  149.4 5.4 %shard_map.83.total = f32[2,512,1024]{2,1,0:T(8,128)S(1)} custom-call(s32[4]{0:T(128)S(1)} %get-tuple-element.177.order, f32[2,256,512]{2,1,0:T(8,128)S(1)} %shard_map.76.own_a, f32[2,256,512]{2,1,0:T(8,128)S(1)} %shard_map.77.own_b, f32[512,4096]{1,0:T(8,128)S(1)} %bitcast.17), custom_call_target="tpu_custom_call" | custom-call | flops 100000 | bytes 1024 | tf_op jit(solution)/shard_map/pallas_call | solution.py:303
  154.8 4.6 %shard_map.85 = (f32[256,256]{1,0:T(8,128)S(1)}, f32[256,256]{1,0:T(8,128)S(1)}, f32[256,256]{1,0:T(8,128)S(1)}, f32[256,256]{1,0:T(8,128)S(1)}, f32[256,512]{1,0:T(8,128)S(1)}, /*index=5*/f32[256,512]{1,0:T(8,128)S(1)}) custom-call(s32[2]{0:T(128)S(1)} %get-tuple-element.100.cores, f32[256,512]{1,0:T(8,128)S(1)} %collective-permute-done.23.got_a, ...), custom_call_target="tpu_custom_call" | custom-call | flops 100000 | bytes 1024 | tf_op jit(solution)/shard_map/pallas_call | solution.py:348
  160.0 4.6 %shard_map.84 = (f32[256,256]{1,0:T(8,128)S(1)}, f32[256,256]{1,0:T(8,128)S(1)}, f32[256,256]{1,0:T(8,128)S(1)}, f32[256,256]{1,0:T(8,128)S(1)}, f32[256,512]{1,0:T(8,128)S(1)}, /*index=5*/f32[256,512]{1,0:T(8,128)S(1)}) custom-call(s32[2]{0:T(128)S(1)} %get-tuple-element.100.cores, f32[256,512]{1,0:T(8,128)S(1)} %collective-permute-done.21.got_a, ...), custom_call_target="tpu_custom_call" | custom-call | flops 100000 | bytes 1024 | tf_op jit(solution)/shard_map/pallas_call | solution.py:348
  165.2 0.9 collective-permute-done.29
  166.7 7.5 %collective-permute-done.31 = f32[512,512]{1,0:T(8,128)S(1)} collective-permute-done((f32[512,512]{1,0:T(8,128)S(1)}, f32[512,512]{1,0:T(8,128)S(1)}, u32[]{:S(2)}, u32[]{:S(2)}) %collective-permute-start.31) | collective-permute-done | bytes 1048608 | tf_op jit(solution)/shard_map/ppermute | solution.py:399
  174.5 1.2 collective-permute-done.33
  176.1 1.5 pad_maximum_fusion
  (121 shorter events, 9.3 us)
Async XLA Ops:
  0.0 17.4 %copy-start = (s32[32,3]{0,1:T(4,128)S(1)}, s32[32,3]{0,1:T(4,128)}, u32[]{:S(2)}) copy-start(s32[32,3]{0,1:T(4,128)} %param.11) | copy-start | bytes 1156
  0.0 20.2 %collective-permute-start = (f32[1024,128]{1,0:T(8,128)}, f32[1024,128]{1,0:T(8,128)S(1)}, u32[]{:S(2)}, u32[]{:S(2)}) collective-permute-start(f32[1024,128]{1,0:T(8,128)} %k_own.1), channel_id=1, source_target_pairs={{0,8},{8,16},{16,24},{24,0},{32,40},{40,48},{48,56},{56,32},{64,72... | collective-permute-start | bytes 1572872 | tf_op jit(solution)/shard_map/ppermute | solution.py:390
  1.5 20.9 %collective-permute-start.1 = (f32[1024,128]{1,0:T(8,128)}, f32[1024,128]{1,0:T(8,128)S(1)}, u32[]{:S(2)}, u32[]{:S(2)}) collective-permute-start(f32[1024,128]{1,0:T(8,128)} %k_own.1), channel_id=1, source_target_pairs={{0,24},{8,0},{16,8},{24,16},{32,56},{40,32},{48,40},{56,48},{64,88... | collective-permute-start | bytes 1572872 | tf_op jit(solution)/shard_map/ppermute | solution.py:390
  2.0 20.4 %collective-permute-start.2 = (f32[1024,128]{1,0:T(8,128)}, f32[1024,128]{1,0:T(8,128)S(1)}, u32[]{:S(2)}, u32[]{:S(2)}) collective-permute-start(f32[1024,128]{1,0:T(8,128)} %v_own.1), channel_id=1, source_target_pairs={{0,32},{8,40},{16,48},{24,56},{32,64},{40,72},{48,80},{56,88},{64,... | collective-permute-start | bytes 1572872 | tf_op jit(solution)/shard_map/ppermute | solution.py:390
  3.9 18.5 %collective-permute-start.3 = (f32[1024,128]{1,0:T(8,128)}, f32[1024,128]{1,0:T(8,128)S(1)}, u32[]{:S(2)}, u32[]{:S(2)}) collective-permute-start(f32[1024,128]{1,0:T(8,128)} %v_own.1), channel_id=1, source_target_pairs={{0,96},{8,104},{16,112},{24,120},{32,0},{40,8},{48,16},{56,24},{64... | collective-permute-start | bytes 1572872 | tf_op jit(solution)/shard_map/ppermute | solution.py:390
  6.6 10.5 %copy-start.5 = (s32[32,8]{0,1:T(8,128)S(1)}, s32[32,8]{0,1:T(8,128)}, u32[]{:S(2)}) copy-start(s32[32,8]{0,1:T(8,128)} %param.10) | copy-start | bytes 3076
  6.6 18.0 %copy-start.2 = (f32[1024,128]{1,0:T(8,128)S(1)}, f32[1024,128]{1,0:T(8,128)}, u32[]{:S(2)}) copy-start(f32[1024,128]{1,0:T(8,128)} %v_own.1) | copy-start | bytes 1572868
  15.5 100.6 %collective-permute-start.19 = (f32[512,2048]{1,0:T(8,128)}, f32[512,2048]{1,0:T(8,128)}, u32[]{:S(2)}, u32[]{:S(2)}) collective-permute-start(f32[512,2048]{1,0:T(8,128)} %get-tuple-element.139), channel_id=1, source_target_pairs={{0,2},{1,3},{2,0},{3,1},{4,6},{5,7},{6,4},{7,5},{8,10},{9,11},{10,... | collective-permute-start | bytes 12582920 | tf_op jit(solution)/shard_map/ppermute | solution.py:399
  20.2 98.2 %collective-permute-start.20 = (f32[512,2048]{1,0:T(8,128)}, f32[512,2048]{1,0:T(8,128)S(1)}, u32[]{:S(2)}, u32[]{:S(2)}) collective-permute-start(f32[512,2048]{1,0:T(8,128)} %get-tuple-element.140), channel_id=1, source_target_pairs={{0,6},{1,7},{2,4},{3,5},{4,2},{5,3},{6,0},{7,1},{8,14},{9,15},{10,... | collective-permute-start | bytes 12582920 | tf_op jit(solution)/shard_map/ppermute | solution.py:399
  22.5 12.3 %collective-permute-start.5 = (f32[1024,128]{1,0:T(8,128)S(1)}, f32[1024,128]{1,0:T(8,128)S(1)}, u32[]{:S(2)}, u32[]{:S(2)}) collective-permute-start(f32[1024,128]{1,0:T(8,128)S(1)} %collective-permute-done.3.refs_5_), channel_id=1, source_target_pairs={{0,96},{8,104},{16,112},{24,120},{32,0},{40,8},{48,16},{56,24},{64... | collective-permute-start | bytes 1572872 | tf_op jit(solution)/shard_map/ppermute | solution.py:390
  24.7 20.1 %copy-start.3 = (f32[1024,128]{1,0:T(8,128)S(1)}, f32[1024,128]{1,0:T(8,128)}, u32[]{:S(2)}) copy-start(f32[1024,128]{1,0:T(8,128)} %k_own.1) | copy-start | bytes 1572868
  24.7 17.4 %collective-permute-start.6 = (f32[1536,128]{1,0:T(8,128)S(1)}, f32[1536,128]{1,0:T(8,128)S(1)}, u32[]{:S(2)}, u32[]{:S(2)}) collective-permute-start(f32[1536,128]{1,0:T(8,128)S(1)} %pad_maximum_fusion.4), channel_id=1, source_target_pairs={{0,8},{8,16},{16,24},{24,0},{32,40},{40,48},{48,56},{56,32},{64,72... | collective-permute-start | bytes 2359304 | tf_op jit(solution)/shard_map/ppermute | solution.py:390
  26.4 17.1 %collective-permute-start.4 = (f32[1536,128]{1,0:T(8,128)S(1)}, f32[1536,128]{1,0:T(8,128)S(1)}, u32[]{:S(2)}, u32[]{:S(2)}) collective-permute-start(f32[1536,128]{1,0:T(8,128)S(1)} %pad_maximum_fusion.3), channel_id=1, source_target_pairs={{0,24},{8,0},{16,8},{24,16},{32,56},{40,32},{48,40},{56,48},{64,88... | collective-permute-start | bytes 2359304 | tf_op jit(solution)/shard_map/ppermute | solution.py:390
  34.8 0.7 collective-permute-start.7
  43.5 22.4 %copy-start.4 = (f32[1024,512]{1,0:T(8,128)S(1)}, f32[1024,512]{1,0:T(8,128)}, u32[]{:S(2)}) copy-start(f32[1024,512]{1,0:T(8,128)} %q.1) | copy-start | bytes 6291460
  43.5 8.0 %collective-permute-start.8 = (f32[512,128]{1,0:T(8,128)S(1)}, f32[512,128]{1,0:T(8,128)S(1)}, u32[]{:S(2)}, u32[]{:S(2)}) collective-permute-start(f32[512,128]{1,0:T(8,128)S(1)} %slice.44), channel_id=1, source_target_pairs={{0,8},{8,16},{16,24},{24,0},{32,40},{40,48},{48,56},{56,32},{64,72... | collective-permute-start | bytes 786440 | tf_op jit(solution)/shard_map/ppermute | solution.py:390
  46.6 16.5 %collective-permute-start.11 = (f32[1024,128]{1,0:T(8,128)S(1)}, f32[1024,128]{1,0:T(8,128)S(1)}, u32[]{:S(2)}, u32[]{:S(2)}) collective-permute-start(f32[1024,128]{1,0:T(8,128)S(1)} %get-tuple-element.113), channel_id=1, source_target_pairs={{0,32},{8,40},{16,48},{24,56},{32,0},{40,8},{48,16},{56,24},{64,96... | collective-permute-start | bytes 1572872 | tf_op jit(solution)/shard_map/ppermute | solution.py:390
  47.0 18.7 %collective-permute-start.12 = (f32[1024,128]{1,0:T(8,128)S(1)}, f32[1024,128]{1,0:T(8,128)S(1)}, u32[]{:S(2)}, u32[]{:S(2)}) collective-permute-start(f32[1024,128]{1,0:T(8,128)S(1)} %get-tuple-element.114), channel_id=1, source_target_pairs={{0,96},{8,104},{16,112},{24,120},{32,64},{40,72},{48,80},{56,88},{... | collective-permute-start | bytes 1572872 | tf_op jit(solution)/shard_map/ppermute | solution.py:390
  51.6 7.1 %collective-permute-start.9 = (f32[512,128]{1,0:T(8,128)S(1)}, f32[512,128]{1,0:T(8,128)S(1)}, u32[]{:S(2)}, u32[]{:S(2)}) collective-permute-start(f32[512,128]{1,0:T(8,128)S(1)} %slice.45), channel_id=1, source_target_pairs={{0,24},{8,0},{16,8},{24,16},{32,56},{40,32},{48,40},{56,48},{64,88... | collective-permute-start | bytes 786440 | tf_op jit(solution)/shard_map/ppermute | solution.py:390
  58.7 18.2 %collective-permute-start.10 = (f32[1024,128]{1,0:T(8,128)S(1)}, f32[1024,128]{1,0:T(8,128)S(1)}, u32[]{:S(2)}, u32[]{:S(2)}) collective-permute-start(f32[1024,128]{1,0:T(8,128)S(1)} %slice.46.refs_2_.k_far), channel_id=1, source_target_pairs={{0,32},{8,40},{32,64},{40,72},{64,96},{72,104},{1,33},{9,41},{33,6... | collective-permute-start | bytes 1572872 | tf_op jit(solution)/shard_map/ppermute | solution.py:390
  63.1 11.2 %collective-permute-start.13 = (f32[1024,128]{1,0:T(8,128)S(1)}, f32[1024,128]{1,0:T(8,128)S(1)}, u32[]{:S(2)}, u32[]{:S(2)}) collective-permute-start(f32[1024,128]{1,0:T(8,128)S(1)} %get-tuple-element.115), channel_id=1, source_target_pairs={{0,8},{8,0},{16,24},{24,16},{32,40},{40,32},{48,56},{56,48},{64,72... | collective-permute-start | bytes 1572872 | tf_op jit(solution)/shard_map/ppermute | solution.py:390
  65.7 11.2 %collective-permute-start.14 = (f32[1024,128]{1,0:T(8,128)S(1)}, f32[1024,128]{1,0:T(8,128)S(1)}, u32[]{:S(2)}, u32[]{:S(2)}) collective-permute-start(f32[1024,128]{1,0:T(8,128)S(1)} %get-tuple-element.116), channel_id=1, source_target_pairs={{0,24},{8,16},{16,8},{24,0},{32,56},{40,48},{48,40},{56,32},{64,88... | collective-permute-start | bytes 1572872 | tf_op jit(solution)/shard_map/ppermute | solution.py:390
  77.0 9.3 %collective-permute-start.18 = (f32[1024,128]{1,0:T(8,128)S(1)}, f32[1024,128]{1,0:T(8,128)S(1)}, u32[]{:S(2)}, u32[]{:S(2)}) collective-permute-start(f32[1024,128]{1,0:T(8,128)S(1)} %add.222), channel_id=1, source_target_pairs={{0,8},{8,0},{16,24},{24,16},{32,40},{40,32},{48,56},{56,48},{64,72... | collective-permute-start | bytes 1572872 | tf_op jit(solution)/shard_map/ppermute | solution.py:390
  78.0 22.5 %collective-permute-start.17 = (f32[1024,128]{1,0:T(8,128)S(1)}, f32[1024,128]{1,0:T(8,128)S(1)}, u32[]{:S(2)}, u32[]{:S(2)}) collective-permute-start(f32[1024,128]{1,0:T(8,128)S(1)} %add.221), channel_id=1, source_target_pairs={{0,24},{8,16},{16,8},{24,0},{32,56},{40,48},{48,40},{56,32},{64,88... | collective-permute-start | bytes 1572872 | tf_op jit(solution)/shard_map/ppermute | solution.py:390
  78.3 22.2 %collective-permute-start.16 = (f32[1024,128]{1,0:T(8,128)S(1)}, f32[1024,128]{1,0:T(8,128)S(1)}, u32[]{:S(2)}, u32[]{:S(2)}) collective-permute-start(f32[1024,128]{1,0:T(8,128)S(1)} %add.220), channel_id=1, source_target_pairs={{0,32},{8,40},{16,48},{24,56},{32,0},{40,8},{48,16},{56,24},{64,96... | collective-permute-start | bytes 1572872 | tf_op jit(solution)/shard_map/ppermute | solution.py:390
  86.3 14.2 %collective-permute-start.15 = (f32[1024,128]{1,0:T(8,128)S(1)}, f32[1024,128]{1,0:T(8,128)S(1)}, u32[]{:S(2)}, u32[]{:S(2)}) collective-permute-start(f32[1024,128]{1,0:T(8,128)S(1)} %add.219), channel_id=1, source_target_pairs={{0,96},{8,104},{16,112},{24,120},{32,64},{40,72},{48,80},{56,88},{... | collective-permute-start | bytes 1572872 | tf_op jit(solution)/shard_map/ppermute | solution.py:390
  100.8 29.0 %slice-start = ((s8[8388608]{0:T(1024)(128)(4,1)}), s8[4194304]{0:T(1024)(128)(4,1)S(1)}, s32[]{:S(2)}) async-start(s8[8388608]{0:T(1024)(128)(4,1)} %bitcast.16), calls=%async_computation | async-start | bytes 8388608
  107.1 22.7 %slice-start.1 = ((s8[8388608]{0:T(1024)(128)(4,1)}), s8[4194304]{0:T(1024)(128)(4,1)S(1)}, s32[]{:S(2)}) async-start(s8[8388608]{0:T(1024)(128)(4,1)} %bitcast.16), calls=%async_computation.1 | async-start | bytes 8388608
  113.5 10.6 %collective-permute-start.21 = (f32[256,512]{1,0:T(8,128)S(1)}, f32[256,512]{1,0:T(8,128)S(1)}, u32[]{:S(2)}, u32[]{:S(2)}) collective-permute-start(f32[256,512]{1,0:T(8,128)S(1)} %get-tuple-element.212), channel_id=1, source_target_pairs={{0,2},{1,3},{2,0},{3,1},{4,6},{5,7},{6,4},{7,5},{8,10},{9,11},{10,... | collective-permute-start | bytes 1572872 | tf_op jit(solution)/shard_map/ppermute | solution.py:399
  114.8 14.9 %collective-permute-start.22 = (f32[256,512]{1,0:T(8,128)S(1)}, f32[256,512]{1,0:T(8,128)S(1)}, u32[]{:S(2)}, u32[]{:S(2)}) collective-permute-start(f32[256,512]{1,0:T(8,128)S(1)} %get-tuple-element.211), channel_id=1, source_target_pairs={{0,6},{1,7},{2,4},{3,5},{4,2},{5,3},{6,0},{7,1},{8,14},{9,15},{10,... | collective-permute-start | bytes 1572872 | tf_op jit(solution)/shard_map/ppermute | solution.py:399
  115.5 24.2 %collective-permute-start.23 = (f32[256,512]{1,0:T(8,128)S(1)}, f32[256,512]{1,0:T(8,128)S(1)}, u32[]{:S(2)}, u32[]{:S(2)}) collective-permute-start(f32[256,512]{1,0:T(8,128)S(1)} %get-tuple-element.210), channel_id=1, source_target_pairs={{0,2},{1,3},{2,0},{3,1},{4,6},{5,7},{6,4},{7,5},{8,10},{9,11},{10,... | collective-permute-start | bytes 1572872 | tf_op jit(solution)/shard_map/ppermute | solution.py:399
  116.2 23.6 %collective-permute-start.24 = (f32[256,512]{1,0:T(8,128)S(1)}, f32[256,512]{1,0:T(8,128)S(1)}, u32[]{:S(2)}, u32[]{:S(2)}) collective-permute-start(f32[256,512]{1,0:T(8,128)S(1)} %get-tuple-element.209), channel_id=1, source_target_pairs={{0,6},{1,7},{2,4},{3,5},{4,2},{5,3},{6,0},{7,1},{8,14},{9,15},{10,... | collective-permute-start | bytes 1572872 | tf_op jit(solution)/shard_map/ppermute | solution.py:399
  139.7 3.6 %collective-permute-start.25 = (f32[256,512]{1,0:T(8,128)S(1)}, f32[256,512]{1,0:T(8,128)S(1)}, u32[]{:S(2)}, u32[]{:S(2)}) collective-permute-start(f32[256,512]{1,0:T(8,128)S(1)} %get-tuple-element.158), channel_id=1, source_target_pairs={{0,1},{1,0},{2,3},{3,2},{4,5},{5,4},{6,7},{7,6},{8,9},{9,8},{10,11... | collective-permute-start | bytes 1572872 | tf_op jit(solution)/shard_map/ppermute | solution.py:399
  139.8 3.5 %collective-permute-start.26 = (f32[256,512]{1,0:T(8,128)S(1)}, f32[256,512]{1,0:T(8,128)S(1)}, u32[]{:S(2)}, u32[]{:S(2)}) collective-permute-start(f32[256,512]{1,0:T(8,128)S(1)} %get-tuple-element.159), channel_id=1, source_target_pairs={{0,1},{1,0},{2,3},{3,2},{4,5},{5,4},{6,7},{7,6},{8,9},{9,8},{10,11... | collective-permute-start | bytes 1572872 | tf_op jit(solution)/shard_map/ppermute | solution.py:399
  143.4 3.8 %collective-permute-start.27 = (f32[256,512]{1,0:T(8,128)S(1)}, f32[256,512]{1,0:T(8,128)S(1)}, u32[]{:S(2)}, u32[]{:S(2)}) collective-permute-start(f32[256,512]{1,0:T(8,128)S(1)} %get-tuple-element.165), channel_id=1, source_target_pairs={{0,1},{1,0},{2,3},{3,2},{4,5},{5,4},{6,7},{7,6},{8,9},{9,8},{10,11... | collective-permute-start | bytes 1572872 | tf_op jit(solution)/shard_map/ppermute | solution.py:399
  143.6 3.6 %collective-permute-start.28 = (f32[256,512]{1,0:T(8,128)S(1)}, f32[256,512]{1,0:T(8,128)S(1)}, u32[]{:S(2)}, u32[]{:S(2)}) collective-permute-start(f32[256,512]{1,0:T(8,128)S(1)} %get-tuple-element.166), channel_id=1, source_target_pairs={{0,1},{1,0},{2,3},{3,2},{4,5},{5,4},{6,7},{7,6},{8,9},{9,8},{10,11... | collective-permute-start | bytes 1572872 | tf_op jit(solution)/shard_map/ppermute | solution.py:399
  147.5 26.7 %collective-permute-start.31 = (f32[512,512]{1,0:T(8,128)S(1)}, f32[512,512]{1,0:T(8,128)S(1)}, u32[]{:S(2)}, u32[]{:S(2)}) collective-permute-start(f32[512,512]{1,0:T(8,128)S(1)} %pad_maximum_fusion.1), channel_id=1, source_target_pairs={{0,6},{1,7},{2,4},{3,5},{4,2},{5,3},{6,0},{7,1},{8,14},{9,15},{10,... | collective-permute-start | bytes 3145736 | tf_op jit(solution)/shard_map/ppermute | solution.py:399
  149.4 26.3 %collective-permute-start.34 = (f32[512,512]{1,0:T(8,128)S(1)}, f32[512,512]{1,0:T(8,128)S(1)}, u32[]{:S(2)}, u32[]{:S(2)}) collective-permute-start(f32[512,512]{1,0:T(8,128)S(1)} %pad_maximum_fusion.2), channel_id=1, source_target_pairs={{0,2},{1,3},{2,0},{3,1},{4,6},{5,7},{6,4},{7,5},{8,10},{9,11},{10,... | collective-permute-start | bytes 3145736 | tf_op jit(solution)/shard_map/ppermute | solution.py:399
  159.4 5.3 %collective-permute-start.35 = (f32[256,256]{1,0:T(8,128)S(1)}, f32[256,256]{1,0:T(8,128)S(1)}, u32[]{:S(2)}, u32[]{:S(2)}) collective-permute-start(f32[256,256]{1,0:T(8,128)S(1)} %get-tuple-element.190), channel_id=1, source_target_pairs={{0,1},{1,0},{2,3},{3,2},{4,5},{5,4},{6,7},{7,6},{8,9},{9,8},{10,11... | collective-permute-start | bytes 786440 | tf_op jit(solution)/shard_map/ppermute | solution.py:399
  159.5 5.6 %collective-permute-start.36 = (f32[256,256]{1,0:T(8,128)S(1)}, f32[256,256]{1,0:T(8,128)S(1)}, u32[]{:S(2)}, u32[]{:S(2)}) collective-permute-start(f32[256,256]{1,0:T(8,128)S(1)} %get-tuple-element.191), channel_id=1, source_target_pairs={{0,1},{1,0},{2,3},{3,2},{4,5},{5,4},{6,7},{7,6},{8,9},{9,8},{10,11... | collective-permute-start | bytes 786440 | tf_op jit(solution)/shard_map/ppermute | solution.py:399
  164.5 1.6 collective-permute-start.29
  164.7 1.8 %collective-permute-start.30 = (f32[256,256]{1,0:T(8,128)S(1)}, f32[256,256]{1,0:T(8,128)S(1)}, u32[]{:S(2)}, u32[]{:S(2)}) collective-permute-start(f32[256,256]{1,0:T(8,128)S(1)} %get-tuple-element.181), channel_id=1, source_target_pairs={{0,1},{1,0},{2,3},{3,2},{4,5},{5,4},{6,7},{7,6},{8,9},{9,8},{10,11... | collective-permute-start | bytes 786440 | tf_op jit(solution)/shard_map/ppermute | solution.py:399
  165.1 9.4 %collective-permute-start.37 = (f32[256,256]{1,0:T(8,128)S(1)}, f32[256,256]{1,0:T(8,128)S(1)}, u32[]{:S(2)}, u32[]{:S(2)}) collective-permute-start(f32[256,256]{1,0:T(8,128)S(1)} %get-tuple-element.193), channel_id=1, source_target_pairs={{0,1},{1,0},{2,3},{3,2},{4,5},{5,4},{6,7},{7,6},{8,9},{9,8},{10,11... | collective-permute-start | bytes 786440 | tf_op jit(solution)/shard_map/ppermute | solution.py:399
  166.2 8.4 %collective-permute-start.38 = (f32[256,256]{1,0:T(8,128)S(1)}, f32[256,256]{1,0:T(8,128)S(1)}, u32[]{:S(2)}, u32[]{:S(2)}) collective-permute-start(f32[256,256]{1,0:T(8,128)S(1)} %get-tuple-element.194), channel_id=1, source_target_pairs={{0,1},{1,0},{2,3},{3,2},{4,5},{5,4},{6,7},{7,6},{8,9},{9,8},{10,11... | collective-permute-start | bytes 786440 | tf_op jit(solution)/shard_map/ppermute | solution.py:399
  166.5 8.0 %collective-permute-start.32 = (f32[256,256]{1,0:T(8,128)S(1)}, f32[256,256]{1,0:T(8,128)S(1)}, u32[]{:S(2)}, u32[]{:S(2)}) collective-permute-start(f32[256,256]{1,0:T(8,128)S(1)} %get-tuple-element.184), channel_id=1, source_target_pairs={{0,1},{1,0},{2,3},{3,2},{4,5},{5,4},{6,7},{7,6},{8,9},{9,8},{10,11... | collective-permute-start | bytes 786440 | tf_op jit(solution)/shard_map/ppermute | solution.py:399
  174.2 1.5 collective-permute-start.33
  176.0 1.5 copy-start.1

commit v14 on v13

--- a/solution.py
+++ b/solution.py
@@ -393,7 +393,6 @@
     k_left = send(key_rows, right)
     k_right = send(key_rows, left)
     v_below = send(value_vectors, up)
-    v_above = send(value_vectors, down)
 
     y = head_index // 2
     over_head = lambda a, bits: lax.ppermute(a, "head", [(i, i ^ bits) for i in range(head_size)])
@@ -429,8 +428,10 @@
     orders = (pass_order, keep_order, cores)
     small = (vert_pos, slash_pos, first_row, back, wraps, orders, k_place, k_held, v_place, v_held)
 
-    (k_left, k_right, v_below, v_above), small = lax.optimization_barrier(
-        ((k_left, k_right, v_below, v_above), small)
+    k_left, late_values = lax.optimization_barrier((k_left, value_vectors))
+    v_above = send(late_values, down)
+    (k_left, k_right, v_below), small = lax.optimization_barrier(
+        ((k_left, k_right, v_below), small)
     )
     vert_pos, slash_pos, first_row, back, wraps, orders, k_place, k_held, v_place, v_held = small
     half = rows // 2
@@ -476,8 +477,8 @@
     own_b = attend(q, *near, half, first_row, arrays)
     got_b = meeting(own_b)
     own_b, near_weight, far_weight = lax.optimization_barrier((own_b, near_weight, far_weight))
-    own_b, got_a = lax.optimization_barrier((own_b, got_a))
     total = project_chip(own_a, own_b, out_weight, pass_order)
+    total, got_a = lax.optimization_barrier((total, got_a))
     product = lambda got, total, unit, keep, **kind: project_pair(
         got, near_weight, far_weight, total, unit, keep, cores, **kind
     )

time: 180 us -> 176 us (0.978)
  waiting for transfers between devices: 61.7 us -> 46.1 us
  starting transfers between devices: 44.5 us -> 52.3 us
  Pallas kernels: 63.8 us -> 66.7 us
    ppermute x20, waiting for transfers between devices: 21.3 us -> 12.7 us  [body(): lax.ppermute(a, 'head', [(i, i ^ bits) for i in range(head_size)])]
    ppermute x19, starting transfers between devices: 31.3 us -> 39.8 us  [body(): send = lambda a, pairs: lax.ppermute(a, 'seq', pairs)]
    ppermute x19, waiting for transfers between devices: 40.5 us -> 33.4 us  [body(): send = lambda a, pairs: lax.ppermute(a, 'seq', pairs)]
    pallas_call x5, Pallas kernels: 19.7 us -> 22.7 us  [project_pair(): pl.pallas_call(functools.partial(pair_kernel, pieces), out_shape=shapes,...]
  transfers between devices with their start and end apart: 39 -> 39, of which waited for: 14 -> 14; matrix products, arithmetic and copies ran while one was open for 2% -> 2% of each run, Pallas kernels for 36% -> 39%
where the time goes in v14:
time: 176 us; the launch traced here: 173 us
  Pallas kernels  66.7 us (38%)
  starting transfers between devices  52.3 us (30%)
  waiting for transfers between devices  46.1 us (26%)
  other arithmetic  4.51 us (3%)
  local copies, waits for them, and re-layouts  1.79 us (1%)
    ppermute x19, starting transfers between devices, body(): send = lambda a, pairs: lax.ppermute(a, 'seq', pairs)  39.8 us
    ppermute x19, waiting for transfers between devices, body(): send = lambda a, pairs: lax.ppermute(a, 'seq', pairs)  33.4 us
    pallas_call x5, Pallas kernels, project_pair(): pl.pallas_call(functools.partial(pair_kernel, pieces), out_shape=shapes,...  22.7 us
    ppermute x20, waiting for transfers between devices, body(): lax.ppermute(a, 'head', [(i, i ^ bits) for i in range(head_size)])  12.7 us
    pallas_call x2, Pallas kernels, attend(): pl.pallas_call(functools.partial(attend_kernel, start), grid=(2, heads //...  12.6 us
    ppermute x20, starting transfers between devices, body(): lax.ppermute(a, 'head', [(i, i ^ bits) for i in range(head_size)])  12.5 us
    pallas_call x2, Pallas kernels, project_chip(): pl.pallas_call(chip_kernel, out_shape=jax.ShapeDtypeStruct((2, 2 * rows,...  10.8 us
    pallas_call x1, Pallas kernels, attend_near(): pl.pallas_call(functools.partial(near_kernel, start), grid=(rows // TILE,...  9.64 us
  transfers between devices with their start and end apart: 39, of which 14 were waited for; matrix products, arithmetic and copies ran while one was open for 2% of the time, Pallas kernels for 39%

profile of v14, /device:TPU:2, one launch (start us, length us, event | category | flops | bytes accessed | tf_op | source)
XLA Modules:
  0.0 172.7 jit_solution(8630600710200802954)
XLA Ops:
  0.0 1.5 collective-permute-start
  1.5 0.5 collective-permute-start.1
  2.0 1.9 %collective-permute-start.2 = (f32[1024,128]{1,0:T(8,128)}, f32[1024,128]{1,0:T(8,128)S(1)}, u32[]{:S(2)}, u32[]{:S(2)}) collective-permute-start(f32[1024,128]{1,0:T(8,128)} %v_own.1), channel_id=1, source_target_pairs={{0,32},{8,40},{16,48},{24,56},{32,64},{40,72},{48,80},{56,88},{64,... | collective-permute-start | bytes 1572872 | tf_op jit(solution)/shard_map/ppermute | solution.py:390
  3.9 0.5 add_xor_fusion.chips
  4.5 8.9 %shard_map.78 = (f32[512,2048]{1,0:T(8,128)}, f32[512,2048]{1,0:T(8,128)}) custom-call(s32[3]{0:T(128)} %add_xor_fusion.chips, f32[512,4096]{1,0:T(8,128)} %w.3, f32[512,4096]{1,0:T(8,128)} %w.3, f32[512,4096]{1,0:T(8,128)} %w.3), custom_call_target="tpu_custom_call" | custom-call | flops 1024 | bytes 1024 | tf_op jit(solution)/shard_map/pallas_call | solution.py:266
  13.4 1.6 collective-permute-start.19
  15.0 2.2 %collective-permute-start.20 = (f32[512,2048]{1,0:T(8,128)}, f32[512,2048]{1,0:T(8,128)}, u32[]{:S(2)}, u32[]{:S(2)}) collective-permute-start(f32[512,2048]{1,0:T(8,128)} %get-tuple-element.144), channel_id=1, source_target_pairs={{0,6},{1,7},{2,4},{3,5},{4,2},{5,3},{6,0},{7,1},{8,14},{9,15},{10,... | collective-permute-start | bytes 12582920 | tf_op jit(solution)/shard_map/ppermute | solution.py:398
  20.3 0.7 collective-permute-start.7
  21.1 2.2 %collective-permute-start.4 = (f32[1024,128]{1,0:T(8,128)S(1)}, f32[1024,128]{1,0:T(8,128)S(1)}, u32[]{:S(2)}, u32[]{:S(2)}) collective-permute-start(f32[1024,128]{1,0:T(8,128)S(1)} %copy-done.2), channel_id=1, source_target_pairs={{0,96},{8,104},{16,112},{24,120},{32,0},{40,8},{48,16},{56,24},{64... | collective-permute-start | bytes 1572872 | tf_op jit(solution)/shard_map/ppermute | solution.py:390
  23.3 1.6 collective-permute-start.6
  25.0 10.6 %collective-permute-start.3 = (f32[1536,128]{1,0:T(8,128)S(1)}, f32[1536,128]{1,0:T(8,128)S(1)}, u32[]{:S(2)}, u32[]{:S(2)}) collective-permute-start(f32[1536,128]{1,0:T(8,128)S(1)} %pad_maximum_fusion.3), channel_id=1, source_target_pairs={{0,24},{8,0},{16,8},{24,16},{32,56},{40,32},{48,40},{56,48},{64,88... | collective-permute-start | bytes 2359304 | tf_op jit(solution)/shard_map/ppermute | solution.py:390
  35.6 3.0 %collective-permute-start.5 = (f32[1024,128]{1,0:T(8,128)S(1)}, f32[1024,128]{1,0:T(8,128)S(1)}, u32[]{:S(2)}, u32[]{:S(2)}) collective-permute-start(f32[1024,128]{1,0:T(8,128)S(1)} %collective-permute-done.4.refs_5_), channel_id=1, source_target_pairs={{0,96},{8,104},{16,112},{24,120},{32,0},{40,8},{48,16},{56,24},{64... | collective-permute-start | bytes 1572872 | tf_op jit(solution)/shard_map/ppermute | solution.py:390
  38.6 3.5 %collective-permute-done.6 = f32[1536,128]{1,0:T(8,128)S(1)} collective-permute-done((f32[1536,128]{1,0:T(8,128)S(1)}, f32[1536,128]{1,0:T(8,128)S(1)}, u32[]{:S(2)}, u32[]{:S(2)}) %collective-permute-start.6) | collective-permute-done | bytes 786464 | tf_op jit(solution)/shard_map/ppermute | solution.py:390
  42.1 8.0 %collective-permute-done.3 = f32[1536,128]{1,0:T(8,128)S(1)} collective-permute-done((f32[1536,128]{1,0:T(8,128)S(1)}, f32[1536,128]{1,0:T(8,128)S(1)}, u32[]{:S(2)}, u32[]{:S(2)}) %collective-permute-start.3) | collective-permute-done | bytes 786464 | tf_op jit(solution)/shard_map/ppermute | solution.py:390
  50.2 1.9 %shard_map.74 = (f32[1024,128]{1,0:T(8,128)S(1)}, f32[1024,128]{1,0:T(8,128)S(1)}, f32[1024,128]{1,0:T(8,128)S(1)}, f32[1024,128]{1,0:T(8,128)S(1)}) custom-call(s32[32]{0:T(128)S(1)} %get-tuple-element.110.k_place, s32[32]{0:T(128)S(1)} %compare_convert_fusion.1.k_held, s32[32]{0:T(128)S(1)} %get-tuple-element.112.v_place, ...), custom_call_target="tpu_custom_call" | custom-call | flops 1024 | bytes 1024 | tf_op jit(solution)/shard_map/pallas_call | solution.py:48
  52.1 2.7 %collective-permute-start.11 = (f32[1024,128]{1,0:T(8,128)S(1)}, f32[1024,128]{1,0:T(8,128)S(1)}, u32[]{:S(2)}, u32[]{:S(2)}) collective-permute-start(f32[1024,128]{1,0:T(8,128)S(1)} %get-tuple-element.115), channel_id=1, source_target_pairs={{0,32},{8,40},{16,48},{24,56},{32,0},{40,8},{48,16},{56,24},{64,96... | collective-permute-start | bytes 1572872 | tf_op jit(solution)/shard_map/ppermute | solution.py:390
  54.8 2.2 %collective-permute-start.12 = (f32[1024,128]{1,0:T(8,128)S(1)}, f32[1024,128]{1,0:T(8,128)S(1)}, u32[]{:S(2)}, u32[]{:S(2)}) collective-permute-start(f32[1024,128]{1,0:T(8,128)S(1)} %get-tuple-element.116), channel_id=1, source_target_pairs={{0,96},{8,104},{16,112},{24,120},{32,64},{40,72},{48,80},{56,88},{... | collective-permute-start | bytes 1572872 | tf_op jit(solution)/shard_map/ppermute | solution.py:390
  57.1 3.2 %collective-permute-start.9 = (f32[512,128]{1,0:T(8,128)S(1)}, f32[512,128]{1,0:T(8,128)S(1)}, u32[]{:S(2)}, u32[]{:S(2)}) collective-permute-start(f32[512,128]{1,0:T(8,128)S(1)} %slice.45), channel_id=1, source_target_pairs={{0,24},{8,0},{16,8},{24,16},{32,56},{40,32},{48,40},{56,48},{64,88... | collective-permute-start | bytes 786440 | tf_op jit(solution)/shard_map/ppermute | solution.py:390
  60.3 4.5 %collective-permute-done.9.v_far_b = f32[512,128]{1,0:T(8,128)S(1)} collective-permute-done((f32[512,128]{1,0:T(8,128)S(1)}, f32[512,128]{1,0:T(8,128)S(1)}, u32[]{:S(2)}, u32[]{:S(2)}) %collective-permute-start.9) | collective-permute-done | bytes 262176 | tf_op jit(solution)/shard_map/ppermute | solution.py:390
  64.8 3.9 %collective-permute-start.10 = (f32[1024,128]{1,0:T(8,128)S(1)}, f32[1024,128]{1,0:T(8,128)S(1)}, u32[]{:S(2)}, u32[]{:S(2)}) collective-permute-start(f32[1024,128]{1,0:T(8,128)S(1)} %slice.46.refs_2_.k_far), channel_id=1, source_target_pairs={{0,32},{8,40},{32,64},{40,72},{64,96},{72,104},{1,33},{9,41},{33,6... | collective-permute-start | bytes 1572872 | tf_op jit(solution)/shard_map/ppermute | solution.py:390
  68.7 2.6 %collective-permute-start.13 = (f32[1024,128]{1,0:T(8,128)S(1)}, f32[1024,128]{1,0:T(8,128)S(1)}, u32[]{:S(2)}, u32[]{:S(2)}) collective-permute-start(f32[1024,128]{1,0:T(8,128)S(1)} %get-tuple-element.117), channel_id=1, source_target_pairs={{0,8},{8,0},{16,24},{24,16},{32,40},{40,32},{48,56},{56,48},{64,72... | collective-permute-start | bytes 1572872 | tf_op jit(solution)/shard_map/ppermute | solution.py:390
  71.5 8.1 %collective-permute-done.13 = f32[1024,128]{1,0:T(8,128)S(1)} collective-permute-done((f32[1024,128]{1,0:T(8,128)S(1)}, f32[1024,128]{1,0:T(8,128)S(1)}, u32[]{:S(2)}, u32[]{:S(2)}) %collective-permute-start.13) | collective-permute-done | bytes 524320 | tf_op jit(solution)/shard_map/ppermute | solution.py:390
  79.6 2.6 %collective-permute-done.14 = f32[1024,128]{1,0:T(8,128)S(1)} collective-permute-done((f32[1024,128]{1,0:T(8,128)S(1)}, f32[1024,128]{1,0:T(8,128)S(1)}, u32[]{:S(2)}, u32[]{:S(2)}) %collective-permute-start.14) | collective-permute-done | bytes 524320 | tf_op jit(solution)/shard_map/ppermute | solution.py:390
  82.3 1.0 collective-permute-start.18
  83.5 1.7 collective-permute-start.16
  85.3 6.3 %collective-permute-done.18 = f32[1024,128]{1,0:T(8,128)S(1)} collective-permute-done((f32[1024,128]{1,0:T(8,128)S(1)}, f32[1024,128]{1,0:T(8,128)S(1)}, u32[]{:S(2)}, u32[]{:S(2)}) %collective-permute-start.18) | collective-permute-done | bytes 524320 | tf_op jit(solution)/shard_map/ppermute | solution.py:390
  91.9 9.6 %shard_map.75 = (f32[1024,512]{1,0:T(8,128)S(1)}, f32[1024,256]{1,0:T(8,128)S(1)}) custom-call(s32[1]{0:T(128)} %bitcast.1.first_row, s32[4,4]{1,0:T(4,128)S(1)} %get-tuple-element.121.back, s32[2]{0:T(128)S(1)} %add_convert_fusion.wraps, f32[1024,512]{1,0:T(8,128)S(1)} %shard_map.73.q, f32[1024,128]{1,0:T(8,128)S(1)} %slice.46.refs_2_.k_far, ...), custom_call_target="tpu_custom_call" | custom-call | flops 100000 | bytes 1024 | tf_op jit(solution)/shard_map/pallas_call | solution.py:179
  102.2 6.3 %shard_map.76.own_a = f32[2,256,512]{2,1,0:T(8,128)S(1)} custom-call(s32[1]{0:T(128)} %bitcast.1.first_row, f32[1024,512]{1,0:T(8,128)S(1)} %shard_map.73.q, f32[1024,512]{1,0:T(8,128)S(1)} %get-tuple-element.134.near, f32[1024,256]{1,0:T(8,128)S(1)} %get-tuple-element.135.stats, f32[1024,128]{1,0:T(8,128)S(1)} %add.223.k_a, f32[1024,128]{1,0:T(8,128)S(1)} %add.224.k_b, ...), custom_call_target="tpu_custom_call" | custom-call | flops 100000 | bytes 1024 | tf_op jit(solution)/shard_map/pallas_call | solution.py:236
  108.5 6.3 %shard_map.77.own_b = f32[2,256,512]{2,1,0:T(8,128)S(1)} custom-call(s32[1]{0:T(128)} %bitcast.1.first_row, f32[1024,512]{1,0:T(8,128)S(1)} %shard_map.73.q, f32[1024,512]{1,0:T(8,128)S(1)} %get-tuple-element.134.near, f32[1024,256]{1,0:T(8,128)S(1)} %get-tuple-element.135.stats, f32[1024,128]{1,0:T(8,128)S(1)} %add.223.k_a, f32[1024,128]{1,0:T(8,128)S(1)} %add.224.k_b, ...), custom_call_target="tpu_custom_call" | custom-call | flops 100000 | bytes 1024 | tf_op jit(solution)/shard_map/pallas_call | solution.py:236
  114.9 1.7 collective-permute-start.21
  116.6 0.7 collective-permute-start.22
  117.6 2.5 %collective-permute-start.24 = (f32[256,512]{1,0:T(8,128)S(1)}, f32[256,512]{1,0:T(8,128)S(1)}, u32[]{:S(2)}, u32[]{:S(2)}) collective-permute-start(f32[256,512]{1,0:T(8,128)S(1)} %get-tuple-element.211), channel_id=1, source_target_pairs={{0,6},{1,7},{2,4},{3,5},{4,2},{5,3},{6,0},{7,1},{8,14},{9,15},{10,... | collective-permute-start | bytes 1572872 | tf_op jit(solution)/shard_map/ppermute | solution.py:398
  120.1 5.4 %shard_map.79.total = f32[2,512,1024]{2,1,0:T(8,128)S(1)} custom-call(s32[4]{0:T(128)S(1)} %get-tuple-element.103.order, f32[2,256,512]{2,1,0:T(8,128)S(1)} %shard_map.76.own_a, f32[2,256,512]{2,1,0:T(8,128)S(1)} %shard_map.77.own_b, f32[512,4096]{1,0:T(8,128)S(1)} %bitcast.17), custom_call_target="tpu_custom_call" | custom-call | flops 100000 | bytes 1024 | tf_op jit(solution)/shard_map/pallas_call | solution.py:303
  125.5 1.3 collective-permute-done.21.got_a
  126.8 1.9 %collective-permute-done.22.got_b = f32[256,512]{1,0:T(8,128)S(1)} collective-permute-done((f32[256,512]{1,0:T(8,128)S(1)}, f32[256,512]{1,0:T(8,128)S(1)}, u32[]{:S(2)}, u32[]{:S(2)}) %collective-permute-start.22) | collective-permute-done | bytes 524320 | tf_op jit(solution)/shard_map/ppermute | solution.py:398
  128.7 5.3 %shard_map.80 = (f32[256,512]{1,0:T(8,128)S(1)}, f32[256,512]{1,0:T(8,128)S(1)}, f32[256,512]{1,0:T(8,128)S(1)}, f32[256,512]{1,0:T(8,128)S(1)}) custom-call(s32[2]{0:T(128)S(1)} %get-tuple-element.102.cores, f32[256,512]{1,0:T(8,128)S(1)} %collective-permute-done.21.got_a, f32[256,512]{1,0:T(8,128)S(1)} %collective-permute-done.22.got_b, ...), custom_call_target="tpu_custom_call" | custom-call | flops 100000 | bytes 1024 | tf_op jit(solution)/shard_map/pallas_call | solution.py:348
  134.3 0.5 collective-permute-start.26
  134.8 3.4 %shard_map.81 = (f32[256,512]{1,0:T(8,128)S(1)}, f32[256,512]{1,0:T(8,128)S(1)}) custom-call(s32[2]{0:T(128)S(1)} %get-tuple-element.102.cores, f32[256,512]{1,0:T(8,128)S(1)} %collective-permute-done.23.got_a, f32[256,512]{1,0:T(8,128)S(1)} %collective-permute-done.24.got_b, f32[512,2048]{1,0:T(8,128)} %collective-permute-done.19.near, ...), custom_call_target="tpu_custom_call" | custom-call | flops 100000 | bytes 1024 | tf_op jit(solution)/shard_map/pallas_call | solution.py:348
  138.3 0.5 collective-permute-start.28
  138.8 3.4 %shard_map.82 = (f32[256,512]{1,0:T(8,128)S(1)}, f32[256,512]{1,0:T(8,128)S(1)}) custom-call(s32[2]{0:T(128)S(1)} %get-tuple-element.102.cores, f32[256,512]{1,0:T(8,128)S(1)} %collective-permute-done.23.got_a, f32[256,512]{1,0:T(8,128)S(1)} %collective-permute-done.24.got_b, f32[512,2048]{1,0:T(8,128)} %collective-permute-done.19.near, ...), custom_call_target="tpu_custom_call" | custom-call | flops 100000 | bytes 1024 | tf_op jit(solution)/shard_map/pallas_call | solution.py:348
  142.7 1.0 collective-permute-start.31
  143.7 5.4 %shard_map.83.total = f32[2,512,1024]{2,1,0:T(8,128)S(1)} custom-call(s32[4]{0:T(128)S(1)} %get-tuple-element.179.order, f32[2,256,512]{2,1,0:T(8,128)S(1)} %shard_map.76.own_a, f32[2,256,512]{2,1,0:T(8,128)S(1)} %shard_map.77.own_b, f32[512,4096]{1,0:T(8,128)S(1)} %bitcast.17), custom_call_target="tpu_custom_call" | custom-call | flops 100000 | bytes 1024 | tf_op jit(solution)/shard_map/pallas_call | solution.py:303
  149.1 5.3 %shard_map.85 = (f32[256,256]{1,0:T(8,128)S(1)}, f32[256,256]{1,0:T(8,128)S(1)}, f32[256,256]{1,0:T(8,128)S(1)}, f32[256,256]{1,0:T(8,128)S(1)}, f32[256,512]{1,0:T(8,128)S(1)}, /*index=5*/f32[256,512]{1,0:T(8,128)S(1)}) custom-call(s32[2]{0:T(128)S(1)} %get-tuple-element.102.cores, f32[256,512]{1,0:T(8,128)S(1)} %collective-permute-done.23.got_a, ...), custom_call_target="tpu_custom_call" | custom-call | flops 100000 | bytes 1024 | tf_op jit(solution)/shard_map/pallas_call | solution.py:348
  155.0 5.3 %shard_map.84 = (f32[256,256]{1,0:T(8,128)S(1)}, f32[256,256]{1,0:T(8,128)S(1)}, f32[256,256]{1,0:T(8,128)S(1)}, f32[256,256]{1,0:T(8,128)S(1)}, f32[256,512]{1,0:T(8,128)S(1)}, /*index=5*/f32[256,512]{1,0:T(8,128)S(1)}) custom-call(s32[2]{0:T(128)S(1)} %get-tuple-element.102.cores, f32[256,512]{1,0:T(8,128)S(1)} %collective-permute-done.21.got_a, ...), custom_call_target="tpu_custom_call" | custom-call | flops 100000 | bytes 1024 | tf_op jit(solution)/shard_map/pallas_call | solution.py:348
  161.0 0.9 collective-permute-done.29
  162.5 6.9 %collective-permute-done.31 = f32[512,512]{1,0:T(8,128)S(1)} collective-permute-done((f32[512,512]{1,0:T(8,128)S(1)}, f32[512,512]{1,0:T(8,128)S(1)}, u32[]{:S(2)}, u32[]{:S(2)}) %collective-permute-start.31) | collective-permute-done | bytes 1048608 | tf_op jit(solution)/shard_map/ppermute | solution.py:398
  169.7 1.2 collective-permute-done.33
  171.2 1.5 pad_maximum_fusion
  (121 shorter events, 7.9 us)
Async XLA Ops:
  0.0 17.5 %copy-start = (s32[32,3]{0,1:T(4,128)S(1)}, s32[32,3]{0,1:T(4,128)}, u32[]{:S(2)}) copy-start(s32[32,3]{0,1:T(4,128)} %param.11) | copy-start | bytes 1156
  0.0 20.2 %collective-permute-start = (f32[1024,128]{1,0:T(8,128)}, f32[1024,128]{1,0:T(8,128)S(1)}, u32[]{:S(2)}, u32[]{:S(2)}) collective-permute-start(f32[1024,128]{1,0:T(8,128)} %k_own.1), channel_id=1, source_target_pairs={{0,8},{8,16},{16,24},{24,0},{32,40},{40,48},{48,56},{56,32},{64,72... | collective-permute-start | bytes 1572872 | tf_op jit(solution)/shard_map/ppermute | solution.py:390
  1.5 18.7 %collective-permute-start.1 = (f32[1024,128]{1,0:T(8,128)}, f32[1024,128]{1,0:T(8,128)S(1)}, u32[]{:S(2)}, u32[]{:S(2)}) collective-permute-start(f32[1024,128]{1,0:T(8,128)} %k_own.1), channel_id=1, source_target_pairs={{0,24},{8,0},{16,8},{24,16},{32,56},{40,32},{48,40},{56,48},{64,88... | collective-permute-start | bytes 1572872 | tf_op jit(solution)/shard_map/ppermute | solution.py:390
  2.0 18.2 %collective-permute-start.2 = (f32[1024,128]{1,0:T(8,128)}, f32[1024,128]{1,0:T(8,128)S(1)}, u32[]{:S(2)}, u32[]{:S(2)}) collective-permute-start(f32[1024,128]{1,0:T(8,128)} %v_own.1), channel_id=1, source_target_pairs={{0,32},{8,40},{16,48},{24,56},{32,64},{40,72},{48,80},{56,88},{64,... | collective-permute-start | bytes 1572872 | tf_op jit(solution)/shard_map/ppermute | solution.py:390
  4.5 12.7 %copy-start.5 = (s32[32,8]{0,1:T(8,128)S(1)}, s32[32,8]{0,1:T(8,128)}, u32[]{:S(2)}) copy-start(s32[32,8]{0,1:T(8,128)} %param.10) | copy-start | bytes 3076
  4.5 16.5 %copy-start.2 = (f32[1024,128]{1,0:T(8,128)S(1)}, f32[1024,128]{1,0:T(8,128)}, u32[]{:S(2)}) copy-start(f32[1024,128]{1,0:T(8,128)} %v_own.1) | copy-start | bytes 1572868
  13.4 104.2 %collective-permute-start.19 = (f32[512,2048]{1,0:T(8,128)}, f32[512,2048]{1,0:T(8,128)}, u32[]{:S(2)}, u32[]{:S(2)}) collective-permute-start(f32[512,2048]{1,0:T(8,128)} %get-tuple-element.143), channel_id=1, source_target_pairs={{0,2},{1,3},{2,0},{3,1},{4,6},{5,7},{6,4},{7,5},{8,10},{9,11},{10,... | collective-permute-start | bytes 12582920 | tf_op jit(solution)/shard_map/ppermute | solution.py:398
  15.0 105.1 %collective-permute-start.20 = (f32[512,2048]{1,0:T(8,128)}, f32[512,2048]{1,0:T(8,128)}, u32[]{:S(2)}, u32[]{:S(2)}) collective-permute-start(f32[512,2048]{1,0:T(8,128)} %get-tuple-element.144), channel_id=1, source_target_pairs={{0,6},{1,7},{2,4},{3,5},{4,2},{5,3},{6,0},{7,1},{8,14},{9,15},{10,... | collective-permute-start | bytes 12582920 | tf_op jit(solution)/shard_map/ppermute | solution.py:398
  20.3 4.7 %collective-permute-start.7 = (f32[1024,128]{1,0:T(8,128)S(1)}, f32[1024,128]{1,0:T(8,128)S(1)}, u32[]{:S(2)}, u32[]{:S(2)}) collective-permute-start(f32[1024,128]{1,0:T(8,128)S(1)} %collective-permute-done.refs_3_.k_left), channel_id=1, source_target_pairs={{0,32},{32,64},{64,96},{1,33},{33,65},{65,97},{2,34},{34,66},{66,9... | collective-permute-start | bytes 1572872 | tf_op jit(solution)/shard_map/ppermute | solution.py:390
  21.1 14.5 %collective-permute-start.4 = (f32[1024,128]{1,0:T(8,128)S(1)}, f32[1024,128]{1,0:T(8,128)S(1)}, u32[]{:S(2)}, u32[]{:S(2)}) collective-permute-start(f32[1024,128]{1,0:T(8,128)S(1)} %copy-done.2), channel_id=1, source_target_pairs={{0,96},{8,104},{16,112},{24,120},{32,0},{40,8},{48,16},{56,24},{64... | collective-permute-start | bytes 1572872 | tf_op jit(solution)/shard_map/ppermute | solution.py:390
  23.3 27.0 %copy-start.3 = (f32[1024,128]{1,0:T(8,128)S(1)}, f32[1024,128]{1,0:T(8,128)}, u32[]{:S(2)}) copy-start(f32[1024,128]{1,0:T(8,128)} %k_own.1) | copy-start | bytes 1572868
  23.3 18.7 %collective-permute-start.6 = (f32[1536,128]{1,0:T(8,128)S(1)}, f32[1536,128]{1,0:T(8,128)S(1)}, u32[]{:S(2)}, u32[]{:S(2)}) collective-permute-start(f32[1536,128]{1,0:T(8,128)S(1)} %pad_maximum_fusion.4), channel_id=1, source_target_pairs={{0,8},{8,16},{16,24},{24,0},{32,40},{40,48},{48,56},{56,32},{64,72... | collective-permute-start | bytes 2359304 | tf_op jit(solution)/shard_map/ppermute | solution.py:390
  25.0 25.1 %collective-permute-start.3 = (f32[1536,128]{1,0:T(8,128)S(1)}, f32[1536,128]{1,0:T(8,128)S(1)}, u32[]{:S(2)}, u32[]{:S(2)}) collective-permute-start(f32[1536,128]{1,0:T(8,128)S(1)} %pad_maximum_fusion.3), channel_id=1, source_target_pairs={{0,24},{8,0},{16,8},{24,16},{32,56},{40,32},{48,40},{56,48},{64,88... | collective-permute-start | bytes 2359304 | tf_op jit(solution)/shard_map/ppermute | solution.py:390
  35.6 14.5 %collective-permute-start.5 = (f32[1024,128]{1,0:T(8,128)S(1)}, f32[1024,128]{1,0:T(8,128)S(1)}, u32[]{:S(2)}, u32[]{:S(2)}) collective-permute-start(f32[1024,128]{1,0:T(8,128)S(1)} %collective-permute-done.4.refs_5_), channel_id=1, source_target_pairs={{0,96},{8,104},{16,112},{24,120},{32,0},{40,8},{48,16},{56,24},{64... | collective-permute-start | bytes 1572872 | tf_op jit(solution)/shard_map/ppermute | solution.py:390
  50.1 21.1 %copy-start.4 = (f32[1024,512]{1,0:T(8,128)S(1)}, f32[1024,512]{1,0:T(8,128)}, u32[]{:S(2)}) copy-start(f32[1024,512]{1,0:T(8,128)} %q.1) | copy-start | bytes 6291460
  50.2 6.9 %collective-permute-start.8 = (f32[512,128]{1,0:T(8,128)S(1)}, f32[512,128]{1,0:T(8,128)S(1)}, u32[]{:S(2)}, u32[]{:S(2)}) collective-permute-start(f32[512,128]{1,0:T(8,128)S(1)} %slice.44), channel_id=1, source_target_pairs={{0,8},{8,16},{16,24},{24,0},{32,40},{40,48},{48,56},{56,32},{64,72... | collective-permute-start | bytes 786440 | tf_op jit(solution)/shard_map/ppermute | solution.py:390
  52.1 16.6 %collective-permute-start.11 = (f32[1024,128]{1,0:T(8,128)S(1)}, f32[1024,128]{1,0:T(8,128)S(1)}, u32[]{:S(2)}, u32[]{:S(2)}) collective-permute-start(f32[1024,128]{1,0:T(8,128)S(1)} %get-tuple-element.115), channel_id=1, source_target_pairs={{0,32},{8,40},{16,48},{24,56},{32,0},{40,8},{48,16},{56,24},{64,96... | collective-permute-start | bytes 1572872 | tf_op jit(solution)/shard_map/ppermute | solution.py:390
  54.8 16.5 %collective-permute-start.12 = (f32[1024,128]{1,0:T(8,128)S(1)}, f32[1024,128]{1,0:T(8,128)S(1)}, u32[]{:S(2)}, u32[]{:S(2)}) collective-permute-start(f32[1024,128]{1,0:T(8,128)S(1)} %get-tuple-element.116), channel_id=1, source_target_pairs={{0,96},{8,104},{16,112},{24,120},{32,64},{40,72},{48,80},{56,88},{... | collective-permute-start | bytes 1572872 | tf_op jit(solution)/shard_map/ppermute | solution.py:390
  57.1 7.7 %collective-permute-start.9 = (f32[512,128]{1,0:T(8,128)S(1)}, f32[512,128]{1,0:T(8,128)S(1)}, u32[]{:S(2)}, u32[]{:S(2)}) collective-permute-start(f32[512,128]{1,0:T(8,128)S(1)} %slice.45), channel_id=1, source_target_pairs={{0,24},{8,0},{16,8},{24,16},{32,56},{40,32},{48,40},{56,48},{64,88... | collective-permute-start | bytes 786440 | tf_op jit(solution)/shard_map/ppermute | solution.py:390
  64.8 17.4 %collective-permute-start.10 = (f32[1024,128]{1,0:T(8,128)S(1)}, f32[1024,128]{1,0:T(8,128)S(1)}, u32[]{:S(2)}, u32[]{:S(2)}) collective-permute-start(f32[1024,128]{1,0:T(8,128)S(1)} %slice.46.refs_2_.k_far), channel_id=1, source_target_pairs={{0,32},{8,40},{32,64},{40,72},{64,96},{72,104},{1,33},{9,41},{33,6... | collective-permute-start | bytes 1572872 | tf_op jit(solution)/shard_map/ppermute | solution.py:390
  68.7 10.9 %collective-permute-start.13 = (f32[1024,128]{1,0:T(8,128)S(1)}, f32[1024,128]{1,0:T(8,128)S(1)}, u32[]{:S(2)}, u32[]{:S(2)}) collective-permute-start(f32[1024,128]{1,0:T(8,128)S(1)} %get-tuple-element.117), channel_id=1, source_target_pairs={{0,8},{8,0},{16,24},{24,16},{32,40},{40,32},{48,56},{56,48},{64,72... | collective-permute-start | bytes 1572872 | tf_op jit(solution)/shard_map/ppermute | solution.py:390
  71.3 10.9 %collective-permute-start.14 = (f32[1024,128]{1,0:T(8,128)S(1)}, f32[1024,128]{1,0:T(8,128)S(1)}, u32[]{:S(2)}, u32[]{:S(2)}) collective-permute-start(f32[1024,128]{1,0:T(8,128)S(1)} %get-tuple-element.118), channel_id=1, source_target_pairs={{0,24},{8,16},{16,8},{24,0},{32,56},{40,48},{48,40},{56,32},{64,88... | collective-permute-start | bytes 1572872 | tf_op jit(solution)/shard_map/ppermute | solution.py:390
  82.3 9.3 %collective-permute-start.18 = (f32[1024,128]{1,0:T(8,128)S(1)}, f32[1024,128]{1,0:T(8,128)S(1)}, u32[]{:S(2)}, u32[]{:S(2)}) collective-permute-start(f32[1024,128]{1,0:T(8,128)S(1)} %add.222), channel_id=1, source_target_pairs={{0,8},{8,0},{16,24},{24,16},{32,40},{40,32},{48,56},{56,48},{64,72... | collective-permute-start | bytes 1572872 | tf_op jit(solution)/shard_map/ppermute | solution.py:390
  83.4 18.1 %collective-permute-start.17 = (f32[1024,128]{1,0:T(8,128)S(1)}, f32[1024,128]{1,0:T(8,128)S(1)}, u32[]{:S(2)}, u32[]{:S(2)}) collective-permute-start(f32[1024,128]{1,0:T(8,128)S(1)} %add.221), channel_id=1, source_target_pairs={{0,24},{8,16},{16,8},{24,0},{32,56},{40,48},{48,40},{56,32},{64,88... | collective-permute-start | bytes 1572872 | tf_op jit(solution)/shard_map/ppermute | solution.py:390
  83.5 18.0 %collective-permute-start.16 = (f32[1024,128]{1,0:T(8,128)S(1)}, f32[1024,128]{1,0:T(8,128)S(1)}, u32[]{:S(2)}, u32[]{:S(2)}) collective-permute-start(f32[1024,128]{1,0:T(8,128)S(1)} %add.220), channel_id=1, source_target_pairs={{0,32},{8,40},{16,48},{24,56},{32,0},{40,8},{48,16},{56,24},{64,96... | collective-permute-start | bytes 1572872 | tf_op jit(solution)/shard_map/ppermute | solution.py:390
  91.5 10.4 %collective-permute-start.15 = (f32[1024,128]{1,0:T(8,128)S(1)}, f32[1024,128]{1,0:T(8,128)S(1)}, u32[]{:S(2)}, u32[]{:S(2)}) collective-permute-start(f32[1024,128]{1,0:T(8,128)S(1)} %add.219), channel_id=1, source_target_pairs={{0,96},{8,104},{16,112},{24,120},{32,64},{40,72},{48,80},{56,88},{... | collective-permute-start | bytes 1572872 | tf_op jit(solution)/shard_map/ppermute | solution.py:390
  102.2 17.9 %slice-start = ((s8[8388608]{0:T(1024)(128)(4,1)}), s8[4194304]{0:T(1024)(128)(4,1)S(1)}, s32[]{:S(2)}) async-start(s8[8388608]{0:T(1024)(128)(4,1)} %bitcast.16), calls=%async_computation | async-start | bytes 8388608
  108.5 11.6 %slice-start.1 = ((s8[8388608]{0:T(1024)(128)(4,1)}), s8[4194304]{0:T(1024)(128)(4,1)S(1)}, s32[]{:S(2)}) async-start(s8[8388608]{0:T(1024)(128)(4,1)} %bitcast.16), calls=%async_computation.1 | async-start | bytes 8388608
  114.9 11.9 %collective-permute-start.21 = (f32[256,512]{1,0:T(8,128)S(1)}, f32[256,512]{1,0:T(8,128)S(1)}, u32[]{:S(2)}, u32[]{:S(2)}) collective-permute-start(f32[256,512]{1,0:T(8,128)S(1)} %get-tuple-element.214), channel_id=1, source_target_pairs={{0,2},{1,3},{2,0},{3,1},{4,6},{5,7},{6,4},{7,5},{8,10},{9,11},{10,... | collective-permute-start | bytes 1572872 | tf_op jit(solution)/shard_map/ppermute | solution.py:398
  116.6 12.1 %collective-permute-start.22 = (f32[256,512]{1,0:T(8,128)S(1)}, f32[256,512]{1,0:T(8,128)S(1)}, u32[]{:S(2)}, u32[]{:S(2)}) collective-permute-start(f32[256,512]{1,0:T(8,128)S(1)} %get-tuple-element.213), channel_id=1, source_target_pairs={{0,6},{1,7},{2,4},{3,5},{4,2},{5,3},{6,0},{7,1},{8,14},{9,15},{10,... | collective-permute-start | bytes 1572872 | tf_op jit(solution)/shard_map/ppermute | solution.py:398
  117.4 16.6 %collective-permute-start.23 = (f32[256,512]{1,0:T(8,128)S(1)}, f32[256,512]{1,0:T(8,128)S(1)}, u32[]{:S(2)}, u32[]{:S(2)}) collective-permute-start(f32[256,512]{1,0:T(8,128)S(1)} %get-tuple-element.212), channel_id=1, source_target_pairs={{0,2},{1,3},{2,0},{3,1},{4,6},{5,7},{6,4},{7,5},{8,10},{9,11},{10,... | collective-permute-start | bytes 1572872 | tf_op jit(solution)/shard_map/ppermute | solution.py:398
  117.6 16.7 %collective-permute-start.24 = (f32[256,512]{1,0:T(8,128)S(1)}, f32[256,512]{1,0:T(8,128)S(1)}, u32[]{:S(2)}, u32[]{:S(2)}) collective-permute-start(f32[256,512]{1,0:T(8,128)S(1)} %get-tuple-element.211), channel_id=1, source_target_pairs={{0,6},{1,7},{2,4},{3,5},{4,2},{5,3},{6,0},{7,1},{8,14},{9,15},{10,... | collective-permute-start | bytes 1572872 | tf_op jit(solution)/shard_map/ppermute | solution.py:398
  134.3 3.9 %collective-permute-start.25 = (f32[256,512]{1,0:T(8,128)S(1)}, f32[256,512]{1,0:T(8,128)S(1)}, u32[]{:S(2)}, u32[]{:S(2)}) collective-permute-start(f32[256,512]{1,0:T(8,128)S(1)} %get-tuple-element.160), channel_id=1, source_target_pairs={{0,1},{1,0},{2,3},{3,2},{4,5},{5,4},{6,7},{7,6},{8,9},{9,8},{10,11... | collective-permute-start | bytes 1572872 | tf_op jit(solution)/shard_map/ppermute | solution.py:398
  134.3 3.9 %collective-permute-start.26 = (f32[256,512]{1,0:T(8,128)S(1)}, f32[256,512]{1,0:T(8,128)S(1)}, u32[]{:S(2)}, u32[]{:S(2)}) collective-permute-start(f32[256,512]{1,0:T(8,128)S(1)} %get-tuple-element.161), channel_id=1, source_target_pairs={{0,1},{1,0},{2,3},{3,2},{4,5},{5,4},{6,7},{7,6},{8,9},{9,8},{10,11... | collective-permute-start | bytes 1572872 | tf_op jit(solution)/shard_map/ppermute | solution.py:398
  138.2 4.1 %collective-permute-start.27 = (f32[256,512]{1,0:T(8,128)S(1)}, f32[256,512]{1,0:T(8,128)S(1)}, u32[]{:S(2)}, u32[]{:S(2)}) collective-permute-start(f32[256,512]{1,0:T(8,128)S(1)} %get-tuple-element.167), channel_id=1, source_target_pairs={{0,1},{1,0},{2,3},{3,2},{4,5},{5,4},{6,7},{7,6},{8,9},{9,8},{10,11... | collective-permute-start | bytes 1572872 | tf_op jit(solution)/shard_map/ppermute | solution.py:398
  138.3 4.0 %collective-permute-start.28 = (f32[256,512]{1,0:T(8,128)S(1)}, f32[256,512]{1,0:T(8,128)S(1)}, u32[]{:S(2)}, u32[]{:S(2)}) collective-permute-start(f32[256,512]{1,0:T(8,128)S(1)} %get-tuple-element.168), channel_id=1, source_target_pairs={{0,1},{1,0},{2,3},{3,2},{4,5},{5,4},{6,7},{7,6},{8,9},{9,8},{10,11... | collective-permute-start | bytes 1572872 | tf_op jit(solution)/shard_map/ppermute | solution.py:398
  142.7 26.7 %collective-permute-start.31 = (f32[512,512]{1,0:T(8,128)S(1)}, f32[512,512]{1,0:T(8,128)S(1)}, u32[]{:S(2)}, u32[]{:S(2)}) collective-permute-start(f32[512,512]{1,0:T(8,128)S(1)} %pad_maximum_fusion.1), channel_id=1, source_target_pairs={{0,6},{1,7},{2,4},{3,5},{4,2},{5,3},{6,0},{7,1},{8,14},{9,15},{10,... | collective-permute-start | bytes 3145736 | tf_op jit(solution)/shard_map/ppermute | solution.py:398
  143.7 27.2 %collective-permute-start.34 = (f32[512,512]{1,0:T(8,128)S(1)}, f32[512,512]{1,0:T(8,128)S(1)}, u32[]{:S(2)}, u32[]{:S(2)}) collective-permute-start(f32[512,512]{1,0:T(8,128)S(1)} %pad_maximum_fusion.2), channel_id=1, source_target_pairs={{0,2},{1,3},{2,0},{3,1},{4,6},{5,7},{6,4},{7,5},{8,10},{9,11},{10,... | collective-permute-start | bytes 3145736 | tf_op jit(solution)/shard_map/ppermute | solution.py:398
  154.4 6.1 %collective-permute-start.35 = (f32[256,256]{1,0:T(8,128)S(1)}, f32[256,256]{1,0:T(8,128)S(1)}, u32[]{:S(2)}, u32[]{:S(2)}) collective-permute-start(f32[256,256]{1,0:T(8,128)S(1)} %get-tuple-element.192), channel_id=1, source_target_pairs={{0,1},{1,0},{2,3},{3,2},{4,5},{5,4},{6,7},{7,6},{8,9},{9,8},{10,11... | collective-permute-start | bytes 786440 | tf_op jit(solution)/shard_map/ppermute | solution.py:398
  154.5 6.4 %collective-permute-start.36 = (f32[256,256]{1,0:T(8,128)S(1)}, f32[256,256]{1,0:T(8,128)S(1)}, u32[]{:S(2)}, u32[]{:S(2)}) collective-permute-start(f32[256,256]{1,0:T(8,128)S(1)} %get-tuple-element.193), channel_id=1, source_target_pairs={{0,1},{1,0},{2,3},{3,2},{4,5},{5,4},{6,7},{7,6},{8,9},{9,8},{10,11... | collective-permute-start | bytes 786440 | tf_op jit(solution)/shard_map/ppermute | solution.py:398
  160.3 1.6 collective-permute-start.29
  160.5 1.8 %collective-permute-start.30 = (f32[256,256]{1,0:T(8,128)S(1)}, f32[256,256]{1,0:T(8,128)S(1)}, u32[]{:S(2)}, u32[]{:S(2)}) collective-permute-start(f32[256,256]{1,0:T(8,128)S(1)} %get-tuple-element.183), channel_id=1, source_target_pairs={{0,1},{1,0},{2,3},{3,2},{4,5},{5,4},{6,7},{7,6},{8,9},{9,8},{10,11... | collective-permute-start | bytes 786440 | tf_op jit(solution)/shard_map/ppermute | solution.py:398
  160.9 8.7 %collective-permute-start.37 = (f32[256,256]{1,0:T(8,128)S(1)}, f32[256,256]{1,0:T(8,128)S(1)}, u32[]{:S(2)}, u32[]{:S(2)}) collective-permute-start(f32[256,256]{1,0:T(8,128)S(1)} %get-tuple-element.195), channel_id=1, source_target_pairs={{0,1},{1,0},{2,3},{3,2},{4,5},{5,4},{6,7},{7,6},{8,9},{9,8},{10,11... | collective-permute-start | bytes 786440 | tf_op jit(solution)/shard_map/ppermute | solution.py:398
  161.9 7.7 %collective-permute-start.38 = (f32[256,256]{1,0:T(8,128)S(1)}, f32[256,256]{1,0:T(8,128)S(1)}, u32[]{:S(2)}, u32[]{:S(2)}) collective-permute-start(f32[256,256]{1,0:T(8,128)S(1)} %get-tuple-element.196), channel_id=1, source_target_pairs={{0,1},{1,0},{2,3},{3,2},{4,5},{5,4},{6,7},{7,6},{8,9},{9,8},{10,11... | collective-permute-start | bytes 786440 | tf_op jit(solution)/shard_map/ppermute | solution.py:398
  162.3 7.4 %collective-permute-start.32 = (f32[256,256]{1,0:T(8,128)S(1)}, f32[256,256]{1,0:T(8,128)S(1)}, u32[]{:S(2)}, u32[]{:S(2)}) collective-permute-start(f32[256,256]{1,0:T(8,128)S(1)} %get-tuple-element.186), channel_id=1, source_target_pairs={{0,1},{1,0},{2,3},{3,2},{4,5},{5,4},{6,7},{7,6},{8,9},{9,8},{10,11... | collective-permute-start | bytes 786440 | tf_op jit(solution)/shard_map/ppermute | solution.py:398
  169.4 1.5 collective-permute-start.33
  171.2 1.5 copy-start.1

commit v15 on v11

--- a/solution.py
+++ b/solution.py
@@ -259,7 +259,7 @@
 
 def take_columns(weight, chips, width):
     rows = weight.shape[0]
-    step = rows // 8
+    step = rows // 4
     out = jax.ShapeDtypeStruct((rows, 2 * width), jnp.float32)
     out_spec = pl.BlockSpec((step, 2 * width), lambda i, o: (i, 0))
     w_spec = lambda at: pl.BlockSpec((step, width), lambda i, o: (i, o[at]))

time: 173 us -> 172 us (level)
  transfers between devices with their start and end apart: 39 -> 39, of which waited for: 16 -> 16; matrix products, arithmetic and copies ran while one was open for 2% -> 2% of each run, Pallas kernels for 38% -> 37%
where the time goes in v15:
time: 172 us; the launch traced here: 171 us
  Pallas kernels  63.7 us (37%)
  waiting for transfers between devices  53.4 us (31%)
  starting transfers between devices  46.3 us (27%)
  other arithmetic  4.64 us (3%)
  local copies, waits for them, and re-layouts  1.8 us (1%)
    ppermute x19, waiting for transfers between devices, body(): send = lambda a, pairs: lax.ppermute(a, 'seq', pairs)  40.9 us
    ppermute x19, starting transfers between devices, body(): send = lambda a, pairs: lax.ppermute(a, 'seq', pairs)  32.4 us
    pallas_call x4, Pallas kernels, project_pair(): pl.pallas_call(pair_kernel, out_shape=[there] * pieces + [here], grid_spe...  21.3 us
    ppermute x20, starting transfers between devices, body(): lax.ppermute(a, 'head', [(i, i ^ bits) for i in range(head_size)])  13.9 us
    pallas_call x2, Pallas kernels, attend(): pl.pallas_call(functools.partial(attend_kernel, start), grid=(2, heads //...  12.6 us
    ppermute x20, waiting for transfers between devices, body(): lax.ppermute(a, 'head', [(i, i ^ bits) for i in range(head_size)])  12.4 us
    pallas_call x2, Pallas kernels, project_chip(): pl.pallas_call(chip_kernel, out_shape=jax.ShapeDtypeStruct((2, 2 * rows,...  10.8 us
    pallas_call x1, Pallas kernels, attend_near(): pl.pallas_call(functools.partial(near_kernel, start), grid=(rows // TILE,...  9.64 us
  transfers between devices with their start and end apart: 39, of which 16 were waited for; matrix products, arithmetic and copies ran while one was open for 2% of the time, Pallas kernels for 37%

profile of v15, /device:TPU:2, one launch (start us, length us, event | category | flops | bytes accessed | tf_op | source)
XLA Modules:
  0.0 170.9 jit_solution(9159404151323083304)
XLA Ops:
  0.5 1.6 collective-permute-start
  2.0 1.9 %collective-permute-start.2 = (f32[1024,128]{1,0:T(8,128)}, f32[1024,128]{1,0:T(8,128)S(1)}, u32[]{:S(2)}, u32[]{:S(2)}) collective-permute-start(f32[1024,128]{1,0:T(8,128)} %v_own.1), channel_id=1, source_target_pairs={{0,32},{8,40},{16,48},{24,56},{32,64},{40,72},{48,80},{56,88},{64,... | collective-permute-start | bytes 1572872 | tf_op jit(solution)/shard_map/ppermute | solution.py:392
  3.9 0.5 add_xor_fusion.chips
  4.5 7.3 %shard_map.78 = (f32[512,2048]{1,0:T(8,128)}, f32[512,2048]{1,0:T(8,128)}) custom-call(s32[3]{0:T(128)} %add_xor_fusion.chips, f32[512,4096]{1,0:T(8,128)} %w.3, f32[512,4096]{1,0:T(8,128)} %w.3, f32[512,4096]{1,0:T(8,128)} %w.3), custom_call_target="tpu_custom_call" | custom-call | flops 1024 | bytes 1024 | tf_op jit(solution)/shard_map/pallas_call | solution.py:266
  11.8 1.6 collective-permute-start.19
  13.3 2.2 %collective-permute-start.20 = (f32[512,2048]{1,0:T(8,128)}, f32[512,2048]{1,0:T(8,128)}, u32[]{:S(2)}, u32[]{:S(2)}) collective-permute-start(f32[512,2048]{1,0:T(8,128)} %get-tuple-element.134), channel_id=1, source_target_pairs={{0,6},{1,7},{2,4},{3,5},{4,2},{5,3},{6,0},{7,1},{8,14},{9,15},{10,... | collective-permute-start | bytes 12582920 | tf_op jit(solution)/shard_map/ppermute | solution.py:400
  18.6 2.2 %collective-permute-start.4 = (f32[1024,128]{1,0:T(8,128)S(1)}, f32[1024,128]{1,0:T(8,128)S(1)}, u32[]{:S(2)}, u32[]{:S(2)}) collective-permute-start(f32[1024,128]{1,0:T(8,128)S(1)} %copy-done.2), channel_id=1, source_target_pairs={{0,96},{8,104},{16,112},{24,120},{32,0},{40,8},{48,16},{56,24},{64... | collective-permute-start | bytes 1572872 | tf_op jit(solution)/shard_map/ppermute | solution.py:392
  20.8 0.7 collective-permute-start.7
  21.7 2.5 %collective-permute-start.3 = (f32[1536,128]{1,0:T(8,128)S(1)}, f32[1536,128]{1,0:T(8,128)S(1)}, u32[]{:S(2)}, u32[]{:S(2)}) collective-permute-start(f32[1536,128]{1,0:T(8,128)S(1)} %pad_maximum_fusion.3), channel_id=1, source_target_pairs={{0,24},{8,0},{16,8},{24,16},{32,56},{40,32},{48,40},{56,48},{64,88... | collective-permute-start | bytes 2359304 | tf_op jit(solution)/shard_map/ppermute | solution.py:392
  24.2 6.9 %collective-permute-done.4.refs_5_ = f32[1024,128]{1,0:T(8,128)S(1)} collective-permute-done((f32[1024,128]{1,0:T(8,128)S(1)}, f32[1024,128]{1,0:T(8,128)S(1)}, u32[]{:S(2)}, u32[]{:S(2)}) %collective-permute-start.4) | collective-permute-done | bytes 524320 | tf_op jit(solution)/shard_map/ppermute | solution.py:392
  31.1 1.5 collective-permute-start.6
  32.6 3.4 %collective-permute-start.5 = (f32[1024,128]{1,0:T(8,128)S(1)}, f32[1024,128]{1,0:T(8,128)S(1)}, u32[]{:S(2)}, u32[]{:S(2)}) collective-permute-start(f32[1024,128]{1,0:T(8,128)S(1)} %collective-permute-done.4.refs_5_), channel_id=1, source_target_pairs={{0,96},{8,104},{16,112},{24,120},{32,0},{40,8},{48,16},{56,24},{64... | collective-permute-start | bytes 1572872 | tf_op jit(solution)/shard_map/ppermute | solution.py:392
  36.0 3.6 %collective-permute-done.3 = f32[1536,128]{1,0:T(8,128)S(1)} collective-permute-done((f32[1536,128]{1,0:T(8,128)S(1)}, f32[1536,128]{1,0:T(8,128)S(1)}, u32[]{:S(2)}, u32[]{:S(2)}) %collective-permute-start.3) | collective-permute-done | bytes 786464 | tf_op jit(solution)/shard_map/ppermute | solution.py:392
  39.6 8.8 %collective-permute-done.6 = f32[1536,128]{1,0:T(8,128)S(1)} collective-permute-done((f32[1536,128]{1,0:T(8,128)S(1)}, f32[1536,128]{1,0:T(8,128)S(1)}, u32[]{:S(2)}, u32[]{:S(2)}) %collective-permute-start.6) | collective-permute-done | bytes 786464 | tf_op jit(solution)/shard_map/ppermute | solution.py:392
  48.5 3.0 %collective-permute-start.9 = (f32[512,128]{1,0:T(8,128)S(1)}, f32[512,128]{1,0:T(8,128)S(1)}, u32[]{:S(2)}, u32[]{:S(2)}) collective-permute-start(f32[512,128]{1,0:T(8,128)S(1)} %slice.69), channel_id=1, source_target_pairs={{0,24},{8,0},{16,8},{24,16},{32,56},{40,32},{48,40},{56,48},{64,88... | collective-permute-start | bytes 786440 | tf_op jit(solution)/shard_map/ppermute | solution.py:392
  51.5 1.8 %shard_map.74 = (f32[1024,128]{1,0:T(8,128)S(1)}, f32[1024,128]{1,0:T(8,128)S(1)}, f32[1024,128]{1,0:T(8,128)S(1)}, f32[1024,128]{1,0:T(8,128)S(1)}) custom-call(s32[32]{0:T(128)S(1)} %get-tuple-element.100.k_place, s32[32]{0:T(128)S(1)} %compare_convert_fusion.1.k_held, s32[32]{0:T(128)S(1)} %get-tuple-element.102.v_place, ...), custom_call_target="tpu_custom_call" | custom-call | flops 1024 | bytes 1024 | tf_op jit(solution)/shard_map/pallas_call | solution.py:48
  53.4 1.6 collective-permute-start.11
  55.0 2.2 %collective-permute-start.12 = (f32[1024,128]{1,0:T(8,128)S(1)}, f32[1024,128]{1,0:T(8,128)S(1)}, u32[]{:S(2)}, u32[]{:S(2)}) collective-permute-start(f32[1024,128]{1,0:T(8,128)S(1)} %get-tuple-element.106), channel_id=1, source_target_pairs={{0,96},{8,104},{16,112},{24,120},{32,64},{40,72},{48,80},{56,88},{... | collective-permute-start | bytes 1572872 | tf_op jit(solution)/shard_map/ppermute | solution.py:392
  57.4 6.4 %collective-permute-done.8.v_far_a = f32[512,128]{1,0:T(8,128)S(1)} collective-permute-done((f32[512,128]{1,0:T(8,128)S(1)}, f32[512,128]{1,0:T(8,128)S(1)}, u32[]{:S(2)}, u32[]{:S(2)}) %collective-permute-start.8) | collective-permute-done | bytes 262176 | tf_op jit(solution)/shard_map/ppermute | solution.py:392
  63.7 3.0 %collective-permute-start.10 = (f32[1024,128]{1,0:T(8,128)S(1)}, f32[1024,128]{1,0:T(8,128)S(1)}, u32[]{:S(2)}, u32[]{:S(2)}) collective-permute-start(f32[1024,128]{1,0:T(8,128)S(1)} %slice.70.refs_2_.k_far), channel_id=1, source_target_pairs={{0,32},{8,40},{32,64},{40,72},{64,96},{72,104},{1,33},{9,41},{33,6... | collective-permute-start | bytes 1572872 | tf_op jit(solution)/shard_map/ppermute | solution.py:392
  66.7 2.9 %collective-permute-start.13 = (f32[1024,128]{1,0:T(8,128)S(1)}, f32[1024,128]{1,0:T(8,128)S(1)}, u32[]{:S(2)}, u32[]{:S(2)}) collective-permute-start(f32[1024,128]{1,0:T(8,128)S(1)} %get-tuple-element.107), channel_id=1, source_target_pairs={{0,8},{8,0},{16,24},{24,16},{32,40},{40,32},{48,56},{56,48},{64,72... | collective-permute-start | bytes 1572872 | tf_op jit(solution)/shard_map/ppermute | solution.py:392
  69.9 7.0 %collective-permute-done.13 = f32[1024,128]{1,0:T(8,128)S(1)} collective-permute-done((f32[1024,128]{1,0:T(8,128)S(1)}, f32[1024,128]{1,0:T(8,128)S(1)}, u32[]{:S(2)}, u32[]{:S(2)}) %collective-permute-start.13) | collective-permute-done | bytes 524320 | tf_op jit(solution)/shard_map/ppermute | solution.py:392
  76.9 1.9 %collective-permute-done.14 = f32[1024,128]{1,0:T(8,128)S(1)} collective-permute-done((f32[1024,128]{1,0:T(8,128)S(1)}, f32[1024,128]{1,0:T(8,128)S(1)}, u32[]{:S(2)}, u32[]{:S(2)}) %collective-permute-start.14) | collective-permute-done | bytes 524320 | tf_op jit(solution)/shard_map/ppermute | solution.py:392
  78.9 0.9 collective-permute-start.15
  80.0 3.0 %collective-permute-start.16 = (f32[1024,128]{1,0:T(8,128)S(1)}, f32[1024,128]{1,0:T(8,128)S(1)}, u32[]{:S(2)}, u32[]{:S(2)}) collective-permute-start(f32[1024,128]{1,0:T(8,128)S(1)} %add.220), channel_id=1, source_target_pairs={{0,32},{8,40},{16,48},{24,56},{32,0},{40,8},{48,16},{56,24},{64,96... | collective-permute-start | bytes 1572872 | tf_op jit(solution)/shard_map/ppermute | solution.py:392
  83.0 6.3 %collective-permute-done.15 = f32[1024,128]{1,0:T(8,128)S(1)} collective-permute-done((f32[1024,128]{1,0:T(8,128)S(1)}, f32[1024,128]{1,0:T(8,128)S(1)}, u32[]{:S(2)}, u32[]{:S(2)}) %collective-permute-start.15) | collective-permute-done | bytes 524320 | tf_op jit(solution)/shard_map/ppermute | solution.py:392
  89.4 1.3 collective-permute-start.18
  90.7 9.6 %shard_map.75 = (f32[1024,512]{1,0:T(8,128)S(1)}, f32[1024,256]{1,0:T(8,128)S(1)}) custom-call(s32[1]{0:T(128)} %bitcast.1.first_row, s32[4,4]{1,0:T(4,128)S(1)} %get-tuple-element.111.back, s32[2]{0:T(128)S(1)} %add_convert_fusion.wraps, f32[1024,512]{1,0:T(8,128)S(1)} %shard_map.73.q, f32[1024,128]{1,0:T(8,128)S(1)} %slice.70.refs_2_.k_far, ...), custom_call_target="tpu_custom_call" | custom-call | flops 100000 | bytes 1024 | tf_op jit(solution)/shard_map/pallas_call | solution.py:179
  100.6 6.3 %shard_map.76.own_a = f32[2,256,512]{2,1,0:T(8,128)S(1)} custom-call(s32[1]{0:T(128)} %bitcast.1.first_row, f32[1024,512]{1,0:T(8,128)S(1)} %shard_map.73.q, f32[1024,512]{1,0:T(8,128)S(1)} %get-tuple-element.124.near, f32[1024,256]{1,0:T(8,128)S(1)} %get-tuple-element.125.stats, f32[1024,128]{1,0:T(8,128)S(1)} %add.223.k_a, f32[1024,128]{1,0:T(8,128)S(1)} %add.224.k_b, ...), custom_call_target="tpu_custom_call" | custom-call | flops 100000 | bytes 1024 | tf_op jit(solution)/shard_map/pallas_call | solution.py:236
  106.9 6.3 %shard_map.77.own_b = f32[2,256,512]{2,1,0:T(8,128)S(1)} custom-call(s32[1]{0:T(128)} %bitcast.1.first_row, f32[1024,512]{1,0:T(8,128)S(1)} %shard_map.73.q, f32[1024,512]{1,0:T(8,128)S(1)} %get-tuple-element.124.near, f32[1024,256]{1,0:T(8,128)S(1)} %get-tuple-element.125.stats, f32[1024,128]{1,0:T(8,128)S(1)} %add.223.k_a, f32[1024,128]{1,0:T(8,128)S(1)} %add.224.k_b, ...), custom_call_target="tpu_custom_call" | custom-call | flops 100000 | bytes 1024 | tf_op jit(solution)/shard_map/pallas_call | solution.py:236
  113.3 1.7 %collective-permute-start.22 = (f32[256,512]{1,0:T(8,128)S(1)}, f32[256,512]{1,0:T(8,128)S(1)}, u32[]{:S(2)}, u32[]{:S(2)}) collective-permute-start(f32[256,512]{1,0:T(8,128)S(1)} %get-tuple-element.197), channel_id=1, source_target_pairs={{0,6},{1,7},{2,4},{3,5},{4,2},{5,3},{6,0},{7,1},{8,14},{9,15},{10,... | collective-permute-start | bytes 1572872 | tf_op jit(solution)/shard_map/ppermute | solution.py:400
  115.1 1.7 collective-permute-start.24
  116.8 1.4 collective-permute-start.23
  118.2 5.4 %shard_map.79.total = f32[2,512,1024]{2,1,0:T(8,128)S(1)} custom-call(s32[4]{0:T(128)S(1)} %get-tuple-element.93.order, f32[2,256,512]{2,1,0:T(8,128)S(1)} %shard_map.76.own_a, f32[2,256,512]{2,1,0:T(8,128)S(1)} %shard_map.77.own_b, f32[512,4096]{1,0:T(8,128)S(1)} %bitcast.33), custom_call_target="tpu_custom_call" | custom-call | flops 100000 | bytes 1024 | tf_op jit(solution)/shard_map/pallas_call | solution.py:303
  123.7 3.8 %collective-permute-done.22.got_b = f32[256,512]{1,0:T(8,128)S(1)} collective-permute-done((f32[256,512]{1,0:T(8,128)S(1)}, f32[256,512]{1,0:T(8,128)S(1)}, u32[]{:S(2)}, u32[]{:S(2)}) %collective-permute-start.22) | collective-permute-done | bytes 524320 | tf_op jit(solution)/shard_map/ppermute | solution.py:400
  127.5 5.3 %shard_map.80 = (f32[256,512]{1,0:T(8,128)S(1)}, f32[256,512]{1,0:T(8,128)S(1)}, f32[2,256,512]{2,1,0:T(8,128)S(1)}) custom-call(s32[2]{0:T(128)S(1)} %get-tuple-element.92.cores, f32[256,512]{1,0:T(8,128)S(1)} %collective-permute-done.21.got_a, f32[256,512]{1,0:T(8,128)S(1)} %collective-permute-done.22.got_b, f32[512,2048]{1,0:T(8,128)} %collective-permute-done.19.near, ...), custom_call_target="tpu_custom_call" | custom-call | flops 100000 | bytes 1024 | tf_op jit(solution)/shard_map/pallas_call | solution.py:350
  133.6 5.3 %shard_map.81 = (f32[256,512]{1,0:T(8,128)S(1)}, f32[256,512]{1,0:T(8,128)S(1)}, f32[2,256,512]{2,1,0:T(8,128)S(1)}) custom-call(s32[2]{0:T(128)S(1)} %get-tuple-element.92.cores, f32[256,512]{1,0:T(8,128)S(1)} %collective-permute-done.23.got_a, f32[256,512]{1,0:T(8,128)S(1)} %collective-permute-done.24.got_b, f32[512,2048]{1,0:T(8,128)} %collective-permute-done.19.near, ...), custom_call_target="tpu_custom_call" | custom-call | flops 100000 | bytes 1024 | tf_op jit(solution)/shard_map/pallas_call | solution.py:350
  139.8 1.2 collective-permute-done.27
  140.9 0.7 collective-permute-done.28
  142.1 1.8 %collective-permute-start.31 = (f32[512,512]{1,0:T(8,128)S(1)}, f32[512,512]{1,0:T(8,128)S(1)}, u32[]{:S(2)}, u32[]{:S(2)}) collective-permute-start(f32[512,512]{1,0:T(8,128)S(1)} %pad_maximum_fusion.1), channel_id=1, source_target_pairs={{0,6},{1,7},{2,4},{3,5},{4,2},{5,3},{6,0},{7,1},{8,14},{9,15},{10,... | collective-permute-start | bytes 3145736 | tf_op jit(solution)/shard_map/ppermute | solution.py:400
  143.9 5.4 %shard_map.82.total = f32[2,512,1024]{2,1,0:T(8,128)S(1)} custom-call(s32[4]{0:T(128)S(1)} %get-tuple-element.161.order, f32[2,256,512]{2,1,0:T(8,128)S(1)} %shard_map.76.own_a, f32[2,256,512]{2,1,0:T(8,128)S(1)} %shard_map.77.own_b, f32[512,4096]{1,0:T(8,128)S(1)} %bitcast.33), custom_call_target="tpu_custom_call" | custom-call | flops 100000 | bytes 1024 | tf_op jit(solution)/shard_map/pallas_call | solution.py:303
  149.3 5.3 %shard_map.84 = (f32[256,256]{1,0:T(8,128)S(1)}, f32[256,256]{1,0:T(8,128)S(1)}, f32[256,256]{1,0:T(8,128)S(1)}, f32[256,256]{1,0:T(8,128)S(1)}, f32[2,256,512]{2,1,0:T(8,128)S(1)}) custom-call(s32[2]{0:T(128)S(1)} %get-tuple-element.92.cores, f32[256,512]{1,0:T(8,128)S(1)} %collective-permute-done.23.got_a, f32[256,512]{1,0:T(8,128)S(1)} %collective-permute-done.24.got_b, ...), custom_call_target="tpu_custom_call" | custom-call | flops 100000 | bytes 1024 | tf_op jit(solution)/shard_map/pallas_call | solution.py:350
  155.3 5.3 %shard_map.83 = (f32[256,256]{1,0:T(8,128)S(1)}, f32[256,256]{1,0:T(8,128)S(1)}, f32[256,256]{1,0:T(8,128)S(1)}, f32[256,256]{1,0:T(8,128)S(1)}, f32[2,256,512]{2,1,0:T(8,128)S(1)}) custom-call(s32[2]{0:T(128)S(1)} %get-tuple-element.92.cores, f32[256,512]{1,0:T(8,128)S(1)} %collective-permute-done.21.got_a, f32[256,512]{1,0:T(8,128)S(1)} %collective-permute-done.22.got_b, ...), custom_call_target="tpu_custom_call" | custom-call | flops 100000 | bytes 1024 | tf_op jit(solution)/shard_map/pallas_call | solution.py:350
  161.7 0.6 collective-permute-done.38
  163.0 0.8 collective-permute-done.32
  164.2 4.3 %collective-permute-done.31 = f32[512,512]{1,0:T(8,128)S(1)} collective-permute-done((f32[512,512]{1,0:T(8,128)S(1)}, f32[512,512]{1,0:T(8,128)S(1)}, u32[]{:S(2)}, u32[]{:S(2)}) %collective-permute-start.31) | collective-permute-done | bytes 1048608 | tf_op jit(solution)/shard_map/ppermute | solution.py:400
  168.8 0.6 slice_add_fusion.3
  169.4 1.5 pad_maximum_fusion
  (117 shorter events, 9.1 us)
Async XLA Ops:
  0.0 16.2 %copy-start = (s32[32,3]{0,1:T(4,128)S(1)}, s32[32,3]{0,1:T(4,128)}, u32[]{:S(2)}) copy-start(s32[32,3]{0,1:T(4,128)} %param.11) | copy-start | bytes 1156
  0.0 20.8 %collective-permute-start.1 = (f32[1024,128]{1,0:T(8,128)}, f32[1024,128]{1,0:T(8,128)S(1)}, u32[]{:S(2)}, u32[]{:S(2)}) collective-permute-start(f32[1024,128]{1,0:T(8,128)} %k_own.1), channel_id=1, source_target_pairs={{0,24},{8,0},{16,8},{24,16},{32,56},{40,32},{48,40},{56,48},{64,88... | collective-permute-start | bytes 1572872 | tf_op jit(solution)/shard_map/ppermute | solution.py:392
  0.5 18.1 %collective-permute-start = (f32[1024,128]{1,0:T(8,128)}, f32[1024,128]{1,0:T(8,128)S(1)}, u32[]{:S(2)}, u32[]{:S(2)}) collective-permute-start(f32[1024,128]{1,0:T(8,128)} %k_own.1), channel_id=1, source_target_pairs={{0,8},{8,16},{16,24},{24,0},{32,40},{40,48},{48,56},{56,32},{64,72... | collective-permute-start | bytes 1572872 | tf_op jit(solution)/shard_map/ppermute | solution.py:392
  2.0 18.8 %collective-permute-start.2 = (f32[1024,128]{1,0:T(8,128)}, f32[1024,128]{1,0:T(8,128)S(1)}, u32[]{:S(2)}, u32[]{:S(2)}) collective-permute-start(f32[1024,128]{1,0:T(8,128)} %v_own.1), channel_id=1, source_target_pairs={{0,32},{8,40},{16,48},{24,56},{32,64},{40,72},{48,80},{56,88},{64,... | collective-permute-start | bytes 1572872 | tf_op jit(solution)/shard_map/ppermute | solution.py:392
  4.5 12.2 %copy-start.5 = (s32[32,8]{0,1:T(8,128)S(1)}, s32[32,8]{0,1:T(8,128)}, u32[]{:S(2)}) copy-start(s32[32,8]{0,1:T(8,128)} %param.10) | copy-start | bytes 3076
  4.5 14.1 %copy-start.2 = (f32[1024,128]{1,0:T(8,128)S(1)}, f32[1024,128]{1,0:T(8,128)}, u32[]{:S(2)}) copy-start(f32[1024,128]{1,0:T(8,128)} %v_own.1) | copy-start | bytes 1572868
  11.8 105.0 %collective-permute-start.19 = (f32[512,2048]{1,0:T(8,128)}, f32[512,2048]{1,0:T(8,128)}, u32[]{:S(2)}, u32[]{:S(2)}) collective-permute-start(f32[512,2048]{1,0:T(8,128)} %get-tuple-element.133), channel_id=1, source_target_pairs={{0,2},{1,3},{2,0},{3,1},{4,6},{5,7},{6,4},{7,5},{8,10},{9,11},{10,... | collective-permute-start | bytes 12582920 | tf_op jit(solution)/shard_map/ppermute | solution.py:400
  13.3 104.9 %collective-permute-start.20 = (f32[512,2048]{1,0:T(8,128)}, f32[512,2048]{1,0:T(8,128)}, u32[]{:S(2)}, u32[]{:S(2)}) collective-permute-start(f32[512,2048]{1,0:T(8,128)} %get-tuple-element.134), channel_id=1, source_target_pairs={{0,6},{1,7},{2,4},{3,5},{4,2},{5,3},{6,0},{7,1},{8,14},{9,15},{10,... | collective-permute-start | bytes 12582920 | tf_op jit(solution)/shard_map/ppermute | solution.py:400
  18.6 12.5 %collective-permute-start.4 = (f32[1024,128]{1,0:T(8,128)S(1)}, f32[1024,128]{1,0:T(8,128)S(1)}, u32[]{:S(2)}, u32[]{:S(2)}) collective-permute-start(f32[1024,128]{1,0:T(8,128)S(1)} %copy-done.2), channel_id=1, source_target_pairs={{0,96},{8,104},{16,112},{24,120},{32,0},{40,8},{48,16},{56,24},{64... | collective-permute-start | bytes 1572872 | tf_op jit(solution)/shard_map/ppermute | solution.py:392
  20.8 11.8 %collective-permute-start.7 = (f32[1024,128]{1,0:T(8,128)S(1)}, f32[1024,128]{1,0:T(8,128)S(1)}, u32[]{:S(2)}, u32[]{:S(2)}) collective-permute-start(f32[1024,128]{1,0:T(8,128)S(1)} %collective-permute-done.refs_3_.k_left), channel_id=1, source_target_pairs={{0,32},{32,64},{64,96},{1,33},{33,65},{65,97},{2,34},{34,66},{66,9... | collective-permute-start | bytes 1572872 | tf_op jit(solution)/shard_map/ppermute | solution.py:392
  21.6 29.9 %copy-start.3 = (f32[1024,128]{1,0:T(8,128)S(1)}, f32[1024,128]{1,0:T(8,128)}, u32[]{:S(2)}) copy-start(f32[1024,128]{1,0:T(8,128)} %k_own.1) | copy-start | bytes 1572868
  21.7 17.9 %collective-permute-start.3 = (f32[1536,128]{1,0:T(8,128)S(1)}, f32[1536,128]{1,0:T(8,128)S(1)}, u32[]{:S(2)}, u32[]{:S(2)}) collective-permute-start(f32[1536,128]{1,0:T(8,128)S(1)} %pad_maximum_fusion.3), channel_id=1, source_target_pairs={{0,24},{8,0},{16,8},{24,16},{32,56},{40,32},{48,40},{56,48},{64,88... | collective-permute-start | bytes 2359304 | tf_op jit(solution)/shard_map/ppermute | solution.py:392
  31.1 17.3 %collective-permute-start.6 = (f32[1536,128]{1,0:T(8,128)S(1)}, f32[1536,128]{1,0:T(8,128)S(1)}, u32[]{:S(2)}, u32[]{:S(2)}) collective-permute-start(f32[1536,128]{1,0:T(8,128)S(1)} %pad_maximum_fusion.4), channel_id=1, source_target_pairs={{0,8},{8,16},{16,24},{24,0},{32,40},{40,48},{48,56},{56,32},{64,72... | collective-permute-start | bytes 2359304 | tf_op jit(solution)/shard_map/ppermute | solution.py:392
  32.6 15.8 %collective-permute-start.5 = (f32[1024,128]{1,0:T(8,128)S(1)}, f32[1024,128]{1,0:T(8,128)S(1)}, u32[]{:S(2)}, u32[]{:S(2)}) collective-permute-start(f32[1024,128]{1,0:T(8,128)S(1)} %collective-permute-done.4.refs_5_), channel_id=1, source_target_pairs={{0,96},{8,104},{16,112},{24,120},{32,0},{40,8},{48,16},{56,24},{64... | collective-permute-start | bytes 1572872 | tf_op jit(solution)/shard_map/ppermute | solution.py:392
  48.5 21.1 %copy-start.4 = (f32[1024,512]{1,0:T(8,128)S(1)}, f32[1024,512]{1,0:T(8,128)}, u32[]{:S(2)}) copy-start(f32[1024,512]{1,0:T(8,128)} %q.1) | copy-start | bytes 6291460
  48.5 8.7 %collective-permute-start.9 = (f32[512,128]{1,0:T(8,128)S(1)}, f32[512,128]{1,0:T(8,128)S(1)}, u32[]{:S(2)}, u32[]{:S(2)}) collective-permute-start(f32[512,128]{1,0:T(8,128)S(1)} %slice.69), channel_id=1, source_target_pairs={{0,24},{8,0},{16,8},{24,16},{32,56},{40,32},{48,40},{56,48},{64,88... | collective-permute-start | bytes 786440 | tf_op jit(solution)/shard_map/ppermute | solution.py:392
  53.4 13.4 %collective-permute-start.11 = (f32[1024,128]{1,0:T(8,128)S(1)}, f32[1024,128]{1,0:T(8,128)S(1)}, u32[]{:S(2)}, u32[]{:S(2)}) collective-permute-start(f32[1024,128]{1,0:T(8,128)S(1)} %get-tuple-element.105), channel_id=1, source_target_pairs={{0,32},{8,40},{16,48},{24,56},{32,0},{40,8},{48,16},{56,24},{64,96... | collective-permute-start | bytes 1572872 | tf_op jit(solution)/shard_map/ppermute | solution.py:392
  55.0 14.6 %collective-permute-start.12 = (f32[1024,128]{1,0:T(8,128)S(1)}, f32[1024,128]{1,0:T(8,128)S(1)}, u32[]{:S(2)}, u32[]{:S(2)}) collective-permute-start(f32[1024,128]{1,0:T(8,128)S(1)} %get-tuple-element.106), channel_id=1, source_target_pairs={{0,96},{8,104},{16,112},{24,120},{32,64},{40,72},{48,80},{56,88},{... | collective-permute-start | bytes 1572872 | tf_op jit(solution)/shard_map/ppermute | solution.py:392
  57.3 6.4 %collective-permute-start.8 = (f32[512,128]{1,0:T(8,128)S(1)}, f32[512,128]{1,0:T(8,128)S(1)}, u32[]{:S(2)}, u32[]{:S(2)}) collective-permute-start(f32[512,128]{1,0:T(8,128)S(1)} %slice.68), channel_id=1, source_target_pairs={{0,8},{8,16},{16,24},{24,0},{32,40},{40,48},{48,56},{56,32},{64,72... | collective-permute-start | bytes 786440 | tf_op jit(solution)/shard_map/ppermute | solution.py:392
  63.7 15.1 %collective-permute-start.10 = (f32[1024,128]{1,0:T(8,128)S(1)}, f32[1024,128]{1,0:T(8,128)S(1)}, u32[]{:S(2)}, u32[]{:S(2)}) collective-permute-start(f32[1024,128]{1,0:T(8,128)S(1)} %slice.70.refs_2_.k_far), channel_id=1, source_target_pairs={{0,32},{8,40},{32,64},{40,72},{64,96},{72,104},{1,33},{9,41},{33,6... | collective-permute-start | bytes 1572872 | tf_op jit(solution)/shard_map/ppermute | solution.py:392
  66.7 10.2 %collective-permute-start.13 = (f32[1024,128]{1,0:T(8,128)S(1)}, f32[1024,128]{1,0:T(8,128)S(1)}, u32[]{:S(2)}, u32[]{:S(2)}) collective-permute-start(f32[1024,128]{1,0:T(8,128)S(1)} %get-tuple-element.107), channel_id=1, source_target_pairs={{0,8},{8,0},{16,24},{24,16},{32,40},{40,32},{48,56},{56,48},{64,72... | collective-permute-start | bytes 1572872 | tf_op jit(solution)/shard_map/ppermute | solution.py:392
  69.6 9.2 %collective-permute-start.14 = (f32[1024,128]{1,0:T(8,128)S(1)}, f32[1024,128]{1,0:T(8,128)S(1)}, u32[]{:S(2)}, u32[]{:S(2)}) collective-permute-start(f32[1024,128]{1,0:T(8,128)S(1)} %get-tuple-element.108), channel_id=1, source_target_pairs={{0,24},{8,16},{16,8},{24,0},{32,56},{40,48},{48,40},{56,32},{64,88... | collective-permute-start | bytes 1572872 | tf_op jit(solution)/shard_map/ppermute | solution.py:392
  78.9 10.5 %collective-permute-start.15 = (f32[1024,128]{1,0:T(8,128)S(1)}, f32[1024,128]{1,0:T(8,128)S(1)}, u32[]{:S(2)}, u32[]{:S(2)}) collective-permute-start(f32[1024,128]{1,0:T(8,128)S(1)} %add.219), channel_id=1, source_target_pairs={{0,96},{8,104},{16,112},{24,120},{32,64},{40,72},{48,80},{56,88},{... | collective-permute-start | bytes 1572872 | tf_op jit(solution)/shard_map/ppermute | solution.py:392
  80.0 20.4 %collective-permute-start.16 = (f32[1024,128]{1,0:T(8,128)S(1)}, f32[1024,128]{1,0:T(8,128)S(1)}, u32[]{:S(2)}, u32[]{:S(2)}) collective-permute-start(f32[1024,128]{1,0:T(8,128)S(1)} %add.220), channel_id=1, source_target_pairs={{0,32},{8,40},{16,48},{24,56},{32,0},{40,8},{48,16},{56,24},{64,96... | collective-permute-start | bytes 1572872 | tf_op jit(solution)/shard_map/ppermute | solution.py:392
  83.0 17.3 %collective-permute-start.17 = (f32[1024,128]{1,0:T(8,128)S(1)}, f32[1024,128]{1,0:T(8,128)S(1)}, u32[]{:S(2)}, u32[]{:S(2)}) collective-permute-start(f32[1024,128]{1,0:T(8,128)S(1)} %add.221), channel_id=1, source_target_pairs={{0,24},{8,16},{16,8},{24,0},{32,56},{40,48},{48,40},{56,32},{64,88... | collective-permute-start | bytes 1572872 | tf_op jit(solution)/shard_map/ppermute | solution.py:392
  89.4 11.0 %collective-permute-start.18 = (f32[1024,128]{1,0:T(8,128)S(1)}, f32[1024,128]{1,0:T(8,128)S(1)}, u32[]{:S(2)}, u32[]{:S(2)}) collective-permute-start(f32[1024,128]{1,0:T(8,128)S(1)} %add.222), channel_id=1, source_target_pairs={{0,8},{8,0},{16,24},{24,16},{32,40},{40,32},{48,56},{56,48},{64,72... | collective-permute-start | bytes 1572872 | tf_op jit(solution)/shard_map/ppermute | solution.py:392
  100.6 17.6 %slice-start = ((s8[8388608]{0:T(1024)(128)(4,1)}), s8[4194304]{0:T(1024)(128)(4,1)S(1)}, s32[]{:S(2)}) async-start(s8[8388608]{0:T(1024)(128)(4,1)} %bitcast.32), calls=%async_computation | async-start | bytes 8388608
  106.9 11.3 %slice-start.1 = ((s8[8388608]{0:T(1024)(128)(4,1)}), s8[4194304]{0:T(1024)(128)(4,1)S(1)}, s32[]{:S(2)}) async-start(s8[8388608]{0:T(1024)(128)(4,1)} %bitcast.32), calls=%async_computation.1 | async-start | bytes 8388608
  113.3 14.1 %collective-permute-start.22 = (f32[256,512]{1,0:T(8,128)S(1)}, f32[256,512]{1,0:T(8,128)S(1)}, u32[]{:S(2)}, u32[]{:S(2)}) collective-permute-start(f32[256,512]{1,0:T(8,128)S(1)} %get-tuple-element.197), channel_id=1, source_target_pairs={{0,6},{1,7},{2,4},{3,5},{4,2},{5,3},{6,0},{7,1},{8,14},{9,15},{10,... | collective-permute-start | bytes 1572872 | tf_op jit(solution)/shard_map/ppermute | solution.py:400
  115.0 12.4 %collective-permute-start.21 = (f32[256,512]{1,0:T(8,128)S(1)}, f32[256,512]{1,0:T(8,128)S(1)}, u32[]{:S(2)}, u32[]{:S(2)}) collective-permute-start(f32[256,512]{1,0:T(8,128)S(1)} %get-tuple-element.198), channel_id=1, source_target_pairs={{0,2},{1,3},{2,0},{3,1},{4,6},{5,7},{6,4},{7,5},{8,10},{9,11},{10,... | collective-permute-start | bytes 1572872 | tf_op jit(solution)/shard_map/ppermute | solution.py:400
  115.1 18.0 %collective-permute-start.24 = (f32[256,512]{1,0:T(8,128)S(1)}, f32[256,512]{1,0:T(8,128)S(1)}, u32[]{:S(2)}, u32[]{:S(2)}) collective-permute-start(f32[256,512]{1,0:T(8,128)S(1)} %get-tuple-element.195), channel_id=1, source_target_pairs={{0,6},{1,7},{2,4},{3,5},{4,2},{5,3},{6,0},{7,1},{8,14},{9,15},{10,... | collective-permute-start | bytes 1572872 | tf_op jit(solution)/shard_map/ppermute | solution.py:400
  116.8 16.3 %collective-permute-start.23 = (f32[256,512]{1,0:T(8,128)S(1)}, f32[256,512]{1,0:T(8,128)S(1)}, u32[]{:S(2)}, u32[]{:S(2)}) collective-permute-start(f32[256,512]{1,0:T(8,128)S(1)} %get-tuple-element.196), channel_id=1, source_target_pairs={{0,2},{1,3},{2,0},{3,1},{4,6},{5,7},{6,4},{7,5},{8,10},{9,11},{10,... | collective-permute-start | bytes 1572872 | tf_op jit(solution)/shard_map/ppermute | solution.py:400
  133.1 5.8 %collective-permute-start.25 = (f32[256,512]{1,0:T(8,128)S(1)}, f32[256,512]{1,0:T(8,128)S(1)}, u32[]{:S(2)}, u32[]{:S(2)}) collective-permute-start(f32[256,512]{1,0:T(8,128)S(1)} %get-tuple-element.150), channel_id=1, source_target_pairs={{0,1},{1,0},{2,3},{3,2},{4,5},{5,4},{6,7},{7,6},{8,9},{9,8},{10,11... | collective-permute-start | bytes 1572872 | tf_op jit(solution)/shard_map/ppermute | solution.py:400
  133.1 5.8 %collective-permute-start.26 = (f32[256,512]{1,0:T(8,128)S(1)}, f32[256,512]{1,0:T(8,128)S(1)}, u32[]{:S(2)}, u32[]{:S(2)}) collective-permute-start(f32[256,512]{1,0:T(8,128)S(1)} %get-tuple-element.151), channel_id=1, source_target_pairs={{0,1},{1,0},{2,3},{3,2},{4,5},{5,4},{6,7},{7,6},{8,9},{9,8},{10,11... | collective-permute-start | bytes 1572872 | tf_op jit(solution)/shard_map/ppermute | solution.py:400
  138.9 2.0 %collective-permute-start.27 = (f32[256,512]{1,0:T(8,128)S(1)}, f32[256,512]{1,0:T(8,128)S(1)}, u32[]{:S(2)}, u32[]{:S(2)}) collective-permute-start(f32[256,512]{1,0:T(8,128)S(1)} %get-tuple-element.154), channel_id=1, source_target_pairs={{0,1},{1,0},{2,3},{3,2},{4,5},{5,4},{6,7},{7,6},{8,9},{9,8},{10,11... | collective-permute-start | bytes 1572872 | tf_op jit(solution)/shard_map/ppermute | solution.py:400
  139.0 2.6 %collective-permute-start.28 = (f32[256,512]{1,0:T(8,128)S(1)}, f32[256,512]{1,0:T(8,128)S(1)}, u32[]{:S(2)}, u32[]{:S(2)}) collective-permute-start(f32[256,512]{1,0:T(8,128)S(1)} %get-tuple-element.156), channel_id=1, source_target_pairs={{0,1},{1,0},{2,3},{3,2},{4,5},{5,4},{6,7},{7,6},{8,9},{9,8},{10,11... | collective-permute-start | bytes 1572872 | tf_op jit(solution)/shard_map/ppermute | solution.py:400
  142.1 26.5 %collective-permute-start.31 = (f32[512,512]{1,0:T(8,128)S(1)}, f32[512,512]{1,0:T(8,128)S(1)}, u32[]{:S(2)}, u32[]{:S(2)}) collective-permute-start(f32[512,512]{1,0:T(8,128)S(1)} %pad_maximum_fusion.1), channel_id=1, source_target_pairs={{0,6},{1,7},{2,4},{3,5},{4,2},{5,3},{6,0},{7,1},{8,14},{9,15},{10,... | collective-permute-start | bytes 3145736 | tf_op jit(solution)/shard_map/ppermute | solution.py:400
  143.9 24.9 %collective-permute-start.34 = (f32[512,512]{1,0:T(8,128)S(1)}, f32[512,512]{1,0:T(8,128)S(1)}, u32[]{:S(2)}, u32[]{:S(2)}) collective-permute-start(f32[512,512]{1,0:T(8,128)S(1)} %pad_maximum_fusion.2), channel_id=1, source_target_pairs={{0,2},{1,3},{2,0},{3,1},{4,6},{5,7},{6,4},{7,5},{8,10},{9,11},{10,... | collective-permute-start | bytes 3145736 | tf_op jit(solution)/shard_map/ppermute | solution.py:400
  154.6 6.0 %collective-permute-start.35 = (f32[256,256]{1,0:T(8,128)S(1)}, f32[256,256]{1,0:T(8,128)S(1)}, u32[]{:S(2)}, u32[]{:S(2)}) collective-permute-start(f32[256,256]{1,0:T(8,128)S(1)} %get-tuple-element.173), channel_id=1, source_target_pairs={{0,1},{1,0},{2,3},{3,2},{4,5},{5,4},{6,7},{7,6},{8,9},{9,8},{10,11... | collective-permute-start | bytes 786440 | tf_op jit(solution)/shard_map/ppermute | solution.py:400
  154.7 6.4 %collective-permute-start.36 = (f32[256,256]{1,0:T(8,128)S(1)}, f32[256,256]{1,0:T(8,128)S(1)}, u32[]{:S(2)}, u32[]{:S(2)}) collective-permute-start(f32[256,256]{1,0:T(8,128)S(1)} %get-tuple-element.174), channel_id=1, source_target_pairs={{0,1},{1,0},{2,3},{3,2},{4,5},{5,4},{6,7},{7,6},{8,9},{9,8},{10,11... | collective-permute-start | bytes 786440 | tf_op jit(solution)/shard_map/ppermute | solution.py:400
  155.2 6.0 %collective-permute-start.37 = (f32[256,256]{1,0:T(8,128)S(1)}, f32[256,256]{1,0:T(8,128)S(1)}, u32[]{:S(2)}, u32[]{:S(2)}) collective-permute-start(f32[256,256]{1,0:T(8,128)S(1)} %get-tuple-element.175), channel_id=1, source_target_pairs={{0,1},{1,0},{2,3},{3,2},{4,5},{5,4},{6,7},{7,6},{8,9},{9,8},{10,11... | collective-permute-start | bytes 786440 | tf_op jit(solution)/shard_map/ppermute | solution.py:400
  160.6 1.7 collective-permute-start.38
  161.1 1.5 collective-permute-start.29
  161.2 1.8 %collective-permute-start.30 = (f32[256,256]{1,0:T(8,128)S(1)}, f32[256,256]{1,0:T(8,128)S(1)}, u32[]{:S(2)}, u32[]{:S(2)}) collective-permute-start(f32[256,256]{1,0:T(8,128)S(1)} %get-tuple-element.165), channel_id=1, source_target_pairs={{0,1},{1,0},{2,3},{3,2},{4,5},{5,4},{6,7},{7,6},{8,9},{9,8},{10,11... | collective-permute-start | bytes 786440 | tf_op jit(solution)/shard_map/ppermute | solution.py:400
  162.3 1.5 collective-permute-start.32
  162.7 1.5 collective-permute-start.33
  169.4 1.5 copy-start.1
